TPU v7x, 32 devices: a whole 2x2x4 slice. The times are simulated.
32 devices in a mesh: dist: 2 (over core), rows: 16 (over z, y, x).
Axes of the slice: x: 2, y: 2, z: 4, core: 2. Of those that a mesh axis runs over, the one named last changes fastest.
Arguments:
- holograms: bfloat16 [1, 4, 4, 1024, 1024], P(None, None, 'dist', 'rows'), may hold values from -6 to 6
- propagation: float32 [4], replicated, may hold values from 100 to 1000
- weights: bfloat16 [4, 1024, 1024], P(None, None, 'dist'), may hold values from -0.09375 to 0.09375
- angle_order: int32 [1, 4], replicated, may hold values from 0 to 3, each once within a row
- slab_rows: int32 [16], replicated, may hold values from 0 to 128, as said below
Outputs:
- slab: bfloat16 [2048, 1024], P('rows', 'dist')
Inputs may be any that keep to these rules, and one draw needn't show every extreme that they name: Owners 2j and 2j+1 together own 128 slices: slab_rows[2j] + slab_rows[2j+1] = 128, so owner 2j holds slices 2j 64 onward and owner 2j+1 the rest of that pair's range; in every draw some owner holds 128.
All inputs are finite; a program needn't handle non-finite values.
Results may differ from a plain program's by a relative error of at most 0.02.
Values may be sent and summed in bfloat16 or wider, within the bound.
No kernel may reach another device: no remote copies, remote signals or barrier semaphores. Data moves between devices by JAX's collectives and lax.ppermute only.
A program may use at most 128 MiB of HBM per device.

v0:
```python
import math

import jax
import jax.numpy as jnp
from jax import lax
from jax.sharding import PartitionSpec as P

absorb_ratio = 0.1
regularizer = 0.05


def swapped(value, axis, bit):
    mask = 2**bit
    pairs = [(source, source ^ mask) for source in range(lax.axis_size(axis))]
    return lax.ppermute(value, axis, pairs)


def dft_tables(length):
    index = jnp.arange(length, dtype=jnp.int32)
    product = index[:, None] * index[None, :] % length
    turned = product.astype(jnp.float32) * (2.0 * math.pi / length)
    factor = 1.0 / math.sqrt(length)
    return (
        (jnp.cos(turned) * factor).astype(jnp.bfloat16),
        (jnp.sin(turned) * factor).astype(jnp.bfloat16),
    )


def on_device(holograms, propagation, weights, angle_order, slab_rows):
    mbatch, angles, dist_dev, rows_dev, width = holograms.shape
    groups = lax.axis_size("rows")
    capacity = 2 * rows_dev
    cosine, sine = dft_tables(width)
    col_cos = cosine.reshape(groups, rows_dev, width)
    col_sin = sine.reshape(groups, rows_dev, width)
    index = jnp.arange(width, dtype=jnp.int32)
    signed = jnp.where(index < width // 2, index, index - width).astype(jnp.float32)
    device = lax.axis_index("rows")
    local_freq = lax.dynamic_slice_in_dim(signed, device * rows_dev, rows_dev, 0)
    radius = (local_freq[:, None] ** 2 + signed[None, :] ** 2) / float(width * width)
    chirp = propagation[:, None, None] * radius[None]
    transfer = 2.0 * (jnp.sin(chirp) + absorb_ratio * jnp.cos(chirp))
    denom = jnp.sum(transfer * transfer, axis=0) + regularizer
    mine = lax.dynamic_slice_in_dim(transfer, lax.axis_index("dist") * dist_dev, dist_dev, 0)
    parity = device % 2
    offset = parity * slab_rows[device - parity]
    count = slab_rows[device]
    slot = jnp.arange(capacity, dtype=jnp.int32)[:, None]
    source = jnp.arange(capacity, dtype=jnp.int32)[None, :]
    select = ((source == offset + slot) & (slot < count)).astype(jnp.float32)
    flat = holograms[0].reshape(angles * dist_dev * rows_dev, width)
    row_re = jnp.dot(flat, cosine, preferred_element_type=jnp.float32).astype(jnp.bfloat16)
    row_im = (-jnp.dot(flat, sine, preferred_element_type=jnp.float32)).astype(jnp.bfloat16)
    row_re = row_re.reshape(angles * dist_dev, rows_dev, width)
    row_im = row_im.reshape(angles * dist_dev, rows_dev, width)
    pieces = (
        lax.all_to_all(row_re, "rows", split_axis=2, concat_axis=2, tiled=True),
        lax.all_to_all(row_im, "rows", split_axis=2, concat_axis=2, tiled=True),
    )
    items = pieces[0].shape[0]
    real_part = pieces[0].reshape(items, rows_dev, groups, rows_dev)
    imag_part = pieces[1].reshape(items, rows_dev, groups, rows_dev)
    out_re = jnp.einsum("aysk,syq->akq", real_part, col_cos, preferred_element_type=jnp.float32)
    out_re = out_re + jnp.einsum(
        "aysk,syq->akq", imag_part, col_sin, preferred_element_type=jnp.float32
    )
    out_im = jnp.einsum("aysk,syq->akq", imag_part, col_cos, preferred_element_type=jnp.float32)
    out_im = out_im - jnp.einsum(
        "aysk,syq->akq", real_part, col_sin, preferred_element_type=jnp.float32
    )
    spec_re = out_re
    spec_im = out_im
    spec_re = spec_re.reshape(angles, dist_dev, rows_dev, width)
    spec_im = spec_im.reshape(angles, dist_dev, rows_dev, width)
    numer_re = jnp.sum(mine[None] * spec_re, axis=1)
    numer_im = jnp.sum(mine[None] * spec_im, axis=1)
    numer_re, numer_im = (
        lax.psum_scatter(
            numer_re.astype(jnp.bfloat16), "dist", scatter_dimension=0, tiled=True
        ).astype(jnp.float32),
        lax.psum_scatter(
            numer_im.astype(jnp.bfloat16), "dist", scatter_dimension=0, tiled=True
        ).astype(jnp.float32),
    )
    spec_phase_re = (numer_re / denom).astype(jnp.bfloat16)
    spec_phase_im = (numer_im / denom).astype(jnp.bfloat16)
    half_re = jnp.einsum("akq,qy->aky", spec_phase_re, cosine, preferred_element_type=jnp.float32)
    half_re = (
        half_re - jnp.einsum("akq,qy->aky", spec_phase_im, sine, preferred_element_type=jnp.float32)
    ).astype(jnp.bfloat16)
    half_im = jnp.einsum("akq,qy->aky", spec_phase_im, cosine, preferred_element_type=jnp.float32)
    half_im = (
        half_im + jnp.einsum("akq,qy->aky", spec_phase_re, sine, preferred_element_type=jnp.float32)
    ).astype(jnp.bfloat16)
    pieces = (
        lax.all_to_all(half_re, "rows", split_axis=2, concat_axis=2, tiled=True),
        lax.all_to_all(half_im, "rows", split_axis=2, concat_axis=2, tiled=True),
    )
    items = pieces[0].shape[0]
    real_part = pieces[0].reshape(items, rows_dev, groups, rows_dev)
    imag_part = pieces[1].reshape(items, rows_dev, groups, rows_dev)
    result = jnp.einsum("aksy,skx->ayx", real_part, col_cos, preferred_element_type=jnp.float32)
    phase = (
        result - jnp.einsum("aksy,skx->ayx", imag_part, col_sin, preferred_element_type=jnp.float32)
    ).astype(jnp.bfloat16)
    chosen = weights[0 + angle_order[0]]
    partner = swapped(phase, "rows", 0)
    lower = jnp.where(parity == 1, partner, phase)
    upper = jnp.where(parity == 1, phase, partner)
    paired = jnp.concatenate([lower, upper], axis=1)
    rows_in = jnp.einsum(
        "ij,ajx->aix", select.astype(jnp.bfloat16), paired, preferred_element_type=jnp.float32
    ).astype(jnp.bfloat16)
    recon = jnp.einsum(
        "ayx,axp->yp",
        lax.all_gather(rows_in, "dist", axis=0, tiled=True),
        chosen,
        preferred_element_type=jnp.float32,
    )
    return recon.astype(jnp.bfloat16)


def solution(mesh):
    return jax.shard_map(
        on_device,
        mesh=mesh,
        in_specs=(P(None, None, "dist", "rows", None), P(), P(None, None, "dist"), P(), P()),
        out_specs=P("rows", "dist"),
        check_vma=False,
    )
```

profile of v0, /device:TPU:0, one launch (start us, length us, event | category | flops | bytes accessed | tf_op | source)
XLA Modules:
  0.0 330.8 jit_solution(11319298059359370535)
XLA Ops:
  6.5 0.0 copy-start
  6.5 1.2 copy-done
  7.8 18.8 %fusion.40 = bf16[1024,512]{0,1:T(8,128)(2,1)} fusion(bf16[512,1024]{1,0:T(8,128)(2,1)S(1)} %bitcast.113), kind=kOutput, calls=%fused_computation.48 | convolution fusion | flops 1091043328 | bytes 2097152 | tf_op jit(solution)/shard_map/dot_general | solution.py:52
  26.6 2.6 copy.10
  29.2 2.2 reshape.156
  31.5 8.4 %all-to-all-start = ((bf16[16,2,16384]{2,1,0:T(2,128)(2,1)}), bf16[16,2,16384]{2,1,0:T(2,128)(2,1)}, u32[]{:S(2)}, u32[]{:S(2)}) async-start(bf16[16,2,16384]{2,1,0:T(2,128)(2,1)} %reshape.156), calls=%async_computation | async-start | bytes 2097152 | tf_op jit(solution)/shard_map/all_to_all | solution.py:57
  39.8 18.9 %negate_convert_fusion = bf16[1024,512]{0,1:T(8,128)(2,1)} fusion(bf16[512,1024]{1,0:T(8,128)(2,1)S(1)} %bitcast.112), kind=kOutput, calls=%fused_computation.37 | convolution fusion | flops 1091567616 | bytes 2097152 | tf_op jit(solution)/shard_map/dot_general | solution.py:53
  58.7 2.6 copy.12
  61.4 2.2 reshape.154
  63.6 0.7 all-to-all-done
  64.3 6.2 %all-to-all-start.1 = ((bf16[16,2,16384]{2,1,0:T(2,128)(2,1)}), bf16[16,2,16384]{2,1,0:T(2,128)(2,1)}, u32[]{:S(2)}, u32[]{:S(2)}) async-start(bf16[16,2,16384]{2,1,0:T(2,128)(2,1)} %reshape.154), calls=%async_computation.1 | async-start | bytes 2097152 | tf_op jit(solution)/shard_map/all_to_all | solution.py:58
  70.5 0.5 reduce-scatter.3.cloned.1.call-start
  71.1 0.1 dynamic-slice_multiply_fusion
  71.2 0.1 add_multiply_fusion
  71.2 0.0 copy-done.3
  71.3 3.9 %multiply_reduce_fusion.2 = (f32[64,1024]{1,0:T(8,128)S(1)}, f32[4,64,1024]{2,1,0:T(8,128)S(1)}) fusion(f32[64,1024]{1,0:T(8,128)S(1)} %add_multiply_fusion, f32[4]{0:T(128)S(1)} %copy-done.3), kind=kLoop, calls=%fused_computation.64 | loop fusion | flops 1507328 | bytes 1572880 | tf_op jit(solution)/shard_map/reduce_sum | solution.py:43
  75.1 0.9 constant_dynamic-slice_fusion
  76.0 4.7 %reshape.157 = bf16[1024,8,64]{2,1,0:T(8,128)(2,1)} reshape(bf16[16,2,16384]{2,1,0:T(2,128)(2,1)} %all-to-all-done) | data formatting | bytes 2097152
  80.7 1.9 copy.11
  82.6 11.9 %all-to-all-done.1 = bf16[16,2,16384]{2,1,0:T(2,128)(2,1)} async-done(((bf16[16,2,16384]{2,1,0:T(2,128)(2,1)}), bf16[16,2,16384]{2,1,0:T(2,128)(2,1)}, u32[]{:S(2)}, u32[]{:S(2)}) %all-to-all-start.1) | async-done | bytes 1048608 | tf_op jit(solution)/shard_map/all_to_all | solution.py:58
  94.4 4.8 %reshape.155 = bf16[1024,8,64]{2,1,0:T(8,128)(2,1)} reshape(bf16[16,2,16384]{2,1,0:T(2,128)(2,1)} %all-to-all-done.1) | data formatting | bytes 2097152
  99.3 1.9 copy.13
  101.1 16.9 %fusion.24 = f32[8,64,1024,1]{2,1,3,0:T(8,128)S(1)} fusion(bf16[8,64,16,64]{1,3,2,0:T(8,128)(2,1)S(1)} %bitcast.114, s32[16,64]{1,0:T(8,128)S(1)} %multiply_add_fusion), kind=kOutput, calls=%fused_computation.39 | convolution fusion | flops 1090519040 | bytes 3149824 | tf_op jit(solution)/shard_map/aysk,syq->akq/dot_general | solution.py:68
  118.0 17.0 %fusion.26 = f32[8,64,1024,1]{2,1,3,0:T(8,128)S(1)} fusion(bf16[8,64,16,64]{1,3,2,0:T(8,128)(2,1)S(1)} %bitcast.122, s32[16,64]{1,0:T(8,128)S(1)} %multiply_add_fusion), kind=kOutput, calls=%fused_computation.40 | convolution fusion | flops 1090519040 | bytes 3149824 | tf_op jit(solution)/shard_map/aysk,syq->akq/dot_general | solution.py:64
  135.0 0.0 copy-start.1
  135.0 17.0 %bitcast_subtract_fusion = f32[8,64,1024]{2,1,0:T(8,128)S(1)} fusion(f32[8,64,1024,1]{2,1,3,0:T(8,128)S(1)} %fusion.24, bf16[8,64,16,64]{1,3,2,0:T(8,128)(2,1)S(1)} %bitcast.123, s32[16,64]{1,0:T(8,128)S(1)} %multiply_add_fusion), kind=kOutput, calls=%fused_computation.29 | convolution fusion | flops 1091043328 | bytes 5246976 | tf_op jit(solution)/shard_map/aysk,syq->akq/dot_general | solution.py:67
  152.1 0.0 copy-done.1
  152.1 18.2 %multiply_reduce_fusion.1 = (bf16[4,64,1024]{2,1,0:T(8,128)(2,1)}, bf16[4,64,1024]{2,1,0:T(8,128)(2,1)}) fusion(f32[2,64,1024]{2,1,0:T(8,128)S(1)} %copy-done.1, f32[8,64,1024]{2,1,0:T(8,128)S(1)} %bitcast_subtract_fusion, f32[8,64,1024,1]{2,1,3,0:T(8,128)S(1)} %fusion.26, bf16[8,64,16,64]{1,3,2,0:T(8,128)(2,1)S(1)} %bitcast.115, ...), kind=kOutput, calls=%fused_computation.36 | convolution fusion | flops 1092616192 | bytes 6819840 | tf_op jit(solution)/shard_map/aysk,syq->akq/dot_general | solution.py:63
  170.3 0.0 reduce-scatter.3.cloned.1.call-update
  170.3 0.2 reduce-scatter.5.cloned.1.call-start
  170.5 0.5 reduce-scatter.5.cloned.1.call-update
  171.1 7.5 %reduce-scatter.3.cloned.1.call-done = bf16[2,64,1024]{2,1,0:T(8,128)(2,1)} async-done(((bf16[4,64,1024]{2,1,0:T(8,128)(2,1)}), bf16[2,64,1024]{2,1,0:T(8,128)(2,1)}) %reduce-scatter.3.cloned.1.call-update) | async-done | bytes 262160 | tf_op jit(solution)/shard_map/reduce_scatter | solution.py:78
  178.6 17.0 %fusion.14 = f32[2,64,1024]{2,1,0:T(8,128)S(1)} fusion(bf16[2,64,1024]{2,1,0:T(8,128)(2,1)} %reduce-scatter.3.cloned.1.call-done, f32[64,1024]{1,0:T(8,128)S(1)} %broadcast_add_fusion), kind=kOutput, calls=%fused_computation.25 | convolution fusion | flops 285605888 | bytes 1048576 | tf_op jit(solution)/shard_map/akq,qy->aky/dot_general | solution.py:93
  195.6 0.0 reduce-scatter.5.cloned.1.call-done
  195.6 0.0 copy-start.5
  195.6 17.1 %fusion.57 = bf16[2,64,1024]{2,1,0:T(8,128)(2,1)S(1)} fusion(f32[2,64,1024]{2,1,0:T(8,128)S(1)} %fusion.14, bf16[2,64,1024]{2,1,0:T(8,128)(2,1)} %reduce-scatter.5.cloned.1.call-done, f32[64,1024]{1,0:T(8,128)S(1)} %broadcast_add_fusion), kind=kOutput, calls=%fused_computation.56 | convolution fusion | flops 285868032 | bytes 1310720 | tf_op jit(solution)/shard_map/akq,qy->aky/dot_general | solution.py:91
  212.8 0.4 copy.16
  213.2 1.1 reshape.160
  214.3 6.9 %all-to-all-start.3 = ((bf16[16,2,4096]{2,1,0:T(2,128)(2,1)}), bf16[16,2,4096]{2,1,0:T(2,128)(2,1)S(1)}, u32[]{:S(2)}, u32[]{:S(2)}) async-start(bf16[16,2,4096]{2,1,0:T(2,128)(2,1)} %reshape.160), calls=%async_computation.5 | async-start | bytes 524288 | tf_op jit(solution)/shard_map/all_to_all | solution.py:97
  221.2 16.0 %fusion.16 = f32[2,64,1024]{2,1,0:T(8,128)S(1)} fusion(bf16[2,64,1024]{2,1,0:T(8,128)(2,1)S(1)} %copy-done.5, f32[64,1024]{1,0:T(8,128)S(1)} %broadcast_add_fusion), kind=kOutput, calls=%fused_computation.27 | convolution fusion | flops 285605888 | bytes 1048576 | tf_op jit(solution)/shard_map/akq,qy->aky/dot_general | solution.py:89
  237.3 16.1 %fusion.60 = bf16[2,64,1024]{2,1,0:T(8,128)(2,1)S(1)} fusion(f32[2,64,1024]{2,1,0:T(8,128)S(1)} %fusion.16, bf16[2,64,1024]{2,1,0:T(8,128)(2,1)S(1)} %copy-done.4, f32[64,1024]{1,0:T(8,128)S(1)} %broadcast_add_fusion), kind=kOutput, calls=%fused_computation.57 | convolution fusion | flops 285868032 | bytes 1310720 | tf_op jit(solution)/shard_map/akq,qy->aky/dot_general | solution.py:87
  253.4 0.4 copy.14
  253.8 1.1 reshape.158
  254.9 0.0 all-to-all-done.3
  254.9 6.9 %all-to-all-start.2 = ((bf16[16,2,4096]{2,1,0:T(2,128)(2,1)}), bf16[16,2,4096]{2,1,0:T(2,128)(2,1)S(1)}, u32[]{:S(2)}, u32[]{:S(2)}) async-start(bf16[16,2,4096]{2,1,0:T(2,128)(2,1)} %reshape.158), calls=%async_computation.4 | async-start | bytes 524288 | tf_op jit(solution)/shard_map/all_to_all | solution.py:96
  261.8 0.2 all-gather.2.cloned.1.call-start
  262.0 0.3 reshape.161
  262.4 0.1 copy.17
  262.5 9.1 %all-to-all-done.2 = bf16[16,2,4096]{2,1,0:T(2,128)(2,1)S(1)} async-done(((bf16[16,2,4096]{2,1,0:T(2,128)(2,1)}), bf16[16,2,4096]{2,1,0:T(2,128)(2,1)S(1)}, u32[]{:S(2)}, u32[]{:S(2)}) %all-to-all-start.2) | async-done | bytes 262176 | tf_op jit(solution)/shard_map/all_to_all | solution.py:96
  271.6 0.3 reshape.159
  272.0 0.1 copy.15
  272.0 15.9 %fusion.42 = f32[2,64,1024]{2,1,0:T(8,128)S(1)} fusion(bf16[2,64,16,64]{1,3,2,0:T(8,128)(2,1)S(1)} %bitcast.129, s32[16,64]{1,0:T(8,128)S(1)} %multiply_add_fusion), kind=kOutput, calls=%fused_computation.51 | convolution fusion | flops 285212672 | bytes 790528 | tf_op jit(solution)/shard_map/aksy,skx->ayx/dot_general | solution.py:102
  288.0 0.0 copy-start.2
  288.0 0.0 copy-start.6
  288.0 16.1 %fusion.63 = bf16[2,64,1024]{2,1,0:T(8,128)(2,1)S(1)} fusion(f32[2,64,1024]{2,1,0:T(8,128)S(1)} %fusion.42, bf16[2,64,16,64]{1,3,2,0:T(8,128)(2,1)S(1)} %bitcast.128, s32[16,64]{1,0:T(8,128)S(1)} %multiply_add_fusion), kind=kOutput, calls=%fused_computation.58 | convolution fusion | flops 285474816 | bytes 1052672 | tf_op jit(solution)/shard_map/aksy,skx->ayx/dot_general | solution.py:104
  304.1 0.8 collective-permute-start
  305.0 0.6 fusion.142
  306.2 0.7 iota_compare_fusion.1
  306.9 3.7 %collective-permute-done = bf16[2,64,1024]{2,1,0:T(8,128)(2,1)S(1)} collective-permute-done((bf16[2,64,1024]{2,1,0:T(8,128)(2,1)S(1)}, bf16[2,64,1024]{2,1,0:T(8,128)(2,1)S(1)}, u32[]{:S(2)}, u32[]{:S(2)}) %collective-permute-start) | collective-permute-done | bytes 262176 | tf_op jit(solution)/shard_map/ppermute | solution.py:15
  310.6 1.2 fusion.41
  311.8 0.0 all-gather.2.cloned.1.call-update
  311.9 5.0 %gather_fusion = bf16[4,1024,512]{2,1,0:T(8,128)(2,1)} fusion(bf16[4,1024,512]{2,1,0:T(8,128)(2,1)} %param.7, s32[1024]{0:T(1024)S(1)} %pad_clamp_fusion), kind=kCustom, calls=%fused_computation | custom fusion | bytes 8388624 | tf_op jit(solution)/shard_map/gather | solution.py:106
  316.8 3.2 all-gather.2.cloned.1.call-done
  320.0 3.9 %fusion.66 = bf16[128,512]{1,0:T(8,128)(2,1)} fusion(bf16[4,128,1024]{2,1,0:T(8,128)(2,1)} %all-gather.2.cloned.1.call-done, bf16[4,1024,512]{2,1,0:T(8,128)(2,1)} %gather_fusion), kind=kOutput, calls=%fused_computation.60 | convolution fusion | flops 536936448 | bytes 5373952 | tf_op jit(solution)/shard_map/ayx,axp->yp/dot_general | solution.py:114
  (14 shorter events, 0.1 us)
Async XLA Ops:
  6.5 1.2 copy-start
  31.5 32.9 %all-to-all-start = ((bf16[16,2,16384]{2,1,0:T(2,128)(2,1)}), bf16[16,2,16384]{2,1,0:T(2,128)(2,1)}, u32[]{:S(2)}, u32[]{:S(2)}) async-start(bf16[16,2,16384]{2,1,0:T(2,128)(2,1)} %reshape.156), calls=%async_computation | async-start | bytes 2097152 | tf_op jit(solution)/shard_map/all_to_all | solution.py:57
  58.7 12.6 %copy-start.3 = (f32[4]{0:T(128)S(1)}, f32[4]{0:T(128)}, u32[]{:S(2)}) copy-start(f32[4]{0:T(128)} %param.6) | copy-start | bytes 52
  64.3 30.1 %all-to-all-start.1 = ((bf16[16,2,16384]{2,1,0:T(2,128)(2,1)}), bf16[16,2,16384]{2,1,0:T(2,128)(2,1)}, u32[]{:S(2)}, u32[]{:S(2)}) async-start(bf16[16,2,16384]{2,1,0:T(2,128)(2,1)} %reshape.154), calls=%async_computation.1 | async-start | bytes 2097152 | tf_op jit(solution)/shard_map/all_to_all | solution.py:58
  70.5 108.1 %reduce-scatter.3.cloned.1.call-start = ((), (), s32[]{:S(2)}) async-start(), calls=%async_computation.6 | async-start | bytes 786432 | tf_op jit(solution)/shard_map/reduce_scatter | solution.py:78
  135.0 17.0 %copy-start.1 = (f32[2,64,1024]{2,1,0:T(8,128)S(1)}, f32[2,64,1024]{2,1,0:T(8,128)}, u32[]{:S(2)}) copy-start(f32[2,64,1024]{2,1,0:T(8,128)} %constant_dynamic-slice_fusion) | copy-start | bytes 1572868
  170.3 25.3 %reduce-scatter.5.cloned.1.call-start = ((), (), s32[]{:S(2)}) async-start(), calls=%async_computation.7 | async-start | bytes 786432 | tf_op jit(solution)/shard_map/reduce_scatter | solution.py:81
  195.6 25.6 %copy-start.5 = (bf16[2,64,1024]{2,1,0:T(8,128)(2,1)S(1)}, bf16[2,64,1024]{2,1,0:T(8,128)(2,1)}, u32[]{:S(2)}) copy-start(bf16[2,64,1024]{2,1,0:T(8,128)(2,1)} %reduce-scatter.5.cloned.1.call-done) | copy-start | bytes 786436
  214.3 40.6 %all-to-all-start.3 = ((bf16[16,2,4096]{2,1,0:T(2,128)(2,1)}), bf16[16,2,4096]{2,1,0:T(2,128)(2,1)S(1)}, u32[]{:S(2)}, u32[]{:S(2)}) async-start(bf16[16,2,4096]{2,1,0:T(2,128)(2,1)} %reshape.160), calls=%async_computation.5 | async-start | bytes 524288 | tf_op jit(solution)/shard_map/all_to_all | solution.py:97
  221.2 16.0 %copy-start.4 = (bf16[2,64,1024]{2,1,0:T(8,128)(2,1)S(1)}, bf16[2,64,1024]{2,1,0:T(8,128)(2,1)}, u32[]{:S(2)}) copy-start(bf16[2,64,1024]{2,1,0:T(8,128)(2,1)} %reduce-scatter.3.cloned.1.call-done) | copy-start | bytes 786436
  254.9 16.7 %all-to-all-start.2 = ((bf16[16,2,4096]{2,1,0:T(2,128)(2,1)}), bf16[16,2,4096]{2,1,0:T(2,128)(2,1)S(1)}, u32[]{:S(2)}, u32[]{:S(2)}) async-start(bf16[16,2,4096]{2,1,0:T(2,128)(2,1)} %reshape.158), calls=%async_computation.4 | async-start | bytes 524288 | tf_op jit(solution)/shard_map/all_to_all | solution.py:96
  261.8 58.1 %all-gather.2.cloned.1.call-start = ((), (), s32[]{:S(2)}) async-start(), calls=%async_computation.8 | async-start | bytes 1572864 | tf_op jit(solution)/shard_map/all_gather | solution.py:116
  288.0 17.0 %copy-start.2 = (s32[16]{0:T(128)S(1)}, s32[16]{0:T(128)}, u32[]{:S(2)}) copy-start(s32[16]{0:T(128)} %param.9) | copy-start | bytes 196
  288.0 23.8 %copy-start.6 = (s32[1,4]{1,0:T(1,128)S(1)}, s32[1,4]{1,0:T(1,128)}, u32[]{:S(2)}) copy-start(s32[1,4]{1,0:T(1,128)} %param.8) | copy-start | bytes 52
  304.1 6.4 %collective-permute-start = (bf16[2,64,1024]{2,1,0:T(8,128)(2,1)S(1)}, bf16[2,64,1024]{2,1,0:T(8,128)(2,1)S(1)}, u32[]{:S(2)}, u32[]{:S(2)}) collective-permute-start(bf16[2,64,1024]{2,1,0:T(8,128)(2,1)S(1)} %fusion.63), channel_id=1, source_target_pairs={{0,1},{1,0},{2,3},{3,2},{4,5},{5,4},{6,7},{7,6},{8,9},{9,8},{10,11... | collective-permute-start | bytes 786440 | tf_op jit(solution)/shard_map/ppermute | solution.py:15
Sparse Core Ops, SparseCore 0:
  170.4 8.1 reduce-scatter.2
  181.0 9.1 reduce-scatter.4
  311.9 7.9 all-gather.1
where the time goes:
time: 337 us; the launch traced here: 331 us
  matrix products  210 us (62%)
  waiting for transfers between devices  36.7 us (11%)
  local copies, waits for them, and re-layouts  34.6 us (10%)
  starting transfers between devices  30.2 us (9%)
  between operations  14.5 us (4%)
  other arithmetic  4.78 us (1%)
    dot_general x1, matrix products, on_device(): jnp.dot(flat, sine, preferred_element_type=jnp.float32)  18.9 us
    dot_general x1, matrix products, on_device(): jnp.dot(flat, cosine, preferred_element_type=jnp.float32)  18.8 us
    dot_general x1, matrix products, on_device(): jnp.einsum('aysk,syq->akq', real_part, col_cos, preferred_element_type=jn...  18.2 us
    unnamed x22, local copies, waits for them, and re-layouts  18.2 us
    dot_general x1, matrix products, on_device(): jnp.einsum('akq,qy->aky', spec_phase_im, cosine, preferred_element_type=j...  17.1 us
    dot_general x1, matrix products, on_device(): jnp.einsum('aysk,syq->akq', imag_part, col_sin, preferred_element_type=jn...  17 us
    dot_general x1, matrix products, on_device(): jnp.einsum('aysk,syq->akq', imag_part, col_cos, preferred_element_type=jn...  17 us
    dot_general x1, matrix products, on_device(): jnp.einsum('akq,qy->aky', spec_phase_re, sine, preferred_element_type=jnp...  17 us
  transfers between devices with their start and end apart: 8, of which 6 were waited for; matrix products, arithmetic and copies ran while one was open for 28% of the time, Pallas kernels for 0%

commit v1 on v0

v1 whole, which is shorter than its diff:
```python
import math

import jax
import jax.numpy as jnp
import numpy as np
from jax import lax
from jax.sharding import PartitionSpec as P

absorb_ratio = 0.1
regularizer = 0.05


def hartley(length):
    index = np.arange(length)
    turned = (index[:, None] * index[None, :] % length) * (2.0 * math.pi / length)
    table = (np.cos(turned) + np.sin(turned)) / math.sqrt(length)
    return table.astype(jnp.bfloat16)


def signed_square(index, length):
    signed = jnp.where(index < length // 2, index, index - length).astype(jnp.float32)
    return signed * signed / float(length * length)


def filters(propagation, rows_sq, cols_sq):
    first = propagation[:, None] * rows_sq[None]
    second = propagation[:, None] * cols_sq[None]
    sin_b, cos_b = jnp.sin(second), jnp.cos(second)
    with_sin = 2.0 * (cos_b - absorb_ratio * sin_b)
    with_cos = 2.0 * (sin_b + absorb_ratio * cos_b)
    transfer = (
        jnp.sin(first)[:, :, None] * with_sin[:, None, :]
        + jnp.cos(first)[:, :, None] * with_cos[:, None, :]
    )
    denom = jnp.sum(transfer * transfer, axis=0) + regularizer
    return transfer / denom


def on_device(holograms, propagation, weights, angle_order, slab_rows):
    mbatch, angles, dist_dev, rows_dev, width = holograms.shape
    groups = lax.axis_size("rows")
    cores = lax.axis_size("dist")
    capacity = 2 * rows_dev
    own = angles // cores
    cols = width // groups
    dists = dist_dev * cores
    device = lax.axis_index("rows")
    table = jnp.asarray(hartley(width))
    index = jnp.arange(width, dtype=jnp.int32)
    my_cols = device * cols + jnp.arange(cols, dtype=jnp.int32)
    gain = filters(propagation, signed_square(my_cols, width), signed_square(index, width))

    mine = lax.all_to_all(holograms[0], "dist", split_axis=0, concat_axis=1, tiled=True)
    flat = mine.reshape(own * dists * rows_dev, width)
    spec = jnp.einsum("kx,mx->km", table, flat, preferred_element_type=jnp.float32)
    spec = spec.astype(jnp.bfloat16).reshape(groups, cols, own * dists * rows_dev)
    spec = lax.all_to_all(spec, "rows", split_axis=0, concat_axis=0, tiled=True)
    spec = spec.reshape(groups, cols, own, dists, rows_dev).transpose(1, 2, 3, 0, 4)
    spec = spec.reshape(cols * own * dists, width)
    full = jnp.dot(spec, table, preferred_element_type=jnp.float32)
    full = full.reshape(cols, own, dists, width)
    full = jnp.sum(full * gain.transpose(1, 0, 2)[:, None], axis=2).astype(jnp.bfloat16)
    half = jnp.einsum("yq,akq->yak", table, full.transpose(1, 0, 2), preferred_element_type=jnp.float32)
    half = half.astype(jnp.bfloat16).reshape(groups, rows_dev, own * cols)
    half = lax.all_to_all(half, "rows", split_axis=0, concat_axis=0, tiled=True)
    half = half.reshape(groups, rows_dev, own, cols).transpose(2, 1, 0, 3)
    half = half.reshape(own * rows_dev, width)
    phase = jnp.dot(half, table, preferred_element_type=jnp.float32)
    phase = phase.astype(jnp.bfloat16).reshape(own, rows_dev, width)
    phase = lax.all_gather(phase, "dist", axis=0, tiled=True)
    place = (angle_order[0][None, :] == jnp.arange(angles)[:, None]).astype(jnp.bfloat16)
    phase = jnp.einsum("wa,ayx->wyx", place, phase, preferred_element_type=jnp.float32)
    recon = jnp.einsum(
        "wyx,wxp->yp",
        phase.astype(jnp.bfloat16),
        weights,
        preferred_element_type=jnp.float32,
    ).astype(jnp.bfloat16)
    parity = device % 2
    offset = parity * slab_rows[device - parity]
    count = slab_rows[device]
    pairs = [(source, source ^ 1) for source in range(groups)]
    partner = lax.ppermute(recon, "rows", pairs)
    lower = jnp.where(parity == 1, partner, recon)
    upper = jnp.where(parity == 1, recon, partner)
    paired = jnp.concatenate([lower, upper], axis=0)
    slot = jnp.arange(capacity, dtype=jnp.int32)[:, None]
    source = jnp.arange(capacity, dtype=jnp.int32)[None, :]
    select = ((source == offset + slot) & (slot < count)).astype(jnp.bfloat16)
    return jnp.dot(select, paired, preferred_element_type=jnp.float32).astype(jnp.bfloat16)


def solution(mesh):
    return jax.shard_map(
        on_device,
        mesh=mesh,
        in_specs=(P(None, None, "dist", "rows", None), P(), P(None, None, "dist"), P(), P()),
        out_specs=P("rows", "dist"),
        check_vma=False,
    )
```

time: 337 us -> 79.1 us (0.23); the launches traced: 331 us -> 78.7 us
  matrix products: 210 us -> 8.73 us
  local copies, waits for them, and re-layouts: 34.6 us -> 10.3 us
  starting transfers between devices: 30.2 us -> 16 us
  between operations: 14.5 us -> 0.98 us
  blocking collectives: 0 us -> 8.13 us
  waiting for transfers between devices: 36.7 us -> 31.9 us
    dot_general x14 -> x7, matrix products: 210 us -> 8.73 us  [the longest x1 3.02 us: on_device(): full = jnp.dot(spec, table, preferred_element_type=jnp.float32)]
    unnamed x22 -> x16, local copies, waits for them, and re-layouts: 18.2 us -> 0.04 us
    all_to_all x4 -> x2, starting transfers between devices: 28.4 us -> 14.5 us  [the longest x1 8.44 us: on_device(): spec = lax.all_to_all(spec, 'rows', split_axis=0, concat_axis=0, tiled=True)]
    all_to_all x4 -> x2, waiting for transfers between devices: 21.7 us -> 29.8 us  [the longest x1 22.7 us: on_device(): spec = lax.all_to_all(spec, 'rows', split_axis=0, concat_axis=0, tiled=True)]
    reduce_scatter x2 -> x0, waiting for transfers between devices: 7.56 us -> none  [the longest x1 7.54 us: on_device(): lax.psum_scatter(numer_re.astype(jnp.bfloat16), 'dist', scatter_dimension...]
    all_to_all x0 -> x1, blocking collectives: none -> 5.81 us  [on_device(): lax.all_to_all(holograms[0], 'dist', split_axis=0, concat_axis=1, tiled=T...]
    gather x1 -> x0, local copies, waits for them, and re-layouts: 4.95 us -> none  [on_device(): chosen = weights[0 + angle_order[0]]]
    all_to_all x4 -> x1, local copies, waits for them, and re-layouts: 3.87 us -> 0.08 us  [on_device(): lax.all_to_all(holograms[0], 'dist', split_axis=0, concat_axis=1, tiled=T...]
  transfers between devices with their start and end apart: 8 -> 3, of which waited for: 6 -> 3; matrix products, arithmetic and copies ran while one was open for 28% -> 4% of each run, Pallas kernels for 0% -> 0%
where the time goes in v1:
time: 79.1 us; the launch traced here: 78.7 us
  waiting for transfers between devices  31.9 us (40%)
  starting transfers between devices  16 us (20%)
  local copies, waits for them, and re-layouts  10.3 us (13%)
  matrix products  8.73 us (11%)
  blocking collectives  8.13 us (10%)
  other arithmetic  2.58 us (3%)
  between operations  0.98 us (1%)
    all_to_all x1, waiting for transfers between devices, on_device(): spec = lax.all_to_all(spec, 'rows', split_axis=0, concat_axis=0, tiled=True)  22.7 us
    all_to_all x1, starting transfers between devices, on_device(): spec = lax.all_to_all(spec, 'rows', split_axis=0, concat_axis=0, tiled=True)  8.44 us
    all_to_all x1, waiting for transfers between devices, on_device(): half = lax.all_to_all(half, 'rows', split_axis=0, concat_axis=0, tiled=True)  7.1 us
    all_to_all x1, starting transfers between devices, on_device(): half = lax.all_to_all(half, 'rows', split_axis=0, concat_axis=0, tiled=True)  6.08 us
    all_to_all x1, blocking collectives, on_device(): lax.all_to_all(holograms[0], 'dist', split_axis=0, concat_axis=1, tiled=T...  5.81 us
    dot_general x1, local copies, waits for them, and re-layouts, on_device(): full = jnp.dot(spec, table, preferred_element_type=jnp.float32)  3.32 us
    dot_general x1, matrix products, on_device(): full = jnp.dot(spec, table, preferred_element_type=jnp.float32)  3.02 us
    transpose x1, local copies, waits for them, and re-layouts, on_device(): spec.reshape(groups, cols, own, dists, rows_dev).transpose(1, 2, 3, 0, 4)  2.68 us
  transfers between devices with their start and end apart: 3, of which 3 were waited for; matrix products, arithmetic and copies ran while one was open for 4% of the time, Pallas kernels for 0%

profile of v1, /device:TPU:0, one launch (start us, length us, event | category | flops | bytes accessed | tf_op | source)
XLA Modules:
  0.0 78.7 jit_solution(11795058131678964568)
XLA Ops:
  0.0 0.0 copy-start.1
  0.0 5.8 %all_to_all.25 = bf16[4,2,64,1024]{3,2,1,0:T(8,128)(2,1)S(1)} all-to-all(bf16[4,2,64,1024]{3,2,1,0:T(8,128)(2,1)} %bitcast.50), channel_id=1, replica_groups=mesh['dist'=2,'rows'=16] {'dist'}, dimensions={0} | all-to-all | bytes 2097152 | tf_op jit(solution)/shard_map/all_to_all | solution.py:53
  5.8 0.1 copy.19
  5.9 0.0 copy-done.1
  5.9 2.3 %convolution_convert_fusion = bf16[1024,512]{1,0:T(8,128)(2,1)} fusion(bf16[1024,1024]{1,0:T(8,128)(2,1)S(1)} %copy-done.1, bf16[512,1024]{1,0:T(8,128)(2,1)S(1)} %bitcast.51), kind=kOutput, calls=%fused_computation.1 | convolution fusion | flops 1074266112 | bytes 4194304 | tf_op jit(solution)/shard_map/kx,mx->km/dot_general | solution.py:55
  8.2 0.0 copy-start.5
  8.2 8.4 %all-to-all-start.1 = ((bf16[16,64,512]{2,1,0:T(8,128)(2,1)}), bf16[16,64,512]{2,1,0:T(8,128)(2,1)S(1)}, u32[]{:S(2)}, u32[]{:S(2)}) async-start(bf16[16,64,512]{2,1,0:T(8,128)(2,1)} %bitcast.8), calls=%async_computation.1 | async-start | bytes 2097152 | tf_op jit(solution)/shard_map/all_to_all | solution.py:57
  16.7 0.0 copy-done.5
  16.7 0.1 multiply_sine_fusion.1
  16.8 0.2 fusion.15
  17.0 0.2 multiply_reduce_fusion.1
  17.2 0.1 multiply_sine_fusion.2
  17.4 1.2 %add_divide_fusion = f32[64,4,1024]{2,0,1:T(8,128)} fusion(f32[64,1024]{1,0:T(8,128)S(1)} %broadcast_add_fusion, f32[4,1024]{1,0:T(4,128)S(1)} %get-tuple-element.8, f32[64,4]{0,1:T(4,128)S(1)} %get-tuple-element.10, f32[4,1024]{1,0:T(4,128)S(1)} %get-tuple-element.7, f32[64,4]{0,1:T(4,128)S(1)} %get-tuple-element.9), kind=kLoop, calls=%fused_computation.10 | loop fusion | flops 1048576 | bytes 1345536 | tf_op jit(solution)/shard_map/div | solution.py:36
  18.6 22.7 %all-to-all-done.1 = bf16[16,64,512]{2,1,0:T(8,128)(2,1)S(1)} async-done(((bf16[16,64,512]{2,1,0:T(8,128)(2,1)}), bf16[16,64,512]{2,1,0:T(8,128)(2,1)S(1)}, u32[]{:S(2)}, u32[]{:S(2)}) %all-to-all-start.1) | async-done | bytes 1048608 | tf_op jit(solution)/shard_map/all_to_all | solution.py:57
  41.3 1.1 %reshape.174 = bf16[16,64,2,4,64]{4,3,2,1,0:T(4,128)(2,1)S(1)} reshape(bf16[16,64,512]{2,1,0:T(8,128)(2,1)S(1)} %all-to-all-done.1) | data formatting | bytes 2097152 | tf_op jit(solution)/shard_map/reshape | solution.py:58
  42.3 2.7 %copy.20 = bf16[64,2,4,16,64]{4,3,0,2,1:T(8,128)(2,1)} copy(bf16[64,2,4,16,64]{4,2,1,0,3:T(4,128)(2,1)S(1)} %bitcast.46) | data formatting | bytes 2097152 | tf_op jit(solution)/shard_map/transpose | solution.py:58
  45.0 0.0 copy-start.4
  45.0 3.3 %dot_general.24 = bf16[64,2,4,1024]{3,0,2,1:T(8,128)(2,1)S(1)} reshape(bf16[64,2,4,16,64]{4,3,0,2,1:T(8,128)(2,1)} %copy.20) | data formatting | bytes 2097152 | tf_op jit(solution)/shard_map/dot_general | solution.py:60
  48.4 0.0 copy-done.4
  48.4 0.0 copy-start.3
  48.4 3.0 %multiply_reduce_fusion = bf16[64,2,1024]{2,0,1:T(8,128)(2,1)S(1)} fusion(bf16[64,2,4,1024]{3,0,2,1:T(8,128)(2,1)S(1)} %dot_general.24, bf16[1024,1024,1,1]{1,0,3,2:T(8,128)(2,1)} %constant.47, f32[64,4,1024]{2,0,1:T(8,128)S(1)} %copy-done.4), kind=kOutput, calls=%fused_computation | convolution fusion | flops 1074659328 | bytes 4456448 | tf_op jit(solution)/shard_map/dot_general | solution.py:60
  51.4 0.0 copy-done.3
  51.4 0.0 copy-start.6
  51.4 0.8 %fusion = bf16[1024,2,64]{0,2,1:T(8,128)(2,1)S(1)} fusion(bf16[1024,1024,1]{1,0,2:T(8,128)(2,1)S(1)} %copy-done.3, bf16[64,2,1024]{2,0,1:T(8,128)(2,1)S(1)} %multiply_reduce_fusion), kind=kOutput, calls=%fused_computation.5 | convolution fusion | flops 268566528 | bytes 2621440 | tf_op jit(solution)/shard_map/yq,akq->yak/dot_general | solution.py:63
  52.3 0.3 reshape.175
  52.6 0.0 copy-start.2
  52.6 1.1 %copy.21 = bf16[16,64,128]{2,1,0:T(8,128)(2,1)} copy(bf16[16,64,128]{1,0,2:T(8,128)(2,1)S(1)} %reshape.175) | data formatting | bytes 524288 | tf_op jit(solution)/shard_map/reshape | solution.py:64
  53.8 6.1 %all-to-all-start.2 = ((bf16[16,64,128]{2,1,0:T(8,128)(2,1)}), bf16[16,64,128]{2,1,0:T(8,128)(2,1)S(1)}, u32[]{:S(2)}, u32[]{:S(2)}) async-start(bf16[16,64,128]{2,1,0:T(8,128)(2,1)} %copy.21), calls=%async_computation.2 | async-start | bytes 524288 | tf_op jit(solution)/shard_map/all_to_all | solution.py:65
  59.9 0.0 copy-done.6
  59.9 0.7 fusion.27
  61.3 7.1 %all-to-all-done.2 = bf16[16,64,128]{2,1,0:T(8,128)(2,1)S(1)} async-done(((bf16[16,64,128]{2,1,0:T(8,128)(2,1)}), bf16[16,64,128]{2,1,0:T(8,128)(2,1)S(1)}, u32[]{:S(2)}, u32[]{:S(2)}) %all-to-all-start.2) | async-done | bytes 262176 | tf_op jit(solution)/shard_map/all_to_all | solution.py:65
  68.4 0.2 reshape.176
  68.6 0.3 copy.31
  69.0 0.0 copy-start.7
  69.0 0.3 reshape.177
  69.4 0.0 copy-done.2
  69.4 0.0 copy-start
  69.4 0.5 convolution_convert_fusion.2
  69.8 2.3 %all_gather.3 = bf16[4,64,1024]{2,1,0:T(8,128)(2,1)S(1)} all-gather(bf16[2,64,1024]{2,1,0:T(8,128)(2,1)S(1)} %bitcast.49), channel_id=1, replica_groups=mesh['dist'=2,'rows'=16] {'dist'}, dimensions={0}, use_global_device_ids=true | all-gather | bytes 786432 | tf_op jit(solution)/shard_map/all_gather | solution.py:70
  72.2 0.0 copy-done.7
  72.2 0.5 convolution_convert_fusion.1
  72.7 0.0 copy-done
  72.7 0.8 fusion.1
  73.4 1.5 %collective-permute-start = (bf16[64,512]{1,0:T(8,128)(2,1)S(1)}, bf16[64,512]{1,0:T(8,128)(2,1)S(1)}, u32[]{:S(2)}, u32[]{:S(2)}) collective-permute-start(bf16[64,512]{1,0:T(8,128)(2,1)S(1)} %fusion.1), channel_id=1, source_target_pairs={{0,1},{1,0},{2,3},{3,2},{4,5},{5,4},{6,7},{7,6},{8,9},{9,8},{10,11... | collective-permute-start | bytes 196616 | tf_op jit(solution)/shard_map/ppermute | solution.py:83
  75.0 0.6 iota_compare_fusion.2
  75.6 2.2 %collective-permute-done = bf16[64,512]{1,0:T(8,128)(2,1)S(1)} collective-permute-done((bf16[64,512]{1,0:T(8,128)(2,1)S(1)}, bf16[64,512]{1,0:T(8,128)(2,1)S(1)}, u32[]{:S(2)}, u32[]{:S(2)}) %collective-permute-start) | collective-permute-done | bytes 65568 | tf_op jit(solution)/shard_map/ppermute | solution.py:83
  77.8 0.9 %convolution_convert_fusion.4 = bf16[128,512]{1,0:T(8,128)(2,1)} fusion(bf16[64,512]{1,0:T(8,128)(2,1)S(1)} %get-tuple-element.6, bf16[64,512]{1,0:T(8,128)(2,1)S(1)} %get-tuple-element.5, s32[128]{0:T(128)S(1)} %iota_add_fusion, pred[128]{0:T(512)(128)(4,1)S(1)} %iota_compare_fusion.2), kind=kOutput, calls=%fused_computation.6 | convolution fusion | flops 17137664 | bytes 262784 | tf_op jit(solution)/shard_map/dot_general | solution.py:90
  (5 shorter events, 0.1 us)
Async XLA Ops:
  0.0 5.9 %copy-start.1 = (bf16[1024,1024]{1,0:T(8,128)(2,1)S(1)}, bf16[1024,1024]{1,0:T(8,128)(2,1)}, u32[]{:S(2)}) copy-start(bf16[1024,1024]{1,0:T(8,128)(2,1)} %constant.46.clone) | copy-start | bytes 6291460
  8.2 8.5 %copy-start.5 = (f32[4]{0:T(128)S(1)}, f32[4]{0:T(128)}, u32[]{:S(2)}) copy-start(f32[4]{0:T(128)} %param.7) | copy-start | bytes 52
  8.2 33.1 %all-to-all-start.1 = ((bf16[16,64,512]{2,1,0:T(8,128)(2,1)}), bf16[16,64,512]{2,1,0:T(8,128)(2,1)S(1)}, u32[]{:S(2)}, u32[]{:S(2)}) async-start(bf16[16,64,512]{2,1,0:T(8,128)(2,1)} %bitcast.8), calls=%async_computation.1 | async-start | bytes 2097152 | tf_op jit(solution)/shard_map/all_to_all | solution.py:57
  45.0 3.3 %copy-start.4 = (f32[64,4,1024]{2,0,1:T(8,128)S(1)}, f32[64,4,1024]{2,0,1:T(8,128)}, u32[]{:S(2)}) copy-start(f32[64,4,1024]{2,0,1:T(8,128)} %add_divide_fusion) | copy-start | bytes 3145732
  48.4 3.0 %copy-start.3 = (bf16[1024,1024,1]{1,0,2:T(8,128)(2,1)S(1)}, bf16[1024,1024,1]{1,0,2:T(8,128)(2,1)}, u32[]{:S(2)}) copy-start(bf16[1024,1024,1]{1,0,2:T(8,128)(2,1)} %constant.48) | copy-start | bytes 6291460
  51.4 8.5 %copy-start.6 = (s32[16]{0:T(128)S(1)}, s32[16]{0:T(128)}, u32[]{:S(2)}) copy-start(s32[16]{0:T(128)} %param.10) | copy-start | bytes 196
  52.6 16.7 %copy-start.2 = (bf16[1024,1024]{1,0:T(8,128)(2,1)S(1)}, bf16[1024,1024]{1,0:T(8,128)(2,1)}, u32[]{:S(2)}) copy-start(bf16[1024,1024]{1,0:T(8,128)(2,1)} %constant.46.clone) | copy-start | bytes 6291460
  53.8 14.6 %all-to-all-start.2 = ((bf16[16,64,128]{2,1,0:T(8,128)(2,1)}), bf16[16,64,128]{2,1,0:T(8,128)(2,1)S(1)}, u32[]{:S(2)}, u32[]{:S(2)}) async-start(bf16[16,64,128]{2,1,0:T(8,128)(2,1)} %copy.21), calls=%async_computation.2 | async-start | bytes 524288 | tf_op jit(solution)/shard_map/all_to_all | solution.py:65
  69.0 3.2 %copy-start.7 = (s32[1,4]{1,0:T(1,128)S(1)}, s32[1,4]{1,0:T(1,128)}, u32[]{:S(2)}) copy-start(s32[1,4]{1,0:T(1,128)} %param.9) | copy-start | bytes 52
  69.4 3.3 %copy-start = (bf16[4,1024,512]{2,1,0:T(8,128)(2,1)S(1)}, bf16[4,1024,512]{2,1,0:T(8,128)(2,1)}, u32[]{:S(2)}) copy-start(bf16[4,1024,512]{2,1,0:T(8,128)(2,1)} %param.8) | copy-start | bytes 12582916
  73.4 4.3 %collective-permute-start = (bf16[64,512]{1,0:T(8,128)(2,1)S(1)}, bf16[64,512]{1,0:T(8,128)(2,1)S(1)}, u32[]{:S(2)}, u32[]{:S(2)}) collective-permute-start(bf16[64,512]{1,0:T(8,128)(2,1)S(1)} %fusion.1), channel_id=1, source_target_pairs={{0,1},{1,0},{2,3},{3,2},{4,5},{5,4},{6,7},{7,6},{8,9},{9,8},{10,11... | collective-permute-start | bytes 196616 | tf_op jit(solution)/shard_map/ppermute | solution.py:83

commit v2 on v1

v2 whole, which is shorter than its diff:
```python
import math

import jax
import jax.numpy as jnp
import numpy as np
from jax import lax
from jax.experimental import pallas as pl
from jax.experimental.pallas import tpu as pltpu
from jax.sharding import PartitionSpec as P

absorb_ratio = 0.1
regularizer = 0.05
bf16 = jnp.bfloat16
f32 = jnp.float32


def hartley(length):
    index = np.arange(length)
    turned = (index[:, None] * index[None, :] % length) * (2.0 * math.pi / length)
    table = (np.cos(turned) + np.sin(turned)) / math.sqrt(length)
    return table.astype(bf16)


def signed_square(index, length):
    signed = jnp.where(index < length // 2, index, index - length).astype(f32)
    return signed * signed / float(length * length)


def filters(propagation, rows_sq, cols_sq):
    first = propagation[:, None] * rows_sq[None]
    second = propagation[:, None] * cols_sq[None]
    sin_b, cos_b = jnp.sin(second), jnp.cos(second)
    with_sin = 2.0 * (cos_b - absorb_ratio * sin_b)
    with_cos = 2.0 * (sin_b + absorb_ratio * cos_b)
    transfer = (
        jnp.sin(first)[:, :, None] * with_sin[:, None, :]
        + jnp.cos(first)[:, :, None] * with_cos[:, None, :]
    )
    denom = jnp.sum(transfer * transfer, axis=0) + regularizer
    return transfer / denom


def flat_plan(holograms, propagation, weights, angle_order, slab_rows):
    mbatch, angles, dist_dev, rows_dev, width = holograms.shape
    groups = lax.axis_size("rows")
    cores = lax.axis_size("dist")
    capacity = 2 * rows_dev
    own = angles // cores
    cols = width // groups
    dists = dist_dev * cores
    device = lax.axis_index("rows")
    table = jnp.asarray(hartley(width))
    index = jnp.arange(width, dtype=jnp.int32)
    my_cols = device * cols + jnp.arange(cols, dtype=jnp.int32)
    gain = filters(propagation, signed_square(my_cols, width), signed_square(index, width))

    mine = lax.all_to_all(holograms[0], "dist", split_axis=0, concat_axis=1, tiled=True)
    flat = mine.reshape(own * dists * rows_dev, width)
    spec = jnp.einsum("kx,mx->km", table, flat, preferred_element_type=f32)
    spec = spec.astype(bf16).reshape(groups, cols, own * dists * rows_dev)
    spec = lax.all_to_all(spec, "rows", split_axis=0, concat_axis=0, tiled=True)
    spec = spec.reshape(groups, cols, own, dists, rows_dev).transpose(1, 2, 3, 0, 4)
    spec = spec.reshape(cols * own * dists, width)
    full = jnp.dot(spec, table, preferred_element_type=f32)
    full = full.reshape(cols, own, dists, width)
    full = jnp.sum(full * gain.transpose(1, 0, 2)[:, None], axis=2).astype(bf16)
    half = jnp.einsum("yq,akq->yak", table, full.transpose(1, 0, 2), preferred_element_type=f32)
    half = half.astype(bf16).reshape(groups, rows_dev, own * cols)
    half = lax.all_to_all(half, "rows", split_axis=0, concat_axis=0, tiled=True)
    half = half.reshape(groups, rows_dev, own, cols).transpose(2, 1, 0, 3)
    half = half.reshape(own * rows_dev, width)
    phase = jnp.dot(half, table, preferred_element_type=f32)
    phase = phase.astype(bf16).reshape(own, rows_dev, width)
    phase = lax.all_gather(phase, "dist", axis=0, tiled=True)
    place = (angle_order[0][None, :] == jnp.arange(angles)[:, None]).astype(bf16)
    phase = jnp.einsum("wa,ayx->wyx", place, phase, preferred_element_type=f32)
    recon = jnp.einsum(
        "wyx,wxp->yp", phase.astype(bf16), weights, preferred_element_type=f32
    ).astype(bf16)
    parity = device % 2
    offset = parity * slab_rows[device - parity]
    count = slab_rows[device]
    pairs = [(source, source ^ 1) for source in range(groups)]
    partner = lax.ppermute(recon, "rows", pairs)
    lower = jnp.where(parity == 1, partner, recon)
    upper = jnp.where(parity == 1, recon, partner)
    paired = jnp.concatenate([lower, upper], axis=0)
    slot = jnp.arange(capacity, dtype=jnp.int32)[:, None]
    source = jnp.arange(capacity, dtype=jnp.int32)[None, :]
    select = ((source == offset + slot) & (slot < count)).astype(bf16)
    return jnp.dot(select, paired, preferred_element_type=f32).astype(bf16)


def row_kernel(inner, cores, own, chunk, place, holo, table, *outs):
    core, spot = place[0], place[1]
    block = table.shape[1] // inner
    dist_dev, rows_dev, width = holo.shape[1:]
    for rel in range(inner):
        start = pl.multiple_of((spot ^ rel) * block, block)
        part = table[:, pl.ds(start, block)]
        for other in range(cores):
            angle = (core ^ other) * own + chunk
            flat = holo[angle].reshape(dist_dev * rows_dev, width)
            got = jnp.dot(flat, part, preferred_element_type=f32)
            outs[rel * cores + other][...] = got.astype(bf16).reshape(dist_dev, rows_dev, block)


def column_kernel(inner, cores, outer, place, table, gain, *refs):
    pieces = refs[: inner * cores]
    out, first, last, stack, total, spectrum = refs[inner * cores :]
    spot, plane = place[1], place[2]
    dist_dev, rows_dev, block = pieces[0].shape
    depth = inner * rows_dev
    for rel in range(inner):
        start = pl.multiple_of((spot ^ rel) * rows_dev, rows_dev)
        for other in range(cores):
            for d in range(dist_dev):
                stack[other * dist_dev + d, pl.ds(start, rows_dev), :] = pieces[rel * cores + other][d]
    part = table[:, pl.ds(pl.multiple_of(plane * depth, depth), depth)]
    for d in range(cores * dist_dev):
        got = jnp.dot(part, stack[d], preferred_element_type=f32) * gain[d].astype(f32)
        if d == 0:
            total[...] = got
        else:
            total[...] += got
    spectrum[...] = total[...].astype(bf16)
    for z in range(outer):
        got = jnp.dot(
            table[z * depth : (z + 1) * depth, :], spectrum[...], preferred_element_type=f32
        ).astype(bf16)
        out[z] = got
        if z == 0:
            first[...] = got
        if z == outer - 1:
            last[...] = got


def recon_kernel(inner, cores, own, place, order, slabs, weights, *refs):
    halves = refs[: cores * own]
    outs = refs[cores * own :]
    core, spot, plane = place[0], place[1], place[2]
    depth, block = halves[0].shape
    capacity = 2 * depth // inner
    rows_dev = depth // inner
    joined = jnp.concatenate([half[...] for half in halves], axis=1)
    stacked = jnp.concatenate(
        [
            weights[order[0, (core ^ other) * own + chunk]]
            for other in range(cores)
            for chunk in range(own)
        ],
        axis=0,
    )
    slot = lax.broadcasted_iota(jnp.int32, (capacity, depth), 0)
    source = lax.broadcasted_iota(jnp.int32, (capacity, depth), 1)
    for rel in range(inner):
        there = spot ^ rel
        parity = there % 2
        owner = plane * inner + there
        offset = (there - parity) * rows_dev + parity * slabs[owner - parity]
        select = (source == slot + offset) & (slot < slabs[owner])
        select = jnp.where(select, 1.0, 0.0).astype(bf16)
        rows = jnp.dot(select, joined, preferred_element_type=f32).astype(bf16)
        got = jnp.dot(rows, stacked, preferred_element_type=f32)
        outs[rel][...] = got.astype(outs[rel].dtype)


def vmem(count):
    return [pl.BlockSpec(memory_space=pltpu.VMEM)] * count


def smem(count):
    return [pl.BlockSpec(memory_space=pltpu.SMEM)] * count


def plane_plan(inner, holograms, propagation, weights, angle_order, slab_rows):
    mbatch, angles, dist_dev, rows_dev, width = holograms.shape
    groups = lax.axis_size("rows")
    cores = lax.axis_size("dist")
    outer = groups // inner
    own = angles // cores
    block = width // inner
    depth = inner * rows_dev
    dists = cores * dist_dev
    pixels = weights.shape[2]
    capacity = 2 * rows_dev
    params = pltpu.CompilerParams(vmem_limit_bytes=40 * 2**20)

    device = lax.axis_index("rows")
    core = lax.axis_index("dist")
    plane, spot = device // inner, device % inner
    place = jnp.stack([core, spot, plane]).astype(jnp.int32)
    table = jnp.asarray(hartley(width))

    def sent(value, rel, other):
        if rel == 0 and other == 0:
            return value
        pairs = [
            (c * groups + r, (c ^ other) * groups + (r ^ rel))
            for c in range(cores)
            for r in range(groups)
        ]
        return lax.ppermute(value, ("dist", "rows"), pairs)

    arrived = []
    for chunk in range(own):
        pieces = pl.pallas_call(
            lambda *refs, chunk=chunk: row_kernel(inner, cores, own, chunk, *refs),
            out_shape=[jax.ShapeDtypeStruct((dist_dev, rows_dev, block), bf16)] * (inner * cores),
            in_specs=smem(1) + vmem(2),
            out_specs=vmem(inner * cores),
            compiler_params=params,
            cost_estimate=pl.CostEstimate(
                flops=2 * cores * dist_dev * rows_dev * width * width,
                bytes_accessed=2 * width * width + 4 * cores * dist_dev * rows_dev * width,
                transcendentals=0,
            ),
            name="row_spectra",
        )(place, holograms[0], table)
        arrived.append(
            [
                sent(pieces[rel * cores + other], rel, other)
                for rel in range(inner)
                for other in range(cores)
            ]
        )

    index = jnp.arange(width, dtype=jnp.int32)
    my_cols = spot * block + jnp.arange(block, dtype=jnp.int32)
    ordered = jnp.concatenate(
        [
            lax.dynamic_slice_in_dim(propagation, (core ^ other) * dist_dev, dist_dev, 0)
            for other in range(cores)
        ]
    )
    gain = filters(ordered, signed_square(index, width), signed_square(my_cols, width)).astype(bf16)

    my_table = lax.dynamic_slice_in_dim(table, spot * block, block, 0)
    turned = jnp.einsum("kx,wxp->wkp", my_table, weights, preferred_element_type=f32).astype(bf16)

    halves = []
    for chunk in range(own):
        parts, low, high = pl.pallas_call(
            lambda *refs: column_kernel(inner, cores, outer, *refs),
            out_shape=[jax.ShapeDtypeStruct((outer, depth, block), bf16)]
            + [jax.ShapeDtypeStruct((depth, block), bf16)] * 2,
            in_specs=smem(1) + vmem(2 + inner * cores),
            out_specs=vmem(3),
            scratch_shapes=[
                pltpu.VMEM((dists, depth, block), bf16),
                pltpu.VMEM((width, block), f32),
                pltpu.VMEM((width, block), bf16),
            ],
            compiler_params=params,
            cost_estimate=pl.CostEstimate(
                flops=2 * width * block * (dists * depth + width),
                bytes_accessed=2 * width * width + 2 * dists * width * block,
                transcendentals=0,
            ),
            name="columns",
        )(place, table, gain, *arrived[chunk])
        up = down = None
        for step in range(1, outer):
            if step == 1:
                to_up, to_down = high, low
            else:
                to_up = lax.dynamic_index_in_dim(parts, outer - step + plane, 0, False) + up
                to_down = lax.dynamic_index_in_dim(parts, step - outer + plane, 0, False) + down
            up_pairs = [
                (z * inner + i, (z + 1) * inner + i)
                for z in range(min(step, outer - 1))
                for i in range(inner)
            ]
            down_pairs = [(groups - 1 - a, groups - 1 - b) for a, b in up_pairs]
            up = lax.ppermute(to_up, "rows", up_pairs)
            down = lax.ppermute(to_down, "rows", down_pairs)
        mine = lax.dynamic_index_in_dim(parts, plane, 0, False).astype(f32)
        halves.append((mine + up.astype(f32) + down.astype(f32)).astype(bf16))
    halves = [sent(half, 0, other) for other in range(cores) for half in halves]

    slabs = pl.pallas_call(
        lambda *refs: recon_kernel(inner, cores, own, *refs),
        out_shape=[jax.ShapeDtypeStruct((capacity, pixels), f32)]
        + [jax.ShapeDtypeStruct((capacity, pixels), bf16)] * (inner - 1),
        in_specs=smem(3) + vmem(1 + cores * own),
        out_specs=vmem(inner),
        compiler_params=params,
        cost_estimate=pl.CostEstimate(
            flops=2 * inner * capacity * angles * block * (depth + pixels),
            bytes_accessed=2 * angles * block * (depth + pixels) + 2 * inner * capacity * pixels,
            transcendentals=0,
        ),
        name="recon_parts",
    )(place, angle_order, slab_rows, turned, *halves)
    total = slabs[0]
    for rel in range(1, inner):
        total = total + sent(slabs[rel], rel, 0).astype(f32)
    return total.astype(bf16)


def on_device(holograms, propagation, weights, angle_order, slab_rows):
    mbatch, angles, dist_dev, rows_dev, width = holograms.shape
    groups = lax.axis_size("rows")
    inner = 2 ** (int(math.log2(groups)) // 2)
    block = width // inner
    fits = (
        inner * (groups // inner) == groups
        and rows_dev % 16 == 0
        and block % 128 == 0
        and inner * rows_dev % 128 == 0
    )
    if fits:
        return plane_plan(inner, holograms, propagation, weights, angle_order, slab_rows)
    return flat_plan(holograms, propagation, weights, angle_order, slab_rows)


def solution(mesh):
    return jax.shard_map(
        on_device,
        mesh=mesh,
        in_specs=(P(None, None, "dist", "rows", None), P(), P(None, None, "dist"), P(), P()),
        out_specs=P("rows", "dist"),
        check_vma=False,
    )
```

time: 79.1 us -> 82.6 us (1.044)
  starting transfers between devices: 16 us -> 42.6 us
  waiting for transfers between devices: 31.9 us -> 15.2 us
  Pallas kernels: 0 us -> 10.3 us
  blocking collectives: 8.13 us -> 0 us
  matrix products: 8.73 us -> 1.28 us
  local copies, waits for them, and re-layouts: 10.3 us -> 7.85 us
  other arithmetic: 2.58 us -> 4.46 us
    ppermute x1 -> x31, starting transfers between devices: 1.5 us -> 42.6 us  [the longest x6 19.5 us: plane_plan(): up = lax.ppermute(to_up, 'rows', up_pairs)]
    all_to_all x2 -> x0, waiting for transfers between devices: 29.8 us -> none  [the longest x1 22.7 us: on_device(): spec = lax.all_to_all(spec, 'rows', split_axis=0, concat_axis=0, tiled=True)]
    all_to_all x2 -> x0, starting transfers between devices: 14.5 us -> none  [the longest x1 8.44 us: on_device(): spec = lax.all_to_all(spec, 'rows', split_axis=0, concat_axis=0, tiled=True)]
    ppermute x1 -> x31, waiting for transfers between devices: 2.17 us -> 15.2 us  [the longest x6 7.51 us: plane_plan(): down = lax.ppermute(to_down, 'rows', down_pairs)]
    pallas_call x0 -> x5, Pallas kernels: none -> 10.3 us  [the longest x2 4.65 us: plane_plan(): pl.pallas_call(lambda *refs: column_kernel(inner, cores, outer, *refs), o...]
    dot_general x7 -> x1, matrix products: 8.73 us -> 1.28 us  [plane_plan(): jnp.einsum('kx,wxp->wkp', my_table, weights, preferred_element_type=f32)]
    unnamed x16 -> x26, local copies, waits for them, and re-layouts: 0.04 us -> 7.04 us
    all_to_all x1 -> x0, blocking collectives: 5.81 us -> none  [on_device(): lax.all_to_all(holograms[0], 'dist', split_axis=0, concat_axis=1, tiled=T...]
  transfers between devices with their start and end apart: 3 -> 31, of which waited for: 3 -> 5; matrix products, arithmetic and copies ran while one was open for 4% -> 7% of each run, Pallas kernels for 0% -> 8%
where the time goes in v2:
time: 82.6 us; the launch traced here: 82.1 us
  starting transfers between devices  42.6 us (52%)
  waiting for transfers between devices  15.2 us (18%)
  Pallas kernels  10.3 us (12%)
  local copies, waits for them, and re-layouts  7.85 us (10%)
  other arithmetic  4.46 us (5%)
  matrix products  1.28 us (2%)
    ppermute x6, starting transfers between devices, plane_plan(): up = lax.ppermute(to_up, 'rows', up_pairs)  19.5 us
    ppermute x19, starting transfers between devices, sent(): return lax.ppermute(value, ('dist', 'rows'), pairs)  17.8 us
    ppermute x6, waiting for transfers between devices, plane_plan(): down = lax.ppermute(to_down, 'rows', down_pairs)  7.51 us
    unnamed x26, local copies, waits for them, and re-layouts  7.04 us
    ppermute x19, waiting for transfers between devices, sent(): return lax.ppermute(value, ('dist', 'rows'), pairs)  6.54 us
    ppermute x6, starting transfers between devices, plane_plan(): down = lax.ppermute(to_down, 'rows', down_pairs)  5.26 us
    pallas_call x2, Pallas kernels, plane_plan(): pl.pallas_call(lambda *refs: column_kernel(inner, cores, outer, *refs), o...  4.65 us
    pallas_call x2, Pallas kernels, plane_plan(): pl.pallas_call(lambda *refs, chunk=chunk: row_kernel(inner, cores, own, c...  3.79 us
  transfers between devices with their start and end apart: 31, of which 5 were waited for; matrix products, arithmetic and copies ran while one was open for 7% of the time, Pallas kernels for 8%

profile of v2, /device:TPU:0, one launch (start us, length us, event | category | flops | bytes accessed | tf_op | source)
XLA Modules:
  0.0 82.1 jit_solution(422725411912670685)
XLA Ops:
  0.0 0.1 pad_add_fusion.refs_0_
  0.1 1.6 %copy-done = bf16[1024,1024]{1,0:T(8,128)(2,1)S(1)} copy-done((bf16[1024,1024]{1,0:T(8,128)(2,1)S(1)}, bf16[1024,1024]{1,0:T(8,128)(2,1)}, u32[]{:S(2)}) %copy-start) | copy-done | bytes 2097176
  1.7 1.2 %copy-done.4 = bf16[1,4,2,64,1024]{4,3,2,1,0:T(8,128)(2,1)S(1)} copy-done((bf16[1,4,2,64,1024]{4,3,2,1,0:T(8,128)(2,1)S(1)}, bf16[1,4,2,64,1024]{4,3,2,1,0:T(8,128)(2,1)}, u32[]{:S(2)}) %copy-start.4) | copy-done | bytes 1048600
  2.9 1.9 %row_spectra.3 = (bf16[2,64,256]{2,1,0:T(8,128)(2,1)S(1)}, bf16[2,64,256]{2,1,0:T(8,128)(2,1)}, bf16[2,64,256]{2,1,0:T(8,128)(2,1)}, bf16[2,64,256]{2,1,0:T(8,12...) custom-call(s32[3]{0:T(128)S(1)} %pad_add_fusion.refs_0_, ...), custom_call_target="tpu_custom_call" | custom-call | flops 536870912 | bytes 3145728 | tf_op jit(solution)/shard_map/row_spectra/pallas_call | solution.py:207
  4.8 0.6 copy-done.7
  5.4 0.4 collective-permute-start.13
  5.8 2.5 %collective-permute-start.14 = (bf16[2,64,256]{2,1,0:T(8,128)(2,1)}, bf16[2,64,256]{2,1,0:T(8,128)(2,1)S(1)}, u32[]{:S(2)}, u32[]{:S(2)}) collective-permute-start(bf16[2,64,256]{2,1,0:T(8,128)(2,1)} %get-tuple-element.44), channel_id=1, source_target_pairs={{0,1},{1,0},{2,3},{3,2},{4,5},{5,4},{6,7},{7,6},{8,9},{9,8},{10,11... | collective-permute-start | bytes 196616 | tf_op jit(solution)/shard_map/ppermute | solution.py:203
  8.3 0.1 collective-permute-start.15
  8.5 1.7 %collective-permute-start.16 = (bf16[2,64,256]{2,1,0:T(8,128)(2,1)}, bf16[2,64,256]{2,1,0:T(8,128)(2,1)S(1)}, u32[]{:S(2)}, u32[]{:S(2)}) collective-permute-start(bf16[2,64,256]{2,1,0:T(8,128)(2,1)} %get-tuple-element.46), channel_id=1, source_target_pairs={{0,2},{1,3},{2,0},{3,1},{4,6},{5,7},{6,4},{7,5},{8,10},{9,11},{10,... | collective-permute-start | bytes 196616 | tf_op jit(solution)/shard_map/ppermute | solution.py:203
  10.2 0.0 collective-permute-start.17
  10.2 0.8 fusion.20
  11.1 0.1 pad_maximum_fusion
  11.1 0.1 fusion.11
  11.3 0.2 multiply_sine_fusion
  11.5 1.5 %multiply_reduce_fusion = f32[1024,256]{1,0:T(8,128)S(1)} fusion(f32[4,256]{1,0:T(4,128)S(1)} %get-tuple-element.64, f32[4,1024]{1,0:T(4,128)S(1)} %get-tuple-element.62, f32[4,256]{1,0:T(4,128)S(1)} %get-tuple-element.63, f32[4,1024]{1,0:T(4,128)S(1)} %get-tuple-element.61), kind=kLoop, calls=%fused_computation.1 | loop fusion | flops 4980736 | bytes 1089536 | tf_op jit(solution)/shard_map/reduce_sum | solution.py:39
  13.0 0.1 broadcast_add_fusion
  13.1 1.9 %row_spectra.2 = (bf16[2,64,256]{2,1,0:T(8,128)(2,1)S(1)}, bf16[2,64,256]{2,1,0:T(8,128)(2,1)S(1)}, bf16[2,64,256]{2,1,0:T(8,128)(2,1)S(1)}, bf16[2,64,256]{2,1,...) custom-call(s32[3]{0:T(128)S(1)} %pad_add_fusion.refs_0_, ...), custom_call_target="tpu_custom_call" | custom-call | flops 536870912 | bytes 3145728 | tf_op jit(solution)/shard_map/row_spectra/pallas_call | solution.py:207
  15.1 0.0 collective-permute-done.13.refs_4_
  15.1 2.5 %collective-permute-start.18 = (bf16[2,64,256]{2,1,0:T(8,128)(2,1)}, bf16[2,64,256]{2,1,0:T(8,128)(2,1)S(1)}, u32[]{:S(2)}, u32[]{:S(2)}) collective-permute-start(bf16[2,64,256]{2,1,0:T(8,128)(2,1)} %copy-done.9), channel_id=1, source_target_pairs={{0,3},{1,2},{2,1},{3,0},{4,7},{5,6},{6,5},{7,4},{8,11},{9,10},{10,... | collective-permute-start | bytes 196616 | tf_op jit(solution)/shard_map/ppermute | solution.py:203
  17.6 0.2 collective-permute-start.19
  17.8 0.3 collective-permute-start
  18.1 1.6 %collective-permute-start.1 = (bf16[2,64,256]{2,1,0:T(8,128)(2,1)S(1)}, bf16[2,64,256]{2,1,0:T(8,128)(2,1)S(1)}, u32[]{:S(2)}, u32[]{:S(2)}) collective-permute-start(bf16[2,64,256]{2,1,0:T(8,128)(2,1)S(1)} %get-tuple-element.33), channel_id=1, source_target_pairs={{0,1},{1,0},{2,3},{3,2},{4,5},{5,4},{6,7},{7,6},{8,9},{9,8},{10,11... | collective-permute-start | bytes 196616 | tf_op jit(solution)/shard_map/ppermute | solution.py:203
  19.7 1.3 %divide_convert_fusion.refs_2_ = bf16[4,1024,256]{2,1,0:T(8,128)(2,1)S(1)} fusion(f32[1024,256]{1,0:T(8,128)S(1)} %broadcast_add_fusion, f32[4,256]{1,0:T(4,128)S(1)} %get-tuple-element.64, f32[4,1024]{1,0:T(4,128)S(1)} %get-tuple-element.62, f32[4,256]{1,0:T(4,128)S(1)} %get-tuple-element.63, f32[4,1024]{1,0:T(4,128)S(1)} %get-tuple-element.61), kind=kLoop, calls=%fused_computation | loop fusion | flops 5242880 | bytes 3186688 | tf_op jit(solution)/shard_map/convert_element_type | solution.py:236
  21.1 0.1 collective-permute-start.2
  21.2 0.0 collective-permute-done.18.refs_9_
  21.2 1.6 %collective-permute-start.3 = (bf16[2,64,256]{2,1,0:T(8,128)(2,1)}, bf16[2,64,256]{2,1,0:T(8,128)(2,1)S(1)}, u32[]{:S(2)}, u32[]{:S(2)}) collective-permute-start(bf16[2,64,256]{2,1,0:T(8,128)(2,1)} %get-tuple-element.35), channel_id=1, source_target_pairs={{0,2},{1,3},{2,0},{3,1},{4,6},{5,7},{6,4},{7,5},{8,10},{9,11},{10,... | collective-permute-start | bytes 196616 | tf_op jit(solution)/shard_map/ppermute | solution.py:203
  22.8 0.7 collective-permute-start.4
  23.5 2.1 %collective-permute-start.5 = (bf16[2,64,256]{2,1,0:T(8,128)(2,1)}, bf16[2,64,256]{2,1,0:T(8,128)(2,1)S(1)}, u32[]{:S(2)}, u32[]{:S(2)}) collective-permute-start(bf16[2,64,256]{2,1,0:T(8,128)(2,1)} %get-tuple-element.37), channel_id=1, source_target_pairs={{0,3},{1,2},{2,1},{3,0},{4,7},{5,6},{6,5},{7,4},{8,11},{9,10},{10,... | collective-permute-start | bytes 196616 | tf_op jit(solution)/shard_map/ppermute | solution.py:203
  25.6 0.2 collective-permute-start.6
  25.8 2.8 %columns.3 = (bf16[4,256,256]{2,1,0:T(8,128)(2,1)S(1)}, bf16[256,256]{1,0:T(8,128)(2,1)S(1)}, bf16[256,256]{1,0:T(8,128)(2,1)}) custom-call(s32[3]{0:T(128)S(1)} %pad_add_fusion.refs_0_, bf16[1024,1024]{1,0:T(8,128)(2,1)S(1)} %copy-done.1, bf16[4,1024,256]{2,1,0:T(8,128)(2,1)S(1)} %divide_convert_fusion.refs_2_, ...), custom_call_target="tpu_custom_call" | custom-call | flops 1073741824 | bytes 4194304 | tf_op jit(solution)/shard_map/columns/pallas_call | solution.py:243
  28.6 1.3 %copy-done.2 = bf16[4,1024,256]{2,1,0:T(8,128)(2,1)} copy-done((bf16[4,1024,256]{2,1,0:T(8,128)(2,1)}, bf16[4,1024,256]{2,1,0:T(8,128)(2,1)S(1)}, u32[]{:S(2)}) %copy-start.2) | copy-done | bytes 2097176
  29.9 0.7 copy-done.6
  30.6 3.5 %collective-permute-start.20 = (bf16[256,256]{1,0:T(8,128)(2,1)}, bf16[256,256]{1,0:T(8,128)(2,1)S(1)}, u32[]{:S(2)}, u32[]{:S(2)}) collective-permute-start(bf16[256,256]{1,0:T(8,128)(2,1)} %get-tuple-element.51), channel_id=1, source_target_pairs={{0,4},{1,5},{2,6},{3,7},{16,20},{17,21},{18,22},{19,23}} | collective-permute-start | bytes 393224 | tf_op jit(solution)/shard_map/ppermute | solution.py:275
  34.1 0.7 collective-permute-start.23
  34.8 1.6 %copy-done.3 = bf16[4,1024,256]{2,1,0:T(8,128)(2,1)S(1)} copy-done((bf16[4,1024,256]{2,1,0:T(8,128)(2,1)S(1)}, bf16[4,1024,256]{2,1,0:T(8,128)(2,1)}, u32[]{:S(2)}) %copy-start.3) | copy-done | bytes 2097176
  36.4 1.8 %columns.2 = (bf16[4,256,256]{2,1,0:T(8,128)(2,1)S(1)}, bf16[256,256]{1,0:T(8,128)(2,1)S(1)}, bf16[256,256]{1,0:T(8,128)(2,1)S(1)}) custom-call(s32[3]{0:T(128)S(1)} %pad_add_fusion.refs_0_, bf16[1024,1024]{1,0:T(8,128)(2,1)S(1)} %copy-done.1, bf16[4,1024,256]{2,1,0:T(8,128)(2,1)S(1)} %copy-done.3, bf16[2,64,256]{2,1,0:T(8,128)(2,1)S(1)} %get-tuple-element.31.refs_3_, ...), custom_call_target="tpu_custom_call" | custom-call | flops 1073741824 | bytes 4194304 | tf_op jit(solution)/shard_map/columns/pallas_call | solution.py:243
  38.3 1.3 %collective-permute-start.7 = (bf16[256,256]{1,0:T(8,128)(2,1)S(1)}, bf16[256,256]{1,0:T(8,128)(2,1)S(1)}, u32[]{:S(2)}, u32[]{:S(2)}) collective-permute-start(bf16[256,256]{1,0:T(8,128)(2,1)S(1)} %get-tuple-element.40), channel_id=1, source_target_pairs={{0,4},{1,5},{2,6},{3,7},{16,20},{17,21},{18,22},{19,23}} | collective-permute-start | bytes 393224 | tf_op jit(solution)/shard_map/ppermute | solution.py:275
  39.6 0.7 collective-permute-start.10
  40.3 2.0 %collective-permute-start.21 = (bf16[256,256]{1,0:T(8,128)(2,1)S(1)}, bf16[256,256]{1,0:T(8,128)(2,1)S(1)}, u32[]{:S(2)}, u32[]{:S(2)}) collective-permute-start(bf16[256,256]{1,0:T(8,128)(2,1)S(1)} %bitcast_add_fusion.2), channel_id=1, source_target_pairs={{0,4},{1,5},{2,6},{3,7},{4,8},{5,9},{6,10},{7,11},{16,20},{17,21},... | collective-permute-start | bytes 393224 | tf_op jit(solution)/shard_map/ppermute | solution.py:275
  42.3 1.1 %collective-permute-done.7 = bf16[256,256]{1,0:T(8,128)(2,1)S(1)} collective-permute-done((bf16[256,256]{1,0:T(8,128)(2,1)S(1)}, bf16[256,256]{1,0:T(8,128)(2,1)S(1)}, u32[]{:S(2)}, u32[]{:S(2)}) %collective-permute-start.7) | collective-permute-done | bytes 131104 | tf_op jit(solution)/shard_map/ppermute | solution.py:275
  43.4 4.4 %collective-permute-start.8 = (bf16[256,256]{1,0:T(8,128)(2,1)S(1)}, bf16[256,256]{1,0:T(8,128)(2,1)S(1)}, u32[]{:S(2)}, u32[]{:S(2)}) collective-permute-start(bf16[256,256]{1,0:T(8,128)(2,1)S(1)} %bitcast_add_fusion.6), channel_id=1, source_target_pairs={{0,4},{1,5},{2,6},{3,7},{4,8},{5,9},{6,10},{7,11},{16,20},{17,21},... | collective-permute-start | bytes 393224 | tf_op jit(solution)/shard_map/ppermute | solution.py:275
  47.9 0.7 collective-permute-start.24
  48.6 3.2 %collective-permute-start.22 = (bf16[256,256]{1,0:T(8,128)(2,1)S(1)}, bf16[256,256]{1,0:T(8,128)(2,1)S(1)}, u32[]{:S(2)}, u32[]{:S(2)}) collective-permute-start(bf16[256,256]{1,0:T(8,128)(2,1)S(1)} %get-tuple-element.57), channel_id=1, source_target_pairs={{0,4},{1,5},{2,6},{3,7},{4,8},{5,9},{6,10},{7,11},{8,12},{9,13},{1... | collective-permute-start | bytes 393224 | tf_op jit(solution)/shard_map/ppermute | solution.py:275
  51.8 0.7 collective-permute-start.11
  52.5 5.2 %collective-permute-start.9 = (bf16[256,256]{1,0:T(8,128)(2,1)S(1)}, bf16[256,256]{1,0:T(8,128)(2,1)S(1)}, u32[]{:S(2)}, u32[]{:S(2)}) collective-permute-start(bf16[256,256]{1,0:T(8,128)(2,1)S(1)} %get-tuple-element.59), channel_id=1, source_target_pairs={{0,4},{1,5},{2,6},{3,7},{4,8},{5,9},{6,10},{7,11},{8,12},{9,13},{1... | collective-permute-start | bytes 393224 | tf_op jit(solution)/shard_map/ppermute | solution.py:275
  57.7 1.3 %collective-permute-start.25 = (bf16[256,256]{1,0:T(8,128)(2,1)S(1)}, bf16[256,256]{1,0:T(8,128)(2,1)S(1)}, u32[]{:S(2)}, u32[]{:S(2)}) collective-permute-start(bf16[256,256]{1,0:T(8,128)(2,1)S(1)} %bitcast_add_fusion.1), channel_id=1, source_target_pairs={{15,11},{14,10},{13,9},{12,8},{11,7},{10,6},{9,5},{8,4},{7,3},{6,2... | collective-permute-start | bytes 393224 | tf_op jit(solution)/shard_map/ppermute | solution.py:276
  59.1 1.3 %collective-permute-start.12 = (bf16[256,256]{1,0:T(8,128)(2,1)S(1)}, bf16[256,256]{1,0:T(8,128)(2,1)S(1)}, u32[]{:S(2)}, u32[]{:S(2)}) collective-permute-start(bf16[256,256]{1,0:T(8,128)(2,1)S(1)} %bitcast_add_fusion.5), channel_id=1, source_target_pairs={{15,11},{14,10},{13,9},{12,8},{11,7},{10,6},{9,5},{8,4},{7,3},{6,2... | collective-permute-start | bytes 393224 | tf_op jit(solution)/shard_map/ppermute | solution.py:276
  60.4 6.2 %collective-permute-done.25 = bf16[256,256]{1,0:T(8,128)(2,1)S(1)} collective-permute-done((bf16[256,256]{1,0:T(8,128)(2,1)S(1)}, bf16[256,256]{1,0:T(8,128)(2,1)S(1)}, u32[]{:S(2)}, u32[]{:S(2)}) %collective-permute-start.25) | collective-permute-done | bytes 131104 | tf_op jit(solution)/shard_map/ppermute | solution.py:276
  66.6 0.1 fusion.4.refs_5_
  66.6 0.1 collective-permute-start.27
  66.7 1.3 %collective-permute-done.12 = bf16[256,256]{1,0:T(8,128)(2,1)S(1)} collective-permute-done((bf16[256,256]{1,0:T(8,128)(2,1)S(1)}, bf16[256,256]{1,0:T(8,128)(2,1)S(1)}, u32[]{:S(2)}, u32[]{:S(2)}) %collective-permute-start.12) | collective-permute-done | bytes 131104 | tf_op jit(solution)/shard_map/ppermute | solution.py:276
  68.0 0.1 fusion.6.refs_4_
  68.1 0.0 copy-start.10
  68.1 0.0 copy-start.11
  68.1 0.1 collective-permute-start.26
  68.2 1.3 %fusion.refs_3_ = bf16[4,256,512]{2,1,0:T(8,128)(2,1)S(1)} fusion(bf16[4,1024,512]{2,1,0:T(8,128)(2,1)S(1)} %copy-done.12, bf16[1024,1024]{1,0:T(8,128)(2,1)S(1)} %copy-done.1, s32[]{:T(128)S(6)} %select_n.59), kind=kOutput, calls=%fused_computation.4 | convolution fusion | flops 1074266112 | bytes 5767172 | tf_op jit(solution)/shard_map/kx,wxp->wkp/dot_general | solution.py:239
  69.5 0.0 collective-permute-done.26.refs_6_
  69.5 1.8 %recon_parts.1 = (f32[128,512]{1,0:T(8,128)S(1)}, bf16[128,512]{1,0:T(8,128)(2,1)S(1)}, bf16[128,512]{1,0:T(8,128)(2,1)S(1)}, bf16[128,512]{1,0:T(8,128)(2,1)S(1)}) custom-call(s32[3]{0:T(128)S(1)} %pad_add_fusion.refs_0_, s32[1,4]{1,0:T(1,128)S(1)} %copy-done.10, s32[16]{0:T(128)S(1)} %copy-done.11, bf16[4,256,512]{2,1,0:T(8,128)(2,1)S(1)} %fusion.refs_3_, ...), custom_call_target="tpu_custom_call" | custom-call | flops 805306368 | bytes 2097152 | tf_op jit(solution)/shard_map/recon_parts/pallas_call | solution.py:281
  71.4 1.6 %collective-permute-start.28 = (bf16[128,512]{1,0:T(8,128)(2,1)S(1)}, bf16[128,512]{1,0:T(8,128)(2,1)S(1)}, u32[]{:S(2)}, u32[]{:S(2)}) collective-permute-start(bf16[128,512]{1,0:T(8,128)(2,1)S(1)} %get-tuple-element.54), channel_id=1, source_target_pairs={{0,1},{1,0},{2,3},{3,2},{4,5},{5,4},{6,7},{7,6},{8,9},{9,8},{10,11... | collective-permute-start | bytes 393224 | tf_op jit(solution)/shard_map/ppermute | solution.py:203
  73.0 1.1 %collective-permute-start.29 = (bf16[128,512]{1,0:T(8,128)(2,1)S(1)}, bf16[128,512]{1,0:T(8,128)(2,1)S(1)}, u32[]{:S(2)}, u32[]{:S(2)}) collective-permute-start(bf16[128,512]{1,0:T(8,128)(2,1)S(1)} %get-tuple-element.55), channel_id=1, source_target_pairs={{0,2},{1,3},{2,0},{3,1},{4,6},{5,7},{6,4},{7,5},{8,10},{9,11},{10,... | collective-permute-start | bytes 393224 | tf_op jit(solution)/shard_map/ppermute | solution.py:203
  74.1 0.9 %collective-permute-start.30 = (bf16[128,512]{1,0:T(8,128)(2,1)S(1)}, bf16[128,512]{1,0:T(8,128)(2,1)S(1)}, u32[]{:S(2)}, u32[]{:S(2)}) collective-permute-start(bf16[128,512]{1,0:T(8,128)(2,1)S(1)} %get-tuple-element.56), channel_id=1, source_target_pairs={{0,3},{1,2},{2,1},{3,0},{4,7},{5,6},{6,5},{7,4},{8,11},{9,10},{10,... | collective-permute-start | bytes 393224 | tf_op jit(solution)/shard_map/ppermute | solution.py:203
  74.9 2.7 %collective-permute-done.28 = bf16[128,512]{1,0:T(8,128)(2,1)S(1)} collective-permute-done((bf16[128,512]{1,0:T(8,128)(2,1)S(1)}, bf16[128,512]{1,0:T(8,128)(2,1)S(1)}, u32[]{:S(2)}, u32[]{:S(2)}) %collective-permute-start.28) | collective-permute-done | bytes 131104 | tf_op jit(solution)/shard_map/ppermute | solution.py:203
  77.6 3.8 %collective-permute-done.29 = bf16[128,512]{1,0:T(8,128)(2,1)S(1)} collective-permute-done((bf16[128,512]{1,0:T(8,128)(2,1)S(1)}, bf16[128,512]{1,0:T(8,128)(2,1)S(1)}, u32[]{:S(2)}, u32[]{:S(2)}) %collective-permute-start.29) | collective-permute-done | bytes 131104 | tf_op jit(solution)/shard_map/ppermute | solution.py:203
  81.4 0.7 add_convert_fusion
  (49 shorter events, 0.3 us)
Async XLA Ops:
  0.1 1.6 %copy-start = (bf16[1024,1024]{1,0:T(8,128)(2,1)S(1)}, bf16[1024,1024]{1,0:T(8,128)(2,1)}, u32[]{:S(2)}) copy-start(bf16[1024,1024]{1,0:T(8,128)(2,1)} %constant.96.clone.refs_2_.refs_1_) | copy-start | bytes 6291460
  1.7 1.2 %copy-start.4 = (bf16[1,4,2,64,1024]{4,3,2,1,0:T(8,128)(2,1)S(1)}, bf16[1,4,2,64,1024]{4,3,2,1,0:T(8,128)(2,1)}, u32[]{:S(2)}) copy-start(bf16[1,4,2,64,1024]{4,3,2,1,0:T(8,128)(2,1)} %param.6) | copy-start | bytes 3145732
  2.9 10.2 %copy-start.1 = (bf16[1024,1024]{1,0:T(8,128)(2,1)S(1)}, bf16[1024,1024]{1,0:T(8,128)(2,1)}, u32[]{:S(2)}) copy-start(bf16[1024,1024]{1,0:T(8,128)(2,1)} %constant.96.clone.refs_2_.refs_1_) | copy-start | bytes 6291460
  2.9 10.2 %copy-start.5 = (bf16[1,4,2,64,1024]{4,3,2,1,0:T(8,128)(2,1)S(1)}, bf16[1,4,2,64,1024]{4,3,2,1,0:T(8,128)(2,1)}, u32[]{:S(2)}) copy-start(bf16[1,4,2,64,1024]{4,3,2,1,0:T(8,128)(2,1)} %param.6) | copy-start | bytes 3145732
  4.8 0.6 copy-start.7
  5.4 7.6 %copy-start.9 = (bf16[2,64,256]{2,1,0:T(8,128)(2,1)}, bf16[2,64,256]{2,1,0:T(8,128)(2,1)S(1)}, u32[]{:S(2)}) copy-start(bf16[2,64,256]{2,1,0:T(8,128)(2,1)S(1)} %get-tuple-element.48) | copy-start | bytes 196612
  5.4 9.7 %collective-permute-start.13 = (bf16[2,64,256]{2,1,0:T(8,128)(2,1)}, bf16[2,64,256]{2,1,0:T(8,128)(2,1)S(1)}, u32[]{:S(2)}, u32[]{:S(2)}) collective-permute-start(bf16[2,64,256]{2,1,0:T(8,128)(2,1)} %get-tuple-element.43), channel_id=1, source_target_pairs={{0,16},{1,17},{2,18},{3,19},{4,20},{5,21},{6,22},{7,23},{8,24},{9,... | collective-permute-start | bytes 196616 | tf_op jit(solution)/shard_map/ppermute | solution.py:203
  5.8 11.8 %collective-permute-start.14 = (bf16[2,64,256]{2,1,0:T(8,128)(2,1)}, bf16[2,64,256]{2,1,0:T(8,128)(2,1)S(1)}, u32[]{:S(2)}, u32[]{:S(2)}) collective-permute-start(bf16[2,64,256]{2,1,0:T(8,128)(2,1)} %get-tuple-element.44), channel_id=1, source_target_pairs={{0,1},{1,0},{2,3},{3,2},{4,5},{5,4},{6,7},{7,6},{8,9},{9,8},{10,11... | collective-permute-start | bytes 196616 | tf_op jit(solution)/shard_map/ppermute | solution.py:203
  8.3 9.5 %collective-permute-start.15 = (bf16[2,64,256]{2,1,0:T(8,128)(2,1)}, bf16[2,64,256]{2,1,0:T(8,128)(2,1)S(1)}, u32[]{:S(2)}, u32[]{:S(2)}) collective-permute-start(bf16[2,64,256]{2,1,0:T(8,128)(2,1)} %get-tuple-element.45), channel_id=1, source_target_pairs={{0,17},{1,16},{2,19},{3,18},{4,21},{5,20},{6,23},{7,22},{8,25},{9,... | collective-permute-start | bytes 196616 | tf_op jit(solution)/shard_map/ppermute | solution.py:203
  8.5 9.6 %collective-permute-start.16 = (bf16[2,64,256]{2,1,0:T(8,128)(2,1)}, bf16[2,64,256]{2,1,0:T(8,128)(2,1)S(1)}, u32[]{:S(2)}, u32[]{:S(2)}) collective-permute-start(bf16[2,64,256]{2,1,0:T(8,128)(2,1)} %get-tuple-element.46), channel_id=1, source_target_pairs={{0,2},{1,3},{2,0},{3,1},{4,6},{5,7},{6,4},{7,5},{8,10},{9,11},{10,... | collective-permute-start | bytes 196616 | tf_op jit(solution)/shard_map/ppermute | solution.py:203
  10.2 10.9 %collective-permute-start.17 = (bf16[2,64,256]{2,1,0:T(8,128)(2,1)}, bf16[2,64,256]{2,1,0:T(8,128)(2,1)}, u32[]{:S(2)}, u32[]{:S(2)}) collective-permute-start(bf16[2,64,256]{2,1,0:T(8,128)(2,1)} %get-tuple-element.47), channel_id=1, source_target_pairs={{0,18},{1,19},{2,16},{3,17},{4,22},{5,23},{6,20},{7,21},{8,26},{9,... | collective-permute-start | bytes 196616 | tf_op jit(solution)/shard_map/ppermute | solution.py:203
  10.2 7.4 %copy-start.8 = (bf16[2,64,256]{2,1,0:T(8,128)(2,1)S(1)}, bf16[2,64,256]{2,1,0:T(8,128)(2,1)}, u32[]{:S(2)}) copy-start(bf16[2,64,256]{2,1,0:T(8,128)(2,1)} %copy-done.7) | copy-start | bytes 196612
  15.1 6.1 %collective-permute-start.18 = (bf16[2,64,256]{2,1,0:T(8,128)(2,1)}, bf16[2,64,256]{2,1,0:T(8,128)(2,1)S(1)}, u32[]{:S(2)}, u32[]{:S(2)}) collective-permute-start(bf16[2,64,256]{2,1,0:T(8,128)(2,1)} %copy-done.9), channel_id=1, source_target_pairs={{0,3},{1,2},{2,1},{3,0},{4,7},{5,6},{6,5},{7,4},{8,11},{9,10},{10,... | collective-permute-start | bytes 196616 | tf_op jit(solution)/shard_map/ppermute | solution.py:203
  17.6 5.2 %collective-permute-start.19 = (bf16[2,64,256]{2,1,0:T(8,128)(2,1)S(1)}, bf16[2,64,256]{2,1,0:T(8,128)(2,1)S(1)}, u32[]{:S(2)}, u32[]{:S(2)}) collective-permute-start(bf16[2,64,256]{2,1,0:T(8,128)(2,1)S(1)} %copy-done.8), channel_id=1, source_target_pairs={{0,19},{1,18},{2,17},{3,16},{4,23},{5,22},{6,21},{7,20},{8,27},{9,... | collective-permute-start | bytes 196616 | tf_op jit(solution)/shard_map/ppermute | solution.py:203
  17.8 5.7 %collective-permute-start = (bf16[2,64,256]{2,1,0:T(8,128)(2,1)S(1)}, bf16[2,64,256]{2,1,0:T(8,128)(2,1)S(1)}, u32[]{:S(2)}, u32[]{:S(2)}) collective-permute-start(bf16[2,64,256]{2,1,0:T(8,128)(2,1)S(1)} %get-tuple-element.32), channel_id=1, source_target_pairs={{0,16},{1,17},{2,18},{3,19},{4,20},{5,21},{6,22},{7,23},{8,24},{9,... | collective-permute-start | bytes 196616 | tf_op jit(solution)/shard_map/ppermute | solution.py:203
  18.1 7.5 %collective-permute-start.1 = (bf16[2,64,256]{2,1,0:T(8,128)(2,1)S(1)}, bf16[2,64,256]{2,1,0:T(8,128)(2,1)S(1)}, u32[]{:S(2)}, u32[]{:S(2)}) collective-permute-start(bf16[2,64,256]{2,1,0:T(8,128)(2,1)S(1)} %get-tuple-element.33), channel_id=1, source_target_pairs={{0,1},{1,0},{2,3},{3,2},{4,5},{5,4},{6,7},{7,6},{8,9},{9,8},{10,11... | collective-permute-start | bytes 196616 | tf_op jit(solution)/shard_map/ppermute | solution.py:203
  21.1 9.5 %collective-permute-start.2 = (bf16[2,64,256]{2,1,0:T(8,128)(2,1)S(1)}, bf16[2,64,256]{2,1,0:T(8,128)(2,1)S(1)}, u32[]{:S(2)}, u32[]{:S(2)}) collective-permute-start(bf16[2,64,256]{2,1,0:T(8,128)(2,1)S(1)} %get-tuple-element.34), channel_id=1, source_target_pairs={{0,17},{1,16},{2,19},{3,18},{4,21},{5,20},{6,23},{7,22},{8,25},{9,... | collective-permute-start | bytes 196616 | tf_op jit(solution)/shard_map/ppermute | solution.py:203
  21.2 12.9 %collective-permute-start.3 = (bf16[2,64,256]{2,1,0:T(8,128)(2,1)}, bf16[2,64,256]{2,1,0:T(8,128)(2,1)S(1)}, u32[]{:S(2)}, u32[]{:S(2)}) collective-permute-start(bf16[2,64,256]{2,1,0:T(8,128)(2,1)} %get-tuple-element.35), channel_id=1, source_target_pairs={{0,2},{1,3},{2,0},{3,1},{4,6},{5,7},{6,4},{7,5},{8,10},{9,11},{10,... | collective-permute-start | bytes 196616 | tf_op jit(solution)/shard_map/ppermute | solution.py:203
  22.8 12.0 %collective-permute-start.4 = (bf16[2,64,256]{2,1,0:T(8,128)(2,1)}, bf16[2,64,256]{2,1,0:T(8,128)(2,1)S(1)}, u32[]{:S(2)}, u32[]{:S(2)}) collective-permute-start(bf16[2,64,256]{2,1,0:T(8,128)(2,1)} %get-tuple-element.36), channel_id=1, source_target_pairs={{0,18},{1,19},{2,16},{3,17},{4,22},{5,23},{6,20},{7,21},{8,26},{9,... | collective-permute-start | bytes 196616 | tf_op jit(solution)/shard_map/ppermute | solution.py:203
  23.5 11.3 %collective-permute-start.5 = (bf16[2,64,256]{2,1,0:T(8,128)(2,1)}, bf16[2,64,256]{2,1,0:T(8,128)(2,1)S(1)}, u32[]{:S(2)}, u32[]{:S(2)}) collective-permute-start(bf16[2,64,256]{2,1,0:T(8,128)(2,1)} %get-tuple-element.37), channel_id=1, source_target_pairs={{0,3},{1,2},{2,1},{3,0},{4,7},{5,6},{6,5},{7,4},{8,11},{9,10},{10,... | collective-permute-start | bytes 196616 | tf_op jit(solution)/shard_map/ppermute | solution.py:203
  25.6 9.2 %collective-permute-start.6 = (bf16[2,64,256]{2,1,0:T(8,128)(2,1)}, bf16[2,64,256]{2,1,0:T(8,128)(2,1)S(1)}, u32[]{:S(2)}, u32[]{:S(2)}) collective-permute-start(bf16[2,64,256]{2,1,0:T(8,128)(2,1)} %get-tuple-element.38), channel_id=1, source_target_pairs={{0,19},{1,18},{2,17},{3,16},{4,23},{5,22},{6,21},{7,20},{8,27},{9,... | collective-permute-start | bytes 196616 | tf_op jit(solution)/shard_map/ppermute | solution.py:203
  28.6 1.3 %copy-start.2 = (bf16[4,1024,256]{2,1,0:T(8,128)(2,1)}, bf16[4,1024,256]{2,1,0:T(8,128)(2,1)S(1)}, u32[]{:S(2)}) copy-start(bf16[4,1024,256]{2,1,0:T(8,128)(2,1)S(1)} %divide_convert_fusion.refs_2_) | copy-start | bytes 6291460
  29.9 0.7 copy-start.6
  30.6 9.7 %collective-permute-start.20 = (bf16[256,256]{1,0:T(8,128)(2,1)}, bf16[256,256]{1,0:T(8,128)(2,1)S(1)}, u32[]{:S(2)}, u32[]{:S(2)}) collective-permute-start(bf16[256,256]{1,0:T(8,128)(2,1)} %get-tuple-element.51), channel_id=1, source_target_pairs={{0,4},{1,5},{2,6},{3,7},{16,20},{17,21},{18,22},{19,23}} | collective-permute-start | bytes 393224 | tf_op jit(solution)/shard_map/ppermute | solution.py:275
  34.1 13.7 %collective-permute-start.23 = (bf16[256,256]{1,0:T(8,128)(2,1)}, bf16[256,256]{1,0:T(8,128)(2,1)S(1)}, u32[]{:S(2)}, u32[]{:S(2)}) collective-permute-start(bf16[256,256]{1,0:T(8,128)(2,1)} %copy-done.6), channel_id=1, source_target_pairs={{15,11},{14,10},{13,9},{12,8},{31,27},{30,26},{29,25},{28,24}} | collective-permute-start | bytes 393224 | tf_op jit(solution)/shard_map/ppermute | solution.py:276
  34.8 1.6 %copy-start.3 = (bf16[4,1024,256]{2,1,0:T(8,128)(2,1)S(1)}, bf16[4,1024,256]{2,1,0:T(8,128)(2,1)}, u32[]{:S(2)}) copy-start(bf16[4,1024,256]{2,1,0:T(8,128)(2,1)} %copy-done.2) | copy-start | bytes 6291460
  36.4 31.8 %copy-start.12 = (bf16[4,1024,512]{2,1,0:T(8,128)(2,1)S(1)}, bf16[4,1024,512]{2,1,0:T(8,128)(2,1)}, u32[]{:S(2)}) copy-start(bf16[4,1024,512]{2,1,0:T(8,128)(2,1)} %param.8) | copy-start | bytes 12582916
  38.3 5.2 %collective-permute-start.7 = (bf16[256,256]{1,0:T(8,128)(2,1)S(1)}, bf16[256,256]{1,0:T(8,128)(2,1)S(1)}, u32[]{:S(2)}, u32[]{:S(2)}) collective-permute-start(bf16[256,256]{1,0:T(8,128)(2,1)S(1)} %get-tuple-element.40), channel_id=1, source_target_pairs={{0,4},{1,5},{2,6},{3,7},{16,20},{17,21},{18,22},{19,23}} | collective-permute-start | bytes 393224 | tf_op jit(solution)/shard_map/ppermute | solution.py:275
  39.6 12.2 %collective-permute-start.10 = (bf16[256,256]{1,0:T(8,128)(2,1)S(1)}, bf16[256,256]{1,0:T(8,128)(2,1)S(1)}, u32[]{:S(2)}, u32[]{:S(2)}) collective-permute-start(bf16[256,256]{1,0:T(8,128)(2,1)S(1)} %get-tuple-element.41), channel_id=1, source_target_pairs={{15,11},{14,10},{13,9},{12,8},{31,27},{30,26},{29,25},{28,24}} | collective-permute-start | bytes 393224 | tf_op jit(solution)/shard_map/ppermute | solution.py:276
  40.3 7.6 %collective-permute-start.21 = (bf16[256,256]{1,0:T(8,128)(2,1)S(1)}, bf16[256,256]{1,0:T(8,128)(2,1)S(1)}, u32[]{:S(2)}, u32[]{:S(2)}) collective-permute-start(bf16[256,256]{1,0:T(8,128)(2,1)S(1)} %bitcast_add_fusion.2), channel_id=1, source_target_pairs={{0,4},{1,5},{2,6},{3,7},{4,8},{5,9},{6,10},{7,11},{16,20},{17,21},... | collective-permute-start | bytes 393224 | tf_op jit(solution)/shard_map/ppermute | solution.py:275
  43.4 8.3 %collective-permute-start.8 = (bf16[256,256]{1,0:T(8,128)(2,1)S(1)}, bf16[256,256]{1,0:T(8,128)(2,1)S(1)}, u32[]{:S(2)}, u32[]{:S(2)}) collective-permute-start(bf16[256,256]{1,0:T(8,128)(2,1)S(1)} %bitcast_add_fusion.6), channel_id=1, source_target_pairs={{0,4},{1,5},{2,6},{3,7},{4,8},{5,9},{6,10},{7,11},{16,20},{17,21},... | collective-permute-start | bytes 393224 | tf_op jit(solution)/shard_map/ppermute | solution.py:275
  47.9 9.8 %collective-permute-start.24 = (bf16[256,256]{1,0:T(8,128)(2,1)S(1)}, bf16[256,256]{1,0:T(8,128)(2,1)S(1)}, u32[]{:S(2)}, u32[]{:S(2)}) collective-permute-start(bf16[256,256]{1,0:T(8,128)(2,1)S(1)} %get-tuple-element.58), channel_id=1, source_target_pairs={{15,11},{14,10},{13,9},{12,8},{11,7},{10,6},{9,5},{8,4},{31,27},{3... | collective-permute-start | bytes 393224 | tf_op jit(solution)/shard_map/ppermute | solution.py:276
  48.6 11.8 %collective-permute-start.22 = (bf16[256,256]{1,0:T(8,128)(2,1)S(1)}, bf16[256,256]{1,0:T(8,128)(2,1)S(1)}, u32[]{:S(2)}, u32[]{:S(2)}) collective-permute-start(bf16[256,256]{1,0:T(8,128)(2,1)S(1)} %get-tuple-element.57), channel_id=1, source_target_pairs={{0,4},{1,5},{2,6},{3,7},{4,8},{5,9},{6,10},{7,11},{8,12},{9,13},{1... | collective-permute-start | bytes 393224 | tf_op jit(solution)/shard_map/ppermute | solution.py:275
  51.8 7.2 %collective-permute-start.11 = (bf16[256,256]{1,0:T(8,128)(2,1)S(1)}, bf16[256,256]{1,0:T(8,128)(2,1)S(1)}, u32[]{:S(2)}, u32[]{:S(2)}) collective-permute-start(bf16[256,256]{1,0:T(8,128)(2,1)S(1)} %get-tuple-element.60), channel_id=1, source_target_pairs={{15,11},{14,10},{13,9},{12,8},{11,7},{10,6},{9,5},{8,4},{31,27},{3... | collective-permute-start | bytes 393224 | tf_op jit(solution)/shard_map/ppermute | solution.py:276
  52.5 14.2 %collective-permute-start.9 = (bf16[256,256]{1,0:T(8,128)(2,1)S(1)}, bf16[256,256]{1,0:T(8,128)(2,1)S(1)}, u32[]{:S(2)}, u32[]{:S(2)}) collective-permute-start(bf16[256,256]{1,0:T(8,128)(2,1)S(1)} %get-tuple-element.59), channel_id=1, source_target_pairs={{0,4},{1,5},{2,6},{3,7},{4,8},{5,9},{6,10},{7,11},{8,12},{9,13},{1... | collective-permute-start | bytes 393224 | tf_op jit(solution)/shard_map/ppermute | solution.py:275
  57.7 8.8 %collective-permute-start.25 = (bf16[256,256]{1,0:T(8,128)(2,1)S(1)}, bf16[256,256]{1,0:T(8,128)(2,1)S(1)}, u32[]{:S(2)}, u32[]{:S(2)}) collective-permute-start(bf16[256,256]{1,0:T(8,128)(2,1)S(1)} %bitcast_add_fusion.1), channel_id=1, source_target_pairs={{15,11},{14,10},{13,9},{12,8},{11,7},{10,6},{9,5},{8,4},{7,3},{6,2... | collective-permute-start | bytes 393224 | tf_op jit(solution)/shard_map/ppermute | solution.py:276
  59.1 9.0 %collective-permute-start.12 = (bf16[256,256]{1,0:T(8,128)(2,1)S(1)}, bf16[256,256]{1,0:T(8,128)(2,1)S(1)}, u32[]{:S(2)}, u32[]{:S(2)}) collective-permute-start(bf16[256,256]{1,0:T(8,128)(2,1)S(1)} %bitcast_add_fusion.5), channel_id=1, source_target_pairs={{15,11},{14,10},{13,9},{12,8},{11,7},{10,6},{9,5},{8,4},{7,3},{6,2... | collective-permute-start | bytes 393224 | tf_op jit(solution)/shard_map/ppermute | solution.py:276
  66.6 2.9 %collective-permute-start.27 = (bf16[256,256]{1,0:T(8,128)(2,1)S(1)}, bf16[256,256]{1,0:T(8,128)(2,1)S(1)}, u32[]{:S(2)}, u32[]{:S(2)}) collective-permute-start(bf16[256,256]{1,0:T(8,128)(2,1)S(1)} %fusion.4.refs_5_), channel_id=1, source_target_pairs={{0,16},{1,17},{2,18},{3,19},{4,20},{5,21},{6,22},{7,23},{8,24},{9,... | collective-permute-start | bytes 393224 | tf_op jit(solution)/shard_map/ppermute | solution.py:203
  68.1 1.4 %copy-start.10 = (s32[1,4]{1,0:T(1,128)S(1)}, s32[1,4]{1,0:T(1,128)}, u32[]{:S(2)}) copy-start(s32[1,4]{1,0:T(1,128)} %refs_1_.3) | copy-start | bytes 52
  68.1 1.4 %copy-start.11 = (s32[16]{0:T(128)S(1)}, s32[16]{0:T(128)}, u32[]{:S(2)}) copy-start(s32[16]{0:T(128)} %refs_2_.3) | copy-start | bytes 196
  68.1 1.4 %collective-permute-start.26 = (bf16[256,256]{1,0:T(8,128)(2,1)S(1)}, bf16[256,256]{1,0:T(8,128)(2,1)S(1)}, u32[]{:S(2)}, u32[]{:S(2)}) collective-permute-start(bf16[256,256]{1,0:T(8,128)(2,1)S(1)} %fusion.6.refs_4_), channel_id=1, source_target_pairs={{0,16},{1,17},{2,18},{3,19},{4,20},{5,21},{6,22},{7,23},{8,24},{9,... | collective-permute-start | bytes 393224 | tf_op jit(solution)/shard_map/ppermute | solution.py:203
  71.4 6.2 %collective-permute-start.28 = (bf16[128,512]{1,0:T(8,128)(2,1)S(1)}, bf16[128,512]{1,0:T(8,128)(2,1)S(1)}, u32[]{:S(2)}, u32[]{:S(2)}) collective-permute-start(bf16[128,512]{1,0:T(8,128)(2,1)S(1)} %get-tuple-element.54), channel_id=1, source_target_pairs={{0,1},{1,0},{2,3},{3,2},{4,5},{5,4},{6,7},{7,6},{8,9},{9,8},{10,11... | collective-permute-start | bytes 393224 | tf_op jit(solution)/shard_map/ppermute | solution.py:203
  73.0 8.4 %collective-permute-start.29 = (bf16[128,512]{1,0:T(8,128)(2,1)S(1)}, bf16[128,512]{1,0:T(8,128)(2,1)S(1)}, u32[]{:S(2)}, u32[]{:S(2)}) collective-permute-start(bf16[128,512]{1,0:T(8,128)(2,1)S(1)} %get-tuple-element.55), channel_id=1, source_target_pairs={{0,2},{1,3},{2,0},{3,1},{4,6},{5,7},{6,4},{7,5},{8,10},{9,11},{10,... | collective-permute-start | bytes 393224 | tf_op jit(solution)/shard_map/ppermute | solution.py:203
  74.1 7.3 %collective-permute-start.30 = (bf16[128,512]{1,0:T(8,128)(2,1)S(1)}, bf16[128,512]{1,0:T(8,128)(2,1)S(1)}, u32[]{:S(2)}, u32[]{:S(2)}) collective-permute-start(bf16[128,512]{1,0:T(8,128)(2,1)S(1)} %get-tuple-element.56), channel_id=1, source_target_pairs={{0,3},{1,2},{2,1},{3,0},{4,7},{5,6},{6,5},{7,4},{8,11},{9,10},{10,... | collective-permute-start | bytes 393224 | tf_op jit(solution)/shard_map/ppermute | solution.py:203

commit v3 on v2

v3 whole, which is shorter than its diff:
```python
import math

import jax
import jax.numpy as jnp
import numpy as np
from jax import lax
from jax.experimental import pallas as pl
from jax.experimental.pallas import tpu as pltpu
from jax.sharding import PartitionSpec as P

absorb_ratio = 0.1
regularizer = 0.05
bf16 = jnp.bfloat16
f32 = jnp.float32


def hartley(length):
    index = np.arange(length)
    turned = (index[:, None] * index[None, :] % length) * (2.0 * math.pi / length)
    table = (np.cos(turned) + np.sin(turned)) / math.sqrt(length)
    return table.astype(bf16)


def signed_square(index, length):
    signed = jnp.where(index < length // 2, index, index - length).astype(f32)
    return signed * signed / float(length * length)


def filters(propagation, rows_sq, cols_sq):
    first = propagation[:, None] * rows_sq[None]
    second = propagation[:, None] * cols_sq[None]
    sin_b, cos_b = jnp.sin(second), jnp.cos(second)
    with_sin = 2.0 * (cos_b - absorb_ratio * sin_b)
    with_cos = 2.0 * (sin_b + absorb_ratio * cos_b)
    transfer = (
        jnp.sin(first)[:, :, None] * with_sin[:, None, :]
        + jnp.cos(first)[:, :, None] * with_cos[:, None, :]
    )
    denom = jnp.sum(transfer * transfer, axis=0) + regularizer
    return transfer / denom


def flat_plan(holograms, propagation, weights, angle_order, slab_rows):
    mbatch, angles, dist_dev, rows_dev, width = holograms.shape
    groups = lax.axis_size("rows")
    cores = lax.axis_size("dist")
    capacity = 2 * rows_dev
    own = angles // cores
    cols = width // groups
    dists = dist_dev * cores
    device = lax.axis_index("rows")
    table = jnp.asarray(hartley(width))
    index = jnp.arange(width, dtype=jnp.int32)
    my_cols = device * cols + jnp.arange(cols, dtype=jnp.int32)
    gain = filters(propagation, signed_square(my_cols, width), signed_square(index, width))

    mine = lax.all_to_all(holograms[0], "dist", split_axis=0, concat_axis=1, tiled=True)
    flat = mine.reshape(own * dists * rows_dev, width)
    spec = jnp.einsum("kx,mx->km", table, flat, preferred_element_type=f32)
    spec = spec.astype(bf16).reshape(groups, cols, own * dists * rows_dev)
    spec = lax.all_to_all(spec, "rows", split_axis=0, concat_axis=0, tiled=True)
    spec = spec.reshape(groups, cols, own, dists, rows_dev).transpose(1, 2, 3, 0, 4)
    spec = spec.reshape(cols * own * dists, width)
    full = jnp.dot(spec, table, preferred_element_type=f32)
    full = full.reshape(cols, own, dists, width)
    full = jnp.sum(full * gain.transpose(1, 0, 2)[:, None], axis=2).astype(bf16)
    half = jnp.einsum("yq,akq->yak", table, full.transpose(1, 0, 2), preferred_element_type=f32)
    half = half.astype(bf16).reshape(groups, rows_dev, own * cols)
    half = lax.all_to_all(half, "rows", split_axis=0, concat_axis=0, tiled=True)
    half = half.reshape(groups, rows_dev, own, cols).transpose(2, 1, 0, 3)
    half = half.reshape(own * rows_dev, width)
    phase = jnp.dot(half, table, preferred_element_type=f32)
    phase = phase.astype(bf16).reshape(own, rows_dev, width)
    phase = lax.all_gather(phase, "dist", axis=0, tiled=True)
    place = (angle_order[0][None, :] == jnp.arange(angles)[:, None]).astype(bf16)
    phase = jnp.einsum("wa,ayx->wyx", place, phase, preferred_element_type=f32)
    recon = jnp.einsum(
        "wyx,wxp->yp", phase.astype(bf16), weights, preferred_element_type=f32
    ).astype(bf16)
    parity = device % 2
    offset = parity * slab_rows[device - parity]
    count = slab_rows[device]
    pairs = [(source, source ^ 1) for source in range(groups)]
    partner = lax.ppermute(recon, "rows", pairs)
    lower = jnp.where(parity == 1, partner, recon)
    upper = jnp.where(parity == 1, recon, partner)
    paired = jnp.concatenate([lower, upper], axis=0)
    slot = jnp.arange(capacity, dtype=jnp.int32)[:, None]
    source = jnp.arange(capacity, dtype=jnp.int32)[None, :]
    select = ((source == offset + slot) & (slot < count)).astype(bf16)
    return jnp.dot(select, paired, preferred_element_type=f32).astype(bf16)


def row_kernel(inner, place, here, there, table, *outs):
    spot = place[1]
    block = table.shape[1] // inner
    for rel in range(inner):
        start = pl.multiple_of((spot ^ rel) * block, block)
        part = table[:, pl.ds(start, block)]
        at = 0
        for source in (here, there):
            dist_dev, rows_dev, width = source.shape[1:]
            flat = source[0].reshape(dist_dev * rows_dev, width)
            got = jnp.dot(flat, part, preferred_element_type=f32).astype(bf16)
            outs[rel][at : at + dist_dev] = got.reshape(dist_dev, rows_dev, block)
            at += dist_dev


def column_kernel(inner, outer, place, table, gain, *refs):
    pieces = refs[:inner]
    out, stack, total, spectrum = refs[inner:]
    spot, plane = place[1], place[2]
    dists, rows_dev, block = pieces[0].shape
    depth = inner * rows_dev
    for rel in range(inner):
        start = pl.multiple_of((spot ^ rel) * rows_dev, rows_dev)
        for d in range(dists):
            stack[d, pl.ds(start, rows_dev), :] = pieces[rel][d]
    part = table[:, pl.ds(pl.multiple_of(plane * depth, depth), depth)]
    for d in range(dists):
        got = jnp.dot(part, stack[d], preferred_element_type=f32) * gain[d].astype(f32)
        if d == 0:
            total[...] = got
        else:
            total[...] += got
    spectrum[...] = total[...].astype(bf16)
    for z in range(outer):
        got = jnp.dot(
            table[z * depth : (z + 1) * depth, :], spectrum[...], preferred_element_type=f32
        )
        out[z] = got.astype(bf16)


def phase_kernel(inner, place, table, *refs):
    pieces = refs[:inner]
    out, joined = refs[inner:]
    spot = place[1]
    block = table.shape[1] // inner
    for rel in range(inner):
        start = pl.multiple_of((spot ^ rel) * block, block)
        joined[:, pl.ds(start, block)] = pieces[rel][...]
    out[...] = jnp.dot(joined[...], table[...], preferred_element_type=f32).astype(bf16)


def recon_kernel(cores, own, chunk, place, order, slabs, weights, before, *refs):
    phases = refs[:cores]
    out = refs[cores]
    core = place[0]
    total = None if before is None else before[...]
    for other in range(cores):
        chosen = weights[order[0, (core ^ other) * own + chunk]]
        got = jnp.dot(phases[other][...], chosen, preferred_element_type=f32)
        total = got if total is None else total + got
    if slabs is None:
        out[...] = total
        return
    capacity = total.shape[0]
    device = place[3]
    parity = device % 2
    offset = parity * slabs[device - parity]
    slot = lax.broadcasted_iota(jnp.int32, (capacity, capacity), 0)
    source = lax.broadcasted_iota(jnp.int32, (capacity, capacity), 1)
    select = (source == slot + offset) & (slot < slabs[device])
    select = jnp.where(select, 1.0, 0.0).astype(bf16)
    got = jnp.dot(select, total.astype(bf16), preferred_element_type=f32)
    out[...] = got.astype(bf16)


def vmem(count):
    return [pl.BlockSpec(memory_space=pltpu.VMEM)] * count


def smem(count):
    return [pl.BlockSpec(memory_space=pltpu.SMEM)] * count


def plane_plan(inner, holograms, propagation, weights, angle_order, slab_rows):
    mbatch, angles, dist_dev, rows_dev, width = holograms.shape
    groups = lax.axis_size("rows")
    cores = lax.axis_size("dist")
    outer = groups // inner
    own = angles // cores
    block = width // inner
    depth = inner * rows_dev
    dists = cores * dist_dev
    pixels = weights.shape[2]
    capacity = 2 * rows_dev
    params = pltpu.CompilerParams(vmem_limit_bytes=20 * 2**20)

    device = lax.axis_index("rows")
    core = lax.axis_index("dist")
    plane, spot = device // inner, device % inner
    place = jnp.stack([core, spot, plane, device]).astype(jnp.int32)
    table = jnp.asarray(hartley(width))

    def sent(value, rel, other):
        if rel == 0 and other == 0:
            return value
        pairs = [
            (c * groups + r, (c ^ other) * groups + (r ^ rel))
            for c in range(cores)
            for r in range(groups)
        ]
        return lax.ppermute(value, ("dist", "rows"), pairs)

    other_angles = lax.dynamic_slice_in_dim(holograms[0], (core ^ 1) * own, own, 0)
    partner = sent(other_angles, 0, 1)

    arrived = []
    for chunk in range(own):
        pieces = pl.pallas_call(
            lambda *refs: row_kernel(inner, *refs),
            out_shape=[jax.ShapeDtypeStruct((dists, rows_dev, block), bf16)] * inner,
            grid_spec=pltpu.PrefetchScalarGridSpec(
                num_scalar_prefetch=1,
                grid=(1,),
                in_specs=[
                    pl.BlockSpec(
                        (1, dist_dev, rows_dev, width),
                        lambda i, place, chunk=chunk: (place[0] * own + chunk, 0, 0, 0),
                    ),
                    pl.BlockSpec(
                        (1, dist_dev, rows_dev, width), lambda i, place, chunk=chunk: (chunk, 0, 0, 0)
                    ),
                ]
                + vmem(1),
                out_specs=vmem(inner),
            ),
            compiler_params=params,
            cost_estimate=pl.CostEstimate(
                flops=2 * dists * rows_dev * width * width,
                bytes_accessed=2 * width * width + 4 * dists * rows_dev * width,
                transcendentals=0,
            ),
            name="row_spectra",
        )(place, holograms[0], partner, table)
        arrived.append([sent(pieces[rel], rel, 0) for rel in range(inner)])

    index = jnp.arange(width, dtype=jnp.int32)
    my_cols = spot * block + jnp.arange(block, dtype=jnp.int32)
    ordered = jnp.concatenate(
        [
            lax.dynamic_slice_in_dim(propagation, (core ^ other) * dist_dev, dist_dev, 0)
            for other in range(cores)
        ]
    )
    gain = filters(ordered, signed_square(index, width), signed_square(my_cols, width)).astype(bf16)

    def plane_sum(parts):
        if outer != 4:
            teams = [[z * inner + i for z in range(outer)] for i in range(inner)]
            return lax.psum_scatter(
                parts, "rows", scatter_dimension=0, axis_index_groups=teams, tiled=False
            ).astype(f32)

        def moved(value, steps):
            return lax.ppermute(
                value, "rows", [(a * inner + i, b * inner + i) for a, b in steps for i in range(inner)]
            )

        away = lax.dynamic_slice_in_dim(parts, jnp.where(plane < 2, 2, 0), 2, 0)
        got = moved(away, [(0, 1), (3, 2)])
        joint = (away.astype(f32) + got.astype(f32)).astype(bf16)
        across = moved(joint, [(1, 2), (2, 1)]).astype(f32)
        near = lax.dynamic_index_in_dim(parts, plane ^ 1, 0, False).astype(f32)
        near = (near + lax.dynamic_index_in_dim(across, (plane ^ 1) % 2, 0, False)).astype(bf16)
        last = moved(near, [(0, 1), (1, 0), (2, 3), (3, 2)]).astype(f32)
        mine = lax.dynamic_index_in_dim(parts, plane, 0, False).astype(f32)
        return mine + lax.dynamic_index_in_dim(across, plane % 2, 0, False) + last

    total = None
    for chunk in range(own):
        parts = pl.pallas_call(
            lambda *refs: column_kernel(inner, outer, *refs),
            out_shape=jax.ShapeDtypeStruct((outer, depth, block), bf16),
            in_specs=smem(1) + vmem(2 + inner),
            out_specs=pl.BlockSpec(memory_space=pltpu.VMEM),
            scratch_shapes=[
                pltpu.VMEM((dists, depth, block), bf16),
                pltpu.VMEM((width, block), f32),
                pltpu.VMEM((width, block), bf16),
            ],
            compiler_params=params,
            cost_estimate=pl.CostEstimate(
                flops=2 * width * block * (dists * depth + width),
                bytes_accessed=2 * width * width + 2 * dists * width * block,
                transcendentals=0,
            ),
            name="columns",
        )(place, table, gain, *arrived[chunk])
        half = plane_sum(parts).astype(bf16)
        pair_rows = {}
        for rel in range(0, inner, 2):
            start = ((spot ^ rel) // 2) * capacity
            pair_rows[rel] = lax.dynamic_slice_in_dim(half, start, capacity, 0)
        pieces = [sent(pair_rows[rel - rel % 2], rel, 0) for rel in range(inner)]
        phase = pl.pallas_call(
            lambda *refs: phase_kernel(inner, *refs),
            out_shape=jax.ShapeDtypeStruct((capacity, width), bf16),
            in_specs=smem(1) + vmem(1 + inner),
            out_specs=pl.BlockSpec(memory_space=pltpu.VMEM),
            scratch_shapes=[pltpu.VMEM((capacity, width), bf16)],
            compiler_params=params,
            cost_estimate=pl.CostEstimate(
                flops=2 * capacity * width * width,
                bytes_accessed=2 * width * width + 4 * capacity * width,
                transcendentals=0,
            ),
            name="phase",
        )(place, table, *pieces)
        phases = [sent(phase, 0, other) for other in range(cores)]
        first, final = chunk == 0, chunk == own - 1

        def recon(place, order, *refs, first=first, final=final, chunk=chunk):
            refs = list(refs)
            slabs = refs.pop(0) if final else None
            chosen = refs.pop(0)
            before = None if first else refs.pop(0)
            recon_kernel(cores, own, chunk, place, order, slabs, chosen, before, *refs)

        scalars = [place, angle_order] + ([slab_rows] if final else [])
        arrays = [weights] + ([] if first else [total]) + phases
        total = pl.pallas_call(
            recon,
            out_shape=jax.ShapeDtypeStruct((capacity, pixels), bf16 if final else f32),
            in_specs=smem(len(scalars)) + vmem(len(arrays)),
            out_specs=pl.BlockSpec(memory_space=pltpu.VMEM),
            compiler_params=params,
            cost_estimate=pl.CostEstimate(
                flops=2 * cores * capacity * width * pixels,
                bytes_accessed=2 * cores * width * (capacity + pixels),
                transcendentals=0,
            ),
            name="recon",
        )(*scalars, *arrays)
    return total


def on_device(holograms, propagation, weights, angle_order, slab_rows):
    mbatch, angles, dist_dev, rows_dev, width = holograms.shape
    groups = lax.axis_size("rows")
    inner = 2 ** (int(math.log2(groups)) // 2)
    block = width // inner
    fits = (
        inner * (groups // inner) == groups
        and rows_dev % 16 == 0
        and block % 128 == 0
        and inner * rows_dev % 128 == 0
        and inner % 2 == 0
        and lax.axis_size("dist") == 2
    )
    if fits:
        return plane_plan(inner, holograms, propagation, weights, angle_order, slab_rows)
    return flat_plan(holograms, propagation, weights, angle_order, slab_rows)


def solution(mesh):
    return jax.shard_map(
        on_device,
        mesh=mesh,
        in_specs=(P(None, None, "dist", "rows", None), P(), P(None, None, "dist"), P(), P()),
        out_specs=P("rows", "dist"),
        check_vma=False,
    )
```

time: 82.6 us -> 71.7 us (0.87)
  waiting for transfers between devices: 15.2 us -> 7.01 us
  starting transfers between devices: 42.6 us -> 36.2 us
  other arithmetic: 4.46 us -> 9.79 us
  local copies, waits for them, and re-layouts: 7.85 us -> 3.74 us
  Pallas kernels: 10.3 us -> 14.2 us
  matrix products: 1.28 us -> 0 us
    ppermute x12 -> x6, starting transfers between devices: 24.8 us -> 18.2 us  [moved(): lax.ppermute(value, 'rows', [(a * inner + i, b * inner + i) for a, b in s...]
    unnamed x26 -> x18, local copies, waits for them, and re-layouts: 7.04 us -> 0.82 us
    ppermute x12 -> x6, waiting for transfers between devices: 8.62 us -> 4.43 us  [moved(): lax.ppermute(value, 'rows', [(a * inner + i, b * inner + i) for a, b in s...]
    ppermute x19 -> x15, waiting for transfers between devices: 6.54 us -> 2.58 us  [sent(): return lax.ppermute(value, ('dist', 'rows'), pairs)]
    pallas_call x5 -> x8, Pallas kernels: 10.3 us -> 14.2 us  [the longest x2 5.28 us: plane_plan(): pl.pallas_call(lambda *refs: row_kernel(inner, *refs), out_shape=[jax.Sha...]
    convert_element_type x3 -> x8, other arithmetic: 0.84 us -> 4.35 us  [the longest x2 1.53 us: plane_sum(): joint = (away.astype(f32) + got.astype(f32)).astype(bf16)]
    dynamic_slice x0 -> x5, local copies, waits for them, and re-layouts: none -> 2.11 us  [the longest x1 2.02 us: plane_plan(): lax.dynamic_slice_in_dim(holograms[0], (core ^ 1) * own, own, 0)]
    convert_element_type x1, other arithmetic: 1.34 us -> 3.33 us  [plane_plan(): filters(ordered, signed_square(index, width), signed_square(my_cols, width))]
  transfers between devices with their start and end apart: 31 -> 21, of which waited for: 5 -> 5; matrix products, arithmetic and copies ran while one was open for 7% -> 15% of each run, Pallas kernels for 8% -> 13%
where the time goes in v3:
time: 71.7 us; the launch traced here: 71.4 us
  starting transfers between devices  36.2 us (50%)
  Pallas kernels  14.2 us (20%)
  other arithmetic  9.79 us (14%)
  waiting for transfers between devices  7.01 us (10%)
  local copies, waits for them, and re-layouts  3.74 us (5%)
    ppermute x6, starting transfers between devices, moved(): lax.ppermute(value, 'rows', [(a * inner + i, b * inner + i) for a, b in s...  18.2 us
    ppermute x15, starting transfers between devices, sent(): return lax.ppermute(value, ('dist', 'rows'), pairs)  18 us
    pallas_call x2, Pallas kernels, plane_plan(): pl.pallas_call(lambda *refs: row_kernel(inner, *refs), out_shape=[jax.Sha...  5.28 us
    ppermute x6, waiting for transfers between devices, moved(): lax.ppermute(value, 'rows', [(a * inner + i, b * inner + i) for a, b in s...  4.43 us
    pallas_call x2, Pallas kernels, plane_plan(): pl.pallas_call(lambda *refs: column_kernel(inner, outer, *refs), out_shap...  4.11 us
    convert_element_type x1, other arithmetic, plane_plan(): filters(ordered, signed_square(index, width), signed_square(my_cols, width))  3.33 us
    pallas_call x2, Pallas kernels, plane_plan(): pl.pallas_call(recon, out_shape=jax.ShapeDtypeStruct((capacity, pixels),...  2.85 us
    ppermute x15, waiting for transfers between devices, sent(): return lax.ppermute(value, ('dist', 'rows'), pairs)  2.58 us
  transfers between devices with their start and end apart: 21, of which 5 were waited for; matrix products, arithmetic and copies ran while one was open for 15% of the time, Pallas kernels for 13%

profile of v3, /device:TPU:0, one launch (start us, length us, event | category | flops | bytes accessed | tf_op | source)
XLA Modules:
  0.0 71.4 jit_solution(10975769640084559482)
XLA Ops:
  0.0 2.0 %dynamic-slice_bitcast_fusion = bf16[2,2,64,1024]{3,2,1,0:T(8,128)(2,1)} fusion(bf16[1,4,2,64,1024]{4,3,2,1,0:T(8,128)(2,1)} %param.6, s32[]{:T(128)S(6)} %select_n.90), kind=kLoop, calls=%fused_computation.5 | loop fusion | bytes 1048580 | tf_op jit(solution)/shard_map/dynamic_slice | solution.py:206
  2.0 0.5 collective-permute-start
  2.5 0.8 %fusion.16 = (f32[2]{0:T(128)S(1)}, f32[2]{0:T(128)S(1)}) fusion(f32[4]{0:T(128)} %param.7, s32[]{:T(128)S(6)} %select_n.89, s32[]{:T(128)S(6)} %select_n.90), kind=kLoop, calls=%fused_computation.41 | loop fusion | bytes 40 | tf_op jit(solution)/shard_map/dynamic_slice | solution.py:243
  3.3 0.1 pad_maximum_fusion
  3.4 0.1 fusion.8
  3.5 0.2 multiply_sine_fusion
  3.7 0.1 pad_add_fusion.refs_0_.place
  3.8 1.5 %multiply_reduce_fusion = f32[1024,256]{1,0:T(8,128)S(1)} fusion(f32[4,256]{1,0:T(4,128)S(1)} %get-tuple-element.28, f32[4,1024]{1,0:T(4,128)S(1)} %get-tuple-element.26, f32[4,256]{1,0:T(4,128)S(1)} %get-tuple-element.27, f32[4,1024]{1,0:T(4,128)S(1)} %get-tuple-element.25), kind=kLoop, calls=%fused_computation.1 | loop fusion | flops 4980736 | bytes 1089536 | tf_op jit(solution)/shard_map/reduce_sum | solution.py:39
  5.4 0.1 broadcast_add_fusion
  5.5 0.0 collective-permute-done.refs_2_
  5.5 2.9 %row_spectra.2 = (bf16[4,64,256]{2,1,0:T(8,128)(2,1)S(1)}, bf16[4,64,256]{2,1,0:T(8,128)(2,1)}, bf16[4,64,256]{2,1,0:T(8,128)(2,1)}, bf16[4,64,256]{2,1,0:T(8,128)(2,1)}) custom-call(s32[4]{0:T(128)S(1)} %pad_add_fusion.refs_0_.place, bf16[4,2,64,1024]{3,2,1,0:T(8,128)(2,1)S(1)} %bitcast.19, bf16[2,2,64,1024]{3,2,1,0:T(8,128)(2,1)} %collective-permute-done.refs_2_, ...), custom_call_target="tpu_custom_call" | custom-call | flops 536870912 | bytes 3145728 | tf_op jit(solution)/shard_map/row_spectra/pallas_call | solution.py:211
  8.5 2.5 %collective-permute-start.1 = (bf16[4,64,256]{2,1,0:T(8,128)(2,1)}, bf16[4,64,256]{2,1,0:T(8,128)(2,1)S(1)}, u32[]{:S(2)}, u32[]{:S(2)}) collective-permute-start(bf16[4,64,256]{2,1,0:T(8,128)(2,1)} %get-tuple-element.14), channel_id=1, source_target_pairs={{0,1},{1,0},{2,3},{3,2},{4,5},{5,4},{6,7},{7,6},{8,9},{9,8},{10,11... | collective-permute-start | bytes 393224 | tf_op jit(solution)/shard_map/ppermute | solution.py:204
  11.0 1.5 %collective-permute-start.2 = (bf16[4,64,256]{2,1,0:T(8,128)(2,1)}, bf16[4,64,256]{2,1,0:T(8,128)(2,1)S(1)}, u32[]{:S(2)}, u32[]{:S(2)}) collective-permute-start(bf16[4,64,256]{2,1,0:T(8,128)(2,1)} %get-tuple-element.15), channel_id=1, source_target_pairs={{0,2},{1,3},{2,0},{3,1},{4,6},{5,7},{6,4},{7,5},{8,10},{9,11},{10,... | collective-permute-start | bytes 393224 | tf_op jit(solution)/shard_map/ppermute | solution.py:204
  12.5 0.0 collective-permute-start.3
  12.5 3.3 %divide_convert_fusion.refs_2_ = bf16[4,1024,256]{2,1,0:T(8,128)(2,1)} fusion(f32[1024,256]{1,0:T(8,128)S(1)} %broadcast_add_fusion, f32[4,256]{1,0:T(4,128)S(1)} %get-tuple-element.28, f32[4,1024]{1,0:T(4,128)} %copy-done.8, f32[4,256]{1,0:T(4,128)S(1)} %get-tuple-element.27, f32[4,1024]{1,0:T(4,128)} %copy-done.7), kind=kLoop, calls=%fused_computation | loop fusion | flops 5242880 | bytes 3186688 | tf_op jit(solution)/shard_map/convert_element_type | solution.py:247
  15.8 2.3 %row_spectra.3 = (bf16[4,64,256]{2,1,0:T(8,128)(2,1)S(1)}, bf16[4,64,256]{2,1,0:T(8,128)(2,1)S(1)}, bf16[4,64,256]{2,1,0:T(8,128)(2,1)S(1)}, bf16[4,64,256]{2,1,0:T(8,128)(2,1)S(1)}) custom-call(s32[4]{0:T(128)S(1)} %pad_add_fusion.refs_0_.place, bf16[4,2,64,1024]{3,2,1,0:T(8,128)(2,1)S(1)} %bitcast.20, ...), custom_call_target="tpu_custom_call" | custom-call | flops 536870912 | bytes 3145728 | tf_op jit(solution)/shard_map/row_spectra/pallas_call | solution.py:211
  18.1 2.1 %collective-permute-start.11 = (bf16[4,64,256]{2,1,0:T(8,128)(2,1)S(1)}, bf16[4,64,256]{2,1,0:T(8,128)(2,1)S(1)}, u32[]{:S(2)}, u32[]{:S(2)}) collective-permute-start(bf16[4,64,256]{2,1,0:T(8,128)(2,1)S(1)} %get-tuple-element.18), channel_id=1, source_target_pairs={{0,1},{1,0},{2,3},{3,2},{4,5},{5,4},{6,7},{7,6},{8,9},{9,8},{10,11... | collective-permute-start | bytes 393224 | tf_op jit(solution)/shard_map/ppermute | solution.py:204
  20.2 1.5 %collective-permute-start.12 = (bf16[4,64,256]{2,1,0:T(8,128)(2,1)S(1)}, bf16[4,64,256]{2,1,0:T(8,128)(2,1)S(1)}, u32[]{:S(2)}, u32[]{:S(2)}) collective-permute-start(bf16[4,64,256]{2,1,0:T(8,128)(2,1)S(1)} %get-tuple-element.19), channel_id=1, source_target_pairs={{0,2},{1,3},{2,0},{3,1},{4,6},{5,7},{6,4},{7,5},{8,10},{9,11},{10,... | collective-permute-start | bytes 393224 | tf_op jit(solution)/shard_map/ppermute | solution.py:204
  21.7 0.0 collective-permute-done.1.refs_4_
  21.7 0.1 collective-permute-start.13
  21.8 0.0 collective-permute-done.2.refs_5_
  21.8 0.0 collective-permute-done.3.refs_6_
  21.8 2.2 %columns.2 = bf16[4,256,256]{2,1,0:T(8,128)(2,1)S(1)} custom-call(s32[4]{0:T(128)S(1)} %pad_add_fusion.refs_0_.place, bf16[1024,1024]{1,0:T(8,128)(2,1)S(1)} %copy-done, bf16[4,1024,256]{2,1,0:T(8,128)(2,1)S(1)} %copy-done.1, bf16[4,64,256]{2,1,0:T(8,128)(2,1)S(1)} %get-tuple-element.13.refs_3_, bf16[4,64,256]{2,1,0:T(8,128)(2,1)S(1)} %collective-permute-done.1.refs_4_, ...), custom_call_target="tpu_custom_call" | custom-call | flops 1073741824 | bytes 4194304 | tf_op jit(solution)/shard_map/columns/pallas_call | solution.py:273
  24.0 3.9 %collective-permute-start.4 = (bf16[2,256,256]{2,1,0:T(8,128)(2,1)S(1)}, bf16[2,256,256]{2,1,0:T(8,128)(2,1)S(1)}, u32[]{:S(2)}, u32[]{:S(2)}) collective-permute-start(bf16[2,256,256]{2,1,0:T(8,128)(2,1)S(1)} %constant_dynamic-slice_fusion.5), channel_id=1, source_target_pairs={{0,4},{1,5},{2,6},{3,7},{12,8},{13,9},{14,10},{15,11},{16,20},{17,... | collective-permute-start | bytes 786440 | tf_op jit(solution)/shard_map/ppermute | solution.py:257
  28.0 0.0 collective-permute-done.12.refs_5_
  28.0 0.0 collective-permute-done.13.refs_6_
  28.0 1.9 %columns.3 = bf16[4,256,256]{2,1,0:T(8,128)(2,1)S(1)} custom-call(s32[4]{0:T(128)S(1)} %pad_add_fusion.refs_0_.place, bf16[1024,1024]{1,0:T(8,128)(2,1)S(1)} %copy-done, bf16[4,1024,256]{2,1,0:T(8,128)(2,1)S(1)} %copy-done.1, bf16[4,64,256]{2,1,0:T(8,128)(2,1)S(1)} %get-tuple-element.17.refs_3_, bf16[4,64,256]{2,1,0:T(8,128)(2,1)S(1)} %collective-permute-done.11.refs_4_, ...), custom_call_target="tpu_custom_call" | custom-call | flops 1073741824 | bytes 4194304 | tf_op jit(solution)/shard_map/columns/pallas_call | solution.py:273
  29.9 3.5 %collective-permute-start.14 = (bf16[2,256,256]{2,1,0:T(8,128)(2,1)S(1)}, bf16[2,256,256]{2,1,0:T(8,128)(2,1)S(1)}, u32[]{:S(2)}, u32[]{:S(2)}) collective-permute-start(bf16[2,256,256]{2,1,0:T(8,128)(2,1)S(1)} %constant_dynamic-slice_fusion.2), channel_id=1, source_target_pairs={{0,4},{1,5},{2,6},{3,7},{12,8},{13,9},{14,10},{15,11},{16,20},{17,... | collective-permute-start | bytes 786440 | tf_op jit(solution)/shard_map/ppermute | solution.py:257
  33.4 0.0 collective-permute-done.4
  33.4 0.8 %add_convert_fusion.1 = bf16[2,256,256]{2,1,0:T(8,128)(2,1)} fusion(bf16[2,256,256]{2,1,0:T(8,128)(2,1)S(1)} %collective-permute-done.4, bf16[4,256,256]{2,1,0:T(8,128)(2,1)S(1)} %columns.2, s32[]{:T(128)S(6)} %select_n.94), kind=kLoop, calls=%fused_computation.4 | loop fusion | flops 524288 | bytes 786436 | tf_op jit(solution)/shard_map/convert_element_type | solution.py:263
  34.2 1.4 %collective-permute-start.5 = (bf16[2,256,256]{2,1,0:T(8,128)(2,1)}, bf16[2,256,256]{2,1,0:T(8,128)(2,1)}, u32[]{:S(2)}, u32[]{:S(2)}) collective-permute-start(bf16[2,256,256]{2,1,0:T(8,128)(2,1)} %add_convert_fusion.1), channel_id=1, source_target_pairs={{4,8},{5,9},{6,10},{7,11},{8,4},{9,5},{10,6},{11,7},{20,24},{21,25... | collective-permute-start | bytes 786440 | tf_op jit(solution)/shard_map/ppermute | solution.py:257
  35.6 2.6 %collective-permute-done.14 = bf16[2,256,256]{2,1,0:T(8,128)(2,1)S(1)} collective-permute-done((bf16[2,256,256]{2,1,0:T(8,128)(2,1)S(1)}, bf16[2,256,256]{2,1,0:T(8,128)(2,1)S(1)}, u32[]{:S(2)}, u32[]{:S(2)}) %collective-permute-start.14) | collective-permute-done | bytes 262176 | tf_op jit(solution)/shard_map/ppermute | solution.py:257
  38.1 0.8 %add_convert_fusion = bf16[2,256,256]{2,1,0:T(8,128)(2,1)} fusion(bf16[2,256,256]{2,1,0:T(8,128)(2,1)S(1)} %collective-permute-done.14, bf16[4,256,256]{2,1,0:T(8,128)(2,1)S(1)} %columns.3, s32[]{:T(128)S(6)} %select_n.94), kind=kLoop, calls=%fused_computation.3 | loop fusion | flops 524288 | bytes 786436 | tf_op jit(solution)/shard_map/convert_element_type | solution.py:263
  38.9 0.7 collective-permute-start.15
  39.6 1.0 %convert_element_type.88 = f32[2,256,256]{2,1,0:T(8,128)S(1)} convert(bf16[2,256,256]{2,1,0:T(8,128)(2,1)} %collective-permute-done.5) | non-fusion elementwise | flops 131072 | bytes 786432 | tf_op jit(solution)/shard_map/convert_element_type | solution.py:264
  40.6 0.8 %copy-done.6 = f32[2,256,256]{2,1,0:T(8,128)} copy-done((f32[2,256,256]{2,1,0:T(8,128)}, f32[2,256,256]{2,1,0:T(8,128)S(1)}, u32[]{:S(2)}) %copy-start.6) | copy-done | bytes 524312
  41.4 0.7 fusion.2
  42.1 6.5 %collective-permute-start.6 = (bf16[256,256]{1,0:T(8,128)(2,1)}, bf16[256,256]{1,0:T(8,128)(2,1)S(1)}, u32[]{:S(2)}, u32[]{:S(2)}) collective-permute-start(bf16[256,256]{1,0:T(8,128)(2,1)} %fusion.2), channel_id=1, source_target_pairs={{0,4},{1,5},{2,6},{3,7},{4,0},{5,1},{6,2},{7,3},{8,12},{9,13},{10,... | collective-permute-start | bytes 393224 | tf_op jit(solution)/shard_map/ppermute | solution.py:257
  48.6 0.0 collective-permute-done.15
  48.7 2.2 %collective-permute-start.16 = (bf16[256,256]{1,0:T(8,128)(2,1)S(1)}, bf16[256,256]{1,0:T(8,128)(2,1)S(1)}, u32[]{:S(2)}, u32[]{:S(2)}) collective-permute-start(bf16[256,256]{1,0:T(8,128)(2,1)S(1)} %fusion.3), channel_id=1, source_target_pairs={{0,4},{1,5},{2,6},{3,7},{4,0},{5,1},{6,2},{7,3},{8,12},{9,13},{10,... | collective-permute-start | bytes 393224 | tf_op jit(solution)/shard_map/ppermute | solution.py:257
  50.9 1.8 %collective-permute-done.6 = bf16[256,256]{1,0:T(8,128)(2,1)S(1)} collective-permute-done((bf16[256,256]{1,0:T(8,128)(2,1)}, bf16[256,256]{1,0:T(8,128)(2,1)S(1)}, u32[]{:S(2)}, u32[]{:S(2)}) %collective-permute-start.6) | collective-permute-done | bytes 131104 | tf_op jit(solution)/shard_map/ppermute | solution.py:257
  52.7 1.0 %fusion.1 = bf16[256,256]{1,0:T(8,128)(2,1)S(1)} fusion(bf16[256,256]{1,0:T(8,128)(2,1)S(1)} %collective-permute-done.6, f32[2,256,256]{2,1,0:T(8,128)} %copy-done.6, s32[]{:T(128)S(6)} %select_n.96, bf16[4,256,256]{2,1,0:T(8,128)(2,1)S(1)} %columns.2, s32[]{:T(128)S(6)} %select_n.93), kind=kLoop, calls=%fused_computation.10 | loop fusion | flops 327680 | bytes 655368 | tf_op jit(solution)/shard_map/convert_element_type | solution.py:291
  53.8 2.7 %collective-permute-start.8 = (bf16[128,256]{1,0:T(8,128)(2,1)S(1)}, bf16[128,256]{1,0:T(8,128)(2,1)S(1)}, u32[]{:S(2)}, u32[]{:S(2)}) collective-permute-start(bf16[128,256]{1,0:T(8,128)(2,1)S(1)} %get-tuple-element.23), channel_id=1, source_target_pairs={{0,2},{1,3},{2,0},{3,1},{4,6},{5,7},{6,4},{7,5},{8,10},{9,11},{10,... | collective-permute-start | bytes 196616 | tf_op jit(solution)/shard_map/ppermute | solution.py:204
  56.4 1.0 %collective-permute-start.9 = (bf16[128,256]{1,0:T(8,128)(2,1)S(1)}, bf16[128,256]{1,0:T(8,128)(2,1)S(1)}, u32[]{:S(2)}, u32[]{:S(2)}) collective-permute-start(bf16[128,256]{1,0:T(8,128)(2,1)S(1)} %get-tuple-element.23), channel_id=1, source_target_pairs={{0,3},{1,2},{2,1},{3,0},{4,7},{5,6},{6,5},{7,4},{8,11},{9,10},{10,... | collective-permute-start | bytes 196616 | tf_op jit(solution)/shard_map/ppermute | solution.py:204
  57.5 0.5 collective-permute-start.7
  58.0 0.0 collective-permute-done.16
  58.0 0.1 fusion
  58.1 1.6 %collective-permute-start.17 = (bf16[128,256]{1,0:T(8,128)(2,1)S(1)}, bf16[128,256]{1,0:T(8,128)(2,1)S(1)}, u32[]{:S(2)}, u32[]{:S(2)}) collective-permute-start(bf16[128,256]{1,0:T(8,128)(2,1)S(1)} %get-tuple-element.22.refs_2_), channel_id=1, source_target_pairs={{0,1},{1,0},{2,3},{3,2},{4,5},{5,4},{6,7},{7,6},{8,9},{9,8},{10,11... | collective-permute-start | bytes 196616 | tf_op jit(solution)/shard_map/ppermute | solution.py:204
  59.7 1.9 %collective-permute-start.18 = (bf16[128,256]{1,0:T(8,128)(2,1)S(1)}, bf16[128,256]{1,0:T(8,128)(2,1)S(1)}, u32[]{:S(2)}, u32[]{:S(2)}) collective-permute-start(bf16[128,256]{1,0:T(8,128)(2,1)S(1)} %get-tuple-element.21), channel_id=1, source_target_pairs={{0,2},{1,3},{2,0},{3,1},{4,6},{5,7},{6,4},{7,5},{8,10},{9,11},{10,... | collective-permute-start | bytes 196616 | tf_op jit(solution)/shard_map/ppermute | solution.py:204
  61.6 0.1 collective-permute-done.7.refs_3_
  61.8 2.1 %collective-permute-start.19 = (bf16[128,256]{1,0:T(8,128)(2,1)S(1)}, bf16[128,256]{1,0:T(8,128)(2,1)S(1)}, u32[]{:S(2)}, u32[]{:S(2)}) collective-permute-start(bf16[128,256]{1,0:T(8,128)(2,1)S(1)} %get-tuple-element.21), channel_id=1, source_target_pairs={{0,3},{1,2},{2,1},{3,0},{4,7},{5,6},{6,5},{7,4},{8,11},{9,10},{10,... | collective-permute-start | bytes 196616 | tf_op jit(solution)/shard_map/ppermute | solution.py:204
  63.8 0.0 collective-permute-done.8.refs_4_
  63.8 0.0 collective-permute-done.9.refs_5_
  63.8 1.0 %phase.2.refs_1_ = bf16[128,1024]{1,0:T(8,128)(2,1)S(1)} custom-call(s32[4]{0:T(128)S(1)} %pad_add_fusion.refs_0_.place, bf16[1024,1024]{1,0:T(8,128)(2,1)S(1)} %copy-done, bf16[128,256]{1,0:T(8,128)(2,1)S(1)} %get-tuple-element.24.refs_2_, bf16[128,256]{1,0:T(8,128)(2,1)S(1)} %collective-permute-done.7.refs_3_, ...), custom_call_target="tpu_custom_call" | custom-call | flops 268435456 | bytes 2621440 | tf_op jit(solution)/shard_map/phase/pallas_call | solution.py:297
  64.9 0.0 copy-start.5
  64.9 0.1 collective-permute-start.10
  65.0 0.0 collective-permute-done.18.refs_4_
  65.0 1.9 %collective-permute-done.19.refs_5_ = bf16[128,256]{1,0:T(8,128)(2,1)S(1)} collective-permute-done((bf16[128,256]{1,0:T(8,128)(2,1)S(1)}, bf16[128,256]{1,0:T(8,128)(2,1)S(1)}, u32[]{:S(2)}, u32[]{:S(2)}) %collective-permute-start.19) | collective-permute-done | bytes 65568 | tf_op jit(solution)/shard_map/ppermute | solution.py:204
  66.9 1.0 %phase.3.refs_3_ = bf16[128,1024]{1,0:T(8,128)(2,1)S(1)} custom-call(s32[4]{0:T(128)S(1)} %pad_add_fusion.refs_0_.place, bf16[1024,1024]{1,0:T(8,128)(2,1)S(1)} %copy-done, bf16[128,256]{1,0:T(8,128)(2,1)S(1)} %get-tuple-element.22.refs_2_, bf16[128,256]{1,0:T(8,128)(2,1)S(1)} %collective-permute-done.17.refs_3_, ...), custom_call_target="tpu_custom_call" | custom-call | flops 268435456 | bytes 2621440 | tf_op jit(solution)/shard_map/phase/pallas_call | solution.py:297
  67.9 0.1 collective-permute-start.20
  68.0 0.0 collective-permute-done.10.refs_2_
  68.0 1.0 %recon.2.refs_2_ = f32[128,512]{1,0:T(8,128)S(1)} custom-call(s32[4]{0:T(128)S(1)} %pad_add_fusion.refs_0_.place, s32[1,4]{1,0:T(1,128)S(1)} %copy-done.4, bf16[4,1024,512]{2,1,0:T(8,128)(2,1)S(1)} %copy-done.2, bf16[128,1024]{1,0:T(8,128)(2,1)S(1)} %phase.2.refs_1_, bf16[128,1024]{1,0:T(8,128)(2,1)S(1)} %collective-permute-done.10.refs_2_), custom_call_target="tpu_custom_call" | custom-call | flops 268435456 | bytes 2621440 | tf_op jit(solution)/shard_map/recon/pallas_call | solution.py:323
  69.1 0.5 collective-permute-done.20.refs_4_
  69.5 1.8 %recon.3 = bf16[128,512]{1,0:T(8,128)(2,1)} custom-call(s32[4]{0:T(128)S(1)} %pad_add_fusion.refs_0_.place, s32[1,4]{1,0:T(1,128)S(1)} %copy-done.4, s32[16]{0:T(128)S(1)} %copy-done.5, bf16[4,1024,512]{2,1,0:T(8,128)(2,1)S(1)} %copy-done.2, f32[128,512]{1,0:T(8,128)S(1)} %recon.2.refs_2_, bf16[128,1024]{1,0:T(8,128)(2,1)S(1)} %phase.3.refs_3_, ...), custom_call_target="tpu_custom_call" | custom-call | flops 268435456 | bytes 2621440 | tf_op jit(solution)/shard_map/recon/pallas_call | solution.py:323
  (27 shorter events, 0.2 us)
Async XLA Ops:
  0.0 5.5 %copy-start = (bf16[1024,1024]{1,0:T(8,128)(2,1)S(1)}, bf16[1024,1024]{1,0:T(8,128)(2,1)}, u32[]{:S(2)}) copy-start(bf16[1024,1024]{1,0:T(8,128)(2,1)} %constant.121.clone.refs_3_.refs_1_) | copy-start | bytes 6291460
  0.0 5.5 %copy-start.3 = (bf16[1,4,2,64,1024]{4,3,2,1,0:T(8,128)(2,1)S(1)}, bf16[1,4,2,64,1024]{4,3,2,1,0:T(8,128)(2,1)}, u32[]{:S(2)}) copy-start(bf16[1,4,2,64,1024]{4,3,2,1,0:T(8,128)(2,1)} %param.6) | copy-start | bytes 3145732
  2.0 3.4 %collective-permute-start = (bf16[2,2,64,1024]{3,2,1,0:T(8,128)(2,1)}, bf16[2,2,64,1024]{3,2,1,0:T(8,128)(2,1)}, u32[]{:S(2)}, u32[]{:S(2)}) collective-permute-start(bf16[2,2,64,1024]{3,2,1,0:T(8,128)(2,1)} %dynamic-slice_bitcast_fusion), channel_id=1, source_target_pairs={{0,16},{1,17},{2,18},{3,19},{4,20},{5,21},{6,22},{7,23},{8,24},{9,... | collective-permute-start | bytes 1572872 | tf_op jit(solution)/shard_map/ppermute | solution.py:204
  3.7 1.8 %copy-start.7 = (f32[4,1024]{1,0:T(4,128)}, f32[4,1024]{1,0:T(4,128)S(1)}, u32[]{:S(2)}) copy-start(f32[4,1024]{1,0:T(4,128)S(1)} %get-tuple-element.25) | copy-start | bytes 49156
  3.7 1.8 %copy-start.8 = (f32[4,1024]{1,0:T(4,128)}, f32[4,1024]{1,0:T(4,128)S(1)}, u32[]{:S(2)}) copy-start(f32[4,1024]{1,0:T(4,128)S(1)} %get-tuple-element.26) | copy-start | bytes 49156
  8.5 13.2 %collective-permute-start.1 = (bf16[4,64,256]{2,1,0:T(8,128)(2,1)}, bf16[4,64,256]{2,1,0:T(8,128)(2,1)S(1)}, u32[]{:S(2)}, u32[]{:S(2)}) collective-permute-start(bf16[4,64,256]{2,1,0:T(8,128)(2,1)} %get-tuple-element.14), channel_id=1, source_target_pairs={{0,1},{1,0},{2,3},{3,2},{4,5},{5,4},{6,7},{7,6},{8,9},{9,8},{10,11... | collective-permute-start | bytes 393224 | tf_op jit(solution)/shard_map/ppermute | solution.py:204
  11.0 10.8 %collective-permute-start.2 = (bf16[4,64,256]{2,1,0:T(8,128)(2,1)}, bf16[4,64,256]{2,1,0:T(8,128)(2,1)S(1)}, u32[]{:S(2)}, u32[]{:S(2)}) collective-permute-start(bf16[4,64,256]{2,1,0:T(8,128)(2,1)} %get-tuple-element.15), channel_id=1, source_target_pairs={{0,2},{1,3},{2,0},{3,1},{4,6},{5,7},{6,4},{7,5},{8,10},{9,11},{10,... | collective-permute-start | bytes 393224 | tf_op jit(solution)/shard_map/ppermute | solution.py:204
  12.5 9.3 %collective-permute-start.3 = (bf16[4,64,256]{2,1,0:T(8,128)(2,1)}, bf16[4,64,256]{2,1,0:T(8,128)(2,1)}, u32[]{:S(2)}, u32[]{:S(2)}) collective-permute-start(bf16[4,64,256]{2,1,0:T(8,128)(2,1)} %get-tuple-element.16), channel_id=1, source_target_pairs={{0,3},{1,2},{2,1},{3,0},{4,7},{5,6},{6,5},{7,4},{8,11},{9,10},{10,... | collective-permute-start | bytes 393224 | tf_op jit(solution)/shard_map/ppermute | solution.py:204
  15.8 6.0 %copy-start.1 = (bf16[4,1024,256]{2,1,0:T(8,128)(2,1)S(1)}, bf16[4,1024,256]{2,1,0:T(8,128)(2,1)}, u32[]{:S(2)}) copy-start(bf16[4,1024,256]{2,1,0:T(8,128)(2,1)} %divide_convert_fusion.refs_2_) | copy-start | bytes 6291460
  18.1 9.8 %collective-permute-start.11 = (bf16[4,64,256]{2,1,0:T(8,128)(2,1)S(1)}, bf16[4,64,256]{2,1,0:T(8,128)(2,1)S(1)}, u32[]{:S(2)}, u32[]{:S(2)}) collective-permute-start(bf16[4,64,256]{2,1,0:T(8,128)(2,1)S(1)} %get-tuple-element.18), channel_id=1, source_target_pairs={{0,1},{1,0},{2,3},{3,2},{4,5},{5,4},{6,7},{7,6},{8,9},{9,8},{10,11... | collective-permute-start | bytes 393224 | tf_op jit(solution)/shard_map/ppermute | solution.py:204
  20.2 7.8 %collective-permute-start.12 = (bf16[4,64,256]{2,1,0:T(8,128)(2,1)S(1)}, bf16[4,64,256]{2,1,0:T(8,128)(2,1)S(1)}, u32[]{:S(2)}, u32[]{:S(2)}) collective-permute-start(bf16[4,64,256]{2,1,0:T(8,128)(2,1)S(1)} %get-tuple-element.19), channel_id=1, source_target_pairs={{0,2},{1,3},{2,0},{3,1},{4,6},{5,7},{6,4},{7,5},{8,10},{9,11},{10,... | collective-permute-start | bytes 393224 | tf_op jit(solution)/shard_map/ppermute | solution.py:204
  21.7 6.3 %collective-permute-start.13 = (bf16[4,64,256]{2,1,0:T(8,128)(2,1)S(1)}, bf16[4,64,256]{2,1,0:T(8,128)(2,1)S(1)}, u32[]{:S(2)}, u32[]{:S(2)}) collective-permute-start(bf16[4,64,256]{2,1,0:T(8,128)(2,1)S(1)} %get-tuple-element.20), channel_id=1, source_target_pairs={{0,3},{1,2},{2,1},{3,0},{4,7},{5,6},{6,5},{7,4},{8,11},{9,10},{10,... | collective-permute-start | bytes 393224 | tf_op jit(solution)/shard_map/ppermute | solution.py:204
  24.0 9.4 %collective-permute-start.4 = (bf16[2,256,256]{2,1,0:T(8,128)(2,1)S(1)}, bf16[2,256,256]{2,1,0:T(8,128)(2,1)S(1)}, u32[]{:S(2)}, u32[]{:S(2)}) collective-permute-start(bf16[2,256,256]{2,1,0:T(8,128)(2,1)S(1)} %constant_dynamic-slice_fusion.5), channel_id=1, source_target_pairs={{0,4},{1,5},{2,6},{3,7},{12,8},{13,9},{14,10},{15,11},{16,20},{17,... | collective-permute-start | bytes 786440 | tf_op jit(solution)/shard_map/ppermute | solution.py:257
  29.9 8.2 %collective-permute-start.14 = (bf16[2,256,256]{2,1,0:T(8,128)(2,1)S(1)}, bf16[2,256,256]{2,1,0:T(8,128)(2,1)S(1)}, u32[]{:S(2)}, u32[]{:S(2)}) collective-permute-start(bf16[2,256,256]{2,1,0:T(8,128)(2,1)S(1)} %constant_dynamic-slice_fusion.2), channel_id=1, source_target_pairs={{0,4},{1,5},{2,6},{3,7},{12,8},{13,9},{14,10},{15,11},{16,20},{17,... | collective-permute-start | bytes 786440 | tf_op jit(solution)/shard_map/ppermute | solution.py:257
  34.2 5.4 %collective-permute-start.5 = (bf16[2,256,256]{2,1,0:T(8,128)(2,1)}, bf16[2,256,256]{2,1,0:T(8,128)(2,1)}, u32[]{:S(2)}, u32[]{:S(2)}) collective-permute-start(bf16[2,256,256]{2,1,0:T(8,128)(2,1)} %add_convert_fusion.1), channel_id=1, source_target_pairs={{4,8},{5,9},{6,10},{7,11},{8,4},{9,5},{10,6},{11,7},{20,24},{21,25... | collective-permute-start | bytes 786440 | tf_op jit(solution)/shard_map/ppermute | solution.py:257
  38.9 9.7 %collective-permute-start.15 = (bf16[2,256,256]{2,1,0:T(8,128)(2,1)}, bf16[2,256,256]{2,1,0:T(8,128)(2,1)S(1)}, u32[]{:S(2)}, u32[]{:S(2)}) collective-permute-start(bf16[2,256,256]{2,1,0:T(8,128)(2,1)} %add_convert_fusion), channel_id=1, source_target_pairs={{4,8},{5,9},{6,10},{7,11},{8,4},{9,5},{10,6},{11,7},{20,24},{21,25... | collective-permute-start | bytes 786440 | tf_op jit(solution)/shard_map/ppermute | solution.py:257
  40.6 0.8 %copy-start.6 = (f32[2,256,256]{2,1,0:T(8,128)}, f32[2,256,256]{2,1,0:T(8,128)S(1)}, u32[]{:S(2)}) copy-start(f32[2,256,256]{2,1,0:T(8,128)S(1)} %convert_element_type.88) | copy-start | bytes 1572868
  42.1 10.6 %collective-permute-start.6 = (bf16[256,256]{1,0:T(8,128)(2,1)}, bf16[256,256]{1,0:T(8,128)(2,1)S(1)}, u32[]{:S(2)}, u32[]{:S(2)}) collective-permute-start(bf16[256,256]{1,0:T(8,128)(2,1)} %fusion.2), channel_id=1, source_target_pairs={{0,4},{1,5},{2,6},{3,7},{4,0},{5,1},{6,2},{7,3},{8,12},{9,13},{10,... | collective-permute-start | bytes 393224 | tf_op jit(solution)/shard_map/ppermute | solution.py:257
  48.6 19.4 %copy-start.2 = (bf16[4,1024,512]{2,1,0:T(8,128)(2,1)S(1)}, bf16[4,1024,512]{2,1,0:T(8,128)(2,1)}, u32[]{:S(2)}) copy-start(bf16[4,1024,512]{2,1,0:T(8,128)(2,1)} %refs_1_.5) | copy-start | bytes 12582916
  48.6 19.4 %copy-start.4 = (s32[1,4]{1,0:T(1,128)S(1)}, s32[1,4]{1,0:T(1,128)}, u32[]{:S(2)}) copy-start(s32[1,4]{1,0:T(1,128)} %order.3) | copy-start | bytes 52
  48.7 9.3 %collective-permute-start.16 = (bf16[256,256]{1,0:T(8,128)(2,1)S(1)}, bf16[256,256]{1,0:T(8,128)(2,1)S(1)}, u32[]{:S(2)}, u32[]{:S(2)}) collective-permute-start(bf16[256,256]{1,0:T(8,128)(2,1)S(1)} %fusion.3), channel_id=1, source_target_pairs={{0,4},{1,5},{2,6},{3,7},{4,0},{5,1},{6,2},{7,3},{8,12},{9,13},{10,... | collective-permute-start | bytes 393224 | tf_op jit(solution)/shard_map/ppermute | solution.py:257
  53.8 10.1 %collective-permute-start.8 = (bf16[128,256]{1,0:T(8,128)(2,1)S(1)}, bf16[128,256]{1,0:T(8,128)(2,1)S(1)}, u32[]{:S(2)}, u32[]{:S(2)}) collective-permute-start(bf16[128,256]{1,0:T(8,128)(2,1)S(1)} %get-tuple-element.23), channel_id=1, source_target_pairs={{0,2},{1,3},{2,0},{3,1},{4,6},{5,7},{6,4},{7,5},{8,10},{9,11},{10,... | collective-permute-start | bytes 196616 | tf_op jit(solution)/shard_map/ppermute | solution.py:204
  56.4 7.4 %collective-permute-start.9 = (bf16[128,256]{1,0:T(8,128)(2,1)S(1)}, bf16[128,256]{1,0:T(8,128)(2,1)S(1)}, u32[]{:S(2)}, u32[]{:S(2)}) collective-permute-start(bf16[128,256]{1,0:T(8,128)(2,1)S(1)} %get-tuple-element.23), channel_id=1, source_target_pairs={{0,3},{1,2},{2,1},{3,0},{4,7},{5,6},{6,5},{7,4},{8,11},{9,10},{10,... | collective-permute-start | bytes 196616 | tf_op jit(solution)/shard_map/ppermute | solution.py:204
  57.5 4.3 %collective-permute-start.7 = (bf16[128,256]{1,0:T(8,128)(2,1)S(1)}, bf16[128,256]{1,0:T(8,128)(2,1)S(1)}, u32[]{:S(2)}, u32[]{:S(2)}) collective-permute-start(bf16[128,256]{1,0:T(8,128)(2,1)S(1)} %get-tuple-element.24.refs_2_), channel_id=1, source_target_pairs={{0,1},{1,0},{2,3},{3,2},{4,5},{5,4},{6,7},{7,6},{8,9},{9,8},{10,11... | collective-permute-start | bytes 196616 | tf_op jit(solution)/shard_map/ppermute | solution.py:204
  58.1 6.9 %collective-permute-start.17 = (bf16[128,256]{1,0:T(8,128)(2,1)S(1)}, bf16[128,256]{1,0:T(8,128)(2,1)S(1)}, u32[]{:S(2)}, u32[]{:S(2)}) collective-permute-start(bf16[128,256]{1,0:T(8,128)(2,1)S(1)} %get-tuple-element.22.refs_2_), channel_id=1, source_target_pairs={{0,1},{1,0},{2,3},{3,2},{4,5},{5,4},{6,7},{7,6},{8,9},{9,8},{10,11... | collective-permute-start | bytes 196616 | tf_op jit(solution)/shard_map/ppermute | solution.py:204
  59.7 5.3 %collective-permute-start.18 = (bf16[128,256]{1,0:T(8,128)(2,1)S(1)}, bf16[128,256]{1,0:T(8,128)(2,1)S(1)}, u32[]{:S(2)}, u32[]{:S(2)}) collective-permute-start(bf16[128,256]{1,0:T(8,128)(2,1)S(1)} %get-tuple-element.21), channel_id=1, source_target_pairs={{0,2},{1,3},{2,0},{3,1},{4,6},{5,7},{6,4},{7,5},{8,10},{9,11},{10,... | collective-permute-start | bytes 196616 | tf_op jit(solution)/shard_map/ppermute | solution.py:204
  61.8 5.2 %collective-permute-start.19 = (bf16[128,256]{1,0:T(8,128)(2,1)S(1)}, bf16[128,256]{1,0:T(8,128)(2,1)S(1)}, u32[]{:S(2)}, u32[]{:S(2)}) collective-permute-start(bf16[128,256]{1,0:T(8,128)(2,1)S(1)} %get-tuple-element.21), channel_id=1, source_target_pairs={{0,3},{1,2},{2,1},{3,0},{4,7},{5,6},{6,5},{7,4},{8,11},{9,10},{10,... | collective-permute-start | bytes 196616 | tf_op jit(solution)/shard_map/ppermute | solution.py:204
  64.9 4.7 %copy-start.5 = (s32[16]{0:T(128)S(1)}, s32[16]{0:T(128)}, u32[]{:S(2)}) copy-start(s32[16]{0:T(128)} %refs_0_.3) | copy-start | bytes 196
  64.9 3.1 %collective-permute-start.10 = (bf16[128,1024]{1,0:T(8,128)(2,1)S(1)}, bf16[128,1024]{1,0:T(8,128)(2,1)S(1)}, u32[]{:S(2)}, u32[]{:S(2)}) collective-permute-start(bf16[128,1024]{1,0:T(8,128)(2,1)S(1)} %phase.2.refs_1_), channel_id=1, source_target_pairs={{0,16},{1,17},{2,18},{3,19},{4,20},{5,21},{6,22},{7,23},{8,24},{9,... | collective-permute-start | bytes 786440 | tf_op jit(solution)/shard_map/ppermute | solution.py:204
  67.9 1.6 %collective-permute-start.20 = (bf16[128,1024]{1,0:T(8,128)(2,1)S(1)}, bf16[128,1024]{1,0:T(8,128)(2,1)S(1)}, u32[]{:S(2)}, u32[]{:S(2)}) collective-permute-start(bf16[128,1024]{1,0:T(8,128)(2,1)S(1)} %phase.3.refs_3_), channel_id=1, source_target_pairs={{0,16},{1,17},{2,18},{3,19},{4,20},{5,21},{6,22},{7,23},{8,24},{9,... | collective-permute-start | bytes 786440 | tf_op jit(solution)/shard_map/ppermute | solution.py:204

commit v4 on v3

--- a/solution.py
+++ b/solution.py
@@ -91,31 +91,45 @@
     return jnp.dot(select, paired, preferred_element_type=f32).astype(bf16)
 
 
-def row_kernel(inner, place, here, there, table, *outs):
-    spot = place[1]
-    block = table.shape[1] // inner
-    for rel in range(inner):
-        start = pl.multiple_of((spot ^ rel) * block, block)
-        part = table[:, pl.ds(start, block)]
-        at = 0
-        for source in (here, there):
-            dist_dev, rows_dev, width = source.shape[1:]
-            flat = source[0].reshape(dist_dev * rows_dev, width)
-            got = jnp.dot(flat, part, preferred_element_type=f32).astype(bf16)
-            outs[rel][at : at + dist_dev] = got.reshape(dist_dev, rows_dev, block)
-            at += dist_dev
-
-
-def column_kernel(inner, outer, place, table, gain, *refs):
-    pieces = refs[:inner]
-    out, stack, total, spectrum = refs[inner:]
-    spot, plane = place[1], place[2]
-    dists, rows_dev, block = pieces[0].shape
+def row_kernel(inner, holo, table, out):
+    cores, _, dist_dev, rows_dev, width = holo.shape
+    block = width // inner
+    flat = holo[...].reshape(cores * dist_dev * rows_dev, width)
+    for spot in range(inner):
+        part = table[:, spot * block : (spot + 1) * block]
+        got = jnp.dot(flat, part, preferred_element_type=f32).astype(bf16)
+        got = got.reshape(cores, dist_dev, rows_dev, block)
+        for core in range(cores):
+            out[core * inner + spot] = got[core]
+
+
+def filter_kernel(sin_a, cos_a, with_sin, with_cos, out):
+    dists, width, block = out.shape
+    step = 128
+    for at in range(0, width, step):
+        rows = pl.ds(at, step)
+        transfer = [
+            sin_a[rows, d : d + 1] * with_sin[d : d + 1, :] + cos_a[rows, d : d + 1] * with_cos[d : d + 1, :]
+            for d in range(dists)
+        ]
+        denom = transfer[0] * transfer[0]
+        for value in transfer[1:]:
+            denom = denom + value * value
+        scale = 1.0 / (denom + regularizer)
+        for d in range(dists):
+            out[d, rows, :] = (transfer[d] * scale).astype(bf16)
+
+
+def column_kernel(inner, outer, place, table, gain, pieces, out, stack, total, spectrum):
+    plane = place[1]
+    _, dist_dev, rows_dev, block = pieces.shape
+    dists = gain.shape[0]
     depth = inner * rows_dev
-    for rel in range(inner):
-        start = pl.multiple_of((spot ^ rel) * rows_dev, rows_dev)
-        for d in range(dists):
-            stack[d, pl.ds(start, rows_dev), :] = pieces[rel][d]
+    for d in range(dists):
+        for spot in range(inner):
+            stack[d, spot * rows_dev : (spot + 1) * rows_dev, :] = pieces[
+                d // dist_dev * inner + spot, d % dist_dev
+            ]
     part = table[:, pl.ds(pl.multiple_of(plane * depth, depth), depth)]
     for d in range(dists):
         got = jnp.dot(part, stack[d], preferred_element_type=f32) * gain[d].astype(f32)
@@ -131,14 +145,22 @@
         out[z] = got.astype(bf16)
 
 
-def phase_kernel(inner, place, table, *refs):
-    pieces = refs[:inner]
-    out, joined = refs[inner:]
-    spot = place[1]
-    block = table.shape[1] // inner
-    for rel in range(inner):
-        start = pl.multiple_of((spot ^ rel) * block, block)
-        joined[:, pl.ds(start, block)] = pieces[rel][...]
+def half_kernel(inner, parts, out):
+    outer, depth, block = parts.shape
+    capacity = 2 * depth // inner
+    for at in range(0, depth, capacity):
+        rows = parts[0, at : at + capacity, :].astype(f32)
+        for z in range(1, outer):
+            rows = rows + parts[z, at : at + capacity, :].astype(f32)
+        rows = rows.astype(bf16)
+        for twin in range(2):
+            out[at // capacity * 2 + twin] = rows
+
+
+def phase_kernel(table, pieces, out, joined):
+    inner, capacity, block = pieces.shape
+    for spot in range(inner):
+        joined[:, spot * block : (spot + 1) * block] = pieces[spot]
     out[...] = jnp.dot(joined[...], table[...], preferred_element_type=f32).astype(bf16)
 
 
@@ -155,7 +177,7 @@
         out[...] = total
         return
     capacity = total.shape[0]
-    device = place[3]
+    device = place[2]
     parity = device % 2
     offset = parity * slabs[device - parity]
     slot = lax.broadcasted_iota(jnp.int32, (capacity, capacity), 0)
@@ -187,93 +209,74 @@
     capacity = 2 * rows_dev
     params = pltpu.CompilerParams(vmem_limit_bytes=20 * 2**20)
 
+    def cost(flops, *arrays):
+        return pl.CostEstimate(
+            flops=flops, bytes_accessed=sum(2 * math.prod(a) for a in arrays), transcendentals=0
+        )
+
     device = lax.axis_index("rows")
     core = lax.axis_index("dist")
     plane, spot = device // inner, device % inner
-    place = jnp.stack([core, spot, plane, device]).astype(jnp.int32)
+    place = jnp.stack([core, plane, device]).astype(jnp.int32)
     table = jnp.asarray(hartley(width))
-
-    def sent(value, rel, other):
-        if rel == 0 and other == 0:
-            return value
-        pairs = [
-            (c * groups + r, (c ^ other) * groups + (r ^ rel))
-            for c in range(cores)
-            for r in range(groups)
-        ]
-        return lax.ppermute(value, ("dist", "rows"), pairs)
-
-    other_angles = lax.dynamic_slice_in_dim(holograms[0], (core ^ 1) * own, own, 0)
-    partner = sent(other_angles, 0, 1)
-
+    in_plane = [[z * inner + i for i in range(inner)] for z in range(outer)]
+    in_line = [[z * inner + i for z in range(outer)] for i in range(inner)]
+    with_cores = [[c * groups + r for c in range(cores) for r in team] for team in in_plane]
+
+    def exchanged(value, axes, teams):
+        return lax.all_to_all(
+            value, axes, split_axis=0, concat_axis=0, axis_index_groups=teams, tiled=True
+        )
+
+    by_core = holograms[0].reshape(cores, own, dist_dev, rows_dev, width)
     arrived = []
     for chunk in range(own):
         pieces = pl.pallas_call(
             lambda *refs: row_kernel(inner, *refs),
-            out_shape=[jax.ShapeDtypeStruct((dists, rows_dev, block), bf16)] * inner,
-            grid_spec=pltpu.PrefetchScalarGridSpec(
-                num_scalar_prefetch=1,
-                grid=(1,),
-                in_specs=[
-                    pl.BlockSpec(
-                        (1, dist_dev, rows_dev, width),
-                        lambda i, place, chunk=chunk: (place[0] * own + chunk, 0, 0, 0),
-                    ),
-                    pl.BlockSpec(
-                        (1, dist_dev, rows_dev, width), lambda i, place, chunk=chunk: (chunk, 0, 0, 0)
-                    ),
-                ]
-                + vmem(1),
-                out_specs=vmem(inner),
-            ),
-            compiler_params=params,
-            cost_estimate=pl.CostEstimate(
-                flops=2 * dists * rows_dev * width * width,
-                bytes_accessed=2 * width * width + 4 * dists * rows_dev * width,
-                transcendentals=0,
+            out_shape=jax.ShapeDtypeStruct((cores * inner, dist_dev, rows_dev, block), bf16),
+            grid=(1,),
+            in_specs=[
+                pl.BlockSpec(
+                    (cores, 1, dist_dev, rows_dev, width),
+                    lambda i, chunk=chunk: (0, chunk, 0, 0, 0),
+                )
+            ]
+            + vmem(1),
+            out_specs=pl.BlockSpec(memory_space=pltpu.VMEM),
+            compiler_params=params,
+            cost_estimate=cost(
+                2 * dists * rows_dev * width * width, (width, width), (2, dists, rows_dev, width)
             ),
             name="row_spectra",
-        )(place, holograms[0], partner, table)
-        arrived.append([sent(pieces[rel], rel, 0) for rel in range(inner)])
+        )(by_core, table)
+        arrived.append(exchanged(pieces, ("dist", "rows"), with_cores))
 
     index = jnp.arange(width, dtype=jnp.int32)
     my_cols = spot * block + jnp.arange(block, dtype=jnp.int32)
-    ordered = jnp.concatenate(
-        [
-            lax.dynamic_slice_in_dim(propagation, (core ^ other) * dist_dev, dist_dev, 0)
-            for other in range(cores)
-        ]
+    first = signed_square(index, width)[:, None] * propagation[None]
+    second = propagation[:, None] * signed_square(my_cols, width)[None]
+    sin_b, cos_b = jnp.sin(second), jnp.cos(second)
+    gain = pl.pallas_call(
+        filter_kernel,
+        out_shape=jax.ShapeDtypeStruct((dists, width, block), bf16),
+        in_specs=vmem(4),
+        out_specs=pl.BlockSpec(memory_space=pltpu.VMEM),
+        compiler_params=params,
+        cost_estimate=cost(32 * width * block, (dists, width, block)),
+        name="filters",
+    )(
+        jnp.sin(first),
+        jnp.cos(first),
+        2.0 * (cos_b - absorb_ratio * sin_b),
+        2.0 * (sin_b + absorb_ratio * cos_b),
     )
-    gain = filters(ordered, signed_square(index, width), signed_square(my_cols, width)).astype(bf16)
-
-    def plane_sum(parts):
-        if outer != 4:
-            teams = [[z * inner + i for z in range(outer)] for i in range(inner)]
-            return lax.psum_scatter(
-                parts, "rows", scatter_dimension=0, axis_index_groups=teams, tiled=False
-            ).astype(f32)
-
-        def moved(value, steps):
-            return lax.ppermute(
-                value, "rows", [(a * inner + i, b * inner + i) for a, b in steps for i in range(inner)]
-            )
-
-        away = lax.dynamic_slice_in_dim(parts, jnp.where(plane < 2, 2, 0), 2, 0)
-        got = moved(away, [(0, 1), (3, 2)])
-        joint = (away.astype(f32) + got.astype(f32)).astype(bf16)
-        across = moved(joint, [(1, 2), (2, 1)]).astype(f32)
-        near = lax.dynamic_index_in_dim(parts, plane ^ 1, 0, False).astype(f32)
-        near = (near + lax.dynamic_index_in_dim(across, (plane ^ 1) % 2, 0, False)).astype(bf16)
-        last = moved(near, [(0, 1), (1, 0), (2, 3), (3, 2)]).astype(f32)
-        mine = lax.dynamic_index_in_dim(parts, plane, 0, False).astype(f32)
-        return mine + lax.dynamic_index_in_dim(across, plane % 2, 0, False) + last
 
     total = None
     for chunk in range(own):
         parts = pl.pallas_call(
             lambda *refs: column_kernel(inner, outer, *refs),
             out_shape=jax.ShapeDtypeStruct((outer, depth, block), bf16),
-            in_specs=smem(1) + vmem(2 + inner),
+            in_specs=smem(1) + vmem(3),
             out_specs=pl.BlockSpec(memory_space=pltpu.VMEM),
             scratch_shapes=[
                 pltpu.VMEM((dists, depth, block), bf16),
@@ -281,55 +284,53 @@
                 pltpu.VMEM((width, block), bf16),
             ],
             compiler_params=params,
-            cost_estimate=pl.CostEstimate(
-                flops=2 * width * block * (dists * depth + width),
-                bytes_accessed=2 * width * width + 2 * dists * width * block,
-                transcendentals=0,
+            cost_estimate=cost(
+                2 * width * block * (dists * depth + width), (width, width), (dists, width, block)
             ),
             name="columns",
-        )(place, table, gain, *arrived[chunk])
-        half = plane_sum(parts).astype(bf16)
-        pair_rows = {}
-        for rel in range(0, inner, 2):
-            start = ((spot ^ rel) // 2) * capacity
-            pair_rows[rel] = lax.dynamic_slice_in_dim(half, start, capacity, 0)
-        pieces = [sent(pair_rows[rel - rel % 2], rel, 0) for rel in range(inner)]
+        )(place, table, gain, arrived[chunk])
+        parts = exchanged(parts, "rows", in_line)
+        halves = pl.pallas_call(
+            lambda *refs: half_kernel(inner, *refs),
+            out_shape=jax.ShapeDtypeStruct((inner, capacity, block), bf16),
+            in_specs=vmem(1),
+            out_specs=pl.BlockSpec(memory_space=pltpu.VMEM),
+            compiler_params=params,
+            cost_estimate=cost(outer * depth * block, (2, outer, depth, block)),
+            name="half",
+        )(parts)
+        halves = exchanged(halves, "rows", in_plane)
         phase = pl.pallas_call(
-            lambda *refs: phase_kernel(inner, *refs),
+            phase_kernel,
             out_shape=jax.ShapeDtypeStruct((capacity, width), bf16),
-            in_specs=smem(1) + vmem(1 + inner),
+            in_specs=vmem(2),
             out_specs=pl.BlockSpec(memory_space=pltpu.VMEM),
             scratch_shapes=[pltpu.VMEM((capacity, width), bf16)],
             compiler_params=params,
-            cost_estimate=pl.CostEstimate(
-                flops=2 * capacity * width * width,
-                bytes_accessed=2 * width * width + 4 * capacity * width,
-                transcendentals=0,
-            ),
+            cost_estimate=cost(2 * capacity * width * width, (width, width), (2, capacity, width)),
             name="phase",
-        )(place, table, *pieces)
-        phases = [sent(phase, 0, other) for other in range(cores)]
-        first, final = chunk == 0, chunk == own - 1
-
-        def recon(place, order, *refs, first=first, final=final, chunk=chunk):
+        )(table, halves)
+        swaps = [(c, c ^ 1) for c in range(cores)]
+        phases = [phase, lax.ppermute(phase, "dist", swaps)]
+        opening, final = chunk == 0, chunk == own - 1
+
+        def recon(place, order, *refs, opening=opening, final=final, chunk=chunk):
             refs = list(refs)
             slabs = refs.pop(0) if final else None
             chosen = refs.pop(0)
-            before = None if first else refs.pop(0)
+            before = None if opening else refs.pop(0)
             recon_kernel(cores, own, chunk, place, order, slabs, chosen, before, *refs)
 
         scalars = [place, angle_order] + ([slab_rows] if final else [])
-        arrays = [weights] + ([] if first else [total]) + phases
+        arrays = [weights] + ([] if opening else [total]) + phases
         total = pl.pallas_call(
             recon,
             out_shape=jax.ShapeDtypeStruct((capacity, pixels), bf16 if final else f32),
             in_specs=smem(len(scalars)) + vmem(len(arrays)),
             out_specs=pl.BlockSpec(memory_space=pltpu.VMEM),
             compiler_params=params,
-            cost_estimate=pl.CostEstimate(
-                flops=2 * cores * capacity * width * pixels,
-                bytes_accessed=2 * cores * width * (capacity + pixels),
-                transcendentals=0,
+            cost_estimate=cost(
+                2 * cores * capacity * width * pixels, (cores, width, capacity + pixels)
             ),
             name="recon",
         )(*scalars, *arrays)

time: 71.7 us -> 94.3 us (1.32)
  waiting for transfers between devices: 7.01 us -> 42.4 us
  starting transfers between devices: 36.2 us -> 24.3 us
  local copies, waits for them, and re-layouts: 3.74 us -> 12.3 us
  other arithmetic: 9.79 us -> 2.1 us
  Pallas kernels: 14.2 us -> 12.2 us
    all_to_all x0 -> x6, waiting for transfers between devices: none -> 42.4 us  [exchanged(): lax.all_to_all(value, axes, split_axis=0, concat_axis=0, axis_index_group...]
    ppermute x21 -> x2, starting transfers between devices: 36.2 us -> 0.14 us  [plane_plan(): phases = [phase, lax.ppermute(phase, 'dist', swaps)]]
    all_to_all x0 -> x6, starting transfers between devices: none -> 24.1 us  [exchanged(): lax.all_to_all(value, axes, split_axis=0, concat_axis=0, axis_index_group...]
    unnamed x18 -> x30, local copies, waits for them, and re-layouts: 0.82 us -> 12.3 us
    convert_element_type x9 -> x0, other arithmetic: 7.67 us -> none  [the longest x1 3.33 us: plane_plan(): filters(ordered, signed_square(index, width), signed_square(my_cols, width))]
    ppermute x21 -> x2, waiting for transfers between devices: 7.01 us -> 0.01 us  [plane_plan(): phases = [phase, lax.ppermute(phase, 'dist', swaps)]]
    dynamic_slice x6 -> x0, local copies, waits for them, and re-layouts: 2.92 us -> none  [the longest x1 2.02 us: plane_plan(): lax.dynamic_slice_in_dim(holograms[0], (core ^ 1) * own, own, 0)]
    pallas_call x4 -> x7, Pallas kernels: 7.29 us -> 5.29 us  [the longest x2 1.56 us: plane_plan(): pl.pallas_call(lambda *refs: half_kernel(inner, *refs), out_shape=jax.Sha...]
  transfers between devices with their start and end apart: 21 -> 8, of which waited for: 5 -> 6; matrix products, arithmetic and copies ran while one was open for 15% -> 2% of each run, Pallas kernels for 13% -> 10%
where the time goes in v4:
time: 94.3 us; the launch traced here: 93.5 us
  waiting for transfers between devices  42.4 us (45%)
  starting transfers between devices  24.3 us (26%)
  local copies, waits for them, and re-layouts  12.3 us (13%)
  Pallas kernels  12.2 us (13%)
  other arithmetic  2.1 us (2%)
    all_to_all x6, waiting for transfers between devices, exchanged(): lax.all_to_all(value, axes, split_axis=0, concat_axis=0, axis_index_group...  42.4 us
    all_to_all x6, starting transfers between devices, exchanged(): lax.all_to_all(value, axes, split_axis=0, concat_axis=0, axis_index_group...  24.1 us
    unnamed x30, local copies, waits for them, and re-layouts  12.3 us
    pallas_call x2, Pallas kernels, plane_plan(): pl.pallas_call(lambda *refs: column_kernel(inner, outer, *refs), out_shap...  4.08 us
    pallas_call x2, Pallas kernels, plane_plan(): pl.pallas_call(recon, out_shape=jax.ShapeDtypeStruct((capacity, pixels),...  2.82 us
  transfers between devices with their start and end apart: 8, of which 6 were waited for; matrix products, arithmetic and copies ran while one was open for 2% of the time, Pallas kernels for 10%

profile of v4, /device:TPU:0, one launch (start us, length us, event | category | flops | bytes accessed | tf_op | source)
XLA Modules:
  0.0 93.5 jit_solution(9677784088453825769)
XLA Ops:
  0.0 0.0 copy-start
  0.0 1.6 %copy-done = bf16[1024,1024]{1,0:T(8,128)(2,1)S(1)} copy-done((bf16[1024,1024]{1,0:T(8,128)(2,1)S(1)}, bf16[1024,1024]{1,0:T(8,128)(2,1)}, u32[]{:S(2)}) %copy-start) | copy-done | bytes 2097176
  1.6 0.0 copy-start.6
  1.6 1.2 %copy-done.6 = bf16[1,4,2,64,1024]{4,3,2,1,0:T(8,128)(2,1)S(1)} copy-done((bf16[1,4,2,64,1024]{4,3,2,1,0:T(8,128)(2,1)S(1)}, bf16[1,4,2,64,1024]{4,3,2,1,0:T(8,128)(2,1)}, u32[]{:S(2)}) %copy-start.6) | copy-done | bytes 1048600
  2.8 0.0 copy-start.1
  2.8 0.0 copy-start.7
  2.8 0.7 row_spectra.2
  3.5 0.0 copy-start.9
  3.5 0.8 copy-done.9
  4.3 5.2 %all-to-all-start = ((bf16[8,2,64,256]{3,2,1,0:T(8,128)(2,1)}), bf16[8,2,64,256]{3,2,1,0:T(8,128)(2,1)}, u32[]{:S(2)}, u32[]{:S(2)}) async-start(bf16[8,2,64,256]{3,2,1,0:T(8,128)(2,1)} %copy-done.9), calls=%async_computation | async-start | bytes 1048576 | tf_op jit(solution)/shard_map/all_to_all | solution.py:227
  9.5 0.0 copy-done.1
  9.5 0.0 copy-done.7
  9.5 0.0 copy-start.14
  9.5 0.7 row_spectra.3
  10.2 0.0 copy-start.8
  10.3 0.8 copy-done.8
  11.1 0.0 copy-done.14
  11.1 0.1 fusion.5
  11.2 7.7 %all-to-all-done.refs_3_ = bf16[8,2,64,256]{3,2,1,0:T(8,128)(2,1)} async-done(((bf16[8,2,64,256]{3,2,1,0:T(8,128)(2,1)}), bf16[8,2,64,256]{3,2,1,0:T(8,128)(2,1)}, u32[]{:S(2)}, u32[]{:S(2)}) %all-to-all-start) | async-done | bytes 524320 | tf_op jit(solution)/shard_map/all_to_all | solution.py:227
  18.9 3.5 %all-to-all-start.3 = ((bf16[8,2,64,256]{3,2,1,0:T(8,128)(2,1)}), bf16[8,2,64,256]{3,2,1,0:T(8,128)(2,1)S(1)}, u32[]{:S(2)}, u32[]{:S(2)}) async-start(bf16[8,2,64,256]{3,2,1,0:T(8,128)(2,1)} %copy-done.8), calls=%async_computation.3 | async-start | bytes 1048576 | tf_op jit(solution)/shard_map/all_to_all | solution.py:227
  22.4 1.9 %multiply_cosine_fusion = (f32[1024,4]{1,0:T(8,128)S(1)}, f32[1024,4]{1,0:T(8,128)S(1)}) fusion(f32[1024]{0:T(1024)S(1)} %fusion.8, f32[4]{0:T(128)S(1)} %copy-done.14), kind=kLoop, calls=%fused_computation | loop fusion | flops 4096 | bytes 36880 | tf_op jit(solution)/shard_map/cos | solution.py:269
  24.3 1.4 %filters.1.refs_2_ = bf16[4,1024,256]{2,1,0:T(8,128)(2,1)S(1)} custom-call(f32[1024,4]{1,0:T(8,128)S(1)} %get-tuple-element.6.sin_a, f32[1024,4]{1,0:T(8,128)S(1)} %get-tuple-element.5.cos_a, f32[4,256]{1,0:T(4,128)S(1)} %get-tuple-element.8.with_sin, f32[4,256]{1,0:T(4,128)S(1)} %get-tuple-element.7.with_cos), custom_call_target="tpu_custom_call" | custom-call | flops 8388608 | bytes 2097152 | tf_op jit(solution)/shard_map/filters/pallas_call | solution.py:259
  25.7 0.1 pad_add_fusion.refs_0_.place
  25.8 2.3 %columns.2 = bf16[4,256,256]{2,1,0:T(8,128)(2,1)S(1)} custom-call(s32[3]{0:T(128)S(1)} %pad_add_fusion.refs_0_.place, bf16[1024,1024]{1,0:T(8,128)(2,1)S(1)} %copy-done.1, bf16[4,1024,256]{2,1,0:T(8,128)(2,1)S(1)} %filters.1.refs_2_, bf16[8,2,64,256]{3,2,1,0:T(8,128)(2,1)} %all-to-all-done.refs_3_), custom_call_target="tpu_custom_call" | custom-call | flops 1073741824 | bytes 4194304 | tf_op jit(solution)/shard_map/columns/pallas_call | solution.py:276
  28.1 0.0 copy-start.2
  28.1 1.3 %copy-done.2 = bf16[4,1024,256]{2,1,0:T(8,128)(2,1)} copy-done((bf16[4,1024,256]{2,1,0:T(8,128)(2,1)}, bf16[4,1024,256]{2,1,0:T(8,128)(2,1)S(1)}, u32[]{:S(2)}) %copy-start.2) | copy-done | bytes 2097176
  29.4 0.0 copy-start.10
  29.4 0.8 copy-done.10
  30.2 1.3 %all-to-all-done.3.refs_3_ = bf16[8,2,64,256]{3,2,1,0:T(8,128)(2,1)S(1)} async-done(((bf16[8,2,64,256]{3,2,1,0:T(8,128)(2,1)}), bf16[8,2,64,256]{3,2,1,0:T(8,128)(2,1)S(1)}, u32[]{:S(2)}, u32[]{:S(2)}) %all-to-all-start.3) | async-done | bytes 524320 | tf_op jit(solution)/shard_map/all_to_all | solution.py:227
  31.6 5.2 %all-to-all-start.1 = ((bf16[4,256,256]{2,1,0:T(8,128)(2,1)}), bf16[4,256,256]{2,1,0:T(8,128)(2,1)S(1)}, u32[]{:S(2)}, u32[]{:S(2)}) async-start(bf16[4,256,256]{2,1,0:T(8,128)(2,1)} %copy-done.10), calls=%async_computation.1 | async-start | bytes 1048576 | tf_op jit(solution)/shard_map/all_to_all | solution.py:227
  36.8 0.0 copy-start.3
  36.8 1.6 %copy-done.3 = bf16[4,1024,256]{2,1,0:T(8,128)(2,1)S(1)} copy-done((bf16[4,1024,256]{2,1,0:T(8,128)(2,1)S(1)}, bf16[4,1024,256]{2,1,0:T(8,128)(2,1)}, u32[]{:S(2)}) %copy-start.3) | copy-done | bytes 2097176
  38.4 1.8 %columns.3 = bf16[4,256,256]{2,1,0:T(8,128)(2,1)S(1)} custom-call(s32[3]{0:T(128)S(1)} %pad_add_fusion.refs_0_.place, bf16[1024,1024]{1,0:T(8,128)(2,1)S(1)} %copy-done.1, bf16[4,1024,256]{2,1,0:T(8,128)(2,1)S(1)} %copy-done.3, bf16[8,2,64,256]{3,2,1,0:T(8,128)(2,1)S(1)} %all-to-all-done.3.refs_3_), custom_call_target="tpu_custom_call" | custom-call | flops 1073741824 | bytes 4194304 | tf_op jit(solution)/shard_map/columns/pallas_call | solution.py:276
  40.2 0.0 copy-start.11
  40.2 0.8 copy-done.11
  41.0 10.7 %all-to-all-done.1.refs_0_ = bf16[4,256,256]{2,1,0:T(8,128)(2,1)S(1)} async-done(((bf16[4,256,256]{2,1,0:T(8,128)(2,1)}), bf16[4,256,256]{2,1,0:T(8,128)(2,1)S(1)}, u32[]{:S(2)}, u32[]{:S(2)}) %all-to-all-start.1) | async-done | bytes 524320 | tf_op jit(solution)/shard_map/all_to_all | solution.py:227
  51.7 3.5 %all-to-all-start.4 = ((bf16[4,256,256]{2,1,0:T(8,128)(2,1)}), bf16[4,256,256]{2,1,0:T(8,128)(2,1)S(1)}, u32[]{:S(2)}, u32[]{:S(2)}) async-start(bf16[4,256,256]{2,1,0:T(8,128)(2,1)} %copy-done.11), calls=%async_computation.4 | async-start | bytes 1048576 | tf_op jit(solution)/shard_map/all_to_all | solution.py:227
  55.2 0.8 half.2
  56.0 13.3 %all-to-all-done.4.refs_0_ = bf16[4,256,256]{2,1,0:T(8,128)(2,1)S(1)} async-done(((bf16[4,256,256]{2,1,0:T(8,128)(2,1)}), bf16[4,256,256]{2,1,0:T(8,128)(2,1)S(1)}, u32[]{:S(2)}, u32[]{:S(2)}) %all-to-all-start.4) | async-done | bytes 524320 | tf_op jit(solution)/shard_map/all_to_all | solution.py:227
  69.3 3.4 %all-to-all-start.2 = ((bf16[4,128,256]{2,1,0:T(8,128)(2,1)}), bf16[4,128,256]{2,1,0:T(8,128)(2,1)S(1)}, u32[]{:S(2)}, u32[]{:S(2)}) async-start(bf16[4,128,256]{2,1,0:T(8,128)(2,1)} %half.2), calls=%async_computation.2 | async-start | bytes 524288 | tf_op jit(solution)/shard_map/all_to_all | solution.py:227
  72.7 0.8 half.3
  73.5 4.6 %all-to-all-done.2.pieces = bf16[4,128,256]{2,1,0:T(8,128)(2,1)S(1)} async-done(((bf16[4,128,256]{2,1,0:T(8,128)(2,1)}), bf16[4,128,256]{2,1,0:T(8,128)(2,1)S(1)}, u32[]{:S(2)}, u32[]{:S(2)}) %all-to-all-start.2) | async-done | bytes 262176 | tf_op jit(solution)/shard_map/all_to_all | solution.py:227
  78.0 3.4 %all-to-all-start.5 = ((bf16[4,128,256]{2,1,0:T(8,128)(2,1)}), bf16[4,128,256]{2,1,0:T(8,128)(2,1)S(1)}, u32[]{:S(2)}, u32[]{:S(2)}) async-start(bf16[4,128,256]{2,1,0:T(8,128)(2,1)} %half.3), calls=%async_computation.5 | async-start | bytes 524288 | tf_op jit(solution)/shard_map/all_to_all | solution.py:227
  81.4 0.0 copy-start.12
  81.4 0.5 phase.2.refs_1_
  81.9 0.1 collective-permute-start
  82.0 4.8 %all-to-all-done.5.pieces = bf16[4,128,256]{2,1,0:T(8,128)(2,1)S(1)} async-done(((bf16[4,128,256]{2,1,0:T(8,128)(2,1)}), bf16[4,128,256]{2,1,0:T(8,128)(2,1)S(1)}, u32[]{:S(2)}, u32[]{:S(2)}) %all-to-all-start.5) | async-done | bytes 262176 | tf_op jit(solution)/shard_map/all_to_all | solution.py:227
  86.8 0.0 copy-start.13
  86.8 0.4 phase.3.refs_3_
  87.2 0.1 collective-permute-start.1
  87.3 0.0 collective-permute-done.refs_2_
  87.3 0.0 copy-done.12
  87.3 0.0 copy-start.4
  87.3 2.2 %copy-done.4 = bf16[4,1024,512]{2,1,0:T(8,128)(2,1)S(1)} copy-done((bf16[4,1024,512]{2,1,0:T(8,128)(2,1)S(1)}, bf16[4,1024,512]{2,1,0:T(8,128)(2,1)}, u32[]{:S(2)}) %copy-start.4) | copy-done | bytes 4194328
  89.5 0.0 copy-start.5
  89.5 1.0 %recon.2.refs_2_ = f32[128,512]{1,0:T(8,128)S(1)} custom-call(s32[3]{0:T(128)S(1)} %pad_add_fusion.refs_0_.place, s32[1,4]{1,0:T(1,128)S(1)} %copy-done.12, bf16[4,1024,512]{2,1,0:T(8,128)(2,1)S(1)} %copy-done.4, bf16[128,1024]{1,0:T(8,128)(2,1)S(1)} %phase.2.refs_1_, bf16[128,1024]{1,0:T(8,128)(2,1)S(1)} %collective-permute-done.refs_2_), custom_call_target="tpu_custom_call" | custom-call | flops 268435456 | bytes 2621440 | tf_op jit(solution)/shard_map/recon/pallas_call | solution.py:326
  90.5 0.0 collective-permute-done.1.refs_4_
  90.5 0.0 copy-done.13
  90.5 1.2 %copy-done.5 = bf16[4,1024,512]{2,1,0:T(8,128)(2,1)S(1)} copy-done((bf16[4,1024,512]{2,1,0:T(8,128)(2,1)S(1)}, bf16[4,1024,512]{2,1,0:T(8,128)(2,1)}, u32[]{:S(2)}) %copy-start.5) | copy-done | bytes 4194328
  91.7 1.8 %recon.3 = bf16[128,512]{1,0:T(8,128)(2,1)} custom-call(s32[3]{0:T(128)S(1)} %pad_add_fusion.refs_0_.place, s32[1,4]{1,0:T(1,128)S(1)} %copy-done.12, s32[16]{0:T(128)S(1)} %copy-done.13, bf16[4,1024,512]{2,1,0:T(8,128)(2,1)S(1)} %copy-done.5, f32[128,512]{1,0:T(8,128)S(1)} %recon.2.refs_2_, bf16[128,1024]{1,0:T(8,128)(2,1)S(1)} %phase.3.refs_3_, ...), custom_call_target="tpu_custom_call" | custom-call | flops 268435456 | bytes 2621440 | tf_op jit(solution)/shard_map/recon/pallas_call | solution.py:326
  (2 shorter events, 0.0 us)
Async XLA Ops:
  0.0 1.6 %copy-start = (bf16[1024,1024]{1,0:T(8,128)(2,1)S(1)}, bf16[1024,1024]{1,0:T(8,128)(2,1)}, u32[]{:S(2)}) copy-start(bf16[1024,1024]{1,0:T(8,128)(2,1)} %constant.56.clone.refs_1_.table) | copy-start | bytes 6291460
  1.6 1.2 %copy-start.6 = (bf16[1,4,2,64,1024]{4,3,2,1,0:T(8,128)(2,1)S(1)}, bf16[1,4,2,64,1024]{4,3,2,1,0:T(8,128)(2,1)}, u32[]{:S(2)}) copy-start(bf16[1,4,2,64,1024]{4,3,2,1,0:T(8,128)(2,1)} %param.6) | copy-start | bytes 3145732
  2.8 6.7 %copy-start.1 = (bf16[1024,1024]{1,0:T(8,128)(2,1)S(1)}, bf16[1024,1024]{1,0:T(8,128)(2,1)}, u32[]{:S(2)}) copy-start(bf16[1024,1024]{1,0:T(8,128)(2,1)} %constant.56.clone.refs_1_.table) | copy-start | bytes 6291460
  2.8 6.7 %copy-start.7 = (bf16[1,4,2,64,1024]{4,3,2,1,0:T(8,128)(2,1)S(1)}, bf16[1,4,2,64,1024]{4,3,2,1,0:T(8,128)(2,1)}, u32[]{:S(2)}) copy-start(bf16[1,4,2,64,1024]{4,3,2,1,0:T(8,128)(2,1)} %param.6) | copy-start | bytes 3145732
  3.5 0.8 copy-start.9
  4.3 14.5 %all-to-all-start = ((bf16[8,2,64,256]{3,2,1,0:T(8,128)(2,1)}), bf16[8,2,64,256]{3,2,1,0:T(8,128)(2,1)}, u32[]{:S(2)}, u32[]{:S(2)}) async-start(bf16[8,2,64,256]{3,2,1,0:T(8,128)(2,1)} %copy-done.9), calls=%async_computation | async-start | bytes 1048576 | tf_op jit(solution)/shard_map/all_to_all | solution.py:227
  9.5 1.6 %copy-start.14 = (f32[4]{0:T(128)S(1)}, f32[4]{0:T(128)}, u32[]{:S(2)}) copy-start(f32[4]{0:T(128)} %param.7) | copy-start | bytes 52
  10.2 0.8 copy-start.8
  18.9 12.7 %all-to-all-start.3 = ((bf16[8,2,64,256]{3,2,1,0:T(8,128)(2,1)}), bf16[8,2,64,256]{3,2,1,0:T(8,128)(2,1)S(1)}, u32[]{:S(2)}, u32[]{:S(2)}) async-start(bf16[8,2,64,256]{3,2,1,0:T(8,128)(2,1)} %copy-done.8), calls=%async_computation.3 | async-start | bytes 1048576 | tf_op jit(solution)/shard_map/all_to_all | solution.py:227
  28.1 1.4 %copy-start.2 = (bf16[4,1024,256]{2,1,0:T(8,128)(2,1)}, bf16[4,1024,256]{2,1,0:T(8,128)(2,1)S(1)}, u32[]{:S(2)}) copy-start(bf16[4,1024,256]{2,1,0:T(8,128)(2,1)S(1)} %filters.1.refs_2_) | copy-start | bytes 6291460
  29.4 0.8 copy-start.10
  31.6 20.1 %all-to-all-start.1 = ((bf16[4,256,256]{2,1,0:T(8,128)(2,1)}), bf16[4,256,256]{2,1,0:T(8,128)(2,1)S(1)}, u32[]{:S(2)}, u32[]{:S(2)}) async-start(bf16[4,256,256]{2,1,0:T(8,128)(2,1)} %copy-done.10), calls=%async_computation.1 | async-start | bytes 1048576 | tf_op jit(solution)/shard_map/all_to_all | solution.py:227
  36.8 1.6 %copy-start.3 = (bf16[4,1024,256]{2,1,0:T(8,128)(2,1)S(1)}, bf16[4,1024,256]{2,1,0:T(8,128)(2,1)}, u32[]{:S(2)}) copy-start(bf16[4,1024,256]{2,1,0:T(8,128)(2,1)} %copy-done.2) | copy-start | bytes 6291460
  40.2 0.8 copy-start.11
  51.7 17.5 %all-to-all-start.4 = ((bf16[4,256,256]{2,1,0:T(8,128)(2,1)}), bf16[4,256,256]{2,1,0:T(8,128)(2,1)S(1)}, u32[]{:S(2)}, u32[]{:S(2)}) async-start(bf16[4,256,256]{2,1,0:T(8,128)(2,1)} %copy-done.11), calls=%async_computation.4 | async-start | bytes 1048576 | tf_op jit(solution)/shard_map/all_to_all | solution.py:227
  69.3 8.8 %all-to-all-start.2 = ((bf16[4,128,256]{2,1,0:T(8,128)(2,1)}), bf16[4,128,256]{2,1,0:T(8,128)(2,1)S(1)}, u32[]{:S(2)}, u32[]{:S(2)}) async-start(bf16[4,128,256]{2,1,0:T(8,128)(2,1)} %half.2), calls=%async_computation.2 | async-start | bytes 524288 | tf_op jit(solution)/shard_map/all_to_all | solution.py:227
  78.0 8.8 %all-to-all-start.5 = ((bf16[4,128,256]{2,1,0:T(8,128)(2,1)}), bf16[4,128,256]{2,1,0:T(8,128)(2,1)S(1)}, u32[]{:S(2)}, u32[]{:S(2)}) async-start(bf16[4,128,256]{2,1,0:T(8,128)(2,1)} %half.3), calls=%async_computation.5 | async-start | bytes 524288 | tf_op jit(solution)/shard_map/all_to_all | solution.py:227
  81.4 5.9 %copy-start.12 = (s32[1,4]{1,0:T(1,128)S(1)}, s32[1,4]{1,0:T(1,128)}, u32[]{:S(2)}) copy-start(s32[1,4]{1,0:T(1,128)} %order.3) | copy-start | bytes 52
  81.9 5.4 %collective-permute-start = (bf16[128,1024]{1,0:T(8,128)(2,1)S(1)}, bf16[128,1024]{1,0:T(8,128)(2,1)S(1)}, u32[]{:S(2)}, u32[]{:S(2)}) collective-permute-start(bf16[128,1024]{1,0:T(8,128)(2,1)S(1)} %phase.2.refs_1_), channel_id=1, source_target_pairs={{0,16},{16,0},{1,17},{17,1},{2,18},{18,2},{3,19},{19,3},{4,20},{20... | collective-permute-start | bytes 786440 | tf_op jit(solution)/shard_map/ppermute | solution.py:314
  86.8 3.8 %copy-start.13 = (s32[16]{0:T(128)S(1)}, s32[16]{0:T(128)}, u32[]{:S(2)}) copy-start(s32[16]{0:T(128)} %refs_0_.3) | copy-start | bytes 196
  87.2 3.3 %collective-permute-start.1 = (bf16[128,1024]{1,0:T(8,128)(2,1)S(1)}, bf16[128,1024]{1,0:T(8,128)(2,1)S(1)}, u32[]{:S(2)}, u32[]{:S(2)}) collective-permute-start(bf16[128,1024]{1,0:T(8,128)(2,1)S(1)} %phase.3.refs_3_), channel_id=1, source_target_pairs={{0,16},{16,0},{1,17},{17,1},{2,18},{18,2},{3,19},{19,3},{4,20},{20... | collective-permute-start | bytes 786440 | tf_op jit(solution)/shard_map/ppermute | solution.py:314
  87.3 2.2 %copy-start.4 = (bf16[4,1024,512]{2,1,0:T(8,128)(2,1)S(1)}, bf16[4,1024,512]{2,1,0:T(8,128)(2,1)}, u32[]{:S(2)}) copy-start(bf16[4,1024,512]{2,1,0:T(8,128)(2,1)} %refs_1_.5) | copy-start | bytes 12582916
  89.5 2.2 %copy-start.5 = (bf16[4,1024,512]{2,1,0:T(8,128)(2,1)S(1)}, bf16[4,1024,512]{2,1,0:T(8,128)(2,1)}, u32[]{:S(2)}) copy-start(bf16[4,1024,512]{2,1,0:T(8,128)(2,1)} %refs_1_.5) | copy-start | bytes 12582916

commit v5 on v3

v5 whole, which is shorter than its diff:
```python
import math

import jax
import jax.numpy as jnp
import numpy as np
from jax import lax
from jax.experimental import pallas as pl
from jax.experimental.pallas import tpu as pltpu
from jax.sharding import PartitionSpec as P

absorb_ratio = 0.1
regularizer = 0.05
bf16 = jnp.bfloat16
f32 = jnp.float32


def hartley(length):
    index = np.arange(length)
    turned = (index[:, None] * index[None, :] % length) * (2.0 * math.pi / length)
    table = (np.cos(turned) + np.sin(turned)) / math.sqrt(length)
    return table.astype(bf16)


def signed_square(index, length):
    signed = jnp.where(index < length // 2, index, index - length).astype(f32)
    return signed * signed / float(length * length)


def filters(propagation, rows_sq, cols_sq):
    first = propagation[:, None] * rows_sq[None]
    second = propagation[:, None] * cols_sq[None]
    sin_b, cos_b = jnp.sin(second), jnp.cos(second)
    with_sin = 2.0 * (cos_b - absorb_ratio * sin_b)
    with_cos = 2.0 * (sin_b + absorb_ratio * cos_b)
    transfer = (
        jnp.sin(first)[:, :, None] * with_sin[:, None, :]
        + jnp.cos(first)[:, :, None] * with_cos[:, None, :]
    )
    denom = jnp.sum(transfer * transfer, axis=0) + regularizer
    return transfer / denom


def flat_plan(holograms, propagation, weights, angle_order, slab_rows):
    mbatch, angles, dist_dev, rows_dev, width = holograms.shape
    groups = lax.axis_size("rows")
    cores = lax.axis_size("dist")
    capacity = 2 * rows_dev
    own = angles // cores
    cols = width // groups
    dists = dist_dev * cores
    device = lax.axis_index("rows")
    table = jnp.asarray(hartley(width))
    index = jnp.arange(width, dtype=jnp.int32)
    my_cols = device * cols + jnp.arange(cols, dtype=jnp.int32)
    gain = filters(propagation, signed_square(my_cols, width), signed_square(index, width))

    mine = lax.all_to_all(holograms[0], "dist", split_axis=0, concat_axis=1, tiled=True)
    flat = mine.reshape(own * dists * rows_dev, width)
    spec = jnp.einsum("kx,mx->km", table, flat, preferred_element_type=f32)
    spec = spec.astype(bf16).reshape(groups, cols, own * dists * rows_dev)
    spec = lax.all_to_all(spec, "rows", split_axis=0, concat_axis=0, tiled=True)
    spec = spec.reshape(groups, cols, own, dists, rows_dev).transpose(1, 2, 3, 0, 4)
    spec = spec.reshape(cols * own * dists, width)
    full = jnp.dot(spec, table, preferred_element_type=f32)
    full = full.reshape(cols, own, dists, width)
    full = jnp.sum(full * gain.transpose(1, 0, 2)[:, None], axis=2).astype(bf16)
    half = jnp.einsum("yq,akq->yak", table, full.transpose(1, 0, 2), preferred_element_type=f32)
    half = half.astype(bf16).reshape(groups, rows_dev, own * cols)
    half = lax.all_to_all(half, "rows", split_axis=0, concat_axis=0, tiled=True)
    half = half.reshape(groups, rows_dev, own, cols).transpose(2, 1, 0, 3)
    half = half.reshape(own * rows_dev, width)
    phase = jnp.dot(half, table, preferred_element_type=f32)
    phase = phase.astype(bf16).reshape(own, rows_dev, width)
    phase = lax.all_gather(phase, "dist", axis=0, tiled=True)
    place = (angle_order[0][None, :] == jnp.arange(angles)[:, None]).astype(bf16)
    phase = jnp.einsum("wa,ayx->wyx", place, phase, preferred_element_type=f32)
    recon = jnp.einsum(
        "wyx,wxp->yp", phase.astype(bf16), weights, preferred_element_type=f32
    ).astype(bf16)
    parity = device % 2
    offset = parity * slab_rows[device - parity]
    count = slab_rows[device]
    pairs = [(source, source ^ 1) for source in range(groups)]
    partner = lax.ppermute(recon, "rows", pairs)
    lower = jnp.where(parity == 1, partner, recon)
    upper = jnp.where(parity == 1, recon, partner)
    paired = jnp.concatenate([lower, upper], axis=0)
    slot = jnp.arange(capacity, dtype=jnp.int32)[:, None]
    source = jnp.arange(capacity, dtype=jnp.int32)[None, :]
    select = ((source == offset + slot) & (slot < count)).astype(bf16)
    return jnp.dot(select, paired, preferred_element_type=f32).astype(bf16)


def take_kernel(holo, out):
    out[...] = holo[...]


def row_kernel(inner, place, here, there, table, *outs):
    spot = place[1]
    dist_dev, rows_dev, width = here.shape[1:]
    block = width // inner
    flat = jnp.concatenate(
        [source[0].reshape(dist_dev * rows_dev, width) for source in (here, there)], axis=0
    )
    for rel in range(inner):
        part = table[:, pl.ds(pl.multiple_of((spot ^ rel) * block, block), block)]
        got = jnp.dot(flat, part, preferred_element_type=f32).astype(bf16)
        outs[rel][...] = got.reshape(2 * dist_dev, rows_dev, block)


def filter_kernel(waves_a, with_sin, with_cos, out):
    dists, width, block = out.shape
    turned = waves_a[...].T
    step = 128
    for at in range(0, width, step):
        rows = turned[at : at + step]
        transfer = [
            rows[:, d : d + 1] * with_sin[d : d + 1, :]
            + rows[:, dists + d : dists + d + 1] * with_cos[d : d + 1, :]
            for d in range(dists)
        ]
        denom = transfer[0] * transfer[0]
        for value in transfer[1:]:
            denom = denom + value * value
        scale = 1.0 / (denom + regularizer)
        for d in range(dists):
            out[d, at : at + step, :] = (transfer[d] * scale).astype(bf16)


def column_kernel(inner, outer, place, table, gain, *refs):
    pieces = refs[:inner]
    away, keep, stack, total, spectrum = refs[inner:]
    spot, plane = place[1], place[2]
    dists, rows_dev, block = pieces[0].shape
    depth = inner * rows_dev
    for rel in range(inner):
        start = pl.multiple_of((spot ^ rel) * rows_dev, rows_dev)
        for d in range(dists):
            stack[d, pl.ds(start, rows_dev), :] = pieces[rel][d]
    part = table[:, pl.ds(pl.multiple_of(plane * depth, depth), depth)]
    for d in range(dists):
        got = jnp.dot(part, stack[d], preferred_element_type=f32) * gain[d].astype(f32)
        if d == 0:
            total[...] = got
        else:
            total[...] += got
    spectrum[...] = total[...].astype(bf16)
    half = outer // 2
    side = plane // half
    for out, first in ((away, (1 - side) * half), (keep, side * half)):
        rows = pl.ds(pl.multiple_of(first * depth, half * depth), half * depth)
        got = jnp.dot(table[rows, :], spectrum[...], preferred_element_type=f32)
        out[...] = got.astype(bf16).reshape(half, depth, block)


def add_kernel(one, two, out):
    out[...] = (one[...].astype(f32) + two[...].astype(f32)).astype(bf16)


def near_kernel(place, keep, across, out):
    plane = place[2]
    which = (plane ^ 1) % 2
    inside = (plane == 1) | (plane == 2)
    more = jnp.where(inside, across[which].astype(f32), 0.0)
    out[...] = (keep[which].astype(f32) + more).astype(bf16)


def half_kernel(inner, place, *refs):
    mine, other = refs[-2:]
    own = len(refs[:-2]) // 3
    spot, plane = place[1], place[2]
    which = plane % 2
    inside = (plane == 1) | (plane == 2)
    capacity = mine.shape[1]
    for chunk in range(own):
        keep, across, last = refs[3 * chunk : 3 * chunk + 3]
        for out, pair in ((mine, spot // 2), (other, 1 - spot // 2)):
            rows = pl.ds(pl.multiple_of(pair * capacity, capacity), capacity)
            more = jnp.where(inside, across[which, rows, :].astype(f32), 0.0)
            got = keep[which, rows, :].astype(f32) + more + last[rows, :].astype(f32)
            out[chunk] = got.astype(bf16)


def phase_kernel(inner, place, table, *refs):
    pieces = refs[:inner]
    out, joined = refs[inner:]
    spot = place[1]
    own, capacity, block = pieces[0].shape
    for rel in range(inner):
        columns = pl.ds(pl.multiple_of((spot ^ rel) * block, block), block)
        joined[:, columns] = pieces[rel][...].reshape(own * capacity, block)
    got = jnp.dot(joined[...], table[...], preferred_element_type=f32)
    out[...] = got.astype(bf16).reshape(own, capacity, inner * block)


def recon_kernel(own, place, order, slabs, here, there, weights, out, total):
    step = pl.program_id(0)
    phase = jnp.where(step < own, here[0], there[0])
    got = jnp.dot(phase, weights[0], preferred_element_type=f32)

    @pl.when(step == 0)
    def _():
        total[...] = got

    @pl.when(step > 0)
    def _():
        total[...] += got

    @pl.when(step == 2 * own - 1)
    def _():
        capacity = total.shape[0]
        device = place[3]
        parity = device % 2
        offset = parity * slabs[device - parity]
        slot = lax.broadcasted_iota(jnp.int32, (capacity, capacity), 0)
        source = lax.broadcasted_iota(jnp.int32, (capacity, capacity), 1)
        select = (source == slot + offset) & (slot < slabs[device])
        select = jnp.where(select, 1.0, 0.0).astype(bf16)
        picked = jnp.dot(select, total[...].astype(bf16), preferred_element_type=f32)
        out[...] = picked.astype(bf16)


def vmem(count):
    return [pl.BlockSpec(memory_space=pltpu.VMEM)] * count


def smem(count):
    return [pl.BlockSpec(memory_space=pltpu.SMEM)] * count


def plane_plan(inner, holograms, propagation, weights, angle_order, slab_rows):
    mbatch, angles, dist_dev, rows_dev, width = holograms.shape
    groups = lax.axis_size("rows")
    cores = lax.axis_size("dist")
    outer = groups // inner
    own = angles // cores
    block = width // inner
    depth = inner * rows_dev
    dists = cores * dist_dev
    pixels = weights.shape[2]
    capacity = 2 * rows_dev
    params = pltpu.CompilerParams(vmem_limit_bytes=16 * 2**20)
    one_out = pl.BlockSpec(memory_space=pltpu.VMEM)

    def cost(flops, *arrays):
        return pl.CostEstimate(
            flops=flops, bytes_accessed=sum(2 * math.prod(a) for a in arrays), transcendentals=0
        )

    def shaped(*shape):
        return jax.ShapeDtypeStruct(shape, bf16)

    device = lax.axis_index("rows")
    core = lax.axis_index("dist")
    plane, spot = device // inner, device % inner
    place = jnp.stack([core, spot, plane, device]).astype(jnp.int32)
    table = jnp.asarray(hartley(width))

    def sent(value, target):
        pairs = []
        for c in range(cores):
            for r in range(groups):
                to_core, to_row = target(c, r)
                pairs.append((c * groups + r, to_core * groups + to_row))
        return lax.ppermute(value, ("dist", "rows"), pairs)

    def to_other_core(c, r):
        return c ^ 1, r

    def to_spot(rel):
        return lambda c, r: (c, r ^ rel)

    def to_near_plane(c, r):
        return c, (r // inner ^ 1) * inner + r % inner

    def to_middle(c, r):
        z = r // inner
        return (c, (3 - z) * inner + r % inner) if z in (1, 2) else (c ^ 1, r)

    other_angles = pl.pallas_call(
        lambda place, holo, out: take_kernel(holo, out),
        out_shape=shaped(own, dist_dev, rows_dev, width),
        grid_spec=pltpu.PrefetchScalarGridSpec(
            num_scalar_prefetch=1,
            grid=(1,),
            in_specs=[
                pl.BlockSpec(
                    (own, dist_dev, rows_dev, width), lambda i, place: (place[0] ^ 1, 0, 0, 0)
                )
            ],
            out_specs=one_out,
        ),
        compiler_params=params,
        cost_estimate=cost(0, (2, own, dist_dev, rows_dev, width)),
        name="other_angles",
    )(place, holograms[0])
    partner = sent(other_angles, to_other_core)

    arrived = []
    for chunk in range(own):
        pieces = pl.pallas_call(
            lambda *refs: row_kernel(inner, *refs),
            out_shape=[shaped(dists, rows_dev, block)] * inner,
            grid_spec=pltpu.PrefetchScalarGridSpec(
                num_scalar_prefetch=1,
                grid=(1,),
                in_specs=[
                    pl.BlockSpec(
                        (1, dist_dev, rows_dev, width),
                        lambda i, place, chunk=chunk: (place[0] * own + chunk, 0, 0, 0),
                    ),
                    pl.BlockSpec(
                        (1, dist_dev, rows_dev, width), lambda i, place, chunk=chunk: (chunk, 0, 0, 0)
                    ),
                ]
                + vmem(1),
                out_specs=vmem(inner),
            ),
            compiler_params=params,
            cost_estimate=cost(
                2 * dists * rows_dev * width * width, (width, width), (2, dists, rows_dev, width)
            ),
            name="row_spectra",
        )(place, holograms[0], partner, table)
        arrived.append([pieces[0]] + [sent(pieces[rel], to_spot(rel)) for rel in range(1, inner)])

    index = jnp.arange(width, dtype=jnp.int32)
    my_cols = spot * block + jnp.arange(block, dtype=jnp.int32)
    ordered = jnp.concatenate(
        [
            lax.dynamic_slice_in_dim(propagation, (core ^ other) * dist_dev, dist_dev, 0)
            for other in range(cores)
        ]
    )
    first = ordered[:, None] * signed_square(index, width)[None]
    second = ordered[:, None] * signed_square(my_cols, width)[None]
    sin_b, cos_b = jnp.sin(second), jnp.cos(second)
    gain = pl.pallas_call(
        filter_kernel,
        out_shape=shaped(dists, width, block),
        in_specs=vmem(3),
        out_specs=one_out,
        compiler_params=params,
        cost_estimate=cost(32 * width * block, (dists, width, block)),
        name="filters",
    )(
        jnp.concatenate([jnp.sin(first), jnp.cos(first)], axis=0),
        2.0 * (cos_b - absorb_ratio * sin_b),
        2.0 * (sin_b + absorb_ratio * cos_b),
    )

    sums = []
    for chunk in range(own):
        away, keep = pl.pallas_call(
            lambda *refs: column_kernel(inner, outer, *refs),
            out_shape=[shaped(outer // 2, depth, block)] * 2,
            in_specs=smem(1) + vmem(2 + inner),
            out_specs=vmem(2),
            scratch_shapes=[
                pltpu.VMEM((dists, depth, block), bf16),
                pltpu.VMEM((width, block), f32),
                pltpu.VMEM((width, block), bf16),
            ],
            compiler_params=params,
            cost_estimate=cost(
                2 * width * block * (dists * depth + width), (width, width), (dists, width, block)
            ),
            name="columns",
        )(place, table, gain, *arrived[chunk])
        joint = pl.pallas_call(
            add_kernel,
            out_shape=shaped(outer // 2, depth, block),
            in_specs=vmem(2),
            out_specs=one_out,
            compiler_params=params,
            cost_estimate=cost(outer * depth * block, (3, outer // 2, depth, block)),
            name="joint",
        )(away, sent(away, to_near_plane))
        across = sent(joint, to_middle)
        near = pl.pallas_call(
            near_kernel,
            out_shape=shaped(depth, block),
            in_specs=smem(1) + vmem(2),
            out_specs=one_out,
            compiler_params=params,
            cost_estimate=cost(depth * block, (3, depth, block)),
            name="near",
        )(place, keep, across)
        sums += [keep, across, sent(near, to_near_plane)]

    mine, other = pl.pallas_call(
        lambda *refs: half_kernel(inner, *refs),
        out_shape=[shaped(own, capacity, block)] * 2,
        in_specs=smem(1) + vmem(len(sums)),
        out_specs=vmem(2),
        compiler_params=params,
        cost_estimate=cost(own * depth * block, (5, own, depth, block)),
        name="half",
    )(place, *sums)
    pieces = [mine] + [sent(mine if rel < 2 else other, to_spot(rel)) for rel in range(1, inner)]
    phase = pl.pallas_call(
        lambda *refs: phase_kernel(inner, *refs),
        out_shape=shaped(own, capacity, width),
        in_specs=smem(1) + vmem(1 + inner),
        out_specs=one_out,
        scratch_shapes=[pltpu.VMEM((own * capacity, width), bf16)],
        compiler_params=params,
        cost_estimate=cost(
            2 * own * capacity * width * width, (width, width), (2, own, capacity, width)
        ),
        name="phase",
    )(place, table, *pieces)
    there = sent(phase, to_other_core)

    def angle_of(step, place):
        return (place[0] ^ (step // own)) * own + step % own

    return pl.pallas_call(
        lambda *refs: recon_kernel(own, *refs),
        out_shape=shaped(capacity, pixels),
        grid_spec=pltpu.PrefetchScalarGridSpec(
            num_scalar_prefetch=3,
            grid=(angles,),
            in_specs=[
                pl.BlockSpec(
                    (1, capacity, width), lambda i, place, order, slabs: (jnp.minimum(i, own - 1), 0, 0)
                ),
                pl.BlockSpec(
                    (1, capacity, width), lambda i, place, order, slabs: (jnp.maximum(i - own, 0), 0, 0)
                ),
                pl.BlockSpec(
                    (1, width, pixels),
                    lambda i, place, order, slabs: (order[angle_of(i, place)], 0, 0),
                ),
            ],
            out_specs=one_out,
            scratch_shapes=[pltpu.VMEM((capacity, pixels), f32)],
        ),
        compiler_params=params,
        cost_estimate=cost(
            2 * angles * capacity * width * pixels, (angles, width, capacity + pixels)
        ),
        name="recon",
    )(place, angle_order[0], slab_rows, phase, there, weights)


def on_device(holograms, propagation, weights, angle_order, slab_rows):
    mbatch, angles, dist_dev, rows_dev, width = holograms.shape
    groups = lax.axis_size("rows")
    inner = 2 ** (int(math.log2(groups)) // 2)
    block = width // inner
    fits = (
        inner * (groups // inner) == groups
        and rows_dev % 16 == 0
        and block % 128 == 0
        and inner * rows_dev % 128 == 0
        and inner == 4
        and groups == inner * inner
        and lax.axis_size("dist") == 2
    )
    if fits:
        return plane_plan(inner, holograms, propagation, weights, angle_order, slab_rows)
    return flat_plan(holograms, propagation, weights, angle_order, slab_rows)


def solution(mesh):
    return jax.shard_map(
        on_device,
        mesh=mesh,
        in_specs=(P(None, None, "dist", "rows", None), P(), P(None, None, "dist"), P(), P()),
        out_specs=P("rows", "dist"),
        check_vma=False,
    )
```

time: 71.7 us -> 61.5 us (0.86)
  starting transfers between devices: 36.2 us -> 24.4 us
  waiting for transfers between devices: 7.01 us -> 17.8 us
  other arithmetic: 9.79 us -> 0.5 us
    ppermute x6 -> x0, starting transfers between devices: 18.2 us -> none  [moved(): lax.ppermute(value, 'rows', [(a * inner + i, b * inner + i) for a, b in s...]
    ppermute x15 -> x17, waiting for transfers between devices: 2.58 us -> 17.8 us  [sent(): return lax.ppermute(value, ('dist', 'rows'), pairs)]
    convert_element_type x9 -> x0, other arithmetic: 7.67 us -> none  [the longest x1 3.33 us: plane_plan(): filters(ordered, signed_square(index, width), signed_square(my_cols, width))]
    ppermute x15 -> x17, starting transfers between devices: 18 us -> 24.4 us  [sent(): return lax.ppermute(value, ('dist', 'rows'), pairs)]
    ppermute x6 -> x0, waiting for transfers between devices: 4.43 us -> none  [moved(): lax.ppermute(value, 'rows', [(a * inner + i, b * inner + i) for a, b in s...]
    dynamic_slice x5 -> x0, local copies, waits for them, and re-layouts: 2.11 us -> none  [the longest x1 2.02 us: plane_plan(): lax.dynamic_slice_in_dim(holograms[0], (core ^ 1) * own, own, 0)]
    unnamed x18 -> x14, local copies, waits for them, and re-layouts: 0.82 us -> 2.84 us
    reduce_sum x1 -> x0, other arithmetic: 1.53 us -> none  [filters(): denom = jnp.sum(transfer * transfer, axis=0) + regularizer]
  transfers between devices with their start and end apart: 21 -> 17, of which waited for: 5 -> 9; matrix products, arithmetic and copies ran while one was open for 15% -> 2% of each run, Pallas kernels for 13% -> 13%
where the time goes in v5:
time: 61.5 us; the launch traced here: 61.3 us
  starting transfers between devices  24.4 us (40%)
  waiting for transfers between devices  17.8 us (29%)
  Pallas kernels  14.7 us (24%)
  local copies, waits for them, and re-layouts  3.65 us (6%)
    ppermute x17, starting transfers between devices, sent(): return lax.ppermute(value, ('dist', 'rows'), pairs)  24.4 us
    ppermute x17, waiting for transfers between devices, sent(): return lax.ppermute(value, ('dist', 'rows'), pairs)  17.8 us
    pallas_call x2, Pallas kernels, plane_plan(): pl.pallas_call(lambda *refs: column_kernel(inner, outer, *refs), out_shap...  3.7 us
    unnamed x14, local copies, waits for them, and re-layouts  2.84 us
    pallas_call x1, Pallas kernels, plane_plan(): pl.pallas_call(lambda *refs: recon_kernel(own, *refs), out_shape=shaped(c...  2.8 us
    pallas_call x2, Pallas kernels, plane_plan(): pl.pallas_call(lambda *refs: row_kernel(inner, *refs), out_shape=[shaped(...  2.58 us
    pallas_call x1, Pallas kernels, plane_plan(): pl.pallas_call(filter_kernel, out_shape=shaped(dists, width, block), in_s...  1.78 us
    pallas_call x1, Pallas kernels, plane_plan(): pl.pallas_call(lambda *refs: phase_kernel(inner, *refs), out_shape=shaped...  1.3 us
  transfers between devices with their start and end apart: 17, of which 9 were waited for; matrix products, arithmetic and copies ran while one was open for 2% of the time, Pallas kernels for 13%

profile of v5, /device:TPU:0, one launch (start us, length us, event | category | flops | bytes accessed | tf_op | source)
XLA Modules:
  0.0 61.3 jit_solution(12003732867874621050)
XLA Ops:
  0.0 0.1 pad_add_fusion.place.refs_0_
  0.1 0.0 copy-start.2
  0.1 1.2 %copy-done.2 = bf16[1,4,2,64,1024]{4,3,2,1,0:T(8,128)(2,1)S(1)} copy-done((bf16[1,4,2,64,1024]{4,3,2,1,0:T(8,128)(2,1)S(1)}, bf16[1,4,2,64,1024]{4,3,2,1,0:T(8,128)(2,1)}, u32[]{:S(2)}) %copy-start.2) | copy-done | bytes 1048600
  1.3 0.0 copy-start.3
  1.3 0.6 other_angles.1
  1.9 0.5 collective-permute-start
  2.4 0.8 %fusion.12 = (f32[2]{0:T(128)S(1)}, f32[2]{0:T(128)S(1)}) fusion(f32[4]{0:T(128)} %param.7, s32[]{:T(128)S(6)} %select_n.35, s32[]{:T(128)S(6)} %select_n.36), kind=kLoop, calls=%fused_computation.21 | loop fusion | bytes 40 | tf_op jit(solution)/shard_map/dynamic_slice | solution.py:331
  3.2 0.1 pad_maximum_fusion.1
  3.3 0.2 multiply_sine_fusion
  3.5 0.4 collective-permute-done.refs_2_
  3.9 0.0 copy-done.3
  4.0 1.6 %copy-done = bf16[1024,1024]{1,0:T(8,128)(2,1)S(1)} copy-done((bf16[1024,1024]{1,0:T(8,128)(2,1)S(1)}, bf16[1024,1024]{1,0:T(8,128)(2,1)}, u32[]{:S(2)}) %copy-start) | copy-done | bytes 2097176
  5.5 1.3 %row_spectra.3 = (bf16[4,64,256]{2,1,0:T(8,128)(2,1)S(1)}, bf16[4,64,256]{2,1,0:T(8,128)(2,1)S(1)}, bf16[4,64,256]{2,1,0:T(8,128)(2,1)S(1)}, bf16[4,64,256]{2,1,0:T(8,128)(2,1)S(1)}) custom-call(s32[4]{0:T(128)S(1)} %pad_add_fusion.place.refs_0_, bf16[4,2,64,1024]{3,2,1,0:T(8,128)(2,1)S(1)} %bitcast.7, ...), custom_call_target="tpu_custom_call" | custom-call | flops 536870912 | bytes 3145728 | tf_op jit(solution)/shard_map/row_spectra/pallas_call | solution.py:301
  6.8 2.9 %collective-permute-start.7 = (bf16[4,64,256]{2,1,0:T(8,128)(2,1)S(1)}, bf16[4,64,256]{2,1,0:T(8,128)(2,1)S(1)}, u32[]{:S(2)}, u32[]{:S(2)}) collective-permute-start(bf16[4,64,256]{2,1,0:T(8,128)(2,1)S(1)} %get-tuple-element.26), channel_id=1, source_target_pairs={{0,1},{1,0},{2,3},{3,2},{4,5},{5,4},{6,7},{7,6},{8,9},{9,8},{10,11... | collective-permute-start | bytes 393224 | tf_op jit(solution)/shard_map/ppermute | solution.py:265
  9.8 0.1 fusion.5
  9.9 1.6 %collective-permute-start.8 = (bf16[4,64,256]{2,1,0:T(8,128)(2,1)S(1)}, bf16[4,64,256]{2,1,0:T(8,128)(2,1)S(1)}, u32[]{:S(2)}, u32[]{:S(2)}) collective-permute-start(bf16[4,64,256]{2,1,0:T(8,128)(2,1)S(1)} %get-tuple-element.27), channel_id=1, source_target_pairs={{0,2},{1,3},{2,0},{3,1},{4,6},{5,7},{6,4},{7,5},{8,10},{9,11},{10,... | collective-permute-start | bytes 393224 | tf_op jit(solution)/shard_map/ppermute | solution.py:265
  11.5 0.1 collective-permute-start.9
  11.5 1.3 %row_spectra.2 = (bf16[4,64,256]{2,1,0:T(8,128)(2,1)S(1)}, bf16[4,64,256]{2,1,0:T(8,128)(2,1)S(1)}, bf16[4,64,256]{2,1,0:T(8,128)(2,1)S(1)}, bf16[4,64,256]{2,1,0:T(8,128)(2,1)S(1)}) custom-call(s32[4]{0:T(128)S(1)} %pad_add_fusion.place.refs_0_, bf16[4,2,64,1024]{3,2,1,0:T(8,128)(2,1)S(1)} %bitcast.8, ...), custom_call_target="tpu_custom_call" | custom-call | flops 536870912 | bytes 3145728 | tf_op jit(solution)/shard_map/row_spectra/pallas_call | solution.py:301
  12.8 2.0 %collective-permute-start.1 = (bf16[4,64,256]{2,1,0:T(8,128)(2,1)S(1)}, bf16[4,64,256]{2,1,0:T(8,128)(2,1)S(1)}, u32[]{:S(2)}, u32[]{:S(2)}) collective-permute-start(bf16[4,64,256]{2,1,0:T(8,128)(2,1)S(1)} %get-tuple-element.20), channel_id=1, source_target_pairs={{0,1},{1,0},{2,3},{3,2},{4,5},{5,4},{6,7},{7,6},{8,9},{9,8},{10,11... | collective-permute-start | bytes 393224 | tf_op jit(solution)/shard_map/ppermute | solution.py:265
  14.8 1.5 %collective-permute-start.2 = (bf16[4,64,256]{2,1,0:T(8,128)(2,1)S(1)}, bf16[4,64,256]{2,1,0:T(8,128)(2,1)S(1)}, u32[]{:S(2)}, u32[]{:S(2)}) collective-permute-start(bf16[4,64,256]{2,1,0:T(8,128)(2,1)S(1)} %get-tuple-element.21), channel_id=1, source_target_pairs={{0,2},{1,3},{2,0},{3,1},{4,6},{5,7},{6,4},{7,5},{8,10},{9,11},{10,... | collective-permute-start | bytes 393224 | tf_op jit(solution)/shard_map/ppermute | solution.py:265
  16.3 0.0 collective-permute-done.7.refs_4_
  16.3 0.7 %collective-permute-start.3 = (bf16[4,64,256]{2,1,0:T(8,128)(2,1)S(1)}, bf16[4,64,256]{2,1,0:T(8,128)(2,1)S(1)}, u32[]{:S(2)}, u32[]{:S(2)}) collective-permute-start(bf16[4,64,256]{2,1,0:T(8,128)(2,1)S(1)} %get-tuple-element.22), channel_id=1, source_target_pairs={{0,3},{1,2},{2,1},{3,0},{4,7},{5,6},{6,5},{7,4},{8,11},{9,10},{10,... | collective-permute-start | bytes 393224 | tf_op jit(solution)/shard_map/ppermute | solution.py:265
  17.1 1.8 %filters.1.refs_2_ = bf16[4,1024,256]{2,1,0:T(8,128)(2,1)S(1)} custom-call(f32[8,1024]{1,0:T(8,128)S(1)} %pad_maximum_fusion.waves_a, f32[4,256]{1,0:T(4,128)S(1)} %get-tuple-element.36.with_sin, f32[4,256]{1,0:T(4,128)S(1)} %get-tuple-element.35.with_cos), custom_call_target="tpu_custom_call" | custom-call | flops 8388608 | bytes 2097152 | tf_op jit(solution)/shard_map/filters/pallas_call | solution.py:338
  18.9 0.0 collective-permute-done.8.refs_5_
  18.9 0.0 collective-permute-done.9.refs_6_
  18.9 0.0 copy-done.1
  18.9 1.9 %columns.3 = (bf16[2,256,256]{2,1,0:T(8,128)(2,1)S(1)}, bf16[2,256,256]{2,1,0:T(8,128)(2,1)S(1)}) custom-call(s32[4]{0:T(128)S(1)} %pad_add_fusion.place.refs_0_, bf16[1024,1024]{1,0:T(8,128)(2,1)S(1)} %copy-done.1, bf16[4,1024,256]{2,1,0:T(8,128)(2,1)S(1)} %filters.1.refs_2_, bf16[4,64,256]{2,1,0:T(8,128)(2,1)S(1)} %get-tuple-element.25.refs_3_, ...), custom_call_target="tpu_custom_call" | custom-call | flops 1073741824 | bytes 4194304 | tf_op jit(solution)/shard_map/columns/pallas_call | solution.py:354
  20.7 1.7 %collective-permute-start.10 = (bf16[2,256,256]{2,1,0:T(8,128)(2,1)S(1)}, bf16[2,256,256]{2,1,0:T(8,128)(2,1)S(1)}, u32[]{:S(2)}, u32[]{:S(2)}) collective-permute-start(bf16[2,256,256]{2,1,0:T(8,128)(2,1)S(1)} %get-tuple-element.30.one), channel_id=1, source_target_pairs={{0,4},{1,5},{2,6},{3,7},{4,0},{5,1},{6,2},{7,3},{8,12},{9,13},{10,... | collective-permute-start | bytes 786440 | tf_op jit(solution)/shard_map/ppermute | solution.py:265
  22.4 0.0 collective-permute-done.1.refs_4_
  22.4 1.2 %collective-permute-done.2.refs_5_ = bf16[4,64,256]{2,1,0:T(8,128)(2,1)S(1)} collective-permute-done((bf16[4,64,256]{2,1,0:T(8,128)(2,1)S(1)}, bf16[4,64,256]{2,1,0:T(8,128)(2,1)S(1)}, u32[]{:S(2)}, u32[]{:S(2)}) %collective-permute-start.2) | collective-permute-done | bytes 131104 | tf_op jit(solution)/shard_map/ppermute | solution.py:265
  23.6 0.0 collective-permute-done.3.refs_6_
  23.6 1.8 %columns.2 = (bf16[2,256,256]{2,1,0:T(8,128)(2,1)S(1)}, bf16[2,256,256]{2,1,0:T(8,128)(2,1)S(1)}) custom-call(s32[4]{0:T(128)S(1)} %pad_add_fusion.place.refs_0_, bf16[1024,1024]{1,0:T(8,128)(2,1)S(1)} %copy-done.1, bf16[4,1024,256]{2,1,0:T(8,128)(2,1)S(1)} %filters.1.refs_2_, bf16[4,64,256]{2,1,0:T(8,128)(2,1)S(1)} %get-tuple-element.19.refs_3_, ...), custom_call_target="tpu_custom_call" | custom-call | flops 1073741824 | bytes 4194304 | tf_op jit(solution)/shard_map/columns/pallas_call | solution.py:354
  25.5 1.7 %collective-permute-start.4 = (bf16[2,256,256]{2,1,0:T(8,128)(2,1)S(1)}, bf16[2,256,256]{2,1,0:T(8,128)(2,1)S(1)}, u32[]{:S(2)}, u32[]{:S(2)}) collective-permute-start(bf16[2,256,256]{2,1,0:T(8,128)(2,1)S(1)} %get-tuple-element.24.one), channel_id=1, source_target_pairs={{0,4},{1,5},{2,6},{3,7},{4,0},{5,1},{6,2},{7,3},{8,12},{9,13},{10,... | collective-permute-start | bytes 786440 | tf_op jit(solution)/shard_map/ppermute | solution.py:265
  27.2 0.6 collective-permute-done.10.two
  27.7 0.1 joint.3
  27.8 0.1 collective-permute-start.11
  27.9 5.0 %collective-permute-done.4.two = bf16[2,256,256]{2,1,0:T(8,128)(2,1)S(1)} collective-permute-done((bf16[2,256,256]{2,1,0:T(8,128)(2,1)S(1)}, bf16[2,256,256]{2,1,0:T(8,128)(2,1)S(1)}, u32[]{:S(2)}, u32[]{:S(2)}) %collective-permute-start.4) | collective-permute-done | bytes 262176 | tf_op jit(solution)/shard_map/ppermute | solution.py:265
  32.9 0.1 joint.2
  32.9 0.1 collective-permute-start.5
  33.0 0.0 collective-permute-done.11.across.refs_5_
  33.0 0.6 near.3
  33.6 3.3 %collective-permute-start.12 = (bf16[256,256]{1,0:T(8,128)(2,1)S(1)}, bf16[256,256]{1,0:T(8,128)(2,1)S(1)}, u32[]{:S(2)}, u32[]{:S(2)}) collective-permute-start(bf16[256,256]{1,0:T(8,128)(2,1)S(1)} %near.3), channel_id=1, source_target_pairs={{0,4},{1,5},{2,6},{3,7},{4,0},{5,1},{6,2},{7,3},{8,12},{9,13},{10,... | collective-permute-start | bytes 393224 | tf_op jit(solution)/shard_map/ppermute | solution.py:265
  36.9 0.0 collective-permute-done.5.across.refs_2_
  36.9 0.6 near.2
  37.5 0.0 copy-start.4
  37.5 0.0 copy-start.5
  37.5 0.0 copy-start.6
  37.5 4.6 %collective-permute-start.6 = (bf16[256,256]{1,0:T(8,128)(2,1)S(1)}, bf16[256,256]{1,0:T(8,128)(2,1)S(1)}, u32[]{:S(2)}, u32[]{:S(2)}) collective-permute-start(bf16[256,256]{1,0:T(8,128)(2,1)S(1)} %near.2), channel_id=1, source_target_pairs={{0,4},{1,5},{2,6},{3,7},{4,0},{5,1},{6,2},{7,3},{8,12},{9,13},{10,... | collective-permute-start | bytes 393224 | tf_op jit(solution)/shard_map/ppermute | solution.py:265
  42.1 0.0 collective-permute-done.12.refs_6_
  42.1 2.9 %collective-permute-done.6.refs_3_ = bf16[256,256]{1,0:T(8,128)(2,1)S(1)} collective-permute-done((bf16[256,256]{1,0:T(8,128)(2,1)S(1)}, bf16[256,256]{1,0:T(8,128)(2,1)S(1)}, u32[]{:S(2)}, u32[]{:S(2)}) %collective-permute-start.6) | collective-permute-done | bytes 131104 | tf_op jit(solution)/shard_map/ppermute | solution.py:265
  45.1 0.7 %half.1 = (bf16[2,128,256]{2,1,0:T(8,128)(2,1)S(1)}, bf16[2,128,256]{2,1,0:T(8,128)(2,1)S(1)}) custom-call(s32[4]{0:T(128)S(1)} %pad_add_fusion.place.refs_0_, bf16[2,256,256]{2,1,0:T(8,128)(2,1)S(1)} %get-tuple-element.23.keep.refs_1_, bf16[2,256,256]{2,1,0:T(8,128)(2,1)S(1)} %collective-permute-done.5.across.refs_2_, ...), custom_call_target="tpu_custom_call" | custom-call | flops 131072 | bytes 1310720 | tf_op jit(solution)/shard_map/half/pallas_call | solution.py:391
  45.8 1.5 %collective-permute-start.13 = (bf16[2,128,256]{2,1,0:T(8,128)(2,1)S(1)}, bf16[2,128,256]{2,1,0:T(8,128)(2,1)S(1)}, u32[]{:S(2)}, u32[]{:S(2)}) collective-permute-start(bf16[2,128,256]{2,1,0:T(8,128)(2,1)S(1)} %get-tuple-element.31.refs_2_), channel_id=1, source_target_pairs={{0,1},{1,0},{2,3},{3,2},{4,5},{5,4},{6,7},{7,6},{8,9},{9,8},{10,11... | collective-permute-start | bytes 393224 | tf_op jit(solution)/shard_map/ppermute | solution.py:265
  47.2 2.2 %collective-permute-start.15 = (bf16[2,128,256]{2,1,0:T(8,128)(2,1)S(1)}, bf16[2,128,256]{2,1,0:T(8,128)(2,1)S(1)}, u32[]{:S(2)}, u32[]{:S(2)}) collective-permute-start(bf16[2,128,256]{2,1,0:T(8,128)(2,1)S(1)} %get-tuple-element.32), channel_id=1, source_target_pairs={{0,3},{1,2},{2,1},{3,0},{4,7},{5,6},{6,5},{7,4},{8,11},{9,10},{10,... | collective-permute-start | bytes 393224 | tf_op jit(solution)/shard_map/ppermute | solution.py:265
  49.4 0.0 collective-permute-start.14
  49.4 1.9 %collective-permute-done.13.refs_3_ = bf16[2,128,256]{2,1,0:T(8,128)(2,1)S(1)} collective-permute-done((bf16[2,128,256]{2,1,0:T(8,128)(2,1)S(1)}, bf16[2,128,256]{2,1,0:T(8,128)(2,1)S(1)}, u32[]{:S(2)}, u32[]{:S(2)}) %collective-permute-start.13) | collective-permute-done | bytes 131104 | tf_op jit(solution)/shard_map/ppermute | solution.py:265
  51.3 2.5 %collective-permute-done.15.refs_5_ = bf16[2,128,256]{2,1,0:T(8,128)(2,1)S(1)} collective-permute-done((bf16[2,128,256]{2,1,0:T(8,128)(2,1)S(1)}, bf16[2,128,256]{2,1,0:T(8,128)(2,1)S(1)}, u32[]{:S(2)}, u32[]{:S(2)}) %collective-permute-start.15) | collective-permute-done | bytes 131104 | tf_op jit(solution)/shard_map/ppermute | solution.py:265
  53.8 1.3 %collective-permute-done.14.refs_4_ = bf16[2,128,256]{2,1,0:T(8,128)(2,1)S(1)} collective-permute-done((bf16[2,128,256]{2,1,0:T(8,128)(2,1)S(1)}, bf16[2,128,256]{2,1,0:T(8,128)(2,1)S(1)}, u32[]{:S(2)}, u32[]{:S(2)}) %collective-permute-start.14) | collective-permute-done | bytes 131104 | tf_op jit(solution)/shard_map/ppermute | solution.py:265
  55.2 1.3 %phase.1.refs_3_ = bf16[2,128,1024]{2,1,0:T(8,128)(2,1)S(1)} custom-call(s32[4]{0:T(128)S(1)} %pad_add_fusion.place.refs_0_, bf16[1024,1024]{1,0:T(8,128)(2,1)S(1)} %copy-done.1, bf16[2,128,256]{2,1,0:T(8,128)(2,1)S(1)} %get-tuple-element.31.refs_2_, bf16[2,128,256]{2,1,0:T(8,128)(2,1)S(1)} %collective-permute-done.13.refs_3_, ...), custom_call_target="tpu_custom_call" | custom-call | flops 536870912 | bytes 3145728 | tf_op jit(solution)/shard_map/phase/pallas_call | solution.py:401
  56.5 0.1 collective-permute-start.16
  56.6 1.9 %collective-permute-done.16.refs_4_ = bf16[2,128,1024]{2,1,0:T(8,128)(2,1)S(1)} collective-permute-done((bf16[2,128,1024]{2,1,0:T(8,128)(2,1)S(1)}, bf16[2,128,1024]{2,1,0:T(8,128)(2,1)S(1)}, u32[]{:S(2)}, u32[]{:S(2)}) %collective-permute-start.16) | collective-permute-done | bytes 524320 | tf_op jit(solution)/shard_map/ppermute | solution.py:265
  58.5 0.0 copy-done.4
  58.5 0.0 copy-done.5
  58.5 0.0 copy-done.6
  58.5 2.8 %recon.1 = bf16[128,512]{1,0:T(8,128)(2,1)} custom-call(s32[4]{0:T(128)S(1)} %pad_add_fusion.place.refs_0_, s32[4]{0:T(128)S(1)} %bitcast.9, s32[16]{0:T(128)S(1)} %copy-done.6, bf16[2,128,1024]{2,1,0:T(8,128)(2,1)S(1)} %phase.1.refs_3_, bf16[2,128,1024]{2,1,0:T(8,128)(2,1)S(1)} %collective-permute-done.16.refs_4_, bf16[4,1024,512]{2,1,0:T(8,128)(2,1)S(1)} %copy-done.4), custom_call_target="tpu_custom_call" | custom-call | flops 536870912 | bytes 5242880 | tf_op jit(solution)/shard_map/recon/pallas_call | solution.py:418
  (5 shorter events, 0.0 us)
Async XLA Ops:
  0.1 1.2 %copy-start.2 = (bf16[1,4,2,64,1024]{4,3,2,1,0:T(8,128)(2,1)S(1)}, bf16[1,4,2,64,1024]{4,3,2,1,0:T(8,128)(2,1)}, u32[]{:S(2)}) copy-start(bf16[1,4,2,64,1024]{4,3,2,1,0:T(8,128)(2,1)} %param.6) | copy-start | bytes 3145732
  1.3 2.6 %copy-start.3 = (bf16[1,4,2,64,1024]{4,3,2,1,0:T(8,128)(2,1)S(1)}, bf16[1,4,2,64,1024]{4,3,2,1,0:T(8,128)(2,1)}, u32[]{:S(2)}) copy-start(bf16[1,4,2,64,1024]{4,3,2,1,0:T(8,128)(2,1)} %param.6) | copy-start | bytes 3145732
  1.9 2.1 %collective-permute-start = (bf16[2,2,64,1024]{3,2,1,0:T(8,128)(2,1)S(1)}, bf16[2,2,64,1024]{3,2,1,0:T(8,128)(2,1)S(1)}, u32[]{:S(2)}, u32[]{:S(2)}) collective-permute-start(bf16[2,2,64,1024]{3,2,1,0:T(8,128)(2,1)S(1)} %other_angles.1), channel_id=1, source_target_pairs={{0,16},{1,17},{2,18},{3,19},{4,20},{5,21},{6,22},{7,23},{8,24},{9,... | collective-permute-start | bytes 1572872 | tf_op jit(solution)/shard_map/ppermute | solution.py:265
  4.0 1.6 %copy-start = (bf16[1024,1024]{1,0:T(8,128)(2,1)S(1)}, bf16[1024,1024]{1,0:T(8,128)(2,1)}, u32[]{:S(2)}) copy-start(bf16[1024,1024]{1,0:T(8,128)(2,1)} %constant.59.clone.refs_3_.refs_1_) | copy-start | bytes 6291460
  6.8 9.5 %collective-permute-start.7 = (bf16[4,64,256]{2,1,0:T(8,128)(2,1)S(1)}, bf16[4,64,256]{2,1,0:T(8,128)(2,1)S(1)}, u32[]{:S(2)}, u32[]{:S(2)}) collective-permute-start(bf16[4,64,256]{2,1,0:T(8,128)(2,1)S(1)} %get-tuple-element.26), channel_id=1, source_target_pairs={{0,1},{1,0},{2,3},{3,2},{4,5},{5,4},{6,7},{7,6},{8,9},{9,8},{10,11... | collective-permute-start | bytes 393224 | tf_op jit(solution)/shard_map/ppermute | solution.py:265
  9.9 9.0 %collective-permute-start.8 = (bf16[4,64,256]{2,1,0:T(8,128)(2,1)S(1)}, bf16[4,64,256]{2,1,0:T(8,128)(2,1)S(1)}, u32[]{:S(2)}, u32[]{:S(2)}) collective-permute-start(bf16[4,64,256]{2,1,0:T(8,128)(2,1)S(1)} %get-tuple-element.27), channel_id=1, source_target_pairs={{0,2},{1,3},{2,0},{3,1},{4,6},{5,7},{6,4},{7,5},{8,10},{9,11},{10,... | collective-permute-start | bytes 393224 | tf_op jit(solution)/shard_map/ppermute | solution.py:265
  11.5 7.4 %copy-start.1 = (bf16[1024,1024]{1,0:T(8,128)(2,1)S(1)}, bf16[1024,1024]{1,0:T(8,128)(2,1)}, u32[]{:S(2)}) copy-start(bf16[1024,1024]{1,0:T(8,128)(2,1)} %constant.59.clone.refs_3_.refs_1_) | copy-start | bytes 6291460
  11.5 7.4 %collective-permute-start.9 = (bf16[4,64,256]{2,1,0:T(8,128)(2,1)S(1)}, bf16[4,64,256]{2,1,0:T(8,128)(2,1)S(1)}, u32[]{:S(2)}, u32[]{:S(2)}) collective-permute-start(bf16[4,64,256]{2,1,0:T(8,128)(2,1)S(1)} %get-tuple-element.28), channel_id=1, source_target_pairs={{0,3},{1,2},{2,1},{3,0},{4,7},{5,6},{6,5},{7,4},{8,11},{9,10},{10,... | collective-permute-start | bytes 393224 | tf_op jit(solution)/shard_map/ppermute | solution.py:265
  12.8 9.6 %collective-permute-start.1 = (bf16[4,64,256]{2,1,0:T(8,128)(2,1)S(1)}, bf16[4,64,256]{2,1,0:T(8,128)(2,1)S(1)}, u32[]{:S(2)}, u32[]{:S(2)}) collective-permute-start(bf16[4,64,256]{2,1,0:T(8,128)(2,1)S(1)} %get-tuple-element.20), channel_id=1, source_target_pairs={{0,1},{1,0},{2,3},{3,2},{4,5},{5,4},{6,7},{7,6},{8,9},{9,8},{10,11... | collective-permute-start | bytes 393224 | tf_op jit(solution)/shard_map/ppermute | solution.py:265
  14.8 8.8 %collective-permute-start.2 = (bf16[4,64,256]{2,1,0:T(8,128)(2,1)S(1)}, bf16[4,64,256]{2,1,0:T(8,128)(2,1)S(1)}, u32[]{:S(2)}, u32[]{:S(2)}) collective-permute-start(bf16[4,64,256]{2,1,0:T(8,128)(2,1)S(1)} %get-tuple-element.21), channel_id=1, source_target_pairs={{0,2},{1,3},{2,0},{3,1},{4,6},{5,7},{6,4},{7,5},{8,10},{9,11},{10,... | collective-permute-start | bytes 393224 | tf_op jit(solution)/shard_map/ppermute | solution.py:265
  16.3 7.3 %collective-permute-start.3 = (bf16[4,64,256]{2,1,0:T(8,128)(2,1)S(1)}, bf16[4,64,256]{2,1,0:T(8,128)(2,1)S(1)}, u32[]{:S(2)}, u32[]{:S(2)}) collective-permute-start(bf16[4,64,256]{2,1,0:T(8,128)(2,1)S(1)} %get-tuple-element.22), channel_id=1, source_target_pairs={{0,3},{1,2},{2,1},{3,0},{4,7},{5,6},{6,5},{7,4},{8,11},{9,10},{10,... | collective-permute-start | bytes 393224 | tf_op jit(solution)/shard_map/ppermute | solution.py:265
  20.7 7.0 %collective-permute-start.10 = (bf16[2,256,256]{2,1,0:T(8,128)(2,1)S(1)}, bf16[2,256,256]{2,1,0:T(8,128)(2,1)S(1)}, u32[]{:S(2)}, u32[]{:S(2)}) collective-permute-start(bf16[2,256,256]{2,1,0:T(8,128)(2,1)S(1)} %get-tuple-element.30.one), channel_id=1, source_target_pairs={{0,4},{1,5},{2,6},{3,7},{4,0},{5,1},{6,2},{7,3},{8,12},{9,13},{10,... | collective-permute-start | bytes 786440 | tf_op jit(solution)/shard_map/ppermute | solution.py:265
  25.5 7.4 %collective-permute-start.4 = (bf16[2,256,256]{2,1,0:T(8,128)(2,1)S(1)}, bf16[2,256,256]{2,1,0:T(8,128)(2,1)S(1)}, u32[]{:S(2)}, u32[]{:S(2)}) collective-permute-start(bf16[2,256,256]{2,1,0:T(8,128)(2,1)S(1)} %get-tuple-element.24.one), channel_id=1, source_target_pairs={{0,4},{1,5},{2,6},{3,7},{4,0},{5,1},{6,2},{7,3},{8,12},{9,13},{10,... | collective-permute-start | bytes 786440 | tf_op jit(solution)/shard_map/ppermute | solution.py:265
  27.8 5.2 %collective-permute-start.11 = (bf16[2,256,256]{2,1,0:T(8,128)(2,1)S(1)}, bf16[2,256,256]{2,1,0:T(8,128)(2,1)S(1)}, u32[]{:S(2)}, u32[]{:S(2)}) collective-permute-start(bf16[2,256,256]{2,1,0:T(8,128)(2,1)S(1)} %joint.3), channel_id=1, source_target_pairs={{0,16},{1,17},{2,18},{3,19},{4,8},{5,9},{6,10},{7,11},{8,4},{9,5},... | collective-permute-start | bytes 786440 | tf_op jit(solution)/shard_map/ppermute | solution.py:265
  32.9 4.0 %collective-permute-start.5 = (bf16[2,256,256]{2,1,0:T(8,128)(2,1)S(1)}, bf16[2,256,256]{2,1,0:T(8,128)(2,1)S(1)}, u32[]{:S(2)}, u32[]{:S(2)}) collective-permute-start(bf16[2,256,256]{2,1,0:T(8,128)(2,1)S(1)} %joint.2), channel_id=1, source_target_pairs={{0,16},{1,17},{2,18},{3,19},{4,8},{5,9},{6,10},{7,11},{8,4},{9,5},... | collective-permute-start | bytes 786440 | tf_op jit(solution)/shard_map/ppermute | solution.py:265
  33.6 8.5 %collective-permute-start.12 = (bf16[256,256]{1,0:T(8,128)(2,1)S(1)}, bf16[256,256]{1,0:T(8,128)(2,1)S(1)}, u32[]{:S(2)}, u32[]{:S(2)}) collective-permute-start(bf16[256,256]{1,0:T(8,128)(2,1)S(1)} %near.3), channel_id=1, source_target_pairs={{0,4},{1,5},{2,6},{3,7},{4,0},{5,1},{6,2},{7,3},{8,12},{9,13},{10,... | collective-permute-start | bytes 393224 | tf_op jit(solution)/shard_map/ppermute | solution.py:265
  37.5 21.0 %copy-start.4 = (bf16[4,1024,512]{2,1,0:T(8,128)(2,1)S(1)}, bf16[4,1024,512]{2,1,0:T(8,128)(2,1)}, u32[]{:S(2)}) copy-start(bf16[4,1024,512]{2,1,0:T(8,128)(2,1)} %refs_5_.1) | copy-start | bytes 12582916
  37.5 20.9 %copy-start.5 = (s32[1,4]{1,0:T(1,128)S(1)}, s32[1,4]{1,0:T(1,128)}, u32[]{:S(2)}) copy-start(s32[1,4]{1,0:T(1,128)} %param.9) | copy-start | bytes 52
  37.5 20.9 %copy-start.6 = (s32[16]{0:T(128)S(1)}, s32[16]{0:T(128)}, u32[]{:S(2)}) copy-start(s32[16]{0:T(128)} %refs_2_.1) | copy-start | bytes 196
  37.5 7.5 %collective-permute-start.6 = (bf16[256,256]{1,0:T(8,128)(2,1)S(1)}, bf16[256,256]{1,0:T(8,128)(2,1)S(1)}, u32[]{:S(2)}, u32[]{:S(2)}) collective-permute-start(bf16[256,256]{1,0:T(8,128)(2,1)S(1)} %near.2), channel_id=1, source_target_pairs={{0,4},{1,5},{2,6},{3,7},{4,0},{5,1},{6,2},{7,3},{8,12},{9,13},{10,... | collective-permute-start | bytes 393224 | tf_op jit(solution)/shard_map/ppermute | solution.py:265
  45.8 5.6 %collective-permute-start.13 = (bf16[2,128,256]{2,1,0:T(8,128)(2,1)S(1)}, bf16[2,128,256]{2,1,0:T(8,128)(2,1)S(1)}, u32[]{:S(2)}, u32[]{:S(2)}) collective-permute-start(bf16[2,128,256]{2,1,0:T(8,128)(2,1)S(1)} %get-tuple-element.31.refs_2_), channel_id=1, source_target_pairs={{0,1},{1,0},{2,3},{3,2},{4,5},{5,4},{6,7},{7,6},{8,9},{9,8},{10,11... | collective-permute-start | bytes 393224 | tf_op jit(solution)/shard_map/ppermute | solution.py:265
  47.2 6.6 %collective-permute-start.15 = (bf16[2,128,256]{2,1,0:T(8,128)(2,1)S(1)}, bf16[2,128,256]{2,1,0:T(8,128)(2,1)S(1)}, u32[]{:S(2)}, u32[]{:S(2)}) collective-permute-start(bf16[2,128,256]{2,1,0:T(8,128)(2,1)S(1)} %get-tuple-element.32), channel_id=1, source_target_pairs={{0,3},{1,2},{2,1},{3,0},{4,7},{5,6},{6,5},{7,4},{8,11},{9,10},{10,... | collective-permute-start | bytes 393224 | tf_op jit(solution)/shard_map/ppermute | solution.py:265
  49.4 5.8 %collective-permute-start.14 = (bf16[2,128,256]{2,1,0:T(8,128)(2,1)S(1)}, bf16[2,128,256]{2,1,0:T(8,128)(2,1)S(1)}, u32[]{:S(2)}, u32[]{:S(2)}) collective-permute-start(bf16[2,128,256]{2,1,0:T(8,128)(2,1)S(1)} %get-tuple-element.32), channel_id=1, source_target_pairs={{0,2},{1,3},{2,0},{3,1},{4,6},{5,7},{6,4},{7,5},{8,10},{9,11},{10,... | collective-permute-start | bytes 393224 | tf_op jit(solution)/shard_map/ppermute | solution.py:265
  56.5 2.0 %collective-permute-start.16 = (bf16[2,128,1024]{2,1,0:T(8,128)(2,1)S(1)}, bf16[2,128,1024]{2,1,0:T(8,128)(2,1)S(1)}, u32[]{:S(2)}, u32[]{:S(2)}) collective-permute-start(bf16[2,128,1024]{2,1,0:T(8,128)(2,1)S(1)} %phase.1.refs_3_), channel_id=1, source_target_pairs={{0,16},{1,17},{2,18},{3,19},{4,20},{5,21},{6,22},{7,23},{8,24},{9,... | collective-permute-start | bytes 1572872 | tf_op jit(solution)/shard_map/ppermute | solution.py:265

commit v6 on v5

--- a/solution.py
+++ b/solution.py
@@ -91,16 +91,13 @@
     return jnp.dot(select, paired, preferred_element_type=f32).astype(bf16)
 
 
-def take_kernel(holo, out):
-    out[...] = holo[...]
-
-
-def row_kernel(inner, place, here, there, table, *outs):
-    spot = place[1]
+def row_kernel(inner, own, chunk, place, here, there, table, after, *outs):
+    core, spot = place[0], place[1]
     dist_dev, rows_dev, width = here.shape[1:]
     block = width // inner
+    angle = core * own + chunk
     flat = jnp.concatenate(
-        [source[0].reshape(dist_dev * rows_dev, width) for source in (here, there)], axis=0
+        [source[angle].reshape(dist_dev * rows_dev, width) for source in (here, there)], axis=0
     )
     for rel in range(inner):
         part = table[:, pl.ds(pl.multiple_of((spot ^ rel) * block, block), block)]
@@ -165,63 +162,57 @@
     out[...] = (keep[which].astype(f32) + more).astype(bf16)
 
 
-def half_kernel(inner, place, *refs):
-    mine, other = refs[-2:]
-    own = len(refs[:-2]) // 3
+def half_kernel(place, keep, across, last, after, mine, other):
     spot, plane = place[1], place[2]
     which = plane % 2
     inside = (plane == 1) | (plane == 2)
-    capacity = mine.shape[1]
-    for chunk in range(own):
-        keep, across, last = refs[3 * chunk : 3 * chunk + 3]
-        for out, pair in ((mine, spot // 2), (other, 1 - spot // 2)):
-            rows = pl.ds(pl.multiple_of(pair * capacity, capacity), capacity)
-            more = jnp.where(inside, across[which, rows, :].astype(f32), 0.0)
-            got = keep[which, rows, :].astype(f32) + more + last[rows, :].astype(f32)
-            out[chunk] = got.astype(bf16)
+    capacity = mine.shape[0]
+    for out, pair in ((mine, spot // 2), (other, 1 - spot // 2)):
+        rows = pl.ds(pl.multiple_of(pair * capacity, capacity), capacity)
+        more = jnp.where(inside, across[which, rows, :].astype(f32), 0.0)
+        got = keep[which, rows, :].astype(f32) + more + last[rows, :].astype(f32)
+        out[...] = got.astype(bf16)
 
 
 def phase_kernel(inner, place, table, *refs):
     pieces = refs[:inner]
-    out, joined = refs[inner:]
+    out, joined = refs[-2:]
     spot = place[1]
-    own, capacity, block = pieces[0].shape
+    block = pieces[0].shape[1]
     for rel in range(inner):
         columns = pl.ds(pl.multiple_of((spot ^ rel) * block, block), block)
-        joined[:, columns] = pieces[rel][...].reshape(own * capacity, block)
-    got = jnp.dot(joined[...], table[...], preferred_element_type=f32)
-    out[...] = got.astype(bf16).reshape(own, capacity, inner * block)
-
-
-def recon_kernel(own, place, order, slabs, here, there, weights, out, total):
-    step = pl.program_id(0)
-    phase = jnp.where(step < own, here[0], there[0])
-    got = jnp.dot(phase, weights[0], preferred_element_type=f32)
-
-    @pl.when(step == 0)
-    def _():
-        total[...] = got
-
-    @pl.when(step > 0)
-    def _():
-        total[...] += got
-
-    @pl.when(step == 2 * own - 1)
-    def _():
-        capacity = total.shape[0]
-        device = place[3]
-        parity = device % 2
-        offset = parity * slabs[device - parity]
-        slot = lax.broadcasted_iota(jnp.int32, (capacity, capacity), 0)
-        source = lax.broadcasted_iota(jnp.int32, (capacity, capacity), 1)
-        select = (source == slot + offset) & (slot < slabs[device])
-        select = jnp.where(select, 1.0, 0.0).astype(bf16)
-        picked = jnp.dot(select, total[...].astype(bf16), preferred_element_type=f32)
-        out[...] = picked.astype(bf16)
+        joined[:, columns] = pieces[rel][...]
+    out[...] = jnp.dot(joined[...], table[...], preferred_element_type=f32).astype(bf16)
+
+
+def recon_kernel(place, order, phase, weights, out):
+    out[...] = jnp.dot(phase[...], weights[0], preferred_element_type=f32)
+
+
+def recon_more_kernel(place, order, phase, weights, before, out):
+    out[...] = before[...] + jnp.dot(phase[...], weights[0], preferred_element_type=f32)
+
+
+def recon_last_kernel(place, order, slabs, phase, weights, before, out):
+    total = before[...] + jnp.dot(phase[...], weights[0], preferred_element_type=f32)
+    capacity = total.shape[0]
+    device = place[3]
+    parity = device % 2
+    offset = parity * slabs[device - parity]
+    slot = lax.broadcasted_iota(jnp.int32, (capacity, capacity), 0)
+    source = lax.broadcasted_iota(jnp.int32, (capacity, capacity), 1)
+    select = (source == slot + offset) & (slot < slabs[device])
+    select = jnp.where(select, 1.0, 0.0).astype(bf16)
+    picked = jnp.dot(select, total.astype(bf16), preferred_element_type=f32)
+    out[...] = picked.astype(bf16)
 
 
 def vmem(count):
     return [pl.BlockSpec(memory_space=pltpu.VMEM)] * count
+
+
+def unread(count):
+    return [pl.BlockSpec(memory_space=pl.ANY)] * count
 
 
 def smem(count):
@@ -276,53 +267,6 @@
     def to_middle(c, r):
         z = r // inner
         return (c, (3 - z) * inner + r % inner) if z in (1, 2) else (c ^ 1, r)
-
-    other_angles = pl.pallas_call(
-        lambda place, holo, out: take_kernel(holo, out),
-        out_shape=shaped(own, dist_dev, rows_dev, width),
-        grid_spec=pltpu.PrefetchScalarGridSpec(
-            num_scalar_prefetch=1,
-            grid=(1,),
-            in_specs=[
-                pl.BlockSpec(
-                    (own, dist_dev, rows_dev, width), lambda i, place: (place[0] ^ 1, 0, 0, 0)
-                )
-            ],
-            out_specs=one_out,
-        ),
-        compiler_params=params,
-        cost_estimate=cost(0, (2, own, dist_dev, rows_dev, width)),
-        name="other_angles",
-    )(place, holograms[0])
-    partner = sent(other_angles, to_other_core)
-
-    arrived = []
-    for chunk in range(own):
-        pieces = pl.pallas_call(
-            lambda *refs: row_kernel(inner, *refs),
-            out_shape=[shaped(dists, rows_dev, block)] * inner,
-            grid_spec=pltpu.PrefetchScalarGridSpec(
-                num_scalar_prefetch=1,
-                grid=(1,),
-                in_specs=[
-                    pl.BlockSpec(
-                        (1, dist_dev, rows_dev, width),
-                        lambda i, place, chunk=chunk: (place[0] * own + chunk, 0, 0, 0),
-                    ),
-                    pl.BlockSpec(
-                        (1, dist_dev, rows_dev, width), lambda i, place, chunk=chunk: (chunk, 0, 0, 0)
-                    ),
-                ]
-                + vmem(1),
-                out_specs=vmem(inner),
-            ),
-            compiler_params=params,
-            cost_estimate=cost(
-                2 * dists * rows_dev * width * width, (width, width), (2, dists, rows_dev, width)
-            ),
-            name="row_spectra",
-        )(place, holograms[0], partner, table)
-        arrived.append([pieces[0]] + [sent(pieces[rel], to_spot(rel)) for rel in range(1, inner)])
 
     index = jnp.arange(width, dtype=jnp.int32)
     my_cols = spot * block + jnp.arange(block, dtype=jnp.int32)
@@ -349,6 +293,22 @@
         2.0 * (sin_b + absorb_ratio * cos_b),
     )
 
+    partner = sent(holograms[0], to_other_core)
+    arrived = []
+    for chunk in range(own):
+        pieces = pl.pallas_call(
+            lambda *refs, chunk=chunk: row_kernel(inner, own, chunk, *refs),
+            out_shape=[shaped(dists, rows_dev, block)] * inner,
+            in_specs=smem(1) + vmem(3) + unread(1),
+            out_specs=vmem(inner),
+            compiler_params=params,
+            cost_estimate=cost(
+                2 * dists * rows_dev * width * width, (width, width), (2, dists, rows_dev, width)
+            ),
+            name="row_spectra",
+        )(place, holograms[0], partner, table, gain)
+        arrived.append([pieces[0]] + [sent(pieces[rel], to_spot(rel)) for rel in range(1, inner)])
+
     sums = []
     for chunk in range(own):
         away, keep = pl.pallas_call(
@@ -386,62 +346,66 @@
             cost_estimate=cost(depth * block, (3, depth, block)),
             name="near",
         )(place, keep, across)
-        sums += [keep, across, sent(near, to_near_plane)]
-
-    mine, other = pl.pallas_call(
-        lambda *refs: half_kernel(inner, *refs),
-        out_shape=[shaped(own, capacity, block)] * 2,
-        in_specs=smem(1) + vmem(len(sums)),
-        out_specs=vmem(2),
-        compiler_params=params,
-        cost_estimate=cost(own * depth * block, (5, own, depth, block)),
-        name="half",
-    )(place, *sums)
-    pieces = [mine] + [sent(mine if rel < 2 else other, to_spot(rel)) for rel in range(1, inner)]
-    phase = pl.pallas_call(
-        lambda *refs: phase_kernel(inner, *refs),
-        out_shape=shaped(own, capacity, width),
-        in_specs=smem(1) + vmem(1 + inner),
-        out_specs=one_out,
-        scratch_shapes=[pltpu.VMEM((own * capacity, width), bf16)],
-        compiler_params=params,
-        cost_estimate=cost(
-            2 * own * capacity * width * width, (width, width), (2, own, capacity, width)
-        ),
-        name="phase",
-    )(place, table, *pieces)
-    there = sent(phase, to_other_core)
-
-    def angle_of(step, place):
-        return (place[0] ^ (step // own)) * own + step % own
-
-    return pl.pallas_call(
-        lambda *refs: recon_kernel(own, *refs),
-        out_shape=shaped(capacity, pixels),
-        grid_spec=pltpu.PrefetchScalarGridSpec(
-            num_scalar_prefetch=3,
-            grid=(angles,),
-            in_specs=[
-                pl.BlockSpec(
-                    (1, capacity, width), lambda i, place, order, slabs: (jnp.minimum(i, own - 1), 0, 0)
-                ),
-                pl.BlockSpec(
-                    (1, capacity, width), lambda i, place, order, slabs: (jnp.maximum(i - own, 0), 0, 0)
-                ),
-                pl.BlockSpec(
-                    (1, width, pixels),
-                    lambda i, place, order, slabs: (order[angle_of(i, place)], 0, 0),
-                ),
-            ],
+        sums.append((keep, across, sent(near, to_near_plane)))
+
+    def recon(kernel, out_type, other, chunk, scalars, phase, *before):
+        def angle(place):
+            return (place[0] ^ other) * own + chunk
+
+        return pl.pallas_call(
+            kernel,
+            out_shape=jax.ShapeDtypeStruct((capacity, pixels), out_type),
+            grid_spec=pltpu.PrefetchScalarGridSpec(
+                num_scalar_prefetch=len(scalars),
+                grid=(1,),
+                in_specs=vmem(1)
+                + [
+                    pl.BlockSpec(
+                        (1, width, pixels),
+                        lambda i, place, order, *slabs: (order[angle(place)], 0, 0),
+                    )
+                ]
+                + vmem(len(before)),
+                out_specs=one_out,
+            ),
+            compiler_params=params,
+            cost_estimate=cost(2 * capacity * width * pixels, (width, capacity + pixels)),
+            name="recon",
+        )(*scalars, phase, weights, *before)
+
+    total = None
+    scalars = (place, angle_order[0])
+    for chunk in range(own):
+        mine, other = pl.pallas_call(
+            half_kernel,
+            out_shape=[shaped(capacity, block)] * 2,
+            in_specs=smem(1) + vmem(3) + unread(1),
+            out_specs=vmem(2),
+            compiler_params=params,
+            cost_estimate=cost(depth * block, (5, depth, block)),
+            name="half",
+        )(place, *sums[chunk], near)
+        pieces = [mine] + [sent(mine if rel < 2 else other, to_spot(rel)) for rel in range(1, inner)]
+        phase = pl.pallas_call(
+            lambda *refs: phase_kernel(inner, *refs),
+            out_shape=shaped(capacity, width),
+            in_specs=smem(1) + vmem(1 + inner) + unread(0 if total is None else 1),
             out_specs=one_out,
-            scratch_shapes=[pltpu.VMEM((capacity, pixels), f32)],
-        ),
-        compiler_params=params,
-        cost_estimate=cost(
-            2 * angles * capacity * width * pixels, (angles, width, capacity + pixels)
-        ),
-        name="recon",
-    )(place, angle_order[0], slab_rows, phase, there, weights)
+            scratch_shapes=[pltpu.VMEM((capacity, width), bf16)],
+            compiler_params=params,
+            cost_estimate=cost(2 * capacity * width * width, (width, width), (2, capacity, width)),
+            name="phase",
+        )(place, table, *pieces, *([] if total is None else [total]))
+        there = sent(phase, to_other_core)
+        if total is None:
+            total = recon(recon_kernel, f32, 0, chunk, scalars, phase)
+        else:
+            total = recon(recon_more_kernel, f32, 0, chunk, scalars, phase, total)
+        if chunk < own - 1:
+            total = recon(recon_more_kernel, f32, 1, chunk, scalars, there, total)
+        else:
+            total = recon(recon_last_kernel, bf16, 1, chunk, scalars + (slab_rows,), there, total)
+    return total
 
 
 def on_device(holograms, propagation, weights, angle_order, slab_rows):

time: 61.5 us -> 66.7 us (1.085)
  waiting for transfers between devices: 17.8 us -> 21.1 us
  Pallas kernels: 14.7 us -> 16.8 us
  local copies, waits for them, and re-layouts: 3.65 us -> 2.16 us
  starting transfers between devices: 24.4 us -> 25.6 us
    ppermute x17 -> x21, waiting for transfers between devices: 17.8 us -> 21.1 us  [sent(): return lax.ppermute(value, ('dist', 'rows'), pairs)]
    unnamed x14 -> x10, local copies, waits for them, and re-layouts: 2.84 us -> 1.25 us
    pallas_call x5 -> x8, Pallas kernels: 6.62 us -> 8.05 us  [the longest x4 4.26 us: recon(): pl.pallas_call(kernel, out_shape=jax.ShapeDtypeStruct((capacity, pixels),...]
    ppermute x17 -> x21, starting transfers between devices: 24.4 us -> 25.6 us  [sent(): return lax.ppermute(value, ('dist', 'rows'), pairs)]
    pallas_call x1 -> x2, Pallas kernels: 1.3 us -> 2 us  [plane_plan(): pl.pallas_call(lambda *refs: phase_kernel(inner, *refs), out_shape=shaped...]
  transfers between devices with their start and end apart: 17 -> 21, of which waited for: 9 -> 12; matrix products, arithmetic and copies ran while one was open for 2% -> 2% of each run, Pallas kernels for 13% -> 17%
where the time goes in v6:
time: 66.7 us; the launch traced here: 66.5 us
  starting transfers between devices  25.6 us (38%)
  waiting for transfers between devices  21.1 us (32%)
  Pallas kernels  16.8 us (25%)
  local copies, waits for them, and re-layouts  2.16 us (3%)
    ppermute x21, starting transfers between devices, sent(): return lax.ppermute(value, ('dist', 'rows'), pairs)  25.6 us
    ppermute x21, waiting for transfers between devices, sent(): return lax.ppermute(value, ('dist', 'rows'), pairs)  21.1 us
    pallas_call x4, Pallas kernels, recon(): pl.pallas_call(kernel, out_shape=jax.ShapeDtypeStruct((capacity, pixels),...  4.26 us
    pallas_call x2, Pallas kernels, plane_plan(): pl.pallas_call(lambda *refs: column_kernel(inner, outer, *refs), out_shap...  3.7 us
    pallas_call x2, Pallas kernels, plane_plan(): pl.pallas_call(lambda *refs, chunk=chunk: row_kernel(inner, own, chunk, *...  2.57 us
    pallas_call x2, Pallas kernels, plane_plan(): pl.pallas_call(lambda *refs: phase_kernel(inner, *refs), out_shape=shaped...  2 us
    pallas_call x1, Pallas kernels, plane_plan(): pl.pallas_call(filter_kernel, out_shape=shaped(dists, width, block), in_s...  1.78 us
  transfers between devices with their start and end apart: 21, of which 12 were waited for; matrix products, arithmetic and copies ran while one was open for 2% of the time, Pallas kernels for 17%

profile of v6, /device:TPU:0, one launch (start us, length us, event | category | flops | bytes accessed | tf_op | source)
XLA Modules:
  0.0 66.5 jit_solution(3439753321776079297)
XLA Ops:
  0.0 0.5 collective-permute-start
  0.5 0.9 %fusion.12 = (f32[2]{0:T(128)S(1)}, f32[2]{0:T(128)S(1)}) fusion(f32[4]{0:T(128)} %param.7, s32[]{:T(128)S(6)} %select_n.35, s32[]{:T(128)S(6)} %select_n.36), kind=kLoop, calls=%fused_computation.21 | loop fusion | bytes 40 | tf_op jit(solution)/shard_map/dynamic_slice | solution.py:275
  1.4 0.1 pad_maximum_fusion.1
  1.5 0.2 multiply_sine_fusion
  1.7 0.1 fusion.5
  1.8 1.8 %filters.1.refs_4_.refs_2_ = bf16[4,1024,256]{2,1,0:T(8,128)(2,1)S(1)} custom-call(f32[8,1024]{1,0:T(8,128)S(1)} %pad_maximum_fusion.waves_a, f32[4,256]{1,0:T(4,128)S(1)} %get-tuple-element.40.with_sin, f32[4,256]{1,0:T(4,128)S(1)} %get-tuple-element.39.with_cos), custom_call_target="tpu_custom_call" | custom-call | flops 8388608 | bytes 2097152 | tf_op jit(solution)/shard_map/filters/pallas_call | solution.py:282
  3.6 0.1 pad_add_fusion.refs_0_.place
  3.7 0.0 collective-permute-done.refs_2_
  3.7 1.2 %copy-done.2 = bf16[1,4,2,64,1024]{4,3,2,1,0:T(8,128)(2,1)S(1)} copy-done((bf16[1,4,2,64,1024]{4,3,2,1,0:T(8,128)(2,1)S(1)}, bf16[1,4,2,64,1024]{4,3,2,1,0:T(8,128)(2,1)}, u32[]{:S(2)}) %copy-start.2) | copy-done | bytes 1048600
  4.9 1.3 %row_spectra.3 = (bf16[4,64,256]{2,1,0:T(8,128)(2,1)S(1)}, bf16[4,64,256]{2,1,0:T(8,128)(2,1)S(1)}, bf16[4,64,256]{2,1,0:T(8,128)(2,1)S(1)}, bf16[4,64,256]{2,1,0:T(8,128)(2,1)S(1)}) custom-call(s32[4]{0:T(128)S(1)} %pad_add_fusion.refs_0_.place, bf16[4,2,64,1024]{3,2,1,0:T(8,128)(2,1)S(1)} %bitcast.7, ...), custom_call_target="tpu_custom_call" | custom-call | flops 536870912 | bytes 3145728 | tf_op jit(solution)/shard_map/row_spectra/pallas_call | solution.py:299
  6.2 2.5 %collective-permute-start.10 = (bf16[4,64,256]{2,1,0:T(8,128)(2,1)S(1)}, bf16[4,64,256]{2,1,0:T(8,128)(2,1)S(1)}, u32[]{:S(2)}, u32[]{:S(2)}) collective-permute-start(bf16[4,64,256]{2,1,0:T(8,128)(2,1)S(1)} %get-tuple-element.30), channel_id=1, source_target_pairs={{0,1},{1,0},{2,3},{3,2},{4,5},{5,4},{6,7},{7,6},{8,9},{9,8},{10,11... | collective-permute-start | bytes 393224 | tf_op jit(solution)/shard_map/ppermute | solution.py:256
  8.7 1.5 %collective-permute-start.11 = (bf16[4,64,256]{2,1,0:T(8,128)(2,1)S(1)}, bf16[4,64,256]{2,1,0:T(8,128)(2,1)S(1)}, u32[]{:S(2)}, u32[]{:S(2)}) collective-permute-start(bf16[4,64,256]{2,1,0:T(8,128)(2,1)S(1)} %get-tuple-element.31), channel_id=1, source_target_pairs={{0,2},{1,3},{2,0},{3,1},{4,6},{5,7},{6,4},{7,5},{8,10},{9,11},{10,... | collective-permute-start | bytes 393224 | tf_op jit(solution)/shard_map/ppermute | solution.py:256
  10.3 0.0 collective-permute-start.12
  10.3 1.3 %row_spectra.2 = (bf16[4,64,256]{2,1,0:T(8,128)(2,1)S(1)}, bf16[4,64,256]{2,1,0:T(8,128)(2,1)S(1)}, bf16[4,64,256]{2,1,0:T(8,128)(2,1)S(1)}, bf16[4,64,256]{2,1,0:T(8,128)(2,1)S(1)}) custom-call(s32[4]{0:T(128)S(1)} %pad_add_fusion.refs_0_.place, bf16[4,2,64,1024]{3,2,1,0:T(8,128)(2,1)S(1)} %bitcast.8, ...), custom_call_target="tpu_custom_call" | custom-call | flops 536870912 | bytes 3145728 | tf_op jit(solution)/shard_map/row_spectra/pallas_call | solution.py:299
  11.6 2.0 %collective-permute-start.1 = (bf16[4,64,256]{2,1,0:T(8,128)(2,1)S(1)}, bf16[4,64,256]{2,1,0:T(8,128)(2,1)S(1)}, u32[]{:S(2)}, u32[]{:S(2)}) collective-permute-start(bf16[4,64,256]{2,1,0:T(8,128)(2,1)S(1)} %get-tuple-element.22), channel_id=1, source_target_pairs={{0,1},{1,0},{2,3},{3,2},{4,5},{5,4},{6,7},{7,6},{8,9},{9,8},{10,11... | collective-permute-start | bytes 393224 | tf_op jit(solution)/shard_map/ppermute | solution.py:256
  13.6 1.5 %collective-permute-start.2 = (bf16[4,64,256]{2,1,0:T(8,128)(2,1)S(1)}, bf16[4,64,256]{2,1,0:T(8,128)(2,1)S(1)}, u32[]{:S(2)}, u32[]{:S(2)}) collective-permute-start(bf16[4,64,256]{2,1,0:T(8,128)(2,1)S(1)} %get-tuple-element.23), channel_id=1, source_target_pairs={{0,2},{1,3},{2,0},{3,1},{4,6},{5,7},{6,4},{7,5},{8,10},{9,11},{10,... | collective-permute-start | bytes 393224 | tf_op jit(solution)/shard_map/ppermute | solution.py:256
  15.1 0.0 collective-permute-done.10.refs_4_
  15.1 0.9 %collective-permute-start.3 = (bf16[4,64,256]{2,1,0:T(8,128)(2,1)S(1)}, bf16[4,64,256]{2,1,0:T(8,128)(2,1)S(1)}, u32[]{:S(2)}, u32[]{:S(2)}) collective-permute-start(bf16[4,64,256]{2,1,0:T(8,128)(2,1)S(1)} %get-tuple-element.24), channel_id=1, source_target_pairs={{0,3},{1,2},{2,1},{3,0},{4,7},{5,6},{6,5},{7,4},{8,11},{9,10},{10,... | collective-permute-start | bytes 393224 | tf_op jit(solution)/shard_map/ppermute | solution.py:256
  16.0 0.9 %collective-permute-done.11.refs_5_ = bf16[4,64,256]{2,1,0:T(8,128)(2,1)S(1)} collective-permute-done((bf16[4,64,256]{2,1,0:T(8,128)(2,1)S(1)}, bf16[4,64,256]{2,1,0:T(8,128)(2,1)S(1)}, u32[]{:S(2)}, u32[]{:S(2)}) %collective-permute-start.11) | collective-permute-done | bytes 131104 | tf_op jit(solution)/shard_map/ppermute | solution.py:256
  16.9 0.7 %collective-permute-done.12.refs_6_ = bf16[4,64,256]{2,1,0:T(8,128)(2,1)S(1)} collective-permute-done((bf16[4,64,256]{2,1,0:T(8,128)(2,1)S(1)}, bf16[4,64,256]{2,1,0:T(8,128)(2,1)S(1)}, u32[]{:S(2)}, u32[]{:S(2)}) %collective-permute-start.12) | collective-permute-done | bytes 131104 | tf_op jit(solution)/shard_map/ppermute | solution.py:256
  17.6 1.8 %columns.3 = (bf16[2,256,256]{2,1,0:T(8,128)(2,1)S(1)}, bf16[2,256,256]{2,1,0:T(8,128)(2,1)S(1)}) custom-call(s32[4]{0:T(128)S(1)} %pad_add_fusion.refs_0_.place, bf16[1024,1024]{1,0:T(8,128)(2,1)S(1)} %copy-done, bf16[4,1024,256]{2,1,0:T(8,128)(2,1)S(1)} %filters.1.refs_4_.refs_2_, bf16[4,64,256]{2,1,0:T(8,128)(2,1)S(1)} %get-tuple-element.29.refs_3_, ...), custom_call_target="tpu_custom_call" | custom-call | flops 1073741824 | bytes 4194304 | tf_op jit(solution)/shard_map/columns/pallas_call | solution.py:314
  19.4 1.6 %collective-permute-start.13 = (bf16[2,256,256]{2,1,0:T(8,128)(2,1)S(1)}, bf16[2,256,256]{2,1,0:T(8,128)(2,1)S(1)}, u32[]{:S(2)}, u32[]{:S(2)}) collective-permute-start(bf16[2,256,256]{2,1,0:T(8,128)(2,1)S(1)} %get-tuple-element.34.one), channel_id=1, source_target_pairs={{0,4},{1,5},{2,6},{3,7},{4,0},{5,1},{6,2},{7,3},{8,12},{9,13},{10,... | collective-permute-start | bytes 786440 | tf_op jit(solution)/shard_map/ppermute | solution.py:256
  21.1 0.0 collective-permute-done.1.refs_4_
  21.1 1.6 %collective-permute-done.2.refs_5_ = bf16[4,64,256]{2,1,0:T(8,128)(2,1)S(1)} collective-permute-done((bf16[4,64,256]{2,1,0:T(8,128)(2,1)S(1)}, bf16[4,64,256]{2,1,0:T(8,128)(2,1)S(1)}, u32[]{:S(2)}, u32[]{:S(2)}) %collective-permute-start.2) | collective-permute-done | bytes 131104 | tf_op jit(solution)/shard_map/ppermute | solution.py:256
  22.7 1.9 %columns.2 = (bf16[2,256,256]{2,1,0:T(8,128)(2,1)S(1)}, bf16[2,256,256]{2,1,0:T(8,128)(2,1)S(1)}) custom-call(s32[4]{0:T(128)S(1)} %pad_add_fusion.refs_0_.place, bf16[1024,1024]{1,0:T(8,128)(2,1)S(1)} %copy-done, bf16[4,1024,256]{2,1,0:T(8,128)(2,1)S(1)} %filters.1.refs_4_.refs_2_, bf16[4,64,256]{2,1,0:T(8,128)(2,1)S(1)} %get-tuple-element.21.refs_3_, ...), custom_call_target="tpu_custom_call" | custom-call | flops 1073741824 | bytes 4194304 | tf_op jit(solution)/shard_map/columns/pallas_call | solution.py:314
  24.6 1.6 %collective-permute-start.4 = (bf16[2,256,256]{2,1,0:T(8,128)(2,1)S(1)}, bf16[2,256,256]{2,1,0:T(8,128)(2,1)S(1)}, u32[]{:S(2)}, u32[]{:S(2)}) collective-permute-start(bf16[2,256,256]{2,1,0:T(8,128)(2,1)S(1)} %get-tuple-element.26.one), channel_id=1, source_target_pairs={{0,4},{1,5},{2,6},{3,7},{4,0},{5,1},{6,2},{7,3},{8,12},{9,13},{10,... | collective-permute-start | bytes 786440 | tf_op jit(solution)/shard_map/ppermute | solution.py:256
  26.2 0.2 collective-permute-done.13.two
  26.5 0.1 joint.3
  26.5 0.1 collective-permute-start.14
  26.6 5.5 %collective-permute-done.4.two = bf16[2,256,256]{2,1,0:T(8,128)(2,1)S(1)} collective-permute-done((bf16[2,256,256]{2,1,0:T(8,128)(2,1)S(1)}, bf16[2,256,256]{2,1,0:T(8,128)(2,1)S(1)}, u32[]{:S(2)}, u32[]{:S(2)}) %collective-permute-start.4) | collective-permute-done | bytes 262176 | tf_op jit(solution)/shard_map/ppermute | solution.py:256
  32.1 0.1 joint.2
  32.2 0.1 collective-permute-start.5
  32.3 0.0 collective-permute-done.14.across
  32.3 0.6 near.3
  32.9 3.2 %collective-permute-start.15 = (bf16[256,256]{1,0:T(8,128)(2,1)S(1)}, bf16[256,256]{1,0:T(8,128)(2,1)S(1)}, u32[]{:S(2)}, u32[]{:S(2)}) collective-permute-start(bf16[256,256]{1,0:T(8,128)(2,1)S(1)} %near.3), channel_id=1, source_target_pairs={{0,4},{1,5},{2,6},{3,7},{4,0},{5,1},{6,2},{7,3},{8,12},{9,13},{10,... | collective-permute-start | bytes 393224 | tf_op jit(solution)/shard_map/ppermute | solution.py:256
  36.1 0.6 near.2.after
  36.7 0.0 copy-start.1
  36.7 0.0 copy-start.3
  36.7 2.3 %collective-permute-done.15.last = bf16[256,256]{1,0:T(8,128)(2,1)S(1)} collective-permute-done((bf16[256,256]{1,0:T(8,128)(2,1)S(1)}, bf16[256,256]{1,0:T(8,128)(2,1)S(1)}, u32[]{:S(2)}, u32[]{:S(2)}) %collective-permute-start.15) | collective-permute-done | bytes 131104 | tf_op jit(solution)/shard_map/ppermute | solution.py:256
  39.0 0.6 half.3
  39.6 1.7 %collective-permute-start.16 = (bf16[128,256]{1,0:T(8,128)(2,1)S(1)}, bf16[128,256]{1,0:T(8,128)(2,1)S(1)}, u32[]{:S(2)}, u32[]{:S(2)}) collective-permute-start(bf16[128,256]{1,0:T(8,128)(2,1)S(1)} %get-tuple-element.35.refs_2_), channel_id=1, source_target_pairs={{0,1},{1,0},{2,3},{3,2},{4,5},{5,4},{6,7},{7,6},{8,9},{9,8},{10,11... | collective-permute-start | bytes 196616 | tf_op jit(solution)/shard_map/ppermute | solution.py:256
  41.4 1.1 %collective-permute-start.17 = (bf16[128,256]{1,0:T(8,128)(2,1)S(1)}, bf16[128,256]{1,0:T(8,128)(2,1)S(1)}, u32[]{:S(2)}, u32[]{:S(2)}) collective-permute-start(bf16[128,256]{1,0:T(8,128)(2,1)S(1)} %get-tuple-element.36), channel_id=1, source_target_pairs={{0,2},{1,3},{2,0},{3,1},{4,6},{5,7},{6,4},{7,5},{8,10},{9,11},{10,... | collective-permute-start | bytes 196616 | tf_op jit(solution)/shard_map/ppermute | solution.py:256
  42.5 0.7 %collective-permute-start.18 = (bf16[128,256]{1,0:T(8,128)(2,1)S(1)}, bf16[128,256]{1,0:T(8,128)(2,1)S(1)}, u32[]{:S(2)}, u32[]{:S(2)}) collective-permute-start(bf16[128,256]{1,0:T(8,128)(2,1)S(1)} %get-tuple-element.36), channel_id=1, source_target_pairs={{0,3},{1,2},{2,1},{3,0},{4,7},{5,6},{6,5},{7,4},{8,11},{9,10},{10,... | collective-permute-start | bytes 196616 | tf_op jit(solution)/shard_map/ppermute | solution.py:256
  43.2 1.3 %collective-permute-done.16.refs_3_ = bf16[128,256]{1,0:T(8,128)(2,1)S(1)} collective-permute-done((bf16[128,256]{1,0:T(8,128)(2,1)S(1)}, bf16[128,256]{1,0:T(8,128)(2,1)S(1)}, u32[]{:S(2)}, u32[]{:S(2)}) %collective-permute-start.16) | collective-permute-done | bytes 65568 | tf_op jit(solution)/shard_map/ppermute | solution.py:256
  44.5 1.1 %collective-permute-done.17.refs_4_ = bf16[128,256]{1,0:T(8,128)(2,1)S(1)} collective-permute-done((bf16[128,256]{1,0:T(8,128)(2,1)S(1)}, bf16[128,256]{1,0:T(8,128)(2,1)S(1)}, u32[]{:S(2)}, u32[]{:S(2)}) %collective-permute-start.17) | collective-permute-done | bytes 65568 | tf_op jit(solution)/shard_map/ppermute | solution.py:256
  45.6 2.0 %collective-permute-done.18.refs_5_ = bf16[128,256]{1,0:T(8,128)(2,1)S(1)} collective-permute-done((bf16[128,256]{1,0:T(8,128)(2,1)S(1)}, bf16[128,256]{1,0:T(8,128)(2,1)S(1)}, u32[]{:S(2)}, u32[]{:S(2)}) %collective-permute-start.18) | collective-permute-done | bytes 65568 | tf_op jit(solution)/shard_map/ppermute | solution.py:256
  47.6 1.0 %phase.2 = bf16[128,1024]{1,0:T(8,128)(2,1)S(1)} custom-call(s32[4]{0:T(128)S(1)} %pad_add_fusion.refs_0_.place, bf16[1024,1024]{1,0:T(8,128)(2,1)S(1)} %copy-done, bf16[128,256]{1,0:T(8,128)(2,1)S(1)} %get-tuple-element.35.refs_2_, bf16[128,256]{1,0:T(8,128)(2,1)S(1)} %collective-permute-done.16.refs_3_, ...), custom_call_target="tpu_custom_call" | custom-call | flops 268435456 | bytes 2621440 | tf_op jit(solution)/shard_map/phase/pallas_call | solution.py:389
  48.6 0.1 collective-permute-start.19
  48.7 2.8 %collective-permute-start.6 = (bf16[256,256]{1,0:T(8,128)(2,1)S(1)}, bf16[256,256]{1,0:T(8,128)(2,1)S(1)}, u32[]{:S(2)}, u32[]{:S(2)}) collective-permute-start(bf16[256,256]{1,0:T(8,128)(2,1)S(1)} %near.2.after), channel_id=1, source_target_pairs={{0,4},{1,5},{2,6},{3,7},{4,0},{5,1},{6,2},{7,3},{8,12},{9,13},{10,... | collective-permute-start | bytes 393224 | tf_op jit(solution)/shard_map/ppermute | solution.py:256
  51.5 4.1 %collective-permute-done.6.last = bf16[256,256]{1,0:T(8,128)(2,1)S(1)} collective-permute-done((bf16[256,256]{1,0:T(8,128)(2,1)S(1)}, bf16[256,256]{1,0:T(8,128)(2,1)S(1)}, u32[]{:S(2)}, u32[]{:S(2)}) %collective-permute-start.6) | collective-permute-done | bytes 131104 | tf_op jit(solution)/shard_map/ppermute | solution.py:256
  55.6 0.6 half.2
  56.3 0.4 collective-permute-start.7
  56.6 0.4 collective-permute-start.8
  57.0 2.8 %collective-permute-start.9 = (bf16[128,256]{1,0:T(8,128)(2,1)S(1)}, bf16[128,256]{1,0:T(8,128)(2,1)S(1)}, u32[]{:S(2)}, u32[]{:S(2)}) collective-permute-start(bf16[128,256]{1,0:T(8,128)(2,1)S(1)} %get-tuple-element.28), channel_id=1, source_target_pairs={{0,3},{1,2},{2,1},{3,0},{4,7},{5,6},{6,5},{7,4},{8,11},{9,10},{10,... | collective-permute-start | bytes 196616 | tf_op jit(solution)/shard_map/ppermute | solution.py:256
  59.8 0.9 %recon.4.before = f32[128,512]{1,0:T(8,128)S(1)} custom-call(s32[4]{0:T(128)S(1)} %pad_add_fusion.refs_0_.place, s32[4]{0:T(128)S(1)} %bitcast.9, bf16[128,1024]{1,0:T(8,128)(2,1)S(1)} %phase.2, bf16[4,1024,512]{2,1,0:T(8,128)(2,1)S(1)} %copy-done.1), custom_call_target="tpu_custom_call" | custom-call | flops 134217728 | bytes 1310720 | tf_op jit(solution)/shard_map/recon/pallas_call | solution.py:355
  60.7 0.9 %recon.5.refs_6_.before = f32[128,512]{1,0:T(8,128)S(1)} custom-call(s32[4]{0:T(128)S(1)} %pad_add_fusion.refs_0_.place, s32[4]{0:T(128)S(1)} %bitcast.10, bf16[128,1024]{1,0:T(8,128)(2,1)S(1)} %collective-permute-done.19.phase, bf16[4,1024,512]{2,1,0:T(8,128)(2,1)S(1)} %copy-done.1, f32[128,512]{1,0:T(8,128)S(1)} %recon.4.before), custom_call_target="tpu_custom_call" | custom-call | flops 134217728 | bytes 1310720 | tf_op jit(solution)/shard_map/recon/pallas_call | solution.py:355
  61.6 0.0 collective-permute-done.7.refs_3_
  61.6 0.6 collective-permute-done.9.refs_5_
  62.2 1.0 %phase.3 = bf16[128,1024]{1,0:T(8,128)(2,1)S(1)} custom-call(s32[4]{0:T(128)S(1)} %pad_add_fusion.refs_0_.place, bf16[1024,1024]{1,0:T(8,128)(2,1)S(1)} %copy-done, bf16[128,256]{1,0:T(8,128)(2,1)S(1)} %get-tuple-element.27.refs_2_, bf16[128,256]{1,0:T(8,128)(2,1)S(1)} %collective-permute-done.7.refs_3_, ...), custom_call_target="tpu_custom_call" | custom-call | flops 268435456 | bytes 2621440 | tf_op jit(solution)/shard_map/phase/pallas_call | solution.py:389
  63.2 0.0 copy-start.4
  63.2 0.1 collective-permute-start.20
  63.3 0.9 %recon.6.before = f32[128,512]{1,0:T(8,128)S(1)} custom-call(s32[4]{0:T(128)S(1)} %pad_add_fusion.refs_0_.place, s32[4]{0:T(128)S(1)} %bitcast.11, bf16[128,1024]{1,0:T(8,128)(2,1)S(1)} %phase.3, bf16[4,1024,512]{2,1,0:T(8,128)(2,1)S(1)} %copy-done.1, f32[128,512]{1,0:T(8,128)S(1)} %recon.5.refs_6_.before), custom_call_target="tpu_custom_call" | custom-call | flops 134217728 | bytes 1310720 | tf_op jit(solution)/shard_map/recon/pallas_call | solution.py:355
  64.2 0.7 collective-permute-done.20.phase
  64.8 1.7 %recon.7 = bf16[128,512]{1,0:T(8,128)(2,1)} custom-call(s32[4]{0:T(128)S(1)} %pad_add_fusion.refs_0_.place, s32[4]{0:T(128)S(1)} %bitcast.12, s32[16]{0:T(128)S(1)} %copy-done.4, bf16[128,1024]{1,0:T(8,128)(2,1)S(1)} %collective-permute-done.20.phase, bf16[4,1024,512]{2,1,0:T(8,128)(2,1)S(1)} %copy-done.1, f32[128,512]{1,0:T(8,128)S(1)} %recon.6.before), custom_call_target="tpu_custom_call" | custom-call | flops 134217728 | bytes 1310720 | tf_op jit(solution)/shard_map/recon/pallas_call | solution.py:355
  (13 shorter events, 0.0 us)
Async XLA Ops:
  0.0 3.7 %copy-start = (bf16[1024,1024]{1,0:T(8,128)(2,1)S(1)}, bf16[1024,1024]{1,0:T(8,128)(2,1)}, u32[]{:S(2)}) copy-start(bf16[1024,1024]{1,0:T(8,128)(2,1)} %constant.59.clone.refs_3_.refs_1_) | copy-start | bytes 6291460
  0.0 3.7 %collective-permute-start = (bf16[4,2,64,1024]{3,2,1,0:T(8,128)(2,1)}, bf16[4,2,64,1024]{3,2,1,0:T(8,128)(2,1)S(1)}, u32[]{:S(2)}, u32[]{:S(2)}) collective-permute-start(bf16[4,2,64,1024]{3,2,1,0:T(8,128)(2,1)} %bitcast.6), channel_id=1, source_target_pairs={{0,16},{1,17},{2,18},{3,19},{4,20},{5,21},{6,22},{7,23},{8,24},{9,... | collective-permute-start | bytes 3145736 | tf_op jit(solution)/shard_map/ppermute | solution.py:256
  3.7 1.2 %copy-start.2 = (bf16[1,4,2,64,1024]{4,3,2,1,0:T(8,128)(2,1)S(1)}, bf16[1,4,2,64,1024]{4,3,2,1,0:T(8,128)(2,1)}, u32[]{:S(2)}) copy-start(bf16[1,4,2,64,1024]{4,3,2,1,0:T(8,128)(2,1)} %param.6) | copy-start | bytes 3145732
  6.2 8.9 %collective-permute-start.10 = (bf16[4,64,256]{2,1,0:T(8,128)(2,1)S(1)}, bf16[4,64,256]{2,1,0:T(8,128)(2,1)S(1)}, u32[]{:S(2)}, u32[]{:S(2)}) collective-permute-start(bf16[4,64,256]{2,1,0:T(8,128)(2,1)S(1)} %get-tuple-element.30), channel_id=1, source_target_pairs={{0,1},{1,0},{2,3},{3,2},{4,5},{5,4},{6,7},{7,6},{8,9},{9,8},{10,11... | collective-permute-start | bytes 393224 | tf_op jit(solution)/shard_map/ppermute | solution.py:256
  8.7 8.1 %collective-permute-start.11 = (bf16[4,64,256]{2,1,0:T(8,128)(2,1)S(1)}, bf16[4,64,256]{2,1,0:T(8,128)(2,1)S(1)}, u32[]{:S(2)}, u32[]{:S(2)}) collective-permute-start(bf16[4,64,256]{2,1,0:T(8,128)(2,1)S(1)} %get-tuple-element.31), channel_id=1, source_target_pairs={{0,2},{1,3},{2,0},{3,1},{4,6},{5,7},{6,4},{7,5},{8,10},{9,11},{10,... | collective-permute-start | bytes 393224 | tf_op jit(solution)/shard_map/ppermute | solution.py:256
  10.3 7.3 %collective-permute-start.12 = (bf16[4,64,256]{2,1,0:T(8,128)(2,1)S(1)}, bf16[4,64,256]{2,1,0:T(8,128)(2,1)S(1)}, u32[]{:S(2)}, u32[]{:S(2)}) collective-permute-start(bf16[4,64,256]{2,1,0:T(8,128)(2,1)S(1)} %get-tuple-element.32), channel_id=1, source_target_pairs={{0,3},{1,2},{2,1},{3,0},{4,7},{5,6},{6,5},{7,4},{8,11},{9,10},{10,... | collective-permute-start | bytes 393224 | tf_op jit(solution)/shard_map/ppermute | solution.py:256
  11.6 9.5 %collective-permute-start.1 = (bf16[4,64,256]{2,1,0:T(8,128)(2,1)S(1)}, bf16[4,64,256]{2,1,0:T(8,128)(2,1)S(1)}, u32[]{:S(2)}, u32[]{:S(2)}) collective-permute-start(bf16[4,64,256]{2,1,0:T(8,128)(2,1)S(1)} %get-tuple-element.22), channel_id=1, source_target_pairs={{0,1},{1,0},{2,3},{3,2},{4,5},{5,4},{6,7},{7,6},{8,9},{9,8},{10,11... | collective-permute-start | bytes 393224 | tf_op jit(solution)/shard_map/ppermute | solution.py:256
  13.6 9.1 %collective-permute-start.2 = (bf16[4,64,256]{2,1,0:T(8,128)(2,1)S(1)}, bf16[4,64,256]{2,1,0:T(8,128)(2,1)S(1)}, u32[]{:S(2)}, u32[]{:S(2)}) collective-permute-start(bf16[4,64,256]{2,1,0:T(8,128)(2,1)S(1)} %get-tuple-element.23), channel_id=1, source_target_pairs={{0,2},{1,3},{2,0},{3,1},{4,6},{5,7},{6,4},{7,5},{8,10},{9,11},{10,... | collective-permute-start | bytes 393224 | tf_op jit(solution)/shard_map/ppermute | solution.py:256
  15.1 7.6 %collective-permute-start.3 = (bf16[4,64,256]{2,1,0:T(8,128)(2,1)S(1)}, bf16[4,64,256]{2,1,0:T(8,128)(2,1)S(1)}, u32[]{:S(2)}, u32[]{:S(2)}) collective-permute-start(bf16[4,64,256]{2,1,0:T(8,128)(2,1)S(1)} %get-tuple-element.24), channel_id=1, source_target_pairs={{0,3},{1,2},{2,1},{3,0},{4,7},{5,6},{6,5},{7,4},{8,11},{9,10},{10,... | collective-permute-start | bytes 393224 | tf_op jit(solution)/shard_map/ppermute | solution.py:256
  19.4 7.0 %collective-permute-start.13 = (bf16[2,256,256]{2,1,0:T(8,128)(2,1)S(1)}, bf16[2,256,256]{2,1,0:T(8,128)(2,1)S(1)}, u32[]{:S(2)}, u32[]{:S(2)}) collective-permute-start(bf16[2,256,256]{2,1,0:T(8,128)(2,1)S(1)} %get-tuple-element.34.one), channel_id=1, source_target_pairs={{0,4},{1,5},{2,6},{3,7},{4,0},{5,1},{6,2},{7,3},{8,12},{9,13},{10,... | collective-permute-start | bytes 786440 | tf_op jit(solution)/shard_map/ppermute | solution.py:256
  24.6 7.5 %collective-permute-start.4 = (bf16[2,256,256]{2,1,0:T(8,128)(2,1)S(1)}, bf16[2,256,256]{2,1,0:T(8,128)(2,1)S(1)}, u32[]{:S(2)}, u32[]{:S(2)}) collective-permute-start(bf16[2,256,256]{2,1,0:T(8,128)(2,1)S(1)} %get-tuple-element.26.one), channel_id=1, source_target_pairs={{0,4},{1,5},{2,6},{3,7},{4,0},{5,1},{6,2},{7,3},{8,12},{9,13},{10,... | collective-permute-start | bytes 786440 | tf_op jit(solution)/shard_map/ppermute | solution.py:256
  26.5 5.7 %collective-permute-start.14 = (bf16[2,256,256]{2,1,0:T(8,128)(2,1)S(1)}, bf16[2,256,256]{2,1,0:T(8,128)(2,1)S(1)}, u32[]{:S(2)}, u32[]{:S(2)}) collective-permute-start(bf16[2,256,256]{2,1,0:T(8,128)(2,1)S(1)} %joint.3), channel_id=1, source_target_pairs={{0,16},{1,17},{2,18},{3,19},{4,8},{5,9},{6,10},{7,11},{8,4},{9,5},... | collective-permute-start | bytes 786440 | tf_op jit(solution)/shard_map/ppermute | solution.py:256
  32.2 3.9 %collective-permute-start.5 = (bf16[2,256,256]{2,1,0:T(8,128)(2,1)S(1)}, bf16[2,256,256]{2,1,0:T(8,128)(2,1)S(1)}, u32[]{:S(2)}, u32[]{:S(2)}) collective-permute-start(bf16[2,256,256]{2,1,0:T(8,128)(2,1)S(1)} %joint.2), channel_id=1, source_target_pairs={{0,16},{1,17},{2,18},{3,19},{4,8},{5,9},{6,10},{7,11},{8,4},{9,5},... | collective-permute-start | bytes 786440 | tf_op jit(solution)/shard_map/ppermute | solution.py:256
  32.9 6.1 %collective-permute-start.15 = (bf16[256,256]{1,0:T(8,128)(2,1)S(1)}, bf16[256,256]{1,0:T(8,128)(2,1)S(1)}, u32[]{:S(2)}, u32[]{:S(2)}) collective-permute-start(bf16[256,256]{1,0:T(8,128)(2,1)S(1)} %near.3), channel_id=1, source_target_pairs={{0,4},{1,5},{2,6},{3,7},{4,0},{5,1},{6,2},{7,3},{8,12},{9,13},{10,... | collective-permute-start | bytes 393224 | tf_op jit(solution)/shard_map/ppermute | solution.py:256
  36.7 23.2 %copy-start.1 = (bf16[4,1024,512]{2,1,0:T(8,128)(2,1)S(1)}, bf16[4,1024,512]{2,1,0:T(8,128)(2,1)}, u32[]{:S(2)}) copy-start(bf16[4,1024,512]{2,1,0:T(8,128)(2,1)} %weights.7) | copy-start | bytes 12582916
  36.7 23.1 %copy-start.3 = (s32[1,4]{1,0:T(1,128)S(1)}, s32[1,4]{1,0:T(1,128)}, u32[]{:S(2)}) copy-start(s32[1,4]{1,0:T(1,128)} %param.9) | copy-start | bytes 52
  39.6 4.9 %collective-permute-start.16 = (bf16[128,256]{1,0:T(8,128)(2,1)S(1)}, bf16[128,256]{1,0:T(8,128)(2,1)S(1)}, u32[]{:S(2)}, u32[]{:S(2)}) collective-permute-start(bf16[128,256]{1,0:T(8,128)(2,1)S(1)} %get-tuple-element.35.refs_2_), channel_id=1, source_target_pairs={{0,1},{1,0},{2,3},{3,2},{4,5},{5,4},{6,7},{7,6},{8,9},{9,8},{10,11... | collective-permute-start | bytes 196616 | tf_op jit(solution)/shard_map/ppermute | solution.py:256
  41.4 4.3 %collective-permute-start.17 = (bf16[128,256]{1,0:T(8,128)(2,1)S(1)}, bf16[128,256]{1,0:T(8,128)(2,1)S(1)}, u32[]{:S(2)}, u32[]{:S(2)}) collective-permute-start(bf16[128,256]{1,0:T(8,128)(2,1)S(1)} %get-tuple-element.36), channel_id=1, source_target_pairs={{0,2},{1,3},{2,0},{3,1},{4,6},{5,7},{6,4},{7,5},{8,10},{9,11},{10,... | collective-permute-start | bytes 196616 | tf_op jit(solution)/shard_map/ppermute | solution.py:256
  42.5 5.2 %collective-permute-start.18 = (bf16[128,256]{1,0:T(8,128)(2,1)S(1)}, bf16[128,256]{1,0:T(8,128)(2,1)S(1)}, u32[]{:S(2)}, u32[]{:S(2)}) collective-permute-start(bf16[128,256]{1,0:T(8,128)(2,1)S(1)} %get-tuple-element.36), channel_id=1, source_target_pairs={{0,3},{1,2},{2,1},{3,0},{4,7},{5,6},{6,5},{7,4},{8,11},{9,10},{10,... | collective-permute-start | bytes 196616 | tf_op jit(solution)/shard_map/ppermute | solution.py:256
  48.6 12.0 %collective-permute-start.19 = (bf16[128,1024]{1,0:T(8,128)(2,1)S(1)}, bf16[128,1024]{1,0:T(8,128)(2,1)S(1)}, u32[]{:S(2)}, u32[]{:S(2)}) collective-permute-start(bf16[128,1024]{1,0:T(8,128)(2,1)S(1)} %phase.2), channel_id=1, source_target_pairs={{0,16},{1,17},{2,18},{3,19},{4,20},{5,21},{6,22},{7,23},{8,24},{9,... | collective-permute-start | bytes 786440 | tf_op jit(solution)/shard_map/ppermute | solution.py:256
  48.7 6.9 %collective-permute-start.6 = (bf16[256,256]{1,0:T(8,128)(2,1)S(1)}, bf16[256,256]{1,0:T(8,128)(2,1)S(1)}, u32[]{:S(2)}, u32[]{:S(2)}) collective-permute-start(bf16[256,256]{1,0:T(8,128)(2,1)S(1)} %near.2.after), channel_id=1, source_target_pairs={{0,4},{1,5},{2,6},{3,7},{4,0},{5,1},{6,2},{7,3},{8,12},{9,13},{10,... | collective-permute-start | bytes 393224 | tf_op jit(solution)/shard_map/ppermute | solution.py:256
  56.3 5.3 %collective-permute-start.7 = (bf16[128,256]{1,0:T(8,128)(2,1)S(1)}, bf16[128,256]{1,0:T(8,128)(2,1)S(1)}, u32[]{:S(2)}, u32[]{:S(2)}) collective-permute-start(bf16[128,256]{1,0:T(8,128)(2,1)S(1)} %get-tuple-element.27.refs_2_), channel_id=1, source_target_pairs={{0,1},{1,0},{2,3},{3,2},{4,5},{5,4},{6,7},{7,6},{8,9},{9,8},{10,11... | collective-permute-start | bytes 196616 | tf_op jit(solution)/shard_map/ppermute | solution.py:256
  56.6 5.0 %collective-permute-start.8 = (bf16[128,256]{1,0:T(8,128)(2,1)S(1)}, bf16[128,256]{1,0:T(8,128)(2,1)S(1)}, u32[]{:S(2)}, u32[]{:S(2)}) collective-permute-start(bf16[128,256]{1,0:T(8,128)(2,1)S(1)} %get-tuple-element.28), channel_id=1, source_target_pairs={{0,2},{1,3},{2,0},{3,1},{4,6},{5,7},{6,4},{7,5},{8,10},{9,11},{10,... | collective-permute-start | bytes 196616 | tf_op jit(solution)/shard_map/ppermute | solution.py:256
  57.0 5.2 %collective-permute-start.9 = (bf16[128,256]{1,0:T(8,128)(2,1)S(1)}, bf16[128,256]{1,0:T(8,128)(2,1)S(1)}, u32[]{:S(2)}, u32[]{:S(2)}) collective-permute-start(bf16[128,256]{1,0:T(8,128)(2,1)S(1)} %get-tuple-element.28), channel_id=1, source_target_pairs={{0,3},{1,2},{2,1},{3,0},{4,7},{5,6},{6,5},{7,4},{8,11},{9,10},{10,... | collective-permute-start | bytes 196616 | tf_op jit(solution)/shard_map/ppermute | solution.py:256
  63.2 1.6 %copy-start.4 = (s32[16]{0:T(128)S(1)}, s32[16]{0:T(128)}, u32[]{:S(2)}) copy-start(s32[16]{0:T(128)} %slabs.1) | copy-start | bytes 196
  63.2 1.6 %collective-permute-start.20 = (bf16[128,1024]{1,0:T(8,128)(2,1)S(1)}, bf16[128,1024]{1,0:T(8,128)(2,1)S(1)}, u32[]{:S(2)}, u32[]{:S(2)}) collective-permute-start(bf16[128,1024]{1,0:T(8,128)(2,1)S(1)} %phase.3), channel_id=1, source_target_pairs={{0,16},{1,17},{2,18},{3,19},{4,20},{5,21},{6,22},{7,23},{8,24},{9,... | collective-permute-start | bytes 786440 | tf_op jit(solution)/shard_map/ppermute | solution.py:256

commit v7 on v6

--- a/solution.py
+++ b/solution.py
@@ -91,13 +91,12 @@
     return jnp.dot(select, paired, preferred_element_type=f32).astype(bf16)
 
 
-def row_kernel(inner, own, chunk, place, here, there, table, after, *outs):
-    core, spot = place[0], place[1]
+def row_kernel(inner, place, here, there, table, after, *outs):
+    spot = place[1]
     dist_dev, rows_dev, width = here.shape[1:]
     block = width // inner
-    angle = core * own + chunk
     flat = jnp.concatenate(
-        [source[angle].reshape(dist_dev * rows_dev, width) for source in (here, there)], axis=0
+        [source[0].reshape(dist_dev * rows_dev, width) for source in (here, there)], axis=0
     )
     for rel in range(inner):
         part = table[:, pl.ds(pl.multiple_of((spot ^ rel) * block, block), block)]
@@ -185,26 +184,26 @@
     out[...] = jnp.dot(joined[...], table[...], preferred_element_type=f32).astype(bf16)
 
 
-def recon_kernel(place, order, phase, weights, out):
-    out[...] = jnp.dot(phase[...], weights[0], preferred_element_type=f32)
-
-
-def recon_more_kernel(place, order, phase, weights, before, out):
-    out[...] = before[...] + jnp.dot(phase[...], weights[0], preferred_element_type=f32)
-
-
-def recon_last_kernel(place, order, slabs, phase, weights, before, out):
-    total = before[...] + jnp.dot(phase[...], weights[0], preferred_element_type=f32)
+def recon_kernel(own, chunk, cores, place, order, weights, *refs):
+    phases, out = refs[: len(cores)], refs[-1]
+    total = refs[-2][...] if len(refs) > len(cores) + 1 else None
+    for other, phase in zip(cores, phases):
+        chosen = weights[order[0, (place[0] ^ other) * own + chunk]]
+        got = jnp.dot(phase[...], chosen, preferred_element_type=f32)
+        total = got if total is None else total + got
+    out[...] = total
+
+
+def recon_last_kernel(own, chunk, other, place, order, slabs, weights, phase, before, out):
+    chosen = weights[order[0, (place[0] ^ other) * own + chunk]]
+    total = before[...] + jnp.dot(phase[...], chosen, preferred_element_type=f32)
     capacity = total.shape[0]
     device = place[3]
     parity = device % 2
     offset = parity * slabs[device - parity]
-    slot = lax.broadcasted_iota(jnp.int32, (capacity, capacity), 0)
-    source = lax.broadcasted_iota(jnp.int32, (capacity, capacity), 1)
-    select = (source == slot + offset) & (slot < slabs[device])
-    select = jnp.where(select, 1.0, 0.0).astype(bf16)
-    picked = jnp.dot(select, total.astype(bf16), preferred_element_type=f32)
-    out[...] = picked.astype(bf16)
+    turned = pltpu.roll(total, lax.rem(capacity - offset, capacity), 0)
+    slot = lax.broadcasted_iota(jnp.int32, turned.shape, 0)
+    out[...] = jnp.where(slot < slabs[device], turned, 0.0).astype(bf16)
 
 
 def vmem(count):
@@ -260,6 +259,10 @@
 
     def to_spot(rel):
         return lambda c, r: (c, r ^ rel)
+
+    def spread(pieces):
+        got = {rel: sent(pieces[rel], to_spot(rel)) for rel in (2, 3, 1)}
+        return [pieces[0]] + [got[rel] for rel in range(1, inner)]
 
     def to_near_plane(c, r):
         return c, (r // inner ^ 1) * inner + r % inner
@@ -297,17 +300,29 @@
     arrived = []
     for chunk in range(own):
         pieces = pl.pallas_call(
-            lambda *refs, chunk=chunk: row_kernel(inner, own, chunk, *refs),
+            lambda *refs: row_kernel(inner, *refs),
             out_shape=[shaped(dists, rows_dev, block)] * inner,
-            in_specs=smem(1) + vmem(3) + unread(1),
-            out_specs=vmem(inner),
+            grid_spec=pltpu.PrefetchScalarGridSpec(
+                num_scalar_prefetch=1,
+                grid=(1,),
+                in_specs=[
+                    pl.BlockSpec(
+                        (1, dist_dev, rows_dev, width),
+                        lambda i, place, chunk=chunk: (place[0] * own + chunk, 0, 0, 0),
+                    )
+                ]
+                * 2
+                + vmem(1)
+                + unread(1),
+                out_specs=vmem(inner),
+            ),
             compiler_params=params,
             cost_estimate=cost(
                 2 * dists * rows_dev * width * width, (width, width), (2, dists, rows_dev, width)
             ),
             name="row_spectra",
         )(place, holograms[0], partner, table, gain)
-        arrived.append([pieces[0]] + [sent(pieces[rel], to_spot(rel)) for rel in range(1, inner)])
+        arrived.append(spread(pieces))
 
     sums = []
     for chunk in range(own):
@@ -348,33 +363,19 @@
         )(place, keep, across)
         sums.append((keep, across, sent(near, to_near_plane)))
 
-    def recon(kernel, out_type, other, chunk, scalars, phase, *before):
-        def angle(place):
-            return (place[0] ^ other) * own + chunk
-
+    def recon(kernel, out_type, scalars, *arrays):
         return pl.pallas_call(
             kernel,
             out_shape=jax.ShapeDtypeStruct((capacity, pixels), out_type),
-            grid_spec=pltpu.PrefetchScalarGridSpec(
-                num_scalar_prefetch=len(scalars),
-                grid=(1,),
-                in_specs=vmem(1)
-                + [
-                    pl.BlockSpec(
-                        (1, width, pixels),
-                        lambda i, place, order, *slabs: (order[angle(place)], 0, 0),
-                    )
-                ]
-                + vmem(len(before)),
-                out_specs=one_out,
-            ),
-            compiler_params=params,
-            cost_estimate=cost(2 * capacity * width * pixels, (width, capacity + pixels)),
+            in_specs=smem(len(scalars)) + vmem(1 + len(arrays)),
+            out_specs=one_out,
+            compiler_params=params,
+            cost_estimate=cost(1, (8, pixels)),
             name="recon",
-        )(*scalars, phase, weights, *before)
+        )(*scalars, weights, *arrays)
 
     total = None
-    scalars = (place, angle_order[0])
+    scalars = (place, angle_order)
     for chunk in range(own):
         mine, other = pl.pallas_call(
             half_kernel,
@@ -382,29 +383,36 @@
             in_specs=smem(1) + vmem(3) + unread(1),
             out_specs=vmem(2),
             compiler_params=params,
-            cost_estimate=cost(depth * block, (5, depth, block)),
+            cost_estimate=cost(1, (8, width)),
             name="half",
         )(place, *sums[chunk], near)
-        pieces = [mine] + [sent(mine if rel < 2 else other, to_spot(rel)) for rel in range(1, inner)]
+        pieces = spread([mine, mine, other, other])
         phase = pl.pallas_call(
             lambda *refs: phase_kernel(inner, *refs),
             out_shape=shaped(capacity, width),
-            in_specs=smem(1) + vmem(1 + inner) + unread(0 if total is None else 1),
+            in_specs=smem(1) + vmem(1 + inner),
             out_specs=one_out,
             scratch_shapes=[pltpu.VMEM((capacity, width), bf16)],
             compiler_params=params,
-            cost_estimate=cost(2 * capacity * width * width, (width, width), (2, capacity, width)),
+            cost_estimate=cost(1, (8, width)),
             name="phase",
-        )(place, table, *pieces, *([] if total is None else [total]))
+        )(place, table, *pieces)
         there = sent(phase, to_other_core)
-        if total is None:
-            total = recon(recon_kernel, f32, 0, chunk, scalars, phase)
+        def part(cores, chunk=chunk):
+            return lambda *refs: recon_kernel(own, chunk, cores, *refs)
+
+        before = [] if total is None else [total]
+        if chunk < own - 1:
+            total = recon(part((0, 1)), f32, scalars, phase, there, *before)
         else:
-            total = recon(recon_more_kernel, f32, 0, chunk, scalars, phase, total)
-        if chunk < own - 1:
-            total = recon(recon_more_kernel, f32, 1, chunk, scalars, there, total)
-        else:
-            total = recon(recon_last_kernel, bf16, 1, chunk, scalars + (slab_rows,), there, total)
+            total = recon(part((0,)), f32, scalars, phase, *before)
+            total = recon(
+                lambda *refs, chunk=chunk: recon_last_kernel(own, chunk, 1, *refs),
+                bf16,
+                scalars + (slab_rows,),
+                there,
+                total,
+            )
     return total
 
 

time: 66.7 us -> 58.7 us (0.88)
  waiting for transfers between devices: 21.1 us -> 12.1 us
  starting transfers between devices: 25.6 us -> 27.4 us
  Pallas kernels: 16.8 us -> 16.1 us
    ppermute x21, waiting for transfers between devices: 21.1 us -> 12.1 us  [sent(): return lax.ppermute(value, ('dist', 'rows'), pairs)]
    ppermute x21, starting transfers between devices: 25.6 us -> 27.4 us  [sent(): return lax.ppermute(value, ('dist', 'rows'), pairs)]
    pallas_call x4 -> x3, Pallas kernels: 4.26 us -> 3.48 us  [recon(): pl.pallas_call(kernel, out_shape=jax.ShapeDtypeStruct((capacity, pixels),...]
  transfers between devices with their start and end apart: 21 -> 21, of which waited for: 12 -> 8; matrix products, arithmetic and copies ran while one was open for 2% -> 2% of each run, Pallas kernels for 17% -> 22%
where the time goes in v7:
time: 58.7 us; the launch traced here: 58.5 us
  starting transfers between devices  27.4 us (47%)
  Pallas kernels  16.1 us (27%)
  waiting for transfers between devices  12.1 us (21%)
  local copies, waits for them, and re-layouts  2.16 us (4%)
    ppermute x21, starting transfers between devices, sent(): return lax.ppermute(value, ('dist', 'rows'), pairs)  27.4 us
    ppermute x21, waiting for transfers between devices, sent(): return lax.ppermute(value, ('dist', 'rows'), pairs)  12.1 us
    pallas_call x2, Pallas kernels, plane_plan(): pl.pallas_call(lambda *refs: column_kernel(inner, outer, *refs), out_shap...  3.71 us
    pallas_call x3, Pallas kernels, recon(): pl.pallas_call(kernel, out_shape=jax.ShapeDtypeStruct((capacity, pixels),...  3.48 us
    pallas_call x2, Pallas kernels, plane_plan(): pl.pallas_call(lambda *refs: row_kernel(inner, *refs), out_shape=[shaped(...  2.57 us
    pallas_call x2, Pallas kernels, plane_plan(): pl.pallas_call(lambda *refs: phase_kernel(inner, *refs), out_shape=shaped...  2 us
    pallas_call x1, Pallas kernels, plane_plan(): pl.pallas_call(filter_kernel, out_shape=shaped(dists, width, block), in_s...  1.78 us
    unnamed x10, local copies, waits for them, and re-layouts  1.24 us
  transfers between devices with their start and end apart: 21, of which 8 were waited for; matrix products, arithmetic and copies ran while one was open for 2% of the time, Pallas kernels for 22%

profile of v7, /device:TPU:0, one launch (start us, length us, event | category | flops | bytes accessed | tf_op | source)
XLA Modules:
  0.0 58.5 jit_solution(11361962125374267496)
XLA Ops:
  0.0 0.5 collective-permute-start
  0.5 0.9 %fusion.12 = (f32[2]{0:T(128)S(1)}, f32[2]{0:T(128)S(1)}) fusion(f32[4]{0:T(128)} %param.7, s32[]{:T(128)S(6)} %select_n.35, s32[]{:T(128)S(6)} %select_n.36), kind=kLoop, calls=%fused_computation.21 | loop fusion | bytes 40 | tf_op jit(solution)/shard_map/dynamic_slice | solution.py:278
  1.4 0.1 pad_maximum_fusion.1
  1.5 0.2 multiply_sine_fusion
  1.7 0.1 fusion.5
  1.8 1.8 %filters.1.refs_4_.refs_2_ = bf16[4,1024,256]{2,1,0:T(8,128)(2,1)S(1)} custom-call(f32[8,1024]{1,0:T(8,128)S(1)} %pad_maximum_fusion.waves_a, f32[4,256]{1,0:T(4,128)S(1)} %get-tuple-element.40.with_sin, f32[4,256]{1,0:T(4,128)S(1)} %get-tuple-element.39.with_cos), custom_call_target="tpu_custom_call" | custom-call | flops 8388608 | bytes 2097152 | tf_op jit(solution)/shard_map/filters/pallas_call | solution.py:285
  3.6 0.1 pad_add_fusion.refs_0_.place
  3.7 0.0 collective-permute-done.refs_2_
  3.7 1.2 %copy-done.2 = bf16[1,4,2,64,1024]{4,3,2,1,0:T(8,128)(2,1)S(1)} copy-done((bf16[1,4,2,64,1024]{4,3,2,1,0:T(8,128)(2,1)S(1)}, bf16[1,4,2,64,1024]{4,3,2,1,0:T(8,128)(2,1)}, u32[]{:S(2)}) %copy-start.2) | copy-done | bytes 1048600
  4.9 1.3 %row_spectra.3 = (bf16[4,64,256]{2,1,0:T(8,128)(2,1)S(1)}, bf16[4,64,256]{2,1,0:T(8,128)(2,1)S(1)}, bf16[4,64,256]{2,1,0:T(8,128)(2,1)S(1)}, bf16[4,64,256]{2,1,0:T(8,128)(2,1)S(1)}) custom-call(s32[4]{0:T(128)S(1)} %pad_add_fusion.refs_0_.place, bf16[4,2,64,1024]{3,2,1,0:T(8,128)(2,1)S(1)} %bitcast.6, ...), custom_call_target="tpu_custom_call" | custom-call | flops 536870912 | bytes 3145728 | tf_op jit(solution)/shard_map/row_spectra/pallas_call | solution.py:302
  6.2 2.5 %collective-permute-start.11 = (bf16[4,64,256]{2,1,0:T(8,128)(2,1)S(1)}, bf16[4,64,256]{2,1,0:T(8,128)(2,1)S(1)}, u32[]{:S(2)}, u32[]{:S(2)}) collective-permute-start(bf16[4,64,256]{2,1,0:T(8,128)(2,1)S(1)} %get-tuple-element.30), channel_id=1, source_target_pairs={{0,1},{1,0},{2,3},{3,2},{4,5},{5,4},{6,7},{7,6},{8,9},{9,8},{10,11... | collective-permute-start | bytes 393224 | tf_op jit(solution)/shard_map/ppermute | solution.py:255
  8.7 1.5 %collective-permute-start.12 = (bf16[4,64,256]{2,1,0:T(8,128)(2,1)S(1)}, bf16[4,64,256]{2,1,0:T(8,128)(2,1)S(1)}, u32[]{:S(2)}, u32[]{:S(2)}) collective-permute-start(bf16[4,64,256]{2,1,0:T(8,128)(2,1)S(1)} %get-tuple-element.31), channel_id=1, source_target_pairs={{0,2},{1,3},{2,0},{3,1},{4,6},{5,7},{6,4},{7,5},{8,10},{9,11},{10,... | collective-permute-start | bytes 393224 | tf_op jit(solution)/shard_map/ppermute | solution.py:255
  10.3 0.0 collective-permute-start.13
  10.3 1.3 %row_spectra.2 = (bf16[4,64,256]{2,1,0:T(8,128)(2,1)S(1)}, bf16[4,64,256]{2,1,0:T(8,128)(2,1)S(1)}, bf16[4,64,256]{2,1,0:T(8,128)(2,1)S(1)}, bf16[4,64,256]{2,1,0:T(8,128)(2,1)S(1)}) custom-call(s32[4]{0:T(128)S(1)} %pad_add_fusion.refs_0_.place, bf16[4,2,64,1024]{3,2,1,0:T(8,128)(2,1)S(1)} %bitcast.7, ...), custom_call_target="tpu_custom_call" | custom-call | flops 536870912 | bytes 3145728 | tf_op jit(solution)/shard_map/row_spectra/pallas_call | solution.py:302
  11.6 2.0 %collective-permute-start.1 = (bf16[4,64,256]{2,1,0:T(8,128)(2,1)S(1)}, bf16[4,64,256]{2,1,0:T(8,128)(2,1)S(1)}, u32[]{:S(2)}, u32[]{:S(2)}) collective-permute-start(bf16[4,64,256]{2,1,0:T(8,128)(2,1)S(1)} %get-tuple-element.22), channel_id=1, source_target_pairs={{0,1},{1,0},{2,3},{3,2},{4,5},{5,4},{6,7},{7,6},{8,9},{9,8},{10,11... | collective-permute-start | bytes 393224 | tf_op jit(solution)/shard_map/ppermute | solution.py:255
  13.6 1.5 %collective-permute-start.2 = (bf16[4,64,256]{2,1,0:T(8,128)(2,1)S(1)}, bf16[4,64,256]{2,1,0:T(8,128)(2,1)S(1)}, u32[]{:S(2)}, u32[]{:S(2)}) collective-permute-start(bf16[4,64,256]{2,1,0:T(8,128)(2,1)S(1)} %get-tuple-element.23), channel_id=1, source_target_pairs={{0,2},{1,3},{2,0},{3,1},{4,6},{5,7},{6,4},{7,5},{8,10},{9,11},{10,... | collective-permute-start | bytes 393224 | tf_op jit(solution)/shard_map/ppermute | solution.py:255
  15.1 0.0 collective-permute-done.11.refs_4_
  15.1 0.9 %collective-permute-start.3 = (bf16[4,64,256]{2,1,0:T(8,128)(2,1)S(1)}, bf16[4,64,256]{2,1,0:T(8,128)(2,1)S(1)}, u32[]{:S(2)}, u32[]{:S(2)}) collective-permute-start(bf16[4,64,256]{2,1,0:T(8,128)(2,1)S(1)} %get-tuple-element.24), channel_id=1, source_target_pairs={{0,3},{1,2},{2,1},{3,0},{4,7},{5,6},{6,5},{7,4},{8,11},{9,10},{10,... | collective-permute-start | bytes 393224 | tf_op jit(solution)/shard_map/ppermute | solution.py:255
  16.0 0.9 %collective-permute-done.12.refs_5_ = bf16[4,64,256]{2,1,0:T(8,128)(2,1)S(1)} collective-permute-done((bf16[4,64,256]{2,1,0:T(8,128)(2,1)S(1)}, bf16[4,64,256]{2,1,0:T(8,128)(2,1)S(1)}, u32[]{:S(2)}, u32[]{:S(2)}) %collective-permute-start.12) | collective-permute-done | bytes 131104 | tf_op jit(solution)/shard_map/ppermute | solution.py:255
  16.9 0.7 %collective-permute-done.13.refs_6_ = bf16[4,64,256]{2,1,0:T(8,128)(2,1)S(1)} collective-permute-done((bf16[4,64,256]{2,1,0:T(8,128)(2,1)S(1)}, bf16[4,64,256]{2,1,0:T(8,128)(2,1)S(1)}, u32[]{:S(2)}, u32[]{:S(2)}) %collective-permute-start.13) | collective-permute-done | bytes 131104 | tf_op jit(solution)/shard_map/ppermute | solution.py:255
  17.6 1.9 %columns.3 = (bf16[2,256,256]{2,1,0:T(8,128)(2,1)S(1)}, bf16[2,256,256]{2,1,0:T(8,128)(2,1)S(1)}) custom-call(s32[4]{0:T(128)S(1)} %pad_add_fusion.refs_0_.place, bf16[1024,1024]{1,0:T(8,128)(2,1)S(1)} %copy-done, bf16[4,1024,256]{2,1,0:T(8,128)(2,1)S(1)} %filters.1.refs_4_.refs_2_, bf16[4,64,256]{2,1,0:T(8,128)(2,1)S(1)} %get-tuple-element.29.refs_3_, ...), custom_call_target="tpu_custom_call" | custom-call | flops 1073741824 | bytes 4194304 | tf_op jit(solution)/shard_map/columns/pallas_call | solution.py:329
  19.4 1.6 %collective-permute-start.14 = (bf16[2,256,256]{2,1,0:T(8,128)(2,1)S(1)}, bf16[2,256,256]{2,1,0:T(8,128)(2,1)S(1)}, u32[]{:S(2)}, u32[]{:S(2)}) collective-permute-start(bf16[2,256,256]{2,1,0:T(8,128)(2,1)S(1)} %get-tuple-element.34.one), channel_id=1, source_target_pairs={{0,4},{1,5},{2,6},{3,7},{4,0},{5,1},{6,2},{7,3},{8,12},{9,13},{10,... | collective-permute-start | bytes 786440 | tf_op jit(solution)/shard_map/ppermute | solution.py:255
  21.1 0.0 collective-permute-done.1.refs_4_
  21.1 1.6 %collective-permute-done.2.refs_5_ = bf16[4,64,256]{2,1,0:T(8,128)(2,1)S(1)} collective-permute-done((bf16[4,64,256]{2,1,0:T(8,128)(2,1)S(1)}, bf16[4,64,256]{2,1,0:T(8,128)(2,1)S(1)}, u32[]{:S(2)}, u32[]{:S(2)}) %collective-permute-start.2) | collective-permute-done | bytes 131104 | tf_op jit(solution)/shard_map/ppermute | solution.py:255
  22.7 0.0 collective-permute-done.3.refs_6_
  22.7 1.9 %columns.2 = (bf16[2,256,256]{2,1,0:T(8,128)(2,1)S(1)}, bf16[2,256,256]{2,1,0:T(8,128)(2,1)S(1)}) custom-call(s32[4]{0:T(128)S(1)} %pad_add_fusion.refs_0_.place, bf16[1024,1024]{1,0:T(8,128)(2,1)S(1)} %copy-done, bf16[4,1024,256]{2,1,0:T(8,128)(2,1)S(1)} %filters.1.refs_4_.refs_2_, bf16[4,64,256]{2,1,0:T(8,128)(2,1)S(1)} %get-tuple-element.21.refs_3_, ...), custom_call_target="tpu_custom_call" | custom-call | flops 1073741824 | bytes 4194304 | tf_op jit(solution)/shard_map/columns/pallas_call | solution.py:329
  24.6 1.6 %collective-permute-start.4 = (bf16[2,256,256]{2,1,0:T(8,128)(2,1)S(1)}, bf16[2,256,256]{2,1,0:T(8,128)(2,1)S(1)}, u32[]{:S(2)}, u32[]{:S(2)}) collective-permute-start(bf16[2,256,256]{2,1,0:T(8,128)(2,1)S(1)} %get-tuple-element.26.one), channel_id=1, source_target_pairs={{0,4},{1,5},{2,6},{3,7},{4,0},{5,1},{6,2},{7,3},{8,12},{9,13},{10,... | collective-permute-start | bytes 786440 | tf_op jit(solution)/shard_map/ppermute | solution.py:255
  26.2 0.2 collective-permute-done.14.two
  26.5 0.1 joint.3
  26.5 0.1 collective-permute-start.15
  26.6 5.5 %collective-permute-done.4.two = bf16[2,256,256]{2,1,0:T(8,128)(2,1)S(1)} collective-permute-done((bf16[2,256,256]{2,1,0:T(8,128)(2,1)S(1)}, bf16[2,256,256]{2,1,0:T(8,128)(2,1)S(1)}, u32[]{:S(2)}, u32[]{:S(2)}) %collective-permute-start.4) | collective-permute-done | bytes 262176 | tf_op jit(solution)/shard_map/ppermute | solution.py:255
  32.1 0.1 joint.2
  32.2 0.1 collective-permute-start.5
  32.3 0.0 collective-permute-done.15.across
  32.3 0.6 %near.3 = bf16[256,256]{1,0:T(8,128)(2,1)S(1)} custom-call(s32[4]{0:T(128)S(1)} %pad_add_fusion.refs_0_.place, bf16[2,256,256]{2,1,0:T(8,128)(2,1)S(1)} %get-tuple-element.33.keep, bf16[2,256,256]{2,1,0:T(8,128)(2,1)S(1)} %collective-permute-done.15.across), custom_call_target="tpu_custom_call" | custom-call | flops 65536 | bytes 393216 | tf_op jit(solution)/shard_map/near/pallas_call | solution.py:355
  32.9 3.2 %collective-permute-start.16 = (bf16[256,256]{1,0:T(8,128)(2,1)S(1)}, bf16[256,256]{1,0:T(8,128)(2,1)S(1)}, u32[]{:S(2)}, u32[]{:S(2)}) collective-permute-start(bf16[256,256]{1,0:T(8,128)(2,1)S(1)} %near.3), channel_id=1, source_target_pairs={{0,4},{1,5},{2,6},{3,7},{4,0},{5,1},{6,2},{7,3},{8,12},{9,13},{10,... | collective-permute-start | bytes 393224 | tf_op jit(solution)/shard_map/ppermute | solution.py:255
  36.1 0.0 collective-permute-done.5.across
  36.1 0.6 %near.2.after = bf16[256,256]{1,0:T(8,128)(2,1)S(1)} custom-call(s32[4]{0:T(128)S(1)} %pad_add_fusion.refs_0_.place, bf16[2,256,256]{2,1,0:T(8,128)(2,1)S(1)} %get-tuple-element.25.keep, bf16[2,256,256]{2,1,0:T(8,128)(2,1)S(1)} %collective-permute-done.5.across), custom_call_target="tpu_custom_call" | custom-call | flops 65536 | bytes 393216 | tf_op jit(solution)/shard_map/near/pallas_call | solution.py:355
  36.7 4.6 %collective-permute-start.6 = (bf16[256,256]{1,0:T(8,128)(2,1)S(1)}, bf16[256,256]{1,0:T(8,128)(2,1)S(1)}, u32[]{:S(2)}, u32[]{:S(2)}) collective-permute-start(bf16[256,256]{1,0:T(8,128)(2,1)S(1)} %near.2.after), channel_id=1, source_target_pairs={{0,4},{1,5},{2,6},{3,7},{4,0},{5,1},{6,2},{7,3},{8,12},{9,13},{10,... | collective-permute-start | bytes 393224 | tf_op jit(solution)/shard_map/ppermute | solution.py:255
  41.2 0.0 collective-permute-done.16.last
  41.2 0.6 %half.3 = (bf16[128,256]{1,0:T(8,128)(2,1)S(1)}, bf16[128,256]{1,0:T(8,128)(2,1)S(1)}) custom-call(s32[4]{0:T(128)S(1)} %pad_add_fusion.refs_0_.place, bf16[2,256,256]{2,1,0:T(8,128)(2,1)S(1)} %get-tuple-element.33.keep, bf16[2,256,256]{2,1,0:T(8,128)(2,1)S(1)} %collective-permute-done.15.across, bf16[256,256]{1,0:T(8,128)(2,1)S(1)} %collective-permute-done.16.last, ...), custom_call_target="tpu_custom_call" | custom-call | flops 1 | bytes 16384 | tf_op jit(solution)/shard_map/half/pallas_call | solution.py:380
  41.9 1.9 %collective-permute-start.17 = (bf16[128,256]{1,0:T(8,128)(2,1)S(1)}, bf16[128,256]{1,0:T(8,128)(2,1)S(1)}, u32[]{:S(2)}, u32[]{:S(2)}) collective-permute-start(bf16[128,256]{1,0:T(8,128)(2,1)S(1)} %get-tuple-element.35.refs_2_), channel_id=1, source_target_pairs={{0,1},{1,0},{2,3},{3,2},{4,5},{5,4},{6,7},{7,6},{8,9},{9,8},{10,11... | collective-permute-start | bytes 196616 | tf_op jit(solution)/shard_map/ppermute | solution.py:255
  43.8 1.2 %collective-permute-start.19 = (bf16[128,256]{1,0:T(8,128)(2,1)S(1)}, bf16[128,256]{1,0:T(8,128)(2,1)S(1)}, u32[]{:S(2)}, u32[]{:S(2)}) collective-permute-start(bf16[128,256]{1,0:T(8,128)(2,1)S(1)} %get-tuple-element.36), channel_id=1, source_target_pairs={{0,3},{1,2},{2,1},{3,0},{4,7},{5,6},{6,5},{7,4},{8,11},{9,10},{10,... | collective-permute-start | bytes 196616 | tf_op jit(solution)/shard_map/ppermute | solution.py:255
  45.0 0.4 collective-permute-start.18
  45.4 0.0 collective-permute-done.6.last
  45.4 0.6 %half.2 = (bf16[128,256]{1,0:T(8,128)(2,1)S(1)}, bf16[128,256]{1,0:T(8,128)(2,1)S(1)}) custom-call(s32[4]{0:T(128)S(1)} %pad_add_fusion.refs_0_.place, bf16[2,256,256]{2,1,0:T(8,128)(2,1)S(1)} %get-tuple-element.25.keep, bf16[2,256,256]{2,1,0:T(8,128)(2,1)S(1)} %collective-permute-done.5.across, bf16[256,256]{1,0:T(8,128)(2,1)S(1)} %collective-permute-done.6.last, ...), custom_call_target="tpu_custom_call" | custom-call | flops 1 | bytes 16384 | tf_op jit(solution)/shard_map/half/pallas_call | solution.py:380
  46.0 1.9 %collective-permute-start.7 = (bf16[128,256]{1,0:T(8,128)(2,1)S(1)}, bf16[128,256]{1,0:T(8,128)(2,1)S(1)}, u32[]{:S(2)}, u32[]{:S(2)}) collective-permute-start(bf16[128,256]{1,0:T(8,128)(2,1)S(1)} %get-tuple-element.27.refs_2_), channel_id=1, source_target_pairs={{0,1},{1,0},{2,3},{3,2},{4,5},{5,4},{6,7},{7,6},{8,9},{9,8},{10,11... | collective-permute-start | bytes 196616 | tf_op jit(solution)/shard_map/ppermute | solution.py:255
  48.0 1.2 %collective-permute-start.9 = (bf16[128,256]{1,0:T(8,128)(2,1)S(1)}, bf16[128,256]{1,0:T(8,128)(2,1)S(1)}, u32[]{:S(2)}, u32[]{:S(2)}) collective-permute-start(bf16[128,256]{1,0:T(8,128)(2,1)S(1)} %get-tuple-element.28), channel_id=1, source_target_pairs={{0,3},{1,2},{2,1},{3,0},{4,7},{5,6},{6,5},{7,4},{8,11},{9,10},{10,... | collective-permute-start | bytes 196616 | tf_op jit(solution)/shard_map/ppermute | solution.py:255
  49.2 0.0 collective-permute-done.17.refs_3_
  49.2 0.4 collective-permute-start.8
  49.6 0.0 collective-permute-done.19.refs_5_
  49.6 1.2 %collective-permute-done.18.refs_4_ = bf16[128,256]{1,0:T(8,128)(2,1)S(1)} collective-permute-done((bf16[128,256]{1,0:T(8,128)(2,1)S(1)}, bf16[128,256]{1,0:T(8,128)(2,1)S(1)}, u32[]{:S(2)}, u32[]{:S(2)}) %collective-permute-start.18) | collective-permute-done | bytes 65568 | tf_op jit(solution)/shard_map/ppermute | solution.py:255
  50.8 1.0 %phase.3.refs_3_ = bf16[128,1024]{1,0:T(8,128)(2,1)S(1)} custom-call(s32[4]{0:T(128)S(1)} %pad_add_fusion.refs_0_.place, bf16[1024,1024]{1,0:T(8,128)(2,1)S(1)} %copy-done, bf16[128,256]{1,0:T(8,128)(2,1)S(1)} %get-tuple-element.35.refs_2_, bf16[128,256]{1,0:T(8,128)(2,1)S(1)} %collective-permute-done.17.refs_3_, ...), custom_call_target="tpu_custom_call" | custom-call | flops 1 | bytes 16384 | tf_op jit(solution)/shard_map/phase/pallas_call | solution.py:390
  51.8 0.1 collective-permute-start.20
  51.9 0.0 collective-permute-done.7.refs_3_
  51.9 1.3 %collective-permute-done.9.refs_5_ = bf16[128,256]{1,0:T(8,128)(2,1)S(1)} collective-permute-done((bf16[128,256]{1,0:T(8,128)(2,1)S(1)}, bf16[128,256]{1,0:T(8,128)(2,1)S(1)}, u32[]{:S(2)}, u32[]{:S(2)}) %collective-permute-start.9) | collective-permute-done | bytes 65568 | tf_op jit(solution)/shard_map/ppermute | solution.py:255
  53.2 0.7 %collective-permute-done.8.refs_4_ = bf16[128,256]{1,0:T(8,128)(2,1)S(1)} collective-permute-done((bf16[128,256]{1,0:T(8,128)(2,1)S(1)}, bf16[128,256]{1,0:T(8,128)(2,1)S(1)}, u32[]{:S(2)}, u32[]{:S(2)}) %collective-permute-start.8) | collective-permute-done | bytes 65568 | tf_op jit(solution)/shard_map/ppermute | solution.py:255
  53.8 1.0 %phase.2.refs_3_ = bf16[128,1024]{1,0:T(8,128)(2,1)S(1)} custom-call(s32[4]{0:T(128)S(1)} %pad_add_fusion.refs_0_.place, bf16[1024,1024]{1,0:T(8,128)(2,1)S(1)} %copy-done, bf16[128,256]{1,0:T(8,128)(2,1)S(1)} %get-tuple-element.27.refs_2_, bf16[128,256]{1,0:T(8,128)(2,1)S(1)} %collective-permute-done.7.refs_3_, ...), custom_call_target="tpu_custom_call" | custom-call | flops 1 | bytes 16384 | tf_op jit(solution)/shard_map/phase/pallas_call | solution.py:390
  54.8 0.1 collective-permute-start.10
  55.0 1.0 %recon.3.refs_4_ = f32[128,512]{1,0:T(8,128)S(1)} custom-call(s32[4]{0:T(128)S(1)} %pad_add_fusion.refs_0_.place, s32[1,4]{1,0:T(1,128)S(1)} %copy-done.3, bf16[4,1024,512]{2,1,0:T(8,128)(2,1)S(1)} %copy-done.1, bf16[128,1024]{1,0:T(8,128)(2,1)S(1)} %phase.3.refs_3_, bf16[128,1024]{1,0:T(8,128)(2,1)S(1)} %collective-permute-done.20.refs_4_), custom_call_target="tpu_custom_call" | custom-call | flops 1 | bytes 8192 | tf_op jit(solution)/shard_map/recon/pallas_call | solution.py:367
  56.0 0.0 copy-start.4
  56.0 0.9 %recon.4.refs_5_ = f32[128,512]{1,0:T(8,128)S(1)} custom-call(s32[4]{0:T(128)S(1)} %pad_add_fusion.refs_0_.place, s32[1,4]{1,0:T(1,128)S(1)} %copy-done.3, bf16[4,1024,512]{2,1,0:T(8,128)(2,1)S(1)} %copy-done.1, bf16[128,1024]{1,0:T(8,128)(2,1)S(1)} %phase.2.refs_3_, f32[128,512]{1,0:T(8,128)S(1)} %recon.3.refs_4_), custom_call_target="tpu_custom_call" | custom-call | flops 1 | bytes 8192 | tf_op jit(solution)/shard_map/recon/pallas_call | solution.py:367
  56.8 0.0 collective-permute-done.10.refs_4_
  56.9 1.6 %recon.5 = bf16[128,512]{1,0:T(8,128)(2,1)} custom-call(s32[4]{0:T(128)S(1)} %pad_add_fusion.refs_0_.place, s32[1,4]{1,0:T(1,128)S(1)} %copy-done.3, s32[16]{0:T(128)S(1)} %copy-done.4, bf16[4,1024,512]{2,1,0:T(8,128)(2,1)S(1)} %copy-done.1, bf16[128,1024]{1,0:T(8,128)(2,1)S(1)} %collective-permute-done.10.refs_4_, f32[128,512]{1,0:T(8,128)S(1)} %recon.4.refs_5_), custom_call_target="tpu_custom_call" | custom-call | flops 1 | bytes 8192 | tf_op jit(solution)/shard_map/recon/pallas_call | solution.py:367
  (12 shorter events, 0.0 us)
Async XLA Ops:
  0.0 3.7 %copy-start = (bf16[1024,1024]{1,0:T(8,128)(2,1)S(1)}, bf16[1024,1024]{1,0:T(8,128)(2,1)}, u32[]{:S(2)}) copy-start(bf16[1024,1024]{1,0:T(8,128)(2,1)} %constant.59.clone.refs_3_.refs_1_) | copy-start | bytes 6291460
  0.0 3.7 %collective-permute-start = (bf16[4,2,64,1024]{3,2,1,0:T(8,128)(2,1)}, bf16[4,2,64,1024]{3,2,1,0:T(8,128)(2,1)S(1)}, u32[]{:S(2)}, u32[]{:S(2)}) collective-permute-start(bf16[4,2,64,1024]{3,2,1,0:T(8,128)(2,1)} %bitcast.5), channel_id=1, source_target_pairs={{0,16},{1,17},{2,18},{3,19},{4,20},{5,21},{6,22},{7,23},{8,24},{9,... | collective-permute-start | bytes 3145736 | tf_op jit(solution)/shard_map/ppermute | solution.py:255
  3.7 1.2 %copy-start.2 = (bf16[1,4,2,64,1024]{4,3,2,1,0:T(8,128)(2,1)S(1)}, bf16[1,4,2,64,1024]{4,3,2,1,0:T(8,128)(2,1)}, u32[]{:S(2)}) copy-start(bf16[1,4,2,64,1024]{4,3,2,1,0:T(8,128)(2,1)} %param.6) | copy-start | bytes 3145732
  6.2 8.9 %collective-permute-start.11 = (bf16[4,64,256]{2,1,0:T(8,128)(2,1)S(1)}, bf16[4,64,256]{2,1,0:T(8,128)(2,1)S(1)}, u32[]{:S(2)}, u32[]{:S(2)}) collective-permute-start(bf16[4,64,256]{2,1,0:T(8,128)(2,1)S(1)} %get-tuple-element.30), channel_id=1, source_target_pairs={{0,1},{1,0},{2,3},{3,2},{4,5},{5,4},{6,7},{7,6},{8,9},{9,8},{10,11... | collective-permute-start | bytes 393224 | tf_op jit(solution)/shard_map/ppermute | solution.py:255
  8.7 8.1 %collective-permute-start.12 = (bf16[4,64,256]{2,1,0:T(8,128)(2,1)S(1)}, bf16[4,64,256]{2,1,0:T(8,128)(2,1)S(1)}, u32[]{:S(2)}, u32[]{:S(2)}) collective-permute-start(bf16[4,64,256]{2,1,0:T(8,128)(2,1)S(1)} %get-tuple-element.31), channel_id=1, source_target_pairs={{0,2},{1,3},{2,0},{3,1},{4,6},{5,7},{6,4},{7,5},{8,10},{9,11},{10,... | collective-permute-start | bytes 393224 | tf_op jit(solution)/shard_map/ppermute | solution.py:255
  10.3 7.3 %collective-permute-start.13 = (bf16[4,64,256]{2,1,0:T(8,128)(2,1)S(1)}, bf16[4,64,256]{2,1,0:T(8,128)(2,1)S(1)}, u32[]{:S(2)}, u32[]{:S(2)}) collective-permute-start(bf16[4,64,256]{2,1,0:T(8,128)(2,1)S(1)} %get-tuple-element.32), channel_id=1, source_target_pairs={{0,3},{1,2},{2,1},{3,0},{4,7},{5,6},{6,5},{7,4},{8,11},{9,10},{10,... | collective-permute-start | bytes 393224 | tf_op jit(solution)/shard_map/ppermute | solution.py:255
  11.6 9.5 %collective-permute-start.1 = (bf16[4,64,256]{2,1,0:T(8,128)(2,1)S(1)}, bf16[4,64,256]{2,1,0:T(8,128)(2,1)S(1)}, u32[]{:S(2)}, u32[]{:S(2)}) collective-permute-start(bf16[4,64,256]{2,1,0:T(8,128)(2,1)S(1)} %get-tuple-element.22), channel_id=1, source_target_pairs={{0,1},{1,0},{2,3},{3,2},{4,5},{5,4},{6,7},{7,6},{8,9},{9,8},{10,11... | collective-permute-start | bytes 393224 | tf_op jit(solution)/shard_map/ppermute | solution.py:255
  13.6 9.1 %collective-permute-start.2 = (bf16[4,64,256]{2,1,0:T(8,128)(2,1)S(1)}, bf16[4,64,256]{2,1,0:T(8,128)(2,1)S(1)}, u32[]{:S(2)}, u32[]{:S(2)}) collective-permute-start(bf16[4,64,256]{2,1,0:T(8,128)(2,1)S(1)} %get-tuple-element.23), channel_id=1, source_target_pairs={{0,2},{1,3},{2,0},{3,1},{4,6},{5,7},{6,4},{7,5},{8,10},{9,11},{10,... | collective-permute-start | bytes 393224 | tf_op jit(solution)/shard_map/ppermute | solution.py:255
  15.1 7.6 %collective-permute-start.3 = (bf16[4,64,256]{2,1,0:T(8,128)(2,1)S(1)}, bf16[4,64,256]{2,1,0:T(8,128)(2,1)S(1)}, u32[]{:S(2)}, u32[]{:S(2)}) collective-permute-start(bf16[4,64,256]{2,1,0:T(8,128)(2,1)S(1)} %get-tuple-element.24), channel_id=1, source_target_pairs={{0,3},{1,2},{2,1},{3,0},{4,7},{5,6},{6,5},{7,4},{8,11},{9,10},{10,... | collective-permute-start | bytes 393224 | tf_op jit(solution)/shard_map/ppermute | solution.py:255
  19.4 7.0 %collective-permute-start.14 = (bf16[2,256,256]{2,1,0:T(8,128)(2,1)S(1)}, bf16[2,256,256]{2,1,0:T(8,128)(2,1)S(1)}, u32[]{:S(2)}, u32[]{:S(2)}) collective-permute-start(bf16[2,256,256]{2,1,0:T(8,128)(2,1)S(1)} %get-tuple-element.34.one), channel_id=1, source_target_pairs={{0,4},{1,5},{2,6},{3,7},{4,0},{5,1},{6,2},{7,3},{8,12},{9,13},{10,... | collective-permute-start | bytes 786440 | tf_op jit(solution)/shard_map/ppermute | solution.py:255
  24.6 7.5 %collective-permute-start.4 = (bf16[2,256,256]{2,1,0:T(8,128)(2,1)S(1)}, bf16[2,256,256]{2,1,0:T(8,128)(2,1)S(1)}, u32[]{:S(2)}, u32[]{:S(2)}) collective-permute-start(bf16[2,256,256]{2,1,0:T(8,128)(2,1)S(1)} %get-tuple-element.26.one), channel_id=1, source_target_pairs={{0,4},{1,5},{2,6},{3,7},{4,0},{5,1},{6,2},{7,3},{8,12},{9,13},{10,... | collective-permute-start | bytes 786440 | tf_op jit(solution)/shard_map/ppermute | solution.py:255
  26.5 5.7 %collective-permute-start.15 = (bf16[2,256,256]{2,1,0:T(8,128)(2,1)S(1)}, bf16[2,256,256]{2,1,0:T(8,128)(2,1)S(1)}, u32[]{:S(2)}, u32[]{:S(2)}) collective-permute-start(bf16[2,256,256]{2,1,0:T(8,128)(2,1)S(1)} %joint.3), channel_id=1, source_target_pairs={{0,16},{1,17},{2,18},{3,19},{4,8},{5,9},{6,10},{7,11},{8,4},{9,5},... | collective-permute-start | bytes 786440 | tf_op jit(solution)/shard_map/ppermute | solution.py:255
  32.2 3.9 %collective-permute-start.5 = (bf16[2,256,256]{2,1,0:T(8,128)(2,1)S(1)}, bf16[2,256,256]{2,1,0:T(8,128)(2,1)S(1)}, u32[]{:S(2)}, u32[]{:S(2)}) collective-permute-start(bf16[2,256,256]{2,1,0:T(8,128)(2,1)S(1)} %joint.2), channel_id=1, source_target_pairs={{0,16},{1,17},{2,18},{3,19},{4,8},{5,9},{6,10},{7,11},{8,4},{9,5},... | collective-permute-start | bytes 786440 | tf_op jit(solution)/shard_map/ppermute | solution.py:255
  32.9 8.4 %collective-permute-start.16 = (bf16[256,256]{1,0:T(8,128)(2,1)S(1)}, bf16[256,256]{1,0:T(8,128)(2,1)S(1)}, u32[]{:S(2)}, u32[]{:S(2)}) collective-permute-start(bf16[256,256]{1,0:T(8,128)(2,1)S(1)} %near.3), channel_id=1, source_target_pairs={{0,4},{1,5},{2,6},{3,7},{4,0},{5,1},{6,2},{7,3},{8,12},{9,13},{10,... | collective-permute-start | bytes 393224 | tf_op jit(solution)/shard_map/ppermute | solution.py:255
  36.7 8.8 %collective-permute-start.6 = (bf16[256,256]{1,0:T(8,128)(2,1)S(1)}, bf16[256,256]{1,0:T(8,128)(2,1)S(1)}, u32[]{:S(2)}, u32[]{:S(2)}) collective-permute-start(bf16[256,256]{1,0:T(8,128)(2,1)S(1)} %near.2.after), channel_id=1, source_target_pairs={{0,4},{1,5},{2,6},{3,7},{4,0},{5,1},{6,2},{7,3},{8,12},{9,13},{10,... | collective-permute-start | bytes 393224 | tf_op jit(solution)/shard_map/ppermute | solution.py:255
  41.9 7.3 %collective-permute-start.17 = (bf16[128,256]{1,0:T(8,128)(2,1)S(1)}, bf16[128,256]{1,0:T(8,128)(2,1)S(1)}, u32[]{:S(2)}, u32[]{:S(2)}) collective-permute-start(bf16[128,256]{1,0:T(8,128)(2,1)S(1)} %get-tuple-element.35.refs_2_), channel_id=1, source_target_pairs={{0,1},{1,0},{2,3},{3,2},{4,5},{5,4},{6,7},{7,6},{8,9},{9,8},{10,11... | collective-permute-start | bytes 196616 | tf_op jit(solution)/shard_map/ppermute | solution.py:255
  43.8 5.8 %collective-permute-start.19 = (bf16[128,256]{1,0:T(8,128)(2,1)S(1)}, bf16[128,256]{1,0:T(8,128)(2,1)S(1)}, u32[]{:S(2)}, u32[]{:S(2)}) collective-permute-start(bf16[128,256]{1,0:T(8,128)(2,1)S(1)} %get-tuple-element.36), channel_id=1, source_target_pairs={{0,3},{1,2},{2,1},{3,0},{4,7},{5,6},{6,5},{7,4},{8,11},{9,10},{10,... | collective-permute-start | bytes 196616 | tf_op jit(solution)/shard_map/ppermute | solution.py:255
  45.0 5.8 %collective-permute-start.18 = (bf16[128,256]{1,0:T(8,128)(2,1)S(1)}, bf16[128,256]{1,0:T(8,128)(2,1)S(1)}, u32[]{:S(2)}, u32[]{:S(2)}) collective-permute-start(bf16[128,256]{1,0:T(8,128)(2,1)S(1)} %get-tuple-element.36), channel_id=1, source_target_pairs={{0,2},{1,3},{2,0},{3,1},{4,6},{5,7},{6,4},{7,5},{8,10},{9,11},{10,... | collective-permute-start | bytes 196616 | tf_op jit(solution)/shard_map/ppermute | solution.py:255
  46.0 5.8 %collective-permute-start.7 = (bf16[128,256]{1,0:T(8,128)(2,1)S(1)}, bf16[128,256]{1,0:T(8,128)(2,1)S(1)}, u32[]{:S(2)}, u32[]{:S(2)}) collective-permute-start(bf16[128,256]{1,0:T(8,128)(2,1)S(1)} %get-tuple-element.27.refs_2_), channel_id=1, source_target_pairs={{0,1},{1,0},{2,3},{3,2},{4,5},{5,4},{6,7},{7,6},{8,9},{9,8},{10,11... | collective-permute-start | bytes 196616 | tf_op jit(solution)/shard_map/ppermute | solution.py:255
  48.0 7.0 %copy-start.1 = (bf16[4,1024,512]{2,1,0:T(8,128)(2,1)S(1)}, bf16[4,1024,512]{2,1,0:T(8,128)(2,1)}, u32[]{:S(2)}) copy-start(bf16[4,1024,512]{2,1,0:T(8,128)(2,1)} %refs_3_.3) | copy-start | bytes 12582916
  48.0 7.0 %copy-start.3 = (s32[1,4]{1,0:T(1,128)S(1)}, s32[1,4]{1,0:T(1,128)}, u32[]{:S(2)}) copy-start(s32[1,4]{1,0:T(1,128)} %refs_1_.9) | copy-start | bytes 52
  48.0 5.2 %collective-permute-start.9 = (bf16[128,256]{1,0:T(8,128)(2,1)S(1)}, bf16[128,256]{1,0:T(8,128)(2,1)S(1)}, u32[]{:S(2)}, u32[]{:S(2)}) collective-permute-start(bf16[128,256]{1,0:T(8,128)(2,1)S(1)} %get-tuple-element.28), channel_id=1, source_target_pairs={{0,3},{1,2},{2,1},{3,0},{4,7},{5,6},{6,5},{7,4},{8,11},{9,10},{10,... | collective-permute-start | bytes 196616 | tf_op jit(solution)/shard_map/ppermute | solution.py:255
  49.2 4.7 %collective-permute-start.8 = (bf16[128,256]{1,0:T(8,128)(2,1)S(1)}, bf16[128,256]{1,0:T(8,128)(2,1)S(1)}, u32[]{:S(2)}, u32[]{:S(2)}) collective-permute-start(bf16[128,256]{1,0:T(8,128)(2,1)S(1)} %get-tuple-element.28), channel_id=1, source_target_pairs={{0,2},{1,3},{2,0},{3,1},{4,6},{5,7},{6,4},{7,5},{8,10},{9,11},{10,... | collective-permute-start | bytes 196616 | tf_op jit(solution)/shard_map/ppermute | solution.py:255
  51.8 3.1 %collective-permute-start.20 = (bf16[128,1024]{1,0:T(8,128)(2,1)S(1)}, bf16[128,1024]{1,0:T(8,128)(2,1)S(1)}, u32[]{:S(2)}, u32[]{:S(2)}) collective-permute-start(bf16[128,1024]{1,0:T(8,128)(2,1)S(1)} %phase.3.refs_3_), channel_id=1, source_target_pairs={{0,16},{1,17},{2,18},{3,19},{4,20},{5,21},{6,22},{7,23},{8,24},{9,... | collective-permute-start | bytes 786440 | tf_op jit(solution)/shard_map/ppermute | solution.py:255
  54.8 2.0 %collective-permute-start.10 = (bf16[128,1024]{1,0:T(8,128)(2,1)S(1)}, bf16[128,1024]{1,0:T(8,128)(2,1)S(1)}, u32[]{:S(2)}, u32[]{:S(2)}) collective-permute-start(bf16[128,1024]{1,0:T(8,128)(2,1)S(1)} %phase.2.refs_3_), channel_id=1, source_target_pairs={{0,16},{1,17},{2,18},{3,19},{4,20},{5,21},{6,22},{7,23},{8,24},{9,... | collective-permute-start | bytes 786440 | tf_op jit(solution)/shard_map/ppermute | solution.py:255
  56.0 0.9 %copy-start.4 = (s32[16]{0:T(128)S(1)}, s32[16]{0:T(128)}, u32[]{:S(2)}) copy-start(s32[16]{0:T(128)} %refs_2_.5) | copy-start | bytes 196

commit v8 on v7

--- a/solution.py
+++ b/solution.py
@@ -12,6 +12,8 @@
 regularizer = 0.05
 bf16 = jnp.bfloat16
 f32 = jnp.float32
+send_order = (0, 2, 3, 1)
+tail_order = (0, 1, 3, 2)
 
 
 def hartley(length):
@@ -91,12 +93,18 @@
     return jnp.dot(select, paired, preferred_element_type=f32).astype(bf16)
 
 
-def row_kernel(inner, place, here, there, table, after, *outs):
-    spot = place[1]
-    dist_dev, rows_dev, width = here.shape[1:]
+def position(inner):
+    device = lax.axis_index("rows")
+    return lax.axis_index("dist"), device // inner, device % inner
+
+
+def row_kernel(inner, chunk, here, there, table, after, *outs):
+    core, _, spot = position(inner)
+    own, dist_dev, rows_dev, width = here.shape
     block = width // inner
+    partner = there[core * own + chunk]
     flat = jnp.concatenate(
-        [source[0].reshape(dist_dev * rows_dev, width) for source in (here, there)], axis=0
+        [source.reshape(dist_dev * rows_dev, width) for source in (here[chunk], partner)], axis=0
     )
     for rel in range(inner):
         part = table[:, pl.ds(pl.multiple_of((spot ^ rel) * block, block), block)]
@@ -104,8 +112,12 @@
         outs[rel][...] = got.reshape(2 * dist_dev, rows_dev, block)
 
 
-def filter_kernel(waves_a, with_sin, with_cos, out):
+def filter_kernel(waves_a, with_sin, with_cos, holo, out, mine, arrived):
     dists, width, block = out.shape
+    own = mine.shape[0]
+    core = lax.axis_index("dist")
+    copy = pltpu.make_async_copy(holo.at[pl.ds(core * own, own)], mine, arrived)
+    copy.start()
     turned = waves_a[...].T
     step = 128
     for at in range(0, width, step):
@@ -121,12 +133,13 @@
         scale = 1.0 / (denom + regularizer)
         for d in range(dists):
             out[d, at : at + step, :] = (transfer[d] * scale).astype(bf16)
-
-
-def column_kernel(inner, outer, place, table, gain, *refs):
-    pieces = refs[:inner]
+    copy.wait()
+
+
+def column_kernel(inner, outer, table, gain, *refs):
+    pieces = dict(zip(send_order, refs[:inner]))
     away, keep, stack, total, spectrum = refs[inner:]
-    spot, plane = place[1], place[2]
+    _, plane, spot = position(inner)
     dists, rows_dev, block = pieces[0].shape
     depth = inner * rows_dev
     for rel in range(inner):
@@ -153,16 +166,17 @@
     out[...] = (one[...].astype(f32) + two[...].astype(f32)).astype(bf16)
 
 
-def near_kernel(place, keep, across, out):
-    plane = place[2]
+def near_kernel(inner, keep, across, out):
+    _, plane, _ = position(inner)
     which = (plane ^ 1) % 2
     inside = (plane == 1) | (plane == 2)
     more = jnp.where(inside, across[which].astype(f32), 0.0)
     out[...] = (keep[which].astype(f32) + more).astype(bf16)
 
 
-def half_kernel(place, keep, across, last, after, mine, other):
-    spot, plane = place[1], place[2]
+def half_kernel(inner, keep, across, last, *refs):
+    mine, other = refs[-2:]
+    _, plane, spot = position(inner)
     which = plane % 2
     inside = (plane == 1) | (plane == 2)
     capacity = mine.shape[0]
@@ -173,37 +187,37 @@
         out[...] = got.astype(bf16)
 
 
-def phase_kernel(inner, place, table, *refs):
-    pieces = refs[:inner]
+def phase_kernel(inner, table, *refs):
+    pieces = dict(zip(tail_order, refs[:inner]))
     out, joined = refs[-2:]
-    spot = place[1]
-    block = pieces[0].shape[1]
+    _, _, spot = position(inner)
+    block = refs[0].shape[1]
     for rel in range(inner):
         columns = pl.ds(pl.multiple_of((spot ^ rel) * block, block), block)
         joined[:, columns] = pieces[rel][...]
     out[...] = jnp.dot(joined[...], table[...], preferred_element_type=f32).astype(bf16)
 
 
-def recon_kernel(own, chunk, cores, place, order, weights, *refs):
+def recon_kernel(own, chunk, cores, info, weights, *refs):
+    core = lax.axis_index("dist")
     phases, out = refs[: len(cores)], refs[-1]
     total = refs[-2][...] if len(refs) > len(cores) + 1 else None
     for other, phase in zip(cores, phases):
-        chosen = weights[order[0, (place[0] ^ other) * own + chunk]]
+        chosen = weights[info[(core ^ other) * own + chunk]]
         got = jnp.dot(phase[...], chosen, preferred_element_type=f32)
         total = got if total is None else total + got
     out[...] = total
 
 
-def recon_last_kernel(own, chunk, other, place, order, slabs, weights, phase, before, out):
-    chosen = weights[order[0, (place[0] ^ other) * own + chunk]]
+def recon_last_kernel(own, chunk, other, info, weights, phase, before, out):
+    core = lax.axis_index("dist")
+    chosen = weights[info[(core ^ other) * own + chunk]]
     total = before[...] + jnp.dot(phase[...], chosen, preferred_element_type=f32)
     capacity = total.shape[0]
-    device = place[3]
-    parity = device % 2
-    offset = parity * slabs[device - parity]
+    offset, count = info[weights.shape[0]], info[weights.shape[0] + 1]
     turned = pltpu.roll(total, lax.rem(capacity - offset, capacity), 0)
     slot = lax.broadcasted_iota(jnp.int32, turned.shape, 0)
-    out[...] = jnp.where(slot < slabs[device], turned, 0.0).astype(bf16)
+    out[...] = jnp.where(slot < count, turned, 0.0).astype(bf16)
 
 
 def vmem(count):
@@ -243,7 +257,14 @@
     device = lax.axis_index("rows")
     core = lax.axis_index("dist")
     plane, spot = device // inner, device % inner
-    place = jnp.stack([core, spot, plane, device]).astype(jnp.int32)
+    parity = device % 2
+    info = jnp.concatenate(
+        [
+            angle_order[0],
+            (parity * slab_rows[device - parity])[None],
+            slab_rows[device][None],
+        ]
+    )
     table = jnp.asarray(hartley(width))
 
     def sent(value, target):
@@ -260,9 +281,8 @@
     def to_spot(rel):
         return lambda c, r: (c, r ^ rel)
 
-    def spread(pieces):
-        got = {rel: sent(pieces[rel], to_spot(rel)) for rel in (2, 3, 1)}
-        return [pieces[0]] + [got[rel] for rel in range(1, inner)]
+    def spread(pieces, order):
+        return [sent(pieces[rel], to_spot(rel)) if rel else pieces[rel] for rel in order]
 
     def to_near_plane(c, r):
         return c, (r // inner ^ 1) * inner + r % inner
@@ -282,11 +302,12 @@
     first = ordered[:, None] * signed_square(index, width)[None]
     second = ordered[:, None] * signed_square(my_cols, width)[None]
     sin_b, cos_b = jnp.sin(second), jnp.cos(second)
-    gain = pl.pallas_call(
+    gain, mine = pl.pallas_call(
         filter_kernel,
-        out_shape=shaped(dists, width, block),
-        in_specs=vmem(3),
-        out_specs=one_out,
+        out_shape=[shaped(dists, width, block), shaped(own, dist_dev, rows_dev, width)],
+        in_specs=vmem(3) + unread(1),
+        out_specs=vmem(2),
+        scratch_shapes=[pltpu.SemaphoreType.DMA],
         compiler_params=params,
         cost_estimate=cost(32 * width * block, (dists, width, block)),
         name="filters",
@@ -294,42 +315,31 @@
         jnp.concatenate([jnp.sin(first), jnp.cos(first)], axis=0),
         2.0 * (cos_b - absorb_ratio * sin_b),
         2.0 * (sin_b + absorb_ratio * cos_b),
+        holograms[0],
     )
 
     partner = sent(holograms[0], to_other_core)
     arrived = []
     for chunk in range(own):
         pieces = pl.pallas_call(
-            lambda *refs: row_kernel(inner, *refs),
+            lambda *refs, chunk=chunk: row_kernel(inner, chunk, *refs),
             out_shape=[shaped(dists, rows_dev, block)] * inner,
-            grid_spec=pltpu.PrefetchScalarGridSpec(
-                num_scalar_prefetch=1,
-                grid=(1,),
-                in_specs=[
-                    pl.BlockSpec(
-                        (1, dist_dev, rows_dev, width),
-                        lambda i, place, chunk=chunk: (place[0] * own + chunk, 0, 0, 0),
-                    )
-                ]
-                * 2
-                + vmem(1)
-                + unread(1),
-                out_specs=vmem(inner),
-            ),
+            in_specs=vmem(3) + unread(1),
+            out_specs=vmem(inner),
             compiler_params=params,
             cost_estimate=cost(
                 2 * dists * rows_dev * width * width, (width, width), (2, dists, rows_dev, width)
             ),
             name="row_spectra",
-        )(place, holograms[0], partner, table, gain)
-        arrived.append(spread(pieces))
+        )(mine, partner, table, gain)
+        arrived.append(spread(pieces, send_order))
 
     sums = []
     for chunk in range(own):
         away, keep = pl.pallas_call(
             lambda *refs: column_kernel(inner, outer, *refs),
             out_shape=[shaped(outer // 2, depth, block)] * 2,
-            in_specs=smem(1) + vmem(2 + inner),
+            in_specs=vmem(2 + inner),
             out_specs=vmem(2),
             scratch_shapes=[
                 pltpu.VMEM((dists, depth, block), bf16),
@@ -341,7 +351,7 @@
                 2 * width * block * (dists * depth + width), (width, width), (dists, width, block)
             ),
             name="columns",
-        )(place, table, gain, *arrived[chunk])
+        )(table, gain, *arrived[chunk])
         joint = pl.pallas_call(
             add_kernel,
             out_shape=shaped(outer // 2, depth, block),
@@ -353,63 +363,61 @@
         )(away, sent(away, to_near_plane))
         across = sent(joint, to_middle)
         near = pl.pallas_call(
-            near_kernel,
+            lambda *refs: near_kernel(inner, *refs),
             out_shape=shaped(depth, block),
-            in_specs=smem(1) + vmem(2),
+            in_specs=vmem(2),
             out_specs=one_out,
             compiler_params=params,
             cost_estimate=cost(depth * block, (3, depth, block)),
             name="near",
-        )(place, keep, across)
+        )(keep, across)
         sums.append((keep, across, sent(near, to_near_plane)))
 
-    def recon(kernel, out_type, scalars, *arrays):
+    def recon(kernel, out_type, *arrays):
         return pl.pallas_call(
             kernel,
             out_shape=jax.ShapeDtypeStruct((capacity, pixels), out_type),
-            in_specs=smem(len(scalars)) + vmem(1 + len(arrays)),
+            in_specs=smem(1) + vmem(1 + len(arrays)),
             out_specs=one_out,
             compiler_params=params,
             cost_estimate=cost(1, (8, pixels)),
             name="recon",
-        )(*scalars, weights, *arrays)
+        )(info, weights, *arrays)
 
     total = None
-    scalars = (place, angle_order)
     for chunk in range(own):
-        mine, other = pl.pallas_call(
-            half_kernel,
+        first, second = pl.pallas_call(
+            lambda *refs: half_kernel(inner, *refs),
             out_shape=[shaped(capacity, block)] * 2,
-            in_specs=smem(1) + vmem(3) + unread(1),
+            in_specs=vmem(3) + unread(2),
             out_specs=vmem(2),
             compiler_params=params,
             cost_estimate=cost(1, (8, width)),
             name="half",
-        )(place, *sums[chunk], near)
-        pieces = spread([mine, mine, other, other])
+        )(*sums[chunk], near, info)
+        pieces = spread([first, first, second, second], tail_order)
         phase = pl.pallas_call(
             lambda *refs: phase_kernel(inner, *refs),
             out_shape=shaped(capacity, width),
-            in_specs=smem(1) + vmem(1 + inner),
+            in_specs=vmem(1 + inner),
             out_specs=one_out,
             scratch_shapes=[pltpu.VMEM((capacity, width), bf16)],
             compiler_params=params,
             cost_estimate=cost(1, (8, width)),
             name="phase",
-        )(place, table, *pieces)
+        )(table, *pieces)
         there = sent(phase, to_other_core)
         def part(cores, chunk=chunk):
             return lambda *refs: recon_kernel(own, chunk, cores, *refs)
 
         before = [] if total is None else [total]
         if chunk < own - 1:
-            total = recon(part((0, 1)), f32, scalars, phase, there, *before)
+            total = recon(part((0, 1)), f32, phase, there, *before)
         else:
-            total = recon(part((0,)), f32, scalars, phase, *before)
+            total = recon(part((0,)), f32, phase, *before)
             total = recon(
                 lambda *refs, chunk=chunk: recon_last_kernel(own, chunk, 1, *refs),
                 bf16,
-                scalars + (slab_rows,),
                 there,
                 total,
             )

time: 58.7 us -> 59.3 us (1.010)
  Pallas kernels: 16.1 us -> 11.6 us
  local copies, waits for them, and re-layouts: 2.16 us -> 4.28 us
  waiting for transfers between devices: 12.1 us -> 13.3 us
  between operations: 0.24 us -> 0.9 us
  other arithmetic: 0.51 us -> 1.17 us
    pallas_call x7, Pallas kernels: 6.76 us -> 4.46 us  [the longest x1 1.83 us: plane_plan(): pl.pallas_call(filter_kernel, out_shape=[shaped(dists, width, block), sha...]
    unnamed x10 -> x12, local copies, waits for them, and re-layouts: 1.24 us -> 2.83 us
    ppermute x21, waiting for transfers between devices: 12.1 us -> 13.3 us  [sent(): return lax.ppermute(value, ('dist', 'rows'), pairs)]
    pallas_call x2, Pallas kernels: 3.71 us -> 2.6 us  [plane_plan(): pl.pallas_call(lambda *refs: column_kernel(inner, outer, *refs), out_shap...]
    pallas_call x2, Pallas kernels: 2 us -> 0.92 us  [plane_plan(): pl.pallas_call(lambda *refs: phase_kernel(inner, *refs), out_shape=shaped...]
    concatenate x0 -> x1, other arithmetic: none -> 0.75 us  [plane_plan(): jnp.concatenate([angle_order[0], (parity * slab_rows[device - parity])[No...]
    dynamic_slice x0 -> x1, local copies, waits for them, and re-layouts: none -> 0.65 us  [plane_plan(): slab_rows[device - parity]]
  transfers between devices with their start and end apart: 21 -> 21, of which waited for: 8 -> 9; matrix products, arithmetic and copies ran while one was open for 2% -> 4% of each run, Pallas kernels for 22% -> 16%
where the time goes in v8:
time: 59.3 us; the launch traced here: 59 us
  starting transfers between devices  27.7 us (47%)
  waiting for transfers between devices  13.3 us (22%)
  Pallas kernels  11.6 us (20%)
  local copies, waits for them, and re-layouts  4.28 us (7%)
  other arithmetic  1.17 us (2%)
  between operations  0.9 us (2%)
    ppermute x21, starting transfers between devices, sent(): return lax.ppermute(value, ('dist', 'rows'), pairs)  27.7 us
    ppermute x21, waiting for transfers between devices, sent(): return lax.ppermute(value, ('dist', 'rows'), pairs)  13.3 us
    pallas_call x3, Pallas kernels, recon(): pl.pallas_call(kernel, out_shape=jax.ShapeDtypeStruct((capacity, pixels),...  3.48 us
    unnamed x12, local copies, waits for them, and re-layouts  2.83 us
    pallas_call x2, Pallas kernels, plane_plan(): pl.pallas_call(lambda *refs: column_kernel(inner, outer, *refs), out_shap...  2.6 us
    pallas_call x1, Pallas kernels, plane_plan(): pl.pallas_call(filter_kernel, out_shape=[shaped(dists, width, block), sha...  1.83 us
    pallas_call x2, Pallas kernels, plane_plan(): pl.pallas_call(lambda *refs, chunk=chunk: row_kernel(inner, chunk, *refs)...  1.49 us
  transfers between devices with their start and end apart: 21, of which 9 were waited for; matrix products, arithmetic and copies ran while one was open for 4% of the time, Pallas kernels for 16%

profile of v8, /device:TPU:0, one launch (start us, length us, event | category | flops | bytes accessed | tf_op | source)
XLA Modules:
  0.0 59.0 jit_solution(6415260427367763967)
XLA Ops:
  0.0 0.5 collective-permute-start
  0.5 0.8 %fusion.12 = (f32[2]{0:T(128)S(1)}, f32[2]{0:T(128)S(1)}) fusion(f32[4]{0:T(128)} %param.7, s32[]{:T(128)S(6)} %select_n.42, s32[]{:T(128)S(6)} %select_n.43), kind=kLoop, calls=%fused_computation.21 | loop fusion | bytes 40 | tf_op jit(solution)/shard_map/dynamic_slice | solution.py:298
  1.3 0.1 pad_maximum_fusion.1
  1.4 0.2 multiply_sine_fusion
  1.6 0.1 fusion.5
  1.7 0.0 copy-start.3
  1.7 1.2 %copy-done.3 = bf16[1,4,2,64,1024]{4,3,2,1,0:T(8,128)(2,1)S(1)} copy-done((bf16[1,4,2,64,1024]{4,3,2,1,0:T(8,128)(2,1)S(1)}, bf16[1,4,2,64,1024]{4,3,2,1,0:T(8,128)(2,1)}, u32[]{:S(2)}) %copy-start.3) | copy-done | bytes 1048600
  2.9 1.8 %filters.1 = (bf16[4,1024,256]{2,1,0:T(8,128)(2,1)S(1)}, bf16[2,2,64,1024]{3,2,1,0:T(8,128)(2,1)S(1)}) custom-call(f32[8,1024]{1,0:T(8,128)S(1)} %pad_maximum_fusion.waves_a, f32[4,256]{1,0:T(4,128)S(1)} %get-tuple-element.44.with_sin, f32[4,256]{1,0:T(4,128)S(1)} %get-tuple-element.43.with_cos, bf16[4,2,64,1024]{3,2,1,0:T(8,128)(2,1)S(1)} %bitcast.5), custom_call_target="tpu_custom_call" | custom-call | flops 8388608 | bytes 2097152 | tf_op jit(solution)/shard_map/filters/pallas_call | solution.py:305
  4.8 0.0 collective-permute-done.refs_1_
  4.8 0.0 copy-start
  4.8 1.6 %copy-done = bf16[1024,1024]{1,0:T(8,128)(2,1)S(1)} copy-done((bf16[1024,1024]{1,0:T(8,128)(2,1)S(1)}, bf16[1024,1024]{1,0:T(8,128)(2,1)}, u32[]{:S(2)}) %copy-start) | copy-done | bytes 2097176
  6.4 0.7 %row_spectra.3 = (bf16[4,64,256]{2,1,0:T(8,128)(2,1)S(1)}, bf16[4,64,256]{2,1,0:T(8,128)(2,1)S(1)}, bf16[4,64,256]{2,1,0:T(8,128)(2,1)S(1)}, bf16[4,64,256]{2,1,0:T(8,128)(2,1)S(1)}) custom-call(bf16[2,2,64,1024]{3,2,1,0:T(8,128)(2,1)S(1)} %get-tuple-element.24.refs_0_, bf16[4,2,64,1024]{3,2,1,0:T(8,128)(2,1)S(1)} %collective-permute-done.refs_1_, ...), custom_call_target="tpu_custom_call" | custom-call | flops 536870912 | bytes 3145728 | tf_op jit(solution)/shard_map/row_spectra/pallas_call | solution.py:324
  7.1 2.6 %collective-permute-start.11 = (bf16[4,64,256]{2,1,0:T(8,128)(2,1)S(1)}, bf16[4,64,256]{2,1,0:T(8,128)(2,1)S(1)}, u32[]{:S(2)}, u32[]{:S(2)}) collective-permute-start(bf16[4,64,256]{2,1,0:T(8,128)(2,1)S(1)} %get-tuple-element.34), channel_id=1, source_target_pairs={{0,2},{1,3},{2,0},{3,1},{4,6},{5,7},{6,4},{7,5},{8,10},{9,11},{10,... | collective-permute-start | bytes 393224 | tf_op jit(solution)/shard_map/ppermute | solution.py:276
  9.7 1.4 %collective-permute-start.12 = (bf16[4,64,256]{2,1,0:T(8,128)(2,1)S(1)}, bf16[4,64,256]{2,1,0:T(8,128)(2,1)S(1)}, u32[]{:S(2)}, u32[]{:S(2)}) collective-permute-start(bf16[4,64,256]{2,1,0:T(8,128)(2,1)S(1)} %get-tuple-element.35), channel_id=1, source_target_pairs={{0,3},{1,2},{2,1},{3,0},{4,7},{5,6},{6,5},{7,4},{8,11},{9,10},{10,... | collective-permute-start | bytes 393224 | tf_op jit(solution)/shard_map/ppermute | solution.py:276
  11.1 0.1 collective-permute-start.13
  11.2 0.7 %row_spectra.2 = (bf16[4,64,256]{2,1,0:T(8,128)(2,1)S(1)}, bf16[4,64,256]{2,1,0:T(8,128)(2,1)S(1)}, bf16[4,64,256]{2,1,0:T(8,128)(2,1)S(1)}, bf16[4,64,256]{2,1,0:T(8,128)(2,1)S(1)}) custom-call(bf16[2,2,64,1024]{3,2,1,0:T(8,128)(2,1)S(1)} %get-tuple-element.24.refs_0_, bf16[4,2,64,1024]{3,2,1,0:T(8,128)(2,1)S(1)} %collective-permute-done.refs_1_, ...), custom_call_target="tpu_custom_call" | custom-call | flops 536870912 | bytes 3145728 | tf_op jit(solution)/shard_map/row_spectra/pallas_call | solution.py:324
  12.0 2.0 %collective-permute-start.1 = (bf16[4,64,256]{2,1,0:T(8,128)(2,1)S(1)}, bf16[4,64,256]{2,1,0:T(8,128)(2,1)S(1)}, u32[]{:S(2)}, u32[]{:S(2)}) collective-permute-start(bf16[4,64,256]{2,1,0:T(8,128)(2,1)S(1)} %get-tuple-element.26), channel_id=1, source_target_pairs={{0,2},{1,3},{2,0},{3,1},{4,6},{5,7},{6,4},{7,5},{8,10},{9,11},{10,... | collective-permute-start | bytes 393224 | tf_op jit(solution)/shard_map/ppermute | solution.py:276
  14.0 1.4 %collective-permute-start.2 = (bf16[4,64,256]{2,1,0:T(8,128)(2,1)S(1)}, bf16[4,64,256]{2,1,0:T(8,128)(2,1)S(1)}, u32[]{:S(2)}, u32[]{:S(2)}) collective-permute-start(bf16[4,64,256]{2,1,0:T(8,128)(2,1)S(1)} %get-tuple-element.27), channel_id=1, source_target_pairs={{0,3},{1,2},{2,1},{3,0},{4,7},{5,6},{6,5},{7,4},{8,11},{9,10},{10,... | collective-permute-start | bytes 393224 | tf_op jit(solution)/shard_map/ppermute | solution.py:276
  15.4 1.3 %collective-permute-done.11.refs_3_ = bf16[4,64,256]{2,1,0:T(8,128)(2,1)S(1)} collective-permute-done((bf16[4,64,256]{2,1,0:T(8,128)(2,1)S(1)}, bf16[4,64,256]{2,1,0:T(8,128)(2,1)S(1)}, u32[]{:S(2)}, u32[]{:S(2)}) %collective-permute-start.11) | collective-permute-done | bytes 131104 | tf_op jit(solution)/shard_map/ppermute | solution.py:276
  16.7 2.0 %collective-permute-start.3 = (bf16[4,64,256]{2,1,0:T(8,128)(2,1)S(1)}, bf16[4,64,256]{2,1,0:T(8,128)(2,1)S(1)}, u32[]{:S(2)}, u32[]{:S(2)}) collective-permute-start(bf16[4,64,256]{2,1,0:T(8,128)(2,1)S(1)} %get-tuple-element.28), channel_id=1, source_target_pairs={{0,1},{1,0},{2,3},{3,2},{4,5},{5,4},{6,7},{7,6},{8,9},{9,8},{10,11... | collective-permute-start | bytes 393224 | tf_op jit(solution)/shard_map/ppermute | solution.py:276
  18.8 0.0 collective-permute-done.12.refs_4_
  18.8 0.0 collective-permute-done.13.refs_5_
  18.8 1.3 %columns.3 = (bf16[2,256,256]{2,1,0:T(8,128)(2,1)S(1)}, bf16[2,256,256]{2,1,0:T(8,128)(2,1)S(1)}) custom-call(bf16[1024,1024]{1,0:T(8,128)(2,1)S(1)} %copy-done.1, bf16[4,1024,256]{2,1,0:T(8,128)(2,1)S(1)} %get-tuple-element.23.refs_3_.refs_1_, bf16[4,64,256]{2,1,0:T(8,128)(2,1)S(1)} %get-tuple-element.33.refs_2_, ...), custom_call_target="tpu_custom_call" | custom-call | flops 1073741824 | bytes 4194304 | tf_op jit(solution)/shard_map/columns/pallas_call | solution.py:339
  20.1 1.7 %collective-permute-start.14 = (bf16[2,256,256]{2,1,0:T(8,128)(2,1)S(1)}, bf16[2,256,256]{2,1,0:T(8,128)(2,1)S(1)}, u32[]{:S(2)}, u32[]{:S(2)}) collective-permute-start(bf16[2,256,256]{2,1,0:T(8,128)(2,1)S(1)} %get-tuple-element.38.one), channel_id=1, source_target_pairs={{0,4},{1,5},{2,6},{3,7},{4,0},{5,1},{6,2},{7,3},{8,12},{9,13},{10,... | collective-permute-start | bytes 786440 | tf_op jit(solution)/shard_map/ppermute | solution.py:276
  21.8 0.2 collective-permute-done.1.refs_3_
  21.9 0.7 %collective-permute-done.2.refs_4_ = bf16[4,64,256]{2,1,0:T(8,128)(2,1)S(1)} collective-permute-done((bf16[4,64,256]{2,1,0:T(8,128)(2,1)S(1)}, bf16[4,64,256]{2,1,0:T(8,128)(2,1)S(1)}, u32[]{:S(2)}, u32[]{:S(2)}) %collective-permute-start.2) | collective-permute-done | bytes 131104 | tf_op jit(solution)/shard_map/ppermute | solution.py:276
  22.6 1.0 %collective-permute-done.3.refs_5_ = bf16[4,64,256]{2,1,0:T(8,128)(2,1)S(1)} collective-permute-done((bf16[4,64,256]{2,1,0:T(8,128)(2,1)S(1)}, bf16[4,64,256]{2,1,0:T(8,128)(2,1)S(1)}, u32[]{:S(2)}, u32[]{:S(2)}) %collective-permute-start.3) | collective-permute-done | bytes 131104 | tf_op jit(solution)/shard_map/ppermute | solution.py:276
  23.6 1.3 %columns.2 = (bf16[2,256,256]{2,1,0:T(8,128)(2,1)S(1)}, bf16[2,256,256]{2,1,0:T(8,128)(2,1)S(1)}) custom-call(bf16[1024,1024]{1,0:T(8,128)(2,1)S(1)} %copy-done.1, bf16[4,1024,256]{2,1,0:T(8,128)(2,1)S(1)} %get-tuple-element.23.refs_3_.refs_1_, bf16[4,64,256]{2,1,0:T(8,128)(2,1)S(1)} %get-tuple-element.25.refs_2_, ...), custom_call_target="tpu_custom_call" | custom-call | flops 1073741824 | bytes 4194304 | tf_op jit(solution)/shard_map/columns/pallas_call | solution.py:339
  24.9 0.0 copy-start.4
  25.0 0.0 copy-start.5
  25.0 1.8 %collective-permute-start.4 = (bf16[2,256,256]{2,1,0:T(8,128)(2,1)S(1)}, bf16[2,256,256]{2,1,0:T(8,128)(2,1)S(1)}, u32[]{:S(2)}, u32[]{:S(2)}) collective-permute-start(bf16[2,256,256]{2,1,0:T(8,128)(2,1)S(1)} %get-tuple-element.30.one), channel_id=1, source_target_pairs={{0,4},{1,5},{2,6},{3,7},{4,0},{5,1},{6,2},{7,3},{8,12},{9,13},{10,... | collective-permute-start | bytes 786440 | tf_op jit(solution)/shard_map/ppermute | solution.py:276
  26.8 0.5 collective-permute-done.14.two
  27.3 0.1 joint.3
  27.4 0.1 collective-permute-start.15
  27.4 5.5 %collective-permute-done.4.two = bf16[2,256,256]{2,1,0:T(8,128)(2,1)S(1)} collective-permute-done((bf16[2,256,256]{2,1,0:T(8,128)(2,1)S(1)}, bf16[2,256,256]{2,1,0:T(8,128)(2,1)S(1)}, u32[]{:S(2)}, u32[]{:S(2)}) %collective-permute-start.4) | collective-permute-done | bytes 262176 | tf_op jit(solution)/shard_map/ppermute | solution.py:276
  33.0 0.1 joint.2
  33.0 0.1 collective-permute-start.5
  33.1 0.0 collective-permute-done.15.refs_1_
  33.1 0.1 near.3
  33.2 3.0 %collective-permute-start.16 = (bf16[256,256]{1,0:T(8,128)(2,1)S(1)}, bf16[256,256]{1,0:T(8,128)(2,1)}, u32[]{:S(2)}, u32[]{:S(2)}) collective-permute-start(bf16[256,256]{1,0:T(8,128)(2,1)S(1)} %near.3), channel_id=1, source_target_pairs={{0,4},{1,5},{2,6},{3,7},{4,0},{5,1},{6,2},{7,3},{8,12},{9,13},{10,... | collective-permute-start | bytes 393224 | tf_op jit(solution)/shard_map/ppermute | solution.py:276
  36.2 0.7 %fusion.13 = (s32[1]{0:T(128)}, s32[1]{0:T(128)}) fusion(s32[16]{0:T(128)S(1)} %copy-done.4, s32[]{:T(128)S(6)} %select_n.40, s32[]{:T(128)S(6)} %select_n.41), kind=kLoop, calls=%fused_computation.22 | loop fusion | bytes 24 | tf_op jit(solution)/shard_map/dynamic_slice | solution.py:264
  37.5 0.1 near.2.refs_3_
  37.6 3.8 %collective-permute-start.6 = (bf16[256,256]{1,0:T(8,128)(2,1)S(1)}, bf16[256,256]{1,0:T(8,128)(2,1)S(1)}, u32[]{:S(2)}, u32[]{:S(2)}) collective-permute-start(bf16[256,256]{1,0:T(8,128)(2,1)S(1)} %near.2.refs_3_), channel_id=1, source_target_pairs={{0,4},{1,5},{2,6},{3,7},{4,0},{5,1},{6,2},{7,3},{8,12},{9,13},{10,... | collective-permute-start | bytes 393224 | tf_op jit(solution)/shard_map/ppermute | solution.py:276
  41.4 0.7 %pad_add_fusion.refs_4_.refs_0_ = s32[6]{0:T(128)S(1)} fusion(s32[1]{0:T(128)} %get-tuple-element.48, s32[1]{0:T(128)} %bitcast.2, s32[4]{0:T(128)S(1)} %bitcast.6), kind=kLoop, calls=%fused_computation.19 | loop fusion | flops 12 | bytes 48 | tf_op jit(solution)/shard_map/concatenate | solution.py:261
  42.1 0.0 collective-permute-done.16.refs_2_
  42.1 1.0 %half.3 = (bf16[128,256]{1,0:T(8,128)(2,1)S(1)}, bf16[128,256]{1,0:T(8,128)(2,1)S(1)}) custom-call(bf16[2,256,256]{2,1,0:T(8,128)(2,1)S(1)} %get-tuple-element.37.refs_0_, bf16[2,256,256]{2,1,0:T(8,128)(2,1)S(1)} %collective-permute-done.15.refs_1_, bf16[256,256]{1,0:T(8,128)(2,1)} %collective-permute-done.16.refs_2_, bf16[256,256]{1,0:T(8,128)(2,1)S(1)} %near.2.refs_3_, ...), custom_call_target="tpu_custom_call" | custom-call | flops 1 | bytes 16384 | tf_op jit(solution)/shard_map/half/pallas_call | solution.py:389
  43.1 1.6 %collective-permute-start.17 = (bf16[128,256]{1,0:T(8,128)(2,1)S(1)}, bf16[128,256]{1,0:T(8,128)(2,1)S(1)}, u32[]{:S(2)}, u32[]{:S(2)}) collective-permute-start(bf16[128,256]{1,0:T(8,128)(2,1)S(1)} %get-tuple-element.39.refs_1_), channel_id=1, source_target_pairs={{0,1},{1,0},{2,3},{3,2},{4,5},{5,4},{6,7},{7,6},{8,9},{9,8},{10,11... | collective-permute-start | bytes 196616 | tf_op jit(solution)/shard_map/ppermute | solution.py:276
  44.7 1.5 %collective-permute-start.19 = (bf16[128,256]{1,0:T(8,128)(2,1)S(1)}, bf16[128,256]{1,0:T(8,128)(2,1)S(1)}, u32[]{:S(2)}, u32[]{:S(2)}) collective-permute-start(bf16[128,256]{1,0:T(8,128)(2,1)S(1)} %get-tuple-element.40), channel_id=1, source_target_pairs={{0,2},{1,3},{2,0},{3,1},{4,6},{5,7},{6,4},{7,5},{8,10},{9,11},{10,... | collective-permute-start | bytes 196616 | tf_op jit(solution)/shard_map/ppermute | solution.py:276
  46.1 0.5 collective-permute-start.18
  46.7 0.0 collective-permute-done.6.refs_2_
  46.7 0.1 half.2
  46.7 1.6 %collective-permute-start.7 = (bf16[128,256]{1,0:T(8,128)(2,1)S(1)}, bf16[128,256]{1,0:T(8,128)(2,1)S(1)}, u32[]{:S(2)}, u32[]{:S(2)}) collective-permute-start(bf16[128,256]{1,0:T(8,128)(2,1)S(1)} %get-tuple-element.31.refs_1_), channel_id=1, source_target_pairs={{0,1},{1,0},{2,3},{3,2},{4,5},{5,4},{6,7},{7,6},{8,9},{9,8},{10,11... | collective-permute-start | bytes 196616 | tf_op jit(solution)/shard_map/ppermute | solution.py:276
  48.3 1.5 %collective-permute-start.9 = (bf16[128,256]{1,0:T(8,128)(2,1)S(1)}, bf16[128,256]{1,0:T(8,128)(2,1)S(1)}, u32[]{:S(2)}, u32[]{:S(2)}) collective-permute-start(bf16[128,256]{1,0:T(8,128)(2,1)S(1)} %get-tuple-element.32), channel_id=1, source_target_pairs={{0,2},{1,3},{2,0},{3,1},{4,6},{5,7},{6,4},{7,5},{8,10},{9,11},{10,... | collective-permute-start | bytes 196616 | tf_op jit(solution)/shard_map/ppermute | solution.py:276
  49.8 0.5 collective-permute-start.8
  50.3 1.0 %collective-permute-done.18.refs_3_ = bf16[128,256]{1,0:T(8,128)(2,1)S(1)} collective-permute-done((bf16[128,256]{1,0:T(8,128)(2,1)S(1)}, bf16[128,256]{1,0:T(8,128)(2,1)S(1)}, u32[]{:S(2)}, u32[]{:S(2)}) %collective-permute-start.18) | collective-permute-done | bytes 65568 | tf_op jit(solution)/shard_map/ppermute | solution.py:276
  51.3 0.5 phase.3.refs_2_
  51.8 0.1 collective-permute-start.20
  51.9 0.7 %collective-permute-done.9.refs_4_ = bf16[128,256]{1,0:T(8,128)(2,1)S(1)} collective-permute-done((bf16[128,256]{1,0:T(8,128)(2,1)S(1)}, bf16[128,256]{1,0:T(8,128)(2,1)S(1)}, u32[]{:S(2)}, u32[]{:S(2)}) %collective-permute-start.9) | collective-permute-done | bytes 65568 | tf_op jit(solution)/shard_map/ppermute | solution.py:276
  52.5 2.4 %collective-permute-done.8.refs_3_ = bf16[128,256]{1,0:T(8,128)(2,1)S(1)} collective-permute-done((bf16[128,256]{1,0:T(8,128)(2,1)S(1)}, bf16[128,256]{1,0:T(8,128)(2,1)S(1)}, u32[]{:S(2)}, u32[]{:S(2)}) %collective-permute-start.8) | collective-permute-done | bytes 65568 | tf_op jit(solution)/shard_map/ppermute | solution.py:276
  54.9 0.5 phase.2.refs_2_
  55.4 0.1 collective-permute-start.10
  55.5 1.0 %recon.3.refs_3_ = f32[128,512]{1,0:T(8,128)S(1)} custom-call(s32[6]{0:T(128)S(1)} %pad_add_fusion.refs_4_.refs_0_, bf16[4,1024,512]{2,1,0:T(8,128)(2,1)S(1)} %copy-done.2, bf16[128,1024]{1,0:T(8,128)(2,1)S(1)} %phase.3.refs_2_, bf16[128,1024]{1,0:T(8,128)(2,1)S(1)} %collective-permute-done.20.refs_3_), custom_call_target="tpu_custom_call" | custom-call | flops 1 | bytes 8192 | tf_op jit(solution)/shard_map/recon/pallas_call | solution.py:377
  56.5 0.9 %recon.4.refs_3_ = f32[128,512]{1,0:T(8,128)S(1)} custom-call(s32[6]{0:T(128)S(1)} %pad_add_fusion.refs_4_.refs_0_, bf16[4,1024,512]{2,1,0:T(8,128)(2,1)S(1)} %copy-done.2, bf16[128,1024]{1,0:T(8,128)(2,1)S(1)} %phase.2.refs_2_, f32[128,512]{1,0:T(8,128)S(1)} %recon.3.refs_3_), custom_call_target="tpu_custom_call" | custom-call | flops 1 | bytes 8192 | tf_op jit(solution)/shard_map/recon/pallas_call | solution.py:377
  57.4 1.6 %recon.5 = bf16[128,512]{1,0:T(8,128)(2,1)} custom-call(s32[6]{0:T(128)S(1)} %pad_add_fusion.refs_4_.refs_0_, bf16[4,1024,512]{2,1,0:T(8,128)(2,1)S(1)} %copy-done.2, bf16[128,1024]{1,0:T(8,128)(2,1)S(1)} %collective-permute-done.10.refs_2_, f32[128,512]{1,0:T(8,128)S(1)} %recon.4.refs_3_), custom_call_target="tpu_custom_call" | custom-call | flops 1 | bytes 8192 | tf_op jit(solution)/shard_map/recon/pallas_call | solution.py:377
  (15 shorter events, 0.1 us)
Async XLA Ops:
  0.0 4.8 %collective-permute-start = (bf16[4,2,64,1024]{3,2,1,0:T(8,128)(2,1)}, bf16[4,2,64,1024]{3,2,1,0:T(8,128)(2,1)S(1)}, u32[]{:S(2)}, u32[]{:S(2)}) collective-permute-start(bf16[4,2,64,1024]{3,2,1,0:T(8,128)(2,1)} %bitcast.4), channel_id=1, source_target_pairs={{0,16},{1,17},{2,18},{3,19},{4,20},{5,21},{6,22},{7,23},{8,24},{9,... | collective-permute-start | bytes 3145736 | tf_op jit(solution)/shard_map/ppermute | solution.py:276
  1.7 1.2 %copy-start.3 = (bf16[1,4,2,64,1024]{4,3,2,1,0:T(8,128)(2,1)S(1)}, bf16[1,4,2,64,1024]{4,3,2,1,0:T(8,128)(2,1)}, u32[]{:S(2)}) copy-start(bf16[1,4,2,64,1024]{4,3,2,1,0:T(8,128)(2,1)} %param.6) | copy-start | bytes 3145732
  4.8 1.6 %copy-start = (bf16[1024,1024]{1,0:T(8,128)(2,1)S(1)}, bf16[1024,1024]{1,0:T(8,128)(2,1)}, u32[]{:S(2)}) copy-start(bf16[1024,1024]{1,0:T(8,128)(2,1)} %constant.57.clone.refs_2_.refs_0_) | copy-start | bytes 6291460
  7.1 9.6 %collective-permute-start.11 = (bf16[4,64,256]{2,1,0:T(8,128)(2,1)S(1)}, bf16[4,64,256]{2,1,0:T(8,128)(2,1)S(1)}, u32[]{:S(2)}, u32[]{:S(2)}) collective-permute-start(bf16[4,64,256]{2,1,0:T(8,128)(2,1)S(1)} %get-tuple-element.34), channel_id=1, source_target_pairs={{0,2},{1,3},{2,0},{3,1},{4,6},{5,7},{6,4},{7,5},{8,10},{9,11},{10,... | collective-permute-start | bytes 393224 | tf_op jit(solution)/shard_map/ppermute | solution.py:276
  9.7 9.1 %collective-permute-start.12 = (bf16[4,64,256]{2,1,0:T(8,128)(2,1)S(1)}, bf16[4,64,256]{2,1,0:T(8,128)(2,1)S(1)}, u32[]{:S(2)}, u32[]{:S(2)}) collective-permute-start(bf16[4,64,256]{2,1,0:T(8,128)(2,1)S(1)} %get-tuple-element.35), channel_id=1, source_target_pairs={{0,3},{1,2},{2,1},{3,0},{4,7},{5,6},{6,5},{7,4},{8,11},{9,10},{10,... | collective-permute-start | bytes 393224 | tf_op jit(solution)/shard_map/ppermute | solution.py:276
  11.1 7.6 %copy-start.1 = (bf16[1024,1024]{1,0:T(8,128)(2,1)S(1)}, bf16[1024,1024]{1,0:T(8,128)(2,1)}, u32[]{:S(2)}) copy-start(bf16[1024,1024]{1,0:T(8,128)(2,1)} %constant.57.clone.refs_2_.refs_0_) | copy-start | bytes 6291460
  11.1 7.6 %collective-permute-start.13 = (bf16[4,64,256]{2,1,0:T(8,128)(2,1)S(1)}, bf16[4,64,256]{2,1,0:T(8,128)(2,1)S(1)}, u32[]{:S(2)}, u32[]{:S(2)}) collective-permute-start(bf16[4,64,256]{2,1,0:T(8,128)(2,1)S(1)} %get-tuple-element.36), channel_id=1, source_target_pairs={{0,1},{1,0},{2,3},{3,2},{4,5},{5,4},{6,7},{7,6},{8,9},{9,8},{10,11... | collective-permute-start | bytes 393224 | tf_op jit(solution)/shard_map/ppermute | solution.py:276
  12.0 9.9 %collective-permute-start.1 = (bf16[4,64,256]{2,1,0:T(8,128)(2,1)S(1)}, bf16[4,64,256]{2,1,0:T(8,128)(2,1)S(1)}, u32[]{:S(2)}, u32[]{:S(2)}) collective-permute-start(bf16[4,64,256]{2,1,0:T(8,128)(2,1)S(1)} %get-tuple-element.26), channel_id=1, source_target_pairs={{0,2},{1,3},{2,0},{3,1},{4,6},{5,7},{6,4},{7,5},{8,10},{9,11},{10,... | collective-permute-start | bytes 393224 | tf_op jit(solution)/shard_map/ppermute | solution.py:276
  14.0 8.6 %collective-permute-start.2 = (bf16[4,64,256]{2,1,0:T(8,128)(2,1)S(1)}, bf16[4,64,256]{2,1,0:T(8,128)(2,1)S(1)}, u32[]{:S(2)}, u32[]{:S(2)}) collective-permute-start(bf16[4,64,256]{2,1,0:T(8,128)(2,1)S(1)} %get-tuple-element.27), channel_id=1, source_target_pairs={{0,3},{1,2},{2,1},{3,0},{4,7},{5,6},{6,5},{7,4},{8,11},{9,10},{10,... | collective-permute-start | bytes 393224 | tf_op jit(solution)/shard_map/ppermute | solution.py:276
  16.7 6.9 %collective-permute-start.3 = (bf16[4,64,256]{2,1,0:T(8,128)(2,1)S(1)}, bf16[4,64,256]{2,1,0:T(8,128)(2,1)S(1)}, u32[]{:S(2)}, u32[]{:S(2)}) collective-permute-start(bf16[4,64,256]{2,1,0:T(8,128)(2,1)S(1)} %get-tuple-element.28), channel_id=1, source_target_pairs={{0,1},{1,0},{2,3},{3,2},{4,5},{5,4},{6,7},{7,6},{8,9},{9,8},{10,11... | collective-permute-start | bytes 393224 | tf_op jit(solution)/shard_map/ppermute | solution.py:276
  20.1 7.2 %collective-permute-start.14 = (bf16[2,256,256]{2,1,0:T(8,128)(2,1)S(1)}, bf16[2,256,256]{2,1,0:T(8,128)(2,1)S(1)}, u32[]{:S(2)}, u32[]{:S(2)}) collective-permute-start(bf16[2,256,256]{2,1,0:T(8,128)(2,1)S(1)} %get-tuple-element.38.one), channel_id=1, source_target_pairs={{0,4},{1,5},{2,6},{3,7},{4,0},{5,1},{6,2},{7,3},{8,12},{9,13},{10,... | collective-permute-start | bytes 786440 | tf_op jit(solution)/shard_map/ppermute | solution.py:276
  24.9 11.3 %copy-start.4 = (s32[16]{0:T(128)S(1)}, s32[16]{0:T(128)}, u32[]{:S(2)}) copy-start(s32[16]{0:T(128)} %param.10) | copy-start | bytes 196
  25.0 16.4 %copy-start.5 = (s32[1,4]{1,0:T(1,128)S(1)}, s32[1,4]{1,0:T(1,128)}, u32[]{:S(2)}) copy-start(s32[1,4]{1,0:T(1,128)} %param.9) | copy-start | bytes 52
  25.0 8.0 %collective-permute-start.4 = (bf16[2,256,256]{2,1,0:T(8,128)(2,1)S(1)}, bf16[2,256,256]{2,1,0:T(8,128)(2,1)S(1)}, u32[]{:S(2)}, u32[]{:S(2)}) collective-permute-start(bf16[2,256,256]{2,1,0:T(8,128)(2,1)S(1)} %get-tuple-element.30.one), channel_id=1, source_target_pairs={{0,4},{1,5},{2,6},{3,7},{4,0},{5,1},{6,2},{7,3},{8,12},{9,13},{10,... | collective-permute-start | bytes 786440 | tf_op jit(solution)/shard_map/ppermute | solution.py:276
  27.4 5.8 %collective-permute-start.15 = (bf16[2,256,256]{2,1,0:T(8,128)(2,1)S(1)}, bf16[2,256,256]{2,1,0:T(8,128)(2,1)S(1)}, u32[]{:S(2)}, u32[]{:S(2)}) collective-permute-start(bf16[2,256,256]{2,1,0:T(8,128)(2,1)S(1)} %joint.3), channel_id=1, source_target_pairs={{0,16},{1,17},{2,18},{3,19},{4,8},{5,9},{6,10},{7,11},{8,4},{9,5},... | collective-permute-start | bytes 786440 | tf_op jit(solution)/shard_map/ppermute | solution.py:276
  33.0 4.5 %collective-permute-start.5 = (bf16[2,256,256]{2,1,0:T(8,128)(2,1)S(1)}, bf16[2,256,256]{2,1,0:T(8,128)(2,1)S(1)}, u32[]{:S(2)}, u32[]{:S(2)}) collective-permute-start(bf16[2,256,256]{2,1,0:T(8,128)(2,1)S(1)} %joint.2), channel_id=1, source_target_pairs={{0,16},{1,17},{2,18},{3,19},{4,8},{5,9},{6,10},{7,11},{8,4},{9,5},... | collective-permute-start | bytes 786440 | tf_op jit(solution)/shard_map/ppermute | solution.py:276
  33.2 8.9 %collective-permute-start.16 = (bf16[256,256]{1,0:T(8,128)(2,1)S(1)}, bf16[256,256]{1,0:T(8,128)(2,1)}, u32[]{:S(2)}, u32[]{:S(2)}) collective-permute-start(bf16[256,256]{1,0:T(8,128)(2,1)S(1)} %near.3), channel_id=1, source_target_pairs={{0,4},{1,5},{2,6},{3,7},{4,0},{5,1},{6,2},{7,3},{8,12},{9,13},{10,... | collective-permute-start | bytes 393224 | tf_op jit(solution)/shard_map/ppermute | solution.py:276
  37.6 9.1 %collective-permute-start.6 = (bf16[256,256]{1,0:T(8,128)(2,1)S(1)}, bf16[256,256]{1,0:T(8,128)(2,1)S(1)}, u32[]{:S(2)}, u32[]{:S(2)}) collective-permute-start(bf16[256,256]{1,0:T(8,128)(2,1)S(1)} %near.2.refs_3_), channel_id=1, source_target_pairs={{0,4},{1,5},{2,6},{3,7},{4,0},{5,1},{6,2},{7,3},{8,12},{9,13},{10,... | collective-permute-start | bytes 393224 | tf_op jit(solution)/shard_map/ppermute | solution.py:276
  43.1 6.7 %collective-permute-start.17 = (bf16[128,256]{1,0:T(8,128)(2,1)S(1)}, bf16[128,256]{1,0:T(8,128)(2,1)S(1)}, u32[]{:S(2)}, u32[]{:S(2)}) collective-permute-start(bf16[128,256]{1,0:T(8,128)(2,1)S(1)} %get-tuple-element.39.refs_1_), channel_id=1, source_target_pairs={{0,1},{1,0},{2,3},{3,2},{4,5},{5,4},{6,7},{7,6},{8,9},{9,8},{10,11... | collective-permute-start | bytes 196616 | tf_op jit(solution)/shard_map/ppermute | solution.py:276
  44.7 5.6 %collective-permute-start.19 = (bf16[128,256]{1,0:T(8,128)(2,1)S(1)}, bf16[128,256]{1,0:T(8,128)(2,1)S(1)}, u32[]{:S(2)}, u32[]{:S(2)}) collective-permute-start(bf16[128,256]{1,0:T(8,128)(2,1)S(1)} %get-tuple-element.40), channel_id=1, source_target_pairs={{0,2},{1,3},{2,0},{3,1},{4,6},{5,7},{6,4},{7,5},{8,10},{9,11},{10,... | collective-permute-start | bytes 196616 | tf_op jit(solution)/shard_map/ppermute | solution.py:276
  46.1 5.2 %collective-permute-start.18 = (bf16[128,256]{1,0:T(8,128)(2,1)S(1)}, bf16[128,256]{1,0:T(8,128)(2,1)S(1)}, u32[]{:S(2)}, u32[]{:S(2)}) collective-permute-start(bf16[128,256]{1,0:T(8,128)(2,1)S(1)} %get-tuple-element.40), channel_id=1, source_target_pairs={{0,3},{1,2},{2,1},{3,0},{4,7},{5,6},{6,5},{7,4},{8,11},{9,10},{10,... | collective-permute-start | bytes 196616 | tf_op jit(solution)/shard_map/ppermute | solution.py:276
  46.7 5.1 %collective-permute-start.7 = (bf16[128,256]{1,0:T(8,128)(2,1)S(1)}, bf16[128,256]{1,0:T(8,128)(2,1)S(1)}, u32[]{:S(2)}, u32[]{:S(2)}) collective-permute-start(bf16[128,256]{1,0:T(8,128)(2,1)S(1)} %get-tuple-element.31.refs_1_), channel_id=1, source_target_pairs={{0,1},{1,0},{2,3},{3,2},{4,5},{5,4},{6,7},{7,6},{8,9},{9,8},{10,11... | collective-permute-start | bytes 196616 | tf_op jit(solution)/shard_map/ppermute | solution.py:276
  48.3 7.2 %copy-start.2 = (bf16[4,1024,512]{2,1,0:T(8,128)(2,1)S(1)}, bf16[4,1024,512]{2,1,0:T(8,128)(2,1)}, u32[]{:S(2)}) copy-start(bf16[4,1024,512]{2,1,0:T(8,128)(2,1)} %refs_1_.5) | copy-start | bytes 12582916
  48.3 4.3 %collective-permute-start.9 = (bf16[128,256]{1,0:T(8,128)(2,1)S(1)}, bf16[128,256]{1,0:T(8,128)(2,1)S(1)}, u32[]{:S(2)}, u32[]{:S(2)}) collective-permute-start(bf16[128,256]{1,0:T(8,128)(2,1)S(1)} %get-tuple-element.32), channel_id=1, source_target_pairs={{0,2},{1,3},{2,0},{3,1},{4,6},{5,7},{6,4},{7,5},{8,10},{9,11},{10,... | collective-permute-start | bytes 196616 | tf_op jit(solution)/shard_map/ppermute | solution.py:276
  49.8 5.2 %collective-permute-start.8 = (bf16[128,256]{1,0:T(8,128)(2,1)S(1)}, bf16[128,256]{1,0:T(8,128)(2,1)S(1)}, u32[]{:S(2)}, u32[]{:S(2)}) collective-permute-start(bf16[128,256]{1,0:T(8,128)(2,1)S(1)} %get-tuple-element.32), channel_id=1, source_target_pairs={{0,3},{1,2},{2,1},{3,0},{4,7},{5,6},{6,5},{7,4},{8,11},{9,10},{10,... | collective-permute-start | bytes 196616 | tf_op jit(solution)/shard_map/ppermute | solution.py:276
  51.8 3.7 %collective-permute-start.20 = (bf16[128,1024]{1,0:T(8,128)(2,1)S(1)}, bf16[128,1024]{1,0:T(8,128)(2,1)S(1)}, u32[]{:S(2)}, u32[]{:S(2)}) collective-permute-start(bf16[128,1024]{1,0:T(8,128)(2,1)S(1)} %phase.3.refs_2_), channel_id=1, source_target_pairs={{0,16},{1,17},{2,18},{3,19},{4,20},{5,21},{6,22},{7,23},{8,24},{9,... | collective-permute-start | bytes 786440 | tf_op jit(solution)/shard_map/ppermute | solution.py:276
  55.4 2.0 %collective-permute-start.10 = (bf16[128,1024]{1,0:T(8,128)(2,1)S(1)}, bf16[128,1024]{1,0:T(8,128)(2,1)S(1)}, u32[]{:S(2)}, u32[]{:S(2)}) collective-permute-start(bf16[128,1024]{1,0:T(8,128)(2,1)S(1)} %phase.2.refs_2_), channel_id=1, source_target_pairs={{0,16},{1,17},{2,18},{3,19},{4,20},{5,21},{6,22},{7,23},{8,24},{9,... | collective-permute-start | bytes 786440 | tf_op jit(solution)/shard_map/ppermute | solution.py:276

commit v9 on v8

--- a/solution.py
+++ b/solution.py
@@ -12,8 +12,6 @@
 regularizer = 0.05
 bf16 = jnp.bfloat16
 f32 = jnp.float32
-send_order = (0, 2, 3, 1)
-tail_order = (0, 1, 3, 2)
 
 
 def hartley(length):
@@ -98,27 +96,42 @@
     return lax.axis_index("dist"), device // inner, device % inner
 
 
-def row_kernel(inner, chunk, here, there, table, after, *outs):
+def steps_of(core):
+    return 2 - core, 1 + core
+
+
+def whole_turns(scale, square):
+    turns = scale * square * (0.5 / math.pi)
+    return (turns - jnp.round(turns)) * (2.0 * math.pi)
+
+
+def filter_kernel(inner, propagation, holo, out, mine, arrived):
+    dists, width, block = out.shape
+    own, dist_dev = mine.shape[:2]
     core, _, spot = position(inner)
-    own, dist_dev, rows_dev, width = here.shape
-    block = width // inner
-    partner = there[core * own + chunk]
-    flat = jnp.concatenate(
-        [source.reshape(dist_dev * rows_dev, width) for source in (here[chunk], partner)], axis=0
-    )
-    for rel in range(inner):
-        part = table[:, pl.ds(pl.multiple_of((spot ^ rel) * block, block), block)]
-        got = jnp.dot(flat, part, preferred_element_type=f32).astype(bf16)
-        outs[rel][...] = got.reshape(2 * dist_dev, rows_dev, block)
-
-
-def filter_kernel(waves_a, with_sin, with_cos, holo, out, mine, arrived):
-    dists, width, block = out.shape
-    own = mine.shape[0]
-    core = lax.axis_index("dist")
     copy = pltpu.make_async_copy(holo.at[pl.ds(core * own, own)], mine, arrived)
     copy.start()
-    turned = waves_a[...].T
+
+    def square(first, length):
+        index = lax.broadcasted_iota(jnp.int32, (1, length), 1) + first
+        signed = jnp.where(index < width // 2, index, index - width).astype(f32)
+        return signed * signed * (1.0 / (width * width))
+
+    def phases(first, length):
+        values = square(first, length)
+        rows = []
+        for d in range(dists):
+            other = d // dist_dev
+            scale = propagation[(core ^ other) * dist_dev + d % dist_dev]
+            rows.append(whole_turns(scale, values))
+        return jnp.concatenate(rows, axis=0)
+
+    along = phases(0, width)
+    across = phases(spot * block, block)
+    sin_b, cos_b = jnp.sin(across), jnp.cos(across)
+    with_sin = 2.0 * (cos_b - absorb_ratio * sin_b)
+    with_cos = 2.0 * (sin_b + absorb_ratio * cos_b)
+    turned = jnp.concatenate([jnp.sin(along), jnp.cos(along)], axis=0).T
     step = 128
     for at in range(0, width, step):
         rows = turned[at : at + step]
@@ -136,37 +149,65 @@
     copy.wait()
 
 
-def column_kernel(inner, outer, table, gain, *refs):
-    pieces = dict(zip(send_order, refs[:inner]))
-    away, keep, stack, total, spectrum = refs[inner:]
-    _, plane, spot = position(inner)
-    dists, rows_dev, block = pieces[0].shape
+def row_kernel(inner, chunk, here, there, table, after, stays, leaves, later):
+    core, _, spot = position(inner)
+    first, second = steps_of(core)
+    own, dist_dev, rows_dev, width = here.shape
+    block = width // inner
+    partner = there[core * own + chunk]
+    flat = jnp.concatenate(
+        [source.reshape(dist_dev * rows_dev, width) for source in (here[chunk], partner)], axis=0
+    )
+
+    def part(rel):
+        columns = pl.ds(pl.multiple_of((spot ^ rel) * block, block), block)
+        got = jnp.dot(flat, table[:, columns], preferred_element_type=f32).astype(bf16)
+        return got.reshape(2 * dist_dev, rows_dev, block)
+
+    leaves[0] = part(first)
+    leaves[1] = part(3)
+    later[...] = part(second)
+    stays[...] = part(0)
+
+
+def relay_kernel(later, got, out):
+    out[0] = later[...]
+    out[1] = got[1]
+
+
+def column_kernel(inner, outer, table, gain, stays, got, relayed, *refs):
+    away, keep, stack, total, spectrum = refs
+    core, plane, spot = position(inner)
+    first, second = steps_of(core)
+    dists, rows_dev, block = stays.shape
     depth = inner * rows_dev
-    for rel in range(inner):
+    pieces = ((0, stays), (first, got.at[0]), (second, relayed.at[0]), (3, relayed.at[1]))
+    for rel, piece in pieces:
         start = pl.multiple_of((spot ^ rel) * rows_dev, rows_dev)
         for d in range(dists):
-            stack[d, pl.ds(start, rows_dev), :] = pieces[rel][d]
+            stack[d, pl.ds(start, rows_dev), :] = piece[d]
     part = table[:, pl.ds(pl.multiple_of(plane * depth, depth), depth)]
     for d in range(dists):
-        got = jnp.dot(part, stack[d], preferred_element_type=f32) * gain[d].astype(f32)
+        value = jnp.dot(part, stack[d], preferred_element_type=f32) * gain[d].astype(f32)
         if d == 0:
-            total[...] = got
+            total[...] = value
         else:
-            total[...] += got
+            total[...] += value
     spectrum[...] = total[...].astype(bf16)
     half = outer // 2
     side = plane // half
-    for out, first in ((away, (1 - side) * half), (keep, side * half)):
-        rows = pl.ds(pl.multiple_of(first * depth, half * depth), half * depth)
-        got = jnp.dot(table[rows, :], spectrum[...], preferred_element_type=f32)
-        out[...] = got.astype(bf16).reshape(half, depth, block)
+    for out, low in ((away, (1 - side) * half), (keep, side * half)):
+        rows = pl.ds(pl.multiple_of(low * depth, half * depth), half * depth)
+        value = jnp.dot(table[rows, :], spectrum[...], preferred_element_type=f32)
+        out[...] = value.astype(bf16).reshape(half, depth, block)
 
 
 def add_kernel(one, two, out):
     out[...] = (one[...].astype(f32) + two[...].astype(f32)).astype(bf16)
 
 
-def near_kernel(inner, keep, across, out):
+def near_kernel(inner, keep, across, *refs):
+    out = refs[-1]
     _, plane, _ = position(inner)
     which = (plane ^ 1) % 2
     inside = (plane == 1) | (plane == 2)
@@ -175,57 +216,90 @@
 
 
 def half_kernel(inner, keep, across, last, *refs):
-    mine, other = refs[-2:]
-    _, plane, spot = position(inner)
+    stays, leaves, later = refs[-3:]
+    core, plane, spot = position(inner)
     which = plane % 2
     inside = (plane == 1) | (plane == 2)
-    capacity = mine.shape[0]
-    for out, pair in ((mine, spot // 2), (other, 1 - spot // 2)):
+    capacity = stays.shape[0]
+    got = []
+    for pair in (spot // 2, 1 - spot // 2):
         rows = pl.ds(pl.multiple_of(pair * capacity, capacity), capacity)
         more = jnp.where(inside, across[which, rows, :].astype(f32), 0.0)
-        got = keep[which, rows, :].astype(f32) + more + last[rows, :].astype(f32)
-        out[...] = got.astype(bf16)
-
-
-def phase_kernel(inner, table, *refs):
-    pieces = dict(zip(tail_order, refs[:inner]))
+        value = keep[which, rows, :].astype(f32) + more + last[rows, :].astype(f32)
+        got.append(value.astype(bf16))
+    near, far = got
+    stays[...] = near
+    leaves[0] = jnp.where(core == 0, far, near)
+    leaves[1] = far
+    later[...] = jnp.where(core == 0, near, far)
+
+
+def phase_kernel(inner, table, stays, got, relayed, *refs):
     out, joined = refs[-2:]
-    _, _, spot = position(inner)
-    block = refs[0].shape[1]
-    for rel in range(inner):
+    core, _, spot = position(inner)
+    first, second = steps_of(core)
+    block = stays.shape[1]
+    pieces = ((0, stays), (first, got.at[0]), (second, relayed.at[0]), (3, relayed.at[1]))
+    for rel, piece in pieces:
         columns = pl.ds(pl.multiple_of((spot ^ rel) * block, block), block)
-        joined[:, columns] = pieces[rel][...]
+        joined[:, columns] = piece[...]
     out[...] = jnp.dot(joined[...], table[...], preferred_element_type=f32).astype(bf16)
 
 
-def recon_kernel(own, chunk, cores, info, weights, *refs):
+def choose_kernel(order, slabs, weights, after, chosen, select, arrived):
+    angles = chosen.shape[0]
     core = lax.axis_index("dist")
-    phases, out = refs[: len(cores)], refs[-1]
-    total = refs[-2][...] if len(refs) > len(cores) + 1 else None
-    for other, phase in zip(cores, phases):
-        chosen = weights[info[(core ^ other) * own + chunk]]
-        got = jnp.dot(phase[...], chosen, preferred_element_type=f32)
+    device = lax.axis_index("rows")
+    own = angles // 2
+    copies = [
+        pltpu.make_async_copy(
+            weights.at[order[0, (core ^ (step // own)) * own + step % own]],
+            chosen.at[step],
+            arrived.at[step],
+        )
+        for step in range(angles)
+    ]
+    for copy in copies:
+        copy.start()
+    parity = device % 2
+    offset = parity * slabs[device - parity]
+    slot = lax.broadcasted_iota(jnp.int32, select.shape, 0)
+    source = lax.broadcasted_iota(jnp.int32, select.shape, 1)
+    picked = (source == slot + offset) & (slot < slabs[device])
+    select[...] = jnp.where(picked, 1.0, 0.0).astype(bf16)
+    for copy in copies:
+        copy.wait()
+
+
+def recon_kernel(steps, weights, *refs):
+    phases, out = refs[: len(steps)], refs[-1]
+    total = refs[-2][...] if len(refs) > len(steps) + 1 else None
+    for step, phase in zip(steps, phases):
+        got = jnp.dot(phase[...], weights[step], preferred_element_type=f32)
         total = got if total is None else total + got
     out[...] = total
 
 
-def recon_last_kernel(own, chunk, other, info, weights, phase, before, out):
-    core = lax.axis_index("dist")
-    chosen = weights[info[(core ^ other) * own + chunk]]
-    total = before[...] + jnp.dot(phase[...], chosen, preferred_element_type=f32)
-    capacity = total.shape[0]
-    offset, count = info[weights.shape[0]], info[weights.shape[0] + 1]
-    turned = pltpu.roll(total, lax.rem(capacity - offset, capacity), 0)
-    slot = lax.broadcasted_iota(jnp.int32, turned.shape, 0)
-    out[...] = jnp.where(slot < count, turned, 0.0).astype(bf16)
+def recon_last_kernel(step, weights, phase, before, select, out):
+    total = before[...] + jnp.dot(phase[...], weights[step], preferred_element_type=f32)
+    got = jnp.dot(select[...], total.astype(bf16), preferred_element_type=f32)
+    out[...] = got.astype(bf16)
 
 
 def vmem(count):
     return [pl.BlockSpec(memory_space=pltpu.VMEM)] * count
 
 
+def from_hbm(value):
+    return pltpu.with_memory_space_constraint(value, pltpu.HBM)
+
+
 def unread(count):
     return [pl.BlockSpec(memory_space=pl.ANY)] * count
+
+
+def in_hbm(count):
+    return [pl.BlockSpec(memory_space=pltpu.HBM)] * count
 
 
 def smem(count):
@@ -254,17 +328,6 @@
     def shaped(*shape):
         return jax.ShapeDtypeStruct(shape, bf16)
 
-    device = lax.axis_index("rows")
-    core = lax.axis_index("dist")
-    plane, spot = device // inner, device % inner
-    parity = device % 2
-    info = jnp.concatenate(
-        [
-            angle_order[0],
-            (parity * slab_rows[device - parity])[None],
-            slab_rows[device][None],
-        ]
-    )
     table = jnp.asarray(hartley(width))
 
     def sent(value, target):
@@ -278,11 +341,24 @@
     def to_other_core(c, r):
         return c ^ 1, r
 
-    def to_spot(rel):
-        return lambda c, r: (c, r ^ rel)
-
-    def spread(pieces, order):
-        return [sent(pieces[rel], to_spot(rel)) if rel else pieces[rel] for rel in order]
+    def to_first(c, r):
+        return c, r ^ steps_of(c)[0]
+
+    def to_second(c, r):
+        return c, r ^ steps_of(c)[1]
+
+    def spread(stays, leaves, later):
+        got = sent(leaves, to_first)
+        message = pl.pallas_call(
+            relay_kernel,
+            out_shape=shaped(*leaves.shape),
+            in_specs=vmem(2),
+            out_specs=one_out,
+            compiler_params=params,
+            cost_estimate=cost(1, (8, width)),
+            name="relay",
+        )(later, got)
+        return stays, got, sent(message, to_second)
 
     def to_near_plane(c, r):
         return c, (r // inner ^ 1) * inner + r % inner
@@ -291,55 +367,46 @@
         z = r // inner
         return (c, (3 - z) * inner + r % inner) if z in (1, 2) else (c ^ 1, r)
 
-    index = jnp.arange(width, dtype=jnp.int32)
-    my_cols = spot * block + jnp.arange(block, dtype=jnp.int32)
-    ordered = jnp.concatenate(
-        [
-            lax.dynamic_slice_in_dim(propagation, (core ^ other) * dist_dev, dist_dev, 0)
-            for other in range(cores)
-        ]
-    )
-    first = ordered[:, None] * signed_square(index, width)[None]
-    second = ordered[:, None] * signed_square(my_cols, width)[None]
-    sin_b, cos_b = jnp.sin(second), jnp.cos(second)
+    partner = sent(holograms[0], to_other_core)
     gain, mine = pl.pallas_call(
-        filter_kernel,
-        out_shape=[shaped(dists, width, block), shaped(own, dist_dev, rows_dev, width)],
-        in_specs=vmem(3) + unread(1),
+        lambda *refs: filter_kernel(inner, *refs),
+        out_shape=[
+            shaped(dists, width, block),
+            shaped(own, dist_dev, rows_dev, width),
+        ],
+        in_specs=smem(1) + in_hbm(1),
         out_specs=vmem(2),
         scratch_shapes=[pltpu.SemaphoreType.DMA],
         compiler_params=params,
         cost_estimate=cost(32 * width * block, (dists, width, block)),
         name="filters",
-    )(
-        jnp.concatenate([jnp.sin(first), jnp.cos(first)], axis=0),
-        2.0 * (cos_b - absorb_ratio * sin_b),
-        2.0 * (sin_b + absorb_ratio * cos_b),
-        holograms[0],
-    )
-
-    partner = sent(holograms[0], to_other_core)
+    )(propagation, from_hbm(holograms[0]))
+
     arrived = []
     for chunk in range(own):
         pieces = pl.pallas_call(
             lambda *refs, chunk=chunk: row_kernel(inner, chunk, *refs),
-            out_shape=[shaped(dists, rows_dev, block)] * inner,
+            out_shape=[
+                shaped(dists, rows_dev, block),
+                shaped(2, dists, rows_dev, block),
+                shaped(dists, rows_dev, block),
+            ],
             in_specs=vmem(3) + unread(1),
-            out_specs=vmem(inner),
+            out_specs=vmem(3),
             compiler_params=params,
             cost_estimate=cost(
                 2 * dists * rows_dev * width * width, (width, width), (2, dists, rows_dev, width)
             ),
             name="row_spectra",
         )(mine, partner, table, gain)
-        arrived.append(spread(pieces, send_order))
+        arrived.append(spread(*pieces))
 
     sums = []
     for chunk in range(own):
         away, keep = pl.pallas_call(
             lambda *refs: column_kernel(inner, outer, *refs),
             out_shape=[shaped(outer // 2, depth, block)] * 2,
-            in_specs=vmem(2 + inner),
+            in_specs=vmem(5),
             out_specs=vmem(2),
             scratch_shapes=[
                 pltpu.VMEM((dists, depth, block), bf16),
@@ -362,64 +429,81 @@
             name="joint",
         )(away, sent(away, to_near_plane))
         across = sent(joint, to_middle)
+        last = chunk == own - 1
+        if last:
+            chosen, select = pl.pallas_call(
+                choose_kernel,
+                out_shape=[shaped(angles, width, pixels), shaped(capacity, capacity)],
+                in_specs=smem(2) + in_hbm(1) + unread(1),
+                out_specs=vmem(2),
+                scratch_shapes=[pltpu.SemaphoreType.DMA((angles,))],
+                compiler_params=params,
+                cost_estimate=cost(1, (8, width)),
+                name="choose",
+            )(angle_order, slab_rows, from_hbm(weights), near)
         near = pl.pallas_call(
             lambda *refs: near_kernel(inner, *refs),
             out_shape=shaped(depth, block),
-            in_specs=vmem(2),
+            in_specs=vmem(2) + unread(last),
             out_specs=one_out,
             compiler_params=params,
             cost_estimate=cost(depth * block, (3, depth, block)),
             name="near",
-        )(keep, across)
+        )(keep, across, *([select] if last else []))
         sums.append((keep, across, sent(near, to_near_plane)))
 
     def recon(kernel, out_type, *arrays):
         return pl.pallas_call(
             kernel,
             out_shape=jax.ShapeDtypeStruct((capacity, pixels), out_type),
-            in_specs=smem(1) + vmem(1 + len(arrays)),
+            in_specs=vmem(1 + len(arrays)),
             out_specs=one_out,
             compiler_params=params,
             cost_estimate=cost(1, (8, pixels)),
             name="recon",
-        )(info, weights, *arrays)
+        )(chosen, *arrays)
 
     total = None
     for chunk in range(own):
-        first, second = pl.pallas_call(
+        pieces = pl.pallas_call(
             lambda *refs: half_kernel(inner, *refs),
-            out_shape=[shaped(capacity, block)] * 2,
+            out_shape=[
+                shaped(capacity, block),
+                shaped(2, capacity, block),
+                shaped(capacity, block),
+            ],
             in_specs=vmem(3) + unread(2),
-            out_specs=vmem(2),
+            out_specs=vmem(3),
             compiler_params=params,
             cost_estimate=cost(1, (8, width)),
             name="half",
-        )(*sums[chunk], near, info)
-        pieces = spread([first, first, second, second], tail_order)
+        )(*sums[chunk], near, select)
         phase = pl.pallas_call(
             lambda *refs: phase_kernel(inner, *refs),
             out_shape=shaped(capacity, width),
-            in_specs=vmem(1 + inner),
+            in_specs=vmem(4),
             out_specs=one_out,
             scratch_shapes=[pltpu.VMEM((capacity, width), bf16)],
             compiler_params=params,
             cost_estimate=cost(1, (8, width)),
             name="phase",
-        )(table, *pieces)
+        )(table, *spread(*pieces))
         there = sent(phase, to_other_core)
-        def part(cores, chunk=chunk):
-            return lambda *refs: recon_kernel(own, chunk, cores, *refs)
+
+        def part(*steps):
+            return lambda *refs: recon_kernel(steps, *refs)
 
         before = [] if total is None else [total]
         if chunk < own - 1:
-            total = recon(part((0, 1)), f32, phase, there, *before)
+            total = recon(part(chunk, own + chunk), f32, phase, there, *before)
         else:
-            total = recon(part((0,)), f32, phase, *before)
+            total = recon(part(chunk), f32, phase, *before)
             total = recon(
-                lambda *refs, chunk=chunk: recon_last_kernel(own, chunk, 1, *refs),
+                lambda *refs, chunk=chunk: recon_last_kernel(own + chunk, *refs),
                 bf16,
                 there,
                 total,
+                select,
             )
     return total
 

time: 59.3 us -> 62.9 us (1.061)
  waiting for transfers between devices: 13.3 us -> 22.6 us
  starting transfers between devices: 27.7 us -> 25.1 us
  local copies, waits for them, and re-layouts: 4.28 us -> 2.26 us
  other arithmetic: 1.17 us -> 0 us
  Pallas kernels: 11.6 us -> 12.5 us
  between operations: 0.9 us -> 0.23 us
    ppermute x21 -> x17, waiting for transfers between devices: 13.3 us -> 22.6 us  [sent(): return lax.ppermute(value, ('dist', 'rows'), pairs)]
    pallas_call x1 -> x6, Pallas kernels: 1.83 us -> 5.2 us  [the longest x1 2.76 us: plane_plan(): pl.pallas_call(choose_kernel, out_shape=[shaped(angles, width, pixels), s...]
    ppermute x21 -> x17, starting transfers between devices: 27.7 us -> 25.1 us  [sent(): return lax.ppermute(value, ('dist', 'rows'), pairs)]
    pallas_call x3, Pallas kernels: 3.48 us -> 1.87 us  [recon(): pl.pallas_call(kernel, out_shape=jax.ShapeDtypeStruct((capacity, pixels),...]
    dynamic_slice x2 -> x0, local copies, waits for them, and re-layouts: 1.45 us -> none  [the longest x1 0.8 us: plane_plan(): lax.dynamic_slice_in_dim(propagation, (core ^ other) * dist_dev, dist_dev...]
    pallas_call x2, Pallas kernels: 1.03 us -> 0.15 us  [plane_plan(): pl.pallas_call(lambda *refs: half_kernel(inner, *refs), out_shape=[shaped...]
    concatenate x3 -> x0, other arithmetic: 0.83 us -> none  [the longest x1 0.75 us: plane_plan(): jnp.concatenate([angle_order[0], (parity * slab_rows[device - parity])[No...]
    unnamed x12 -> x10, local copies, waits for them, and re-layouts: 2.83 us -> 2.26 us
  transfers between devices with their start and end apart: 21 -> 17, of which waited for: 9 -> 9; matrix products, arithmetic and copies ran while one was open for 4% -> 0% of each run, Pallas kernels for 16% -> 17%
where the time goes in v9:
time: 62.9 us; the launch traced here: 62.7 us
  starting transfers between devices  25.1 us (40%)
  waiting for transfers between devices  22.6 us (36%)
  Pallas kernels  12.5 us (20%)
  local copies, waits for them, and re-layouts  2.26 us (4%)
    ppermute x17, starting transfers between devices, sent(): return lax.ppermute(value, ('dist', 'rows'), pairs)  25.1 us
    ppermute x17, waiting for transfers between devices, sent(): return lax.ppermute(value, ('dist', 'rows'), pairs)  22.6 us
    pallas_call x1, Pallas kernels, plane_plan(): pl.pallas_call(choose_kernel, out_shape=[shaped(angles, width, pixels), s...  2.76 us
    pallas_call x2, Pallas kernels, plane_plan(): pl.pallas_call(lambda *refs: column_kernel(inner, outer, *refs), out_shap...  2.6 us
    pallas_call x1, Pallas kernels, plane_plan(): pl.pallas_call(lambda *refs: filter_kernel(inner, *refs), out_shape=[shap...  2.38 us
    unnamed x10, local copies, waits for them, and re-layouts  2.26 us
    pallas_call x3, Pallas kernels, recon(): pl.pallas_call(kernel, out_shape=jax.ShapeDtypeStruct((capacity, pixels),...  1.87 us
    pallas_call x2, Pallas kernels, plane_plan(): pl.pallas_call(lambda *refs, chunk=chunk: row_kernel(inner, chunk, *refs)...  1.49 us
  transfers between devices with their start and end apart: 17, of which 9 were waited for; matrix products, arithmetic and copies ran while one was open for 0% of the time, Pallas kernels for 17%

profile of v9, /device:TPU:0, one launch (start us, length us, event | category | flops | bytes accessed | tf_op | source)
XLA Modules:
  0.0 62.7 jit_solution(13726264426453204279)
XLA Ops:
  0.0 0.5 collective-permute-start
  0.5 0.0 copy-start.2
  0.5 0.7 %copy-done.2 = f32[4]{0:T(128)S(1)} copy-done((f32[4]{0:T(128)S(1)}, f32[4]{0:T(128)}, u32[]{:S(2)}) %copy-start.2) | copy-done | bytes 40
  1.1 2.4 %filters.1 = (bf16[4,1024,256]{2,1,0:T(8,128)(2,1)S(1)}, bf16[2,2,64,1024]{3,2,1,0:T(8,128)(2,1)S(1)}) custom-call(f32[4]{0:T(128)S(1)} %copy-done.2, bf16[4,2,64,1024]{3,2,1,0:T(8,128)(2,1)} %bitcast.2), custom_call_target="tpu_custom_call" | custom-call | flops 8388608 | bytes 2097152 | tf_op jit(solution)/shard_map/filters/pallas_call | solution.py:371
  3.5 0.0 collective-permute-done.refs_1_
  3.5 0.0 copy-start
  3.5 1.6 %copy-done = bf16[1024,1024]{1,0:T(8,128)(2,1)S(1)} copy-done((bf16[1024,1024]{1,0:T(8,128)(2,1)S(1)}, bf16[1024,1024]{1,0:T(8,128)(2,1)}, u32[]{:S(2)}) %copy-start) | copy-done | bytes 2097176
  5.1 0.7 %row_spectra.2 = (bf16[4,64,256]{2,1,0:T(8,128)(2,1)S(1)}, bf16[2,4,64,256]{3,2,1,0:T(8,128)(2,1)S(1)}, bf16[4,64,256]{2,1,0:T(8,128)(2,1)S(1)}) custom-call(bf16[2,2,64,1024]{3,2,1,0:T(8,128)(2,1)S(1)} %get-tuple-element.26.refs_0_, bf16[4,2,64,1024]{3,2,1,0:T(8,128)(2,1)S(1)} %collective-permute-done.refs_1_, bf16[1024,1024]{1,0:T(8,128)(2,1)S(1)} %copy-done, ...), custom_call_target="tpu_custom_call" | custom-call | flops 536870912 | bytes 3145728 | tf_op jit(solution)/shard_map/row_spectra/pallas_call | solution.py:387
  5.9 0.0 copy-start.1
  5.9 2.6 %collective-permute-start.1 = (bf16[2,4,64,256]{3,2,1,0:T(8,128)(2,1)S(1)}, bf16[2,4,64,256]{3,2,1,0:T(8,128)(2,1)S(1)}, u32[]{:S(2)}, u32[]{:S(2)}) collective-permute-start(bf16[2,4,64,256]{3,2,1,0:T(8,128)(2,1)S(1)} %get-tuple-element.28), channel_id=1, source_target_pairs={{0,2},{1,3},{2,0},{3,1},{4,6},{5,7},{6,4},{7,5},{8,10},{9,11},{10,... | collective-permute-start | bytes 786440 | tf_op jit(solution)/shard_map/ppermute | solution.py:339
  8.4 0.7 %row_spectra.3 = (bf16[4,64,256]{2,1,0:T(8,128)(2,1)S(1)}, bf16[2,4,64,256]{3,2,1,0:T(8,128)(2,1)S(1)}, bf16[4,64,256]{2,1,0:T(8,128)(2,1)S(1)}) custom-call(bf16[2,2,64,1024]{3,2,1,0:T(8,128)(2,1)S(1)} %get-tuple-element.26.refs_0_, bf16[4,2,64,1024]{3,2,1,0:T(8,128)(2,1)S(1)} %collective-permute-done.refs_1_, bf16[1024,1024]{1,0:T(8,128)(2,1)S(1)} %copy-done, ...), custom_call_target="tpu_custom_call" | custom-call | flops 536870912 | bytes 3145728 | tf_op jit(solution)/shard_map/row_spectra/pallas_call | solution.py:387
  9.2 0.1 collective-permute-start.5
  9.3 3.5 %collective-permute-done.1.got.refs_3_ = bf16[2,4,64,256]{3,2,1,0:T(8,128)(2,1)S(1)} collective-permute-done((bf16[2,4,64,256]{3,2,1,0:T(8,128)(2,1)S(1)}, bf16[2,4,64,256]{3,2,1,0:T(8,128)(2,1)S(1)}, u32[]{:S(2)}, u32[]{:S(2)}) %collective-permute-start.1) | collective-permute-done | bytes 262176 | tf_op jit(solution)/shard_map/ppermute | solution.py:339
  12.8 2.1 %collective-permute-start.2 = (bf16[2,4,64,256]{3,2,1,0:T(8,128)(2,1)S(1)}, bf16[2,4,64,256]{3,2,1,0:T(8,128)(2,1)S(1)}, u32[]{:S(2)}, u32[]{:S(2)}) collective-permute-start(bf16[2,4,64,256]{3,2,1,0:T(8,128)(2,1)S(1)} %relay.4), channel_id=1, source_target_pairs={{0,1},{1,0},{2,3},{3,2},{4,5},{5,4},{6,7},{7,6},{8,9},{9,8},{10,11... | collective-permute-start | bytes 786440 | tf_op jit(solution)/shard_map/ppermute | solution.py:339
  14.9 0.9 %collective-permute-done.5.got.refs_3_ = bf16[2,4,64,256]{3,2,1,0:T(8,128)(2,1)S(1)} collective-permute-done((bf16[2,4,64,256]{3,2,1,0:T(8,128)(2,1)S(1)}, bf16[2,4,64,256]{3,2,1,0:T(8,128)(2,1)S(1)}, u32[]{:S(2)}, u32[]{:S(2)}) %collective-permute-start.5) | collective-permute-done | bytes 262176 | tf_op jit(solution)/shard_map/ppermute | solution.py:339
  15.8 2.3 %collective-permute-start.6 = (bf16[2,4,64,256]{3,2,1,0:T(8,128)(2,1)S(1)}, bf16[2,4,64,256]{3,2,1,0:T(8,128)(2,1)S(1)}, u32[]{:S(2)}, u32[]{:S(2)}) collective-permute-start(bf16[2,4,64,256]{3,2,1,0:T(8,128)(2,1)S(1)} %relay.5), channel_id=1, source_target_pairs={{0,1},{1,0},{2,3},{3,2},{4,5},{5,4},{6,7},{7,6},{8,9},{9,8},{10,11... | collective-permute-start | bytes 786440 | tf_op jit(solution)/shard_map/ppermute | solution.py:339
  18.1 1.2 %collective-permute-done.2.refs_4_ = bf16[2,4,64,256]{3,2,1,0:T(8,128)(2,1)S(1)} collective-permute-done((bf16[2,4,64,256]{3,2,1,0:T(8,128)(2,1)S(1)}, bf16[2,4,64,256]{3,2,1,0:T(8,128)(2,1)S(1)}, u32[]{:S(2)}, u32[]{:S(2)}) %collective-permute-start.2) | collective-permute-done | bytes 262176 | tf_op jit(solution)/shard_map/ppermute | solution.py:339
  19.3 0.0 copy-done.1
  19.3 1.3 %columns.2 = (bf16[2,256,256]{2,1,0:T(8,128)(2,1)S(1)}, bf16[2,256,256]{2,1,0:T(8,128)(2,1)S(1)}) custom-call(bf16[1024,1024]{1,0:T(8,128)(2,1)S(1)} %copy-done.1, bf16[4,1024,256]{2,1,0:T(8,128)(2,1)S(1)} %get-tuple-element.25.refs_3_.refs_1_, bf16[4,64,256]{2,1,0:T(8,128)(2,1)S(1)} %get-tuple-element.27.refs_2_, ...), custom_call_target="tpu_custom_call" | custom-call | flops 1073741824 | bytes 4194304 | tf_op jit(solution)/shard_map/columns/pallas_call | solution.py:406
  20.6 0.0 copy-start.3
  20.6 0.0 copy-start.4
  20.6 2.2 %collective-permute-start.3 = (bf16[2,256,256]{2,1,0:T(8,128)(2,1)S(1)}, bf16[2,256,256]{2,1,0:T(8,128)(2,1)S(1)}, u32[]{:S(2)}, u32[]{:S(2)}) collective-permute-start(bf16[2,256,256]{2,1,0:T(8,128)(2,1)S(1)} %get-tuple-element.31.one), channel_id=1, source_target_pairs={{0,4},{1,5},{2,6},{3,7},{4,0},{5,1},{6,2},{7,3},{8,12},{9,13},{10,... | collective-permute-start | bytes 786440 | tf_op jit(solution)/shard_map/ppermute | solution.py:339
  22.7 0.0 collective-permute-done.6.refs_4_
  22.7 1.3 %columns.3 = (bf16[2,256,256]{2,1,0:T(8,128)(2,1)S(1)}, bf16[2,256,256]{2,1,0:T(8,128)(2,1)S(1)}) custom-call(bf16[1024,1024]{1,0:T(8,128)(2,1)S(1)} %copy-done.1, bf16[4,1024,256]{2,1,0:T(8,128)(2,1)S(1)} %get-tuple-element.25.refs_3_.refs_1_, bf16[4,64,256]{2,1,0:T(8,128)(2,1)S(1)} %get-tuple-element.33.refs_2_, ...), custom_call_target="tpu_custom_call" | custom-call | flops 1073741824 | bytes 4194304 | tf_op jit(solution)/shard_map/columns/pallas_call | solution.py:406
  24.1 1.9 %collective-permute-start.7 = (bf16[2,256,256]{2,1,0:T(8,128)(2,1)S(1)}, bf16[2,256,256]{2,1,0:T(8,128)(2,1)S(1)}, u32[]{:S(2)}, u32[]{:S(2)}) collective-permute-start(bf16[2,256,256]{2,1,0:T(8,128)(2,1)S(1)} %get-tuple-element.37.one), channel_id=1, source_target_pairs={{0,4},{1,5},{2,6},{3,7},{4,0},{5,1},{6,2},{7,3},{8,12},{9,13},{10,... | collective-permute-start | bytes 786440 | tf_op jit(solution)/shard_map/ppermute | solution.py:339
  25.9 4.0 %collective-permute-done.3.two = bf16[2,256,256]{2,1,0:T(8,128)(2,1)S(1)} collective-permute-done((bf16[2,256,256]{2,1,0:T(8,128)(2,1)S(1)}, bf16[2,256,256]{2,1,0:T(8,128)(2,1)S(1)}, u32[]{:S(2)}, u32[]{:S(2)}) %collective-permute-start.3) | collective-permute-done | bytes 262176 | tf_op jit(solution)/shard_map/ppermute | solution.py:339
  30.0 0.1 joint.2
  30.0 0.1 collective-permute-start.4
  30.1 4.0 %collective-permute-done.7.two = bf16[2,256,256]{2,1,0:T(8,128)(2,1)S(1)} collective-permute-done((bf16[2,256,256]{2,1,0:T(8,128)(2,1)S(1)}, bf16[2,256,256]{2,1,0:T(8,128)(2,1)S(1)}, u32[]{:S(2)}, u32[]{:S(2)}) %collective-permute-start.7) | collective-permute-done | bytes 262176 | tf_op jit(solution)/shard_map/ppermute | solution.py:339
  34.1 0.1 joint.3
  34.2 0.1 collective-permute-start.8
  34.3 0.0 collective-permute-done.4.refs_1_
  34.3 0.1 near.2.after
  34.3 5.8 %collective-permute-start.13 = (bf16[256,256]{1,0:T(8,128)(2,1)S(1)}, bf16[256,256]{1,0:T(8,128)(2,1)S(1)}, u32[]{:S(2)}, u32[]{:S(2)}) collective-permute-start(bf16[256,256]{1,0:T(8,128)(2,1)S(1)} %near.2.after), channel_id=1, source_target_pairs={{0,4},{1,5},{2,6},{3,7},{4,0},{5,1},{6,2},{7,3},{8,12},{9,13},{10,... | collective-permute-start | bytes 393224 | tf_op jit(solution)/shard_map/ppermute | solution.py:339
  40.1 0.0 copy-done.3
  40.1 0.0 copy-done.4
  40.1 2.8 %choose.1 = (bf16[4,1024,512]{2,1,0:T(8,128)(2,1)S(1)}, bf16[128,128]{1,0:T(8,128)(2,1)S(1)}) custom-call(s32[1,4]{1,0:T(1,128)S(1)} %copy-done.3, s32[16]{0:T(128)S(1)} %copy-done.4, bf16[4,1024,512]{2,1,0:T(8,128)(2,1)} %weights.1, bf16[256,256]{1,0:T(8,128)(2,1)S(1)} %near.2.after), custom_call_target="tpu_custom_call" | custom-call | flops 1 | bytes 16384 | tf_op jit(solution)/shard_map/choose/pallas_call | solution.py:434
  42.9 0.0 collective-permute-done.8.refs_1_
  42.9 0.1 near.3.refs_3_
  43.0 1.2 %collective-permute-start.9 = (bf16[256,256]{1,0:T(8,128)(2,1)S(1)}, bf16[256,256]{1,0:T(8,128)(2,1)S(1)}, u32[]{:S(2)}, u32[]{:S(2)}) collective-permute-start(bf16[256,256]{1,0:T(8,128)(2,1)S(1)} %near.3.refs_3_), channel_id=1, source_target_pairs={{0,4},{1,5},{2,6},{3,7},{4,0},{5,1},{6,2},{7,3},{8,12},{9,13},{10,... | collective-permute-start | bytes 393224 | tf_op jit(solution)/shard_map/ppermute | solution.py:339
  44.2 0.0 collective-permute-done.13.refs_2_
  44.2 0.1 half.3
  44.3 1.6 %collective-permute-start.14 = (bf16[2,128,256]{2,1,0:T(8,128)(2,1)S(1)}, bf16[2,128,256]{2,1,0:T(8,128)(2,1)S(1)}, u32[]{:S(2)}, u32[]{:S(2)}) collective-permute-start(bf16[2,128,256]{2,1,0:T(8,128)(2,1)S(1)} %get-tuple-element.43), channel_id=1, source_target_pairs={{0,2},{1,3},{2,0},{3,1},{4,6},{5,7},{6,4},{7,5},{8,10},{9,11},{10,... | collective-permute-start | bytes 393224 | tf_op jit(solution)/shard_map/ppermute | solution.py:339
  45.9 2.1 %collective-permute-done.9.refs_2_ = bf16[256,256]{1,0:T(8,128)(2,1)S(1)} collective-permute-done((bf16[256,256]{1,0:T(8,128)(2,1)S(1)}, bf16[256,256]{1,0:T(8,128)(2,1)S(1)}, u32[]{:S(2)}, u32[]{:S(2)}) %collective-permute-start.9) | collective-permute-done | bytes 131104 | tf_op jit(solution)/shard_map/ppermute | solution.py:339
  48.0 0.1 half.2
  48.1 1.6 %collective-permute-start.10 = (bf16[2,128,256]{2,1,0:T(8,128)(2,1)S(1)}, bf16[2,128,256]{2,1,0:T(8,128)(2,1)S(1)}, u32[]{:S(2)}, u32[]{:S(2)}) collective-permute-start(bf16[2,128,256]{2,1,0:T(8,128)(2,1)S(1)} %get-tuple-element.40), channel_id=1, source_target_pairs={{0,2},{1,3},{2,0},{3,1},{4,6},{5,7},{6,4},{7,5},{8,10},{9,11},{10,... | collective-permute-start | bytes 393224 | tf_op jit(solution)/shard_map/ppermute | solution.py:339
  49.7 0.0 collective-permute-done.14.got.refs_2_
  49.7 1.6 %collective-permute-start.15 = (bf16[2,128,256]{2,1,0:T(8,128)(2,1)S(1)}, bf16[2,128,256]{2,1,0:T(8,128)(2,1)S(1)}, u32[]{:S(2)}, u32[]{:S(2)}) collective-permute-start(bf16[2,128,256]{2,1,0:T(8,128)(2,1)S(1)} %relay.7), channel_id=1, source_target_pairs={{0,1},{1,0},{2,3},{3,2},{4,5},{5,4},{6,7},{7,6},{8,9},{9,8},{10,11... | collective-permute-start | bytes 393224 | tf_op jit(solution)/shard_map/ppermute | solution.py:339
  51.3 3.2 %collective-permute-done.10.got.refs_2_ = bf16[2,128,256]{2,1,0:T(8,128)(2,1)S(1)} collective-permute-done((bf16[2,128,256]{2,1,0:T(8,128)(2,1)S(1)}, bf16[2,128,256]{2,1,0:T(8,128)(2,1)S(1)}, u32[]{:S(2)}, u32[]{:S(2)}) %collective-permute-start.10) | collective-permute-done | bytes 131104 | tf_op jit(solution)/shard_map/ppermute | solution.py:339
  54.5 1.6 %collective-permute-start.11 = (bf16[2,128,256]{2,1,0:T(8,128)(2,1)S(1)}, bf16[2,128,256]{2,1,0:T(8,128)(2,1)S(1)}, u32[]{:S(2)}, u32[]{:S(2)}) collective-permute-start(bf16[2,128,256]{2,1,0:T(8,128)(2,1)S(1)} %relay.6), channel_id=1, source_target_pairs={{0,1},{1,0},{2,3},{3,2},{4,5},{5,4},{6,7},{7,6},{8,9},{9,8},{10,11... | collective-permute-start | bytes 393224 | tf_op jit(solution)/shard_map/ppermute | solution.py:339
  56.0 0.0 collective-permute-done.15.refs_3_
  56.1 0.5 phase.3.refs_1_
  56.5 0.1 collective-permute-start.16
  56.6 2.9 %collective-permute-done.11.refs_3_ = bf16[2,128,256]{2,1,0:T(8,128)(2,1)S(1)} collective-permute-done((bf16[2,128,256]{2,1,0:T(8,128)(2,1)S(1)}, bf16[2,128,256]{2,1,0:T(8,128)(2,1)S(1)}, u32[]{:S(2)}, u32[]{:S(2)}) %collective-permute-start.11) | collective-permute-done | bytes 131104 | tf_op jit(solution)/shard_map/ppermute | solution.py:339
  59.5 0.5 phase.2.refs_1_
  60.0 0.1 collective-permute-start.12
  60.1 0.0 collective-permute-done.16.refs_2_
  60.1 0.4 recon.3.refs_2_
  60.5 0.3 recon.4.refs_2_
  60.8 0.7 %collective-permute-done.12.refs_1_ = bf16[128,1024]{1,0:T(8,128)(2,1)S(1)} collective-permute-done((bf16[128,1024]{1,0:T(8,128)(2,1)S(1)}, bf16[128,1024]{1,0:T(8,128)(2,1)S(1)}, u32[]{:S(2)}, u32[]{:S(2)}) %collective-permute-start.12) | collective-permute-done | bytes 262176 | tf_op jit(solution)/shard_map/ppermute | solution.py:339
  61.6 1.1 %recon.5 = bf16[128,512]{1,0:T(8,128)(2,1)} custom-call(bf16[4,1024,512]{2,1,0:T(8,128)(2,1)S(1)} %get-tuple-element.32.refs_0_, bf16[128,1024]{1,0:T(8,128)(2,1)S(1)} %collective-permute-done.12.refs_1_, f32[128,512]{1,0:T(8,128)S(1)} %recon.4.refs_2_, bf16[128,128]{1,0:T(8,128)(2,1)S(1)} %get-tuple-element.38.refs_2_.refs_4_.refs_3_), custom_call_target="tpu_custom_call" | custom-call | flops 1 | bytes 8192 | tf_op jit(solution)/shard_map/recon/pallas_call | solution.py:456
  (4 shorter events, 0.1 us)
Async XLA Ops:
  0.0 3.5 %collective-permute-start = (bf16[4,2,64,1024]{3,2,1,0:T(8,128)(2,1)}, bf16[4,2,64,1024]{3,2,1,0:T(8,128)(2,1)S(1)}, u32[]{:S(2)}, u32[]{:S(2)}) collective-permute-start(bf16[4,2,64,1024]{3,2,1,0:T(8,128)(2,1)} %bitcast.1), channel_id=1, source_target_pairs={{0,16},{1,17},{2,18},{3,19},{4,20},{5,21},{6,22},{7,23},{8,24},{9,... | collective-permute-start | bytes 3145736 | tf_op jit(solution)/shard_map/ppermute | solution.py:339
  0.5 0.7 %copy-start.2 = (f32[4]{0:T(128)S(1)}, f32[4]{0:T(128)}, u32[]{:S(2)}) copy-start(f32[4]{0:T(128)} %refs_0_.5) | copy-start | bytes 52
  3.5 1.6 %copy-start = (bf16[1024,1024]{1,0:T(8,128)(2,1)S(1)}, bf16[1024,1024]{1,0:T(8,128)(2,1)}, u32[]{:S(2)}) copy-start(bf16[1024,1024]{1,0:T(8,128)(2,1)} %constant.2.clone.refs_2_.refs_0_) | copy-start | bytes 6291460
  5.9 13.4 %copy-start.1 = (bf16[1024,1024]{1,0:T(8,128)(2,1)S(1)}, bf16[1024,1024]{1,0:T(8,128)(2,1)}, u32[]{:S(2)}) copy-start(bf16[1024,1024]{1,0:T(8,128)(2,1)} %constant.2.clone.refs_2_.refs_0_) | copy-start | bytes 6291460
  5.9 6.9 %collective-permute-start.1 = (bf16[2,4,64,256]{3,2,1,0:T(8,128)(2,1)S(1)}, bf16[2,4,64,256]{3,2,1,0:T(8,128)(2,1)S(1)}, u32[]{:S(2)}, u32[]{:S(2)}) collective-permute-start(bf16[2,4,64,256]{3,2,1,0:T(8,128)(2,1)S(1)} %get-tuple-element.28), channel_id=1, source_target_pairs={{0,2},{1,3},{2,0},{3,1},{4,6},{5,7},{6,4},{7,5},{8,10},{9,11},{10,... | collective-permute-start | bytes 786440 | tf_op jit(solution)/shard_map/ppermute | solution.py:339
  9.2 6.6 %collective-permute-start.5 = (bf16[2,4,64,256]{3,2,1,0:T(8,128)(2,1)S(1)}, bf16[2,4,64,256]{3,2,1,0:T(8,128)(2,1)S(1)}, u32[]{:S(2)}, u32[]{:S(2)}) collective-permute-start(bf16[2,4,64,256]{3,2,1,0:T(8,128)(2,1)S(1)} %get-tuple-element.34), channel_id=1, source_target_pairs={{0,2},{1,3},{2,0},{3,1},{4,6},{5,7},{6,4},{7,5},{8,10},{9,11},{10,... | collective-permute-start | bytes 786440 | tf_op jit(solution)/shard_map/ppermute | solution.py:339
  12.8 6.4 %collective-permute-start.2 = (bf16[2,4,64,256]{3,2,1,0:T(8,128)(2,1)S(1)}, bf16[2,4,64,256]{3,2,1,0:T(8,128)(2,1)S(1)}, u32[]{:S(2)}, u32[]{:S(2)}) collective-permute-start(bf16[2,4,64,256]{3,2,1,0:T(8,128)(2,1)S(1)} %relay.4), channel_id=1, source_target_pairs={{0,1},{1,0},{2,3},{3,2},{4,5},{5,4},{6,7},{7,6},{8,9},{9,8},{10,11... | collective-permute-start | bytes 786440 | tf_op jit(solution)/shard_map/ppermute | solution.py:339
  15.8 6.9 %collective-permute-start.6 = (bf16[2,4,64,256]{3,2,1,0:T(8,128)(2,1)S(1)}, bf16[2,4,64,256]{3,2,1,0:T(8,128)(2,1)S(1)}, u32[]{:S(2)}, u32[]{:S(2)}) collective-permute-start(bf16[2,4,64,256]{3,2,1,0:T(8,128)(2,1)S(1)} %relay.5), channel_id=1, source_target_pairs={{0,1},{1,0},{2,3},{3,2},{4,5},{5,4},{6,7},{7,6},{8,9},{9,8},{10,11... | collective-permute-start | bytes 786440 | tf_op jit(solution)/shard_map/ppermute | solution.py:339
  20.6 19.6 %copy-start.3 = (s32[1,4]{1,0:T(1,128)S(1)}, s32[1,4]{1,0:T(1,128)}, u32[]{:S(2)}) copy-start(s32[1,4]{1,0:T(1,128)} %order.1) | copy-start | bytes 52
  20.6 19.6 %copy-start.4 = (s32[16]{0:T(128)S(1)}, s32[16]{0:T(128)}, u32[]{:S(2)}) copy-start(s32[16]{0:T(128)} %slabs.1) | copy-start | bytes 196
  20.6 9.4 %collective-permute-start.3 = (bf16[2,256,256]{2,1,0:T(8,128)(2,1)S(1)}, bf16[2,256,256]{2,1,0:T(8,128)(2,1)S(1)}, u32[]{:S(2)}, u32[]{:S(2)}) collective-permute-start(bf16[2,256,256]{2,1,0:T(8,128)(2,1)S(1)} %get-tuple-element.31.one), channel_id=1, source_target_pairs={{0,4},{1,5},{2,6},{3,7},{4,0},{5,1},{6,2},{7,3},{8,12},{9,13},{10,... | collective-permute-start | bytes 786440 | tf_op jit(solution)/shard_map/ppermute | solution.py:339
  24.1 10.0 %collective-permute-start.7 = (bf16[2,256,256]{2,1,0:T(8,128)(2,1)S(1)}, bf16[2,256,256]{2,1,0:T(8,128)(2,1)S(1)}, u32[]{:S(2)}, u32[]{:S(2)}) collective-permute-start(bf16[2,256,256]{2,1,0:T(8,128)(2,1)S(1)} %get-tuple-element.37.one), channel_id=1, source_target_pairs={{0,4},{1,5},{2,6},{3,7},{4,0},{5,1},{6,2},{7,3},{8,12},{9,13},{10,... | collective-permute-start | bytes 786440 | tf_op jit(solution)/shard_map/ppermute | solution.py:339
  30.0 4.2 %collective-permute-start.4 = (bf16[2,256,256]{2,1,0:T(8,128)(2,1)S(1)}, bf16[2,256,256]{2,1,0:T(8,128)(2,1)S(1)}, u32[]{:S(2)}, u32[]{:S(2)}) collective-permute-start(bf16[2,256,256]{2,1,0:T(8,128)(2,1)S(1)} %joint.2), channel_id=1, source_target_pairs={{0,16},{1,17},{2,18},{3,19},{4,8},{5,9},{6,10},{7,11},{8,4},{9,5},... | collective-permute-start | bytes 786440 | tf_op jit(solution)/shard_map/ppermute | solution.py:339
  34.2 8.7 %collective-permute-start.8 = (bf16[2,256,256]{2,1,0:T(8,128)(2,1)S(1)}, bf16[2,256,256]{2,1,0:T(8,128)(2,1)S(1)}, u32[]{:S(2)}, u32[]{:S(2)}) collective-permute-start(bf16[2,256,256]{2,1,0:T(8,128)(2,1)S(1)} %joint.3), channel_id=1, source_target_pairs={{0,16},{1,17},{2,18},{3,19},{4,8},{5,9},{6,10},{7,11},{8,4},{9,5},... | collective-permute-start | bytes 786440 | tf_op jit(solution)/shard_map/ppermute | solution.py:339
  34.3 9.9 %collective-permute-start.13 = (bf16[256,256]{1,0:T(8,128)(2,1)S(1)}, bf16[256,256]{1,0:T(8,128)(2,1)S(1)}, u32[]{:S(2)}, u32[]{:S(2)}) collective-permute-start(bf16[256,256]{1,0:T(8,128)(2,1)S(1)} %near.2.after), channel_id=1, source_target_pairs={{0,4},{1,5},{2,6},{3,7},{4,0},{5,1},{6,2},{7,3},{8,12},{9,13},{10,... | collective-permute-start | bytes 393224 | tf_op jit(solution)/shard_map/ppermute | solution.py:339
  43.0 5.0 %collective-permute-start.9 = (bf16[256,256]{1,0:T(8,128)(2,1)S(1)}, bf16[256,256]{1,0:T(8,128)(2,1)S(1)}, u32[]{:S(2)}, u32[]{:S(2)}) collective-permute-start(bf16[256,256]{1,0:T(8,128)(2,1)S(1)} %near.3.refs_3_), channel_id=1, source_target_pairs={{0,4},{1,5},{2,6},{3,7},{4,0},{5,1},{6,2},{7,3},{8,12},{9,13},{10,... | collective-permute-start | bytes 393224 | tf_op jit(solution)/shard_map/ppermute | solution.py:339
  44.3 5.4 %collective-permute-start.14 = (bf16[2,128,256]{2,1,0:T(8,128)(2,1)S(1)}, bf16[2,128,256]{2,1,0:T(8,128)(2,1)S(1)}, u32[]{:S(2)}, u32[]{:S(2)}) collective-permute-start(bf16[2,128,256]{2,1,0:T(8,128)(2,1)S(1)} %get-tuple-element.43), channel_id=1, source_target_pairs={{0,2},{1,3},{2,0},{3,1},{4,6},{5,7},{6,4},{7,5},{8,10},{9,11},{10,... | collective-permute-start | bytes 393224 | tf_op jit(solution)/shard_map/ppermute | solution.py:339
  48.1 6.4 %collective-permute-start.10 = (bf16[2,128,256]{2,1,0:T(8,128)(2,1)S(1)}, bf16[2,128,256]{2,1,0:T(8,128)(2,1)S(1)}, u32[]{:S(2)}, u32[]{:S(2)}) collective-permute-start(bf16[2,128,256]{2,1,0:T(8,128)(2,1)S(1)} %get-tuple-element.40), channel_id=1, source_target_pairs={{0,2},{1,3},{2,0},{3,1},{4,6},{5,7},{6,4},{7,5},{8,10},{9,11},{10,... | collective-permute-start | bytes 393224 | tf_op jit(solution)/shard_map/ppermute | solution.py:339
  49.7 6.4 %collective-permute-start.15 = (bf16[2,128,256]{2,1,0:T(8,128)(2,1)S(1)}, bf16[2,128,256]{2,1,0:T(8,128)(2,1)S(1)}, u32[]{:S(2)}, u32[]{:S(2)}) collective-permute-start(bf16[2,128,256]{2,1,0:T(8,128)(2,1)S(1)} %relay.7), channel_id=1, source_target_pairs={{0,1},{1,0},{2,3},{3,2},{4,5},{5,4},{6,7},{7,6},{8,9},{9,8},{10,11... | collective-permute-start | bytes 393224 | tf_op jit(solution)/shard_map/ppermute | solution.py:339
  54.5 5.0 %collective-permute-start.11 = (bf16[2,128,256]{2,1,0:T(8,128)(2,1)S(1)}, bf16[2,128,256]{2,1,0:T(8,128)(2,1)S(1)}, u32[]{:S(2)}, u32[]{:S(2)}) collective-permute-start(bf16[2,128,256]{2,1,0:T(8,128)(2,1)S(1)} %relay.6), channel_id=1, source_target_pairs={{0,1},{1,0},{2,3},{3,2},{4,5},{5,4},{6,7},{7,6},{8,9},{9,8},{10,11... | collective-permute-start | bytes 393224 | tf_op jit(solution)/shard_map/ppermute | solution.py:339
  56.5 3.6 %collective-permute-start.16 = (bf16[128,1024]{1,0:T(8,128)(2,1)S(1)}, bf16[128,1024]{1,0:T(8,128)(2,1)S(1)}, u32[]{:S(2)}, u32[]{:S(2)}) collective-permute-start(bf16[128,1024]{1,0:T(8,128)(2,1)S(1)} %phase.3.refs_1_), channel_id=1, source_target_pairs={{0,16},{1,17},{2,18},{3,19},{4,20},{5,21},{6,22},{7,23},{8,24},{9,... | collective-permute-start | bytes 786440 | tf_op jit(solution)/shard_map/ppermute | solution.py:339
  60.0 1.6 %collective-permute-start.12 = (bf16[128,1024]{1,0:T(8,128)(2,1)S(1)}, bf16[128,1024]{1,0:T(8,128)(2,1)S(1)}, u32[]{:S(2)}, u32[]{:S(2)}) collective-permute-start(bf16[128,1024]{1,0:T(8,128)(2,1)S(1)} %phase.2.refs_1_), channel_id=1, source_target_pairs={{0,16},{1,17},{2,18},{3,19},{4,20},{5,21},{6,22},{7,23},{8,24},{9,... | collective-permute-start | bytes 786440 | tf_op jit(solution)/shard_map/ppermute | solution.py:339

commit v10 on v8

--- a/solution.py
+++ b/solution.py
@@ -12,7 +12,7 @@
 regularizer = 0.05
 bf16 = jnp.bfloat16
 f32 = jnp.float32
-send_order = (0, 2, 3, 1)
+send_order = (0, 1, 2, 3)
 tail_order = (0, 1, 3, 2)
 
 
@@ -98,7 +98,15 @@
     return lax.axis_index("dist"), device // inner, device % inner
 
 
-def row_kernel(inner, chunk, here, there, table, after, *outs):
+def take_kernel(holo, after, out, arrived):
+    own = out.shape[0]
+    core = lax.axis_index("dist")
+    copy = pltpu.make_async_copy(holo.at[pl.ds(core * own, own)], out, arrived)
+    copy.start()
+    copy.wait()
+
+
+def row_kernel(inner, chunk, here, there, table, *outs):
     core, _, spot = position(inner)
     own, dist_dev, rows_dev, width = here.shape
     block = width // inner
@@ -112,13 +120,35 @@
         outs[rel][...] = got.reshape(2 * dist_dev, rows_dev, block)
 
 
-def filter_kernel(waves_a, with_sin, with_cos, holo, out, mine, arrived):
+def whole_turns(scale, square):
+    turns = scale * square * (0.5 / math.pi)
+    return (turns - jnp.round(turns)) * (2.0 * math.pi)
+
+
+def filter_kernel(inner, dist_dev, propagation, after, out):
     dists, width, block = out.shape
-    own = mine.shape[0]
-    core = lax.axis_index("dist")
-    copy = pltpu.make_async_copy(holo.at[pl.ds(core * own, own)], mine, arrived)
-    copy.start()
-    turned = waves_a[...].T
+    core, _, spot = position(inner)
+
+    def square(first, length):
+        index = lax.broadcasted_iota(jnp.int32, (1, length), 1) + first
+        signed = jnp.where(index < width // 2, index, index - width).astype(f32)
+        return signed * signed * (1.0 / (width * width))
+
+    def phases(first, length):
+        values = square(first, length)
+        rows = []
+        for d in range(dists):
+            other = d // dist_dev
+            scale = propagation[(core ^ other) * dist_dev + d % dist_dev]
+            rows.append(whole_turns(scale, values))
+        return jnp.concatenate(rows, axis=0)
+
+    along = phases(0, width)
+    across = phases(spot * block, block)
+    sin_b, cos_b = jnp.sin(across), jnp.cos(across)
+    with_sin = 2.0 * (cos_b - absorb_ratio * sin_b)
+    with_cos = 2.0 * (sin_b + absorb_ratio * cos_b)
+    turned = jnp.concatenate([jnp.sin(along), jnp.cos(along)], axis=0).T
     step = 128
     for at in range(0, width, step):
         rows = turned[at : at + step]
@@ -133,12 +163,12 @@
         scale = 1.0 / (denom + regularizer)
         for d in range(dists):
             out[d, at : at + step, :] = (transfer[d] * scale).astype(bf16)
-    copy.wait()
 
 
 def column_kernel(inner, outer, table, gain, *refs):
     pieces = dict(zip(send_order, refs[:inner]))
-    away, keep, stack, total, spectrum = refs[inner:]
+    keep, *away = refs[inner:-3]
+    stack, total, spectrum = refs[-3:]
     _, plane, spot = position(inner)
     dists, rows_dev, block = pieces[0].shape
     depth = inner * rows_dev
@@ -156,35 +186,50 @@
     spectrum[...] = total[...].astype(bf16)
     half = outer // 2
     side = plane // half
-    for out, first in ((away, (1 - side) * half), (keep, side * half)):
-        rows = pl.ds(pl.multiple_of(first * depth, half * depth), half * depth)
-        got = jnp.dot(table[rows, :], spectrum[...], preferred_element_type=f32)
-        out[...] = got.astype(bf16).reshape(half, depth, block)
+
+    def rows_from(low):
+        rows = pl.ds(pl.multiple_of(low * depth, half * depth), half * depth)
+        value = jnp.dot(table[rows, :], spectrum[...], preferred_element_type=f32)
+        return value.astype(bf16).reshape(half, depth, block)
+
+    value = rows_from((1 - side) * half)
+    wide = block // len(away)
+    for split, out in enumerate(away):
+        out[...] = value[:, :, split * wide : (split + 1) * wide]
+    keep[...] = rows_from(side * half)
 
 
 def add_kernel(one, two, out):
     out[...] = (one[...].astype(f32) + two[...].astype(f32)).astype(bf16)
 
 
-def near_kernel(inner, keep, across, out):
+def near_kernel(inner, split, keep, across, out):
     _, plane, _ = position(inner)
     which = (plane ^ 1) % 2
     inside = (plane == 1) | (plane == 2)
     more = jnp.where(inside, across[which].astype(f32), 0.0)
-    out[...] = (keep[which].astype(f32) + more).astype(bf16)
-
-
-def half_kernel(inner, keep, across, last, *refs):
+    wide = out.shape[1]
+    here = keep[which, :, split * wide : (split + 1) * wide].astype(f32)
+    out[...] = (here + more).astype(bf16)
+
+
+def half_kernel(inner, keep, *refs):
     mine, other = refs[-2:]
+    parts = refs[:-2]
+    splits = len(parts) // 2
     _, plane, spot = position(inner)
     which = plane % 2
     inside = (plane == 1) | (plane == 2)
     capacity = mine.shape[0]
-    for out, pair in ((mine, spot // 2), (other, 1 - spot // 2)):
-        rows = pl.ds(pl.multiple_of(pair * capacity, capacity), capacity)
-        more = jnp.where(inside, across[which, rows, :].astype(f32), 0.0)
-        got = keep[which, rows, :].astype(f32) + more + last[rows, :].astype(f32)
-        out[...] = got.astype(bf16)
+    wide = mine.shape[1] // splits
+    for split in range(splits):
+        across, last = parts[2 * split : 2 * split + 2]
+        lanes = slice(split * wide, (split + 1) * wide)
+        for out, pair in ((mine, spot // 2), (other, 1 - spot // 2)):
+            rows = pl.ds(pl.multiple_of(pair * capacity, capacity), capacity)
+            more = jnp.where(inside, across[which, rows, :].astype(f32), 0.0)
+            got = keep[which, rows, lanes].astype(f32) + more + last[rows, :].astype(f32)
+            out[:, lanes] = got.astype(bf16)
 
 
 def phase_kernel(inner, table, *refs):
@@ -198,30 +243,47 @@
     out[...] = jnp.dot(joined[...], table[...], preferred_element_type=f32).astype(bf16)
 
 
-def recon_kernel(own, chunk, cores, info, weights, *refs):
+def recon_kernel(own, chunk, cores, order, weights, *refs):
     core = lax.axis_index("dist")
     phases, out = refs[: len(cores)], refs[-1]
-    total = refs[-2][...] if len(refs) > len(cores) + 1 else None
+    total = None
     for other, phase in zip(cores, phases):
-        chosen = weights[info[(core ^ other) * own + chunk]]
+        chosen = weights[order[0, (core ^ other) * own + chunk]]
         got = jnp.dot(phase[...], chosen, preferred_element_type=f32)
         total = got if total is None else total + got
     out[...] = total
 
 
-def recon_last_kernel(own, chunk, other, info, weights, phase, before, out):
+def recon_next_kernel(own, chunk, order, slabs, weights, phase, before, out, chosen, select):
     core = lax.axis_index("dist")
-    chosen = weights[info[(core ^ other) * own + chunk]]
-    total = before[...] + jnp.dot(phase[...], chosen, preferred_element_type=f32)
-    capacity = total.shape[0]
-    offset, count = info[weights.shape[0]], info[weights.shape[0] + 1]
-    turned = pltpu.roll(total, lax.rem(capacity - offset, capacity), 0)
-    slot = lax.broadcasted_iota(jnp.int32, turned.shape, 0)
-    out[...] = jnp.where(slot < count, turned, 0.0).astype(bf16)
+    device = lax.axis_index("rows")
+    here = weights[order[0, core * own + chunk]]
+    out[...] = before[...] + jnp.dot(phase[...], here, preferred_element_type=f32)
+    chosen[...] = weights[order[0, (core ^ 1) * own + chunk]]
+    parity = device % 2
+    offset = parity * slabs[device - parity]
+    slot = lax.broadcasted_iota(jnp.int32, select.shape, 0)
+    source = lax.broadcasted_iota(jnp.int32, select.shape, 1)
+    picked = (source == slot + offset) & (slot < slabs[device])
+    select[...] = jnp.where(picked, 1.0, 0.0).astype(bf16)
+
+
+def recon_last_kernel(weights, phase, before, select, out):
+    total = before[...] + jnp.dot(phase[...], weights[...], preferred_element_type=f32)
+    got = jnp.dot(select[...], total.astype(bf16), preferred_element_type=f32)
+    out[...] = got.astype(bf16)
 
 
 def vmem(count):
     return [pl.BlockSpec(memory_space=pltpu.VMEM)] * count
+
+
+def from_hbm(value):
+    return pltpu.with_memory_space_constraint(value, pltpu.HBM)
+
+
+def in_hbm(count):
+    return [pl.BlockSpec(memory_space=pltpu.HBM)] * count
 
 
 def unread(count):
@@ -243,6 +305,7 @@
     dists = cores * dist_dev
     pixels = weights.shape[2]
     capacity = 2 * rows_dev
+    splits = block // 128
     params = pltpu.CompilerParams(vmem_limit_bytes=16 * 2**20)
     one_out = pl.BlockSpec(memory_space=pltpu.VMEM)
 
@@ -254,17 +317,6 @@
     def shaped(*shape):
         return jax.ShapeDtypeStruct(shape, bf16)
 
-    device = lax.axis_index("rows")
-    core = lax.axis_index("dist")
-    plane, spot = device // inner, device % inner
-    parity = device % 2
-    info = jnp.concatenate(
-        [
-            angle_order[0],
-            (parity * slab_rows[device - parity])[None],
-            slab_rows[device][None],
-        ]
-    )
     table = jnp.asarray(hartley(width))
 
     def sent(value, target):
@@ -291,56 +343,50 @@
         z = r // inner
         return (c, (3 - z) * inner + r % inner) if z in (1, 2) else (c ^ 1, r)
 
-    index = jnp.arange(width, dtype=jnp.int32)
-    my_cols = spot * block + jnp.arange(block, dtype=jnp.int32)
-    ordered = jnp.concatenate(
-        [
-            lax.dynamic_slice_in_dim(propagation, (core ^ other) * dist_dev, dist_dev, 0)
-            for other in range(cores)
-        ]
-    )
-    first = ordered[:, None] * signed_square(index, width)[None]
-    second = ordered[:, None] * signed_square(my_cols, width)[None]
-    sin_b, cos_b = jnp.sin(second), jnp.cos(second)
-    gain, mine = pl.pallas_call(
-        filter_kernel,
-        out_shape=[shaped(dists, width, block), shaped(own, dist_dev, rows_dev, width)],
-        in_specs=vmem(3) + unread(1),
-        out_specs=vmem(2),
+    partner = sent(holograms[0], to_other_core)
+    mine = pl.pallas_call(
+        take_kernel,
+        out_shape=shaped(own, dist_dev, rows_dev, width),
+        in_specs=in_hbm(1) + vmem(1),
+        out_specs=one_out,
         scratch_shapes=[pltpu.SemaphoreType.DMA],
         compiler_params=params,
-        cost_estimate=cost(32 * width * block, (dists, width, block)),
-        name="filters",
-    )(
-        jnp.concatenate([jnp.sin(first), jnp.cos(first)], axis=0),
-        2.0 * (cos_b - absorb_ratio * sin_b),
-        2.0 * (sin_b + absorb_ratio * cos_b),
-        holograms[0],
-    )
-
-    partner = sent(holograms[0], to_other_core)
+        cost_estimate=cost(1, (8, width)),
+        name="take",
+    )(from_hbm(holograms[0]), table)
     arrived = []
     for chunk in range(own):
         pieces = pl.pallas_call(
             lambda *refs, chunk=chunk: row_kernel(inner, chunk, *refs),
             out_shape=[shaped(dists, rows_dev, block)] * inner,
-            in_specs=vmem(3) + unread(1),
+            in_specs=vmem(3),
             out_specs=vmem(inner),
             compiler_params=params,
             cost_estimate=cost(
                 2 * dists * rows_dev * width * width, (width, width), (2, dists, rows_dev, width)
             ),
             name="row_spectra",
-        )(mine, partner, table, gain)
+        )(mine, partner, table)
         arrived.append(spread(pieces, send_order))
+
+    gain = pl.pallas_call(
+        lambda *refs: filter_kernel(inner, dist_dev, *refs),
+        out_shape=shaped(dists, width, block),
+        in_specs=smem(1) + unread(1),
+        out_specs=one_out,
+        compiler_params=params,
+        cost_estimate=cost(32 * width * block, (dists, width, block)),
+        name="filters",
+    )(propagation, pieces[0])
 
     sums = []
     for chunk in range(own):
-        away, keep = pl.pallas_call(
+        keep, *away = pl.pallas_call(
             lambda *refs: column_kernel(inner, outer, *refs),
-            out_shape=[shaped(outer // 2, depth, block)] * 2,
+            out_shape=[shaped(outer // 2, depth, block)]
+            + [shaped(outer // 2, depth, block // splits)] * splits,
             in_specs=vmem(2 + inner),
-            out_specs=vmem(2),
+            out_specs=vmem(1 + splits),
             scratch_shapes=[
                 pltpu.VMEM((dists, depth, block), bf16),
                 pltpu.VMEM((width, block), f32),
@@ -352,49 +398,41 @@
             ),
             name="columns",
         )(table, gain, *arrived[chunk])
-        joint = pl.pallas_call(
-            add_kernel,
-            out_shape=shaped(outer // 2, depth, block),
-            in_specs=vmem(2),
-            out_specs=one_out,
-            compiler_params=params,
-            cost_estimate=cost(outer * depth * block, (3, outer // 2, depth, block)),
-            name="joint",
-        )(away, sent(away, to_near_plane))
-        across = sent(joint, to_middle)
-        near = pl.pallas_call(
-            lambda *refs: near_kernel(inner, *refs),
-            out_shape=shaped(depth, block),
-            in_specs=vmem(2),
-            out_specs=one_out,
-            compiler_params=params,
-            cost_estimate=cost(depth * block, (3, depth, block)),
-            name="near",
-        )(keep, across)
-        sums.append((keep, across, sent(near, to_near_plane)))
-
-    def recon(kernel, out_type, *arrays):
-        return pl.pallas_call(
-            kernel,
-            out_shape=jax.ShapeDtypeStruct((capacity, pixels), out_type),
-            in_specs=smem(1) + vmem(1 + len(arrays)),
-            out_specs=one_out,
-            compiler_params=params,
-            cost_estimate=cost(1, (8, pixels)),
-            name="recon",
-        )(info, weights, *arrays)
+        parts = [keep]
+        for split in range(splits):
+            joint = pl.pallas_call(
+                add_kernel,
+                out_shape=shaped(outer // 2, depth, block // splits),
+                in_specs=vmem(2),
+                out_specs=one_out,
+                compiler_params=params,
+                cost_estimate=cost(1, (8, width)),
+                name="joint",
+            )(away[split], sent(away[split], to_near_plane))
+            across = sent(joint, to_middle)
+            near = pl.pallas_call(
+                lambda *refs, split=split: near_kernel(inner, split, *refs),
+                out_shape=shaped(depth, block // splits),
+                in_specs=vmem(2),
+                out_specs=one_out,
+                compiler_params=params,
+                cost_estimate=cost(1, (8, width)),
+                name="near",
+            )(keep, across)
+            parts += [across, sent(near, to_near_plane)]
+        sums.append(parts)
 
     total = None
     for chunk in range(own):
         first, second = pl.pallas_call(
             lambda *refs: half_kernel(inner, *refs),
             out_shape=[shaped(capacity, block)] * 2,
-            in_specs=vmem(3) + unread(2),
+            in_specs=vmem(1 + 2 * splits),
             out_specs=vmem(2),
             compiler_params=params,
             cost_estimate=cost(1, (8, width)),
             name="half",
-        )(*sums[chunk], near, info)
+        )(*sums[chunk])
         pieces = spread([first, first, second, second], tail_order)
         phase = pl.pallas_call(
             lambda *refs: phase_kernel(inner, *refs),
@@ -407,20 +445,39 @@
             name="phase",
         )(table, *pieces)
         there = sent(phase, to_other_core)
-        def part(cores, chunk=chunk):
-            return lambda *refs: recon_kernel(own, chunk, cores, *refs)
-
-        before = [] if total is None else [total]
         if chunk < own - 1:
-            total = recon(part((0, 1)), f32, phase, there, *before)
+            total = pl.pallas_call(
+                lambda *refs, chunk=chunk: recon_kernel(own, chunk, (0, 1), *refs),
+                out_shape=jax.ShapeDtypeStruct((capacity, pixels), f32),
+                in_specs=smem(1) + vmem(3),
+                out_specs=one_out,
+                compiler_params=params,
+                cost_estimate=cost(1, (8, width)),
+                name="recon",
+            )(angle_order, weights, phase, there)
         else:
-            total = recon(part((0,)), f32, phase, *before)
-            total = recon(
-                lambda *refs, chunk=chunk: recon_last_kernel(own, chunk, 1, *refs),
-                bf16,
-                there,
-                total,
-            )
+            total, chosen, select = pl.pallas_call(
+                lambda *refs, chunk=chunk: recon_next_kernel(own, chunk, *refs),
+                out_shape=[
+                    jax.ShapeDtypeStruct((capacity, pixels), f32),
+                    shaped(width, pixels),
+                    shaped(capacity, capacity),
+                ],
+                in_specs=smem(2) + vmem(3),
+                out_specs=vmem(3),
+                compiler_params=params,
+                cost_estimate=cost(1, (8, width)),
+                name="recon",
+            )(angle_order, slab_rows, weights, phase, total)
+            total = pl.pallas_call(
+                recon_last_kernel,
+                out_shape=shaped(capacity, pixels),
+                in_specs=vmem(4),
+                out_specs=one_out,
+                compiler_params=params,
+                cost_estimate=cost(1, (8, width)),
+                name="recon",
+            )(chosen, there, total, select)
     return total
 
 
@@ -437,6 +494,7 @@
         and inner == 4
         and groups == inner * inner
         and lax.axis_size("dist") == 2
+        and angles == 2 * lax.axis_size("dist")
     )
     if fits:
         return plane_plan(inner, holograms, propagation, weights, angle_order, slab_rows)

time: 59.3 us -> 53.9 us (0.909)
  waiting for transfers between devices: 13.3 us -> 9.87 us
  local copies, waits for them, and re-layouts: 4.28 us -> 1.61 us
  starting transfers between devices: 27.7 us -> 30 us
  other arithmetic: 1.17 us -> 0 us
  between operations: 0.9 us -> 0.29 us
    ppermute x21 -> x27, waiting for transfers between devices: 13.3 us -> 9.87 us  [sent(): return lax.ppermute(value, ('dist', 'rows'), pairs)]
    ppermute x21 -> x27, starting transfers between devices: 27.7 us -> 30 us  [sent(): return lax.ppermute(value, ('dist', 'rows'), pairs)]
    dynamic_slice x2 -> x0, local copies, waits for them, and re-layouts: 1.45 us -> none  [the longest x1 0.8 us: plane_plan(): lax.dynamic_slice_in_dim(propagation, (core ^ other) * dist_dev, dist_dev...]
    pallas_call x8 -> x13, Pallas kernels: 5.55 us -> 6.77 us  [the longest x1 2.37 us: plane_plan(): pl.pallas_call(lambda *refs: filter_kernel(inner, dist_dev, *refs), out_s...]
    unnamed x12, local copies, waits for them, and re-layouts: 2.83 us -> 1.61 us
    pallas_call x2, Pallas kernels: 1.03 us -> 0.13 us  [plane_plan(): pl.pallas_call(lambda *refs: half_kernel(inner, *refs), out_shape=[shaped...]
    concatenate x3 -> x0, other arithmetic: 0.83 us -> none  [the longest x1 0.75 us: plane_plan(): jnp.concatenate([angle_order[0], (parity * slab_rows[device - parity])[No...]
  transfers between devices with their start and end apart: 21 -> 27, of which waited for: 9 -> 7; matrix products, arithmetic and copies ran while one was open for 4% -> 0% of each run, Pallas kernels for 16% -> 19%
where the time goes in v10:
time: 53.9 us; the launch traced here: 53.6 us
  starting transfers between devices  30 us (56%)
  Pallas kernels  11.9 us (22%)
  waiting for transfers between devices  9.87 us (18%)
  local copies, waits for them, and re-layouts  1.61 us (3%)
    ppermute x27, starting transfers between devices, sent(): return lax.ppermute(value, ('dist', 'rows'), pairs)  30 us
    ppermute x27, waiting for transfers between devices, sent(): return lax.ppermute(value, ('dist', 'rows'), pairs)  9.87 us
    pallas_call x2, Pallas kernels, plane_plan(): pl.pallas_call(lambda *refs: column_kernel(inner, outer, *refs), out_shap...  2.6 us
    pallas_call x1, Pallas kernels, plane_plan(): pl.pallas_call(lambda *refs: filter_kernel(inner, dist_dev, *refs), out_s...  2.37 us
    unnamed x12, local copies, waits for them, and re-layouts  1.61 us
    pallas_call x2, Pallas kernels, plane_plan(): pl.pallas_call(lambda *refs, chunk=chunk: row_kernel(inner, chunk, *refs)...  1.49 us
    pallas_call x1, Pallas kernels, plane_plan(): pl.pallas_call(recon_last_kernel, out_shape=shaped(capacity, pixels), in_...  1.14 us
  transfers between devices with their start and end apart: 27, of which 7 were waited for; matrix products, arithmetic and copies ran while one was open for 0% of the time, Pallas kernels for 19%

profile of v10, /device:TPU:0, one launch (start us, length us, event | category | flops | bytes accessed | tf_op | source)
XLA Modules:
  0.0 53.6 jit_solution(9662418330370463626)
XLA Ops:
  0.0 0.5 collective-permute-start
  0.5 1.6 %copy-done = bf16[1024,1024]{1,0:T(8,128)(2,1)S(1)} copy-done((bf16[1024,1024]{1,0:T(8,128)(2,1)S(1)}, bf16[1024,1024]{1,0:T(8,128)(2,1)}, u32[]{:S(2)}) %copy-start) | copy-done | bytes 2097176
  2.0 1.0 %take.1.refs_0_ = bf16[2,2,64,1024]{3,2,1,0:T(8,128)(2,1)S(1)} custom-call(bf16[4,2,64,1024]{3,2,1,0:T(8,128)(2,1)} %bitcast.2, bf16[1024,1024]{1,0:T(8,128)(2,1)S(1)} %copy-done), custom_call_target="tpu_custom_call" | custom-call | flops 1 | bytes 16384 | tf_op jit(solution)/shard_map/take/pallas_call | solution.py:347
  3.1 0.0 collective-permute-done.refs_1_
  3.1 0.7 %row_spectra.3 = (bf16[4,64,256]{2,1,0:T(8,128)(2,1)S(1)}, bf16[4,64,256]{2,1,0:T(8,128)(2,1)S(1)}, bf16[4,64,256]{2,1,0:T(8,128)(2,1)S(1)}, bf16[4,64,256]{2,1,0:T(8,128)(2,1)S(1)}) custom-call(bf16[2,2,64,1024]{3,2,1,0:T(8,128)(2,1)S(1)} %take.1.refs_0_, bf16[4,2,64,1024]{3,2,1,0:T(8,128)(2,1)S(1)} %collective-permute-done.refs_1_, ...), custom_call_target="tpu_custom_call" | custom-call | flops 536870912 | bytes 3145728 | tf_op jit(solution)/shard_map/row_spectra/pallas_call | solution.py:359
  3.9 0.0 copy-start.4
  3.9 2.8 %collective-permute-start.13 = (bf16[4,64,256]{2,1,0:T(8,128)(2,1)S(1)}, bf16[4,64,256]{2,1,0:T(8,128)(2,1)S(1)}, u32[]{:S(2)}, u32[]{:S(2)}) collective-permute-start(bf16[4,64,256]{2,1,0:T(8,128)(2,1)S(1)} %get-tuple-element.36), channel_id=1, source_target_pairs={{0,1},{1,0},{2,3},{3,2},{4,5},{5,4},{6,7},{7,6},{8,9},{9,8},{10,11... | collective-permute-start | bytes 393224 | tf_op jit(solution)/shard_map/ppermute | solution.py:328
  6.6 1.5 %collective-permute-start.14 = (bf16[4,64,256]{2,1,0:T(8,128)(2,1)S(1)}, bf16[4,64,256]{2,1,0:T(8,128)(2,1)S(1)}, u32[]{:S(2)}, u32[]{:S(2)}) collective-permute-start(bf16[4,64,256]{2,1,0:T(8,128)(2,1)S(1)} %get-tuple-element.37), channel_id=1, source_target_pairs={{0,2},{1,3},{2,0},{3,1},{4,6},{5,7},{6,4},{7,5},{8,10},{9,11},{10,... | collective-permute-start | bytes 393224 | tf_op jit(solution)/shard_map/ppermute | solution.py:328
  8.2 0.0 collective-permute-start.15
  8.2 0.7 %row_spectra.2 = (bf16[4,64,256]{2,1,0:T(8,128)(2,1)S(1)}, bf16[4,64,256]{2,1,0:T(8,128)(2,1)S(1)}, bf16[4,64,256]{2,1,0:T(8,128)(2,1)S(1)}, bf16[4,64,256]{2,1,0:T(8,128)(2,1)S(1)}) custom-call(bf16[2,2,64,1024]{3,2,1,0:T(8,128)(2,1)S(1)} %take.1.refs_0_, bf16[4,2,64,1024]{3,2,1,0:T(8,128)(2,1)S(1)} %collective-permute-done.refs_1_, ...), custom_call_target="tpu_custom_call" | custom-call | flops 536870912 | bytes 3145728 | tf_op jit(solution)/shard_map/row_spectra/pallas_call | solution.py:359
  8.9 2.0 %collective-permute-start.1 = (bf16[4,64,256]{2,1,0:T(8,128)(2,1)S(1)}, bf16[4,64,256]{2,1,0:T(8,128)(2,1)S(1)}, u32[]{:S(2)}, u32[]{:S(2)}) collective-permute-start(bf16[4,64,256]{2,1,0:T(8,128)(2,1)S(1)} %get-tuple-element.27), channel_id=1, source_target_pairs={{0,1},{1,0},{2,3},{3,2},{4,5},{5,4},{6,7},{7,6},{8,9},{9,8},{10,11... | collective-permute-start | bytes 393224 | tf_op jit(solution)/shard_map/ppermute | solution.py:328
  10.9 1.5 %collective-permute-start.2 = (bf16[4,64,256]{2,1,0:T(8,128)(2,1)S(1)}, bf16[4,64,256]{2,1,0:T(8,128)(2,1)S(1)}, u32[]{:S(2)}, u32[]{:S(2)}) collective-permute-start(bf16[4,64,256]{2,1,0:T(8,128)(2,1)S(1)} %get-tuple-element.28), channel_id=1, source_target_pairs={{0,2},{1,3},{2,0},{3,1},{4,6},{5,7},{6,4},{7,5},{8,10},{9,11},{10,... | collective-permute-start | bytes 393224 | tf_op jit(solution)/shard_map/ppermute | solution.py:328
  12.4 0.0 collective-permute-done.13.refs_3_
  12.5 1.5 %collective-permute-start.3 = (bf16[4,64,256]{2,1,0:T(8,128)(2,1)S(1)}, bf16[4,64,256]{2,1,0:T(8,128)(2,1)S(1)}, u32[]{:S(2)}, u32[]{:S(2)}) collective-permute-start(bf16[4,64,256]{2,1,0:T(8,128)(2,1)S(1)} %get-tuple-element.29), channel_id=1, source_target_pairs={{0,3},{1,2},{2,1},{3,0},{4,7},{5,6},{6,5},{7,4},{8,11},{9,10},{10,... | collective-permute-start | bytes 393224 | tf_op jit(solution)/shard_map/ppermute | solution.py:328
  13.9 2.4 %filters.1.refs_1_ = bf16[4,1024,256]{2,1,0:T(8,128)(2,1)S(1)} custom-call(f32[4]{0:T(128)S(1)} %copy-done.4, bf16[4,64,256]{2,1,0:T(8,128)(2,1)S(1)} %get-tuple-element.26.refs_1_.refs_2_), custom_call_target="tpu_custom_call" | custom-call | flops 8388608 | bytes 2097152 | tf_op jit(solution)/shard_map/filters/pallas_call | solution.py:372
  16.3 0.0 collective-permute-done.14.refs_4_
  16.3 1.3 %columns.3 = (bf16[2,256,256]{2,1,0:T(8,128)(2,1)S(1)}, bf16[2,256,128]{2,1,0:T(8,128)(2,1)S(1)}, bf16[2,256,128]{2,1,0:T(8,128)(2,1)S(1)}) custom-call(bf16[1024,1024]{1,0:T(8,128)(2,1)S(1)} %copy-done.1, bf16[4,1024,256]{2,1,0:T(8,128)(2,1)S(1)} %filters.1.refs_1_, bf16[4,64,256]{2,1,0:T(8,128)(2,1)S(1)} %get-tuple-element.35.refs_2_, ...), custom_call_target="tpu_custom_call" | custom-call | flops 1073741824 | bytes 4194304 | tf_op jit(solution)/shard_map/columns/pallas_call | solution.py:384
  17.6 1.6 %collective-permute-start.16 = (bf16[2,256,128]{2,1,0:T(8,128)(2,1)S(1)}, bf16[2,256,128]{2,1,0:T(8,128)(2,1)S(1)}, u32[]{:S(2)}, u32[]{:S(2)}) collective-permute-start(bf16[2,256,128]{2,1,0:T(8,128)(2,1)S(1)} %get-tuple-element.40.one), channel_id=1, source_target_pairs={{0,4},{1,5},{2,6},{3,7},{4,0},{5,1},{6,2},{7,3},{8,12},{9,13},{10,... | collective-permute-start | bytes 393224 | tf_op jit(solution)/shard_map/ppermute | solution.py:328
  19.3 0.5 collective-permute-start.19
  19.7 0.0 collective-permute-done.1.refs_3_
  19.7 0.8 %collective-permute-done.2.refs_4_ = bf16[4,64,256]{2,1,0:T(8,128)(2,1)S(1)} collective-permute-done((bf16[4,64,256]{2,1,0:T(8,128)(2,1)S(1)}, bf16[4,64,256]{2,1,0:T(8,128)(2,1)S(1)}, u32[]{:S(2)}, u32[]{:S(2)}) %collective-permute-start.2) | collective-permute-done | bytes 131104 | tf_op jit(solution)/shard_map/ppermute | solution.py:328
  20.5 1.3 %columns.2 = (bf16[2,256,256]{2,1,0:T(8,128)(2,1)S(1)}, bf16[2,256,128]{2,1,0:T(8,128)(2,1)S(1)}, bf16[2,256,128]{2,1,0:T(8,128)(2,1)S(1)}) custom-call(bf16[1024,1024]{1,0:T(8,128)(2,1)S(1)} %copy-done.1, bf16[4,1024,256]{2,1,0:T(8,128)(2,1)S(1)} %filters.1.refs_1_, bf16[4,64,256]{2,1,0:T(8,128)(2,1)S(1)} %get-tuple-element.26.refs_1_.refs_2_, ...), custom_call_target="tpu_custom_call" | custom-call | flops 1073741824 | bytes 4194304 | tf_op jit(solution)/shard_map/columns/pallas_call | solution.py:384
  21.8 1.6 %collective-permute-start.4 = (bf16[2,256,128]{2,1,0:T(8,128)(2,1)S(1)}, bf16[2,256,128]{2,1,0:T(8,128)(2,1)S(1)}, u32[]{:S(2)}, u32[]{:S(2)}) collective-permute-start(bf16[2,256,128]{2,1,0:T(8,128)(2,1)S(1)} %get-tuple-element.31.one), channel_id=1, source_target_pairs={{0,4},{1,5},{2,6},{3,7},{4,0},{5,1},{6,2},{7,3},{8,12},{9,13},{10,... | collective-permute-start | bytes 393224 | tf_op jit(solution)/shard_map/ppermute | solution.py:328
  23.4 0.5 collective-permute-start.7
  23.9 0.0 collective-permute-done.16.two
  23.9 0.1 collective-permute-start.17
  24.0 0.7 %collective-permute-done.19.two = bf16[2,256,128]{2,1,0:T(8,128)(2,1)S(1)} collective-permute-done((bf16[2,256,128]{2,1,0:T(8,128)(2,1)S(1)}, bf16[2,256,128]{2,1,0:T(8,128)(2,1)S(1)}, u32[]{:S(2)}, u32[]{:S(2)}) %collective-permute-start.19) | collective-permute-done | bytes 131104 | tf_op jit(solution)/shard_map/ppermute | solution.py:328
  24.7 0.1 collective-permute-start.20
  24.8 3.5 %collective-permute-done.4.two = bf16[2,256,128]{2,1,0:T(8,128)(2,1)S(1)} collective-permute-done((bf16[2,256,128]{2,1,0:T(8,128)(2,1)S(1)}, bf16[2,256,128]{2,1,0:T(8,128)(2,1)S(1)}, u32[]{:S(2)}, u32[]{:S(2)}) %collective-permute-start.4) | collective-permute-done | bytes 131104 | tf_op jit(solution)/shard_map/ppermute | solution.py:328
  28.3 0.1 collective-permute-start.5
  28.4 1.8 %collective-permute-done.7.two = bf16[2,256,128]{2,1,0:T(8,128)(2,1)S(1)} collective-permute-done((bf16[2,256,128]{2,1,0:T(8,128)(2,1)S(1)}, bf16[2,256,128]{2,1,0:T(8,128)(2,1)S(1)}, u32[]{:S(2)}, u32[]{:S(2)}) %collective-permute-start.7) | collective-permute-done | bytes 131104 | tf_op jit(solution)/shard_map/ppermute | solution.py:328
  30.2 0.1 collective-permute-start.8
  30.3 0.0 collective-permute-done.17.refs_1_
  30.3 3.2 %collective-permute-start.18 = (bf16[256,128]{1,0:T(8,128)(2,1)S(1)}, bf16[256,128]{1,0:T(8,128)(2,1)S(1)}, u32[]{:S(2)}, u32[]{:S(2)}) collective-permute-start(bf16[256,128]{1,0:T(8,128)(2,1)S(1)} %near.6), channel_id=1, source_target_pairs={{0,4},{1,5},{2,6},{3,7},{4,0},{5,1},{6,2},{7,3},{8,12},{9,13},{10,... | collective-permute-start | bytes 196616 | tf_op jit(solution)/shard_map/ppermute | solution.py:328
  33.5 0.0 collective-permute-done.20.refs_1_.refs_3_
  33.5 1.4 %collective-permute-start.21 = (bf16[256,128]{1,0:T(8,128)(2,1)S(1)}, bf16[256,128]{1,0:T(8,128)(2,1)S(1)}, u32[]{:S(2)}, u32[]{:S(2)}) collective-permute-start(bf16[256,128]{1,0:T(8,128)(2,1)S(1)} %near.7), channel_id=1, source_target_pairs={{0,4},{1,5},{2,6},{3,7},{4,0},{5,1},{6,2},{7,3},{8,12},{9,13},{10,... | collective-permute-start | bytes 196616 | tf_op jit(solution)/shard_map/ppermute | solution.py:328
  34.9 0.0 collective-permute-done.5.refs_1_
  34.9 2.6 %collective-permute-start.6 = (bf16[256,128]{1,0:T(8,128)(2,1)S(1)}, bf16[256,128]{1,0:T(8,128)(2,1)S(1)}, u32[]{:S(2)}, u32[]{:S(2)}) collective-permute-start(bf16[256,128]{1,0:T(8,128)(2,1)S(1)} %near.4), channel_id=1, source_target_pairs={{0,4},{1,5},{2,6},{3,7},{4,0},{5,1},{6,2},{7,3},{8,12},{9,13},{10,... | collective-permute-start | bytes 196616 | tf_op jit(solution)/shard_map/ppermute | solution.py:328
  37.6 1.4 %collective-permute-start.9 = (bf16[256,128]{1,0:T(8,128)(2,1)S(1)}, bf16[256,128]{1,0:T(8,128)(2,1)S(1)}, u32[]{:S(2)}, u32[]{:S(2)}) collective-permute-start(bf16[256,128]{1,0:T(8,128)(2,1)S(1)} %near.5), channel_id=1, source_target_pairs={{0,4},{1,5},{2,6},{3,7},{4,0},{5,1},{6,2},{7,3},{8,12},{9,13},{10,... | collective-permute-start | bytes 196616 | tf_op jit(solution)/shard_map/ppermute | solution.py:328
  38.9 0.0 collective-permute-done.18.refs_2_
  38.9 0.0 collective-permute-done.21.refs_4_
  38.9 0.1 half.3
  39.0 0.9 %collective-permute-start.22 = (bf16[128,256]{1,0:T(8,128)(2,1)S(1)}, bf16[128,256]{1,0:T(8,128)(2,1)S(1)}, u32[]{:S(2)}, u32[]{:S(2)}) collective-permute-start(bf16[128,256]{1,0:T(8,128)(2,1)S(1)} %get-tuple-element.42.refs_1_), channel_id=1, source_target_pairs={{0,1},{1,0},{2,3},{3,2},{4,5},{5,4},{6,7},{7,6},{8,9},{9,8},{10,11... | collective-permute-start | bytes 196616 | tf_op jit(solution)/shard_map/ppermute | solution.py:328
  39.9 1.2 %collective-permute-start.24 = (bf16[128,256]{1,0:T(8,128)(2,1)S(1)}, bf16[128,256]{1,0:T(8,128)(2,1)S(1)}, u32[]{:S(2)}, u32[]{:S(2)}) collective-permute-start(bf16[128,256]{1,0:T(8,128)(2,1)S(1)} %get-tuple-element.43), channel_id=1, source_target_pairs={{0,2},{1,3},{2,0},{3,1},{4,6},{5,7},{6,4},{7,5},{8,10},{9,11},{10,... | collective-permute-start | bytes 196616 | tf_op jit(solution)/shard_map/ppermute | solution.py:328
  41.1 1.5 %collective-permute-start.23 = (bf16[128,256]{1,0:T(8,128)(2,1)S(1)}, bf16[128,256]{1,0:T(8,128)(2,1)S(1)}, u32[]{:S(2)}, u32[]{:S(2)}) collective-permute-start(bf16[128,256]{1,0:T(8,128)(2,1)S(1)} %get-tuple-element.43), channel_id=1, source_target_pairs={{0,3},{1,2},{2,1},{3,0},{4,7},{5,6},{6,5},{7,4},{8,11},{9,10},{10,... | collective-permute-start | bytes 196616 | tf_op jit(solution)/shard_map/ppermute | solution.py:328
  42.6 0.0 collective-permute-done.6.refs_2_
  42.6 0.0 collective-permute-done.9.refs_4_
  42.6 0.1 half.2
  42.6 0.9 %collective-permute-start.10 = (bf16[128,256]{1,0:T(8,128)(2,1)S(1)}, bf16[128,256]{1,0:T(8,128)(2,1)S(1)}, u32[]{:S(2)}, u32[]{:S(2)}) collective-permute-start(bf16[128,256]{1,0:T(8,128)(2,1)S(1)} %get-tuple-element.33.refs_1_), channel_id=1, source_target_pairs={{0,1},{1,0},{2,3},{3,2},{4,5},{5,4},{6,7},{7,6},{8,9},{9,8},{10,11... | collective-permute-start | bytes 196616 | tf_op jit(solution)/shard_map/ppermute | solution.py:328
  43.5 1.2 %collective-permute-start.12 = (bf16[128,256]{1,0:T(8,128)(2,1)S(1)}, bf16[128,256]{1,0:T(8,128)(2,1)S(1)}, u32[]{:S(2)}, u32[]{:S(2)}) collective-permute-start(bf16[128,256]{1,0:T(8,128)(2,1)S(1)} %get-tuple-element.34), channel_id=1, source_target_pairs={{0,2},{1,3},{2,0},{3,1},{4,6},{5,7},{6,4},{7,5},{8,10},{9,11},{10,... | collective-permute-start | bytes 196616 | tf_op jit(solution)/shard_map/ppermute | solution.py:328
  44.7 0.0 collective-permute-done.22.refs_2_
  44.7 1.5 %collective-permute-start.11 = (bf16[128,256]{1,0:T(8,128)(2,1)S(1)}, bf16[128,256]{1,0:T(8,128)(2,1)S(1)}, u32[]{:S(2)}, u32[]{:S(2)}) collective-permute-start(bf16[128,256]{1,0:T(8,128)(2,1)S(1)} %get-tuple-element.34), channel_id=1, source_target_pairs={{0,3},{1,2},{2,1},{3,0},{4,7},{5,6},{6,5},{7,4},{8,11},{9,10},{10,... | collective-permute-start | bytes 196616 | tf_op jit(solution)/shard_map/ppermute | solution.py:328
  46.2 0.0 collective-permute-done.24.refs_4_
  46.2 0.3 collective-permute-done.23.refs_3_
  46.5 0.5 phase.3.refs_2_
  47.0 0.1 collective-permute-start.25
  47.1 0.7 %collective-permute-done.12.refs_4_ = bf16[128,256]{1,0:T(8,128)(2,1)S(1)} collective-permute-done((bf16[128,256]{1,0:T(8,128)(2,1)S(1)}, bf16[128,256]{1,0:T(8,128)(2,1)S(1)}, u32[]{:S(2)}, u32[]{:S(2)}) %collective-permute-start.12) | collective-permute-done | bytes 65568 | tf_op jit(solution)/shard_map/ppermute | solution.py:328
  47.8 2.1 %collective-permute-done.11.refs_3_ = bf16[128,256]{1,0:T(8,128)(2,1)S(1)} collective-permute-done((bf16[128,256]{1,0:T(8,128)(2,1)S(1)}, bf16[128,256]{1,0:T(8,128)(2,1)S(1)}, u32[]{:S(2)}, u32[]{:S(2)}) %collective-permute-start.11) | collective-permute-done | bytes 65568 | tf_op jit(solution)/shard_map/ppermute | solution.py:328
  49.9 0.5 phase.2.refs_3_
  50.4 0.0 copy-start.5
  50.4 0.1 collective-permute-start.26
  50.5 1.0 %recon.3.refs_4_ = f32[128,512]{1,0:T(8,128)S(1)} custom-call(s32[1,4]{1,0:T(1,128)S(1)} %copy-done.3, bf16[4,1024,512]{2,1,0:T(8,128)(2,1)S(1)} %copy-done.2, bf16[128,1024]{1,0:T(8,128)(2,1)S(1)} %phase.3.refs_2_, bf16[128,1024]{1,0:T(8,128)(2,1)S(1)} %collective-permute-done.25.refs_3_), custom_call_target="tpu_custom_call" | custom-call | flops 1 | bytes 16384 | tf_op jit(solution)/shard_map/recon/pallas_call | solution.py:449
  51.5 0.9 %recon.4 = (f32[128,512]{1,0:T(8,128)S(1)}, bf16[1024,512]{1,0:T(8,128)(2,1)S(1)}, bf16[128,128]{1,0:T(8,128)(2,1)S(1)}) custom-call(s32[1,4]{1,0:T(1,128)S(1)} %copy-done.3, s32[16]{0:T(128)S(1)} %copy-done.5, bf16[4,1024,512]{2,1,0:T(8,128)(2,1)S(1)} %copy-done.2, bf16[128,1024]{1,0:T(8,128)(2,1)S(1)} %phase.2.refs_3_, f32[128,512]{1,0:T(8,128)S(1)} %recon.3.refs_4_), custom_call_target="tpu_custom_call" | custom-call | flops 1 | bytes 16384 | tf_op jit(solution)/shard_map/recon/pallas_call | solution.py:459
  52.5 1.1 %recon.5 = bf16[128,512]{1,0:T(8,128)(2,1)} custom-call(bf16[1024,512]{1,0:T(8,128)(2,1)S(1)} %get-tuple-element.44.weights, bf16[128,1024]{1,0:T(8,128)(2,1)S(1)} %collective-permute-done.26.phase, f32[128,512]{1,0:T(8,128)S(1)} %get-tuple-element.45.before, bf16[128,128]{1,0:T(8,128)(2,1)S(1)} %get-tuple-element.46.select), custom_call_target="tpu_custom_call" | custom-call | flops 1 | bytes 16384 | tf_op jit(solution)/shard_map/recon/pallas_call | solution.py:472
  (23 shorter events, 0.3 us)
Async XLA Ops:
  0.0 3.1 %collective-permute-start = (bf16[4,2,64,1024]{3,2,1,0:T(8,128)(2,1)}, bf16[4,2,64,1024]{3,2,1,0:T(8,128)(2,1)S(1)}, u32[]{:S(2)}, u32[]{:S(2)}) collective-permute-start(bf16[4,2,64,1024]{3,2,1,0:T(8,128)(2,1)} %bitcast.1), channel_id=1, source_target_pairs={{0,16},{1,17},{2,18},{3,19},{4,20},{5,21},{6,22},{7,23},{8,24},{9,... | collective-permute-start | bytes 3145736 | tf_op jit(solution)/shard_map/ppermute | solution.py:328
  0.5 1.6 %copy-start = (bf16[1024,1024]{1,0:T(8,128)(2,1)S(1)}, bf16[1024,1024]{1,0:T(8,128)(2,1)}, u32[]{:S(2)}) copy-start(bf16[1024,1024]{1,0:T(8,128)(2,1)} %constant.2.clone.after.refs_2_.refs_0_) | copy-start | bytes 6291460
  3.9 10.0 %copy-start.4 = (f32[4]{0:T(128)S(1)}, f32[4]{0:T(128)}, u32[]{:S(2)}) copy-start(f32[4]{0:T(128)} %refs_0_.7) | copy-start | bytes 52
  3.9 8.6 %collective-permute-start.13 = (bf16[4,64,256]{2,1,0:T(8,128)(2,1)S(1)}, bf16[4,64,256]{2,1,0:T(8,128)(2,1)S(1)}, u32[]{:S(2)}, u32[]{:S(2)}) collective-permute-start(bf16[4,64,256]{2,1,0:T(8,128)(2,1)S(1)} %get-tuple-element.36), channel_id=1, source_target_pairs={{0,1},{1,0},{2,3},{3,2},{4,5},{5,4},{6,7},{7,6},{8,9},{9,8},{10,11... | collective-permute-start | bytes 393224 | tf_op jit(solution)/shard_map/ppermute | solution.py:328
  6.6 9.7 %collective-permute-start.14 = (bf16[4,64,256]{2,1,0:T(8,128)(2,1)S(1)}, bf16[4,64,256]{2,1,0:T(8,128)(2,1)S(1)}, u32[]{:S(2)}, u32[]{:S(2)}) collective-permute-start(bf16[4,64,256]{2,1,0:T(8,128)(2,1)S(1)} %get-tuple-element.37), channel_id=1, source_target_pairs={{0,2},{1,3},{2,0},{3,1},{4,6},{5,7},{6,4},{7,5},{8,10},{9,11},{10,... | collective-permute-start | bytes 393224 | tf_op jit(solution)/shard_map/ppermute | solution.py:328
  8.2 8.2 %copy-start.1 = (bf16[1024,1024]{1,0:T(8,128)(2,1)S(1)}, bf16[1024,1024]{1,0:T(8,128)(2,1)}, u32[]{:S(2)}) copy-start(bf16[1024,1024]{1,0:T(8,128)(2,1)} %constant.2.clone.after.refs_2_.refs_0_) | copy-start | bytes 6291460
  8.2 8.1 %collective-permute-start.15 = (bf16[4,64,256]{2,1,0:T(8,128)(2,1)S(1)}, bf16[4,64,256]{2,1,0:T(8,128)(2,1)S(1)}, u32[]{:S(2)}, u32[]{:S(2)}) collective-permute-start(bf16[4,64,256]{2,1,0:T(8,128)(2,1)S(1)} %get-tuple-element.38), channel_id=1, source_target_pairs={{0,3},{1,2},{2,1},{3,0},{4,7},{5,6},{6,5},{7,4},{8,11},{9,10},{10,... | collective-permute-start | bytes 393224 | tf_op jit(solution)/shard_map/ppermute | solution.py:328
  8.9 10.8 %collective-permute-start.1 = (bf16[4,64,256]{2,1,0:T(8,128)(2,1)S(1)}, bf16[4,64,256]{2,1,0:T(8,128)(2,1)S(1)}, u32[]{:S(2)}, u32[]{:S(2)}) collective-permute-start(bf16[4,64,256]{2,1,0:T(8,128)(2,1)S(1)} %get-tuple-element.27), channel_id=1, source_target_pairs={{0,1},{1,0},{2,3},{3,2},{4,5},{5,4},{6,7},{7,6},{8,9},{9,8},{10,11... | collective-permute-start | bytes 393224 | tf_op jit(solution)/shard_map/ppermute | solution.py:328
  10.9 9.6 %collective-permute-start.2 = (bf16[4,64,256]{2,1,0:T(8,128)(2,1)S(1)}, bf16[4,64,256]{2,1,0:T(8,128)(2,1)S(1)}, u32[]{:S(2)}, u32[]{:S(2)}) collective-permute-start(bf16[4,64,256]{2,1,0:T(8,128)(2,1)S(1)} %get-tuple-element.28), channel_id=1, source_target_pairs={{0,2},{1,3},{2,0},{3,1},{4,6},{5,7},{6,4},{7,5},{8,10},{9,11},{10,... | collective-permute-start | bytes 393224 | tf_op jit(solution)/shard_map/ppermute | solution.py:328
  12.5 8.0 %collective-permute-start.3 = (bf16[4,64,256]{2,1,0:T(8,128)(2,1)S(1)}, bf16[4,64,256]{2,1,0:T(8,128)(2,1)S(1)}, u32[]{:S(2)}, u32[]{:S(2)}) collective-permute-start(bf16[4,64,256]{2,1,0:T(8,128)(2,1)S(1)} %get-tuple-element.29), channel_id=1, source_target_pairs={{0,3},{1,2},{2,1},{3,0},{4,7},{5,6},{6,5},{7,4},{8,11},{9,10},{10,... | collective-permute-start | bytes 393224 | tf_op jit(solution)/shard_map/ppermute | solution.py:328
  17.6 6.3 %collective-permute-start.16 = (bf16[2,256,128]{2,1,0:T(8,128)(2,1)S(1)}, bf16[2,256,128]{2,1,0:T(8,128)(2,1)S(1)}, u32[]{:S(2)}, u32[]{:S(2)}) collective-permute-start(bf16[2,256,128]{2,1,0:T(8,128)(2,1)S(1)} %get-tuple-element.40.one), channel_id=1, source_target_pairs={{0,4},{1,5},{2,6},{3,7},{4,0},{5,1},{6,2},{7,3},{8,12},{9,13},{10,... | collective-permute-start | bytes 393224 | tf_op jit(solution)/shard_map/ppermute | solution.py:328
  19.3 5.4 %collective-permute-start.19 = (bf16[2,256,128]{2,1,0:T(8,128)(2,1)S(1)}, bf16[2,256,128]{2,1,0:T(8,128)(2,1)S(1)}, u32[]{:S(2)}, u32[]{:S(2)}) collective-permute-start(bf16[2,256,128]{2,1,0:T(8,128)(2,1)S(1)} %get-tuple-element.41.one), channel_id=1, source_target_pairs={{0,4},{1,5},{2,6},{3,7},{4,0},{5,1},{6,2},{7,3},{8,12},{9,13},{10,... | collective-permute-start | bytes 393224 | tf_op jit(solution)/shard_map/ppermute | solution.py:328
  21.8 6.5 %collective-permute-start.4 = (bf16[2,256,128]{2,1,0:T(8,128)(2,1)S(1)}, bf16[2,256,128]{2,1,0:T(8,128)(2,1)S(1)}, u32[]{:S(2)}, u32[]{:S(2)}) collective-permute-start(bf16[2,256,128]{2,1,0:T(8,128)(2,1)S(1)} %get-tuple-element.31.one), channel_id=1, source_target_pairs={{0,4},{1,5},{2,6},{3,7},{4,0},{5,1},{6,2},{7,3},{8,12},{9,13},{10,... | collective-permute-start | bytes 393224 | tf_op jit(solution)/shard_map/ppermute | solution.py:328
  23.4 6.7 %collective-permute-start.7 = (bf16[2,256,128]{2,1,0:T(8,128)(2,1)S(1)}, bf16[2,256,128]{2,1,0:T(8,128)(2,1)S(1)}, u32[]{:S(2)}, u32[]{:S(2)}) collective-permute-start(bf16[2,256,128]{2,1,0:T(8,128)(2,1)S(1)} %get-tuple-element.32.one), channel_id=1, source_target_pairs={{0,4},{1,5},{2,6},{3,7},{4,0},{5,1},{6,2},{7,3},{8,12},{9,13},{10,... | collective-permute-start | bytes 393224 | tf_op jit(solution)/shard_map/ppermute | solution.py:328
  23.9 6.3 %collective-permute-start.17 = (bf16[2,256,128]{2,1,0:T(8,128)(2,1)S(1)}, bf16[2,256,128]{2,1,0:T(8,128)(2,1)S(1)}, u32[]{:S(2)}, u32[]{:S(2)}) collective-permute-start(bf16[2,256,128]{2,1,0:T(8,128)(2,1)S(1)} %joint.6), channel_id=1, source_target_pairs={{0,16},{1,17},{2,18},{3,19},{4,8},{5,9},{6,10},{7,11},{8,4},{9,5},... | collective-permute-start | bytes 393224 | tf_op jit(solution)/shard_map/ppermute | solution.py:328
  24.7 8.8 %collective-permute-start.20 = (bf16[2,256,128]{2,1,0:T(8,128)(2,1)S(1)}, bf16[2,256,128]{2,1,0:T(8,128)(2,1)S(1)}, u32[]{:S(2)}, u32[]{:S(2)}) collective-permute-start(bf16[2,256,128]{2,1,0:T(8,128)(2,1)S(1)} %joint.7), channel_id=1, source_target_pairs={{0,16},{1,17},{2,18},{3,19},{4,8},{5,9},{6,10},{7,11},{8,4},{9,5},... | collective-permute-start | bytes 393224 | tf_op jit(solution)/shard_map/ppermute | solution.py:328
  28.3 6.6 %collective-permute-start.5 = (bf16[2,256,128]{2,1,0:T(8,128)(2,1)S(1)}, bf16[2,256,128]{2,1,0:T(8,128)(2,1)S(1)}, u32[]{:S(2)}, u32[]{:S(2)}) collective-permute-start(bf16[2,256,128]{2,1,0:T(8,128)(2,1)S(1)} %joint.4), channel_id=1, source_target_pairs={{0,16},{1,17},{2,18},{3,19},{4,8},{5,9},{6,10},{7,11},{8,4},{9,5},... | collective-permute-start | bytes 393224 | tf_op jit(solution)/shard_map/ppermute | solution.py:328
  30.2 7.4 %collective-permute-start.8 = (bf16[2,256,128]{2,1,0:T(8,128)(2,1)S(1)}, bf16[2,256,128]{2,1,0:T(8,128)(2,1)S(1)}, u32[]{:S(2)}, u32[]{:S(2)}) collective-permute-start(bf16[2,256,128]{2,1,0:T(8,128)(2,1)S(1)} %joint.5), channel_id=1, source_target_pairs={{0,16},{1,17},{2,18},{3,19},{4,8},{5,9},{6,10},{7,11},{8,4},{9,5},... | collective-permute-start | bytes 393224 | tf_op jit(solution)/shard_map/ppermute | solution.py:328
  30.3 8.6 %collective-permute-start.18 = (bf16[256,128]{1,0:T(8,128)(2,1)S(1)}, bf16[256,128]{1,0:T(8,128)(2,1)S(1)}, u32[]{:S(2)}, u32[]{:S(2)}) collective-permute-start(bf16[256,128]{1,0:T(8,128)(2,1)S(1)} %near.6), channel_id=1, source_target_pairs={{0,4},{1,5},{2,6},{3,7},{4,0},{5,1},{6,2},{7,3},{8,12},{9,13},{10,... | collective-permute-start | bytes 196616 | tf_op jit(solution)/shard_map/ppermute | solution.py:328
  33.5 5.4 %collective-permute-start.21 = (bf16[256,128]{1,0:T(8,128)(2,1)S(1)}, bf16[256,128]{1,0:T(8,128)(2,1)S(1)}, u32[]{:S(2)}, u32[]{:S(2)}) collective-permute-start(bf16[256,128]{1,0:T(8,128)(2,1)S(1)} %near.7), channel_id=1, source_target_pairs={{0,4},{1,5},{2,6},{3,7},{4,0},{5,1},{6,2},{7,3},{8,12},{9,13},{10,... | collective-permute-start | bytes 196616 | tf_op jit(solution)/shard_map/ppermute | solution.py:328
  34.9 7.6 %collective-permute-start.6 = (bf16[256,128]{1,0:T(8,128)(2,1)S(1)}, bf16[256,128]{1,0:T(8,128)(2,1)S(1)}, u32[]{:S(2)}, u32[]{:S(2)}) collective-permute-start(bf16[256,128]{1,0:T(8,128)(2,1)S(1)} %near.4), channel_id=1, source_target_pairs={{0,4},{1,5},{2,6},{3,7},{4,0},{5,1},{6,2},{7,3},{8,12},{9,13},{10,... | collective-permute-start | bytes 196616 | tf_op jit(solution)/shard_map/ppermute | solution.py:328
  37.6 5.0 %collective-permute-start.9 = (bf16[256,128]{1,0:T(8,128)(2,1)S(1)}, bf16[256,128]{1,0:T(8,128)(2,1)S(1)}, u32[]{:S(2)}, u32[]{:S(2)}) collective-permute-start(bf16[256,128]{1,0:T(8,128)(2,1)S(1)} %near.5), channel_id=1, source_target_pairs={{0,4},{1,5},{2,6},{3,7},{4,0},{5,1},{6,2},{7,3},{8,12},{9,13},{10,... | collective-permute-start | bytes 196616 | tf_op jit(solution)/shard_map/ppermute | solution.py:328
  39.0 5.7 %collective-permute-start.22 = (bf16[128,256]{1,0:T(8,128)(2,1)S(1)}, bf16[128,256]{1,0:T(8,128)(2,1)S(1)}, u32[]{:S(2)}, u32[]{:S(2)}) collective-permute-start(bf16[128,256]{1,0:T(8,128)(2,1)S(1)} %get-tuple-element.42.refs_1_), channel_id=1, source_target_pairs={{0,1},{1,0},{2,3},{3,2},{4,5},{5,4},{6,7},{7,6},{8,9},{9,8},{10,11... | collective-permute-start | bytes 196616 | tf_op jit(solution)/shard_map/ppermute | solution.py:328
  39.9 6.3 %collective-permute-start.24 = (bf16[128,256]{1,0:T(8,128)(2,1)S(1)}, bf16[128,256]{1,0:T(8,128)(2,1)S(1)}, u32[]{:S(2)}, u32[]{:S(2)}) collective-permute-start(bf16[128,256]{1,0:T(8,128)(2,1)S(1)} %get-tuple-element.43), channel_id=1, source_target_pairs={{0,2},{1,3},{2,0},{3,1},{4,6},{5,7},{6,4},{7,5},{8,10},{9,11},{10,... | collective-permute-start | bytes 196616 | tf_op jit(solution)/shard_map/ppermute | solution.py:328
  41.1 5.4 %collective-permute-start.23 = (bf16[128,256]{1,0:T(8,128)(2,1)S(1)}, bf16[128,256]{1,0:T(8,128)(2,1)S(1)}, u32[]{:S(2)}, u32[]{:S(2)}) collective-permute-start(bf16[128,256]{1,0:T(8,128)(2,1)S(1)} %get-tuple-element.43), channel_id=1, source_target_pairs={{0,3},{1,2},{2,1},{3,0},{4,7},{5,6},{6,5},{7,4},{8,11},{9,10},{10,... | collective-permute-start | bytes 196616 | tf_op jit(solution)/shard_map/ppermute | solution.py:328
  42.6 4.4 %collective-permute-start.10 = (bf16[128,256]{1,0:T(8,128)(2,1)S(1)}, bf16[128,256]{1,0:T(8,128)(2,1)S(1)}, u32[]{:S(2)}, u32[]{:S(2)}) collective-permute-start(bf16[128,256]{1,0:T(8,128)(2,1)S(1)} %get-tuple-element.33.refs_1_), channel_id=1, source_target_pairs={{0,1},{1,0},{2,3},{3,2},{4,5},{5,4},{6,7},{7,6},{8,9},{9,8},{10,11... | collective-permute-start | bytes 196616 | tf_op jit(solution)/shard_map/ppermute | solution.py:328
  43.5 7.0 %copy-start.2 = (bf16[4,1024,512]{2,1,0:T(8,128)(2,1)S(1)}, bf16[4,1024,512]{2,1,0:T(8,128)(2,1)}, u32[]{:S(2)}) copy-start(bf16[4,1024,512]{2,1,0:T(8,128)(2,1)} %refs_2_.3) | copy-start | bytes 12582916
  43.5 7.0 %copy-start.3 = (s32[1,4]{1,0:T(1,128)S(1)}, s32[1,4]{1,0:T(1,128)}, u32[]{:S(2)}) copy-start(s32[1,4]{1,0:T(1,128)} %refs_0_.9) | copy-start | bytes 52
  43.5 4.3 %collective-permute-start.12 = (bf16[128,256]{1,0:T(8,128)(2,1)S(1)}, bf16[128,256]{1,0:T(8,128)(2,1)S(1)}, u32[]{:S(2)}, u32[]{:S(2)}) collective-permute-start(bf16[128,256]{1,0:T(8,128)(2,1)S(1)} %get-tuple-element.34), channel_id=1, source_target_pairs={{0,2},{1,3},{2,0},{3,1},{4,6},{5,7},{6,4},{7,5},{8,10},{9,11},{10,... | collective-permute-start | bytes 196616 | tf_op jit(solution)/shard_map/ppermute | solution.py:328
  44.7 5.2 %collective-permute-start.11 = (bf16[128,256]{1,0:T(8,128)(2,1)S(1)}, bf16[128,256]{1,0:T(8,128)(2,1)S(1)}, u32[]{:S(2)}, u32[]{:S(2)}) collective-permute-start(bf16[128,256]{1,0:T(8,128)(2,1)S(1)} %get-tuple-element.34), channel_id=1, source_target_pairs={{0,3},{1,2},{2,1},{3,0},{4,7},{5,6},{6,5},{7,4},{8,11},{9,10},{10,... | collective-permute-start | bytes 196616 | tf_op jit(solution)/shard_map/ppermute | solution.py:328
  47.0 3.5 %collective-permute-start.25 = (bf16[128,1024]{1,0:T(8,128)(2,1)S(1)}, bf16[128,1024]{1,0:T(8,128)(2,1)S(1)}, u32[]{:S(2)}, u32[]{:S(2)}) collective-permute-start(bf16[128,1024]{1,0:T(8,128)(2,1)S(1)} %phase.3.refs_2_), channel_id=1, source_target_pairs={{0,16},{1,17},{2,18},{3,19},{4,20},{5,21},{6,22},{7,23},{8,24},{9,... | collective-permute-start | bytes 786440 | tf_op jit(solution)/shard_map/ppermute | solution.py:328
  50.4 1.1 %copy-start.5 = (s32[16]{0:T(128)S(1)}, s32[16]{0:T(128)}, u32[]{:S(2)}) copy-start(s32[16]{0:T(128)} %refs_1_.3) | copy-start | bytes 196
  50.4 2.1 %collective-permute-start.26 = (bf16[128,1024]{1,0:T(8,128)(2,1)S(1)}, bf16[128,1024]{1,0:T(8,128)(2,1)S(1)}, u32[]{:S(2)}, u32[]{:S(2)}) collective-permute-start(bf16[128,1024]{1,0:T(8,128)(2,1)S(1)} %phase.2.refs_3_), channel_id=1, source_target_pairs={{0,16},{1,17},{2,18},{3,19},{4,20},{5,21},{6,22},{7,23},{8,24},{9,... | collective-permute-start | bytes 786440 | tf_op jit(solution)/shard_map/ppermute | solution.py:328

commit v11 on v10

--- a/solution.py
+++ b/solution.py
@@ -98,14 +98,6 @@
     return lax.axis_index("dist"), device // inner, device % inner
 
 
-def take_kernel(holo, after, out, arrived):
-    own = out.shape[0]
-    core = lax.axis_index("dist")
-    copy = pltpu.make_async_copy(holo.at[pl.ds(core * own, own)], out, arrived)
-    copy.start()
-    copy.wait()
-
-
 def row_kernel(inner, chunk, here, there, table, *outs):
     core, _, spot = position(inner)
     own, dist_dev, rows_dev, width = here.shape
@@ -121,13 +113,16 @@
 
 
 def whole_turns(scale, square):
-    turns = scale * square * (0.5 / math.pi)
+    turns = scale * square
     return (turns - jnp.round(turns)) * (2.0 * math.pi)
 
 
-def filter_kernel(inner, dist_dev, propagation, after, out):
+def filter_kernel(inner, turns, holo, out, mine, arrived):
     dists, width, block = out.shape
+    own, dist_dev = mine.shape[:2]
     core, _, spot = position(inner)
+    copy = pltpu.make_async_copy(holo.at[pl.ds(core * own, own)], mine, arrived)
+    copy.start()
 
     def square(first, length):
         index = lax.broadcasted_iota(jnp.int32, (1, length), 1) + first
@@ -139,7 +134,7 @@
         rows = []
         for d in range(dists):
             other = d // dist_dev
-            scale = propagation[(core ^ other) * dist_dev + d % dist_dev]
+            scale = turns[(core ^ other) * dist_dev + d % dist_dev]
             rows.append(whole_turns(scale, values))
         return jnp.concatenate(rows, axis=0)
 
@@ -163,6 +158,7 @@
         scale = 1.0 / (denom + regularizer)
         for d in range(dists):
             out[d, at : at + step, :] = (transfer[d] * scale).astype(bf16)
+    copy.wait()
 
 
 def column_kernel(inner, outer, table, gain, *refs):
@@ -243,23 +239,18 @@
     out[...] = jnp.dot(joined[...], table[...], preferred_element_type=f32).astype(bf16)
 
 
-def recon_kernel(own, chunk, cores, order, weights, *refs):
+def recon_kernel(own, order, slabs, weights, *refs):
+    phases = refs[: 2 * own - 1]
+    out, chosen, select = refs[2 * own - 1 :]
     core = lax.axis_index("dist")
-    phases, out = refs[: len(cores)], refs[-1]
+    device = lax.axis_index("rows")
     total = None
-    for other, phase in zip(cores, phases):
-        chosen = weights[order[0, (core ^ other) * own + chunk]]
-        got = jnp.dot(phase[...], chosen, preferred_element_type=f32)
+    for step, phase in enumerate(phases):
+        here = weights[order[0, (core ^ (step % 2)) * own + step // 2]]
+        got = jnp.dot(phase[...], here, preferred_element_type=f32)
         total = got if total is None else total + got
     out[...] = total
-
-
-def recon_next_kernel(own, chunk, order, slabs, weights, phase, before, out, chosen, select):
-    core = lax.axis_index("dist")
-    device = lax.axis_index("rows")
-    here = weights[order[0, core * own + chunk]]
-    out[...] = before[...] + jnp.dot(phase[...], here, preferred_element_type=f32)
-    chosen[...] = weights[order[0, (core ^ 1) * own + chunk]]
+    chosen[...] = weights[order[0, (core ^ 1) * own + own - 1]]
     parity = device % 2
     offset = parity * slabs[device - parity]
     slot = lax.broadcasted_iota(jnp.int32, select.shape, 0)
@@ -309,10 +300,7 @@
     params = pltpu.CompilerParams(vmem_limit_bytes=16 * 2**20)
     one_out = pl.BlockSpec(memory_space=pltpu.VMEM)
 
-    def cost(flops, *arrays):
-        return pl.CostEstimate(
-            flops=flops, bytes_accessed=sum(2 * math.prod(a) for a in arrays), transcendentals=0
-        )
+    cheap = pl.CostEstimate(flops=1, bytes_accessed=1, transcendentals=0)
 
     def shaped(*shape):
         return jax.ShapeDtypeStruct(shape, bf16)
@@ -344,16 +332,19 @@
         return (c, (3 - z) * inner + r % inner) if z in (1, 2) else (c ^ 1, r)
 
     partner = sent(holograms[0], to_other_core)
-    mine = pl.pallas_call(
-        take_kernel,
-        out_shape=shaped(own, dist_dev, rows_dev, width),
-        in_specs=in_hbm(1) + vmem(1),
-        out_specs=one_out,
+    gain, mine = pl.pallas_call(
+        lambda *refs: filter_kernel(inner, *refs),
+        out_shape=[
+            shaped(dists, width, block),
+            shaped(own, dist_dev, rows_dev, width),
+        ],
+        in_specs=smem(1) + in_hbm(1),
+        out_specs=vmem(2),
         scratch_shapes=[pltpu.SemaphoreType.DMA],
         compiler_params=params,
-        cost_estimate=cost(1, (8, width)),
-        name="take",
-    )(from_hbm(holograms[0]), table)
+        cost_estimate=cheap,
+        name="filters",
+    )(propagation * (0.5 / math.pi), from_hbm(holograms[0]))
     arrived = []
     for chunk in range(own):
         pieces = pl.pallas_call(
@@ -362,22 +353,10 @@
             in_specs=vmem(3),
             out_specs=vmem(inner),
             compiler_params=params,
-            cost_estimate=cost(
-                2 * dists * rows_dev * width * width, (width, width), (2, dists, rows_dev, width)
-            ),
+            cost_estimate=cheap,
             name="row_spectra",
         )(mine, partner, table)
         arrived.append(spread(pieces, send_order))
-
-    gain = pl.pallas_call(
-        lambda *refs: filter_kernel(inner, dist_dev, *refs),
-        out_shape=shaped(dists, width, block),
-        in_specs=smem(1) + unread(1),
-        out_specs=one_out,
-        compiler_params=params,
-        cost_estimate=cost(32 * width * block, (dists, width, block)),
-        name="filters",
-    )(propagation, pieces[0])
 
     sums = []
     for chunk in range(own):
@@ -393,9 +372,7 @@
                 pltpu.VMEM((width, block), bf16),
             ],
             compiler_params=params,
-            cost_estimate=cost(
-                2 * width * block * (dists * depth + width), (width, width), (dists, width, block)
-            ),
+            cost_estimate=cheap,
             name="columns",
         )(table, gain, *arrived[chunk])
         parts = [keep]
@@ -406,7 +383,7 @@
                 in_specs=vmem(2),
                 out_specs=one_out,
                 compiler_params=params,
-                cost_estimate=cost(1, (8, width)),
+                cost_estimate=cheap,
                 name="joint",
             )(away[split], sent(away[split], to_near_plane))
             across = sent(joint, to_middle)
@@ -416,13 +393,13 @@
                 in_specs=vmem(2),
                 out_specs=one_out,
                 compiler_params=params,
-                cost_estimate=cost(1, (8, width)),
+                cost_estimate=cheap,
                 name="near",
             )(keep, across)
             parts += [across, sent(near, to_near_plane)]
         sums.append(parts)
 
-    total = None
+    phases = []
     for chunk in range(own):
         first, second = pl.pallas_call(
             lambda *refs: half_kernel(inner, *refs),
@@ -430,7 +407,7 @@
             in_specs=vmem(1 + 2 * splits),
             out_specs=vmem(2),
             compiler_params=params,
-            cost_estimate=cost(1, (8, width)),
+            cost_estimate=cheap,
             name="half",
         )(*sums[chunk])
         pieces = spread([first, first, second, second], tail_order)
@@ -441,44 +418,33 @@
             out_specs=one_out,
             scratch_shapes=[pltpu.VMEM((capacity, width), bf16)],
             compiler_params=params,
-            cost_estimate=cost(1, (8, width)),
+            cost_estimate=cheap,
             name="phase",
         )(table, *pieces)
-        there = sent(phase, to_other_core)
-        if chunk < own - 1:
-            total = pl.pallas_call(
-                lambda *refs, chunk=chunk: recon_kernel(own, chunk, (0, 1), *refs),
-                out_shape=jax.ShapeDtypeStruct((capacity, pixels), f32),
-                in_specs=smem(1) + vmem(3),
-                out_specs=one_out,
-                compiler_params=params,
-                cost_estimate=cost(1, (8, width)),
-                name="recon",
-            )(angle_order, weights, phase, there)
-        else:
-            total, chosen, select = pl.pallas_call(
-                lambda *refs, chunk=chunk: recon_next_kernel(own, chunk, *refs),
-                out_shape=[
-                    jax.ShapeDtypeStruct((capacity, pixels), f32),
-                    shaped(width, pixels),
-                    shaped(capacity, capacity),
-                ],
-                in_specs=smem(2) + vmem(3),
-                out_specs=vmem(3),
-                compiler_params=params,
-                cost_estimate=cost(1, (8, width)),
-                name="recon",
-            )(angle_order, slab_rows, weights, phase, total)
-            total = pl.pallas_call(
-                recon_last_kernel,
-                out_shape=shaped(capacity, pixels),
-                in_specs=vmem(4),
-                out_specs=one_out,
-                compiler_params=params,
-                cost_estimate=cost(1, (8, width)),
-                name="recon",
-            )(chosen, there, total, select)
-    return total
+        phases += [phase, sent(phase, to_other_core)]
+
+    total, chosen, select = pl.pallas_call(
+        lambda *refs: recon_kernel(own, *refs),
+        out_shape=[
+            jax.ShapeDtypeStruct((capacity, pixels), f32),
+            shaped(width, pixels),
+            shaped(capacity, capacity),
+        ],
+        in_specs=smem(2) + vmem(2 * own),
+        out_specs=vmem(3),
+        compiler_params=params,
+        cost_estimate=cheap,
+        name="recon",
+    )(angle_order, slab_rows, weights, *phases[:-1])
+    return pl.pallas_call(
+        recon_last_kernel,
+        out_shape=shaped(capacity, pixels),
+        in_specs=vmem(4),
+        out_specs=one_out,
+        compiler_params=params,
+        cost_estimate=cheap,
+        name="recon",
+    )(chosen, phases[-1], total, select)
 
 
 def on_device(holograms, propagation, weights, angle_order, slab_rows):

time: 53.9 us -> 54.9 us (1.019)
  waiting for transfers between devices: 9.87 us -> 11.9 us
  Pallas kernels: 11.9 us -> 10.1 us
  other arithmetic: 0 us -> 0.66 us
    ppermute x27, waiting for transfers between devices: 9.87 us -> 11.9 us  [sent(): return lax.ppermute(value, ('dist', 'rows'), pairs)]
    pallas_call x4 -> x2, Pallas kernels: 5.38 us -> 3.58 us  [the longest x1 2.38 us: plane_plan(): pl.pallas_call(lambda *refs: filter_kernel(inner, *refs), out_shape=[shap...]
    mul x0 -> x1, other arithmetic: none -> 0.66 us  [plane_plan(): propagation * (0.5 / math.pi)]
    unnamed x12 -> x10, local copies, waits for them, and re-layouts: 1.61 us -> 1.6 us
  transfers between devices with their start and end apart: 27 -> 27, of which waited for: 7 -> 9; matrix products, arithmetic and copies ran while one was open for 0% -> 1% of each run, Pallas kernels for 19% -> 15%
where the time goes in v11:
time: 54.9 us; the launch traced here: 54.8 us
  starting transfers between devices  30.3 us (55%)
  waiting for transfers between devices  11.9 us (22%)
  Pallas kernels  10.1 us (18%)
  local copies, waits for them, and re-layouts  1.6 us (3%)
  other arithmetic  0.66 us (1%)
    ppermute x27, starting transfers between devices, sent(): return lax.ppermute(value, ('dist', 'rows'), pairs)  30.3 us
    ppermute x27, waiting for transfers between devices, sent(): return lax.ppermute(value, ('dist', 'rows'), pairs)  11.9 us
    pallas_call x2, Pallas kernels, plane_plan(): pl.pallas_call(lambda *refs: column_kernel(inner, outer, *refs), out_shap...  2.59 us
    pallas_call x1, Pallas kernels, plane_plan(): pl.pallas_call(lambda *refs: filter_kernel(inner, *refs), out_shape=[shap...  2.38 us
    unnamed x10, local copies, waits for them, and re-layouts  1.6 us
    pallas_call x2, Pallas kernels, plane_plan(): pl.pallas_call(lambda *refs, chunk=chunk: row_kernel(inner, chunk, *refs)...  1.5 us
    pallas_call x1, Pallas kernels, plane_plan(): pl.pallas_call(lambda *refs: recon_kernel(own, *refs), out_shape=[jax.Sha...  1.2 us
    pallas_call x1, Pallas kernels, plane_plan(): pl.pallas_call(recon_last_kernel, out_shape=shaped(capacity, pixels), in_...  1.12 us
  transfers between devices with their start and end apart: 27, of which 9 were waited for; matrix products, arithmetic and copies ran while one was open for 1% of the time, Pallas kernels for 15%

profile of v11, /device:TPU:0, one launch (start us, length us, event | category | flops | bytes accessed | tf_op | source)
XLA Modules:
  0.0 54.8 jit_solution(13721479612168211357)
XLA Ops:
  0.0 0.5 collective-permute-start
  0.5 0.7 %broadcast_multiply_fusion.refs_0_ = f32[4]{0:T(128)S(1)} fusion(f32[4]{0:T(128)} %param.7), kind=kLoop, calls=%fused_computation | loop fusion | flops 4 | bytes 32 | tf_op jit(solution)/shard_map/mul | solution.py:347
  1.1 2.4 %filters.1 = (bf16[4,1024,256]{2,1,0:T(8,128)(2,1)S(1)}, bf16[2,2,64,1024]{3,2,1,0:T(8,128)(2,1)S(1)}) custom-call(f32[4]{0:T(128)S(1)} %broadcast_multiply_fusion.refs_0_, bf16[4,2,64,1024]{3,2,1,0:T(8,128)(2,1)} %bitcast.2), custom_call_target="tpu_custom_call" | custom-call | flops 1 | bytes 1 | tf_op jit(solution)/shard_map/filters/pallas_call | solution.py:335
  3.5 0.0 collective-permute-done.refs_1_
  3.5 0.0 copy-start
  3.5 1.6 %copy-done = bf16[1024,1024]{1,0:T(8,128)(2,1)S(1)} copy-done((bf16[1024,1024]{1,0:T(8,128)(2,1)S(1)}, bf16[1024,1024]{1,0:T(8,128)(2,1)}, u32[]{:S(2)}) %copy-start) | copy-done | bytes 2097176
  5.1 0.7 %row_spectra.2 = (bf16[4,64,256]{2,1,0:T(8,128)(2,1)S(1)}, bf16[4,64,256]{2,1,0:T(8,128)(2,1)S(1)}, bf16[4,64,256]{2,1,0:T(8,128)(2,1)S(1)}, bf16[4,64,256]{2,1,0:T(8,128)(2,1)S(1)}) custom-call(bf16[2,2,64,1024]{3,2,1,0:T(8,128)(2,1)S(1)} %get-tuple-element.29.refs_0_, bf16[4,2,64,1024]{3,2,1,0:T(8,128)(2,1)S(1)} %collective-permute-done.refs_1_, ...), custom_call_target="tpu_custom_call" | custom-call | flops 1 | bytes 1 | tf_op jit(solution)/shard_map/row_spectra/pallas_call | solution.py:350
  5.9 0.0 copy-start.1
  5.9 2.5 %collective-permute-start.1 = (bf16[4,64,256]{2,1,0:T(8,128)(2,1)S(1)}, bf16[4,64,256]{2,1,0:T(8,128)(2,1)S(1)}, u32[]{:S(2)}, u32[]{:S(2)}) collective-permute-start(bf16[4,64,256]{2,1,0:T(8,128)(2,1)S(1)} %get-tuple-element.31), channel_id=1, source_target_pairs={{0,1},{1,0},{2,3},{3,2},{4,5},{5,4},{6,7},{7,6},{8,9},{9,8},{10,11... | collective-permute-start | bytes 393224 | tf_op jit(solution)/shard_map/ppermute | solution.py:316
  8.4 1.5 %collective-permute-start.2 = (bf16[4,64,256]{2,1,0:T(8,128)(2,1)S(1)}, bf16[4,64,256]{2,1,0:T(8,128)(2,1)S(1)}, u32[]{:S(2)}, u32[]{:S(2)}) collective-permute-start(bf16[4,64,256]{2,1,0:T(8,128)(2,1)S(1)} %get-tuple-element.32), channel_id=1, source_target_pairs={{0,2},{1,3},{2,0},{3,1},{4,6},{5,7},{6,4},{7,5},{8,10},{9,11},{10,... | collective-permute-start | bytes 393224 | tf_op jit(solution)/shard_map/ppermute | solution.py:316
  9.9 0.0 collective-permute-start.3
  10.0 0.7 %row_spectra.3 = (bf16[4,64,256]{2,1,0:T(8,128)(2,1)S(1)}, bf16[4,64,256]{2,1,0:T(8,128)(2,1)S(1)}, bf16[4,64,256]{2,1,0:T(8,128)(2,1)S(1)}, bf16[4,64,256]{2,1,0:T(8,128)(2,1)S(1)}) custom-call(bf16[2,2,64,1024]{3,2,1,0:T(8,128)(2,1)S(1)} %get-tuple-element.29.refs_0_, bf16[4,2,64,1024]{3,2,1,0:T(8,128)(2,1)S(1)} %collective-permute-done.refs_1_, ...), custom_call_target="tpu_custom_call" | custom-call | flops 1 | bytes 1 | tf_op jit(solution)/shard_map/row_spectra/pallas_call | solution.py:350
  10.7 2.0 %collective-permute-start.14 = (bf16[4,64,256]{2,1,0:T(8,128)(2,1)S(1)}, bf16[4,64,256]{2,1,0:T(8,128)(2,1)S(1)}, u32[]{:S(2)}, u32[]{:S(2)}) collective-permute-start(bf16[4,64,256]{2,1,0:T(8,128)(2,1)S(1)} %get-tuple-element.40), channel_id=1, source_target_pairs={{0,1},{1,0},{2,3},{3,2},{4,5},{5,4},{6,7},{7,6},{8,9},{9,8},{10,11... | collective-permute-start | bytes 393224 | tf_op jit(solution)/shard_map/ppermute | solution.py:316
  12.7 1.5 %collective-permute-start.15 = (bf16[4,64,256]{2,1,0:T(8,128)(2,1)S(1)}, bf16[4,64,256]{2,1,0:T(8,128)(2,1)S(1)}, u32[]{:S(2)}, u32[]{:S(2)}) collective-permute-start(bf16[4,64,256]{2,1,0:T(8,128)(2,1)S(1)} %get-tuple-element.41), channel_id=1, source_target_pairs={{0,2},{1,3},{2,0},{3,1},{4,6},{5,7},{6,4},{7,5},{8,10},{9,11},{10,... | collective-permute-start | bytes 393224 | tf_op jit(solution)/shard_map/ppermute | solution.py:316
  14.2 0.0 collective-permute-done.1.refs_3_
  14.2 1.4 %collective-permute-start.16 = (bf16[4,64,256]{2,1,0:T(8,128)(2,1)S(1)}, bf16[4,64,256]{2,1,0:T(8,128)(2,1)S(1)}, u32[]{:S(2)}, u32[]{:S(2)}) collective-permute-start(bf16[4,64,256]{2,1,0:T(8,128)(2,1)S(1)} %get-tuple-element.42), channel_id=1, source_target_pairs={{0,3},{1,2},{2,1},{3,0},{4,7},{5,6},{6,5},{7,4},{8,11},{9,10},{10,... | collective-permute-start | bytes 393224 | tf_op jit(solution)/shard_map/ppermute | solution.py:316
  15.7 0.9 %collective-permute-done.2.refs_4_ = bf16[4,64,256]{2,1,0:T(8,128)(2,1)S(1)} collective-permute-done((bf16[4,64,256]{2,1,0:T(8,128)(2,1)S(1)}, bf16[4,64,256]{2,1,0:T(8,128)(2,1)S(1)}, u32[]{:S(2)}, u32[]{:S(2)}) %collective-permute-start.2) | collective-permute-done | bytes 131104 | tf_op jit(solution)/shard_map/ppermute | solution.py:316
  16.6 0.7 %collective-permute-done.3.refs_5_ = bf16[4,64,256]{2,1,0:T(8,128)(2,1)S(1)} collective-permute-done((bf16[4,64,256]{2,1,0:T(8,128)(2,1)S(1)}, bf16[4,64,256]{2,1,0:T(8,128)(2,1)S(1)}, u32[]{:S(2)}, u32[]{:S(2)}) %collective-permute-start.3) | collective-permute-done | bytes 131104 | tf_op jit(solution)/shard_map/ppermute | solution.py:316
  17.3 1.3 %columns.2 = (bf16[2,256,256]{2,1,0:T(8,128)(2,1)S(1)}, bf16[2,256,128]{2,1,0:T(8,128)(2,1)S(1)}, bf16[2,256,128]{2,1,0:T(8,128)(2,1)S(1)}) custom-call(bf16[1024,1024]{1,0:T(8,128)(2,1)S(1)} %copy-done.1, bf16[4,1024,256]{2,1,0:T(8,128)(2,1)S(1)} %get-tuple-element.28.refs_1_, bf16[4,64,256]{2,1,0:T(8,128)(2,1)S(1)} %get-tuple-element.30.refs_2_, ...), custom_call_target="tpu_custom_call" | custom-call | flops 1 | bytes 1 | tf_op jit(solution)/shard_map/columns/pallas_call | solution.py:363
  18.6 1.7 %collective-permute-start.7 = (bf16[2,256,128]{2,1,0:T(8,128)(2,1)S(1)}, bf16[2,256,128]{2,1,0:T(8,128)(2,1)S(1)}, u32[]{:S(2)}, u32[]{:S(2)}) collective-permute-start(bf16[2,256,128]{2,1,0:T(8,128)(2,1)S(1)} %get-tuple-element.36.one), channel_id=1, source_target_pairs={{0,4},{1,5},{2,6},{3,7},{4,0},{5,1},{6,2},{7,3},{8,12},{9,13},{10,... | collective-permute-start | bytes 393224 | tf_op jit(solution)/shard_map/ppermute | solution.py:316
  20.3 0.4 collective-permute-start.4
  20.7 1.8 %collective-permute-done.15.refs_4_ = bf16[4,64,256]{2,1,0:T(8,128)(2,1)S(1)} collective-permute-done((bf16[4,64,256]{2,1,0:T(8,128)(2,1)S(1)}, bf16[4,64,256]{2,1,0:T(8,128)(2,1)S(1)}, u32[]{:S(2)}, u32[]{:S(2)}) %collective-permute-start.15) | collective-permute-done | bytes 131104 | tf_op jit(solution)/shard_map/ppermute | solution.py:316
  22.5 1.3 %columns.3 = (bf16[2,256,256]{2,1,0:T(8,128)(2,1)S(1)}, bf16[2,256,128]{2,1,0:T(8,128)(2,1)S(1)}, bf16[2,256,128]{2,1,0:T(8,128)(2,1)S(1)}) custom-call(bf16[1024,1024]{1,0:T(8,128)(2,1)S(1)} %copy-done.1, bf16[4,1024,256]{2,1,0:T(8,128)(2,1)S(1)} %get-tuple-element.28.refs_1_, bf16[4,64,256]{2,1,0:T(8,128)(2,1)S(1)} %get-tuple-element.39.refs_2_, ...), custom_call_target="tpu_custom_call" | custom-call | flops 1 | bytes 1 | tf_op jit(solution)/shard_map/columns/pallas_call | solution.py:363
  23.8 1.6 %collective-permute-start.20 = (bf16[2,256,128]{2,1,0:T(8,128)(2,1)S(1)}, bf16[2,256,128]{2,1,0:T(8,128)(2,1)S(1)}, u32[]{:S(2)}, u32[]{:S(2)}) collective-permute-start(bf16[2,256,128]{2,1,0:T(8,128)(2,1)S(1)} %get-tuple-element.45.one), channel_id=1, source_target_pairs={{0,4},{1,5},{2,6},{3,7},{4,0},{5,1},{6,2},{7,3},{8,12},{9,13},{10,... | collective-permute-start | bytes 393224 | tf_op jit(solution)/shard_map/ppermute | solution.py:316
  25.4 0.5 collective-permute-start.17
  25.9 0.0 collective-permute-done.7.two
  25.9 0.1 collective-permute-start.8
  26.0 0.0 collective-permute-done.4.two
  26.1 0.5 %collective-permute-start.5 = (bf16[2,256,128]{2,1,0:T(8,128)(2,1)S(1)}, bf16[2,256,128]{2,1,0:T(8,128)(2,1)S(1)}, u32[]{:S(2)}, u32[]{:S(2)}) collective-permute-start(bf16[2,256,128]{2,1,0:T(8,128)(2,1)S(1)} %joint.4), channel_id=1, source_target_pairs={{0,16},{1,17},{2,18},{3,19},{4,8},{5,9},{6,10},{7,11},{8,4},{9,5},... | collective-permute-start | bytes 393224 | tf_op jit(solution)/shard_map/ppermute | solution.py:316
  26.6 3.6 %collective-permute-done.20.two = bf16[2,256,128]{2,1,0:T(8,128)(2,1)S(1)} collective-permute-done((bf16[2,256,128]{2,1,0:T(8,128)(2,1)S(1)}, bf16[2,256,128]{2,1,0:T(8,128)(2,1)S(1)}, u32[]{:S(2)}, u32[]{:S(2)}) %collective-permute-start.20) | collective-permute-done | bytes 131104 | tf_op jit(solution)/shard_map/ppermute | solution.py:316
  30.3 0.1 collective-permute-start.21
  30.3 1.8 %collective-permute-done.17.two = bf16[2,256,128]{2,1,0:T(8,128)(2,1)S(1)} collective-permute-done((bf16[2,256,128]{2,1,0:T(8,128)(2,1)S(1)}, bf16[2,256,128]{2,1,0:T(8,128)(2,1)S(1)}, u32[]{:S(2)}, u32[]{:S(2)}) %collective-permute-start.17) | collective-permute-done | bytes 131104 | tf_op jit(solution)/shard_map/ppermute | solution.py:316
  32.1 0.1 collective-permute-start.18
  32.2 0.0 collective-permute-done.8.refs_1_.refs_3_
  32.3 3.2 %collective-permute-start.9 = (bf16[256,128]{1,0:T(8,128)(2,1)S(1)}, bf16[256,128]{1,0:T(8,128)(2,1)S(1)}, u32[]{:S(2)}, u32[]{:S(2)}) collective-permute-start(bf16[256,128]{1,0:T(8,128)(2,1)S(1)} %near.5), channel_id=1, source_target_pairs={{0,4},{1,5},{2,6},{3,7},{4,0},{5,1},{6,2},{7,3},{8,12},{9,13},{10,... | collective-permute-start | bytes 196616 | tf_op jit(solution)/shard_map/ppermute | solution.py:316
  35.5 1.4 %collective-permute-start.6 = (bf16[256,128]{1,0:T(8,128)(2,1)S(1)}, bf16[256,128]{1,0:T(8,128)(2,1)S(1)}, u32[]{:S(2)}, u32[]{:S(2)}) collective-permute-start(bf16[256,128]{1,0:T(8,128)(2,1)S(1)} %near.4), channel_id=1, source_target_pairs={{0,4},{1,5},{2,6},{3,7},{4,0},{5,1},{6,2},{7,3},{8,12},{9,13},{10,... | collective-permute-start | bytes 196616 | tf_op jit(solution)/shard_map/ppermute | solution.py:316
  36.9 0.0 collective-permute-done.21.refs_1_.refs_3_
  36.9 2.6 %collective-permute-start.22 = (bf16[256,128]{1,0:T(8,128)(2,1)S(1)}, bf16[256,128]{1,0:T(8,128)(2,1)S(1)}, u32[]{:S(2)}, u32[]{:S(2)}) collective-permute-start(bf16[256,128]{1,0:T(8,128)(2,1)S(1)} %near.7), channel_id=1, source_target_pairs={{0,4},{1,5},{2,6},{3,7},{4,0},{5,1},{6,2},{7,3},{8,12},{9,13},{10,... | collective-permute-start | bytes 196616 | tf_op jit(solution)/shard_map/ppermute | solution.py:316
  39.5 0.0 collective-permute-done.18.refs_1_
  39.6 1.4 %collective-permute-start.19 = (bf16[256,128]{1,0:T(8,128)(2,1)S(1)}, bf16[256,128]{1,0:T(8,128)(2,1)S(1)}, u32[]{:S(2)}, u32[]{:S(2)}) collective-permute-start(bf16[256,128]{1,0:T(8,128)(2,1)S(1)} %near.6), channel_id=1, source_target_pairs={{0,4},{1,5},{2,6},{3,7},{4,0},{5,1},{6,2},{7,3},{8,12},{9,13},{10,... | collective-permute-start | bytes 196616 | tf_op jit(solution)/shard_map/ppermute | solution.py:316
  40.9 0.0 collective-permute-done.9.refs_4_
  40.9 0.0 collective-permute-done.6.refs_2_
  40.9 0.1 half.2
  41.0 1.0 %collective-permute-start.10 = (bf16[128,256]{1,0:T(8,128)(2,1)S(1)}, bf16[128,256]{1,0:T(8,128)(2,1)S(1)}, u32[]{:S(2)}, u32[]{:S(2)}) collective-permute-start(bf16[128,256]{1,0:T(8,128)(2,1)S(1)} %get-tuple-element.37.refs_1_), channel_id=1, source_target_pairs={{0,1},{1,0},{2,3},{3,2},{4,5},{5,4},{6,7},{7,6},{8,9},{9,8},{10,11... | collective-permute-start | bytes 196616 | tf_op jit(solution)/shard_map/ppermute | solution.py:316
  42.1 1.4 %collective-permute-start.11 = (bf16[128,256]{1,0:T(8,128)(2,1)S(1)}, bf16[128,256]{1,0:T(8,128)(2,1)S(1)}, u32[]{:S(2)}, u32[]{:S(2)}) collective-permute-start(bf16[128,256]{1,0:T(8,128)(2,1)S(1)} %get-tuple-element.38), channel_id=1, source_target_pairs={{0,3},{1,2},{2,1},{3,0},{4,7},{5,6},{6,5},{7,4},{8,11},{9,10},{10,... | collective-permute-start | bytes 196616 | tf_op jit(solution)/shard_map/ppermute | solution.py:316
  43.5 1.1 %collective-permute-start.12 = (bf16[128,256]{1,0:T(8,128)(2,1)S(1)}, bf16[128,256]{1,0:T(8,128)(2,1)S(1)}, u32[]{:S(2)}, u32[]{:S(2)}) collective-permute-start(bf16[128,256]{1,0:T(8,128)(2,1)S(1)} %get-tuple-element.38), channel_id=1, source_target_pairs={{0,2},{1,3},{2,0},{3,1},{4,6},{5,7},{6,4},{7,5},{8,10},{9,11},{10,... | collective-permute-start | bytes 196616 | tf_op jit(solution)/shard_map/ppermute | solution.py:316
  44.6 0.0 collective-permute-done.22.refs_4_
  44.6 0.0 collective-permute-done.19.refs_2_
  44.6 0.1 half.3
  44.6 1.1 %collective-permute-start.23 = (bf16[128,256]{1,0:T(8,128)(2,1)S(1)}, bf16[128,256]{1,0:T(8,128)(2,1)S(1)}, u32[]{:S(2)}, u32[]{:S(2)}) collective-permute-start(bf16[128,256]{1,0:T(8,128)(2,1)S(1)} %get-tuple-element.46.refs_1_), channel_id=1, source_target_pairs={{0,1},{1,0},{2,3},{3,2},{4,5},{5,4},{6,7},{7,6},{8,9},{9,8},{10,11... | collective-permute-start | bytes 196616 | tf_op jit(solution)/shard_map/ppermute | solution.py:316
  45.7 1.4 %collective-permute-start.24 = (bf16[128,256]{1,0:T(8,128)(2,1)S(1)}, bf16[128,256]{1,0:T(8,128)(2,1)S(1)}, u32[]{:S(2)}, u32[]{:S(2)}) collective-permute-start(bf16[128,256]{1,0:T(8,128)(2,1)S(1)} %get-tuple-element.47), channel_id=1, source_target_pairs={{0,3},{1,2},{2,1},{3,0},{4,7},{5,6},{6,5},{7,4},{8,11},{9,10},{10,... | collective-permute-start | bytes 196616 | tf_op jit(solution)/shard_map/ppermute | solution.py:316
  47.1 0.0 collective-permute-done.10.refs_2_
  47.1 1.1 %collective-permute-start.25 = (bf16[128,256]{1,0:T(8,128)(2,1)S(1)}, bf16[128,256]{1,0:T(8,128)(2,1)S(1)}, u32[]{:S(2)}, u32[]{:S(2)}) collective-permute-start(bf16[128,256]{1,0:T(8,128)(2,1)S(1)} %get-tuple-element.47), channel_id=1, source_target_pairs={{0,2},{1,3},{2,0},{3,1},{4,6},{5,7},{6,4},{7,5},{8,10},{9,11},{10,... | collective-permute-start | bytes 196616 | tf_op jit(solution)/shard_map/ppermute | solution.py:316
  48.2 0.0 collective-permute-done.11.refs_3_
  48.2 0.6 %collective-permute-done.12.refs_4_ = bf16[128,256]{1,0:T(8,128)(2,1)S(1)} collective-permute-done((bf16[128,256]{1,0:T(8,128)(2,1)S(1)}, bf16[128,256]{1,0:T(8,128)(2,1)S(1)}, u32[]{:S(2)}, u32[]{:S(2)}) %collective-permute-start.12) | collective-permute-done | bytes 65568 | tf_op jit(solution)/shard_map/ppermute | solution.py:316
  48.9 0.5 phase.2.refs_3_
  49.3 0.1 collective-permute-start.13
  49.4 1.5 %collective-permute-done.24.refs_3_ = bf16[128,256]{1,0:T(8,128)(2,1)S(1)} collective-permute-done((bf16[128,256]{1,0:T(8,128)(2,1)S(1)}, bf16[128,256]{1,0:T(8,128)(2,1)S(1)}, u32[]{:S(2)}, u32[]{:S(2)}) %collective-permute-start.24) | collective-permute-done | bytes 65568 | tf_op jit(solution)/shard_map/ppermute | solution.py:316
  50.9 0.7 %collective-permute-done.25.refs_4_ = bf16[128,256]{1,0:T(8,128)(2,1)S(1)} collective-permute-done((bf16[128,256]{1,0:T(8,128)(2,1)S(1)}, bf16[128,256]{1,0:T(8,128)(2,1)S(1)}, u32[]{:S(2)}, u32[]{:S(2)}) %collective-permute-start.25) | collective-permute-done | bytes 65568 | tf_op jit(solution)/shard_map/ppermute | solution.py:316
  51.6 0.5 phase.3.refs_5_
  52.0 0.1 collective-permute-start.26
  52.2 1.2 %recon.2 = (f32[128,512]{1,0:T(8,128)S(1)}, bf16[1024,512]{1,0:T(8,128)(2,1)S(1)}, bf16[128,128]{1,0:T(8,128)(2,1)S(1)}) custom-call(s32[1,4]{1,0:T(1,128)S(1)} %copy-done.3, s32[16]{0:T(128)S(1)} %copy-done.4, bf16[4,1024,512]{2,1,0:T(8,128)(2,1)S(1)} %copy-done.2, bf16[128,1024]{1,0:T(8,128)(2,1)S(1)} %phase.2.refs_3_, ...), custom_call_target="tpu_custom_call" | custom-call | flops 1 | bytes 1 | tf_op jit(solution)/shard_map/recon/pallas_call | solution.py:426
  53.4 0.3 collective-permute-done.26.phase
  53.6 1.1 %recon.3 = bf16[128,512]{1,0:T(8,128)(2,1)} custom-call(bf16[1024,512]{1,0:T(8,128)(2,1)S(1)} %get-tuple-element.48.weights, bf16[128,1024]{1,0:T(8,128)(2,1)S(1)} %collective-permute-done.26.phase, f32[128,512]{1,0:T(8,128)S(1)} %get-tuple-element.49.before, bf16[128,128]{1,0:T(8,128)(2,1)S(1)} %get-tuple-element.50.select), custom_call_target="tpu_custom_call" | custom-call | flops 1 | bytes 1 | tf_op jit(solution)/shard_map/recon/pallas_call | solution.py:439
  (20 shorter events, 0.3 us)
Async XLA Ops:
  0.0 3.5 %collective-permute-start = (bf16[4,2,64,1024]{3,2,1,0:T(8,128)(2,1)}, bf16[4,2,64,1024]{3,2,1,0:T(8,128)(2,1)S(1)}, u32[]{:S(2)}, u32[]{:S(2)}) collective-permute-start(bf16[4,2,64,1024]{3,2,1,0:T(8,128)(2,1)} %bitcast.1), channel_id=1, source_target_pairs={{0,16},{1,17},{2,18},{3,19},{4,20},{5,21},{6,22},{7,23},{8,24},{9,... | collective-permute-start | bytes 3145736 | tf_op jit(solution)/shard_map/ppermute | solution.py:316
  3.5 1.6 %copy-start = (bf16[1024,1024]{1,0:T(8,128)(2,1)S(1)}, bf16[1024,1024]{1,0:T(8,128)(2,1)}, u32[]{:S(2)}) copy-start(bf16[1024,1024]{1,0:T(8,128)(2,1)} %constant.4.clone.refs_2_.refs_0_) | copy-start | bytes 6291460
  5.9 11.5 %copy-start.1 = (bf16[1024,1024]{1,0:T(8,128)(2,1)S(1)}, bf16[1024,1024]{1,0:T(8,128)(2,1)}, u32[]{:S(2)}) copy-start(bf16[1024,1024]{1,0:T(8,128)(2,1)} %constant.4.clone.refs_2_.refs_0_) | copy-start | bytes 6291460
  5.9 8.4 %collective-permute-start.1 = (bf16[4,64,256]{2,1,0:T(8,128)(2,1)S(1)}, bf16[4,64,256]{2,1,0:T(8,128)(2,1)S(1)}, u32[]{:S(2)}, u32[]{:S(2)}) collective-permute-start(bf16[4,64,256]{2,1,0:T(8,128)(2,1)S(1)} %get-tuple-element.31), channel_id=1, source_target_pairs={{0,1},{1,0},{2,3},{3,2},{4,5},{5,4},{6,7},{7,6},{8,9},{9,8},{10,11... | collective-permute-start | bytes 393224 | tf_op jit(solution)/shard_map/ppermute | solution.py:316
  8.4 8.2 %collective-permute-start.2 = (bf16[4,64,256]{2,1,0:T(8,128)(2,1)S(1)}, bf16[4,64,256]{2,1,0:T(8,128)(2,1)S(1)}, u32[]{:S(2)}, u32[]{:S(2)}) collective-permute-start(bf16[4,64,256]{2,1,0:T(8,128)(2,1)S(1)} %get-tuple-element.32), channel_id=1, source_target_pairs={{0,2},{1,3},{2,0},{3,1},{4,6},{5,7},{6,4},{7,5},{8,10},{9,11},{10,... | collective-permute-start | bytes 393224 | tf_op jit(solution)/shard_map/ppermute | solution.py:316
  9.9 7.4 %collective-permute-start.3 = (bf16[4,64,256]{2,1,0:T(8,128)(2,1)S(1)}, bf16[4,64,256]{2,1,0:T(8,128)(2,1)S(1)}, u32[]{:S(2)}, u32[]{:S(2)}) collective-permute-start(bf16[4,64,256]{2,1,0:T(8,128)(2,1)S(1)} %get-tuple-element.33), channel_id=1, source_target_pairs={{0,3},{1,2},{2,1},{3,0},{4,7},{5,6},{6,5},{7,4},{8,11},{9,10},{10,... | collective-permute-start | bytes 393224 | tf_op jit(solution)/shard_map/ppermute | solution.py:316
  10.7 10.0 %collective-permute-start.14 = (bf16[4,64,256]{2,1,0:T(8,128)(2,1)S(1)}, bf16[4,64,256]{2,1,0:T(8,128)(2,1)S(1)}, u32[]{:S(2)}, u32[]{:S(2)}) collective-permute-start(bf16[4,64,256]{2,1,0:T(8,128)(2,1)S(1)} %get-tuple-element.40), channel_id=1, source_target_pairs={{0,1},{1,0},{2,3},{3,2},{4,5},{5,4},{6,7},{7,6},{8,9},{9,8},{10,11... | collective-permute-start | bytes 393224 | tf_op jit(solution)/shard_map/ppermute | solution.py:316
  12.7 9.8 %collective-permute-start.15 = (bf16[4,64,256]{2,1,0:T(8,128)(2,1)S(1)}, bf16[4,64,256]{2,1,0:T(8,128)(2,1)S(1)}, u32[]{:S(2)}, u32[]{:S(2)}) collective-permute-start(bf16[4,64,256]{2,1,0:T(8,128)(2,1)S(1)} %get-tuple-element.41), channel_id=1, source_target_pairs={{0,2},{1,3},{2,0},{3,1},{4,6},{5,7},{6,4},{7,5},{8,10},{9,11},{10,... | collective-permute-start | bytes 393224 | tf_op jit(solution)/shard_map/ppermute | solution.py:316
  14.2 8.2 %collective-permute-start.16 = (bf16[4,64,256]{2,1,0:T(8,128)(2,1)S(1)}, bf16[4,64,256]{2,1,0:T(8,128)(2,1)S(1)}, u32[]{:S(2)}, u32[]{:S(2)}) collective-permute-start(bf16[4,64,256]{2,1,0:T(8,128)(2,1)S(1)} %get-tuple-element.42), channel_id=1, source_target_pairs={{0,3},{1,2},{2,1},{3,0},{4,7},{5,6},{6,5},{7,4},{8,11},{9,10},{10,... | collective-permute-start | bytes 393224 | tf_op jit(solution)/shard_map/ppermute | solution.py:316
  18.6 7.3 %collective-permute-start.7 = (bf16[2,256,128]{2,1,0:T(8,128)(2,1)S(1)}, bf16[2,256,128]{2,1,0:T(8,128)(2,1)S(1)}, u32[]{:S(2)}, u32[]{:S(2)}) collective-permute-start(bf16[2,256,128]{2,1,0:T(8,128)(2,1)S(1)} %get-tuple-element.36.one), channel_id=1, source_target_pairs={{0,4},{1,5},{2,6},{3,7},{4,0},{5,1},{6,2},{7,3},{8,12},{9,13},{10,... | collective-permute-start | bytes 393224 | tf_op jit(solution)/shard_map/ppermute | solution.py:316
  20.3 5.7 %collective-permute-start.4 = (bf16[2,256,128]{2,1,0:T(8,128)(2,1)S(1)}, bf16[2,256,128]{2,1,0:T(8,128)(2,1)S(1)}, u32[]{:S(2)}, u32[]{:S(2)}) collective-permute-start(bf16[2,256,128]{2,1,0:T(8,128)(2,1)S(1)} %get-tuple-element.35.one), channel_id=1, source_target_pairs={{0,4},{1,5},{2,6},{3,7},{4,0},{5,1},{6,2},{7,3},{8,12},{9,13},{10,... | collective-permute-start | bytes 393224 | tf_op jit(solution)/shard_map/ppermute | solution.py:316
  23.8 6.4 %collective-permute-start.20 = (bf16[2,256,128]{2,1,0:T(8,128)(2,1)S(1)}, bf16[2,256,128]{2,1,0:T(8,128)(2,1)S(1)}, u32[]{:S(2)}, u32[]{:S(2)}) collective-permute-start(bf16[2,256,128]{2,1,0:T(8,128)(2,1)S(1)} %get-tuple-element.45.one), channel_id=1, source_target_pairs={{0,4},{1,5},{2,6},{3,7},{4,0},{5,1},{6,2},{7,3},{8,12},{9,13},{10,... | collective-permute-start | bytes 393224 | tf_op jit(solution)/shard_map/ppermute | solution.py:316
  25.4 6.7 %collective-permute-start.17 = (bf16[2,256,128]{2,1,0:T(8,128)(2,1)S(1)}, bf16[2,256,128]{2,1,0:T(8,128)(2,1)S(1)}, u32[]{:S(2)}, u32[]{:S(2)}) collective-permute-start(bf16[2,256,128]{2,1,0:T(8,128)(2,1)S(1)} %get-tuple-element.44.one), channel_id=1, source_target_pairs={{0,4},{1,5},{2,6},{3,7},{4,0},{5,1},{6,2},{7,3},{8,12},{9,13},{10,... | collective-permute-start | bytes 393224 | tf_op jit(solution)/shard_map/ppermute | solution.py:316
  25.9 6.3 %collective-permute-start.8 = (bf16[2,256,128]{2,1,0:T(8,128)(2,1)S(1)}, bf16[2,256,128]{2,1,0:T(8,128)(2,1)S(1)}, u32[]{:S(2)}, u32[]{:S(2)}) collective-permute-start(bf16[2,256,128]{2,1,0:T(8,128)(2,1)S(1)} %joint.5), channel_id=1, source_target_pairs={{0,16},{1,17},{2,18},{3,19},{4,8},{5,9},{6,10},{7,11},{8,4},{9,5},... | collective-permute-start | bytes 393224 | tf_op jit(solution)/shard_map/ppermute | solution.py:316
  26.1 9.4 %collective-permute-start.5 = (bf16[2,256,128]{2,1,0:T(8,128)(2,1)S(1)}, bf16[2,256,128]{2,1,0:T(8,128)(2,1)S(1)}, u32[]{:S(2)}, u32[]{:S(2)}) collective-permute-start(bf16[2,256,128]{2,1,0:T(8,128)(2,1)S(1)} %joint.4), channel_id=1, source_target_pairs={{0,16},{1,17},{2,18},{3,19},{4,8},{5,9},{6,10},{7,11},{8,4},{9,5},... | collective-permute-start | bytes 393224 | tf_op jit(solution)/shard_map/ppermute | solution.py:316
  30.3 6.6 %collective-permute-start.21 = (bf16[2,256,128]{2,1,0:T(8,128)(2,1)S(1)}, bf16[2,256,128]{2,1,0:T(8,128)(2,1)S(1)}, u32[]{:S(2)}, u32[]{:S(2)}) collective-permute-start(bf16[2,256,128]{2,1,0:T(8,128)(2,1)S(1)} %joint.7), channel_id=1, source_target_pairs={{0,16},{1,17},{2,18},{3,19},{4,8},{5,9},{6,10},{7,11},{8,4},{9,5},... | collective-permute-start | bytes 393224 | tf_op jit(solution)/shard_map/ppermute | solution.py:316
  32.1 7.4 %collective-permute-start.18 = (bf16[2,256,128]{2,1,0:T(8,128)(2,1)S(1)}, bf16[2,256,128]{2,1,0:T(8,128)(2,1)S(1)}, u32[]{:S(2)}, u32[]{:S(2)}) collective-permute-start(bf16[2,256,128]{2,1,0:T(8,128)(2,1)S(1)} %joint.6), channel_id=1, source_target_pairs={{0,16},{1,17},{2,18},{3,19},{4,8},{5,9},{6,10},{7,11},{8,4},{9,5},... | collective-permute-start | bytes 393224 | tf_op jit(solution)/shard_map/ppermute | solution.py:316
  32.3 8.7 %collective-permute-start.9 = (bf16[256,128]{1,0:T(8,128)(2,1)S(1)}, bf16[256,128]{1,0:T(8,128)(2,1)S(1)}, u32[]{:S(2)}, u32[]{:S(2)}) collective-permute-start(bf16[256,128]{1,0:T(8,128)(2,1)S(1)} %near.5), channel_id=1, source_target_pairs={{0,4},{1,5},{2,6},{3,7},{4,0},{5,1},{6,2},{7,3},{8,12},{9,13},{10,... | collective-permute-start | bytes 196616 | tf_op jit(solution)/shard_map/ppermute | solution.py:316
  35.5 5.5 %collective-permute-start.6 = (bf16[256,128]{1,0:T(8,128)(2,1)S(1)}, bf16[256,128]{1,0:T(8,128)(2,1)S(1)}, u32[]{:S(2)}, u32[]{:S(2)}) collective-permute-start(bf16[256,128]{1,0:T(8,128)(2,1)S(1)} %near.4), channel_id=1, source_target_pairs={{0,4},{1,5},{2,6},{3,7},{4,0},{5,1},{6,2},{7,3},{8,12},{9,13},{10,... | collective-permute-start | bytes 196616 | tf_op jit(solution)/shard_map/ppermute | solution.py:316
  36.9 7.6 %collective-permute-start.22 = (bf16[256,128]{1,0:T(8,128)(2,1)S(1)}, bf16[256,128]{1,0:T(8,128)(2,1)S(1)}, u32[]{:S(2)}, u32[]{:S(2)}) collective-permute-start(bf16[256,128]{1,0:T(8,128)(2,1)S(1)} %near.7), channel_id=1, source_target_pairs={{0,4},{1,5},{2,6},{3,7},{4,0},{5,1},{6,2},{7,3},{8,12},{9,13},{10,... | collective-permute-start | bytes 196616 | tf_op jit(solution)/shard_map/ppermute | solution.py:316
  39.6 5.0 %collective-permute-start.19 = (bf16[256,128]{1,0:T(8,128)(2,1)S(1)}, bf16[256,128]{1,0:T(8,128)(2,1)S(1)}, u32[]{:S(2)}, u32[]{:S(2)}) collective-permute-start(bf16[256,128]{1,0:T(8,128)(2,1)S(1)} %near.6), channel_id=1, source_target_pairs={{0,4},{1,5},{2,6},{3,7},{4,0},{5,1},{6,2},{7,3},{8,12},{9,13},{10,... | collective-permute-start | bytes 196616 | tf_op jit(solution)/shard_map/ppermute | solution.py:316
  41.0 6.1 %collective-permute-start.10 = (bf16[128,256]{1,0:T(8,128)(2,1)S(1)}, bf16[128,256]{1,0:T(8,128)(2,1)S(1)}, u32[]{:S(2)}, u32[]{:S(2)}) collective-permute-start(bf16[128,256]{1,0:T(8,128)(2,1)S(1)} %get-tuple-element.37.refs_1_), channel_id=1, source_target_pairs={{0,1},{1,0},{2,3},{3,2},{4,5},{5,4},{6,7},{7,6},{8,9},{9,8},{10,11... | collective-permute-start | bytes 196616 | tf_op jit(solution)/shard_map/ppermute | solution.py:316
  42.1 6.1 %collective-permute-start.11 = (bf16[128,256]{1,0:T(8,128)(2,1)S(1)}, bf16[128,256]{1,0:T(8,128)(2,1)S(1)}, u32[]{:S(2)}, u32[]{:S(2)}) collective-permute-start(bf16[128,256]{1,0:T(8,128)(2,1)S(1)} %get-tuple-element.38), channel_id=1, source_target_pairs={{0,3},{1,2},{2,1},{3,0},{4,7},{5,6},{6,5},{7,4},{8,11},{9,10},{10,... | collective-permute-start | bytes 196616 | tf_op jit(solution)/shard_map/ppermute | solution.py:316
  43.5 5.4 %collective-permute-start.12 = (bf16[128,256]{1,0:T(8,128)(2,1)S(1)}, bf16[128,256]{1,0:T(8,128)(2,1)S(1)}, u32[]{:S(2)}, u32[]{:S(2)}) collective-permute-start(bf16[128,256]{1,0:T(8,128)(2,1)S(1)} %get-tuple-element.38), channel_id=1, source_target_pairs={{0,2},{1,3},{2,0},{3,1},{4,6},{5,7},{6,4},{7,5},{8,10},{9,11},{10,... | collective-permute-start | bytes 196616 | tf_op jit(solution)/shard_map/ppermute | solution.py:316
  44.6 4.8 %collective-permute-start.23 = (bf16[128,256]{1,0:T(8,128)(2,1)S(1)}, bf16[128,256]{1,0:T(8,128)(2,1)S(1)}, u32[]{:S(2)}, u32[]{:S(2)}) collective-permute-start(bf16[128,256]{1,0:T(8,128)(2,1)S(1)} %get-tuple-element.46.refs_1_), channel_id=1, source_target_pairs={{0,1},{1,0},{2,3},{3,2},{4,5},{5,4},{6,7},{7,6},{8,9},{9,8},{10,11... | collective-permute-start | bytes 196616 | tf_op jit(solution)/shard_map/ppermute | solution.py:316
  45.7 6.4 %copy-start.2 = (bf16[4,1024,512]{2,1,0:T(8,128)(2,1)S(1)}, bf16[4,1024,512]{2,1,0:T(8,128)(2,1)}, u32[]{:S(2)}) copy-start(bf16[4,1024,512]{2,1,0:T(8,128)(2,1)} %refs_2_.3) | copy-start | bytes 12582916
  45.7 6.4 %copy-start.3 = (s32[1,4]{1,0:T(1,128)S(1)}, s32[1,4]{1,0:T(1,128)}, u32[]{:S(2)}) copy-start(s32[1,4]{1,0:T(1,128)} %refs_0_.5) | copy-start | bytes 52
  45.7 6.4 %copy-start.4 = (s32[16]{0:T(128)S(1)}, s32[16]{0:T(128)}, u32[]{:S(2)}) copy-start(s32[16]{0:T(128)} %refs_1_.1) | copy-start | bytes 196
  45.7 5.2 %collective-permute-start.24 = (bf16[128,256]{1,0:T(8,128)(2,1)S(1)}, bf16[128,256]{1,0:T(8,128)(2,1)S(1)}, u32[]{:S(2)}, u32[]{:S(2)}) collective-permute-start(bf16[128,256]{1,0:T(8,128)(2,1)S(1)} %get-tuple-element.47), channel_id=1, source_target_pairs={{0,3},{1,2},{2,1},{3,0},{4,7},{5,6},{6,5},{7,4},{8,11},{9,10},{10,... | collective-permute-start | bytes 196616 | tf_op jit(solution)/shard_map/ppermute | solution.py:316
  47.1 4.5 %collective-permute-start.25 = (bf16[128,256]{1,0:T(8,128)(2,1)S(1)}, bf16[128,256]{1,0:T(8,128)(2,1)S(1)}, u32[]{:S(2)}, u32[]{:S(2)}) collective-permute-start(bf16[128,256]{1,0:T(8,128)(2,1)S(1)} %get-tuple-element.47), channel_id=1, source_target_pairs={{0,2},{1,3},{2,0},{3,1},{4,6},{5,7},{6,4},{7,5},{8,10},{9,11},{10,... | collective-permute-start | bytes 196616 | tf_op jit(solution)/shard_map/ppermute | solution.py:316
  49.3 2.8 %collective-permute-start.13 = (bf16[128,1024]{1,0:T(8,128)(2,1)S(1)}, bf16[128,1024]{1,0:T(8,128)(2,1)S(1)}, u32[]{:S(2)}, u32[]{:S(2)}) collective-permute-start(bf16[128,1024]{1,0:T(8,128)(2,1)S(1)} %phase.2.refs_3_), channel_id=1, source_target_pairs={{0,16},{1,17},{2,18},{3,19},{4,20},{5,21},{6,22},{7,23},{8,24},{9,... | collective-permute-start | bytes 786440 | tf_op jit(solution)/shard_map/ppermute | solution.py:316
  52.0 1.6 %collective-permute-start.26 = (bf16[128,1024]{1,0:T(8,128)(2,1)S(1)}, bf16[128,1024]{1,0:T(8,128)(2,1)S(1)}, u32[]{:S(2)}, u32[]{:S(2)}) collective-permute-start(bf16[128,1024]{1,0:T(8,128)(2,1)S(1)} %phase.3.refs_5_), channel_id=1, source_target_pairs={{0,16},{1,17},{2,18},{3,19},{4,20},{5,21},{6,22},{7,23},{8,24},{9,... | collective-permute-start | bytes 786440 | tf_op jit(solution)/shard_map/ppermute | solution.py:316

commit v12 on v11

--- a/solution.py
+++ b/solution.py
@@ -12,7 +12,7 @@
 regularizer = 0.05
 bf16 = jnp.bfloat16
 f32 = jnp.float32
-send_order = (0, 1, 2, 3)
+send_order = (0, 2, 1, 3)
 tail_order = (0, 1, 3, 2)
 
 
@@ -98,17 +98,20 @@
     return lax.axis_index("dist"), device // inner, device % inner
 
 
-def row_kernel(inner, chunk, here, there, table, *outs):
+def row_kernel(inner, chunk, holo, there, table, after, *refs):
+    outs, flat, loaded = refs[:inner], refs[inner], refs[inner + 1]
     core, _, spot = position(inner)
-    own, dist_dev, rows_dev, width = here.shape
+    angles, dist_dev, rows_dev, width = there.shape
     block = width // inner
-    partner = there[core * own + chunk]
-    flat = jnp.concatenate(
-        [source.reshape(dist_dev * rows_dev, width) for source in (here[chunk], partner)], axis=0
-    )
+    angle = core * (angles // 2) + chunk
+    copy = pltpu.make_async_copy(holo.at[angle], flat.at[pl.ds(0, dist_dev)], loaded)
+    copy.start()
+    flat[dist_dev:] = there[angle]
+    copy.wait()
+    rows = flat[...].reshape(2 * dist_dev * rows_dev, width)
     for rel in range(inner):
         part = table[:, pl.ds(pl.multiple_of((spot ^ rel) * block, block), block)]
-        got = jnp.dot(flat, part, preferred_element_type=f32).astype(bf16)
+        got = jnp.dot(rows, part, preferred_element_type=f32).astype(bf16)
         outs[rel][...] = got.reshape(2 * dist_dev, rows_dev, block)
 
 
@@ -117,12 +120,9 @@
     return (turns - jnp.round(turns)) * (2.0 * math.pi)
 
 
-def filter_kernel(inner, turns, holo, out, mine, arrived):
+def filter_kernel(inner, dist_dev, turns, out):
     dists, width, block = out.shape
-    own, dist_dev = mine.shape[:2]
     core, _, spot = position(inner)
-    copy = pltpu.make_async_copy(holo.at[pl.ds(core * own, own)], mine, arrived)
-    copy.start()
 
     def square(first, length):
         index = lax.broadcasted_iota(jnp.int32, (1, length), 1) + first
@@ -158,7 +158,6 @@
         scale = 1.0 / (denom + regularizer)
         for d in range(dists):
             out[d, at : at + step, :] = (transfer[d] * scale).astype(bf16)
-    copy.wait()
 
 
 def column_kernel(inner, outer, table, gain, *refs):
@@ -210,7 +209,7 @@
 
 
 def half_kernel(inner, keep, *refs):
-    mine, other = refs[-2:]
+    other, mine = refs[-2:]
     parts = refs[:-2]
     splits = len(parts) // 2
     _, plane, spot = position(inner)
@@ -332,30 +331,30 @@
         return (c, (3 - z) * inner + r % inner) if z in (1, 2) else (c ^ 1, r)
 
     partner = sent(holograms[0], to_other_core)
-    gain, mine = pl.pallas_call(
-        lambda *refs: filter_kernel(inner, *refs),
-        out_shape=[
-            shaped(dists, width, block),
-            shaped(own, dist_dev, rows_dev, width),
-        ],
-        in_specs=smem(1) + in_hbm(1),
-        out_specs=vmem(2),
-        scratch_shapes=[pltpu.SemaphoreType.DMA],
+    gain = pl.pallas_call(
+        lambda *refs: filter_kernel(inner, dist_dev, *refs),
+        out_shape=shaped(dists, width, block),
+        in_specs=smem(1),
+        out_specs=one_out,
         compiler_params=params,
         cost_estimate=cheap,
         name="filters",
-    )(propagation * (0.5 / math.pi), from_hbm(holograms[0]))
+    )(propagation * (0.5 / math.pi))
     arrived = []
     for chunk in range(own):
         pieces = pl.pallas_call(
             lambda *refs, chunk=chunk: row_kernel(inner, chunk, *refs),
             out_shape=[shaped(dists, rows_dev, block)] * inner,
-            in_specs=vmem(3),
+            in_specs=in_hbm(1) + vmem(2) + unread(1),
             out_specs=vmem(inner),
+            scratch_shapes=[
+                pltpu.VMEM((dists, rows_dev, width), bf16),
+                pltpu.SemaphoreType.DMA,
+            ],
             compiler_params=params,
             cost_estimate=cheap,
             name="row_spectra",
-        )(mine, partner, table)
+        )(from_hbm(holograms[0]), partner, table, gain)
         arrived.append(spread(pieces, send_order))
 
     sums = []
@@ -401,7 +400,7 @@
 
     phases = []
     for chunk in range(own):
-        first, second = pl.pallas_call(
+        second, first = pl.pallas_call(
             lambda *refs: half_kernel(inner, *refs),
             out_shape=[shaped(capacity, block)] * 2,
             in_specs=vmem(1 + 2 * splits),

time: 54.9 us -> 54 us (0.984)
  Pallas kernels: 10.1 us -> 12 us
  local copies, waits for them, and re-layouts: 1.6 us -> 0.01 us
  starting transfers between devices: 30.3 us -> 29 us
    pallas_call x2, Pallas kernels: 1.5 us -> 3.44 us  [plane_plan(): pl.pallas_call(lambda *refs, chunk=chunk: row_kernel(inner, chunk, *refs)...]
    unnamed x10 -> x8, local copies, waits for them, and re-layouts: 1.6 us -> 0.01 us
    ppermute x27, starting transfers between devices: 30.3 us -> 29 us  [sent(): return lax.ppermute(value, ('dist', 'rows'), pairs)]
  transfers between devices with their start and end apart: 27 -> 27, of which waited for: 9 -> 8; matrix products, arithmetic and copies ran while one was open for 1% -> 2% of each run, Pallas kernels for 15% -> 17%
where the time goes in v12:
time: 54 us; the launch traced here: 53.9 us
  starting transfers between devices  29 us (54%)
  Pallas kernels  12 us (22%)
  waiting for transfers between devices  11.7 us (22%)
  other arithmetic  0.83 us (2%)
    ppermute x27, starting transfers between devices, sent(): return lax.ppermute(value, ('dist', 'rows'), pairs)  29 us
    ppermute x27, waiting for transfers between devices, sent(): return lax.ppermute(value, ('dist', 'rows'), pairs)  11.7 us
    pallas_call x2, Pallas kernels, plane_plan(): pl.pallas_call(lambda *refs, chunk=chunk: row_kernel(inner, chunk, *refs)...  3.44 us
    pallas_call x2, Pallas kernels, plane_plan(): pl.pallas_call(lambda *refs: column_kernel(inner, outer, *refs), out_shap...  2.59 us
    pallas_call x1, Pallas kernels, plane_plan(): pl.pallas_call(lambda *refs: filter_kernel(inner, dist_dev, *refs), out_s...  2.37 us
    pallas_call x1, Pallas kernels, plane_plan(): pl.pallas_call(lambda *refs: recon_kernel(own, *refs), out_shape=[jax.Sha...  1.2 us
    pallas_call x1, Pallas kernels, plane_plan(): pl.pallas_call(recon_last_kernel, out_shape=shaped(capacity, pixels), in_...  1.12 us
  transfers between devices with their start and end apart: 27, of which 8 were waited for; matrix products, arithmetic and copies ran while one was open for 2% of the time, Pallas kernels for 17%

profile of v12, /device:TPU:0, one launch (start us, length us, event | category | flops | bytes accessed | tf_op | source)
XLA Modules:
  0.0 53.9 jit_solution(13484886257967972991)
XLA Ops:
  0.0 0.5 collective-permute-start
  0.5 0.8 %broadcast_multiply_fusion.refs_0_ = f32[4]{0:T(128)S(1)} fusion(f32[4]{0:T(128)} %param.7), kind=kLoop, calls=%fused_computation | loop fusion | flops 4 | bytes 32 | tf_op jit(solution)/shard_map/mul | solution.py:342
  1.3 2.4 %filters.1.refs_3_.refs_1_ = bf16[4,1024,256]{2,1,0:T(8,128)(2,1)S(1)} custom-call(f32[4]{0:T(128)S(1)} %broadcast_multiply_fusion.refs_0_), custom_call_target="tpu_custom_call" | custom-call | flops 1 | bytes 1 | tf_op jit(solution)/shard_map/filters/pallas_call | solution.py:334
  3.7 0.0 collective-permute-done.refs_1_
  3.7 1.7 %row_spectra.2 = (bf16[4,64,256]{2,1,0:T(8,128)(2,1)S(1)}, bf16[4,64,256]{2,1,0:T(8,128)(2,1)S(1)}, bf16[4,64,256]{2,1,0:T(8,128)(2,1)S(1)}, bf16[4,64,256]{2,1,0:T(8,128)(2,1)S(1)}) custom-call(bf16[4,2,64,1024]{3,2,1,0:T(8,128)(2,1)} %bitcast.2, bf16[4,2,64,1024]{3,2,1,0:T(8,128)(2,1)S(1)} %collective-permute-done.refs_1_, bf16[1024,1024]{1,0:T(8,128)(2,1)S(1)} %copy-done, ...), custom_call_target="tpu_custom_call" | custom-call | flops 1 | bytes 1 | tf_op jit(solution)/shard_map/row_spectra/pallas_call | solution.py:345
  5.4 2.6 %collective-permute-start.1 = (bf16[4,64,256]{2,1,0:T(8,128)(2,1)S(1)}, bf16[4,64,256]{2,1,0:T(8,128)(2,1)S(1)}, u32[]{:S(2)}, u32[]{:S(2)}) collective-permute-start(bf16[4,64,256]{2,1,0:T(8,128)(2,1)S(1)} %get-tuple-element.27), channel_id=1, source_target_pairs={{0,2},{1,3},{2,0},{3,1},{4,6},{5,7},{6,4},{7,5},{8,10},{9,11},{10,... | collective-permute-start | bytes 393224 | tf_op jit(solution)/shard_map/ppermute | solution.py:315
  8.0 1.5 %collective-permute-start.2 = (bf16[4,64,256]{2,1,0:T(8,128)(2,1)S(1)}, bf16[4,64,256]{2,1,0:T(8,128)(2,1)S(1)}, u32[]{:S(2)}, u32[]{:S(2)}) collective-permute-start(bf16[4,64,256]{2,1,0:T(8,128)(2,1)S(1)} %get-tuple-element.28), channel_id=1, source_target_pairs={{0,1},{1,0},{2,3},{3,2},{4,5},{5,4},{6,7},{7,6},{8,9},{9,8},{10,11... | collective-permute-start | bytes 393224 | tf_op jit(solution)/shard_map/ppermute | solution.py:315
  9.5 0.1 collective-permute-start.3
  9.5 1.7 %row_spectra.3 = (bf16[4,64,256]{2,1,0:T(8,128)(2,1)S(1)}, bf16[4,64,256]{2,1,0:T(8,128)(2,1)S(1)}, bf16[4,64,256]{2,1,0:T(8,128)(2,1)S(1)}, bf16[4,64,256]{2,1,0:T(8,128)(2,1)S(1)}) custom-call(bf16[4,2,64,1024]{3,2,1,0:T(8,128)(2,1)} %bitcast.3, bf16[4,2,64,1024]{3,2,1,0:T(8,128)(2,1)S(1)} %collective-permute-done.refs_1_, bf16[1024,1024]{1,0:T(8,128)(2,1)S(1)} %copy-done, ...), custom_call_target="tpu_custom_call" | custom-call | flops 1 | bytes 1 | tf_op jit(solution)/shard_map/row_spectra/pallas_call | solution.py:345
  11.2 2.0 %collective-permute-start.14 = (bf16[4,64,256]{2,1,0:T(8,128)(2,1)S(1)}, bf16[4,64,256]{2,1,0:T(8,128)(2,1)S(1)}, u32[]{:S(2)}, u32[]{:S(2)}) collective-permute-start(bf16[4,64,256]{2,1,0:T(8,128)(2,1)S(1)} %get-tuple-element.36), channel_id=1, source_target_pairs={{0,2},{1,3},{2,0},{3,1},{4,6},{5,7},{6,4},{7,5},{8,10},{9,11},{10,... | collective-permute-start | bytes 393224 | tf_op jit(solution)/shard_map/ppermute | solution.py:315
  13.2 1.5 %collective-permute-start.15 = (bf16[4,64,256]{2,1,0:T(8,128)(2,1)S(1)}, bf16[4,64,256]{2,1,0:T(8,128)(2,1)S(1)}, u32[]{:S(2)}, u32[]{:S(2)}) collective-permute-start(bf16[4,64,256]{2,1,0:T(8,128)(2,1)S(1)} %get-tuple-element.37), channel_id=1, source_target_pairs={{0,1},{1,0},{2,3},{3,2},{4,5},{5,4},{6,7},{7,6},{8,9},{9,8},{10,11... | collective-permute-start | bytes 393224 | tf_op jit(solution)/shard_map/ppermute | solution.py:315
  14.7 0.0 collective-permute-done.1.refs_3_
  14.7 0.1 collective-permute-start.16
  14.8 0.0 collective-permute-done.2.refs_4_
  14.8 2.0 %collective-permute-done.3.refs_5_ = bf16[4,64,256]{2,1,0:T(8,128)(2,1)S(1)} collective-permute-done((bf16[4,64,256]{2,1,0:T(8,128)(2,1)S(1)}, bf16[4,64,256]{2,1,0:T(8,128)(2,1)S(1)}, u32[]{:S(2)}, u32[]{:S(2)}) %collective-permute-start.3) | collective-permute-done | bytes 131104 | tf_op jit(solution)/shard_map/ppermute | solution.py:315
  16.8 1.3 %columns.2 = (bf16[2,256,256]{2,1,0:T(8,128)(2,1)S(1)}, bf16[2,256,128]{2,1,0:T(8,128)(2,1)S(1)}, bf16[2,256,128]{2,1,0:T(8,128)(2,1)S(1)}) custom-call(bf16[1024,1024]{1,0:T(8,128)(2,1)S(1)} %copy-done, bf16[4,1024,256]{2,1,0:T(8,128)(2,1)S(1)} %filters.1.refs_3_.refs_1_, bf16[4,64,256]{2,1,0:T(8,128)(2,1)S(1)} %get-tuple-element.26.refs_2_, ...), custom_call_target="tpu_custom_call" | custom-call | flops 1 | bytes 1 | tf_op jit(solution)/shard_map/columns/pallas_call | solution.py:362
  18.1 1.7 %collective-permute-start.7 = (bf16[2,256,128]{2,1,0:T(8,128)(2,1)S(1)}, bf16[2,256,128]{2,1,0:T(8,128)(2,1)S(1)}, u32[]{:S(2)}, u32[]{:S(2)}) collective-permute-start(bf16[2,256,128]{2,1,0:T(8,128)(2,1)S(1)} %get-tuple-element.32.one), channel_id=1, source_target_pairs={{0,4},{1,5},{2,6},{3,7},{4,0},{5,1},{6,2},{7,3},{8,12},{9,13},{10,... | collective-permute-start | bytes 393224 | tf_op jit(solution)/shard_map/ppermute | solution.py:315
  19.8 0.4 collective-permute-start.4
  20.2 0.0 collective-permute-done.14.refs_3_
  20.2 0.0 collective-permute-done.15.refs_4_
  20.2 1.5 %collective-permute-done.16.refs_5_ = bf16[4,64,256]{2,1,0:T(8,128)(2,1)S(1)} collective-permute-done((bf16[4,64,256]{2,1,0:T(8,128)(2,1)S(1)}, bf16[4,64,256]{2,1,0:T(8,128)(2,1)S(1)}, u32[]{:S(2)}, u32[]{:S(2)}) %collective-permute-start.16) | collective-permute-done | bytes 131104 | tf_op jit(solution)/shard_map/ppermute | solution.py:315
  21.7 1.3 %columns.3 = (bf16[2,256,256]{2,1,0:T(8,128)(2,1)S(1)}, bf16[2,256,128]{2,1,0:T(8,128)(2,1)S(1)}, bf16[2,256,128]{2,1,0:T(8,128)(2,1)S(1)}) custom-call(bf16[1024,1024]{1,0:T(8,128)(2,1)S(1)} %copy-done, bf16[4,1024,256]{2,1,0:T(8,128)(2,1)S(1)} %filters.1.refs_3_.refs_1_, bf16[4,64,256]{2,1,0:T(8,128)(2,1)S(1)} %get-tuple-element.35.refs_2_, ...), custom_call_target="tpu_custom_call" | custom-call | flops 1 | bytes 1 | tf_op jit(solution)/shard_map/columns/pallas_call | solution.py:362
  23.0 1.8 %collective-permute-start.20 = (bf16[2,256,128]{2,1,0:T(8,128)(2,1)S(1)}, bf16[2,256,128]{2,1,0:T(8,128)(2,1)S(1)}, u32[]{:S(2)}, u32[]{:S(2)}) collective-permute-start(bf16[2,256,128]{2,1,0:T(8,128)(2,1)S(1)} %get-tuple-element.41.one), channel_id=1, source_target_pairs={{0,4},{1,5},{2,6},{3,7},{4,0},{5,1},{6,2},{7,3},{8,12},{9,13},{10,... | collective-permute-start | bytes 393224 | tf_op jit(solution)/shard_map/ppermute | solution.py:315
  24.8 0.3 collective-permute-start.17
  25.1 0.0 collective-permute-done.7.two
  25.1 0.1 collective-permute-start.8
  25.2 0.0 collective-permute-done.4.two
  25.3 0.5 %collective-permute-start.5 = (bf16[2,256,128]{2,1,0:T(8,128)(2,1)S(1)}, bf16[2,256,128]{2,1,0:T(8,128)(2,1)S(1)}, u32[]{:S(2)}, u32[]{:S(2)}) collective-permute-start(bf16[2,256,128]{2,1,0:T(8,128)(2,1)S(1)} %joint.4), channel_id=1, source_target_pairs={{0,16},{1,17},{2,18},{3,19},{4,8},{5,9},{6,10},{7,11},{8,4},{9,5},... | collective-permute-start | bytes 393224 | tf_op jit(solution)/shard_map/ppermute | solution.py:315
  25.8 3.6 %collective-permute-done.20.two = bf16[2,256,128]{2,1,0:T(8,128)(2,1)S(1)} collective-permute-done((bf16[2,256,128]{2,1,0:T(8,128)(2,1)S(1)}, bf16[2,256,128]{2,1,0:T(8,128)(2,1)S(1)}, u32[]{:S(2)}, u32[]{:S(2)}) %collective-permute-start.20) | collective-permute-done | bytes 131104 | tf_op jit(solution)/shard_map/ppermute | solution.py:315
  29.5 0.1 collective-permute-start.21
  29.5 1.3 %collective-permute-done.17.two = bf16[2,256,128]{2,1,0:T(8,128)(2,1)S(1)} collective-permute-done((bf16[2,256,128]{2,1,0:T(8,128)(2,1)S(1)}, bf16[2,256,128]{2,1,0:T(8,128)(2,1)S(1)}, u32[]{:S(2)}, u32[]{:S(2)}) %collective-permute-start.17) | collective-permute-done | bytes 131104 | tf_op jit(solution)/shard_map/ppermute | solution.py:315
  30.9 0.1 collective-permute-start.18
  30.9 0.0 collective-permute-done.8.refs_1_.refs_3_
  31.0 3.3 %collective-permute-start.9 = (bf16[256,128]{1,0:T(8,128)(2,1)S(1)}, bf16[256,128]{1,0:T(8,128)(2,1)S(1)}, u32[]{:S(2)}, u32[]{:S(2)}) collective-permute-start(bf16[256,128]{1,0:T(8,128)(2,1)S(1)} %near.5), channel_id=1, source_target_pairs={{0,4},{1,5},{2,6},{3,7},{4,0},{5,1},{6,2},{7,3},{8,12},{9,13},{10,... | collective-permute-start | bytes 196616 | tf_op jit(solution)/shard_map/ppermute | solution.py:315
  34.3 0.0 collective-permute-done.5.refs_1_
  34.3 1.8 %collective-permute-start.6 = (bf16[256,128]{1,0:T(8,128)(2,1)S(1)}, bf16[256,128]{1,0:T(8,128)(2,1)S(1)}, u32[]{:S(2)}, u32[]{:S(2)}) collective-permute-start(bf16[256,128]{1,0:T(8,128)(2,1)S(1)} %near.4), channel_id=1, source_target_pairs={{0,4},{1,5},{2,6},{3,7},{4,0},{5,1},{6,2},{7,3},{8,12},{9,13},{10,... | collective-permute-start | bytes 196616 | tf_op jit(solution)/shard_map/ppermute | solution.py:315
  36.2 0.0 collective-permute-done.21.refs_1_.refs_3_
  36.2 2.2 %collective-permute-start.22 = (bf16[256,128]{1,0:T(8,128)(2,1)S(1)}, bf16[256,128]{1,0:T(8,128)(2,1)S(1)}, u32[]{:S(2)}, u32[]{:S(2)}) collective-permute-start(bf16[256,128]{1,0:T(8,128)(2,1)S(1)} %near.7), channel_id=1, source_target_pairs={{0,4},{1,5},{2,6},{3,7},{4,0},{5,1},{6,2},{7,3},{8,12},{9,13},{10,... | collective-permute-start | bytes 196616 | tf_op jit(solution)/shard_map/ppermute | solution.py:315
  38.4 0.0 collective-permute-done.18.refs_1_
  38.4 1.4 %collective-permute-start.19 = (bf16[256,128]{1,0:T(8,128)(2,1)S(1)}, bf16[256,128]{1,0:T(8,128)(2,1)S(1)}, u32[]{:S(2)}, u32[]{:S(2)}) collective-permute-start(bf16[256,128]{1,0:T(8,128)(2,1)S(1)} %near.6), channel_id=1, source_target_pairs={{0,4},{1,5},{2,6},{3,7},{4,0},{5,1},{6,2},{7,3},{8,12},{9,13},{10,... | collective-permute-start | bytes 196616 | tf_op jit(solution)/shard_map/ppermute | solution.py:315
  39.8 0.0 collective-permute-done.9.refs_4_
  39.8 0.0 collective-permute-done.6.refs_2_
  39.8 0.1 half.2
  39.9 1.3 %collective-permute-start.10 = (bf16[128,256]{1,0:T(8,128)(2,1)S(1)}, bf16[128,256]{1,0:T(8,128)(2,1)S(1)}, u32[]{:S(2)}, u32[]{:S(2)}) collective-permute-start(bf16[128,256]{1,0:T(8,128)(2,1)S(1)} %get-tuple-element.33.refs_1_), channel_id=1, source_target_pairs={{0,1},{1,0},{2,3},{3,2},{4,5},{5,4},{6,7},{7,6},{8,9},{9,8},{10,11... | collective-permute-start | bytes 196616 | tf_op jit(solution)/shard_map/ppermute | solution.py:315
  41.2 1.5 %collective-permute-start.11 = (bf16[128,256]{1,0:T(8,128)(2,1)S(1)}, bf16[128,256]{1,0:T(8,128)(2,1)S(1)}, u32[]{:S(2)}, u32[]{:S(2)}) collective-permute-start(bf16[128,256]{1,0:T(8,128)(2,1)S(1)} %get-tuple-element.34), channel_id=1, source_target_pairs={{0,3},{1,2},{2,1},{3,0},{4,7},{5,6},{6,5},{7,4},{8,11},{9,10},{10,... | collective-permute-start | bytes 196616 | tf_op jit(solution)/shard_map/ppermute | solution.py:315
  42.6 0.8 %collective-permute-start.12 = (bf16[128,256]{1,0:T(8,128)(2,1)S(1)}, bf16[128,256]{1,0:T(8,128)(2,1)S(1)}, u32[]{:S(2)}, u32[]{:S(2)}) collective-permute-start(bf16[128,256]{1,0:T(8,128)(2,1)S(1)} %get-tuple-element.34), channel_id=1, source_target_pairs={{0,2},{1,3},{2,0},{3,1},{4,6},{5,7},{6,4},{7,5},{8,10},{9,11},{10,... | collective-permute-start | bytes 196616 | tf_op jit(solution)/shard_map/ppermute | solution.py:315
  43.5 0.0 collective-permute-done.22.refs_4_
  43.5 0.0 collective-permute-done.19.refs_2_
  43.5 0.1 half.3
  43.5 1.3 %collective-permute-start.23 = (bf16[128,256]{1,0:T(8,128)(2,1)S(1)}, bf16[128,256]{1,0:T(8,128)(2,1)S(1)}, u32[]{:S(2)}, u32[]{:S(2)}) collective-permute-start(bf16[128,256]{1,0:T(8,128)(2,1)S(1)} %get-tuple-element.42.refs_1_), channel_id=1, source_target_pairs={{0,1},{1,0},{2,3},{3,2},{4,5},{5,4},{6,7},{7,6},{8,9},{9,8},{10,11... | collective-permute-start | bytes 196616 | tf_op jit(solution)/shard_map/ppermute | solution.py:315
  44.8 1.5 %collective-permute-start.24 = (bf16[128,256]{1,0:T(8,128)(2,1)S(1)}, bf16[128,256]{1,0:T(8,128)(2,1)S(1)}, u32[]{:S(2)}, u32[]{:S(2)}) collective-permute-start(bf16[128,256]{1,0:T(8,128)(2,1)S(1)} %get-tuple-element.43), channel_id=1, source_target_pairs={{0,3},{1,2},{2,1},{3,0},{4,7},{5,6},{6,5},{7,4},{8,11},{9,10},{10,... | collective-permute-start | bytes 196616 | tf_op jit(solution)/shard_map/ppermute | solution.py:315
  46.3 0.0 collective-permute-done.10.refs_2_
  46.3 0.8 %collective-permute-start.25 = (bf16[128,256]{1,0:T(8,128)(2,1)S(1)}, bf16[128,256]{1,0:T(8,128)(2,1)S(1)}, u32[]{:S(2)}, u32[]{:S(2)}) collective-permute-start(bf16[128,256]{1,0:T(8,128)(2,1)S(1)} %get-tuple-element.43), channel_id=1, source_target_pairs={{0,2},{1,3},{2,0},{3,1},{4,6},{5,7},{6,4},{7,5},{8,10},{9,11},{10,... | collective-permute-start | bytes 196616 | tf_op jit(solution)/shard_map/ppermute | solution.py:315
  47.1 0.0 collective-permute-done.11.refs_3_
  47.1 0.5 collective-permute-done.12.refs_4_
  47.6 0.5 phase.2.refs_3_
  48.1 0.1 collective-permute-start.13
  48.1 1.8 %collective-permute-done.24.refs_3_ = bf16[128,256]{1,0:T(8,128)(2,1)S(1)} collective-permute-done((bf16[128,256]{1,0:T(8,128)(2,1)S(1)}, bf16[128,256]{1,0:T(8,128)(2,1)S(1)}, u32[]{:S(2)}, u32[]{:S(2)}) %collective-permute-start.24) | collective-permute-done | bytes 65568 | tf_op jit(solution)/shard_map/ppermute | solution.py:315
  50.0 0.7 %collective-permute-done.25.refs_4_ = bf16[128,256]{1,0:T(8,128)(2,1)S(1)} collective-permute-done((bf16[128,256]{1,0:T(8,128)(2,1)S(1)}, bf16[128,256]{1,0:T(8,128)(2,1)S(1)}, u32[]{:S(2)}, u32[]{:S(2)}) %collective-permute-start.25) | collective-permute-done | bytes 65568 | tf_op jit(solution)/shard_map/ppermute | solution.py:315
  50.7 0.5 phase.3.refs_5_
  51.1 0.1 collective-permute-start.26
  51.2 1.2 %recon.2 = (f32[128,512]{1,0:T(8,128)S(1)}, bf16[1024,512]{1,0:T(8,128)(2,1)S(1)}, bf16[128,128]{1,0:T(8,128)(2,1)S(1)}) custom-call(s32[1,4]{1,0:T(1,128)S(1)} %copy-done.2, s32[16]{0:T(128)S(1)} %copy-done.3, bf16[4,1024,512]{2,1,0:T(8,128)(2,1)S(1)} %copy-done.1, bf16[128,1024]{1,0:T(8,128)(2,1)S(1)} %phase.2.refs_3_, ...), custom_call_target="tpu_custom_call" | custom-call | flops 1 | bytes 1 | tf_op jit(solution)/shard_map/recon/pallas_call | solution.py:425
  52.5 0.3 collective-permute-done.26.phase
  52.7 1.1 %recon.3 = bf16[128,512]{1,0:T(8,128)(2,1)} custom-call(bf16[1024,512]{1,0:T(8,128)(2,1)S(1)} %get-tuple-element.44.weights, bf16[128,1024]{1,0:T(8,128)(2,1)S(1)} %collective-permute-done.26.phase, f32[128,512]{1,0:T(8,128)S(1)} %get-tuple-element.45.before, bf16[128,128]{1,0:T(8,128)(2,1)S(1)} %get-tuple-element.46.select), custom_call_target="tpu_custom_call" | custom-call | flops 1 | bytes 1 | tf_op jit(solution)/shard_map/recon/pallas_call | solution.py:438
  (18 shorter events, 0.3 us)
Async XLA Ops:
  0.0 3.7 %copy-start = (bf16[1024,1024]{1,0:T(8,128)(2,1)S(1)}, bf16[1024,1024]{1,0:T(8,128)(2,1)}, u32[]{:S(2)}) copy-start(bf16[1024,1024]{1,0:T(8,128)(2,1)} %constant.4.clone.refs_2_.refs_0_) | copy-start | bytes 6291460
  0.0 3.7 %collective-permute-start = (bf16[4,2,64,1024]{3,2,1,0:T(8,128)(2,1)}, bf16[4,2,64,1024]{3,2,1,0:T(8,128)(2,1)S(1)}, u32[]{:S(2)}, u32[]{:S(2)}) collective-permute-start(bf16[4,2,64,1024]{3,2,1,0:T(8,128)(2,1)} %bitcast.1), channel_id=1, source_target_pairs={{0,16},{1,17},{2,18},{3,19},{4,20},{5,21},{6,22},{7,23},{8,24},{9,... | collective-permute-start | bytes 3145736 | tf_op jit(solution)/shard_map/ppermute | solution.py:315
  5.4 9.3 %collective-permute-start.1 = (bf16[4,64,256]{2,1,0:T(8,128)(2,1)S(1)}, bf16[4,64,256]{2,1,0:T(8,128)(2,1)S(1)}, u32[]{:S(2)}, u32[]{:S(2)}) collective-permute-start(bf16[4,64,256]{2,1,0:T(8,128)(2,1)S(1)} %get-tuple-element.27), channel_id=1, source_target_pairs={{0,2},{1,3},{2,0},{3,1},{4,6},{5,7},{6,4},{7,5},{8,10},{9,11},{10,... | collective-permute-start | bytes 393224 | tf_op jit(solution)/shard_map/ppermute | solution.py:315
  8.0 6.8 %collective-permute-start.2 = (bf16[4,64,256]{2,1,0:T(8,128)(2,1)S(1)}, bf16[4,64,256]{2,1,0:T(8,128)(2,1)S(1)}, u32[]{:S(2)}, u32[]{:S(2)}) collective-permute-start(bf16[4,64,256]{2,1,0:T(8,128)(2,1)S(1)} %get-tuple-element.28), channel_id=1, source_target_pairs={{0,1},{1,0},{2,3},{3,2},{4,5},{5,4},{6,7},{7,6},{8,9},{9,8},{10,11... | collective-permute-start | bytes 393224 | tf_op jit(solution)/shard_map/ppermute | solution.py:315
  9.5 7.3 %collective-permute-start.3 = (bf16[4,64,256]{2,1,0:T(8,128)(2,1)S(1)}, bf16[4,64,256]{2,1,0:T(8,128)(2,1)S(1)}, u32[]{:S(2)}, u32[]{:S(2)}) collective-permute-start(bf16[4,64,256]{2,1,0:T(8,128)(2,1)S(1)} %get-tuple-element.29), channel_id=1, source_target_pairs={{0,3},{1,2},{2,1},{3,0},{4,7},{5,6},{6,5},{7,4},{8,11},{9,10},{10,... | collective-permute-start | bytes 393224 | tf_op jit(solution)/shard_map/ppermute | solution.py:315
  11.2 8.9 %collective-permute-start.14 = (bf16[4,64,256]{2,1,0:T(8,128)(2,1)S(1)}, bf16[4,64,256]{2,1,0:T(8,128)(2,1)S(1)}, u32[]{:S(2)}, u32[]{:S(2)}) collective-permute-start(bf16[4,64,256]{2,1,0:T(8,128)(2,1)S(1)} %get-tuple-element.36), channel_id=1, source_target_pairs={{0,2},{1,3},{2,0},{3,1},{4,6},{5,7},{6,4},{7,5},{8,10},{9,11},{10,... | collective-permute-start | bytes 393224 | tf_op jit(solution)/shard_map/ppermute | solution.py:315
  13.2 6.9 %collective-permute-start.15 = (bf16[4,64,256]{2,1,0:T(8,128)(2,1)S(1)}, bf16[4,64,256]{2,1,0:T(8,128)(2,1)S(1)}, u32[]{:S(2)}, u32[]{:S(2)}) collective-permute-start(bf16[4,64,256]{2,1,0:T(8,128)(2,1)S(1)} %get-tuple-element.37), channel_id=1, source_target_pairs={{0,1},{1,0},{2,3},{3,2},{4,5},{5,4},{6,7},{7,6},{8,9},{9,8},{10,11... | collective-permute-start | bytes 393224 | tf_op jit(solution)/shard_map/ppermute | solution.py:315
  14.7 7.0 %collective-permute-start.16 = (bf16[4,64,256]{2,1,0:T(8,128)(2,1)S(1)}, bf16[4,64,256]{2,1,0:T(8,128)(2,1)S(1)}, u32[]{:S(2)}, u32[]{:S(2)}) collective-permute-start(bf16[4,64,256]{2,1,0:T(8,128)(2,1)S(1)} %get-tuple-element.38), channel_id=1, source_target_pairs={{0,3},{1,2},{2,1},{3,0},{4,7},{5,6},{6,5},{7,4},{8,11},{9,10},{10,... | collective-permute-start | bytes 393224 | tf_op jit(solution)/shard_map/ppermute | solution.py:315
  18.1 7.0 %collective-permute-start.7 = (bf16[2,256,128]{2,1,0:T(8,128)(2,1)S(1)}, bf16[2,256,128]{2,1,0:T(8,128)(2,1)S(1)}, u32[]{:S(2)}, u32[]{:S(2)}) collective-permute-start(bf16[2,256,128]{2,1,0:T(8,128)(2,1)S(1)} %get-tuple-element.32.one), channel_id=1, source_target_pairs={{0,4},{1,5},{2,6},{3,7},{4,0},{5,1},{6,2},{7,3},{8,12},{9,13},{10,... | collective-permute-start | bytes 393224 | tf_op jit(solution)/shard_map/ppermute | solution.py:315
  19.8 5.4 %collective-permute-start.4 = (bf16[2,256,128]{2,1,0:T(8,128)(2,1)S(1)}, bf16[2,256,128]{2,1,0:T(8,128)(2,1)S(1)}, u32[]{:S(2)}, u32[]{:S(2)}) collective-permute-start(bf16[2,256,128]{2,1,0:T(8,128)(2,1)S(1)} %get-tuple-element.31.one), channel_id=1, source_target_pairs={{0,4},{1,5},{2,6},{3,7},{4,0},{5,1},{6,2},{7,3},{8,12},{9,13},{10,... | collective-permute-start | bytes 393224 | tf_op jit(solution)/shard_map/ppermute | solution.py:315
  23.0 6.4 %collective-permute-start.20 = (bf16[2,256,128]{2,1,0:T(8,128)(2,1)S(1)}, bf16[2,256,128]{2,1,0:T(8,128)(2,1)S(1)}, u32[]{:S(2)}, u32[]{:S(2)}) collective-permute-start(bf16[2,256,128]{2,1,0:T(8,128)(2,1)S(1)} %get-tuple-element.41.one), channel_id=1, source_target_pairs={{0,4},{1,5},{2,6},{3,7},{4,0},{5,1},{6,2},{7,3},{8,12},{9,13},{10,... | collective-permute-start | bytes 393224 | tf_op jit(solution)/shard_map/ppermute | solution.py:315
  24.8 6.0 %collective-permute-start.17 = (bf16[2,256,128]{2,1,0:T(8,128)(2,1)S(1)}, bf16[2,256,128]{2,1,0:T(8,128)(2,1)S(1)}, u32[]{:S(2)}, u32[]{:S(2)}) collective-permute-start(bf16[2,256,128]{2,1,0:T(8,128)(2,1)S(1)} %get-tuple-element.40.one), channel_id=1, source_target_pairs={{0,4},{1,5},{2,6},{3,7},{4,0},{5,1},{6,2},{7,3},{8,12},{9,13},{10,... | collective-permute-start | bytes 393224 | tf_op jit(solution)/shard_map/ppermute | solution.py:315
  25.1 5.8 %collective-permute-start.8 = (bf16[2,256,128]{2,1,0:T(8,128)(2,1)S(1)}, bf16[2,256,128]{2,1,0:T(8,128)(2,1)S(1)}, u32[]{:S(2)}, u32[]{:S(2)}) collective-permute-start(bf16[2,256,128]{2,1,0:T(8,128)(2,1)S(1)} %joint.5), channel_id=1, source_target_pairs={{0,16},{1,17},{2,18},{3,19},{4,8},{5,9},{6,10},{7,11},{8,4},{9,5},... | collective-permute-start | bytes 393224 | tf_op jit(solution)/shard_map/ppermute | solution.py:315
  25.3 9.0 %collective-permute-start.5 = (bf16[2,256,128]{2,1,0:T(8,128)(2,1)S(1)}, bf16[2,256,128]{2,1,0:T(8,128)(2,1)S(1)}, u32[]{:S(2)}, u32[]{:S(2)}) collective-permute-start(bf16[2,256,128]{2,1,0:T(8,128)(2,1)S(1)} %joint.4), channel_id=1, source_target_pairs={{0,16},{1,17},{2,18},{3,19},{4,8},{5,9},{6,10},{7,11},{8,4},{9,5},... | collective-permute-start | bytes 393224 | tf_op jit(solution)/shard_map/ppermute | solution.py:315
  29.5 6.7 %collective-permute-start.21 = (bf16[2,256,128]{2,1,0:T(8,128)(2,1)S(1)}, bf16[2,256,128]{2,1,0:T(8,128)(2,1)S(1)}, u32[]{:S(2)}, u32[]{:S(2)}) collective-permute-start(bf16[2,256,128]{2,1,0:T(8,128)(2,1)S(1)} %joint.7), channel_id=1, source_target_pairs={{0,16},{1,17},{2,18},{3,19},{4,8},{5,9},{6,10},{7,11},{8,4},{9,5},... | collective-permute-start | bytes 393224 | tf_op jit(solution)/shard_map/ppermute | solution.py:315
  30.9 7.5 %collective-permute-start.18 = (bf16[2,256,128]{2,1,0:T(8,128)(2,1)S(1)}, bf16[2,256,128]{2,1,0:T(8,128)(2,1)S(1)}, u32[]{:S(2)}, u32[]{:S(2)}) collective-permute-start(bf16[2,256,128]{2,1,0:T(8,128)(2,1)S(1)} %joint.6), channel_id=1, source_target_pairs={{0,16},{1,17},{2,18},{3,19},{4,8},{5,9},{6,10},{7,11},{8,4},{9,5},... | collective-permute-start | bytes 393224 | tf_op jit(solution)/shard_map/ppermute | solution.py:315
  31.0 8.8 %collective-permute-start.9 = (bf16[256,128]{1,0:T(8,128)(2,1)S(1)}, bf16[256,128]{1,0:T(8,128)(2,1)S(1)}, u32[]{:S(2)}, u32[]{:S(2)}) collective-permute-start(bf16[256,128]{1,0:T(8,128)(2,1)S(1)} %near.5), channel_id=1, source_target_pairs={{0,4},{1,5},{2,6},{3,7},{4,0},{5,1},{6,2},{7,3},{8,12},{9,13},{10,... | collective-permute-start | bytes 196616 | tf_op jit(solution)/shard_map/ppermute | solution.py:315
  34.3 5.5 %collective-permute-start.6 = (bf16[256,128]{1,0:T(8,128)(2,1)S(1)}, bf16[256,128]{1,0:T(8,128)(2,1)S(1)}, u32[]{:S(2)}, u32[]{:S(2)}) collective-permute-start(bf16[256,128]{1,0:T(8,128)(2,1)S(1)} %near.4), channel_id=1, source_target_pairs={{0,4},{1,5},{2,6},{3,7},{4,0},{5,1},{6,2},{7,3},{8,12},{9,13},{10,... | collective-permute-start | bytes 196616 | tf_op jit(solution)/shard_map/ppermute | solution.py:315
  36.2 7.3 %collective-permute-start.22 = (bf16[256,128]{1,0:T(8,128)(2,1)S(1)}, bf16[256,128]{1,0:T(8,128)(2,1)S(1)}, u32[]{:S(2)}, u32[]{:S(2)}) collective-permute-start(bf16[256,128]{1,0:T(8,128)(2,1)S(1)} %near.7), channel_id=1, source_target_pairs={{0,4},{1,5},{2,6},{3,7},{4,0},{5,1},{6,2},{7,3},{8,12},{9,13},{10,... | collective-permute-start | bytes 196616 | tf_op jit(solution)/shard_map/ppermute | solution.py:315
  38.4 5.0 %collective-permute-start.19 = (bf16[256,128]{1,0:T(8,128)(2,1)S(1)}, bf16[256,128]{1,0:T(8,128)(2,1)S(1)}, u32[]{:S(2)}, u32[]{:S(2)}) collective-permute-start(bf16[256,128]{1,0:T(8,128)(2,1)S(1)} %near.6), channel_id=1, source_target_pairs={{0,4},{1,5},{2,6},{3,7},{4,0},{5,1},{6,2},{7,3},{8,12},{9,13},{10,... | collective-permute-start | bytes 196616 | tf_op jit(solution)/shard_map/ppermute | solution.py:315
  39.9 6.4 %collective-permute-start.10 = (bf16[128,256]{1,0:T(8,128)(2,1)S(1)}, bf16[128,256]{1,0:T(8,128)(2,1)S(1)}, u32[]{:S(2)}, u32[]{:S(2)}) collective-permute-start(bf16[128,256]{1,0:T(8,128)(2,1)S(1)} %get-tuple-element.33.refs_1_), channel_id=1, source_target_pairs={{0,1},{1,0},{2,3},{3,2},{4,5},{5,4},{6,7},{7,6},{8,9},{9,8},{10,11... | collective-permute-start | bytes 196616 | tf_op jit(solution)/shard_map/ppermute | solution.py:315
  41.2 5.9 %collective-permute-start.11 = (bf16[128,256]{1,0:T(8,128)(2,1)S(1)}, bf16[128,256]{1,0:T(8,128)(2,1)S(1)}, u32[]{:S(2)}, u32[]{:S(2)}) collective-permute-start(bf16[128,256]{1,0:T(8,128)(2,1)S(1)} %get-tuple-element.34), channel_id=1, source_target_pairs={{0,3},{1,2},{2,1},{3,0},{4,7},{5,6},{6,5},{7,4},{8,11},{9,10},{10,... | collective-permute-start | bytes 196616 | tf_op jit(solution)/shard_map/ppermute | solution.py:315
  42.6 4.9 %collective-permute-start.12 = (bf16[128,256]{1,0:T(8,128)(2,1)S(1)}, bf16[128,256]{1,0:T(8,128)(2,1)S(1)}, u32[]{:S(2)}, u32[]{:S(2)}) collective-permute-start(bf16[128,256]{1,0:T(8,128)(2,1)S(1)} %get-tuple-element.34), channel_id=1, source_target_pairs={{0,2},{1,3},{2,0},{3,1},{4,6},{5,7},{6,4},{7,5},{8,10},{9,11},{10,... | collective-permute-start | bytes 196616 | tf_op jit(solution)/shard_map/ppermute | solution.py:315
  43.5 4.6 %collective-permute-start.23 = (bf16[128,256]{1,0:T(8,128)(2,1)S(1)}, bf16[128,256]{1,0:T(8,128)(2,1)S(1)}, u32[]{:S(2)}, u32[]{:S(2)}) collective-permute-start(bf16[128,256]{1,0:T(8,128)(2,1)S(1)} %get-tuple-element.42.refs_1_), channel_id=1, source_target_pairs={{0,1},{1,0},{2,3},{3,2},{4,5},{5,4},{6,7},{7,6},{8,9},{9,8},{10,11... | collective-permute-start | bytes 196616 | tf_op jit(solution)/shard_map/ppermute | solution.py:315
  44.8 6.4 %copy-start.1 = (bf16[4,1024,512]{2,1,0:T(8,128)(2,1)S(1)}, bf16[4,1024,512]{2,1,0:T(8,128)(2,1)}, u32[]{:S(2)}) copy-start(bf16[4,1024,512]{2,1,0:T(8,128)(2,1)} %refs_2_.3) | copy-start | bytes 12582916
  44.8 6.4 %copy-start.2 = (s32[1,4]{1,0:T(1,128)S(1)}, s32[1,4]{1,0:T(1,128)}, u32[]{:S(2)}) copy-start(s32[1,4]{1,0:T(1,128)} %refs_0_.5) | copy-start | bytes 52
  44.8 6.4 %copy-start.3 = (s32[16]{0:T(128)S(1)}, s32[16]{0:T(128)}, u32[]{:S(2)}) copy-start(s32[16]{0:T(128)} %refs_1_.1) | copy-start | bytes 196
  44.8 5.2 %collective-permute-start.24 = (bf16[128,256]{1,0:T(8,128)(2,1)S(1)}, bf16[128,256]{1,0:T(8,128)(2,1)S(1)}, u32[]{:S(2)}, u32[]{:S(2)}) collective-permute-start(bf16[128,256]{1,0:T(8,128)(2,1)S(1)} %get-tuple-element.43), channel_id=1, source_target_pairs={{0,3},{1,2},{2,1},{3,0},{4,7},{5,6},{6,5},{7,4},{8,11},{9,10},{10,... | collective-permute-start | bytes 196616 | tf_op jit(solution)/shard_map/ppermute | solution.py:315
  46.3 4.4 %collective-permute-start.25 = (bf16[128,256]{1,0:T(8,128)(2,1)S(1)}, bf16[128,256]{1,0:T(8,128)(2,1)S(1)}, u32[]{:S(2)}, u32[]{:S(2)}) collective-permute-start(bf16[128,256]{1,0:T(8,128)(2,1)S(1)} %get-tuple-element.43), channel_id=1, source_target_pairs={{0,2},{1,3},{2,0},{3,1},{4,6},{5,7},{6,4},{7,5},{8,10},{9,11},{10,... | collective-permute-start | bytes 196616 | tf_op jit(solution)/shard_map/ppermute | solution.py:315
  48.1 3.2 %collective-permute-start.13 = (bf16[128,1024]{1,0:T(8,128)(2,1)S(1)}, bf16[128,1024]{1,0:T(8,128)(2,1)S(1)}, u32[]{:S(2)}, u32[]{:S(2)}) collective-permute-start(bf16[128,1024]{1,0:T(8,128)(2,1)S(1)} %phase.2.refs_3_), channel_id=1, source_target_pairs={{0,16},{1,17},{2,18},{3,19},{4,20},{5,21},{6,22},{7,23},{8,24},{9,... | collective-permute-start | bytes 786440 | tf_op jit(solution)/shard_map/ppermute | solution.py:315
  51.1 1.6 %collective-permute-start.26 = (bf16[128,1024]{1,0:T(8,128)(2,1)S(1)}, bf16[128,1024]{1,0:T(8,128)(2,1)S(1)}, u32[]{:S(2)}, u32[]{:S(2)}) collective-permute-start(bf16[128,1024]{1,0:T(8,128)(2,1)S(1)} %phase.3.refs_5_), channel_id=1, source_target_pairs={{0,16},{1,17},{2,18},{3,19},{4,20},{5,21},{6,22},{7,23},{8,24},{9,... | collective-permute-start | bytes 786440 | tf_op jit(solution)/shard_map/ppermute | solution.py:315

commit v13 on v12

--- a/solution.py
+++ b/solution.py
@@ -13,7 +13,7 @@
 bf16 = jnp.bfloat16
 f32 = jnp.float32
 send_order = (0, 2, 1, 3)
-tail_order = (0, 1, 3, 2)
+tail_order = (0, 2, 3, 1)
 
 
 def hartley(length):
@@ -98,21 +98,24 @@
     return lax.axis_index("dist"), device // inner, device % inner
 
 
-def row_kernel(inner, chunk, holo, there, table, after, *refs):
-    outs, flat, loaded = refs[:inner], refs[inner], refs[inner + 1]
+def row_kernel(inner, holo, there, table, after, *refs):
+    outs, mine, loaded = refs[:-2], refs[-2], refs[-1]
+    own = len(outs) // inner
     core, _, spot = position(inner)
-    angles, dist_dev, rows_dev, width = there.shape
+    _, dist_dev, rows_dev, width = there.shape
     block = width // inner
-    angle = core * (angles // 2) + chunk
-    copy = pltpu.make_async_copy(holo.at[angle], flat.at[pl.ds(0, dist_dev)], loaded)
+    copy = pltpu.make_async_copy(holo.at[pl.ds(core * own, own)], mine, loaded)
     copy.start()
-    flat[dist_dev:] = there[angle]
-    copy.wait()
-    rows = flat[...].reshape(2 * dist_dev * rows_dev, width)
-    for rel in range(inner):
-        part = table[:, pl.ds(pl.multiple_of((spot ^ rel) * block, block), block)]
-        got = jnp.dot(rows, part, preferred_element_type=f32).astype(bf16)
-        outs[rel][...] = got.reshape(2 * dist_dev, rows_dev, block)
+    for first, source in ((dist_dev, there.at[pl.ds(core * own, own)]), (0, mine)):
+        if first == 0:
+            copy.wait()
+        rows = source[...].reshape(own * dist_dev * rows_dev, width)
+        for rel in range(inner):
+            part = table[:, pl.ds(pl.multiple_of((spot ^ rel) * block, block), block)]
+            got = jnp.dot(rows, part, preferred_element_type=f32).astype(bf16)
+            got = got.reshape(own, dist_dev, rows_dev, block)
+            for chunk in range(own):
+                outs[chunk * inner + rel][first : first + dist_dev] = got[chunk]
 
 
 def whole_turns(scale, square):
@@ -340,22 +343,22 @@
         cost_estimate=cheap,
         name="filters",
     )(propagation * (0.5 / math.pi))
-    arrived = []
-    for chunk in range(own):
-        pieces = pl.pallas_call(
-            lambda *refs, chunk=chunk: row_kernel(inner, chunk, *refs),
-            out_shape=[shaped(dists, rows_dev, block)] * inner,
-            in_specs=in_hbm(1) + vmem(2) + unread(1),
-            out_specs=vmem(inner),
-            scratch_shapes=[
-                pltpu.VMEM((dists, rows_dev, width), bf16),
-                pltpu.SemaphoreType.DMA,
-            ],
-            compiler_params=params,
-            cost_estimate=cheap,
-            name="row_spectra",
-        )(from_hbm(holograms[0]), partner, table, gain)
-        arrived.append(spread(pieces, send_order))
+    pieces = pl.pallas_call(
+        lambda *refs: row_kernel(inner, *refs),
+        out_shape=[shaped(dists, rows_dev, block)] * (own * inner),
+        in_specs=in_hbm(1) + vmem(2) + unread(1),
+        out_specs=vmem(own * inner),
+        scratch_shapes=[
+            pltpu.VMEM((own, dist_dev, rows_dev, width), bf16),
+            pltpu.SemaphoreType.DMA,
+        ],
+        compiler_params=params,
+        cost_estimate=cheap,
+        name="row_spectra",
+    )(from_hbm(holograms[0]), partner, table, gain)
+    arrived = [
+        spread(pieces[chunk * inner : (chunk + 1) * inner], send_order) for chunk in range(own)
+    ]
 
     sums = []
     for chunk in range(own):

time: 54 us -> 54.1 us (level)
  starting transfers between devices: 29 us -> 30.7 us
  Pallas kernels: 12 us -> 10.4 us
    ppermute x27, starting transfers between devices: 29 us -> 30.7 us  [sent(): return lax.ppermute(value, ('dist', 'rows'), pairs)]
    pallas_call x2 -> x1, Pallas kernels: 3.44 us -> 1.82 us  [plane_plan(): pl.pallas_call(lambda *refs: row_kernel(inner, *refs), out_shape=[shaped(...]
  transfers between devices with their start and end apart: 27 -> 27, of which waited for: 8 -> 8; matrix products, arithmetic and copies ran while one was open for 2% -> 2% of each run, Pallas kernels for 17% -> 14%
where the time goes in v13:
time: 54.1 us; the launch traced here: 53.9 us
  starting transfers between devices  30.7 us (57%)
  waiting for transfers between devices  11.8 us (22%)
  Pallas kernels  10.4 us (19%)
  other arithmetic  0.83 us (2%)
    ppermute x27, starting transfers between devices, sent(): return lax.ppermute(value, ('dist', 'rows'), pairs)  30.7 us
    ppermute x27, waiting for transfers between devices, sent(): return lax.ppermute(value, ('dist', 'rows'), pairs)  11.8 us
    pallas_call x2, Pallas kernels, plane_plan(): pl.pallas_call(lambda *refs: column_kernel(inner, outer, *refs), out_shap...  2.59 us
    pallas_call x1, Pallas kernels, plane_plan(): pl.pallas_call(lambda *refs: filter_kernel(inner, dist_dev, *refs), out_s...  2.37 us
    pallas_call x1, Pallas kernels, plane_plan(): pl.pallas_call(lambda *refs: row_kernel(inner, *refs), out_shape=[shaped(...  1.82 us
    pallas_call x1, Pallas kernels, plane_plan(): pl.pallas_call(lambda *refs: recon_kernel(own, *refs), out_shape=[jax.Sha...  1.2 us
    pallas_call x1, Pallas kernels, plane_plan(): pl.pallas_call(recon_last_kernel, out_shape=shaped(capacity, pixels), in_...  1.12 us
  transfers between devices with their start and end apart: 27, of which 8 were waited for; matrix products, arithmetic and copies ran while one was open for 2% of the time, Pallas kernels for 14%

profile of v13, /device:TPU:0, one launch (start us, length us, event | category | flops | bytes accessed | tf_op | source)
XLA Modules:
  0.0 53.9 jit_solution(755709524661359462)
XLA Ops:
  0.0 0.5 collective-permute-start
  0.5 0.8 %broadcast_multiply_fusion.refs_0_ = f32[4]{0:T(128)S(1)} fusion(f32[4]{0:T(128)} %param.7), kind=kLoop, calls=%fused_computation | loop fusion | flops 4 | bytes 32 | tf_op jit(solution)/shard_map/mul | solution.py:345
  1.3 2.4 %filters.1.refs_3_.refs_1_ = bf16[4,1024,256]{2,1,0:T(8,128)(2,1)S(1)} custom-call(f32[4]{0:T(128)S(1)} %broadcast_multiply_fusion.refs_0_), custom_call_target="tpu_custom_call" | custom-call | flops 1 | bytes 1 | tf_op jit(solution)/shard_map/filters/pallas_call | solution.py:337
  3.7 0.0 collective-permute-done.refs_1_
  3.7 1.8 %row_spectra.1 = (bf16[4,64,256]{2,1,0:T(8,128)(2,1)S(1)}, bf16[4,64,256]{2,1,0:T(8,128)(2,1)S(1)}, bf16[4,64,256]{2,1,0:T(8,128)(2,1)S(1)}, bf16[4,64,256]{2,1,...) custom-call(bf16[4,2,64,1024]{3,2,1,0:T(8,128)(2,1)} %bitcast.2, ...), custom_call_target="tpu_custom_call" | custom-call | flops 1 | bytes 1 | tf_op jit(solution)/shard_map/row_spectra/pallas_call | solution.py:346
  5.5 2.6 %collective-permute-start.1 = (bf16[4,64,256]{2,1,0:T(8,128)(2,1)S(1)}, bf16[4,64,256]{2,1,0:T(8,128)(2,1)S(1)}, u32[]{:S(2)}, u32[]{:S(2)}) collective-permute-start(bf16[4,64,256]{2,1,0:T(8,128)(2,1)S(1)} %get-tuple-element.27), channel_id=1, source_target_pairs={{0,2},{1,3},{2,0},{3,1},{4,6},{5,7},{6,4},{7,5},{8,10},{9,11},{10,... | collective-permute-start | bytes 393224 | tf_op jit(solution)/shard_map/ppermute | solution.py:318
  8.1 1.5 %collective-permute-start.2 = (bf16[4,64,256]{2,1,0:T(8,128)(2,1)S(1)}, bf16[4,64,256]{2,1,0:T(8,128)(2,1)S(1)}, u32[]{:S(2)}, u32[]{:S(2)}) collective-permute-start(bf16[4,64,256]{2,1,0:T(8,128)(2,1)S(1)} %get-tuple-element.28), channel_id=1, source_target_pairs={{0,1},{1,0},{2,3},{3,2},{4,5},{5,4},{6,7},{7,6},{8,9},{9,8},{10,11... | collective-permute-start | bytes 393224 | tf_op jit(solution)/shard_map/ppermute | solution.py:318
  9.6 0.0 collective-permute-start.3
  9.6 1.9 %collective-permute-start.14 = (bf16[4,64,256]{2,1,0:T(8,128)(2,1)S(1)}, bf16[4,64,256]{2,1,0:T(8,128)(2,1)S(1)}, u32[]{:S(2)}, u32[]{:S(2)}) collective-permute-start(bf16[4,64,256]{2,1,0:T(8,128)(2,1)S(1)} %get-tuple-element.36), channel_id=1, source_target_pairs={{0,2},{1,3},{2,0},{3,1},{4,6},{5,7},{6,4},{7,5},{8,10},{9,11},{10,... | collective-permute-start | bytes 393224 | tf_op jit(solution)/shard_map/ppermute | solution.py:318
  11.6 1.5 %collective-permute-start.15 = (bf16[4,64,256]{2,1,0:T(8,128)(2,1)S(1)}, bf16[4,64,256]{2,1,0:T(8,128)(2,1)S(1)}, u32[]{:S(2)}, u32[]{:S(2)}) collective-permute-start(bf16[4,64,256]{2,1,0:T(8,128)(2,1)S(1)} %get-tuple-element.37), channel_id=1, source_target_pairs={{0,1},{1,0},{2,3},{3,2},{4,5},{5,4},{6,7},{7,6},{8,9},{9,8},{10,11... | collective-permute-start | bytes 393224 | tf_op jit(solution)/shard_map/ppermute | solution.py:318
  13.1 0.0 collective-permute-done.1.refs_3_
  13.1 1.8 %collective-permute-start.16 = (bf16[4,64,256]{2,1,0:T(8,128)(2,1)S(1)}, bf16[4,64,256]{2,1,0:T(8,128)(2,1)S(1)}, u32[]{:S(2)}, u32[]{:S(2)}) collective-permute-start(bf16[4,64,256]{2,1,0:T(8,128)(2,1)S(1)} %get-tuple-element.38), channel_id=1, source_target_pairs={{0,3},{1,2},{2,1},{3,0},{4,7},{5,6},{6,5},{7,4},{8,11},{9,10},{10,... | collective-permute-start | bytes 393224 | tf_op jit(solution)/shard_map/ppermute | solution.py:318
  14.8 0.0 collective-permute-done.2.refs_4_
  14.8 2.1 %collective-permute-done.3.refs_5_ = bf16[4,64,256]{2,1,0:T(8,128)(2,1)S(1)} collective-permute-done((bf16[4,64,256]{2,1,0:T(8,128)(2,1)S(1)}, bf16[4,64,256]{2,1,0:T(8,128)(2,1)S(1)}, u32[]{:S(2)}, u32[]{:S(2)}) %collective-permute-start.3) | collective-permute-done | bytes 131104 | tf_op jit(solution)/shard_map/ppermute | solution.py:318
  16.9 1.3 %columns.2 = (bf16[2,256,256]{2,1,0:T(8,128)(2,1)S(1)}, bf16[2,256,128]{2,1,0:T(8,128)(2,1)S(1)}, bf16[2,256,128]{2,1,0:T(8,128)(2,1)S(1)}) custom-call(bf16[1024,1024]{1,0:T(8,128)(2,1)S(1)} %copy-done, bf16[4,1024,256]{2,1,0:T(8,128)(2,1)S(1)} %filters.1.refs_3_.refs_1_, bf16[4,64,256]{2,1,0:T(8,128)(2,1)S(1)} %get-tuple-element.26.refs_2_, ...), custom_call_target="tpu_custom_call" | custom-call | flops 1 | bytes 1 | tf_op jit(solution)/shard_map/columns/pallas_call | solution.py:365
  18.2 1.7 %collective-permute-start.4 = (bf16[2,256,128]{2,1,0:T(8,128)(2,1)S(1)}, bf16[2,256,128]{2,1,0:T(8,128)(2,1)S(1)}, u32[]{:S(2)}, u32[]{:S(2)}) collective-permute-start(bf16[2,256,128]{2,1,0:T(8,128)(2,1)S(1)} %get-tuple-element.31.one), channel_id=1, source_target_pairs={{0,4},{1,5},{2,6},{3,7},{4,0},{5,1},{6,2},{7,3},{8,12},{9,13},{10,... | collective-permute-start | bytes 393224 | tf_op jit(solution)/shard_map/ppermute | solution.py:318
  19.9 0.4 collective-permute-start.7
  20.3 0.0 collective-permute-done.14.refs_3_
  20.3 0.0 collective-permute-done.15.refs_4_
  20.3 1.5 %collective-permute-done.16.refs_5_ = bf16[4,64,256]{2,1,0:T(8,128)(2,1)S(1)} collective-permute-done((bf16[4,64,256]{2,1,0:T(8,128)(2,1)S(1)}, bf16[4,64,256]{2,1,0:T(8,128)(2,1)S(1)}, u32[]{:S(2)}, u32[]{:S(2)}) %collective-permute-start.16) | collective-permute-done | bytes 131104 | tf_op jit(solution)/shard_map/ppermute | solution.py:318
  21.8 1.3 %columns.3 = (bf16[2,256,256]{2,1,0:T(8,128)(2,1)S(1)}, bf16[2,256,128]{2,1,0:T(8,128)(2,1)S(1)}, bf16[2,256,128]{2,1,0:T(8,128)(2,1)S(1)}) custom-call(bf16[1024,1024]{1,0:T(8,128)(2,1)S(1)} %copy-done, bf16[4,1024,256]{2,1,0:T(8,128)(2,1)S(1)} %filters.1.refs_3_.refs_1_, bf16[4,64,256]{2,1,0:T(8,128)(2,1)S(1)} %get-tuple-element.35.refs_2_, ...), custom_call_target="tpu_custom_call" | custom-call | flops 1 | bytes 1 | tf_op jit(solution)/shard_map/columns/pallas_call | solution.py:365
  23.1 1.8 %collective-permute-start.17 = (bf16[2,256,128]{2,1,0:T(8,128)(2,1)S(1)}, bf16[2,256,128]{2,1,0:T(8,128)(2,1)S(1)}, u32[]{:S(2)}, u32[]{:S(2)}) collective-permute-start(bf16[2,256,128]{2,1,0:T(8,128)(2,1)S(1)} %get-tuple-element.40.one), channel_id=1, source_target_pairs={{0,4},{1,5},{2,6},{3,7},{4,0},{5,1},{6,2},{7,3},{8,12},{9,13},{10,... | collective-permute-start | bytes 393224 | tf_op jit(solution)/shard_map/ppermute | solution.py:318
  24.9 0.3 collective-permute-start.20
  25.2 0.0 collective-permute-done.4.two
  25.2 0.1 collective-permute-start.5
  25.3 0.0 collective-permute-done.7.two
  25.4 0.5 %collective-permute-start.8 = (bf16[2,256,128]{2,1,0:T(8,128)(2,1)S(1)}, bf16[2,256,128]{2,1,0:T(8,128)(2,1)S(1)}, u32[]{:S(2)}, u32[]{:S(2)}) collective-permute-start(bf16[2,256,128]{2,1,0:T(8,128)(2,1)S(1)} %joint.5), channel_id=1, source_target_pairs={{0,16},{1,17},{2,18},{3,19},{4,8},{5,9},{6,10},{7,11},{8,4},{9,5},... | collective-permute-start | bytes 393224 | tf_op jit(solution)/shard_map/ppermute | solution.py:318
  25.9 3.6 %collective-permute-done.17.two = bf16[2,256,128]{2,1,0:T(8,128)(2,1)S(1)} collective-permute-done((bf16[2,256,128]{2,1,0:T(8,128)(2,1)S(1)}, bf16[2,256,128]{2,1,0:T(8,128)(2,1)S(1)}, u32[]{:S(2)}, u32[]{:S(2)}) %collective-permute-start.17) | collective-permute-done | bytes 131104 | tf_op jit(solution)/shard_map/ppermute | solution.py:318
  29.6 0.1 collective-permute-start.18
  29.6 1.3 %collective-permute-done.20.two = bf16[2,256,128]{2,1,0:T(8,128)(2,1)S(1)} collective-permute-done((bf16[2,256,128]{2,1,0:T(8,128)(2,1)S(1)}, bf16[2,256,128]{2,1,0:T(8,128)(2,1)S(1)}, u32[]{:S(2)}, u32[]{:S(2)}) %collective-permute-start.20) | collective-permute-done | bytes 131104 | tf_op jit(solution)/shard_map/ppermute | solution.py:318
  31.0 0.1 collective-permute-start.21
  31.0 0.0 collective-permute-done.5.refs_1_
  31.1 3.3 %collective-permute-start.6 = (bf16[256,128]{1,0:T(8,128)(2,1)S(1)}, bf16[256,128]{1,0:T(8,128)(2,1)S(1)}, u32[]{:S(2)}, u32[]{:S(2)}) collective-permute-start(bf16[256,128]{1,0:T(8,128)(2,1)S(1)} %near.4), channel_id=1, source_target_pairs={{0,4},{1,5},{2,6},{3,7},{4,0},{5,1},{6,2},{7,3},{8,12},{9,13},{10,... | collective-permute-start | bytes 196616 | tf_op jit(solution)/shard_map/ppermute | solution.py:318
  34.4 0.0 collective-permute-done.8.refs_1_.refs_3_
  34.4 1.8 %collective-permute-start.9 = (bf16[256,128]{1,0:T(8,128)(2,1)S(1)}, bf16[256,128]{1,0:T(8,128)(2,1)S(1)}, u32[]{:S(2)}, u32[]{:S(2)}) collective-permute-start(bf16[256,128]{1,0:T(8,128)(2,1)S(1)} %near.5), channel_id=1, source_target_pairs={{0,4},{1,5},{2,6},{3,7},{4,0},{5,1},{6,2},{7,3},{8,12},{9,13},{10,... | collective-permute-start | bytes 196616 | tf_op jit(solution)/shard_map/ppermute | solution.py:318
  36.2 0.0 collective-permute-done.18.refs_1_
  36.3 2.2 %collective-permute-start.19 = (bf16[256,128]{1,0:T(8,128)(2,1)S(1)}, bf16[256,128]{1,0:T(8,128)(2,1)S(1)}, u32[]{:S(2)}, u32[]{:S(2)}) collective-permute-start(bf16[256,128]{1,0:T(8,128)(2,1)S(1)} %near.6), channel_id=1, source_target_pairs={{0,4},{1,5},{2,6},{3,7},{4,0},{5,1},{6,2},{7,3},{8,12},{9,13},{10,... | collective-permute-start | bytes 196616 | tf_op jit(solution)/shard_map/ppermute | solution.py:318
  38.5 0.0 collective-permute-done.21.refs_1_.refs_3_
  38.5 1.4 %collective-permute-start.22 = (bf16[256,128]{1,0:T(8,128)(2,1)S(1)}, bf16[256,128]{1,0:T(8,128)(2,1)S(1)}, u32[]{:S(2)}, u32[]{:S(2)}) collective-permute-start(bf16[256,128]{1,0:T(8,128)(2,1)S(1)} %near.7), channel_id=1, source_target_pairs={{0,4},{1,5},{2,6},{3,7},{4,0},{5,1},{6,2},{7,3},{8,12},{9,13},{10,... | collective-permute-start | bytes 196616 | tf_op jit(solution)/shard_map/ppermute | solution.py:318
  39.9 0.0 collective-permute-done.6.refs_2_
  39.9 0.0 collective-permute-done.9.refs_4_
  39.9 0.1 half.2
  40.0 1.3 %collective-permute-start.12 = (bf16[128,256]{1,0:T(8,128)(2,1)S(1)}, bf16[128,256]{1,0:T(8,128)(2,1)S(1)}, u32[]{:S(2)}, u32[]{:S(2)}) collective-permute-start(bf16[128,256]{1,0:T(8,128)(2,1)S(1)} %get-tuple-element.33.refs_1_), channel_id=1, source_target_pairs={{0,1},{1,0},{2,3},{3,2},{4,5},{5,4},{6,7},{7,6},{8,9},{9,8},{10,11... | collective-permute-start | bytes 196616 | tf_op jit(solution)/shard_map/ppermute | solution.py:318
  41.3 1.5 %collective-permute-start.11 = (bf16[128,256]{1,0:T(8,128)(2,1)S(1)}, bf16[128,256]{1,0:T(8,128)(2,1)S(1)}, u32[]{:S(2)}, u32[]{:S(2)}) collective-permute-start(bf16[128,256]{1,0:T(8,128)(2,1)S(1)} %get-tuple-element.34), channel_id=1, source_target_pairs={{0,3},{1,2},{2,1},{3,0},{4,7},{5,6},{6,5},{7,4},{8,11},{9,10},{10,... | collective-permute-start | bytes 196616 | tf_op jit(solution)/shard_map/ppermute | solution.py:318
  42.8 0.8 %collective-permute-start.10 = (bf16[128,256]{1,0:T(8,128)(2,1)S(1)}, bf16[128,256]{1,0:T(8,128)(2,1)S(1)}, u32[]{:S(2)}, u32[]{:S(2)}) collective-permute-start(bf16[128,256]{1,0:T(8,128)(2,1)S(1)} %get-tuple-element.34), channel_id=1, source_target_pairs={{0,2},{1,3},{2,0},{3,1},{4,6},{5,7},{6,4},{7,5},{8,10},{9,11},{10,... | collective-permute-start | bytes 196616 | tf_op jit(solution)/shard_map/ppermute | solution.py:318
  43.6 0.0 collective-permute-done.19.refs_2_
  43.6 0.0 collective-permute-done.22.refs_4_
  43.6 0.1 half.3
  43.6 1.3 %collective-permute-start.25 = (bf16[128,256]{1,0:T(8,128)(2,1)S(1)}, bf16[128,256]{1,0:T(8,128)(2,1)S(1)}, u32[]{:S(2)}, u32[]{:S(2)}) collective-permute-start(bf16[128,256]{1,0:T(8,128)(2,1)S(1)} %get-tuple-element.42.refs_1_), channel_id=1, source_target_pairs={{0,1},{1,0},{2,3},{3,2},{4,5},{5,4},{6,7},{7,6},{8,9},{9,8},{10,11... | collective-permute-start | bytes 196616 | tf_op jit(solution)/shard_map/ppermute | solution.py:318
  44.9 1.5 %collective-permute-start.24 = (bf16[128,256]{1,0:T(8,128)(2,1)S(1)}, bf16[128,256]{1,0:T(8,128)(2,1)S(1)}, u32[]{:S(2)}, u32[]{:S(2)}) collective-permute-start(bf16[128,256]{1,0:T(8,128)(2,1)S(1)} %get-tuple-element.43), channel_id=1, source_target_pairs={{0,3},{1,2},{2,1},{3,0},{4,7},{5,6},{6,5},{7,4},{8,11},{9,10},{10,... | collective-permute-start | bytes 196616 | tf_op jit(solution)/shard_map/ppermute | solution.py:318
  46.4 0.0 collective-permute-done.12.refs_4_
  46.4 0.8 %collective-permute-start.23 = (bf16[128,256]{1,0:T(8,128)(2,1)S(1)}, bf16[128,256]{1,0:T(8,128)(2,1)S(1)}, u32[]{:S(2)}, u32[]{:S(2)}) collective-permute-start(bf16[128,256]{1,0:T(8,128)(2,1)S(1)} %get-tuple-element.43), channel_id=1, source_target_pairs={{0,2},{1,3},{2,0},{3,1},{4,6},{5,7},{6,4},{7,5},{8,10},{9,11},{10,... | collective-permute-start | bytes 196616 | tf_op jit(solution)/shard_map/ppermute | solution.py:318
  47.2 0.0 collective-permute-done.11.refs_3_
  47.2 0.5 collective-permute-done.10.refs_2_
  47.7 0.5 phase.2.refs_3_
  48.2 0.1 collective-permute-start.13
  48.3 0.0 collective-permute-done.25.refs_4_
  48.3 1.8 %collective-permute-done.24.refs_3_ = bf16[128,256]{1,0:T(8,128)(2,1)S(1)} collective-permute-done((bf16[128,256]{1,0:T(8,128)(2,1)S(1)}, bf16[128,256]{1,0:T(8,128)(2,1)S(1)}, u32[]{:S(2)}, u32[]{:S(2)}) %collective-permute-start.24) | collective-permute-done | bytes 65568 | tf_op jit(solution)/shard_map/ppermute | solution.py:318
  50.1 0.7 %collective-permute-done.23.refs_2_ = bf16[128,256]{1,0:T(8,128)(2,1)S(1)} collective-permute-done((bf16[128,256]{1,0:T(8,128)(2,1)S(1)}, bf16[128,256]{1,0:T(8,128)(2,1)S(1)}, u32[]{:S(2)}, u32[]{:S(2)}) %collective-permute-start.23) | collective-permute-done | bytes 65568 | tf_op jit(solution)/shard_map/ppermute | solution.py:318
  50.8 0.5 phase.3.refs_5_
  51.2 0.1 collective-permute-start.26
  51.3 1.2 %recon.2 = (f32[128,512]{1,0:T(8,128)S(1)}, bf16[1024,512]{1,0:T(8,128)(2,1)S(1)}, bf16[128,128]{1,0:T(8,128)(2,1)S(1)}) custom-call(s32[1,4]{1,0:T(1,128)S(1)} %copy-done.2, s32[16]{0:T(128)S(1)} %copy-done.3, bf16[4,1024,512]{2,1,0:T(8,128)(2,1)S(1)} %copy-done.1, bf16[128,1024]{1,0:T(8,128)(2,1)S(1)} %phase.2.refs_3_, ...), custom_call_target="tpu_custom_call" | custom-call | flops 1 | bytes 1 | tf_op jit(solution)/shard_map/recon/pallas_call | solution.py:428
  52.6 0.3 collective-permute-done.26.phase
  52.8 1.1 %recon.3 = bf16[128,512]{1,0:T(8,128)(2,1)} custom-call(bf16[1024,512]{1,0:T(8,128)(2,1)S(1)} %get-tuple-element.44.weights, bf16[128,1024]{1,0:T(8,128)(2,1)S(1)} %collective-permute-done.26.phase, f32[128,512]{1,0:T(8,128)S(1)} %get-tuple-element.45.before, bf16[128,128]{1,0:T(8,128)(2,1)S(1)} %get-tuple-element.46.select), custom_call_target="tpu_custom_call" | custom-call | flops 1 | bytes 1 | tf_op jit(solution)/shard_map/recon/pallas_call | solution.py:441
  (17 shorter events, 0.3 us)
Async XLA Ops:
  0.0 3.7 %copy-start = (bf16[1024,1024]{1,0:T(8,128)(2,1)S(1)}, bf16[1024,1024]{1,0:T(8,128)(2,1)}, u32[]{:S(2)}) copy-start(bf16[1024,1024]{1,0:T(8,128)(2,1)} %constant.4.clone.refs_2_.refs_0_) | copy-start | bytes 6291460
  0.0 3.7 %collective-permute-start = (bf16[4,2,64,1024]{3,2,1,0:T(8,128)(2,1)}, bf16[4,2,64,1024]{3,2,1,0:T(8,128)(2,1)S(1)}, u32[]{:S(2)}, u32[]{:S(2)}) collective-permute-start(bf16[4,2,64,1024]{3,2,1,0:T(8,128)(2,1)} %bitcast.1), channel_id=1, source_target_pairs={{0,16},{1,17},{2,18},{3,19},{4,20},{5,21},{6,22},{7,23},{8,24},{9,... | collective-permute-start | bytes 3145736 | tf_op jit(solution)/shard_map/ppermute | solution.py:318
  5.5 7.6 %collective-permute-start.1 = (bf16[4,64,256]{2,1,0:T(8,128)(2,1)S(1)}, bf16[4,64,256]{2,1,0:T(8,128)(2,1)S(1)}, u32[]{:S(2)}, u32[]{:S(2)}) collective-permute-start(bf16[4,64,256]{2,1,0:T(8,128)(2,1)S(1)} %get-tuple-element.27), channel_id=1, source_target_pairs={{0,2},{1,3},{2,0},{3,1},{4,6},{5,7},{6,4},{7,5},{8,10},{9,11},{10,... | collective-permute-start | bytes 393224 | tf_op jit(solution)/shard_map/ppermute | solution.py:318
  8.1 6.8 %collective-permute-start.2 = (bf16[4,64,256]{2,1,0:T(8,128)(2,1)S(1)}, bf16[4,64,256]{2,1,0:T(8,128)(2,1)S(1)}, u32[]{:S(2)}, u32[]{:S(2)}) collective-permute-start(bf16[4,64,256]{2,1,0:T(8,128)(2,1)S(1)} %get-tuple-element.28), channel_id=1, source_target_pairs={{0,1},{1,0},{2,3},{3,2},{4,5},{5,4},{6,7},{7,6},{8,9},{9,8},{10,11... | collective-permute-start | bytes 393224 | tf_op jit(solution)/shard_map/ppermute | solution.py:318
  9.6 7.3 %collective-permute-start.3 = (bf16[4,64,256]{2,1,0:T(8,128)(2,1)S(1)}, bf16[4,64,256]{2,1,0:T(8,128)(2,1)S(1)}, u32[]{:S(2)}, u32[]{:S(2)}) collective-permute-start(bf16[4,64,256]{2,1,0:T(8,128)(2,1)S(1)} %get-tuple-element.29), channel_id=1, source_target_pairs={{0,3},{1,2},{2,1},{3,0},{4,7},{5,6},{6,5},{7,4},{8,11},{9,10},{10,... | collective-permute-start | bytes 393224 | tf_op jit(solution)/shard_map/ppermute | solution.py:318
  9.6 10.7 %collective-permute-start.14 = (bf16[4,64,256]{2,1,0:T(8,128)(2,1)S(1)}, bf16[4,64,256]{2,1,0:T(8,128)(2,1)S(1)}, u32[]{:S(2)}, u32[]{:S(2)}) collective-permute-start(bf16[4,64,256]{2,1,0:T(8,128)(2,1)S(1)} %get-tuple-element.36), channel_id=1, source_target_pairs={{0,2},{1,3},{2,0},{3,1},{4,6},{5,7},{6,4},{7,5},{8,10},{9,11},{10,... | collective-permute-start | bytes 393224 | tf_op jit(solution)/shard_map/ppermute | solution.py:318
  11.6 8.7 %collective-permute-start.15 = (bf16[4,64,256]{2,1,0:T(8,128)(2,1)S(1)}, bf16[4,64,256]{2,1,0:T(8,128)(2,1)S(1)}, u32[]{:S(2)}, u32[]{:S(2)}) collective-permute-start(bf16[4,64,256]{2,1,0:T(8,128)(2,1)S(1)} %get-tuple-element.37), channel_id=1, source_target_pairs={{0,1},{1,0},{2,3},{3,2},{4,5},{5,4},{6,7},{7,6},{8,9},{9,8},{10,11... | collective-permute-start | bytes 393224 | tf_op jit(solution)/shard_map/ppermute | solution.py:318
  13.1 8.7 %collective-permute-start.16 = (bf16[4,64,256]{2,1,0:T(8,128)(2,1)S(1)}, bf16[4,64,256]{2,1,0:T(8,128)(2,1)S(1)}, u32[]{:S(2)}, u32[]{:S(2)}) collective-permute-start(bf16[4,64,256]{2,1,0:T(8,128)(2,1)S(1)} %get-tuple-element.38), channel_id=1, source_target_pairs={{0,3},{1,2},{2,1},{3,0},{4,7},{5,6},{6,5},{7,4},{8,11},{9,10},{10,... | collective-permute-start | bytes 393224 | tf_op jit(solution)/shard_map/ppermute | solution.py:318
  18.2 7.0 %collective-permute-start.4 = (bf16[2,256,128]{2,1,0:T(8,128)(2,1)S(1)}, bf16[2,256,128]{2,1,0:T(8,128)(2,1)S(1)}, u32[]{:S(2)}, u32[]{:S(2)}) collective-permute-start(bf16[2,256,128]{2,1,0:T(8,128)(2,1)S(1)} %get-tuple-element.31.one), channel_id=1, source_target_pairs={{0,4},{1,5},{2,6},{3,7},{4,0},{5,1},{6,2},{7,3},{8,12},{9,13},{10,... | collective-permute-start | bytes 393224 | tf_op jit(solution)/shard_map/ppermute | solution.py:318
  19.9 5.4 %collective-permute-start.7 = (bf16[2,256,128]{2,1,0:T(8,128)(2,1)S(1)}, bf16[2,256,128]{2,1,0:T(8,128)(2,1)S(1)}, u32[]{:S(2)}, u32[]{:S(2)}) collective-permute-start(bf16[2,256,128]{2,1,0:T(8,128)(2,1)S(1)} %get-tuple-element.32.one), channel_id=1, source_target_pairs={{0,4},{1,5},{2,6},{3,7},{4,0},{5,1},{6,2},{7,3},{8,12},{9,13},{10,... | collective-permute-start | bytes 393224 | tf_op jit(solution)/shard_map/ppermute | solution.py:318
  23.1 6.4 %collective-permute-start.17 = (bf16[2,256,128]{2,1,0:T(8,128)(2,1)S(1)}, bf16[2,256,128]{2,1,0:T(8,128)(2,1)S(1)}, u32[]{:S(2)}, u32[]{:S(2)}) collective-permute-start(bf16[2,256,128]{2,1,0:T(8,128)(2,1)S(1)} %get-tuple-element.40.one), channel_id=1, source_target_pairs={{0,4},{1,5},{2,6},{3,7},{4,0},{5,1},{6,2},{7,3},{8,12},{9,13},{10,... | collective-permute-start | bytes 393224 | tf_op jit(solution)/shard_map/ppermute | solution.py:318
  24.9 6.0 %collective-permute-start.20 = (bf16[2,256,128]{2,1,0:T(8,128)(2,1)S(1)}, bf16[2,256,128]{2,1,0:T(8,128)(2,1)S(1)}, u32[]{:S(2)}, u32[]{:S(2)}) collective-permute-start(bf16[2,256,128]{2,1,0:T(8,128)(2,1)S(1)} %get-tuple-element.41.one), channel_id=1, source_target_pairs={{0,4},{1,5},{2,6},{3,7},{4,0},{5,1},{6,2},{7,3},{8,12},{9,13},{10,... | collective-permute-start | bytes 393224 | tf_op jit(solution)/shard_map/ppermute | solution.py:318
  25.2 5.8 %collective-permute-start.5 = (bf16[2,256,128]{2,1,0:T(8,128)(2,1)S(1)}, bf16[2,256,128]{2,1,0:T(8,128)(2,1)S(1)}, u32[]{:S(2)}, u32[]{:S(2)}) collective-permute-start(bf16[2,256,128]{2,1,0:T(8,128)(2,1)S(1)} %joint.4), channel_id=1, source_target_pairs={{0,16},{1,17},{2,18},{3,19},{4,8},{5,9},{6,10},{7,11},{8,4},{9,5},... | collective-permute-start | bytes 393224 | tf_op jit(solution)/shard_map/ppermute | solution.py:318
  25.4 9.0 %collective-permute-start.8 = (bf16[2,256,128]{2,1,0:T(8,128)(2,1)S(1)}, bf16[2,256,128]{2,1,0:T(8,128)(2,1)S(1)}, u32[]{:S(2)}, u32[]{:S(2)}) collective-permute-start(bf16[2,256,128]{2,1,0:T(8,128)(2,1)S(1)} %joint.5), channel_id=1, source_target_pairs={{0,16},{1,17},{2,18},{3,19},{4,8},{5,9},{6,10},{7,11},{8,4},{9,5},... | collective-permute-start | bytes 393224 | tf_op jit(solution)/shard_map/ppermute | solution.py:318
  29.6 6.7 %collective-permute-start.18 = (bf16[2,256,128]{2,1,0:T(8,128)(2,1)S(1)}, bf16[2,256,128]{2,1,0:T(8,128)(2,1)S(1)}, u32[]{:S(2)}, u32[]{:S(2)}) collective-permute-start(bf16[2,256,128]{2,1,0:T(8,128)(2,1)S(1)} %joint.6), channel_id=1, source_target_pairs={{0,16},{1,17},{2,18},{3,19},{4,8},{5,9},{6,10},{7,11},{8,4},{9,5},... | collective-permute-start | bytes 393224 | tf_op jit(solution)/shard_map/ppermute | solution.py:318
  31.0 7.5 %collective-permute-start.21 = (bf16[2,256,128]{2,1,0:T(8,128)(2,1)S(1)}, bf16[2,256,128]{2,1,0:T(8,128)(2,1)S(1)}, u32[]{:S(2)}, u32[]{:S(2)}) collective-permute-start(bf16[2,256,128]{2,1,0:T(8,128)(2,1)S(1)} %joint.7), channel_id=1, source_target_pairs={{0,16},{1,17},{2,18},{3,19},{4,8},{5,9},{6,10},{7,11},{8,4},{9,5},... | collective-permute-start | bytes 393224 | tf_op jit(solution)/shard_map/ppermute | solution.py:318
  31.1 8.8 %collective-permute-start.6 = (bf16[256,128]{1,0:T(8,128)(2,1)S(1)}, bf16[256,128]{1,0:T(8,128)(2,1)S(1)}, u32[]{:S(2)}, u32[]{:S(2)}) collective-permute-start(bf16[256,128]{1,0:T(8,128)(2,1)S(1)} %near.4), channel_id=1, source_target_pairs={{0,4},{1,5},{2,6},{3,7},{4,0},{5,1},{6,2},{7,3},{8,12},{9,13},{10,... | collective-permute-start | bytes 196616 | tf_op jit(solution)/shard_map/ppermute | solution.py:318
  34.4 5.5 %collective-permute-start.9 = (bf16[256,128]{1,0:T(8,128)(2,1)S(1)}, bf16[256,128]{1,0:T(8,128)(2,1)S(1)}, u32[]{:S(2)}, u32[]{:S(2)}) collective-permute-start(bf16[256,128]{1,0:T(8,128)(2,1)S(1)} %near.5), channel_id=1, source_target_pairs={{0,4},{1,5},{2,6},{3,7},{4,0},{5,1},{6,2},{7,3},{8,12},{9,13},{10,... | collective-permute-start | bytes 196616 | tf_op jit(solution)/shard_map/ppermute | solution.py:318
  36.3 7.3 %collective-permute-start.19 = (bf16[256,128]{1,0:T(8,128)(2,1)S(1)}, bf16[256,128]{1,0:T(8,128)(2,1)S(1)}, u32[]{:S(2)}, u32[]{:S(2)}) collective-permute-start(bf16[256,128]{1,0:T(8,128)(2,1)S(1)} %near.6), channel_id=1, source_target_pairs={{0,4},{1,5},{2,6},{3,7},{4,0},{5,1},{6,2},{7,3},{8,12},{9,13},{10,... | collective-permute-start | bytes 196616 | tf_op jit(solution)/shard_map/ppermute | solution.py:318
  38.5 5.0 %collective-permute-start.22 = (bf16[256,128]{1,0:T(8,128)(2,1)S(1)}, bf16[256,128]{1,0:T(8,128)(2,1)S(1)}, u32[]{:S(2)}, u32[]{:S(2)}) collective-permute-start(bf16[256,128]{1,0:T(8,128)(2,1)S(1)} %near.7), channel_id=1, source_target_pairs={{0,4},{1,5},{2,6},{3,7},{4,0},{5,1},{6,2},{7,3},{8,12},{9,13},{10,... | collective-permute-start | bytes 196616 | tf_op jit(solution)/shard_map/ppermute | solution.py:318
  40.0 6.4 %collective-permute-start.12 = (bf16[128,256]{1,0:T(8,128)(2,1)S(1)}, bf16[128,256]{1,0:T(8,128)(2,1)S(1)}, u32[]{:S(2)}, u32[]{:S(2)}) collective-permute-start(bf16[128,256]{1,0:T(8,128)(2,1)S(1)} %get-tuple-element.33.refs_1_), channel_id=1, source_target_pairs={{0,1},{1,0},{2,3},{3,2},{4,5},{5,4},{6,7},{7,6},{8,9},{9,8},{10,11... | collective-permute-start | bytes 196616 | tf_op jit(solution)/shard_map/ppermute | solution.py:318
  41.3 5.9 %collective-permute-start.11 = (bf16[128,256]{1,0:T(8,128)(2,1)S(1)}, bf16[128,256]{1,0:T(8,128)(2,1)S(1)}, u32[]{:S(2)}, u32[]{:S(2)}) collective-permute-start(bf16[128,256]{1,0:T(8,128)(2,1)S(1)} %get-tuple-element.34), channel_id=1, source_target_pairs={{0,3},{1,2},{2,1},{3,0},{4,7},{5,6},{6,5},{7,4},{8,11},{9,10},{10,... | collective-permute-start | bytes 196616 | tf_op jit(solution)/shard_map/ppermute | solution.py:318
  42.8 5.0 %collective-permute-start.10 = (bf16[128,256]{1,0:T(8,128)(2,1)S(1)}, bf16[128,256]{1,0:T(8,128)(2,1)S(1)}, u32[]{:S(2)}, u32[]{:S(2)}) collective-permute-start(bf16[128,256]{1,0:T(8,128)(2,1)S(1)} %get-tuple-element.34), channel_id=1, source_target_pairs={{0,2},{1,3},{2,0},{3,1},{4,6},{5,7},{6,4},{7,5},{8,10},{9,11},{10,... | collective-permute-start | bytes 196616 | tf_op jit(solution)/shard_map/ppermute | solution.py:318
  43.6 4.6 %collective-permute-start.25 = (bf16[128,256]{1,0:T(8,128)(2,1)S(1)}, bf16[128,256]{1,0:T(8,128)(2,1)S(1)}, u32[]{:S(2)}, u32[]{:S(2)}) collective-permute-start(bf16[128,256]{1,0:T(8,128)(2,1)S(1)} %get-tuple-element.42.refs_1_), channel_id=1, source_target_pairs={{0,1},{1,0},{2,3},{3,2},{4,5},{5,4},{6,7},{7,6},{8,9},{9,8},{10,11... | collective-permute-start | bytes 196616 | tf_op jit(solution)/shard_map/ppermute | solution.py:318
  44.9 6.4 %copy-start.1 = (bf16[4,1024,512]{2,1,0:T(8,128)(2,1)S(1)}, bf16[4,1024,512]{2,1,0:T(8,128)(2,1)}, u32[]{:S(2)}) copy-start(bf16[4,1024,512]{2,1,0:T(8,128)(2,1)} %refs_2_.2) | copy-start | bytes 12582916
  44.9 6.4 %copy-start.2 = (s32[1,4]{1,0:T(1,128)S(1)}, s32[1,4]{1,0:T(1,128)}, u32[]{:S(2)}) copy-start(s32[1,4]{1,0:T(1,128)} %refs_0_.5) | copy-start | bytes 52
  44.9 6.4 %copy-start.3 = (s32[16]{0:T(128)S(1)}, s32[16]{0:T(128)}, u32[]{:S(2)}) copy-start(s32[16]{0:T(128)} %refs_1_.1) | copy-start | bytes 196
  44.9 5.2 %collective-permute-start.24 = (bf16[128,256]{1,0:T(8,128)(2,1)S(1)}, bf16[128,256]{1,0:T(8,128)(2,1)S(1)}, u32[]{:S(2)}, u32[]{:S(2)}) collective-permute-start(bf16[128,256]{1,0:T(8,128)(2,1)S(1)} %get-tuple-element.43), channel_id=1, source_target_pairs={{0,3},{1,2},{2,1},{3,0},{4,7},{5,6},{6,5},{7,4},{8,11},{9,10},{10,... | collective-permute-start | bytes 196616 | tf_op jit(solution)/shard_map/ppermute | solution.py:318
  46.4 4.4 %collective-permute-start.23 = (bf16[128,256]{1,0:T(8,128)(2,1)S(1)}, bf16[128,256]{1,0:T(8,128)(2,1)S(1)}, u32[]{:S(2)}, u32[]{:S(2)}) collective-permute-start(bf16[128,256]{1,0:T(8,128)(2,1)S(1)} %get-tuple-element.43), channel_id=1, source_target_pairs={{0,2},{1,3},{2,0},{3,1},{4,6},{5,7},{6,4},{7,5},{8,10},{9,11},{10,... | collective-permute-start | bytes 196616 | tf_op jit(solution)/shard_map/ppermute | solution.py:318
  48.2 3.1 %collective-permute-start.13 = (bf16[128,1024]{1,0:T(8,128)(2,1)S(1)}, bf16[128,1024]{1,0:T(8,128)(2,1)S(1)}, u32[]{:S(2)}, u32[]{:S(2)}) collective-permute-start(bf16[128,1024]{1,0:T(8,128)(2,1)S(1)} %phase.2.refs_3_), channel_id=1, source_target_pairs={{0,16},{1,17},{2,18},{3,19},{4,20},{5,21},{6,22},{7,23},{8,24},{9,... | collective-permute-start | bytes 786440 | tf_op jit(solution)/shard_map/ppermute | solution.py:318
  51.2 1.6 %collective-permute-start.26 = (bf16[128,1024]{1,0:T(8,128)(2,1)S(1)}, bf16[128,1024]{1,0:T(8,128)(2,1)S(1)}, u32[]{:S(2)}, u32[]{:S(2)}) collective-permute-start(bf16[128,1024]{1,0:T(8,128)(2,1)S(1)} %phase.3.refs_5_), channel_id=1, source_target_pairs={{0,16},{1,17},{2,18},{3,19},{4,20},{5,21},{6,22},{7,23},{8,24},{9,... | collective-permute-start | bytes 786440 | tf_op jit(solution)/shard_map/ppermute | solution.py:318

commit v14 on v13

--- a/solution.py
+++ b/solution.py
@@ -12,8 +12,6 @@
 regularizer = 0.05
 bf16 = jnp.bfloat16
 f32 = jnp.float32
-send_order = (0, 2, 1, 3)
-tail_order = (0, 2, 3, 1)
 
 
 def hartley(length):
@@ -119,7 +117,7 @@
 
 
 def whole_turns(scale, square):
-    turns = scale * square
+    turns = scale * square * (0.5 / math.pi)
     return (turns - jnp.round(turns)) * (2.0 * math.pi)
 
 
@@ -164,7 +162,7 @@
 
 
 def column_kernel(inner, outer, table, gain, *refs):
-    pieces = dict(zip(send_order, refs[:inner]))
+    pieces = refs[:inner]
     keep, *away = refs[inner:-3]
     stack, total, spectrum = refs[-3:]
     _, plane, spot = position(inner)
@@ -231,7 +229,7 @@
 
 
 def phase_kernel(inner, table, *refs):
-    pieces = dict(zip(tail_order, refs[:inner]))
+    pieces = refs[:inner]
     out, joined = refs[-2:]
     _, _, spot = position(inner)
     block = refs[0].shape[1]
@@ -323,8 +321,10 @@
     def to_spot(rel):
         return lambda c, r: (c, r ^ rel)
 
-    def spread(pieces, order):
-        return [sent(pieces[rel], to_spot(rel)) if rel else pieces[rel] for rel in order]
+    def spread(stays, along_x, along_y, diagonal):
+        first = sent(diagonal, to_spot(2))
+        other = first if along_y is diagonal else sent(along_y, to_spot(2))
+        return [stays, sent(along_x, to_spot(1)), other, sent(first, to_spot(1))]
 
     def to_near_plane(c, r):
         return c, (r // inner ^ 1) * inner + r % inner
@@ -342,7 +342,7 @@
         compiler_params=params,
         cost_estimate=cheap,
         name="filters",
-    )(propagation * (0.5 / math.pi))
+    )(from_hbm(propagation))
     pieces = pl.pallas_call(
         lambda *refs: row_kernel(inner, *refs),
         out_shape=[shaped(dists, rows_dev, block)] * (own * inner),
@@ -357,7 +357,7 @@
         name="row_spectra",
     )(from_hbm(holograms[0]), partner, table, gain)
     arrived = [
-        spread(pieces[chunk * inner : (chunk + 1) * inner], send_order) for chunk in range(own)
+        spread(*pieces[chunk * inner : (chunk + 1) * inner]) for chunk in range(own)
     ]
 
     sums = []
@@ -412,7 +412,7 @@
             cost_estimate=cheap,
             name="half",
         )(*sums[chunk])
-        pieces = spread([first, first, second, second], tail_order)
+        pieces = spread(first, first, second, second)
         phase = pl.pallas_call(
             lambda *refs: phase_kernel(inner, *refs),
             out_shape=shaped(capacity, width),

time: 54.1 us -> 55 us (1.017)
  starting transfers between devices: 30.7 us -> 32.1 us
  other arithmetic: 0.83 us -> 0 us
    ppermute x27 -> x29, starting transfers between devices: 30.7 us -> 32.1 us  [sent(): return lax.ppermute(value, ('dist', 'rows'), pairs)]
    mul x1 -> x0, other arithmetic: 0.83 us -> none  [plane_plan(): propagation * (0.5 / math.pi)]
    ppermute x27 -> x29, waiting for transfers between devices: 11.8 us -> 11.8 us  [sent(): return lax.ppermute(value, ('dist', 'rows'), pairs)]
  transfers between devices with their start and end apart: 27 -> 29, of which waited for: 8 -> 13; matrix products, arithmetic and copies ran while one was open for 2% -> 0% of each run, Pallas kernels for 14% -> 14%
where the time goes in v14:
time: 55 us; the launch traced here: 54.9 us
  starting transfers between devices  32.1 us (58%)
  waiting for transfers between devices  11.8 us (21%)
  Pallas kernels  10.7 us (19%)
    ppermute x29, starting transfers between devices, sent(): return lax.ppermute(value, ('dist', 'rows'), pairs)  32.1 us
    ppermute x29, waiting for transfers between devices, sent(): return lax.ppermute(value, ('dist', 'rows'), pairs)  11.8 us
    pallas_call x1, Pallas kernels, plane_plan(): pl.pallas_call(lambda *refs: filter_kernel(inner, dist_dev, *refs), out_s...  2.62 us
    pallas_call x2, Pallas kernels, plane_plan(): pl.pallas_call(lambda *refs: column_kernel(inner, outer, *refs), out_shap...  2.59 us
    pallas_call x1, Pallas kernels, plane_plan(): pl.pallas_call(lambda *refs: row_kernel(inner, *refs), out_shape=[shaped(...  1.83 us
    pallas_call x1, Pallas kernels, plane_plan(): pl.pallas_call(lambda *refs: recon_kernel(own, *refs), out_shape=[jax.Sha...  1.2 us
    pallas_call x1, Pallas kernels, plane_plan(): pl.pallas_call(recon_last_kernel, out_shape=shaped(capacity, pixels), in_...  1.12 us
  transfers between devices with their start and end apart: 29, of which 13 were waited for; matrix products, arithmetic and copies ran while one was open for 0% of the time, Pallas kernels for 14%

profile of v14, /device:TPU:0, one launch (start us, length us, event | category | flops | bytes accessed | tf_op | source)
XLA Modules:
  0.0 54.9 jit_solution(3805068262812286267)
XLA Ops:
  0.0 0.5 collective-permute-start
  0.5 2.6 %filters.1.refs_3_.refs_1_ = bf16[4,1024,256]{2,1,0:T(8,128)(2,1)S(1)} custom-call(f32[4]{0:T(128)} %refs_0_.6), custom_call_target="tpu_custom_call" | custom-call | flops 1 | bytes 1 | tf_op jit(solution)/shard_map/filters/pallas_call | solution.py:337
  3.1 0.0 collective-permute-done.refs_1_
  3.1 1.8 %row_spectra.1 = (bf16[4,64,256]{2,1,0:T(8,128)(2,1)S(1)}, bf16[4,64,256]{2,1,0:T(8,128)(2,1)S(1)}, bf16[4,64,256]{2,1,0:T(8,128)(2,1)S(1)}, bf16[4,64,256]{2,1,...) custom-call(bf16[4,2,64,1024]{3,2,1,0:T(8,128)(2,1)} %bitcast.2, ...), custom_call_target="tpu_custom_call" | custom-call | flops 1 | bytes 1 | tf_op jit(solution)/shard_map/row_spectra/pallas_call | solution.py:346
  4.9 2.8 %collective-permute-start.3 = (bf16[4,64,256]{2,1,0:T(8,128)(2,1)S(1)}, bf16[4,64,256]{2,1,0:T(8,128)(2,1)S(1)}, u32[]{:S(2)}, u32[]{:S(2)}) collective-permute-start(bf16[4,64,256]{2,1,0:T(8,128)(2,1)S(1)} %get-tuple-element.29), channel_id=1, source_target_pairs={{0,2},{1,3},{2,0},{3,1},{4,6},{5,7},{6,4},{7,5},{8,10},{9,11},{10,... | collective-permute-start | bytes 393224 | tf_op jit(solution)/shard_map/ppermute | solution.py:316
  7.7 1.5 %collective-permute-start.1 = (bf16[4,64,256]{2,1,0:T(8,128)(2,1)S(1)}, bf16[4,64,256]{2,1,0:T(8,128)(2,1)S(1)}, u32[]{:S(2)}, u32[]{:S(2)}) collective-permute-start(bf16[4,64,256]{2,1,0:T(8,128)(2,1)S(1)} %get-tuple-element.27), channel_id=1, source_target_pairs={{0,1},{1,0},{2,3},{3,2},{4,5},{5,4},{6,7},{7,6},{8,9},{9,8},{10,11... | collective-permute-start | bytes 393224 | tf_op jit(solution)/shard_map/ppermute | solution.py:316
  9.2 0.5 collective-permute-start.17
  9.7 1.5 %collective-permute-start.2 = (bf16[4,64,256]{2,1,0:T(8,128)(2,1)S(1)}, bf16[4,64,256]{2,1,0:T(8,128)(2,1)S(1)}, u32[]{:S(2)}, u32[]{:S(2)}) collective-permute-start(bf16[4,64,256]{2,1,0:T(8,128)(2,1)S(1)} %get-tuple-element.28), channel_id=1, source_target_pairs={{0,2},{1,3},{2,0},{3,1},{4,6},{5,7},{6,4},{7,5},{8,10},{9,11},{10,... | collective-permute-start | bytes 393224 | tf_op jit(solution)/shard_map/ppermute | solution.py:316
  11.2 0.4 collective-permute-done.3
  11.6 2.4 %collective-permute-start.4 = (bf16[4,64,256]{2,1,0:T(8,128)(2,1)S(1)}, bf16[4,64,256]{2,1,0:T(8,128)(2,1)S(1)}, u32[]{:S(2)}, u32[]{:S(2)}) collective-permute-start(bf16[4,64,256]{2,1,0:T(8,128)(2,1)S(1)} %collective-permute-done.3), channel_id=1, source_target_pairs={{0,1},{1,0},{2,3},{3,2},{4,5},{5,4},{6,7},{7,6},{8,9},{9,8},{10,11... | collective-permute-start | bytes 393224 | tf_op jit(solution)/shard_map/ppermute | solution.py:316
  14.0 0.0 collective-permute-start.15
  14.1 0.0 collective-permute-done.1.refs_3_
  14.1 2.0 %collective-permute-start.16 = (bf16[4,64,256]{2,1,0:T(8,128)(2,1)S(1)}, bf16[4,64,256]{2,1,0:T(8,128)(2,1)S(1)}, u32[]{:S(2)}, u32[]{:S(2)}) collective-permute-start(bf16[4,64,256]{2,1,0:T(8,128)(2,1)S(1)} %get-tuple-element.37), channel_id=1, source_target_pairs={{0,2},{1,3},{2,0},{3,1},{4,6},{5,7},{6,4},{7,5},{8,10},{9,11},{10,... | collective-permute-start | bytes 393224 | tf_op jit(solution)/shard_map/ppermute | solution.py:316
  16.1 0.0 collective-permute-done.17
  16.1 1.5 %collective-permute-start.18 = (bf16[4,64,256]{2,1,0:T(8,128)(2,1)S(1)}, bf16[4,64,256]{2,1,0:T(8,128)(2,1)S(1)}, u32[]{:S(2)}, u32[]{:S(2)}) collective-permute-start(bf16[4,64,256]{2,1,0:T(8,128)(2,1)S(1)} %collective-permute-done.17), channel_id=1, source_target_pairs={{0,1},{1,0},{2,3},{3,2},{4,5},{5,4},{6,7},{7,6},{8,9},{9,8},{10,11... | collective-permute-start | bytes 393224 | tf_op jit(solution)/shard_map/ppermute | solution.py:316
  17.6 0.8 %collective-permute-done.2.refs_4_ = bf16[4,64,256]{2,1,0:T(8,128)(2,1)S(1)} collective-permute-done((bf16[4,64,256]{2,1,0:T(8,128)(2,1)S(1)}, bf16[4,64,256]{2,1,0:T(8,128)(2,1)S(1)}, u32[]{:S(2)}, u32[]{:S(2)}) %collective-permute-start.2) | collective-permute-done | bytes 131104 | tf_op jit(solution)/shard_map/ppermute | solution.py:316
  18.4 0.0 collective-permute-done.4.refs_5_
  18.5 1.3 %columns.2 = (bf16[2,256,256]{2,1,0:T(8,128)(2,1)S(1)}, bf16[2,256,128]{2,1,0:T(8,128)(2,1)S(1)}, bf16[2,256,128]{2,1,0:T(8,128)(2,1)S(1)}) custom-call(bf16[1024,1024]{1,0:T(8,128)(2,1)S(1)} %copy-done, bf16[4,1024,256]{2,1,0:T(8,128)(2,1)S(1)} %filters.1.refs_3_.refs_1_, bf16[4,64,256]{2,1,0:T(8,128)(2,1)S(1)} %get-tuple-element.26.refs_2_, ...), custom_call_target="tpu_custom_call" | custom-call | flops 1 | bytes 1 | tf_op jit(solution)/shard_map/columns/pallas_call | solution.py:365
  19.8 1.7 %collective-permute-start.5 = (bf16[2,256,128]{2,1,0:T(8,128)(2,1)S(1)}, bf16[2,256,128]{2,1,0:T(8,128)(2,1)S(1)}, u32[]{:S(2)}, u32[]{:S(2)}) collective-permute-start(bf16[2,256,128]{2,1,0:T(8,128)(2,1)S(1)} %get-tuple-element.31.one), channel_id=1, source_target_pairs={{0,4},{1,5},{2,6},{3,7},{4,0},{5,1},{6,2},{7,3},{8,12},{9,13},{10,... | collective-permute-start | bytes 393224 | tf_op jit(solution)/shard_map/ppermute | solution.py:316
  21.4 0.4 collective-permute-start.8
  21.8 0.0 collective-permute-done.15.refs_3_
  21.9 0.0 collective-permute-done.16.refs_4_
  21.9 0.4 collective-permute-done.18.refs_5_
  22.2 1.3 %columns.3 = (bf16[2,256,256]{2,1,0:T(8,128)(2,1)S(1)}, bf16[2,256,128]{2,1,0:T(8,128)(2,1)S(1)}, bf16[2,256,128]{2,1,0:T(8,128)(2,1)S(1)}) custom-call(bf16[1024,1024]{1,0:T(8,128)(2,1)S(1)} %copy-done, bf16[4,1024,256]{2,1,0:T(8,128)(2,1)S(1)} %filters.1.refs_3_.refs_1_, bf16[4,64,256]{2,1,0:T(8,128)(2,1)S(1)} %get-tuple-element.35.refs_2_, ...), custom_call_target="tpu_custom_call" | custom-call | flops 1 | bytes 1 | tf_op jit(solution)/shard_map/columns/pallas_call | solution.py:365
  23.5 1.5 %collective-permute-start.19 = (bf16[2,256,128]{2,1,0:T(8,128)(2,1)S(1)}, bf16[2,256,128]{2,1,0:T(8,128)(2,1)S(1)}, u32[]{:S(2)}, u32[]{:S(2)}) collective-permute-start(bf16[2,256,128]{2,1,0:T(8,128)(2,1)S(1)} %get-tuple-element.40.one), channel_id=1, source_target_pairs={{0,4},{1,5},{2,6},{3,7},{4,0},{5,1},{6,2},{7,3},{8,12},{9,13},{10,... | collective-permute-start | bytes 393224 | tf_op jit(solution)/shard_map/ppermute | solution.py:316
  25.1 0.5 collective-permute-start.22
  25.6 0.0 collective-permute-done.5.two
  25.7 0.1 collective-permute-start.6
  25.7 2.2 %collective-permute-done.8.two = bf16[2,256,128]{2,1,0:T(8,128)(2,1)S(1)} collective-permute-done((bf16[2,256,128]{2,1,0:T(8,128)(2,1)S(1)}, bf16[2,256,128]{2,1,0:T(8,128)(2,1)S(1)}, u32[]{:S(2)}, u32[]{:S(2)}) %collective-permute-start.8) | collective-permute-done | bytes 131104 | tf_op jit(solution)/shard_map/ppermute | solution.py:316
  27.9 0.1 collective-permute-start.9
  28.0 2.4 %collective-permute-done.19.two = bf16[2,256,128]{2,1,0:T(8,128)(2,1)S(1)} collective-permute-done((bf16[2,256,128]{2,1,0:T(8,128)(2,1)S(1)}, bf16[2,256,128]{2,1,0:T(8,128)(2,1)S(1)}, u32[]{:S(2)}, u32[]{:S(2)}) %collective-permute-start.19) | collective-permute-done | bytes 131104 | tf_op jit(solution)/shard_map/ppermute | solution.py:316
  30.4 0.1 collective-permute-start.20
  30.5 1.3 %collective-permute-done.22.two = bf16[2,256,128]{2,1,0:T(8,128)(2,1)S(1)} collective-permute-done((bf16[2,256,128]{2,1,0:T(8,128)(2,1)S(1)}, bf16[2,256,128]{2,1,0:T(8,128)(2,1)S(1)}, u32[]{:S(2)}, u32[]{:S(2)}) %collective-permute-start.22) | collective-permute-done | bytes 131104 | tf_op jit(solution)/shard_map/ppermute | solution.py:316
  31.8 0.1 collective-permute-start.23
  31.9 0.0 collective-permute-done.6.refs_1_
  32.0 3.2 %collective-permute-start.7 = (bf16[256,128]{1,0:T(8,128)(2,1)S(1)}, bf16[256,128]{1,0:T(8,128)(2,1)S(1)}, u32[]{:S(2)}, u32[]{:S(2)}) collective-permute-start(bf16[256,128]{1,0:T(8,128)(2,1)S(1)} %near.4), channel_id=1, source_target_pairs={{0,4},{1,5},{2,6},{3,7},{4,0},{5,1},{6,2},{7,3},{8,12},{9,13},{10,... | collective-permute-start | bytes 196616 | tf_op jit(solution)/shard_map/ppermute | solution.py:316
  35.2 0.0 collective-permute-done.9.refs_1_.refs_3_
  35.3 0.7 %collective-permute-start.10 = (bf16[256,128]{1,0:T(8,128)(2,1)S(1)}, bf16[256,128]{1,0:T(8,128)(2,1)S(1)}, u32[]{:S(2)}, u32[]{:S(2)}) collective-permute-start(bf16[256,128]{1,0:T(8,128)(2,1)S(1)} %near.5), channel_id=1, source_target_pairs={{0,4},{1,5},{2,6},{3,7},{4,0},{5,1},{6,2},{7,3},{8,12},{9,13},{10,... | collective-permute-start | bytes 196616 | tf_op jit(solution)/shard_map/ppermute | solution.py:316
  35.9 0.0 collective-permute-done.20.refs_1_
  36.0 1.9 %collective-permute-start.21 = (bf16[256,128]{1,0:T(8,128)(2,1)S(1)}, bf16[256,128]{1,0:T(8,128)(2,1)S(1)}, u32[]{:S(2)}, u32[]{:S(2)}) collective-permute-start(bf16[256,128]{1,0:T(8,128)(2,1)S(1)} %near.6), channel_id=1, source_target_pairs={{0,4},{1,5},{2,6},{3,7},{4,0},{5,1},{6,2},{7,3},{8,12},{9,13},{10,... | collective-permute-start | bytes 196616 | tf_op jit(solution)/shard_map/ppermute | solution.py:316
  37.9 0.0 collective-permute-done.23.refs_1_.refs_3_
  37.9 1.4 %collective-permute-start.24 = (bf16[256,128]{1,0:T(8,128)(2,1)S(1)}, bf16[256,128]{1,0:T(8,128)(2,1)S(1)}, u32[]{:S(2)}, u32[]{:S(2)}) collective-permute-start(bf16[256,128]{1,0:T(8,128)(2,1)S(1)} %near.7), channel_id=1, source_target_pairs={{0,4},{1,5},{2,6},{3,7},{4,0},{5,1},{6,2},{7,3},{8,12},{9,13},{10,... | collective-permute-start | bytes 196616 | tf_op jit(solution)/shard_map/ppermute | solution.py:316
  39.3 0.0 collective-permute-done.7.refs_2_
  39.3 0.3 collective-permute-done.10.refs_4_
  39.6 0.1 half.2
  39.7 1.9 %collective-permute-start.12 = (bf16[128,256]{1,0:T(8,128)(2,1)S(1)}, bf16[128,256]{1,0:T(8,128)(2,1)S(1)}, u32[]{:S(2)}, u32[]{:S(2)}) collective-permute-start(bf16[128,256]{1,0:T(8,128)(2,1)S(1)} %get-tuple-element.34), channel_id=1, source_target_pairs={{0,2},{1,3},{2,0},{3,1},{4,6},{5,7},{6,4},{7,5},{8,10},{9,11},{10,... | collective-permute-start | bytes 196616 | tf_op jit(solution)/shard_map/ppermute | solution.py:316
  41.6 0.7 %collective-permute-done.24.refs_4_ = bf16[256,128]{1,0:T(8,128)(2,1)S(1)} collective-permute-done((bf16[256,128]{1,0:T(8,128)(2,1)S(1)}, bf16[256,128]{1,0:T(8,128)(2,1)S(1)}, u32[]{:S(2)}, u32[]{:S(2)}) %collective-permute-start.24) | collective-permute-done | bytes 65568 | tf_op jit(solution)/shard_map/ppermute | solution.py:316
  42.2 0.1 half.3
  42.3 1.6 %collective-permute-start.26 = (bf16[128,256]{1,0:T(8,128)(2,1)S(1)}, bf16[128,256]{1,0:T(8,128)(2,1)S(1)}, u32[]{:S(2)}, u32[]{:S(2)}) collective-permute-start(bf16[128,256]{1,0:T(8,128)(2,1)S(1)} %get-tuple-element.43), channel_id=1, source_target_pairs={{0,2},{1,3},{2,0},{3,1},{4,6},{5,7},{6,4},{7,5},{8,10},{9,11},{10,... | collective-permute-start | bytes 196616 | tf_op jit(solution)/shard_map/ppermute | solution.py:316
  43.9 1.5 %collective-permute-start.11 = (bf16[128,256]{1,0:T(8,128)(2,1)S(1)}, bf16[128,256]{1,0:T(8,128)(2,1)S(1)}, u32[]{:S(2)}, u32[]{:S(2)}) collective-permute-start(bf16[128,256]{1,0:T(8,128)(2,1)S(1)} %get-tuple-element.33.refs_1_), channel_id=1, source_target_pairs={{0,1},{1,0},{2,3},{3,2},{4,5},{5,4},{6,7},{7,6},{8,9},{9,8},{10,11... | collective-permute-start | bytes 196616 | tf_op jit(solution)/shard_map/ppermute | solution.py:316
  45.4 0.5 collective-permute-start.13
  45.9 1.5 %collective-permute-start.25 = (bf16[128,256]{1,0:T(8,128)(2,1)S(1)}, bf16[128,256]{1,0:T(8,128)(2,1)S(1)}, u32[]{:S(2)}, u32[]{:S(2)}) collective-permute-start(bf16[128,256]{1,0:T(8,128)(2,1)S(1)} %get-tuple-element.42.refs_1_), channel_id=1, source_target_pairs={{0,1},{1,0},{2,3},{3,2},{4,5},{5,4},{6,7},{7,6},{8,9},{9,8},{10,11... | collective-permute-start | bytes 196616 | tf_op jit(solution)/shard_map/ppermute | solution.py:316
  47.4 0.6 %collective-permute-start.27 = (bf16[128,256]{1,0:T(8,128)(2,1)S(1)}, bf16[128,256]{1,0:T(8,128)(2,1)S(1)}, u32[]{:S(2)}, u32[]{:S(2)}) collective-permute-start(bf16[128,256]{1,0:T(8,128)(2,1)S(1)} %collective-permute-done.26.refs_3_), channel_id=1, source_target_pairs={{0,1},{1,0},{2,3},{3,2},{4,5},{5,4},{6,7},{7,6},{8,9},{9,8},{10,11... | collective-permute-start | bytes 196616 | tf_op jit(solution)/shard_map/ppermute | solution.py:316
  48.0 0.1 collective-permute-done.11.refs_2_
  48.1 1.5 %collective-permute-done.13.refs_4_ = bf16[128,256]{1,0:T(8,128)(2,1)S(1)} collective-permute-done((bf16[128,256]{1,0:T(8,128)(2,1)S(1)}, bf16[128,256]{1,0:T(8,128)(2,1)S(1)}, u32[]{:S(2)}, u32[]{:S(2)}) %collective-permute-start.13) | collective-permute-done | bytes 65568 | tf_op jit(solution)/shard_map/ppermute | solution.py:316
  49.6 0.5 phase.2.refs_3_
  50.1 0.1 collective-permute-start.14
  50.2 0.2 collective-permute-done.25.refs_2_
  50.3 1.3 %collective-permute-done.27.refs_4_ = bf16[128,256]{1,0:T(8,128)(2,1)S(1)} collective-permute-done((bf16[128,256]{1,0:T(8,128)(2,1)S(1)}, bf16[128,256]{1,0:T(8,128)(2,1)S(1)}, u32[]{:S(2)}, u32[]{:S(2)}) %collective-permute-start.27) | collective-permute-done | bytes 65568 | tf_op jit(solution)/shard_map/ppermute | solution.py:316
  51.7 0.5 phase.3.refs_5_
  52.1 0.1 collective-permute-start.28
  52.3 1.2 %recon.2 = (f32[128,512]{1,0:T(8,128)S(1)}, bf16[1024,512]{1,0:T(8,128)(2,1)S(1)}, bf16[128,128]{1,0:T(8,128)(2,1)S(1)}) custom-call(s32[1,4]{1,0:T(1,128)S(1)} %copy-done.2, s32[16]{0:T(128)S(1)} %copy-done.3, bf16[4,1024,512]{2,1,0:T(8,128)(2,1)S(1)} %copy-done.1, bf16[128,1024]{1,0:T(8,128)(2,1)S(1)} %phase.2.refs_3_, ...), custom_call_target="tpu_custom_call" | custom-call | flops 1 | bytes 1 | tf_op jit(solution)/shard_map/recon/pallas_call | solution.py:428
  53.5 0.3 collective-permute-done.28.phase
  53.7 1.1 %recon.3 = bf16[128,512]{1,0:T(8,128)(2,1)} custom-call(bf16[1024,512]{1,0:T(8,128)(2,1)S(1)} %get-tuple-element.44.weights, bf16[128,1024]{1,0:T(8,128)(2,1)S(1)} %collective-permute-done.28.phase, f32[128,512]{1,0:T(8,128)S(1)} %get-tuple-element.45.before, bf16[128,128]{1,0:T(8,128)(2,1)S(1)} %get-tuple-element.46.select), custom_call_target="tpu_custom_call" | custom-call | flops 1 | bytes 1 | tf_op jit(solution)/shard_map/recon/pallas_call | solution.py:441
  (20 shorter events, 0.3 us)
Async XLA Ops:
  0.0 3.1 %copy-start = (bf16[1024,1024]{1,0:T(8,128)(2,1)S(1)}, bf16[1024,1024]{1,0:T(8,128)(2,1)}, u32[]{:S(2)}) copy-start(bf16[1024,1024]{1,0:T(8,128)(2,1)} %constant.2.clone.refs_2_.refs_0_) | copy-start | bytes 6291460
  0.0 3.1 %collective-permute-start = (bf16[4,2,64,1024]{3,2,1,0:T(8,128)(2,1)}, bf16[4,2,64,1024]{3,2,1,0:T(8,128)(2,1)S(1)}, u32[]{:S(2)}, u32[]{:S(2)}) collective-permute-start(bf16[4,2,64,1024]{3,2,1,0:T(8,128)(2,1)} %bitcast.1), channel_id=1, source_target_pairs={{0,16},{1,17},{2,18},{3,19},{4,20},{5,21},{6,22},{7,23},{8,24},{9,... | collective-permute-start | bytes 3145736 | tf_op jit(solution)/shard_map/ppermute | solution.py:316
  4.9 6.7 %collective-permute-start.3 = (bf16[4,64,256]{2,1,0:T(8,128)(2,1)S(1)}, bf16[4,64,256]{2,1,0:T(8,128)(2,1)S(1)}, u32[]{:S(2)}, u32[]{:S(2)}) collective-permute-start(bf16[4,64,256]{2,1,0:T(8,128)(2,1)S(1)} %get-tuple-element.29), channel_id=1, source_target_pairs={{0,2},{1,3},{2,0},{3,1},{4,6},{5,7},{6,4},{7,5},{8,10},{9,11},{10,... | collective-permute-start | bytes 393224 | tf_op jit(solution)/shard_map/ppermute | solution.py:316
  7.7 6.4 %collective-permute-start.1 = (bf16[4,64,256]{2,1,0:T(8,128)(2,1)S(1)}, bf16[4,64,256]{2,1,0:T(8,128)(2,1)S(1)}, u32[]{:S(2)}, u32[]{:S(2)}) collective-permute-start(bf16[4,64,256]{2,1,0:T(8,128)(2,1)S(1)} %get-tuple-element.27), channel_id=1, source_target_pairs={{0,1},{1,0},{2,3},{3,2},{4,5},{5,4},{6,7},{7,6},{8,9},{9,8},{10,11... | collective-permute-start | bytes 393224 | tf_op jit(solution)/shard_map/ppermute | solution.py:316
  9.2 6.9 %collective-permute-start.17 = (bf16[4,64,256]{2,1,0:T(8,128)(2,1)S(1)}, bf16[4,64,256]{2,1,0:T(8,128)(2,1)S(1)}, u32[]{:S(2)}, u32[]{:S(2)}) collective-permute-start(bf16[4,64,256]{2,1,0:T(8,128)(2,1)S(1)} %get-tuple-element.38), channel_id=1, source_target_pairs={{0,2},{1,3},{2,0},{3,1},{4,6},{5,7},{6,4},{7,5},{8,10},{9,11},{10,... | collective-permute-start | bytes 393224 | tf_op jit(solution)/shard_map/ppermute | solution.py:316
  9.7 8.7 %collective-permute-start.2 = (bf16[4,64,256]{2,1,0:T(8,128)(2,1)S(1)}, bf16[4,64,256]{2,1,0:T(8,128)(2,1)S(1)}, u32[]{:S(2)}, u32[]{:S(2)}) collective-permute-start(bf16[4,64,256]{2,1,0:T(8,128)(2,1)S(1)} %get-tuple-element.28), channel_id=1, source_target_pairs={{0,2},{1,3},{2,0},{3,1},{4,6},{5,7},{6,4},{7,5},{8,10},{9,11},{10,... | collective-permute-start | bytes 393224 | tf_op jit(solution)/shard_map/ppermute | solution.py:316
  11.6 6.8 %collective-permute-start.4 = (bf16[4,64,256]{2,1,0:T(8,128)(2,1)S(1)}, bf16[4,64,256]{2,1,0:T(8,128)(2,1)S(1)}, u32[]{:S(2)}, u32[]{:S(2)}) collective-permute-start(bf16[4,64,256]{2,1,0:T(8,128)(2,1)S(1)} %collective-permute-done.3), channel_id=1, source_target_pairs={{0,1},{1,0},{2,3},{3,2},{4,5},{5,4},{6,7},{7,6},{8,9},{9,8},{10,11... | collective-permute-start | bytes 393224 | tf_op jit(solution)/shard_map/ppermute | solution.py:316
  14.0 7.8 %collective-permute-start.15 = (bf16[4,64,256]{2,1,0:T(8,128)(2,1)S(1)}, bf16[4,64,256]{2,1,0:T(8,128)(2,1)S(1)}, u32[]{:S(2)}, u32[]{:S(2)}) collective-permute-start(bf16[4,64,256]{2,1,0:T(8,128)(2,1)S(1)} %get-tuple-element.36), channel_id=1, source_target_pairs={{0,1},{1,0},{2,3},{3,2},{4,5},{5,4},{6,7},{7,6},{8,9},{9,8},{10,11... | collective-permute-start | bytes 393224 | tf_op jit(solution)/shard_map/ppermute | solution.py:316
  14.1 7.8 %collective-permute-start.16 = (bf16[4,64,256]{2,1,0:T(8,128)(2,1)S(1)}, bf16[4,64,256]{2,1,0:T(8,128)(2,1)S(1)}, u32[]{:S(2)}, u32[]{:S(2)}) collective-permute-start(bf16[4,64,256]{2,1,0:T(8,128)(2,1)S(1)} %get-tuple-element.37), channel_id=1, source_target_pairs={{0,2},{1,3},{2,0},{3,1},{4,6},{5,7},{6,4},{7,5},{8,10},{9,11},{10,... | collective-permute-start | bytes 393224 | tf_op jit(solution)/shard_map/ppermute | solution.py:316
  16.1 6.1 %collective-permute-start.18 = (bf16[4,64,256]{2,1,0:T(8,128)(2,1)S(1)}, bf16[4,64,256]{2,1,0:T(8,128)(2,1)S(1)}, u32[]{:S(2)}, u32[]{:S(2)}) collective-permute-start(bf16[4,64,256]{2,1,0:T(8,128)(2,1)S(1)} %collective-permute-done.17), channel_id=1, source_target_pairs={{0,1},{1,0},{2,3},{3,2},{4,5},{5,4},{6,7},{7,6},{8,9},{9,8},{10,11... | collective-permute-start | bytes 393224 | tf_op jit(solution)/shard_map/ppermute | solution.py:316
  19.8 5.9 %collective-permute-start.5 = (bf16[2,256,128]{2,1,0:T(8,128)(2,1)S(1)}, bf16[2,256,128]{2,1,0:T(8,128)(2,1)S(1)}, u32[]{:S(2)}, u32[]{:S(2)}) collective-permute-start(bf16[2,256,128]{2,1,0:T(8,128)(2,1)S(1)} %get-tuple-element.31.one), channel_id=1, source_target_pairs={{0,4},{1,5},{2,6},{3,7},{4,0},{5,1},{6,2},{7,3},{8,12},{9,13},{10,... | collective-permute-start | bytes 393224 | tf_op jit(solution)/shard_map/ppermute | solution.py:316
  21.4 6.5 %collective-permute-start.8 = (bf16[2,256,128]{2,1,0:T(8,128)(2,1)S(1)}, bf16[2,256,128]{2,1,0:T(8,128)(2,1)S(1)}, u32[]{:S(2)}, u32[]{:S(2)}) collective-permute-start(bf16[2,256,128]{2,1,0:T(8,128)(2,1)S(1)} %get-tuple-element.32.one), channel_id=1, source_target_pairs={{0,4},{1,5},{2,6},{3,7},{4,0},{5,1},{6,2},{7,3},{8,12},{9,13},{10,... | collective-permute-start | bytes 393224 | tf_op jit(solution)/shard_map/ppermute | solution.py:316
  23.5 6.9 %collective-permute-start.19 = (bf16[2,256,128]{2,1,0:T(8,128)(2,1)S(1)}, bf16[2,256,128]{2,1,0:T(8,128)(2,1)S(1)}, u32[]{:S(2)}, u32[]{:S(2)}) collective-permute-start(bf16[2,256,128]{2,1,0:T(8,128)(2,1)S(1)} %get-tuple-element.40.one), channel_id=1, source_target_pairs={{0,4},{1,5},{2,6},{3,7},{4,0},{5,1},{6,2},{7,3},{8,12},{9,13},{10,... | collective-permute-start | bytes 393224 | tf_op jit(solution)/shard_map/ppermute | solution.py:316
  25.1 6.7 %collective-permute-start.22 = (bf16[2,256,128]{2,1,0:T(8,128)(2,1)S(1)}, bf16[2,256,128]{2,1,0:T(8,128)(2,1)S(1)}, u32[]{:S(2)}, u32[]{:S(2)}) collective-permute-start(bf16[2,256,128]{2,1,0:T(8,128)(2,1)S(1)} %get-tuple-element.41.one), channel_id=1, source_target_pairs={{0,4},{1,5},{2,6},{3,7},{4,0},{5,1},{6,2},{7,3},{8,12},{9,13},{10,... | collective-permute-start | bytes 393224 | tf_op jit(solution)/shard_map/ppermute | solution.py:316
  25.7 6.3 %collective-permute-start.6 = (bf16[2,256,128]{2,1,0:T(8,128)(2,1)S(1)}, bf16[2,256,128]{2,1,0:T(8,128)(2,1)S(1)}, u32[]{:S(2)}, u32[]{:S(2)}) collective-permute-start(bf16[2,256,128]{2,1,0:T(8,128)(2,1)S(1)} %joint.4), channel_id=1, source_target_pairs={{0,16},{1,17},{2,18},{3,19},{4,8},{5,9},{6,10},{7,11},{8,4},{9,5},... | collective-permute-start | bytes 393224 | tf_op jit(solution)/shard_map/ppermute | solution.py:316
  27.9 7.3 %collective-permute-start.9 = (bf16[2,256,128]{2,1,0:T(8,128)(2,1)S(1)}, bf16[2,256,128]{2,1,0:T(8,128)(2,1)S(1)}, u32[]{:S(2)}, u32[]{:S(2)}) collective-permute-start(bf16[2,256,128]{2,1,0:T(8,128)(2,1)S(1)} %joint.5), channel_id=1, source_target_pairs={{0,16},{1,17},{2,18},{3,19},{4,8},{5,9},{6,10},{7,11},{8,4},{9,5},... | collective-permute-start | bytes 393224 | tf_op jit(solution)/shard_map/ppermute | solution.py:316
  30.4 5.5 %collective-permute-start.20 = (bf16[2,256,128]{2,1,0:T(8,128)(2,1)S(1)}, bf16[2,256,128]{2,1,0:T(8,128)(2,1)S(1)}, u32[]{:S(2)}, u32[]{:S(2)}) collective-permute-start(bf16[2,256,128]{2,1,0:T(8,128)(2,1)S(1)} %joint.6), channel_id=1, source_target_pairs={{0,16},{1,17},{2,18},{3,19},{4,8},{5,9},{6,10},{7,11},{8,4},{9,5},... | collective-permute-start | bytes 393224 | tf_op jit(solution)/shard_map/ppermute | solution.py:316
  31.8 6.0 %collective-permute-start.23 = (bf16[2,256,128]{2,1,0:T(8,128)(2,1)S(1)}, bf16[2,256,128]{2,1,0:T(8,128)(2,1)S(1)}, u32[]{:S(2)}, u32[]{:S(2)}) collective-permute-start(bf16[2,256,128]{2,1,0:T(8,128)(2,1)S(1)} %joint.7), channel_id=1, source_target_pairs={{0,16},{1,17},{2,18},{3,19},{4,8},{5,9},{6,10},{7,11},{8,4},{9,5},... | collective-permute-start | bytes 393224 | tf_op jit(solution)/shard_map/ppermute | solution.py:316
  32.0 7.3 %collective-permute-start.7 = (bf16[256,128]{1,0:T(8,128)(2,1)S(1)}, bf16[256,128]{1,0:T(8,128)(2,1)S(1)}, u32[]{:S(2)}, u32[]{:S(2)}) collective-permute-start(bf16[256,128]{1,0:T(8,128)(2,1)S(1)} %near.4), channel_id=1, source_target_pairs={{0,4},{1,5},{2,6},{3,7},{4,0},{5,1},{6,2},{7,3},{8,12},{9,13},{10,... | collective-permute-start | bytes 196616 | tf_op jit(solution)/shard_map/ppermute | solution.py:316
  35.3 4.3 %collective-permute-start.10 = (bf16[256,128]{1,0:T(8,128)(2,1)S(1)}, bf16[256,128]{1,0:T(8,128)(2,1)S(1)}, u32[]{:S(2)}, u32[]{:S(2)}) collective-permute-start(bf16[256,128]{1,0:T(8,128)(2,1)S(1)} %near.5), channel_id=1, source_target_pairs={{0,4},{1,5},{2,6},{3,7},{4,0},{5,1},{6,2},{7,3},{8,12},{9,13},{10,... | collective-permute-start | bytes 196616 | tf_op jit(solution)/shard_map/ppermute | solution.py:316
  36.0 5.6 %collective-permute-start.21 = (bf16[256,128]{1,0:T(8,128)(2,1)S(1)}, bf16[256,128]{1,0:T(8,128)(2,1)S(1)}, u32[]{:S(2)}, u32[]{:S(2)}) collective-permute-start(bf16[256,128]{1,0:T(8,128)(2,1)S(1)} %near.6), channel_id=1, source_target_pairs={{0,4},{1,5},{2,6},{3,7},{4,0},{5,1},{6,2},{7,3},{8,12},{9,13},{10,... | collective-permute-start | bytes 196616 | tf_op jit(solution)/shard_map/ppermute | solution.py:316
  37.9 4.3 %collective-permute-start.24 = (bf16[256,128]{1,0:T(8,128)(2,1)S(1)}, bf16[256,128]{1,0:T(8,128)(2,1)S(1)}, u32[]{:S(2)}, u32[]{:S(2)}) collective-permute-start(bf16[256,128]{1,0:T(8,128)(2,1)S(1)} %near.7), channel_id=1, source_target_pairs={{0,4},{1,5},{2,6},{3,7},{4,0},{5,1},{6,2},{7,3},{8,12},{9,13},{10,... | collective-permute-start | bytes 196616 | tf_op jit(solution)/shard_map/ppermute | solution.py:316
  39.7 5.7 %collective-permute-start.12 = (bf16[128,256]{1,0:T(8,128)(2,1)S(1)}, bf16[128,256]{1,0:T(8,128)(2,1)S(1)}, u32[]{:S(2)}, u32[]{:S(2)}) collective-permute-start(bf16[128,256]{1,0:T(8,128)(2,1)S(1)} %get-tuple-element.34), channel_id=1, source_target_pairs={{0,2},{1,3},{2,0},{3,1},{4,6},{5,7},{6,4},{7,5},{8,10},{9,11},{10,... | collective-permute-start | bytes 196616 | tf_op jit(solution)/shard_map/ppermute | solution.py:316
  42.3 5.1 %collective-permute-start.26 = (bf16[128,256]{1,0:T(8,128)(2,1)S(1)}, bf16[128,256]{1,0:T(8,128)(2,1)S(1)}, u32[]{:S(2)}, u32[]{:S(2)}) collective-permute-start(bf16[128,256]{1,0:T(8,128)(2,1)S(1)} %get-tuple-element.43), channel_id=1, source_target_pairs={{0,2},{1,3},{2,0},{3,1},{4,6},{5,7},{6,4},{7,5},{8,10},{9,11},{10,... | collective-permute-start | bytes 196616 | tf_op jit(solution)/shard_map/ppermute | solution.py:316
  43.9 4.3 %collective-permute-start.11 = (bf16[128,256]{1,0:T(8,128)(2,1)S(1)}, bf16[128,256]{1,0:T(8,128)(2,1)S(1)}, u32[]{:S(2)}, u32[]{:S(2)}) collective-permute-start(bf16[128,256]{1,0:T(8,128)(2,1)S(1)} %get-tuple-element.33.refs_1_), channel_id=1, source_target_pairs={{0,1},{1,0},{2,3},{3,2},{4,5},{5,4},{6,7},{7,6},{8,9},{9,8},{10,11... | collective-permute-start | bytes 196616 | tf_op jit(solution)/shard_map/ppermute | solution.py:316
  45.4 4.3 %collective-permute-start.13 = (bf16[128,256]{1,0:T(8,128)(2,1)S(1)}, bf16[128,256]{1,0:T(8,128)(2,1)S(1)}, u32[]{:S(2)}, u32[]{:S(2)}) collective-permute-start(bf16[128,256]{1,0:T(8,128)(2,1)S(1)} %collective-permute-done.12.refs_3_), channel_id=1, source_target_pairs={{0,1},{1,0},{2,3},{3,2},{4,5},{5,4},{6,7},{7,6},{8,9},{9,8},{10,11... | collective-permute-start | bytes 196616 | tf_op jit(solution)/shard_map/ppermute | solution.py:316
  45.9 6.3 %copy-start.1 = (bf16[4,1024,512]{2,1,0:T(8,128)(2,1)S(1)}, bf16[4,1024,512]{2,1,0:T(8,128)(2,1)}, u32[]{:S(2)}) copy-start(bf16[4,1024,512]{2,1,0:T(8,128)(2,1)} %refs_2_.2) | copy-start | bytes 12582916
  45.9 6.3 %copy-start.2 = (s32[1,4]{1,0:T(1,128)S(1)}, s32[1,4]{1,0:T(1,128)}, u32[]{:S(2)}) copy-start(s32[1,4]{1,0:T(1,128)} %refs_0_.7) | copy-start | bytes 52
  45.9 6.3 %copy-start.3 = (s32[16]{0:T(128)S(1)}, s32[16]{0:T(128)}, u32[]{:S(2)}) copy-start(s32[16]{0:T(128)} %refs_1_.1) | copy-start | bytes 196
  45.9 4.4 %collective-permute-start.25 = (bf16[128,256]{1,0:T(8,128)(2,1)S(1)}, bf16[128,256]{1,0:T(8,128)(2,1)S(1)}, u32[]{:S(2)}, u32[]{:S(2)}) collective-permute-start(bf16[128,256]{1,0:T(8,128)(2,1)S(1)} %get-tuple-element.42.refs_1_), channel_id=1, source_target_pairs={{0,1},{1,0},{2,3},{3,2},{4,5},{5,4},{6,7},{7,6},{8,9},{9,8},{10,11... | collective-permute-start | bytes 196616 | tf_op jit(solution)/shard_map/ppermute | solution.py:316
  47.4 4.3 %collective-permute-start.27 = (bf16[128,256]{1,0:T(8,128)(2,1)S(1)}, bf16[128,256]{1,0:T(8,128)(2,1)S(1)}, u32[]{:S(2)}, u32[]{:S(2)}) collective-permute-start(bf16[128,256]{1,0:T(8,128)(2,1)S(1)} %collective-permute-done.26.refs_3_), channel_id=1, source_target_pairs={{0,1},{1,0},{2,3},{3,2},{4,5},{5,4},{6,7},{7,6},{8,9},{9,8},{10,11... | collective-permute-start | bytes 196616 | tf_op jit(solution)/shard_map/ppermute | solution.py:316
  50.1 2.1 %collective-permute-start.14 = (bf16[128,1024]{1,0:T(8,128)(2,1)S(1)}, bf16[128,1024]{1,0:T(8,128)(2,1)S(1)}, u32[]{:S(2)}, u32[]{:S(2)}) collective-permute-start(bf16[128,1024]{1,0:T(8,128)(2,1)S(1)} %phase.2.refs_3_), channel_id=1, source_target_pairs={{0,16},{1,17},{2,18},{3,19},{4,20},{5,21},{6,22},{7,23},{8,24},{9,... | collective-permute-start | bytes 786440 | tf_op jit(solution)/shard_map/ppermute | solution.py:316
  52.1 1.6 %collective-permute-start.28 = (bf16[128,1024]{1,0:T(8,128)(2,1)S(1)}, bf16[128,1024]{1,0:T(8,128)(2,1)S(1)}, u32[]{:S(2)}, u32[]{:S(2)}) collective-permute-start(bf16[128,1024]{1,0:T(8,128)(2,1)S(1)} %phase.3.refs_5_), channel_id=1, source_target_pairs={{0,16},{1,17},{2,18},{3,19},{4,20},{5,21},{6,22},{7,23},{8,24},{9,... | collective-permute-start | bytes 786440 | tf_op jit(solution)/shard_map/ppermute | solution.py:316

commit v15 on v14

--- a/solution.py
+++ b/solution.py
@@ -163,8 +163,7 @@
 
 def column_kernel(inner, outer, table, gain, *refs):
     pieces = refs[:inner]
-    keep, *away = refs[inner:-3]
-    stack, total, spectrum = refs[-3:]
+    out, stack, total, spectrum = refs[inner:]
     _, plane, spot = position(inner)
     dists, rows_dev, block = pieces[0].shape
     depth = inner * rows_dev
@@ -180,52 +179,15 @@
         else:
             total[...] += got
     spectrum[...] = total[...].astype(bf16)
-    half = outer // 2
-    side = plane // half
-
-    def rows_from(low):
-        rows = pl.ds(pl.multiple_of(low * depth, half * depth), half * depth)
-        value = jnp.dot(table[rows, :], spectrum[...], preferred_element_type=f32)
-        return value.astype(bf16).reshape(half, depth, block)
-
-    value = rows_from((1 - side) * half)
-    wide = block // len(away)
-    for split, out in enumerate(away):
-        out[...] = value[:, :, split * wide : (split + 1) * wide]
-    keep[...] = rows_from(side * half)
-
-
-def add_kernel(one, two, out):
-    out[...] = (one[...].astype(f32) + two[...].astype(f32)).astype(bf16)
-
-
-def near_kernel(inner, split, keep, across, out):
-    _, plane, _ = position(inner)
-    which = (plane ^ 1) % 2
-    inside = (plane == 1) | (plane == 2)
-    more = jnp.where(inside, across[which].astype(f32), 0.0)
-    wide = out.shape[1]
-    here = keep[which, :, split * wide : (split + 1) * wide].astype(f32)
-    out[...] = (here + more).astype(bf16)
-
-
-def half_kernel(inner, keep, *refs):
-    other, mine = refs[-2:]
-    parts = refs[:-2]
-    splits = len(parts) // 2
-    _, plane, spot = position(inner)
-    which = plane % 2
-    inside = (plane == 1) | (plane == 2)
+    value = jnp.dot(table[...], spectrum[...], preferred_element_type=f32)
+    out[...] = value.astype(bf16).reshape(outer, depth, block)
+
+
+def half_kernel(inner, half, other, mine):
+    _, _, spot = position(inner)
     capacity = mine.shape[0]
-    wide = mine.shape[1] // splits
-    for split in range(splits):
-        across, last = parts[2 * split : 2 * split + 2]
-        lanes = slice(split * wide, (split + 1) * wide)
-        for out, pair in ((mine, spot // 2), (other, 1 - spot // 2)):
-            rows = pl.ds(pl.multiple_of(pair * capacity, capacity), capacity)
-            more = jnp.where(inside, across[which, rows, :].astype(f32), 0.0)
-            got = keep[which, rows, lanes].astype(f32) + more + last[rows, :].astype(f32)
-            out[:, lanes] = got.astype(bf16)
+    for out, pair in ((mine, spot // 2), (other, 1 - spot // 2)):
+        out[...] = half[pl.ds(pl.multiple_of(pair * capacity, capacity), capacity), :]
 
 
 def phase_kernel(inner, table, *refs):
@@ -296,7 +258,6 @@
     dists = cores * dist_dev
     pixels = weights.shape[2]
     capacity = 2 * rows_dev
-    splits = block // 128
     params = pltpu.CompilerParams(vmem_limit_bytes=16 * 2**20)
     one_out = pl.BlockSpec(memory_space=pltpu.VMEM)
 
@@ -326,12 +287,9 @@
         other = first if along_y is diagonal else sent(along_y, to_spot(2))
         return [stays, sent(along_x, to_spot(1)), other, sent(first, to_spot(1))]
 
-    def to_near_plane(c, r):
-        return c, (r // inner ^ 1) * inner + r % inner
-
-    def to_middle(c, r):
-        z = r // inner
-        return (c, (3 - z) * inner + r % inner) if z in (1, 2) else (c ^ 1, r)
+    def direct(stays, along_x, along_y, diagonal):
+        first = sent(along_y, to_spot(2))
+        return [stays, sent(along_x, to_spot(1)), first, sent(diagonal, to_spot(3))]
 
     partner = sent(holograms[0], to_other_core)
     gain = pl.pallas_call(
@@ -357,17 +315,17 @@
         name="row_spectra",
     )(from_hbm(holograms[0]), partner, table, gain)
     arrived = [
-        spread(*pieces[chunk * inner : (chunk + 1) * inner]) for chunk in range(own)
+        direct(*pieces[chunk * inner : (chunk + 1) * inner]) for chunk in range(own)
     ]
 
     sums = []
+    lines = [[z * inner + i for z in range(outer)] for i in range(inner)]
     for chunk in range(own):
-        keep, *away = pl.pallas_call(
+        parts = pl.pallas_call(
             lambda *refs: column_kernel(inner, outer, *refs),
-            out_shape=[shaped(outer // 2, depth, block)]
-            + [shaped(outer // 2, depth, block // splits)] * splits,
+            out_shape=shaped(outer, depth, block),
             in_specs=vmem(2 + inner),
-            out_specs=vmem(1 + splits),
+            out_specs=one_out,
             scratch_shapes=[
                 pltpu.VMEM((dists, depth, block), bf16),
                 pltpu.VMEM((width, block), f32),
@@ -377,41 +335,23 @@
             cost_estimate=cheap,
             name="columns",
         )(table, gain, *arrived[chunk])
-        parts = [keep]
-        for split in range(splits):
-            joint = pl.pallas_call(
-                add_kernel,
-                out_shape=shaped(outer // 2, depth, block // splits),
-                in_specs=vmem(2),
-                out_specs=one_out,
-                compiler_params=params,
-                cost_estimate=cheap,
-                name="joint",
-            )(away[split], sent(away[split], to_near_plane))
-            across = sent(joint, to_middle)
-            near = pl.pallas_call(
-                lambda *refs, split=split: near_kernel(inner, split, *refs),
-                out_shape=shaped(depth, block // splits),
-                in_specs=vmem(2),
-                out_specs=one_out,
-                compiler_params=params,
-                cost_estimate=cheap,
-                name="near",
-            )(keep, across)
-            parts += [across, sent(near, to_near_plane)]
-        sums.append(parts)
+        sums.append(
+            lax.psum_scatter(
+                parts, "rows", scatter_dimension=0, axis_index_groups=lines, tiled=False
+            )
+        )
 
     phases = []
     for chunk in range(own):
         second, first = pl.pallas_call(
             lambda *refs: half_kernel(inner, *refs),
             out_shape=[shaped(capacity, block)] * 2,
-            in_specs=vmem(1 + 2 * splits),
+            in_specs=vmem(1),
             out_specs=vmem(2),
             compiler_params=params,
             cost_estimate=cheap,
             name="half",
-        )(*sums[chunk])
+        )(sums[chunk])
         pieces = spread(first, first, second, second)
         phase = pl.pallas_call(
             lambda *refs: phase_kernel(inner, *refs),

time: 55 us -> 90.7 us (1.65)
  waiting for transfers between devices: 11.8 us -> 43.5 us
  starting transfers between devices: 32.1 us -> 15.7 us
  between operations: 0.22 us -> 13.5 us
  Pallas kernels: 10.7 us -> 14.3 us
  local copies, waits for them, and re-layouts: 0.01 us -> 3.42 us
    reduce_scatter x0 -> x2, waiting for transfers between devices: none -> 28.5 us  [plane_plan(): lax.psum_scatter(parts, 'rows', scatter_dimension=0, axis_index_groups=li...]
    ppermute x29 -> x15, starting transfers between devices: 32.1 us -> 15.7 us  [sent(): return lax.ppermute(value, ('dist', 'rows'), pairs)]
    pallas_call x2, Pallas kernels: 2.59 us -> 6.2 us  [plane_plan(): pl.pallas_call(lambda *refs: column_kernel(inner, outer, *refs), out_shap...]
    unnamed x8 -> x16, local copies, waits for them, and re-layouts: 0.01 us -> 3.42 us
    ppermute x29 -> x15, waiting for transfers between devices: 11.8 us -> 14.9 us  [sent(): return lax.ppermute(value, ('dist', 'rows'), pairs)]
  transfers between devices with their start and end apart: 29 -> 17, of which waited for: 13 -> 11; matrix products, arithmetic and copies ran while one was open for 0% -> 0% of each run, Pallas kernels for 14% -> 9%
where the time goes in v15:
time: 90.7 us; the launch traced here: 90.5 us
  waiting for transfers between devices  43.5 us (48%)
  starting transfers between devices  15.7 us (17%)
  Pallas kernels  14.3 us (16%)
  between operations  13.5 us (15%)
  local copies, waits for them, and re-layouts  3.42 us (4%)
    reduce_scatter x2, waiting for transfers between devices, plane_plan(): lax.psum_scatter(parts, 'rows', scatter_dimension=0, axis_index_groups=li...  28.5 us
    ppermute x15, starting transfers between devices, sent(): return lax.ppermute(value, ('dist', 'rows'), pairs)  15.7 us
    ppermute x15, waiting for transfers between devices, sent(): return lax.ppermute(value, ('dist', 'rows'), pairs)  14.9 us
    pallas_call x2, Pallas kernels, plane_plan(): pl.pallas_call(lambda *refs: column_kernel(inner, outer, *refs), out_shap...  6.2 us
    unnamed x16, local copies, waits for them, and re-layouts  3.42 us
    pallas_call x1, Pallas kernels, plane_plan(): pl.pallas_call(lambda *refs: filter_kernel(inner, dist_dev, *refs), out_s...  2.62 us
    pallas_call x1, Pallas kernels, plane_plan(): pl.pallas_call(lambda *refs: row_kernel(inner, *refs), out_shape=[shaped(...  2.22 us
  transfers between devices with their start and end apart: 17, of which 11 were waited for; matrix products, arithmetic and copies ran while one was open for 0% of the time, Pallas kernels for 9%

profile of v15, /device:TPU:0, one launch (start us, length us, event | category | flops | bytes accessed | tf_op | source)
XLA Modules:
  0.0 90.5 jit_solution(14345605961524483640)
XLA Ops:
  6.5 0.0 copy-start
  6.5 0.0 reduce-scatter.3.cloned.1.call-start
  6.5 0.5 collective-permute-start
  7.0 2.6 %filters.1.refs_3_.refs_1_ = bf16[4,1024,256]{2,1,0:T(8,128)(2,1)S(1)} custom-call(f32[4]{0:T(128)} %refs_0_.6), custom_call_target="tpu_custom_call" | custom-call | flops 1 | bytes 1 | tf_op jit(solution)/shard_map/filters/pallas_call | solution.py:295
  9.6 0.0 copy-start.1
  9.6 0.0 collective-permute-done.refs_1_
  9.6 0.0 copy-done
  9.7 2.2 %row_spectra.1 = (bf16[4,64,256]{2,1,0:T(8,128)(2,1)S(1)}, bf16[4,64,256]{2,1,0:T(8,128)(2,1)S(1)}, bf16[4,64,256]{2,1,0:T(8,128)(2,1)S(1)}, bf16[4,64,256]{2,1,...) custom-call(bf16[4,2,64,1024]{3,2,1,0:T(8,128)(2,1)} %bitcast.6, ...), custom_call_target="tpu_custom_call" | custom-call | flops 1 | bytes 1 | tf_op jit(solution)/shard_map/row_spectra/pallas_call | solution.py:304
  11.9 2.7 %collective-permute-start.1 = (bf16[4,64,256]{2,1,0:T(8,128)(2,1)S(1)}, bf16[4,64,256]{2,1,0:T(8,128)(2,1)S(1)}, u32[]{:S(2)}, u32[]{:S(2)}) collective-permute-start(bf16[4,64,256]{2,1,0:T(8,128)(2,1)S(1)} %get-tuple-element.21), channel_id=1, source_target_pairs={{0,1},{1,0},{2,3},{3,2},{4,5},{5,4},{6,7},{7,6},{8,9},{9,8},{10,11... | collective-permute-start | bytes 393224 | tf_op jit(solution)/shard_map/ppermute | solution.py:277
  14.6 1.5 %collective-permute-start.2 = (bf16[4,64,256]{2,1,0:T(8,128)(2,1)S(1)}, bf16[4,64,256]{2,1,0:T(8,128)(2,1)S(1)}, u32[]{:S(2)}, u32[]{:S(2)}) collective-permute-start(bf16[4,64,256]{2,1,0:T(8,128)(2,1)S(1)} %get-tuple-element.22), channel_id=1, source_target_pairs={{0,2},{1,3},{2,0},{3,1},{4,6},{5,7},{6,4},{7,5},{8,10},{9,11},{10,... | collective-permute-start | bytes 393224 | tf_op jit(solution)/shard_map/ppermute | solution.py:277
  16.1 0.0 collective-permute-start.3
  16.2 2.4 %collective-permute-done.1.refs_3_ = bf16[4,64,256]{2,1,0:T(8,128)(2,1)S(1)} collective-permute-done((bf16[4,64,256]{2,1,0:T(8,128)(2,1)S(1)}, bf16[4,64,256]{2,1,0:T(8,128)(2,1)S(1)}, u32[]{:S(2)}, u32[]{:S(2)}) %collective-permute-start.1) | collective-permute-done | bytes 131104 | tf_op jit(solution)/shard_map/ppermute | solution.py:277
  18.6 4.2 %collective-permute-done.2.refs_4_ = bf16[4,64,256]{2,1,0:T(8,128)(2,1)S(1)} collective-permute-done((bf16[4,64,256]{2,1,0:T(8,128)(2,1)S(1)}, bf16[4,64,256]{2,1,0:T(8,128)(2,1)S(1)}, u32[]{:S(2)}, u32[]{:S(2)}) %collective-permute-start.2) | collective-permute-done | bytes 131104 | tf_op jit(solution)/shard_map/ppermute | solution.py:277
  22.7 0.0 collective-permute-done.3.refs_5_
  22.7 0.0 copy-done.1
  22.7 3.1 %columns.2 = bf16[4,256,256]{2,1,0:T(8,128)(2,1)} custom-call(bf16[1024,1024]{1,0:T(8,128)(2,1)S(1)} %copy-done, bf16[4,1024,256]{2,1,0:T(8,128)(2,1)S(1)} %filters.1.refs_3_.refs_1_, bf16[4,64,256]{2,1,0:T(8,128)(2,1)S(1)} %get-tuple-element.20.refs_2_, bf16[4,64,256]{2,1,0:T(8,128)(2,1)S(1)} %collective-permute-done.1.refs_3_, ...), custom_call_target="tpu_custom_call" | custom-call | flops 1 | bytes 1 | tf_op jit(solution)/shard_map/columns/pallas_call | solution.py:324
  25.8 0.0 reduce-scatter.3.cloned.1.call-update
  25.9 0.0 reduce-scatter.5.cloned.1.call-start
  25.9 1.3 %collective-permute-start.8 = (bf16[4,64,256]{2,1,0:T(8,128)(2,1)S(1)}, bf16[4,64,256]{2,1,0:T(8,128)(2,1)S(1)}, u32[]{:S(2)}, u32[]{:S(2)}) collective-permute-start(bf16[4,64,256]{2,1,0:T(8,128)(2,1)S(1)} %get-tuple-element.27), channel_id=1, source_target_pairs={{0,1},{1,0},{2,3},{3,2},{4,5},{5,4},{6,7},{7,6},{8,9},{9,8},{10,11... | collective-permute-start | bytes 393224 | tf_op jit(solution)/shard_map/ppermute | solution.py:277
  27.2 0.8 collective-permute-start.9
  28.0 1.4 %collective-permute-start.10 = (bf16[4,64,256]{2,1,0:T(8,128)(2,1)S(1)}, bf16[4,64,256]{2,1,0:T(8,128)(2,1)S(1)}, u32[]{:S(2)}, u32[]{:S(2)}) collective-permute-start(bf16[4,64,256]{2,1,0:T(8,128)(2,1)S(1)} %get-tuple-element.29), channel_id=1, source_target_pairs={{0,3},{1,2},{2,1},{3,0},{4,7},{5,6},{6,5},{7,4},{8,11},{9,10},{10,... | collective-permute-start | bytes 393224 | tf_op jit(solution)/shard_map/ppermute | solution.py:277
  29.5 2.4 %collective-permute-done.8.refs_3_ = bf16[4,64,256]{2,1,0:T(8,128)(2,1)S(1)} collective-permute-done((bf16[4,64,256]{2,1,0:T(8,128)(2,1)S(1)}, bf16[4,64,256]{2,1,0:T(8,128)(2,1)S(1)}, u32[]{:S(2)}, u32[]{:S(2)}) %collective-permute-start.8) | collective-permute-done | bytes 131104 | tf_op jit(solution)/shard_map/ppermute | solution.py:277
  31.9 2.6 %collective-permute-done.9.refs_4_ = bf16[4,64,256]{2,1,0:T(8,128)(2,1)S(1)} collective-permute-done((bf16[4,64,256]{2,1,0:T(8,128)(2,1)S(1)}, bf16[4,64,256]{2,1,0:T(8,128)(2,1)S(1)}, u32[]{:S(2)}, u32[]{:S(2)}) %collective-permute-start.9) | collective-permute-done | bytes 131104 | tf_op jit(solution)/shard_map/ppermute | solution.py:277
  34.5 0.0 collective-permute-done.10.refs_5_
  34.5 0.0 copy-start.2
  34.5 1.6 %copy-done.2 = bf16[4,1024,256]{2,1,0:T(8,128)(2,1)S(1)} copy-done((bf16[4,1024,256]{2,1,0:T(8,128)(2,1)S(1)}, bf16[4,1024,256]{2,1,0:T(8,128)(2,1)}, u32[]{:S(2)}) %copy-start.2) | copy-done | bytes 2097176
  36.1 3.1 %columns.3 = bf16[4,256,256]{2,1,0:T(8,128)(2,1)} custom-call(bf16[1024,1024]{1,0:T(8,128)(2,1)S(1)} %copy-done, bf16[4,1024,256]{2,1,0:T(8,128)(2,1)S(1)} %copy-done.2, bf16[4,64,256]{2,1,0:T(8,128)(2,1)S(1)} %get-tuple-element.26.refs_2_, bf16[4,64,256]{2,1,0:T(8,128)(2,1)S(1)} %collective-permute-done.8.refs_3_, ...), custom_call_target="tpu_custom_call" | custom-call | flops 1 | bytes 1 | tf_op jit(solution)/shard_map/columns/pallas_call | solution.py:324
  39.2 0.0 reduce-scatter.5.cloned.1.call-update
  39.2 8.8 %reduce-scatter.3.cloned.1.call-done = bf16[1,256,256]{2,1,0:T(8,128)(2,1)} async-done(((bf16[4,256,256]{2,1,0:T(8,128)(2,1)}), bf16[1,256,256]{2,1,0:T(8,128)(2,1)}) %reduce-scatter.3.cloned.1.call-update) | async-done | bytes 131088 | tf_op jit(solution)/shard_map/reduce_scatter | solution.py:339
  48.0 0.0 copy-start.4
  48.0 0.9 copy-done.4
  48.9 1.6 %collective-permute-start.5 = (bf16[128,256]{1,0:T(8,128)(2,1)S(1)}, bf16[128,256]{1,0:T(8,128)(2,1)S(1)}, u32[]{:S(2)}, u32[]{:S(2)}) collective-permute-start(bf16[128,256]{1,0:T(8,128)(2,1)S(1)} %get-tuple-element.25), channel_id=1, source_target_pairs={{0,2},{1,3},{2,0},{3,1},{4,6},{5,7},{6,4},{7,5},{8,10},{9,11},{10,... | collective-permute-start | bytes 196616 | tf_op jit(solution)/shard_map/ppermute | solution.py:277
  50.4 19.8 %reduce-scatter.5.cloned.1.call-done = bf16[1,256,256]{2,1,0:T(8,128)(2,1)} async-done(((bf16[4,256,256]{2,1,0:T(8,128)(2,1)}), bf16[1,256,256]{2,1,0:T(8,128)(2,1)}) %reduce-scatter.5.cloned.1.call-update) | async-done | bytes 131088 | tf_op jit(solution)/shard_map/reduce_scatter | solution.py:339
  70.2 0.0 copy-start.5
  70.2 0.9 copy-done.5
  71.1 1.5 %collective-permute-start.12 = (bf16[128,256]{1,0:T(8,128)(2,1)S(1)}, bf16[128,256]{1,0:T(8,128)(2,1)S(1)}, u32[]{:S(2)}, u32[]{:S(2)}) collective-permute-start(bf16[128,256]{1,0:T(8,128)(2,1)S(1)} %get-tuple-element.31), channel_id=1, source_target_pairs={{0,2},{1,3},{2,0},{3,1},{4,6},{5,7},{6,4},{7,5},{8,10},{9,11},{10,... | collective-permute-start | bytes 196616 | tf_op jit(solution)/shard_map/ppermute | solution.py:277
  72.6 1.5 %collective-permute-start.4 = (bf16[128,256]{1,0:T(8,128)(2,1)S(1)}, bf16[128,256]{1,0:T(8,128)(2,1)S(1)}, u32[]{:S(2)}, u32[]{:S(2)}) collective-permute-start(bf16[128,256]{1,0:T(8,128)(2,1)S(1)} %get-tuple-element.24.refs_1_), channel_id=1, source_target_pairs={{0,1},{1,0},{2,3},{3,2},{4,5},{5,4},{6,7},{7,6},{8,9},{9,8},{10,11... | collective-permute-start | bytes 196616 | tf_op jit(solution)/shard_map/ppermute | solution.py:277
  74.2 0.0 collective-permute-done.5.refs_3_
  74.2 0.5 collective-permute-start.6
  74.7 0.0 copy-start.3
  74.7 0.0 copy-start.6
  74.7 0.0 copy-start.7
  74.7 1.5 %collective-permute-start.11 = (bf16[128,256]{1,0:T(8,128)(2,1)S(1)}, bf16[128,256]{1,0:T(8,128)(2,1)S(1)}, u32[]{:S(2)}, u32[]{:S(2)}) collective-permute-start(bf16[128,256]{1,0:T(8,128)(2,1)S(1)} %get-tuple-element.30.refs_1_), channel_id=1, source_target_pairs={{0,1},{1,0},{2,3},{3,2},{4,5},{5,4},{6,7},{7,6},{8,9},{9,8},{10,11... | collective-permute-start | bytes 196616 | tf_op jit(solution)/shard_map/ppermute | solution.py:277
  76.2 0.0 collective-permute-done.12.refs_3_
  76.2 0.7 collective-permute-start.13
  76.9 0.1 collective-permute-done.4.refs_2_
  77.0 1.4 %collective-permute-done.6.refs_4_ = bf16[128,256]{1,0:T(8,128)(2,1)S(1)} collective-permute-done((bf16[128,256]{1,0:T(8,128)(2,1)S(1)}, bf16[128,256]{1,0:T(8,128)(2,1)S(1)}, u32[]{:S(2)}, u32[]{:S(2)}) %collective-permute-start.6) | collective-permute-done | bytes 65568 | tf_op jit(solution)/shard_map/ppermute | solution.py:277
  78.4 0.5 phase.2.refs_3_
  78.9 0.1 collective-permute-start.7
  79.0 0.2 collective-permute-done.11.refs_2_
  79.1 1.3 %collective-permute-done.13.refs_4_ = bf16[128,256]{1,0:T(8,128)(2,1)S(1)} collective-permute-done((bf16[128,256]{1,0:T(8,128)(2,1)S(1)}, bf16[128,256]{1,0:T(8,128)(2,1)S(1)}, u32[]{:S(2)}, u32[]{:S(2)}) %collective-permute-start.13) | collective-permute-done | bytes 65568 | tf_op jit(solution)/shard_map/ppermute | solution.py:277
  80.5 0.5 phase.3.refs_5_
  80.9 0.1 collective-permute-start.14
  81.0 0.0 collective-permute-done.7.refs_4_
  81.0 0.0 copy-done.3
  81.0 0.0 copy-done.6
  81.0 0.0 copy-done.7
  81.0 1.2 %recon.2 = (f32[128,512]{1,0:T(8,128)S(1)}, bf16[1024,512]{1,0:T(8,128)(2,1)S(1)}, bf16[128,128]{1,0:T(8,128)(2,1)S(1)}) custom-call(s32[1,4]{1,0:T(1,128)S(1)} %copy-done.6, s32[16]{0:T(128)S(1)} %copy-done.7, bf16[4,1024,512]{2,1,0:T(8,128)(2,1)S(1)} %copy-done.3, bf16[128,1024]{1,0:T(8,128)(2,1)S(1)} %phase.2.refs_3_, ...), custom_call_target="tpu_custom_call" | custom-call | flops 1 | bytes 1 | tf_op jit(solution)/shard_map/recon/pallas_call | solution.py:368
  82.3 0.3 collective-permute-done.14.phase
  82.5 1.1 %recon.3 = bf16[128,512]{1,0:T(8,128)(2,1)} custom-call(bf16[1024,512]{1,0:T(8,128)(2,1)S(1)} %get-tuple-element.32.weights, bf16[128,1024]{1,0:T(8,128)(2,1)S(1)} %collective-permute-done.14.phase, f32[128,512]{1,0:T(8,128)S(1)} %get-tuple-element.33.before, bf16[128,128]{1,0:T(8,128)(2,1)S(1)} %get-tuple-element.34.select), custom_call_target="tpu_custom_call" | custom-call | flops 1 | bytes 1 | tf_op jit(solution)/shard_map/recon/pallas_call | solution.py:381
  (2 shorter events, 0.0 us)
Async XLA Ops:
  6.5 3.1 %copy-start = (bf16[1024,1024]{1,0:T(8,128)(2,1)S(1)}, bf16[1024,1024]{1,0:T(8,128)(2,1)}, u32[]{:S(2)}) copy-start(bf16[1024,1024]{1,0:T(8,128)(2,1)} %constant.2.clone.refs_2_.refs_0_) | copy-start | bytes 6291460
  6.5 41.4 %reduce-scatter.3.cloned.1.call-start = ((), (), s32[]{:S(2)}) async-start(), calls=%async_computation.2 | async-start | bytes 655360 | tf_op jit(solution)/shard_map/reduce_scatter | solution.py:339
  6.5 3.1 %collective-permute-start = (bf16[4,2,64,1024]{3,2,1,0:T(8,128)(2,1)}, bf16[4,2,64,1024]{3,2,1,0:T(8,128)(2,1)S(1)}, u32[]{:S(2)}, u32[]{:S(2)}) collective-permute-start(bf16[4,2,64,1024]{3,2,1,0:T(8,128)(2,1)} %bitcast.5), channel_id=1, source_target_pairs={{0,16},{1,17},{2,18},{3,19},{4,20},{5,21},{6,22},{7,23},{8,24},{9,... | collective-permute-start | bytes 3145736 | tf_op jit(solution)/shard_map/ppermute | solution.py:277
  9.6 13.1 %copy-start.1 = (bf16[4,1024,256]{2,1,0:T(8,128)(2,1)}, bf16[4,1024,256]{2,1,0:T(8,128)(2,1)S(1)}, u32[]{:S(2)}) copy-start(bf16[4,1024,256]{2,1,0:T(8,128)(2,1)S(1)} %filters.1.refs_3_.refs_1_) | copy-start | bytes 6291460
  11.9 6.7 %collective-permute-start.1 = (bf16[4,64,256]{2,1,0:T(8,128)(2,1)S(1)}, bf16[4,64,256]{2,1,0:T(8,128)(2,1)S(1)}, u32[]{:S(2)}, u32[]{:S(2)}) collective-permute-start(bf16[4,64,256]{2,1,0:T(8,128)(2,1)S(1)} %get-tuple-element.21), channel_id=1, source_target_pairs={{0,1},{1,0},{2,3},{3,2},{4,5},{5,4},{6,7},{7,6},{8,9},{9,8},{10,11... | collective-permute-start | bytes 393224 | tf_op jit(solution)/shard_map/ppermute | solution.py:277
  14.6 8.1 %collective-permute-start.2 = (bf16[4,64,256]{2,1,0:T(8,128)(2,1)S(1)}, bf16[4,64,256]{2,1,0:T(8,128)(2,1)S(1)}, u32[]{:S(2)}, u32[]{:S(2)}) collective-permute-start(bf16[4,64,256]{2,1,0:T(8,128)(2,1)S(1)} %get-tuple-element.22), channel_id=1, source_target_pairs={{0,2},{1,3},{2,0},{3,1},{4,6},{5,7},{6,4},{7,5},{8,10},{9,11},{10,... | collective-permute-start | bytes 393224 | tf_op jit(solution)/shard_map/ppermute | solution.py:277
  16.1 6.6 %collective-permute-start.3 = (bf16[4,64,256]{2,1,0:T(8,128)(2,1)S(1)}, bf16[4,64,256]{2,1,0:T(8,128)(2,1)S(1)}, u32[]{:S(2)}, u32[]{:S(2)}) collective-permute-start(bf16[4,64,256]{2,1,0:T(8,128)(2,1)S(1)} %get-tuple-element.23), channel_id=1, source_target_pairs={{0,3},{1,2},{2,1},{3,0},{4,7},{5,6},{6,5},{7,4},{8,11},{9,10},{10,... | collective-permute-start | bytes 393224 | tf_op jit(solution)/shard_map/ppermute | solution.py:277
  25.9 44.4 %reduce-scatter.5.cloned.1.call-start = ((), (), s32[]{:S(2)}) async-start(), calls=%async_computation.3 | async-start | bytes 655360 | tf_op jit(solution)/shard_map/reduce_scatter | solution.py:339
  25.9 6.0 %collective-permute-start.8 = (bf16[4,64,256]{2,1,0:T(8,128)(2,1)S(1)}, bf16[4,64,256]{2,1,0:T(8,128)(2,1)S(1)}, u32[]{:S(2)}, u32[]{:S(2)}) collective-permute-start(bf16[4,64,256]{2,1,0:T(8,128)(2,1)S(1)} %get-tuple-element.27), channel_id=1, source_target_pairs={{0,1},{1,0},{2,3},{3,2},{4,5},{5,4},{6,7},{7,6},{8,9},{9,8},{10,11... | collective-permute-start | bytes 393224 | tf_op jit(solution)/shard_map/ppermute | solution.py:277
  27.2 7.3 %collective-permute-start.9 = (bf16[4,64,256]{2,1,0:T(8,128)(2,1)S(1)}, bf16[4,64,256]{2,1,0:T(8,128)(2,1)S(1)}, u32[]{:S(2)}, u32[]{:S(2)}) collective-permute-start(bf16[4,64,256]{2,1,0:T(8,128)(2,1)S(1)} %get-tuple-element.28), channel_id=1, source_target_pairs={{0,2},{1,3},{2,0},{3,1},{4,6},{5,7},{6,4},{7,5},{8,10},{9,11},{10,... | collective-permute-start | bytes 393224 | tf_op jit(solution)/shard_map/ppermute | solution.py:277
  28.0 6.5 %collective-permute-start.10 = (bf16[4,64,256]{2,1,0:T(8,128)(2,1)S(1)}, bf16[4,64,256]{2,1,0:T(8,128)(2,1)S(1)}, u32[]{:S(2)}, u32[]{:S(2)}) collective-permute-start(bf16[4,64,256]{2,1,0:T(8,128)(2,1)S(1)} %get-tuple-element.29), channel_id=1, source_target_pairs={{0,3},{1,2},{2,1},{3,0},{4,7},{5,6},{6,5},{7,4},{8,11},{9,10},{10,... | collective-permute-start | bytes 393224 | tf_op jit(solution)/shard_map/ppermute | solution.py:277
  34.5 1.6 %copy-start.2 = (bf16[4,1024,256]{2,1,0:T(8,128)(2,1)S(1)}, bf16[4,1024,256]{2,1,0:T(8,128)(2,1)}, u32[]{:S(2)}) copy-start(bf16[4,1024,256]{2,1,0:T(8,128)(2,1)} %copy-done.1) | copy-start | bytes 6291460
  48.0 0.9 copy-start.4
  48.9 25.3 %collective-permute-start.5 = (bf16[128,256]{1,0:T(8,128)(2,1)S(1)}, bf16[128,256]{1,0:T(8,128)(2,1)S(1)}, u32[]{:S(2)}, u32[]{:S(2)}) collective-permute-start(bf16[128,256]{1,0:T(8,128)(2,1)S(1)} %get-tuple-element.25), channel_id=1, source_target_pairs={{0,2},{1,3},{2,0},{3,1},{4,6},{5,7},{6,4},{7,5},{8,10},{9,11},{10,... | collective-permute-start | bytes 196616 | tf_op jit(solution)/shard_map/ppermute | solution.py:277
  70.2 0.9 copy-start.5
  71.1 5.1 %collective-permute-start.12 = (bf16[128,256]{1,0:T(8,128)(2,1)S(1)}, bf16[128,256]{1,0:T(8,128)(2,1)S(1)}, u32[]{:S(2)}, u32[]{:S(2)}) collective-permute-start(bf16[128,256]{1,0:T(8,128)(2,1)S(1)} %get-tuple-element.31), channel_id=1, source_target_pairs={{0,2},{1,3},{2,0},{3,1},{4,6},{5,7},{6,4},{7,5},{8,10},{9,11},{10,... | collective-permute-start | bytes 196616 | tf_op jit(solution)/shard_map/ppermute | solution.py:277
  72.6 4.4 %collective-permute-start.4 = (bf16[128,256]{1,0:T(8,128)(2,1)S(1)}, bf16[128,256]{1,0:T(8,128)(2,1)S(1)}, u32[]{:S(2)}, u32[]{:S(2)}) collective-permute-start(bf16[128,256]{1,0:T(8,128)(2,1)S(1)} %get-tuple-element.24.refs_1_), channel_id=1, source_target_pairs={{0,1},{1,0},{2,3},{3,2},{4,5},{5,4},{6,7},{7,6},{8,9},{9,8},{10,11... | collective-permute-start | bytes 196616 | tf_op jit(solution)/shard_map/ppermute | solution.py:277
  74.2 4.3 %collective-permute-start.6 = (bf16[128,256]{1,0:T(8,128)(2,1)S(1)}, bf16[128,256]{1,0:T(8,128)(2,1)S(1)}, u32[]{:S(2)}, u32[]{:S(2)}) collective-permute-start(bf16[128,256]{1,0:T(8,128)(2,1)S(1)} %collective-permute-done.5.refs_3_), channel_id=1, source_target_pairs={{0,1},{1,0},{2,3},{3,2},{4,5},{5,4},{6,7},{7,6},{8,9},{9,8},{10,11... | collective-permute-start | bytes 196616 | tf_op jit(solution)/shard_map/ppermute | solution.py:277
  74.7 6.3 %copy-start.3 = (bf16[4,1024,512]{2,1,0:T(8,128)(2,1)S(1)}, bf16[4,1024,512]{2,1,0:T(8,128)(2,1)}, u32[]{:S(2)}) copy-start(bf16[4,1024,512]{2,1,0:T(8,128)(2,1)} %refs_2_.2) | copy-start | bytes 12582916
  74.7 6.3 %copy-start.6 = (s32[1,4]{1,0:T(1,128)S(1)}, s32[1,4]{1,0:T(1,128)}, u32[]{:S(2)}) copy-start(s32[1,4]{1,0:T(1,128)} %refs_0_.7) | copy-start | bytes 52
  74.7 6.3 %copy-start.7 = (s32[16]{0:T(128)S(1)}, s32[16]{0:T(128)}, u32[]{:S(2)}) copy-start(s32[16]{0:T(128)} %refs_1_.1) | copy-start | bytes 196
  74.7 4.4 %collective-permute-start.11 = (bf16[128,256]{1,0:T(8,128)(2,1)S(1)}, bf16[128,256]{1,0:T(8,128)(2,1)S(1)}, u32[]{:S(2)}, u32[]{:S(2)}) collective-permute-start(bf16[128,256]{1,0:T(8,128)(2,1)S(1)} %get-tuple-element.30.refs_1_), channel_id=1, source_target_pairs={{0,1},{1,0},{2,3},{3,2},{4,5},{5,4},{6,7},{7,6},{8,9},{9,8},{10,11... | collective-permute-start | bytes 196616 | tf_op jit(solution)/shard_map/ppermute | solution.py:277
  76.2 4.3 %collective-permute-start.13 = (bf16[128,256]{1,0:T(8,128)(2,1)S(1)}, bf16[128,256]{1,0:T(8,128)(2,1)S(1)}, u32[]{:S(2)}, u32[]{:S(2)}) collective-permute-start(bf16[128,256]{1,0:T(8,128)(2,1)S(1)} %collective-permute-done.12.refs_3_), channel_id=1, source_target_pairs={{0,1},{1,0},{2,3},{3,2},{4,5},{5,4},{6,7},{7,6},{8,9},{9,8},{10,11... | collective-permute-start | bytes 196616 | tf_op jit(solution)/shard_map/ppermute | solution.py:277
  78.9 2.1 %collective-permute-start.7 = (bf16[128,1024]{1,0:T(8,128)(2,1)S(1)}, bf16[128,1024]{1,0:T(8,128)(2,1)S(1)}, u32[]{:S(2)}, u32[]{:S(2)}) collective-permute-start(bf16[128,1024]{1,0:T(8,128)(2,1)S(1)} %phase.2.refs_3_), channel_id=1, source_target_pairs={{0,16},{1,17},{2,18},{3,19},{4,20},{5,21},{6,22},{7,23},{8,24},{9,... | collective-permute-start | bytes 786440 | tf_op jit(solution)/shard_map/ppermute | solution.py:277
  80.9 1.6 %collective-permute-start.14 = (bf16[128,1024]{1,0:T(8,128)(2,1)S(1)}, bf16[128,1024]{1,0:T(8,128)(2,1)S(1)}, u32[]{:S(2)}, u32[]{:S(2)}) collective-permute-start(bf16[128,1024]{1,0:T(8,128)(2,1)S(1)} %phase.3.refs_5_), channel_id=1, source_target_pairs={{0,16},{1,17},{2,18},{3,19},{4,20},{5,21},{6,22},{7,23},{8,24},{9,... | collective-permute-start | bytes 786440 | tf_op jit(solution)/shard_map/ppermute | solution.py:277
Sparse Core Ops, SparseCore 0:
  26.0 21.9 reduce-scatter.2
  50.2 19.9 reduce-scatter.4

commit v16 on v13

--- a/solution.py
+++ b/solution.py
@@ -98,7 +98,7 @@
     return lax.axis_index("dist"), device // inner, device % inner
 
 
-def row_kernel(inner, holo, there, table, after, *refs):
+def row_kernel(inner, holo, there, table, *refs):
     outs, mine, loaded = refs[:-2], refs[-2], refs[-1]
     own = len(outs) // inner
     core, _, spot = position(inner)
@@ -119,11 +119,11 @@
 
 
 def whole_turns(scale, square):
-    turns = scale * square
+    turns = scale * square * (0.5 / math.pi)
     return (turns - jnp.round(turns)) * (2.0 * math.pi)
 
 
-def filter_kernel(inner, dist_dev, turns, out):
+def filter_kernel(inner, dist_dev, turns, after, out):
     dists, width, block = out.shape
     core, _, spot = position(inner)
 
@@ -211,34 +211,38 @@
     out[...] = (here + more).astype(bf16)
 
 
-def half_kernel(inner, keep, *refs):
-    other, mine = refs[-2:]
-    parts = refs[:-2]
-    splits = len(parts) // 2
+def half_kernel(inner, own, *refs):
+    other, mine, again = refs[-3:]
+    each = (len(refs) - 3) // own
     _, plane, spot = position(inner)
     which = plane % 2
     inside = (plane == 1) | (plane == 2)
-    capacity = mine.shape[0]
-    wide = mine.shape[1] // splits
-    for split in range(splits):
-        across, last = parts[2 * split : 2 * split + 2]
-        lanes = slice(split * wide, (split + 1) * wide)
-        for out, pair in ((mine, spot // 2), (other, 1 - spot // 2)):
-            rows = pl.ds(pl.multiple_of(pair * capacity, capacity), capacity)
-            more = jnp.where(inside, across[which, rows, :].astype(f32), 0.0)
-            got = keep[which, rows, lanes].astype(f32) + more + last[rows, :].astype(f32)
-            out[:, lanes] = got.astype(bf16)
+    _, capacity, block = mine.shape
+    wide = block // (each // 2)
+    for chunk in range(own):
+        keep, *parts = refs[chunk * each : (chunk + 1) * each]
+        for split in range(each // 2):
+            across, last = parts[2 * split : 2 * split + 2]
+            lanes = slice(split * wide, (split + 1) * wide)
+            for out, pair in ((mine, spot // 2), (other, 1 - spot // 2)):
+                rows = pl.ds(pl.multiple_of(pair * capacity, capacity), capacity)
+                more = jnp.where(inside, across[which, rows, :].astype(f32), 0.0)
+                got = keep[which, rows, lanes].astype(f32) + more + last[rows, :].astype(f32)
+                out[chunk, :, lanes] = got.astype(bf16)
+    again[...] = other[...]
 
 
 def phase_kernel(inner, table, *refs):
     pieces = dict(zip(tail_order, refs[:inner]))
-    out, joined = refs[-2:]
+    *outs, joined = refs[inner:]
     _, _, spot = position(inner)
-    block = refs[0].shape[1]
+    own, capacity, block = refs[0].shape
     for rel in range(inner):
         columns = pl.ds(pl.multiple_of((spot ^ rel) * block, block), block)
-        joined[:, columns] = pieces[rel][...]
-    out[...] = jnp.dot(joined[...], table[...], preferred_element_type=f32).astype(bf16)
+        joined[:, columns] = pieces[rel][...].reshape(own * capacity, block)
+    got = jnp.dot(joined[...], table[...], preferred_element_type=f32).astype(bf16)
+    for chunk in range(own):
+        outs[chunk][...] = got[chunk * capacity : (chunk + 1) * capacity]
 
 
 def recon_kernel(own, order, slabs, weights, *refs):
@@ -334,19 +338,10 @@
         return (c, (3 - z) * inner + r % inner) if z in (1, 2) else (c ^ 1, r)
 
     partner = sent(holograms[0], to_other_core)
-    gain = pl.pallas_call(
-        lambda *refs: filter_kernel(inner, dist_dev, *refs),
-        out_shape=shaped(dists, width, block),
-        in_specs=smem(1),
-        out_specs=one_out,
-        compiler_params=params,
-        cost_estimate=cheap,
-        name="filters",
-    )(propagation * (0.5 / math.pi))
     pieces = pl.pallas_call(
         lambda *refs: row_kernel(inner, *refs),
         out_shape=[shaped(dists, rows_dev, block)] * (own * inner),
-        in_specs=in_hbm(1) + vmem(2) + unread(1),
+        in_specs=in_hbm(1) + vmem(2),
         out_specs=vmem(own * inner),
         scratch_shapes=[
             pltpu.VMEM((own, dist_dev, rows_dev, width), bf16),
@@ -355,10 +350,20 @@
         compiler_params=params,
         cost_estimate=cheap,
         name="row_spectra",
-    )(from_hbm(holograms[0]), partner, table, gain)
+    )(from_hbm(holograms[0]), partner, table)
     arrived = [
         spread(pieces[chunk * inner : (chunk + 1) * inner], send_order) for chunk in range(own)
     ]
+
+    gain = pl.pallas_call(
+        lambda *refs: filter_kernel(inner, dist_dev, *refs),
+        out_shape=shaped(dists, width, block),
+        in_specs=smem(1) + unread(1),
+        out_specs=one_out,
+        compiler_params=params,
+        cost_estimate=cheap,
+        name="filters",
+    )(from_hbm(propagation), pieces[0])
 
     sums = []
     for chunk in range(own):
@@ -401,29 +406,27 @@
             parts += [across, sent(near, to_near_plane)]
         sums.append(parts)
 
-    phases = []
-    for chunk in range(own):
-        second, first = pl.pallas_call(
-            lambda *refs: half_kernel(inner, *refs),
-            out_shape=[shaped(capacity, block)] * 2,
-            in_specs=vmem(1 + 2 * splits),
-            out_specs=vmem(2),
-            compiler_params=params,
-            cost_estimate=cheap,
-            name="half",
-        )(*sums[chunk])
-        pieces = spread([first, first, second, second], tail_order)
-        phase = pl.pallas_call(
-            lambda *refs: phase_kernel(inner, *refs),
-            out_shape=shaped(capacity, width),
-            in_specs=vmem(1 + inner),
-            out_specs=one_out,
-            scratch_shapes=[pltpu.VMEM((capacity, width), bf16)],
-            compiler_params=params,
-            cost_estimate=cheap,
-            name="phase",
-        )(table, *pieces)
-        phases += [phase, sent(phase, to_other_core)]
+    parts = [part for chunk in sums for part in chunk]
+    second, first, again = pl.pallas_call(
+        lambda *refs: half_kernel(inner, own, *refs),
+        out_shape=[shaped(own, capacity, block)] * 3,
+        in_specs=vmem(len(parts)),
+        out_specs=vmem(3),
+        compiler_params=params,
+        cost_estimate=cheap,
+        name="half",
+    )(*parts)
+    ours = pl.pallas_call(
+        lambda *refs: phase_kernel(inner, *refs),
+        out_shape=[shaped(capacity, width)] * own,
+        in_specs=vmem(1 + inner),
+        out_specs=vmem(own),
+        scratch_shapes=[pltpu.VMEM((own * capacity, width), bf16)],
+        compiler_params=params,
+        cost_estimate=cheap,
+        name="phase",
+    )(table, *spread([first, first, second, again], tail_order))
+    phases = [value for phase in ours for value in (phase, sent(phase, to_other_core))]
 
     total, chosen, select = pl.pallas_call(
         lambda *refs: recon_kernel(own, *refs),

time: 54.1 us -> 56.7 us (1.048)
  waiting for transfers between devices: 11.8 us -> 17.9 us
  starting transfers between devices: 30.7 us -> 26.5 us
  local copies, waits for them, and re-layouts: 0.01 us -> 1.62 us
  other arithmetic: 0.83 us -> 0 us
    ppermute x27 -> x24, waiting for transfers between devices: 11.8 us -> 17.9 us  [sent(): return lax.ppermute(value, ('dist', 'rows'), pairs)]
    ppermute x27 -> x24, starting transfers between devices: 30.7 us -> 26.5 us  [sent(): return lax.ppermute(value, ('dist', 'rows'), pairs)]
    unnamed x8 -> x10, local copies, waits for them, and re-layouts: 0.01 us -> 1.62 us
    mul x1 -> x0, other arithmetic: 0.83 us -> none  [plane_plan(): propagation * (0.5 / math.pi)]
  transfers between devices with their start and end apart: 27 -> 24, of which waited for: 8 -> 11; matrix products, arithmetic and copies ran while one was open for 2% -> 0% of each run, Pallas kernels for 14% -> 12%
where the time goes in v16:
time: 56.7 us; the launch traced here: 56.5 us
  starting transfers between devices  26.5 us (47%)
  waiting for transfers between devices  17.9 us (32%)
  Pallas kernels  10.4 us (18%)
  local copies, waits for them, and re-layouts  1.62 us (3%)
    ppermute x24, starting transfers between devices, sent(): return lax.ppermute(value, ('dist', 'rows'), pairs)  26.5 us
    ppermute x24, waiting for transfers between devices, sent(): return lax.ppermute(value, ('dist', 'rows'), pairs)  17.9 us
    pallas_call x2, Pallas kernels, plane_plan(): pl.pallas_call(lambda *refs: column_kernel(inner, outer, *refs), out_shap...  2.6 us
    pallas_call x1, Pallas kernels, plane_plan(): pl.pallas_call(lambda *refs: filter_kernel(inner, dist_dev, *refs), out_s...  2.49 us
    pallas_call x1, Pallas kernels, plane_plan(): pl.pallas_call(lambda *refs: row_kernel(inner, *refs), out_shape=[shaped(...  1.81 us
    unnamed x10, local copies, waits for them, and re-layouts  1.62 us
    pallas_call x1, Pallas kernels, plane_plan(): pl.pallas_call(lambda *refs: recon_kernel(own, *refs), out_shape=[jax.Sha...  1.2 us
  transfers between devices with their start and end apart: 24, of which 11 were waited for; matrix products, arithmetic and copies ran while one was open for 0% of the time, Pallas kernels for 12%

profile of v16, /device:TPU:0, one launch (start us, length us, event | category | flops | bytes accessed | tf_op | source)
XLA Modules:
  0.0 56.5 jit_solution(590226146442815758)
XLA Ops:
  0.0 0.5 collective-permute-start
  0.5 2.5 %collective-permute-done.refs_1_ = bf16[4,2,64,1024]{3,2,1,0:T(8,128)(2,1)S(1)} collective-permute-done((bf16[4,2,64,1024]{3,2,1,0:T(8,128)(2,1)}, bf16[4,2,64,1024]{3,2,1,0:T(8,128)(2,1)S(1)}, u32[]{:S(2)}, u32[]{:S(2)}) %collective-permute-start) | collective-permute-done | bytes 1048608 | tf_op jit(solution)/shard_map/ppermute | solution.py:322
  3.0 1.6 %copy-done = bf16[1024,1024]{1,0:T(8,128)(2,1)S(1)} copy-done((bf16[1024,1024]{1,0:T(8,128)(2,1)S(1)}, bf16[1024,1024]{1,0:T(8,128)(2,1)}, u32[]{:S(2)}) %copy-start) | copy-done | bytes 2097176
  4.5 1.8 %row_spectra.1 = (bf16[4,64,256]{2,1,0:T(8,128)(2,1)S(1)}, bf16[4,64,256]{2,1,0:T(8,128)(2,1)S(1)}, bf16[4,64,256]{2,1,0:T(8,128)(2,1)S(1)}, bf16[4,64,256]{2,1,...) custom-call(bf16[4,2,64,1024]{3,2,1,0:T(8,128)(2,1)} %bitcast.2, ...), custom_call_target="tpu_custom_call" | custom-call | flops 1 | bytes 1 | tf_op jit(solution)/shard_map/row_spectra/pallas_call | solution.py:341
  6.4 0.0 copy-start.1
  6.4 2.9 %collective-permute-start.10 = (bf16[4,64,256]{2,1,0:T(8,128)(2,1)S(1)}, bf16[4,64,256]{2,1,0:T(8,128)(2,1)S(1)}, u32[]{:S(2)}, u32[]{:S(2)}) collective-permute-start(bf16[4,64,256]{2,1,0:T(8,128)(2,1)S(1)} %get-tuple-element.35), channel_id=1, source_target_pairs={{0,2},{1,3},{2,0},{3,1},{4,6},{5,7},{6,4},{7,5},{8,10},{9,11},{10,... | collective-permute-start | bytes 393224 | tf_op jit(solution)/shard_map/ppermute | solution.py:322
  9.3 1.5 %collective-permute-start.11 = (bf16[4,64,256]{2,1,0:T(8,128)(2,1)S(1)}, bf16[4,64,256]{2,1,0:T(8,128)(2,1)S(1)}, u32[]{:S(2)}, u32[]{:S(2)}) collective-permute-start(bf16[4,64,256]{2,1,0:T(8,128)(2,1)S(1)} %get-tuple-element.36), channel_id=1, source_target_pairs={{0,1},{1,0},{2,3},{3,2},{4,5},{5,4},{6,7},{7,6},{8,9},{9,8},{10,11... | collective-permute-start | bytes 393224 | tf_op jit(solution)/shard_map/ppermute | solution.py:322
  10.8 0.1 collective-permute-start.12
  10.9 1.9 %collective-permute-start.1 = (bf16[4,64,256]{2,1,0:T(8,128)(2,1)S(1)}, bf16[4,64,256]{2,1,0:T(8,128)(2,1)S(1)}, u32[]{:S(2)}, u32[]{:S(2)}) collective-permute-start(bf16[4,64,256]{2,1,0:T(8,128)(2,1)S(1)} %get-tuple-element.28), channel_id=1, source_target_pairs={{0,2},{1,3},{2,0},{3,1},{4,6},{5,7},{6,4},{7,5},{8,10},{9,11},{10,... | collective-permute-start | bytes 393224 | tf_op jit(solution)/shard_map/ppermute | solution.py:322
  12.8 1.5 %collective-permute-start.2 = (bf16[4,64,256]{2,1,0:T(8,128)(2,1)S(1)}, bf16[4,64,256]{2,1,0:T(8,128)(2,1)S(1)}, u32[]{:S(2)}, u32[]{:S(2)}) collective-permute-start(bf16[4,64,256]{2,1,0:T(8,128)(2,1)S(1)} %get-tuple-element.29), channel_id=1, source_target_pairs={{0,1},{1,0},{2,3},{3,2},{4,5},{5,4},{6,7},{7,6},{8,9},{9,8},{10,11... | collective-permute-start | bytes 393224 | tf_op jit(solution)/shard_map/ppermute | solution.py:322
  14.3 0.0 collective-permute-done.10.refs_3_
  14.3 1.6 %collective-permute-start.3 = (bf16[4,64,256]{2,1,0:T(8,128)(2,1)S(1)}, bf16[4,64,256]{2,1,0:T(8,128)(2,1)S(1)}, u32[]{:S(2)}, u32[]{:S(2)}) collective-permute-start(bf16[4,64,256]{2,1,0:T(8,128)(2,1)S(1)} %get-tuple-element.30), channel_id=1, source_target_pairs={{0,3},{1,2},{2,1},{3,0},{4,7},{5,6},{6,5},{7,4},{8,11},{9,10},{10,... | collective-permute-start | bytes 393224 | tf_op jit(solution)/shard_map/ppermute | solution.py:322
  15.9 2.5 %filters.1.refs_1_ = bf16[4,1024,256]{2,1,0:T(8,128)(2,1)S(1)} custom-call(f32[4]{0:T(128)} %refs_0_.5, bf16[4,64,256]{2,1,0:T(8,128)(2,1)S(1)} %get-tuple-element.27.refs_1_.refs_2_), custom_call_target="tpu_custom_call" | custom-call | flops 1 | bytes 1 | tf_op jit(solution)/shard_map/filters/pallas_call | solution.py:358
  18.4 0.0 collective-permute-done.11.refs_4_
  18.4 0.0 collective-permute-done.12.refs_5_
  18.4 0.0 copy-done.1
  18.4 1.3 %columns.3 = (bf16[2,256,256]{2,1,0:T(8,128)(2,1)S(1)}, bf16[2,256,128]{2,1,0:T(8,128)(2,1)S(1)}, bf16[2,256,128]{2,1,0:T(8,128)(2,1)S(1)}) custom-call(bf16[1024,1024]{1,0:T(8,128)(2,1)S(1)} %copy-done.1, bf16[4,1024,256]{2,1,0:T(8,128)(2,1)S(1)} %filters.1.refs_1_, bf16[4,64,256]{2,1,0:T(8,128)(2,1)S(1)} %get-tuple-element.34.refs_2_, ...), custom_call_target="tpu_custom_call" | custom-call | flops 1 | bytes 1 | tf_op jit(solution)/shard_map/columns/pallas_call | solution.py:370
  19.7 1.6 %collective-permute-start.13 = (bf16[2,256,128]{2,1,0:T(8,128)(2,1)S(1)}, bf16[2,256,128]{2,1,0:T(8,128)(2,1)S(1)}, u32[]{:S(2)}, u32[]{:S(2)}) collective-permute-start(bf16[2,256,128]{2,1,0:T(8,128)(2,1)S(1)} %get-tuple-element.39.one), channel_id=1, source_target_pairs={{0,4},{1,5},{2,6},{3,7},{4,0},{5,1},{6,2},{7,3},{8,12},{9,13},{10,... | collective-permute-start | bytes 393224 | tf_op jit(solution)/shard_map/ppermute | solution.py:322
  21.4 0.5 collective-permute-start.16
  21.8 0.0 collective-permute-done.1.refs_3_
  21.8 0.0 collective-permute-done.2.refs_4_
  21.8 1.0 %collective-permute-done.3.refs_5_ = bf16[4,64,256]{2,1,0:T(8,128)(2,1)S(1)} collective-permute-done((bf16[4,64,256]{2,1,0:T(8,128)(2,1)S(1)}, bf16[4,64,256]{2,1,0:T(8,128)(2,1)S(1)}, u32[]{:S(2)}, u32[]{:S(2)}) %collective-permute-start.3) | collective-permute-done | bytes 131104 | tf_op jit(solution)/shard_map/ppermute | solution.py:322
  22.8 1.3 %columns.2 = (bf16[2,256,256]{2,1,0:T(8,128)(2,1)S(1)}, bf16[2,256,128]{2,1,0:T(8,128)(2,1)S(1)}, bf16[2,256,128]{2,1,0:T(8,128)(2,1)S(1)}) custom-call(bf16[1024,1024]{1,0:T(8,128)(2,1)S(1)} %copy-done.1, bf16[4,1024,256]{2,1,0:T(8,128)(2,1)S(1)} %filters.1.refs_1_, bf16[4,64,256]{2,1,0:T(8,128)(2,1)S(1)} %get-tuple-element.27.refs_1_.refs_2_, ...), custom_call_target="tpu_custom_call" | custom-call | flops 1 | bytes 1 | tf_op jit(solution)/shard_map/columns/pallas_call | solution.py:370
  24.1 1.8 %collective-permute-start.4 = (bf16[2,256,128]{2,1,0:T(8,128)(2,1)S(1)}, bf16[2,256,128]{2,1,0:T(8,128)(2,1)S(1)}, u32[]{:S(2)}, u32[]{:S(2)}) collective-permute-start(bf16[2,256,128]{2,1,0:T(8,128)(2,1)S(1)} %get-tuple-element.32.one), channel_id=1, source_target_pairs={{0,4},{1,5},{2,6},{3,7},{4,0},{5,1},{6,2},{7,3},{8,12},{9,13},{10,... | collective-permute-start | bytes 393224 | tf_op jit(solution)/shard_map/ppermute | solution.py:322
  25.9 0.3 collective-permute-start.7
  26.2 0.0 collective-permute-done.13.two
  26.3 0.1 collective-permute-start.14
  26.4 1.3 %collective-permute-done.16.two = bf16[2,256,128]{2,1,0:T(8,128)(2,1)S(1)} collective-permute-done((bf16[2,256,128]{2,1,0:T(8,128)(2,1)S(1)}, bf16[2,256,128]{2,1,0:T(8,128)(2,1)S(1)}, u32[]{:S(2)}, u32[]{:S(2)}) %collective-permute-start.16) | collective-permute-done | bytes 131104 | tf_op jit(solution)/shard_map/ppermute | solution.py:322
  27.7 0.1 collective-permute-start.17
  27.8 2.9 %collective-permute-done.4.two = bf16[2,256,128]{2,1,0:T(8,128)(2,1)S(1)} collective-permute-done((bf16[2,256,128]{2,1,0:T(8,128)(2,1)S(1)}, bf16[2,256,128]{2,1,0:T(8,128)(2,1)S(1)}, u32[]{:S(2)}, u32[]{:S(2)}) %collective-permute-start.4) | collective-permute-done | bytes 131104 | tf_op jit(solution)/shard_map/ppermute | solution.py:322
  30.7 0.1 collective-permute-start.5
  30.8 1.8 %collective-permute-done.7.two = bf16[2,256,128]{2,1,0:T(8,128)(2,1)S(1)} collective-permute-done((bf16[2,256,128]{2,1,0:T(8,128)(2,1)S(1)}, bf16[2,256,128]{2,1,0:T(8,128)(2,1)S(1)}, u32[]{:S(2)}, u32[]{:S(2)}) %collective-permute-start.7) | collective-permute-done | bytes 131104 | tf_op jit(solution)/shard_map/ppermute | solution.py:322
  32.6 0.1 collective-permute-start.8
  32.7 0.0 collective-permute-done.14.refs_1_.refs_6_
  32.7 3.2 %collective-permute-start.15 = (bf16[256,128]{1,0:T(8,128)(2,1)S(1)}, bf16[256,128]{1,0:T(8,128)(2,1)S(1)}, u32[]{:S(2)}, u32[]{:S(2)}) collective-permute-start(bf16[256,128]{1,0:T(8,128)(2,1)S(1)} %near.6), channel_id=1, source_target_pairs={{0,4},{1,5},{2,6},{3,7},{4,0},{5,1},{6,2},{7,3},{8,12},{9,13},{10,... | collective-permute-start | bytes 196616 | tf_op jit(solution)/shard_map/ppermute | solution.py:322
  35.9 0.0 collective-permute-done.17.refs_1_.refs_8_
  35.9 1.2 %collective-permute-start.18 = (bf16[256,128]{1,0:T(8,128)(2,1)S(1)}, bf16[256,128]{1,0:T(8,128)(2,1)S(1)}, u32[]{:S(2)}, u32[]{:S(2)}) collective-permute-start(bf16[256,128]{1,0:T(8,128)(2,1)S(1)} %near.7), channel_id=1, source_target_pairs={{0,4},{1,5},{2,6},{3,7},{4,0},{5,1},{6,2},{7,3},{8,12},{9,13},{10,... | collective-permute-start | bytes 196616 | tf_op jit(solution)/shard_map/ppermute | solution.py:322
  37.1 0.0 collective-permute-done.5.refs_1_
  37.1 0.0 copy-start.2
  37.1 0.0 copy-start.3
  37.1 0.0 copy-start.4
  37.1 2.2 %collective-permute-start.6 = (bf16[256,128]{1,0:T(8,128)(2,1)S(1)}, bf16[256,128]{1,0:T(8,128)(2,1)S(1)}, u32[]{:S(2)}, u32[]{:S(2)}) collective-permute-start(bf16[256,128]{1,0:T(8,128)(2,1)S(1)} %near.4), channel_id=1, source_target_pairs={{0,4},{1,5},{2,6},{3,7},{4,0},{5,1},{6,2},{7,3},{8,12},{9,13},{10,... | collective-permute-start | bytes 196616 | tf_op jit(solution)/shard_map/ppermute | solution.py:322
  39.4 0.0 collective-permute-done.8.refs_1_.refs_3_
  39.4 1.3 %collective-permute-start.9 = (bf16[256,128]{1,0:T(8,128)(2,1)S(1)}, bf16[256,128]{1,0:T(8,128)(2,1)S(1)}, u32[]{:S(2)}, u32[]{:S(2)}) collective-permute-start(bf16[256,128]{1,0:T(8,128)(2,1)S(1)} %near.5), channel_id=1, source_target_pairs={{0,4},{1,5},{2,6},{3,7},{4,0},{5,1},{6,2},{7,3},{8,12},{9,13},{10,... | collective-permute-start | bytes 196616 | tf_op jit(solution)/shard_map/ppermute | solution.py:322
  40.8 0.0 collective-permute-done.15.refs_7_
  40.8 0.0 collective-permute-done.18.refs_9_
  40.8 0.9 %collective-permute-done.6.refs_2_ = bf16[256,128]{1,0:T(8,128)(2,1)S(1)} collective-permute-done((bf16[256,128]{1,0:T(8,128)(2,1)S(1)}, bf16[256,128]{1,0:T(8,128)(2,1)S(1)}, u32[]{:S(2)}, u32[]{:S(2)}) %collective-permute-start.6) | collective-permute-done | bytes 65568 | tf_op jit(solution)/shard_map/ppermute | solution.py:322
  41.7 2.1 %collective-permute-done.9.refs_4_ = bf16[256,128]{1,0:T(8,128)(2,1)S(1)} collective-permute-done((bf16[256,128]{1,0:T(8,128)(2,1)S(1)}, bf16[256,128]{1,0:T(8,128)(2,1)S(1)}, u32[]{:S(2)}, u32[]{:S(2)}) %collective-permute-start.9) | collective-permute-done | bytes 65568 | tf_op jit(solution)/shard_map/ppermute | solution.py:322
  43.7 0.1 half.1
  43.9 1.2 %collective-permute-start.19 = (bf16[2,128,256]{2,1,0:T(8,128)(2,1)S(1)}, bf16[2,128,256]{2,1,0:T(8,128)(2,1)S(1)}, u32[]{:S(2)}, u32[]{:S(2)}) collective-permute-start(bf16[2,128,256]{2,1,0:T(8,128)(2,1)S(1)} %get-tuple-element.42), channel_id=1, source_target_pairs={{0,2},{1,3},{2,0},{3,1},{4,6},{5,7},{6,4},{7,5},{8,10},{9,11},{10,... | collective-permute-start | bytes 393224 | tf_op jit(solution)/shard_map/ppermute | solution.py:322
  45.1 1.5 %collective-permute-start.20 = (bf16[2,128,256]{2,1,0:T(8,128)(2,1)S(1)}, bf16[2,128,256]{2,1,0:T(8,128)(2,1)S(1)}, u32[]{:S(2)}, u32[]{:S(2)}) collective-permute-start(bf16[2,128,256]{2,1,0:T(8,128)(2,1)S(1)} %get-tuple-element.43), channel_id=1, source_target_pairs={{0,3},{1,2},{2,1},{3,0},{4,7},{5,6},{6,5},{7,4},{8,11},{9,10},{10,... | collective-permute-start | bytes 393224 | tf_op jit(solution)/shard_map/ppermute | solution.py:322
  46.5 0.9 %collective-permute-start.21 = (bf16[2,128,256]{2,1,0:T(8,128)(2,1)S(1)}, bf16[2,128,256]{2,1,0:T(8,128)(2,1)S(1)}, u32[]{:S(2)}, u32[]{:S(2)}) collective-permute-start(bf16[2,128,256]{2,1,0:T(8,128)(2,1)S(1)} %get-tuple-element.41.refs_1_), channel_id=1, source_target_pairs={{0,1},{1,0},{2,3},{3,2},{4,5},{5,4},{6,7},{7,6},{8,9},{9,8},{10,11... | collective-permute-start | bytes 393224 | tf_op jit(solution)/shard_map/ppermute | solution.py:322
  47.4 1.5 %collective-permute-done.19.refs_2_ = bf16[2,128,256]{2,1,0:T(8,128)(2,1)S(1)} collective-permute-done((bf16[2,128,256]{2,1,0:T(8,128)(2,1)S(1)}, bf16[2,128,256]{2,1,0:T(8,128)(2,1)S(1)}, u32[]{:S(2)}, u32[]{:S(2)}) %collective-permute-start.19) | collective-permute-done | bytes 131104 | tf_op jit(solution)/shard_map/ppermute | solution.py:322
  48.9 2.0 %collective-permute-done.20.refs_3_ = bf16[2,128,256]{2,1,0:T(8,128)(2,1)S(1)} collective-permute-done((bf16[2,128,256]{2,1,0:T(8,128)(2,1)S(1)}, bf16[2,128,256]{2,1,0:T(8,128)(2,1)S(1)}, u32[]{:S(2)}, u32[]{:S(2)}) %collective-permute-start.20) | collective-permute-done | bytes 131104 | tf_op jit(solution)/shard_map/ppermute | solution.py:322
  50.9 0.8 %collective-permute-done.21.refs_4_ = bf16[2,128,256]{2,1,0:T(8,128)(2,1)S(1)} collective-permute-done((bf16[2,128,256]{2,1,0:T(8,128)(2,1)S(1)}, bf16[2,128,256]{2,1,0:T(8,128)(2,1)S(1)}, u32[]{:S(2)}, u32[]{:S(2)}) %collective-permute-start.21) | collective-permute-done | bytes 131104 | tf_op jit(solution)/shard_map/ppermute | solution.py:322
  51.8 0.8 %phase.1 = (bf16[128,1024]{1,0:T(8,128)(2,1)S(1)}, bf16[128,1024]{1,0:T(8,128)(2,1)S(1)}) custom-call(bf16[1024,1024]{1,0:T(8,128)(2,1)S(1)} %copy-done.1, bf16[2,128,256]{2,1,0:T(8,128)(2,1)S(1)} %get-tuple-element.41.refs_1_, bf16[2,128,256]{2,1,0:T(8,128)(2,1)S(1)} %collective-permute-done.19.refs_2_, ...), custom_call_target="tpu_custom_call" | custom-call | flops 1 | bytes 1 | tf_op jit(solution)/shard_map/phase/pallas_call | solution.py:419
  52.5 0.1 collective-permute-start.22
  52.6 0.5 collective-permute-start.23
  53.1 1.0 %collective-permute-done.22.refs_4_ = bf16[128,1024]{1,0:T(8,128)(2,1)S(1)} collective-permute-done((bf16[128,1024]{1,0:T(8,128)(2,1)S(1)}, bf16[128,1024]{1,0:T(8,128)(2,1)S(1)}, u32[]{:S(2)}, u32[]{:S(2)}) %collective-permute-start.22) | collective-permute-done | bytes 262176 | tf_op jit(solution)/shard_map/ppermute | solution.py:322
  54.1 0.0 copy-done.2
  54.1 0.0 copy-done.3
  54.2 1.2 %recon.2 = (f32[128,512]{1,0:T(8,128)S(1)}, bf16[1024,512]{1,0:T(8,128)(2,1)S(1)}, bf16[128,128]{1,0:T(8,128)(2,1)S(1)}) custom-call(s32[1,4]{1,0:T(1,128)S(1)} %copy-done.3, s32[16]{0:T(128)S(1)} %copy-done.4, bf16[4,1024,512]{2,1,0:T(8,128)(2,1)S(1)} %copy-done.2, bf16[128,1024]{1,0:T(8,128)(2,1)S(1)} %get-tuple-element.44.refs_3_, ...), custom_call_target="tpu_custom_call" | custom-call | flops 1 | bytes 1 | tf_op jit(solution)/shard_map/recon/pallas_call | solution.py:431
  55.4 0.0 collective-permute-done.23.phase
  55.4 1.1 %recon.3 = bf16[128,512]{1,0:T(8,128)(2,1)} custom-call(bf16[1024,512]{1,0:T(8,128)(2,1)S(1)} %get-tuple-element.46.weights, bf16[128,1024]{1,0:T(8,128)(2,1)S(1)} %collective-permute-done.23.phase, f32[128,512]{1,0:T(8,128)S(1)} %get-tuple-element.47.before, bf16[128,128]{1,0:T(8,128)(2,1)S(1)} %get-tuple-element.48.select), custom_call_target="tpu_custom_call" | custom-call | flops 1 | bytes 1 | tf_op jit(solution)/shard_map/recon/pallas_call | solution.py:444
  (10 shorter events, 0.2 us)
Async XLA Ops:
  0.0 3.0 %collective-permute-start = (bf16[4,2,64,1024]{3,2,1,0:T(8,128)(2,1)}, bf16[4,2,64,1024]{3,2,1,0:T(8,128)(2,1)S(1)}, u32[]{:S(2)}, u32[]{:S(2)}) collective-permute-start(bf16[4,2,64,1024]{3,2,1,0:T(8,128)(2,1)} %bitcast.1), channel_id=1, source_target_pairs={{0,16},{1,17},{2,18},{3,19},{4,20},{5,21},{6,22},{7,23},{8,24},{9,... | collective-permute-start | bytes 3145736 | tf_op jit(solution)/shard_map/ppermute | solution.py:322
  3.0 1.6 %copy-start = (bf16[1024,1024]{1,0:T(8,128)(2,1)S(1)}, bf16[1024,1024]{1,0:T(8,128)(2,1)}, u32[]{:S(2)}) copy-start(bf16[1024,1024]{1,0:T(8,128)(2,1)} %constant.2.clone.refs_2_.refs_0_) | copy-start | bytes 6291460
  6.4 12.1 %copy-start.1 = (bf16[1024,1024]{1,0:T(8,128)(2,1)S(1)}, bf16[1024,1024]{1,0:T(8,128)(2,1)}, u32[]{:S(2)}) copy-start(bf16[1024,1024]{1,0:T(8,128)(2,1)} %constant.2.clone.refs_2_.refs_0_) | copy-start | bytes 6291460
  6.4 7.9 %collective-permute-start.10 = (bf16[4,64,256]{2,1,0:T(8,128)(2,1)S(1)}, bf16[4,64,256]{2,1,0:T(8,128)(2,1)S(1)}, u32[]{:S(2)}, u32[]{:S(2)}) collective-permute-start(bf16[4,64,256]{2,1,0:T(8,128)(2,1)S(1)} %get-tuple-element.35), channel_id=1, source_target_pairs={{0,2},{1,3},{2,0},{3,1},{4,6},{5,7},{6,4},{7,5},{8,10},{9,11},{10,... | collective-permute-start | bytes 393224 | tf_op jit(solution)/shard_map/ppermute | solution.py:322
  9.3 9.1 %collective-permute-start.11 = (bf16[4,64,256]{2,1,0:T(8,128)(2,1)S(1)}, bf16[4,64,256]{2,1,0:T(8,128)(2,1)S(1)}, u32[]{:S(2)}, u32[]{:S(2)}) collective-permute-start(bf16[4,64,256]{2,1,0:T(8,128)(2,1)S(1)} %get-tuple-element.36), channel_id=1, source_target_pairs={{0,1},{1,0},{2,3},{3,2},{4,5},{5,4},{6,7},{7,6},{8,9},{9,8},{10,11... | collective-permute-start | bytes 393224 | tf_op jit(solution)/shard_map/ppermute | solution.py:322
  10.8 7.6 %collective-permute-start.12 = (bf16[4,64,256]{2,1,0:T(8,128)(2,1)S(1)}, bf16[4,64,256]{2,1,0:T(8,128)(2,1)S(1)}, u32[]{:S(2)}, u32[]{:S(2)}) collective-permute-start(bf16[4,64,256]{2,1,0:T(8,128)(2,1)S(1)} %get-tuple-element.37), channel_id=1, source_target_pairs={{0,3},{1,2},{2,1},{3,0},{4,7},{5,6},{6,5},{7,4},{8,11},{9,10},{10,... | collective-permute-start | bytes 393224 | tf_op jit(solution)/shard_map/ppermute | solution.py:322
  10.9 11.0 %collective-permute-start.1 = (bf16[4,64,256]{2,1,0:T(8,128)(2,1)S(1)}, bf16[4,64,256]{2,1,0:T(8,128)(2,1)S(1)}, u32[]{:S(2)}, u32[]{:S(2)}) collective-permute-start(bf16[4,64,256]{2,1,0:T(8,128)(2,1)S(1)} %get-tuple-element.28), channel_id=1, source_target_pairs={{0,2},{1,3},{2,0},{3,1},{4,6},{5,7},{6,4},{7,5},{8,10},{9,11},{10,... | collective-permute-start | bytes 393224 | tf_op jit(solution)/shard_map/ppermute | solution.py:322
  12.8 9.0 %collective-permute-start.2 = (bf16[4,64,256]{2,1,0:T(8,128)(2,1)S(1)}, bf16[4,64,256]{2,1,0:T(8,128)(2,1)S(1)}, u32[]{:S(2)}, u32[]{:S(2)}) collective-permute-start(bf16[4,64,256]{2,1,0:T(8,128)(2,1)S(1)} %get-tuple-element.29), channel_id=1, source_target_pairs={{0,1},{1,0},{2,3},{3,2},{4,5},{5,4},{6,7},{7,6},{8,9},{9,8},{10,11... | collective-permute-start | bytes 393224 | tf_op jit(solution)/shard_map/ppermute | solution.py:322
  14.3 8.5 %collective-permute-start.3 = (bf16[4,64,256]{2,1,0:T(8,128)(2,1)S(1)}, bf16[4,64,256]{2,1,0:T(8,128)(2,1)S(1)}, u32[]{:S(2)}, u32[]{:S(2)}) collective-permute-start(bf16[4,64,256]{2,1,0:T(8,128)(2,1)S(1)} %get-tuple-element.30), channel_id=1, source_target_pairs={{0,3},{1,2},{2,1},{3,0},{4,7},{5,6},{6,5},{7,4},{8,11},{9,10},{10,... | collective-permute-start | bytes 393224 | tf_op jit(solution)/shard_map/ppermute | solution.py:322
  19.7 6.5 %collective-permute-start.13 = (bf16[2,256,128]{2,1,0:T(8,128)(2,1)S(1)}, bf16[2,256,128]{2,1,0:T(8,128)(2,1)S(1)}, u32[]{:S(2)}, u32[]{:S(2)}) collective-permute-start(bf16[2,256,128]{2,1,0:T(8,128)(2,1)S(1)} %get-tuple-element.39.one), channel_id=1, source_target_pairs={{0,4},{1,5},{2,6},{3,7},{4,0},{5,1},{6,2},{7,3},{8,12},{9,13},{10,... | collective-permute-start | bytes 393224 | tf_op jit(solution)/shard_map/ppermute | solution.py:322
  21.4 6.3 %collective-permute-start.16 = (bf16[2,256,128]{2,1,0:T(8,128)(2,1)S(1)}, bf16[2,256,128]{2,1,0:T(8,128)(2,1)S(1)}, u32[]{:S(2)}, u32[]{:S(2)}) collective-permute-start(bf16[2,256,128]{2,1,0:T(8,128)(2,1)S(1)} %get-tuple-element.40.one), channel_id=1, source_target_pairs={{0,4},{1,5},{2,6},{3,7},{4,0},{5,1},{6,2},{7,3},{8,12},{9,13},{10,... | collective-permute-start | bytes 393224 | tf_op jit(solution)/shard_map/ppermute | solution.py:322
  24.1 6.5 %collective-permute-start.4 = (bf16[2,256,128]{2,1,0:T(8,128)(2,1)S(1)}, bf16[2,256,128]{2,1,0:T(8,128)(2,1)S(1)}, u32[]{:S(2)}, u32[]{:S(2)}) collective-permute-start(bf16[2,256,128]{2,1,0:T(8,128)(2,1)S(1)} %get-tuple-element.32.one), channel_id=1, source_target_pairs={{0,4},{1,5},{2,6},{3,7},{4,0},{5,1},{6,2},{7,3},{8,12},{9,13},{10,... | collective-permute-start | bytes 393224 | tf_op jit(solution)/shard_map/ppermute | solution.py:322
  25.9 6.6 %collective-permute-start.7 = (bf16[2,256,128]{2,1,0:T(8,128)(2,1)S(1)}, bf16[2,256,128]{2,1,0:T(8,128)(2,1)S(1)}, u32[]{:S(2)}, u32[]{:S(2)}) collective-permute-start(bf16[2,256,128]{2,1,0:T(8,128)(2,1)S(1)} %get-tuple-element.33.one), channel_id=1, source_target_pairs={{0,4},{1,5},{2,6},{3,7},{4,0},{5,1},{6,2},{7,3},{8,12},{9,13},{10,... | collective-permute-start | bytes 393224 | tf_op jit(solution)/shard_map/ppermute | solution.py:322
  26.3 6.4 %collective-permute-start.14 = (bf16[2,256,128]{2,1,0:T(8,128)(2,1)S(1)}, bf16[2,256,128]{2,1,0:T(8,128)(2,1)S(1)}, u32[]{:S(2)}, u32[]{:S(2)}) collective-permute-start(bf16[2,256,128]{2,1,0:T(8,128)(2,1)S(1)} %joint.6), channel_id=1, source_target_pairs={{0,16},{1,17},{2,18},{3,19},{4,8},{5,9},{6,10},{7,11},{8,4},{9,5},... | collective-permute-start | bytes 393224 | tf_op jit(solution)/shard_map/ppermute | solution.py:322
  27.7 8.2 %collective-permute-start.17 = (bf16[2,256,128]{2,1,0:T(8,128)(2,1)S(1)}, bf16[2,256,128]{2,1,0:T(8,128)(2,1)S(1)}, u32[]{:S(2)}, u32[]{:S(2)}) collective-permute-start(bf16[2,256,128]{2,1,0:T(8,128)(2,1)S(1)} %joint.7), channel_id=1, source_target_pairs={{0,16},{1,17},{2,18},{3,19},{4,8},{5,9},{6,10},{7,11},{8,4},{9,5},... | collective-permute-start | bytes 393224 | tf_op jit(solution)/shard_map/ppermute | solution.py:322
  30.7 6.4 %collective-permute-start.5 = (bf16[2,256,128]{2,1,0:T(8,128)(2,1)S(1)}, bf16[2,256,128]{2,1,0:T(8,128)(2,1)S(1)}, u32[]{:S(2)}, u32[]{:S(2)}) collective-permute-start(bf16[2,256,128]{2,1,0:T(8,128)(2,1)S(1)} %joint.4), channel_id=1, source_target_pairs={{0,16},{1,17},{2,18},{3,19},{4,8},{5,9},{6,10},{7,11},{8,4},{9,5},... | collective-permute-start | bytes 393224 | tf_op jit(solution)/shard_map/ppermute | solution.py:322
  32.6 6.8 %collective-permute-start.8 = (bf16[2,256,128]{2,1,0:T(8,128)(2,1)S(1)}, bf16[2,256,128]{2,1,0:T(8,128)(2,1)S(1)}, u32[]{:S(2)}, u32[]{:S(2)}) collective-permute-start(bf16[2,256,128]{2,1,0:T(8,128)(2,1)S(1)} %joint.5), channel_id=1, source_target_pairs={{0,16},{1,17},{2,18},{3,19},{4,8},{5,9},{6,10},{7,11},{8,4},{9,5},... | collective-permute-start | bytes 393224 | tf_op jit(solution)/shard_map/ppermute | solution.py:322
  32.7 8.0 %collective-permute-start.15 = (bf16[256,128]{1,0:T(8,128)(2,1)S(1)}, bf16[256,128]{1,0:T(8,128)(2,1)S(1)}, u32[]{:S(2)}, u32[]{:S(2)}) collective-permute-start(bf16[256,128]{1,0:T(8,128)(2,1)S(1)} %near.6), channel_id=1, source_target_pairs={{0,4},{1,5},{2,6},{3,7},{4,0},{5,1},{6,2},{7,3},{8,12},{9,13},{10,... | collective-permute-start | bytes 196616 | tf_op jit(solution)/shard_map/ppermute | solution.py:322
  35.9 4.8 %collective-permute-start.18 = (bf16[256,128]{1,0:T(8,128)(2,1)S(1)}, bf16[256,128]{1,0:T(8,128)(2,1)S(1)}, u32[]{:S(2)}, u32[]{:S(2)}) collective-permute-start(bf16[256,128]{1,0:T(8,128)(2,1)S(1)} %near.7), channel_id=1, source_target_pairs={{0,4},{1,5},{2,6},{3,7},{4,0},{5,1},{6,2},{7,3},{8,12},{9,13},{10,... | collective-permute-start | bytes 196616 | tf_op jit(solution)/shard_map/ppermute | solution.py:322
  37.1 17.0 %copy-start.2 = (bf16[4,1024,512]{2,1,0:T(8,128)(2,1)S(1)}, bf16[4,1024,512]{2,1,0:T(8,128)(2,1)}, u32[]{:S(2)}) copy-start(bf16[4,1024,512]{2,1,0:T(8,128)(2,1)} %refs_2_.2) | copy-start | bytes 12582916
  37.1 17.0 %copy-start.3 = (s32[1,4]{1,0:T(1,128)S(1)}, s32[1,4]{1,0:T(1,128)}, u32[]{:S(2)}) copy-start(s32[1,4]{1,0:T(1,128)} %refs_0_.6) | copy-start | bytes 52
  37.1 17.0 %copy-start.4 = (s32[16]{0:T(128)S(1)}, s32[16]{0:T(128)}, u32[]{:S(2)}) copy-start(s32[16]{0:T(128)} %refs_1_.1) | copy-start | bytes 196
  37.1 4.5 %collective-permute-start.6 = (bf16[256,128]{1,0:T(8,128)(2,1)S(1)}, bf16[256,128]{1,0:T(8,128)(2,1)S(1)}, u32[]{:S(2)}, u32[]{:S(2)}) collective-permute-start(bf16[256,128]{1,0:T(8,128)(2,1)S(1)} %near.4), channel_id=1, source_target_pairs={{0,4},{1,5},{2,6},{3,7},{4,0},{5,1},{6,2},{7,3},{8,12},{9,13},{10,... | collective-permute-start | bytes 196616 | tf_op jit(solution)/shard_map/ppermute | solution.py:322
  39.4 4.3 %collective-permute-start.9 = (bf16[256,128]{1,0:T(8,128)(2,1)S(1)}, bf16[256,128]{1,0:T(8,128)(2,1)S(1)}, u32[]{:S(2)}, u32[]{:S(2)}) collective-permute-start(bf16[256,128]{1,0:T(8,128)(2,1)S(1)} %near.5), channel_id=1, source_target_pairs={{0,4},{1,5},{2,6},{3,7},{4,0},{5,1},{6,2},{7,3},{8,12},{9,13},{10,... | collective-permute-start | bytes 196616 | tf_op jit(solution)/shard_map/ppermute | solution.py:322
  43.9 5.0 %collective-permute-start.19 = (bf16[2,128,256]{2,1,0:T(8,128)(2,1)S(1)}, bf16[2,128,256]{2,1,0:T(8,128)(2,1)S(1)}, u32[]{:S(2)}, u32[]{:S(2)}) collective-permute-start(bf16[2,128,256]{2,1,0:T(8,128)(2,1)S(1)} %get-tuple-element.42), channel_id=1, source_target_pairs={{0,2},{1,3},{2,0},{3,1},{4,6},{5,7},{6,4},{7,5},{8,10},{9,11},{10,... | collective-permute-start | bytes 393224 | tf_op jit(solution)/shard_map/ppermute | solution.py:322
  45.1 5.9 %collective-permute-start.20 = (bf16[2,128,256]{2,1,0:T(8,128)(2,1)S(1)}, bf16[2,128,256]{2,1,0:T(8,128)(2,1)S(1)}, u32[]{:S(2)}, u32[]{:S(2)}) collective-permute-start(bf16[2,128,256]{2,1,0:T(8,128)(2,1)S(1)} %get-tuple-element.43), channel_id=1, source_target_pairs={{0,3},{1,2},{2,1},{3,0},{4,7},{5,6},{6,5},{7,4},{8,11},{9,10},{10,... | collective-permute-start | bytes 393224 | tf_op jit(solution)/shard_map/ppermute | solution.py:322
  46.5 5.3 %collective-permute-start.21 = (bf16[2,128,256]{2,1,0:T(8,128)(2,1)S(1)}, bf16[2,128,256]{2,1,0:T(8,128)(2,1)S(1)}, u32[]{:S(2)}, u32[]{:S(2)}) collective-permute-start(bf16[2,128,256]{2,1,0:T(8,128)(2,1)S(1)} %get-tuple-element.41.refs_1_), channel_id=1, source_target_pairs={{0,1},{1,0},{2,3},{3,2},{4,5},{5,4},{6,7},{7,6},{8,9},{9,8},{10,11... | collective-permute-start | bytes 393224 | tf_op jit(solution)/shard_map/ppermute | solution.py:322
  52.5 1.6 %collective-permute-start.22 = (bf16[128,1024]{1,0:T(8,128)(2,1)S(1)}, bf16[128,1024]{1,0:T(8,128)(2,1)S(1)}, u32[]{:S(2)}, u32[]{:S(2)}) collective-permute-start(bf16[128,1024]{1,0:T(8,128)(2,1)S(1)} %get-tuple-element.44.refs_3_), channel_id=1, source_target_pairs={{0,16},{1,17},{2,18},{3,19},{4,20},{5,21},{6,22},{7,23},{8,24},{9,... | collective-permute-start | bytes 786440 | tf_op jit(solution)/shard_map/ppermute | solution.py:322
  52.6 2.7 %collective-permute-start.23 = (bf16[128,1024]{1,0:T(8,128)(2,1)S(1)}, bf16[128,1024]{1,0:T(8,128)(2,1)S(1)}, u32[]{:S(2)}, u32[]{:S(2)}) collective-permute-start(bf16[128,1024]{1,0:T(8,128)(2,1)S(1)} %get-tuple-element.45.refs_5_), channel_id=1, source_target_pairs={{0,16},{1,17},{2,18},{3,19},{4,20},{5,21},{6,22},{7,23},{8,24},{9,... | collective-permute-start | bytes 786440 | tf_op jit(solution)/shard_map/ppermute | solution.py:322

commit v17 on v15

--- a/solution.py
+++ b/solution.py
@@ -12,6 +12,8 @@
 regularizer = 0.05
 bf16 = jnp.bfloat16
 f32 = jnp.float32
+send_order = (0, 2, 1, 3)
+tail_order = (0, 2, 3, 1)
 
 
 def hartley(length):
@@ -162,8 +164,8 @@
 
 
 def column_kernel(inner, outer, table, gain, *refs):
-    pieces = refs[:inner]
-    out, stack, total, spectrum = refs[inner:]
+    pieces = dict(zip(send_order, refs[:inner]))
+    *outs, stack, total, spectrum = refs[inner:]
     _, plane, spot = position(inner)
     dists, rows_dev, block = pieces[0].shape
     depth = inner * rows_dev
@@ -179,19 +181,26 @@
         else:
             total[...] += got
     spectrum[...] = total[...].astype(bf16)
-    value = jnp.dot(table[...], spectrum[...], preferred_element_type=f32)
-    out[...] = value.astype(bf16).reshape(outer, depth, block)
-
-
-def half_kernel(inner, half, other, mine):
+    for rel, out in enumerate(outs):
+        rows = pl.ds(pl.multiple_of((plane ^ rel) * depth, depth), depth)
+        value = jnp.dot(table[rows, :], spectrum[...], preferred_element_type=f32)
+        out[...] = value.astype(bf16)
+
+
+def half_kernel(inner, *refs):
+    parts, (other, mine) = refs[:-2], refs[-2:]
     _, _, spot = position(inner)
     capacity = mine.shape[0]
     for out, pair in ((mine, spot // 2), (other, 1 - spot // 2)):
-        out[...] = half[pl.ds(pl.multiple_of(pair * capacity, capacity), capacity), :]
+        rows = pl.ds(pl.multiple_of(pair * capacity, capacity), capacity)
+        got = parts[0][rows, :].astype(f32)
+        for part in parts[1:]:
+            got = got + part[rows, :].astype(f32)
+        out[...] = got.astype(bf16)
 
 
 def phase_kernel(inner, table, *refs):
-    pieces = refs[:inner]
+    pieces = dict(zip(tail_order, refs[:inner]))
     out, joined = refs[-2:]
     _, _, spot = position(inner)
     block = refs[0].shape[1]
@@ -282,14 +291,11 @@
     def to_spot(rel):
         return lambda c, r: (c, r ^ rel)
 
-    def spread(stays, along_x, along_y, diagonal):
-        first = sent(diagonal, to_spot(2))
-        other = first if along_y is diagonal else sent(along_y, to_spot(2))
-        return [stays, sent(along_x, to_spot(1)), other, sent(first, to_spot(1))]
-
-    def direct(stays, along_x, along_y, diagonal):
-        first = sent(along_y, to_spot(2))
-        return [stays, sent(along_x, to_spot(1)), first, sent(diagonal, to_spot(3))]
+    def spread(pieces, order):
+        return [sent(pieces[rel], to_spot(rel)) if rel else pieces[rel] for rel in order]
+
+    def to_plane(rel):
+        return lambda c, r: (c, (r // inner ^ rel) * inner + r % inner)
 
     partner = sent(holograms[0], to_other_core)
     gain = pl.pallas_call(
@@ -315,17 +321,16 @@
         name="row_spectra",
     )(from_hbm(holograms[0]), partner, table, gain)
     arrived = [
-        direct(*pieces[chunk * inner : (chunk + 1) * inner]) for chunk in range(own)
+        spread(pieces[chunk * inner : (chunk + 1) * inner], send_order) for chunk in range(own)
     ]
 
     sums = []
-    lines = [[z * inner + i for z in range(outer)] for i in range(inner)]
     for chunk in range(own):
-        parts = pl.pallas_call(
+        blocks = pl.pallas_call(
             lambda *refs: column_kernel(inner, outer, *refs),
-            out_shape=shaped(outer, depth, block),
+            out_shape=[shaped(depth, block)] * outer,
             in_specs=vmem(2 + inner),
-            out_specs=one_out,
+            out_specs=vmem(outer),
             scratch_shapes=[
                 pltpu.VMEM((dists, depth, block), bf16),
                 pltpu.VMEM((width, block), f32),
@@ -335,24 +340,20 @@
             cost_estimate=cheap,
             name="columns",
         )(table, gain, *arrived[chunk])
-        sums.append(
-            lax.psum_scatter(
-                parts, "rows", scatter_dimension=0, axis_index_groups=lines, tiled=False
-            )
-        )
+        sums.append([sent(blocks[rel], to_plane(rel)) if rel else blocks[0] for rel in (3, 2, 1, 0)])
 
     phases = []
     for chunk in range(own):
         second, first = pl.pallas_call(
             lambda *refs: half_kernel(inner, *refs),
             out_shape=[shaped(capacity, block)] * 2,
-            in_specs=vmem(1),
+            in_specs=vmem(outer),
             out_specs=vmem(2),
             compiler_params=params,
             cost_estimate=cheap,
             name="half",
-        )(sums[chunk])
-        pieces = spread(first, first, second, second)
+        )(*sums[chunk])
+        pieces = spread([first, first, second, second], tail_order)
         phase = pl.pallas_call(
             lambda *refs: phase_kernel(inner, *refs),
             out_shape=shaped(capacity, width),

time: 90.7 us -> 53.1 us (0.59)
  waiting for transfers between devices: 43.5 us -> 10.7 us
  starting transfers between devices: 15.7 us -> 31.7 us
  between operations: 13.5 us -> 0.15 us
  Pallas kernels: 14.3 us -> 10.4 us
  local copies, waits for them, and re-layouts: 3.42 us -> 0.01 us
    reduce_scatter x2 -> x0, waiting for transfers between devices: 28.5 us -> none  [plane_plan(): lax.psum_scatter(parts, 'rows', scatter_dimension=0, axis_index_groups=li...]
    ppermute x15 -> x21, starting transfers between devices: 15.7 us -> 31.7 us  [sent(): return lax.ppermute(value, ('dist', 'rows'), pairs)]
    ppermute x15 -> x21, waiting for transfers between devices: 14.9 us -> 10.7 us  [sent(): return lax.ppermute(value, ('dist', 'rows'), pairs)]
    pallas_call x2, Pallas kernels: 6.2 us -> 2.6 us  [plane_plan(): pl.pallas_call(lambda *refs: column_kernel(inner, outer, *refs), out_shap...]
    unnamed x16 -> x8, local copies, waits for them, and re-layouts: 3.42 us -> 0.01 us
  transfers between devices with their start and end apart: 17 -> 21, of which waited for: 11 -> 7; matrix products, arithmetic and copies ran while one was open for 0% -> 0% of each run, Pallas kernels for 9% -> 14%
where the time goes in v17:
time: 53.1 us; the launch traced here: 52.9 us
  starting transfers between devices  31.7 us (60%)
  waiting for transfers between devices  10.7 us (20%)
  Pallas kernels  10.4 us (20%)
    ppermute x21, starting transfers between devices, sent(): return lax.ppermute(value, ('dist', 'rows'), pairs)  31.7 us
    ppermute x21, waiting for transfers between devices, sent(): return lax.ppermute(value, ('dist', 'rows'), pairs)  10.7 us
    pallas_call x1, Pallas kernels, plane_plan(): pl.pallas_call(lambda *refs: filter_kernel(inner, dist_dev, *refs), out_s...  2.62 us
    pallas_call x2, Pallas kernels, plane_plan(): pl.pallas_call(lambda *refs: column_kernel(inner, outer, *refs), out_shap...  2.6 us
    pallas_call x1, Pallas kernels, plane_plan(): pl.pallas_call(lambda *refs: row_kernel(inner, *refs), out_shape=[shaped(...  1.83 us
    pallas_call x1, Pallas kernels, plane_plan(): pl.pallas_call(lambda *refs: recon_kernel(own, *refs), out_shape=[jax.Sha...  1.2 us
    pallas_call x1, Pallas kernels, plane_plan(): pl.pallas_call(recon_last_kernel, out_shape=shaped(capacity, pixels), in_...  1.12 us
  transfers between devices with their start and end apart: 21, of which 7 were waited for; matrix products, arithmetic and copies ran while one was open for 0% of the time, Pallas kernels for 14%

profile of v17, /device:TPU:0, one launch (start us, length us, event | category | flops | bytes accessed | tf_op | source)
XLA Modules:
  0.0 52.9 jit_solution(8807055983382271956)
XLA Ops:
  0.0 0.0 copy-start
  0.0 0.5 collective-permute-start
  0.5 2.6 %filters.1.refs_3_.refs_1_ = bf16[4,1024,256]{2,1,0:T(8,128)(2,1)S(1)} custom-call(f32[4]{0:T(128)} %refs_0_.6), custom_call_target="tpu_custom_call" | custom-call | flops 1 | bytes 1 | tf_op jit(solution)/shard_map/filters/pallas_call | solution.py:301
  3.1 0.0 collective-permute-done.refs_1_
  3.1 0.0 copy-done
  3.1 1.8 %row_spectra.1 = (bf16[4,64,256]{2,1,0:T(8,128)(2,1)S(1)}, bf16[4,64,256]{2,1,0:T(8,128)(2,1)S(1)}, bf16[4,64,256]{2,1,0:T(8,128)(2,1)S(1)}, bf16[4,64,256]{2,1,...) custom-call(bf16[4,2,64,1024]{3,2,1,0:T(8,128)(2,1)} %bitcast.2, ...), custom_call_target="tpu_custom_call" | custom-call | flops 1 | bytes 1 | tf_op jit(solution)/shard_map/row_spectra/pallas_call | solution.py:310
  4.9 2.8 %collective-permute-start.1 = (bf16[4,64,256]{2,1,0:T(8,128)(2,1)S(1)}, bf16[4,64,256]{2,1,0:T(8,128)(2,1)S(1)}, u32[]{:S(2)}, u32[]{:S(2)}) collective-permute-start(bf16[4,64,256]{2,1,0:T(8,128)(2,1)S(1)} %get-tuple-element.29), channel_id=1, source_target_pairs={{0,2},{1,3},{2,0},{3,1},{4,6},{5,7},{6,4},{7,5},{8,10},{9,11},{10,... | collective-permute-start | bytes 393224 | tf_op jit(solution)/shard_map/ppermute | solution.py:286
  7.7 1.5 %collective-permute-start.2 = (bf16[4,64,256]{2,1,0:T(8,128)(2,1)S(1)}, bf16[4,64,256]{2,1,0:T(8,128)(2,1)S(1)}, u32[]{:S(2)}, u32[]{:S(2)}) collective-permute-start(bf16[4,64,256]{2,1,0:T(8,128)(2,1)S(1)} %get-tuple-element.30), channel_id=1, source_target_pairs={{0,1},{1,0},{2,3},{3,2},{4,5},{5,4},{6,7},{7,6},{8,9},{9,8},{10,11... | collective-permute-start | bytes 393224 | tf_op jit(solution)/shard_map/ppermute | solution.py:286
  9.2 0.0 collective-permute-start.3
  9.3 1.9 %collective-permute-start.11 = (bf16[4,64,256]{2,1,0:T(8,128)(2,1)S(1)}, bf16[4,64,256]{2,1,0:T(8,128)(2,1)S(1)}, u32[]{:S(2)}, u32[]{:S(2)}) collective-permute-start(bf16[4,64,256]{2,1,0:T(8,128)(2,1)S(1)} %get-tuple-element.39), channel_id=1, source_target_pairs={{0,2},{1,3},{2,0},{3,1},{4,6},{5,7},{6,4},{7,5},{8,10},{9,11},{10,... | collective-permute-start | bytes 393224 | tf_op jit(solution)/shard_map/ppermute | solution.py:286
  11.2 1.5 %collective-permute-start.12 = (bf16[4,64,256]{2,1,0:T(8,128)(2,1)S(1)}, bf16[4,64,256]{2,1,0:T(8,128)(2,1)S(1)}, u32[]{:S(2)}, u32[]{:S(2)}) collective-permute-start(bf16[4,64,256]{2,1,0:T(8,128)(2,1)S(1)} %get-tuple-element.40), channel_id=1, source_target_pairs={{0,1},{1,0},{2,3},{3,2},{4,5},{5,4},{6,7},{7,6},{8,9},{9,8},{10,11... | collective-permute-start | bytes 393224 | tf_op jit(solution)/shard_map/ppermute | solution.py:286
  12.7 0.0 collective-permute-done.1.refs_3_
  12.7 1.6 %collective-permute-start.13 = (bf16[4,64,256]{2,1,0:T(8,128)(2,1)S(1)}, bf16[4,64,256]{2,1,0:T(8,128)(2,1)S(1)}, u32[]{:S(2)}, u32[]{:S(2)}) collective-permute-start(bf16[4,64,256]{2,1,0:T(8,128)(2,1)S(1)} %get-tuple-element.41), channel_id=1, source_target_pairs={{0,3},{1,2},{2,1},{3,0},{4,7},{5,6},{6,5},{7,4},{8,11},{9,10},{10,... | collective-permute-start | bytes 393224 | tf_op jit(solution)/shard_map/ppermute | solution.py:286
  14.3 0.0 collective-permute-done.2.refs_4_
  14.3 2.3 %collective-permute-done.3.refs_5_ = bf16[4,64,256]{2,1,0:T(8,128)(2,1)S(1)} collective-permute-done((bf16[4,64,256]{2,1,0:T(8,128)(2,1)S(1)}, bf16[4,64,256]{2,1,0:T(8,128)(2,1)S(1)}, u32[]{:S(2)}, u32[]{:S(2)}) %collective-permute-start.3) | collective-permute-done | bytes 131104 | tf_op jit(solution)/shard_map/ppermute | solution.py:286
  16.6 1.3 %columns.2 = (bf16[256,256]{1,0:T(8,128)(2,1)S(1)}, bf16[256,256]{1,0:T(8,128)(2,1)S(1)}, bf16[256,256]{1,0:T(8,128)(2,1)S(1)}, bf16[256,256]{1,0:T(8,128)(2,1)S(1)}) custom-call(bf16[1024,1024]{1,0:T(8,128)(2,1)S(1)} %copy-done, bf16[4,1024,256]{2,1,0:T(8,128)(2,1)S(1)} %filters.1.refs_3_.refs_1_, bf16[4,64,256]{2,1,0:T(8,128)(2,1)S(1)} %get-tuple-element.28.refs_2_, ...), custom_call_target="tpu_custom_call" | custom-call | flops 1 | bytes 1 | tf_op jit(solution)/shard_map/columns/pallas_call | solution.py:329
  17.9 3.7 %collective-permute-start.4 = (bf16[256,256]{1,0:T(8,128)(2,1)S(1)}, bf16[256,256]{1,0:T(8,128)(2,1)S(1)}, u32[]{:S(2)}, u32[]{:S(2)}) collective-permute-start(bf16[256,256]{1,0:T(8,128)(2,1)S(1)} %get-tuple-element.32), channel_id=1, source_target_pairs={{0,12},{1,13},{2,14},{3,15},{4,8},{5,9},{6,10},{7,11},{8,4},{9,5},... | collective-permute-start | bytes 393224 | tf_op jit(solution)/shard_map/ppermute | solution.py:286
  21.5 0.0 collective-permute-start.5
  21.6 0.0 collective-permute-done.11.refs_3_
  21.6 0.8 %collective-permute-start.6 = (bf16[256,256]{1,0:T(8,128)(2,1)S(1)}, bf16[256,256]{1,0:T(8,128)(2,1)S(1)}, u32[]{:S(2)}, u32[]{:S(2)}) collective-permute-start(bf16[256,256]{1,0:T(8,128)(2,1)S(1)} %get-tuple-element.34), channel_id=1, source_target_pairs={{0,4},{1,5},{2,6},{3,7},{4,0},{5,1},{6,2},{7,3},{8,12},{9,13},{10,... | collective-permute-start | bytes 393224 | tf_op jit(solution)/shard_map/ppermute | solution.py:286
  22.3 0.0 collective-permute-done.12.refs_4_
  22.3 0.0 collective-permute-done.13.refs_5_
  22.3 1.3 %columns.3 = (bf16[256,256]{1,0:T(8,128)(2,1)S(1)}, bf16[256,256]{1,0:T(8,128)(2,1)S(1)}, bf16[256,256]{1,0:T(8,128)(2,1)S(1)}, bf16[256,256]{1,0:T(8,128)(2,1)S(1)}) custom-call(bf16[1024,1024]{1,0:T(8,128)(2,1)S(1)} %copy-done, bf16[4,1024,256]{2,1,0:T(8,128)(2,1)S(1)} %filters.1.refs_3_.refs_1_, bf16[4,64,256]{2,1,0:T(8,128)(2,1)S(1)} %get-tuple-element.38.refs_2_, ...), custom_call_target="tpu_custom_call" | custom-call | flops 1 | bytes 1 | tf_op jit(solution)/shard_map/columns/pallas_call | solution.py:329
  23.6 3.7 %collective-permute-start.14 = (bf16[256,256]{1,0:T(8,128)(2,1)S(1)}, bf16[256,256]{1,0:T(8,128)(2,1)S(1)}, u32[]{:S(2)}, u32[]{:S(2)}) collective-permute-start(bf16[256,256]{1,0:T(8,128)(2,1)S(1)} %get-tuple-element.42), channel_id=1, source_target_pairs={{0,12},{1,13},{2,14},{3,15},{4,8},{5,9},{6,10},{7,11},{8,4},{9,5},... | collective-permute-start | bytes 393224 | tf_op jit(solution)/shard_map/ppermute | solution.py:286
  27.3 0.0 collective-permute-start.15
  27.3 0.0 collective-permute-done.4.refs_0_
  27.3 6.5 %collective-permute-start.16 = (bf16[256,256]{1,0:T(8,128)(2,1)S(1)}, bf16[256,256]{1,0:T(8,128)(2,1)S(1)}, u32[]{:S(2)}, u32[]{:S(2)}) collective-permute-start(bf16[256,256]{1,0:T(8,128)(2,1)S(1)} %get-tuple-element.44), channel_id=1, source_target_pairs={{0,4},{1,5},{2,6},{3,7},{4,0},{5,1},{6,2},{7,3},{8,12},{9,13},{10,... | collective-permute-start | bytes 393224 | tf_op jit(solution)/shard_map/ppermute | solution.py:286
  33.8 4.2 %collective-permute-done.5.refs_1_ = bf16[256,256]{1,0:T(8,128)(2,1)S(1)} collective-permute-done((bf16[256,256]{1,0:T(8,128)(2,1)S(1)}, bf16[256,256]{1,0:T(8,128)(2,1)S(1)}, u32[]{:S(2)}, u32[]{:S(2)}) %collective-permute-start.5) | collective-permute-done | bytes 131104 | tf_op jit(solution)/shard_map/ppermute | solution.py:286
  38.0 0.0 collective-permute-done.6.refs_2_
  38.0 0.1 half.2
  38.1 1.2 %collective-permute-start.9 = (bf16[128,256]{1,0:T(8,128)(2,1)S(1)}, bf16[128,256]{1,0:T(8,128)(2,1)S(1)}, u32[]{:S(2)}, u32[]{:S(2)}) collective-permute-start(bf16[128,256]{1,0:T(8,128)(2,1)S(1)} %get-tuple-element.36.refs_1_), channel_id=1, source_target_pairs={{0,1},{1,0},{2,3},{3,2},{4,5},{5,4},{6,7},{7,6},{8,9},{9,8},{10,11... | collective-permute-start | bytes 196616 | tf_op jit(solution)/shard_map/ppermute | solution.py:286
  39.3 1.5 %collective-permute-start.8 = (bf16[128,256]{1,0:T(8,128)(2,1)S(1)}, bf16[128,256]{1,0:T(8,128)(2,1)S(1)}, u32[]{:S(2)}, u32[]{:S(2)}) collective-permute-start(bf16[128,256]{1,0:T(8,128)(2,1)S(1)} %get-tuple-element.37), channel_id=1, source_target_pairs={{0,3},{1,2},{2,1},{3,0},{4,7},{5,6},{6,5},{7,4},{8,11},{9,10},{10,... | collective-permute-start | bytes 196616 | tf_op jit(solution)/shard_map/ppermute | solution.py:286
  40.8 0.0 collective-permute-done.14.refs_0_
  40.8 0.9 %collective-permute-start.7 = (bf16[128,256]{1,0:T(8,128)(2,1)S(1)}, bf16[128,256]{1,0:T(8,128)(2,1)S(1)}, u32[]{:S(2)}, u32[]{:S(2)}) collective-permute-start(bf16[128,256]{1,0:T(8,128)(2,1)S(1)} %get-tuple-element.37), channel_id=1, source_target_pairs={{0,2},{1,3},{2,0},{3,1},{4,6},{5,7},{6,4},{7,5},{8,10},{9,11},{10,... | collective-permute-start | bytes 196616 | tf_op jit(solution)/shard_map/ppermute | solution.py:286
  41.6 1.0 %collective-permute-done.15.refs_1_ = bf16[256,256]{1,0:T(8,128)(2,1)S(1)} collective-permute-done((bf16[256,256]{1,0:T(8,128)(2,1)S(1)}, bf16[256,256]{1,0:T(8,128)(2,1)S(1)}, u32[]{:S(2)}, u32[]{:S(2)}) %collective-permute-start.15) | collective-permute-done | bytes 131104 | tf_op jit(solution)/shard_map/ppermute | solution.py:286
  42.6 0.0 collective-permute-done.16.refs_2_
  42.6 0.1 half.3
  42.7 1.1 %collective-permute-start.19 = (bf16[128,256]{1,0:T(8,128)(2,1)S(1)}, bf16[128,256]{1,0:T(8,128)(2,1)S(1)}, u32[]{:S(2)}, u32[]{:S(2)}) collective-permute-start(bf16[128,256]{1,0:T(8,128)(2,1)S(1)} %get-tuple-element.46.refs_1_), channel_id=1, source_target_pairs={{0,1},{1,0},{2,3},{3,2},{4,5},{5,4},{6,7},{7,6},{8,9},{9,8},{10,11... | collective-permute-start | bytes 196616 | tf_op jit(solution)/shard_map/ppermute | solution.py:286
  43.8 0.0 copy-start.1
  43.8 0.0 copy-start.2
  43.8 0.0 copy-start.3
  43.8 1.5 %collective-permute-start.18 = (bf16[128,256]{1,0:T(8,128)(2,1)S(1)}, bf16[128,256]{1,0:T(8,128)(2,1)S(1)}, u32[]{:S(2)}, u32[]{:S(2)}) collective-permute-start(bf16[128,256]{1,0:T(8,128)(2,1)S(1)} %get-tuple-element.47), channel_id=1, source_target_pairs={{0,3},{1,2},{2,1},{3,0},{4,7},{5,6},{6,5},{7,4},{8,11},{9,10},{10,... | collective-permute-start | bytes 196616 | tf_op jit(solution)/shard_map/ppermute | solution.py:286
  45.4 0.0 collective-permute-done.9.refs_4_
  45.4 0.9 %collective-permute-start.17 = (bf16[128,256]{1,0:T(8,128)(2,1)S(1)}, bf16[128,256]{1,0:T(8,128)(2,1)S(1)}, u32[]{:S(2)}, u32[]{:S(2)}) collective-permute-start(bf16[128,256]{1,0:T(8,128)(2,1)S(1)} %get-tuple-element.47), channel_id=1, source_target_pairs={{0,2},{1,3},{2,0},{3,1},{4,6},{5,7},{6,4},{7,5},{8,10},{9,11},{10,... | collective-permute-start | bytes 196616 | tf_op jit(solution)/shard_map/ppermute | solution.py:286
  46.3 0.0 collective-permute-done.8.refs_3_
  46.3 0.0 collective-permute-done.7.refs_2_
  46.3 0.5 phase.2.refs_3_
  46.7 0.1 collective-permute-start.10
  46.8 0.8 %collective-permute-done.19.refs_4_ = bf16[128,256]{1,0:T(8,128)(2,1)S(1)} collective-permute-done((bf16[128,256]{1,0:T(8,128)(2,1)S(1)}, bf16[128,256]{1,0:T(8,128)(2,1)S(1)}, u32[]{:S(2)}, u32[]{:S(2)}) %collective-permute-start.19) | collective-permute-done | bytes 65568 | tf_op jit(solution)/shard_map/ppermute | solution.py:286
  47.6 1.4 %collective-permute-done.18.refs_3_ = bf16[128,256]{1,0:T(8,128)(2,1)S(1)} collective-permute-done((bf16[128,256]{1,0:T(8,128)(2,1)S(1)}, bf16[128,256]{1,0:T(8,128)(2,1)S(1)}, u32[]{:S(2)}, u32[]{:S(2)}) %collective-permute-start.18) | collective-permute-done | bytes 65568 | tf_op jit(solution)/shard_map/ppermute | solution.py:286
  49.0 0.7 %collective-permute-done.17.refs_2_ = bf16[128,256]{1,0:T(8,128)(2,1)S(1)} collective-permute-done((bf16[128,256]{1,0:T(8,128)(2,1)S(1)}, bf16[128,256]{1,0:T(8,128)(2,1)S(1)}, u32[]{:S(2)}, u32[]{:S(2)}) %collective-permute-start.17) | collective-permute-done | bytes 65568 | tf_op jit(solution)/shard_map/ppermute | solution.py:286
  49.7 0.5 phase.3.refs_5_
  50.2 0.1 collective-permute-start.20
  50.2 0.0 collective-permute-done.10.refs_4_
  50.3 0.0 copy-done.1
  50.3 0.0 copy-done.2
  50.3 0.0 copy-done.3
  50.3 1.2 %recon.2 = (f32[128,512]{1,0:T(8,128)S(1)}, bf16[1024,512]{1,0:T(8,128)(2,1)S(1)}, bf16[128,128]{1,0:T(8,128)(2,1)S(1)}) custom-call(s32[1,4]{1,0:T(1,128)S(1)} %copy-done.2, s32[16]{0:T(128)S(1)} %copy-done.3, bf16[4,1024,512]{2,1,0:T(8,128)(2,1)S(1)} %copy-done.1, bf16[128,1024]{1,0:T(8,128)(2,1)S(1)} %phase.2.refs_3_, ...), custom_call_target="tpu_custom_call" | custom-call | flops 1 | bytes 1 | tf_op jit(solution)/shard_map/recon/pallas_call | solution.py:369
  51.5 0.3 collective-permute-done.20.phase
  51.8 1.1 %recon.3 = bf16[128,512]{1,0:T(8,128)(2,1)} custom-call(bf16[1024,512]{1,0:T(8,128)(2,1)S(1)} %get-tuple-element.48.weights, bf16[128,1024]{1,0:T(8,128)(2,1)S(1)} %collective-permute-done.20.phase, f32[128,512]{1,0:T(8,128)S(1)} %get-tuple-element.49.before, bf16[128,128]{1,0:T(8,128)(2,1)S(1)} %get-tuple-element.50.select), custom_call_target="tpu_custom_call" | custom-call | flops 1 | bytes 1 | tf_op jit(solution)/shard_map/recon/pallas_call | solution.py:382
Async XLA Ops:
  0.0 3.1 %copy-start = (bf16[1024,1024]{1,0:T(8,128)(2,1)S(1)}, bf16[1024,1024]{1,0:T(8,128)(2,1)}, u32[]{:S(2)}) copy-start(bf16[1024,1024]{1,0:T(8,128)(2,1)} %constant.2.clone.refs_2_.refs_0_) | copy-start | bytes 6291460
  0.0 3.1 %collective-permute-start = (bf16[4,2,64,1024]{3,2,1,0:T(8,128)(2,1)}, bf16[4,2,64,1024]{3,2,1,0:T(8,128)(2,1)S(1)}, u32[]{:S(2)}, u32[]{:S(2)}) collective-permute-start(bf16[4,2,64,1024]{3,2,1,0:T(8,128)(2,1)} %bitcast.1), channel_id=1, source_target_pairs={{0,16},{1,17},{2,18},{3,19},{4,20},{5,21},{6,22},{7,23},{8,24},{9,... | collective-permute-start | bytes 3145736 | tf_op jit(solution)/shard_map/ppermute | solution.py:286
  4.9 7.8 %collective-permute-start.1 = (bf16[4,64,256]{2,1,0:T(8,128)(2,1)S(1)}, bf16[4,64,256]{2,1,0:T(8,128)(2,1)S(1)}, u32[]{:S(2)}, u32[]{:S(2)}) collective-permute-start(bf16[4,64,256]{2,1,0:T(8,128)(2,1)S(1)} %get-tuple-element.29), channel_id=1, source_target_pairs={{0,2},{1,3},{2,0},{3,1},{4,6},{5,7},{6,4},{7,5},{8,10},{9,11},{10,... | collective-permute-start | bytes 393224 | tf_op jit(solution)/shard_map/ppermute | solution.py:286
  7.7 6.6 %collective-permute-start.2 = (bf16[4,64,256]{2,1,0:T(8,128)(2,1)S(1)}, bf16[4,64,256]{2,1,0:T(8,128)(2,1)S(1)}, u32[]{:S(2)}, u32[]{:S(2)}) collective-permute-start(bf16[4,64,256]{2,1,0:T(8,128)(2,1)S(1)} %get-tuple-element.30), channel_id=1, source_target_pairs={{0,1},{1,0},{2,3},{3,2},{4,5},{5,4},{6,7},{7,6},{8,9},{9,8},{10,11... | collective-permute-start | bytes 393224 | tf_op jit(solution)/shard_map/ppermute | solution.py:286
  9.2 7.4 %collective-permute-start.3 = (bf16[4,64,256]{2,1,0:T(8,128)(2,1)S(1)}, bf16[4,64,256]{2,1,0:T(8,128)(2,1)S(1)}, u32[]{:S(2)}, u32[]{:S(2)}) collective-permute-start(bf16[4,64,256]{2,1,0:T(8,128)(2,1)S(1)} %get-tuple-element.31), channel_id=1, source_target_pairs={{0,3},{1,2},{2,1},{3,0},{4,7},{5,6},{6,5},{7,4},{8,11},{9,10},{10,... | collective-permute-start | bytes 393224 | tf_op jit(solution)/shard_map/ppermute | solution.py:286
  9.3 12.3 %collective-permute-start.11 = (bf16[4,64,256]{2,1,0:T(8,128)(2,1)S(1)}, bf16[4,64,256]{2,1,0:T(8,128)(2,1)S(1)}, u32[]{:S(2)}, u32[]{:S(2)}) collective-permute-start(bf16[4,64,256]{2,1,0:T(8,128)(2,1)S(1)} %get-tuple-element.39), channel_id=1, source_target_pairs={{0,2},{1,3},{2,0},{3,1},{4,6},{5,7},{6,4},{7,5},{8,10},{9,11},{10,... | collective-permute-start | bytes 393224 | tf_op jit(solution)/shard_map/ppermute | solution.py:286
  11.2 11.1 %collective-permute-start.12 = (bf16[4,64,256]{2,1,0:T(8,128)(2,1)S(1)}, bf16[4,64,256]{2,1,0:T(8,128)(2,1)S(1)}, u32[]{:S(2)}, u32[]{:S(2)}) collective-permute-start(bf16[4,64,256]{2,1,0:T(8,128)(2,1)S(1)} %get-tuple-element.40), channel_id=1, source_target_pairs={{0,1},{1,0},{2,3},{3,2},{4,5},{5,4},{6,7},{7,6},{8,9},{9,8},{10,11... | collective-permute-start | bytes 393224 | tf_op jit(solution)/shard_map/ppermute | solution.py:286
  12.7 9.6 %collective-permute-start.13 = (bf16[4,64,256]{2,1,0:T(8,128)(2,1)S(1)}, bf16[4,64,256]{2,1,0:T(8,128)(2,1)S(1)}, u32[]{:S(2)}, u32[]{:S(2)}) collective-permute-start(bf16[4,64,256]{2,1,0:T(8,128)(2,1)S(1)} %get-tuple-element.41), channel_id=1, source_target_pairs={{0,3},{1,2},{2,1},{3,0},{4,7},{5,6},{6,5},{7,4},{8,11},{9,10},{10,... | collective-permute-start | bytes 393224 | tf_op jit(solution)/shard_map/ppermute | solution.py:286
  17.9 9.5 %collective-permute-start.4 = (bf16[256,256]{1,0:T(8,128)(2,1)S(1)}, bf16[256,256]{1,0:T(8,128)(2,1)S(1)}, u32[]{:S(2)}, u32[]{:S(2)}) collective-permute-start(bf16[256,256]{1,0:T(8,128)(2,1)S(1)} %get-tuple-element.32), channel_id=1, source_target_pairs={{0,12},{1,13},{2,14},{3,15},{4,8},{5,9},{6,10},{7,11},{8,4},{9,5},... | collective-permute-start | bytes 393224 | tf_op jit(solution)/shard_map/ppermute | solution.py:286
  21.5 16.5 %collective-permute-start.5 = (bf16[256,256]{1,0:T(8,128)(2,1)S(1)}, bf16[256,256]{1,0:T(8,128)(2,1)S(1)}, u32[]{:S(2)}, u32[]{:S(2)}) collective-permute-start(bf16[256,256]{1,0:T(8,128)(2,1)S(1)} %get-tuple-element.33), channel_id=1, source_target_pairs={{0,8},{1,9},{2,10},{3,11},{4,12},{5,13},{6,14},{7,15},{8,0},{9,1},... | collective-permute-start | bytes 393224 | tf_op jit(solution)/shard_map/ppermute | solution.py:286
  21.6 16.5 %collective-permute-start.6 = (bf16[256,256]{1,0:T(8,128)(2,1)S(1)}, bf16[256,256]{1,0:T(8,128)(2,1)S(1)}, u32[]{:S(2)}, u32[]{:S(2)}) collective-permute-start(bf16[256,256]{1,0:T(8,128)(2,1)S(1)} %get-tuple-element.34), channel_id=1, source_target_pairs={{0,4},{1,5},{2,6},{3,7},{4,0},{5,1},{6,2},{7,3},{8,12},{9,13},{10,... | collective-permute-start | bytes 393224 | tf_op jit(solution)/shard_map/ppermute | solution.py:286
  23.6 17.1 %collective-permute-start.14 = (bf16[256,256]{1,0:T(8,128)(2,1)S(1)}, bf16[256,256]{1,0:T(8,128)(2,1)S(1)}, u32[]{:S(2)}, u32[]{:S(2)}) collective-permute-start(bf16[256,256]{1,0:T(8,128)(2,1)S(1)} %get-tuple-element.42), channel_id=1, source_target_pairs={{0,12},{1,13},{2,14},{3,15},{4,8},{5,9},{6,10},{7,11},{8,4},{9,5},... | collective-permute-start | bytes 393224 | tf_op jit(solution)/shard_map/ppermute | solution.py:286
  27.3 15.3 %collective-permute-start.15 = (bf16[256,256]{1,0:T(8,128)(2,1)S(1)}, bf16[256,256]{1,0:T(8,128)(2,1)S(1)}, u32[]{:S(2)}, u32[]{:S(2)}) collective-permute-start(bf16[256,256]{1,0:T(8,128)(2,1)S(1)} %get-tuple-element.43), channel_id=1, source_target_pairs={{0,8},{1,9},{2,10},{3,11},{4,12},{5,13},{6,14},{7,15},{8,0},{9,1},... | collective-permute-start | bytes 393224 | tf_op jit(solution)/shard_map/ppermute | solution.py:286
  27.3 15.3 %collective-permute-start.16 = (bf16[256,256]{1,0:T(8,128)(2,1)S(1)}, bf16[256,256]{1,0:T(8,128)(2,1)S(1)}, u32[]{:S(2)}, u32[]{:S(2)}) collective-permute-start(bf16[256,256]{1,0:T(8,128)(2,1)S(1)} %get-tuple-element.44), channel_id=1, source_target_pairs={{0,4},{1,5},{2,6},{3,7},{4,0},{5,1},{6,2},{7,3},{8,12},{9,13},{10,... | collective-permute-start | bytes 393224 | tf_op jit(solution)/shard_map/ppermute | solution.py:286
  38.1 7.3 %collective-permute-start.9 = (bf16[128,256]{1,0:T(8,128)(2,1)S(1)}, bf16[128,256]{1,0:T(8,128)(2,1)S(1)}, u32[]{:S(2)}, u32[]{:S(2)}) collective-permute-start(bf16[128,256]{1,0:T(8,128)(2,1)S(1)} %get-tuple-element.36.refs_1_), channel_id=1, source_target_pairs={{0,1},{1,0},{2,3},{3,2},{4,5},{5,4},{6,7},{7,6},{8,9},{9,8},{10,11... | collective-permute-start | bytes 196616 | tf_op jit(solution)/shard_map/ppermute | solution.py:286
  39.3 7.0 %collective-permute-start.8 = (bf16[128,256]{1,0:T(8,128)(2,1)S(1)}, bf16[128,256]{1,0:T(8,128)(2,1)S(1)}, u32[]{:S(2)}, u32[]{:S(2)}) collective-permute-start(bf16[128,256]{1,0:T(8,128)(2,1)S(1)} %get-tuple-element.37), channel_id=1, source_target_pairs={{0,3},{1,2},{2,1},{3,0},{4,7},{5,6},{6,5},{7,4},{8,11},{9,10},{10,... | collective-permute-start | bytes 196616 | tf_op jit(solution)/shard_map/ppermute | solution.py:286
  40.8 5.5 %collective-permute-start.7 = (bf16[128,256]{1,0:T(8,128)(2,1)S(1)}, bf16[128,256]{1,0:T(8,128)(2,1)S(1)}, u32[]{:S(2)}, u32[]{:S(2)}) collective-permute-start(bf16[128,256]{1,0:T(8,128)(2,1)S(1)} %get-tuple-element.37), channel_id=1, source_target_pairs={{0,2},{1,3},{2,0},{3,1},{4,6},{5,7},{6,4},{7,5},{8,10},{9,11},{10,... | collective-permute-start | bytes 196616 | tf_op jit(solution)/shard_map/ppermute | solution.py:286
  42.7 4.9 %collective-permute-start.19 = (bf16[128,256]{1,0:T(8,128)(2,1)S(1)}, bf16[128,256]{1,0:T(8,128)(2,1)S(1)}, u32[]{:S(2)}, u32[]{:S(2)}) collective-permute-start(bf16[128,256]{1,0:T(8,128)(2,1)S(1)} %get-tuple-element.46.refs_1_), channel_id=1, source_target_pairs={{0,1},{1,0},{2,3},{3,2},{4,5},{5,4},{6,7},{7,6},{8,9},{9,8},{10,11... | collective-permute-start | bytes 196616 | tf_op jit(solution)/shard_map/ppermute | solution.py:286
  43.8 6.4 %copy-start.1 = (bf16[4,1024,512]{2,1,0:T(8,128)(2,1)S(1)}, bf16[4,1024,512]{2,1,0:T(8,128)(2,1)}, u32[]{:S(2)}) copy-start(bf16[4,1024,512]{2,1,0:T(8,128)(2,1)} %refs_2_.2) | copy-start | bytes 12582916
  43.8 6.4 %copy-start.2 = (s32[1,4]{1,0:T(1,128)S(1)}, s32[1,4]{1,0:T(1,128)}, u32[]{:S(2)}) copy-start(s32[1,4]{1,0:T(1,128)} %refs_0_.7) | copy-start | bytes 52
  43.8 6.4 %copy-start.3 = (s32[16]{0:T(128)S(1)}, s32[16]{0:T(128)}, u32[]{:S(2)}) copy-start(s32[16]{0:T(128)} %refs_1_.1) | copy-start | bytes 196
  43.8 5.2 %collective-permute-start.18 = (bf16[128,256]{1,0:T(8,128)(2,1)S(1)}, bf16[128,256]{1,0:T(8,128)(2,1)S(1)}, u32[]{:S(2)}, u32[]{:S(2)}) collective-permute-start(bf16[128,256]{1,0:T(8,128)(2,1)S(1)} %get-tuple-element.47), channel_id=1, source_target_pairs={{0,3},{1,2},{2,1},{3,0},{4,7},{5,6},{6,5},{7,4},{8,11},{9,10},{10,... | collective-permute-start | bytes 196616 | tf_op jit(solution)/shard_map/ppermute | solution.py:286
  45.4 4.3 %collective-permute-start.17 = (bf16[128,256]{1,0:T(8,128)(2,1)S(1)}, bf16[128,256]{1,0:T(8,128)(2,1)S(1)}, u32[]{:S(2)}, u32[]{:S(2)}) collective-permute-start(bf16[128,256]{1,0:T(8,128)(2,1)S(1)} %get-tuple-element.47), channel_id=1, source_target_pairs={{0,2},{1,3},{2,0},{3,1},{4,6},{5,7},{6,4},{7,5},{8,10},{9,11},{10,... | collective-permute-start | bytes 196616 | tf_op jit(solution)/shard_map/ppermute | solution.py:286
  46.7 3.5 %collective-permute-start.10 = (bf16[128,1024]{1,0:T(8,128)(2,1)S(1)}, bf16[128,1024]{1,0:T(8,128)(2,1)S(1)}, u32[]{:S(2)}, u32[]{:S(2)}) collective-permute-start(bf16[128,1024]{1,0:T(8,128)(2,1)S(1)} %phase.2.refs_3_), channel_id=1, source_target_pairs={{0,16},{1,17},{2,18},{3,19},{4,20},{5,21},{6,22},{7,23},{8,24},{9,... | collective-permute-start | bytes 786440 | tf_op jit(solution)/shard_map/ppermute | solution.py:286
  50.2 1.6 %collective-permute-start.20 = (bf16[128,1024]{1,0:T(8,128)(2,1)S(1)}, bf16[128,1024]{1,0:T(8,128)(2,1)S(1)}, u32[]{:S(2)}, u32[]{:S(2)}) collective-permute-start(bf16[128,1024]{1,0:T(8,128)(2,1)S(1)} %phase.3.refs_5_), channel_id=1, source_target_pairs={{0,16},{1,17},{2,18},{3,19},{4,20},{5,21},{6,22},{7,23},{8,24},{9,... | collective-permute-start | bytes 786440 | tf_op jit(solution)/shard_map/ppermute | solution.py:286

commit v18 on v17

--- a/solution.py
+++ b/solution.py
@@ -181,21 +181,31 @@
         else:
             total[...] += got
     spectrum[...] = total[...].astype(bf16)
-    for rel, out in enumerate(outs):
+    middle = (plane == 1) | (plane == 2)
+    first = jnp.where(middle, 1, 3)
+    for rel, out in zip((0, first, 4 - first, 2), outs):
         rows = pl.ds(pl.multiple_of((plane ^ rel) * depth, depth), depth)
         value = jnp.dot(table[rows, :], spectrum[...], preferred_element_type=f32)
         out[...] = value.astype(bf16)
 
 
-def half_kernel(inner, *refs):
-    parts, (other, mine) = refs[:-2], refs[-2:]
-    _, _, spot = position(inner)
+def far_kernel(inner, *refs):
+    ours, got, out = refs[-3:]
+    _, plane, _ = position(inner)
+    middle = (plane == 1) | (plane == 2)
+    more = jnp.where(middle, got[...].astype(f32), 0.0)
+    out[...] = (ours[...].astype(f32) + more).astype(bf16)
+
+
+def half_kernel(inner, ours, far, near, next_near, across, other, mine):
+    _, plane, spot = position(inner)
+    middle = (plane == 1) | (plane == 2)
     capacity = mine.shape[0]
     for out, pair in ((mine, spot // 2), (other, 1 - spot // 2)):
         rows = pl.ds(pl.multiple_of(pair * capacity, capacity), capacity)
-        got = parts[0][rows, :].astype(f32)
-        for part in parts[1:]:
-            got = got + part[rows, :].astype(f32)
+        inside = next_near[rows, :].astype(f32) + across[rows, :].astype(f32)
+        more = jnp.where(middle, inside, near[rows, :].astype(f32))
+        got = ours[rows, :].astype(f32) + far[rows, :].astype(f32) + more
         out[...] = got.astype(bf16)
 
 
@@ -296,6 +306,10 @@
 
     def to_plane(rel):
         return lambda c, r: (c, (r // inner ^ rel) * inner + r % inner)
+
+    def to_middle(c, r):
+        z = r // inner
+        return (c, (3 - z) * inner + r % inner) if z in (1, 2) else (c ^ 1, r)
 
     partner = sent(holograms[0], to_other_core)
     gain = pl.pallas_call(
@@ -340,14 +354,27 @@
             cost_estimate=cheap,
             name="columns",
         )(table, gain, *arrived[chunk])
-        sums.append([sent(blocks[rel], to_plane(rel)) if rel else blocks[0] for rel in (3, 2, 1, 0)])
+        ours, first, second, third = blocks
+        near = sent(first, to_plane(1))
+        earlier = sums[-1][3:] if sums else []
+        message = pl.pallas_call(
+            lambda *refs: far_kernel(inner, *refs),
+            out_shape=shaped(depth, block),
+            in_specs=unread(len(earlier)) + vmem(2),
+            out_specs=one_out,
+            compiler_params=params,
+            cost_estimate=cheap,
+            name="far",
+        )(*earlier, third, near)
+        far = sent(message, to_plane(2))
+        sums.append([ours, far, near, sent(second, to_plane(1)), sent(second, to_middle)])
 
     phases = []
     for chunk in range(own):
         second, first = pl.pallas_call(
             lambda *refs: half_kernel(inner, *refs),
             out_shape=[shaped(capacity, block)] * 2,
-            in_specs=vmem(outer),
+            in_specs=vmem(5),
             out_specs=vmem(2),
             compiler_params=params,
             cost_estimate=cheap,

time: 53.1 us -> 51.8 us (0.976)
  starting transfers between devices: 31.7 us -> 28.8 us
  waiting for transfers between devices: 10.7 us -> 12 us
    ppermute x21 -> x23, starting transfers between devices: 31.7 us -> 28.8 us  [sent(): return lax.ppermute(value, ('dist', 'rows'), pairs)]
    ppermute x21 -> x23, waiting for transfers between devices: 10.7 us -> 12 us  [sent(): return lax.ppermute(value, ('dist', 'rows'), pairs)]
  transfers between devices with their start and end apart: 21 -> 23, of which waited for: 7 -> 8; matrix products, arithmetic and copies ran while one was open for 0% -> 0% of each run, Pallas kernels for 14% -> 15%
where the time goes in v18:
time: 51.8 us; the launch traced here: 51.6 us
  starting transfers between devices  28.8 us (56%)
  waiting for transfers between devices  12 us (23%)
  Pallas kernels  10.6 us (20%)
    ppermute x23, starting transfers between devices, sent(): return lax.ppermute(value, ('dist', 'rows'), pairs)  28.8 us
    ppermute x23, waiting for transfers between devices, sent(): return lax.ppermute(value, ('dist', 'rows'), pairs)  12 us
    pallas_call x1, Pallas kernels, plane_plan(): pl.pallas_call(lambda *refs: filter_kernel(inner, dist_dev, *refs), out_s...  2.62 us
    pallas_call x2, Pallas kernels, plane_plan(): pl.pallas_call(lambda *refs: column_kernel(inner, outer, *refs), out_shap...  2.59 us
    pallas_call x1, Pallas kernels, plane_plan(): pl.pallas_call(lambda *refs: row_kernel(inner, *refs), out_shape=[shaped(...  1.83 us
    pallas_call x1, Pallas kernels, plane_plan(): pl.pallas_call(lambda *refs: recon_kernel(own, *refs), out_shape=[jax.Sha...  1.2 us
    pallas_call x1, Pallas kernels, plane_plan(): pl.pallas_call(recon_last_kernel, out_shape=shaped(capacity, pixels), in_...  1.12 us
  transfers between devices with their start and end apart: 23, of which 8 were waited for; matrix products, arithmetic and copies ran while one was open for 0% of the time, Pallas kernels for 15%

profile of v18, /device:TPU:0, one launch (start us, length us, event | category | flops | bytes accessed | tf_op | source)
XLA Modules:
  0.0 51.6 jit_solution(7877046050185087756)
XLA Ops:
  0.0 0.0 copy-start
  0.0 0.5 collective-permute-start
  0.5 2.6 %filters.1.refs_3_.refs_1_ = bf16[4,1024,256]{2,1,0:T(8,128)(2,1)S(1)} custom-call(f32[4]{0:T(128)} %refs_0_.6), custom_call_target="tpu_custom_call" | custom-call | flops 1 | bytes 1 | tf_op jit(solution)/shard_map/filters/pallas_call | solution.py:315
  3.1 0.0 collective-permute-done.refs_1_
  3.1 0.0 copy-done
  3.1 1.8 %row_spectra.1 = (bf16[4,64,256]{2,1,0:T(8,128)(2,1)S(1)}, bf16[4,64,256]{2,1,0:T(8,128)(2,1)S(1)}, bf16[4,64,256]{2,1,0:T(8,128)(2,1)S(1)}, bf16[4,64,256]{2,1,...) custom-call(bf16[4,2,64,1024]{3,2,1,0:T(8,128)(2,1)} %bitcast.2, ...), custom_call_target="tpu_custom_call" | custom-call | flops 1 | bytes 1 | tf_op jit(solution)/shard_map/row_spectra/pallas_call | solution.py:324
  4.9 2.8 %collective-permute-start.1 = (bf16[4,64,256]{2,1,0:T(8,128)(2,1)S(1)}, bf16[4,64,256]{2,1,0:T(8,128)(2,1)S(1)}, u32[]{:S(2)}, u32[]{:S(2)}) collective-permute-start(bf16[4,64,256]{2,1,0:T(8,128)(2,1)S(1)} %get-tuple-element.29), channel_id=1, source_target_pairs={{0,2},{1,3},{2,0},{3,1},{4,6},{5,7},{6,4},{7,5},{8,10},{9,11},{10,... | collective-permute-start | bytes 393224 | tf_op jit(solution)/shard_map/ppermute | solution.py:296
  7.7 1.5 %collective-permute-start.2 = (bf16[4,64,256]{2,1,0:T(8,128)(2,1)S(1)}, bf16[4,64,256]{2,1,0:T(8,128)(2,1)S(1)}, u32[]{:S(2)}, u32[]{:S(2)}) collective-permute-start(bf16[4,64,256]{2,1,0:T(8,128)(2,1)S(1)} %get-tuple-element.30), channel_id=1, source_target_pairs={{0,1},{1,0},{2,3},{3,2},{4,5},{5,4},{6,7},{7,6},{8,9},{9,8},{10,11... | collective-permute-start | bytes 393224 | tf_op jit(solution)/shard_map/ppermute | solution.py:296
  9.2 0.0 collective-permute-start.3
  9.3 1.9 %collective-permute-start.12 = (bf16[4,64,256]{2,1,0:T(8,128)(2,1)S(1)}, bf16[4,64,256]{2,1,0:T(8,128)(2,1)S(1)}, u32[]{:S(2)}, u32[]{:S(2)}) collective-permute-start(bf16[4,64,256]{2,1,0:T(8,128)(2,1)S(1)} %get-tuple-element.39), channel_id=1, source_target_pairs={{0,2},{1,3},{2,0},{3,1},{4,6},{5,7},{6,4},{7,5},{8,10},{9,11},{10,... | collective-permute-start | bytes 393224 | tf_op jit(solution)/shard_map/ppermute | solution.py:296
  11.2 1.5 %collective-permute-start.13 = (bf16[4,64,256]{2,1,0:T(8,128)(2,1)S(1)}, bf16[4,64,256]{2,1,0:T(8,128)(2,1)S(1)}, u32[]{:S(2)}, u32[]{:S(2)}) collective-permute-start(bf16[4,64,256]{2,1,0:T(8,128)(2,1)S(1)} %get-tuple-element.40), channel_id=1, source_target_pairs={{0,1},{1,0},{2,3},{3,2},{4,5},{5,4},{6,7},{7,6},{8,9},{9,8},{10,11... | collective-permute-start | bytes 393224 | tf_op jit(solution)/shard_map/ppermute | solution.py:296
  12.7 0.0 collective-permute-done.1.refs_3_
  12.7 1.6 %collective-permute-start.14 = (bf16[4,64,256]{2,1,0:T(8,128)(2,1)S(1)}, bf16[4,64,256]{2,1,0:T(8,128)(2,1)S(1)}, u32[]{:S(2)}, u32[]{:S(2)}) collective-permute-start(bf16[4,64,256]{2,1,0:T(8,128)(2,1)S(1)} %get-tuple-element.41), channel_id=1, source_target_pairs={{0,3},{1,2},{2,1},{3,0},{4,7},{5,6},{6,5},{7,4},{8,11},{9,10},{10,... | collective-permute-start | bytes 393224 | tf_op jit(solution)/shard_map/ppermute | solution.py:296
  14.3 0.0 collective-permute-done.2.refs_4_
  14.3 2.3 %collective-permute-done.3.refs_5_ = bf16[4,64,256]{2,1,0:T(8,128)(2,1)S(1)} collective-permute-done((bf16[4,64,256]{2,1,0:T(8,128)(2,1)S(1)}, bf16[4,64,256]{2,1,0:T(8,128)(2,1)S(1)}, u32[]{:S(2)}, u32[]{:S(2)}) %collective-permute-start.3) | collective-permute-done | bytes 131104 | tf_op jit(solution)/shard_map/ppermute | solution.py:296
  16.6 1.3 %columns.2 = (bf16[256,256]{1,0:T(8,128)(2,1)S(1)}, bf16[256,256]{1,0:T(8,128)(2,1)S(1)}, bf16[256,256]{1,0:T(8,128)(2,1)S(1)}, bf16[256,256]{1,0:T(8,128)(2,1)S(1)}) custom-call(bf16[1024,1024]{1,0:T(8,128)(2,1)S(1)} %copy-done, bf16[4,1024,256]{2,1,0:T(8,128)(2,1)S(1)} %filters.1.refs_3_.refs_1_, bf16[4,64,256]{2,1,0:T(8,128)(2,1)S(1)} %get-tuple-element.28.refs_2_, ...), custom_call_target="tpu_custom_call" | custom-call | flops 1 | bytes 1 | tf_op jit(solution)/shard_map/columns/pallas_call | solution.py:343
  17.9 1.6 %collective-permute-start.4 = (bf16[256,256]{1,0:T(8,128)(2,1)S(1)}, bf16[256,256]{1,0:T(8,128)(2,1)S(1)}, u32[]{:S(2)}, u32[]{:S(2)}) collective-permute-start(bf16[256,256]{1,0:T(8,128)(2,1)S(1)} %get-tuple-element.34), channel_id=1, source_target_pairs={{0,4},{1,5},{2,6},{3,7},{4,0},{5,1},{6,2},{7,3},{8,12},{9,13},{10,... | collective-permute-start | bytes 393224 | tf_op jit(solution)/shard_map/ppermute | solution.py:296
  19.5 0.0 collective-permute-start.7
  19.5 0.0 collective-permute-done.12.refs_3_
  19.5 3.2 %collective-permute-start.6 = (bf16[256,256]{1,0:T(8,128)(2,1)S(1)}, bf16[256,256]{1,0:T(8,128)(2,1)S(1)}, u32[]{:S(2)}, u32[]{:S(2)}) collective-permute-start(bf16[256,256]{1,0:T(8,128)(2,1)S(1)} %get-tuple-element.35), channel_id=1, source_target_pairs={{0,4},{1,5},{2,6},{3,7},{4,0},{5,1},{6,2},{7,3},{8,12},{9,13},{10,... | collective-permute-start | bytes 393224 | tf_op jit(solution)/shard_map/ppermute | solution.py:296
  22.7 0.0 collective-permute-done.13.refs_4_
  22.7 0.0 collective-permute-done.14.refs_5_
  22.7 1.3 %columns.3 = (bf16[256,256]{1,0:T(8,128)(2,1)S(1)}, bf16[256,256]{1,0:T(8,128)(2,1)S(1)}, bf16[256,256]{1,0:T(8,128)(2,1)S(1)}, bf16[256,256]{1,0:T(8,128)(2,1)S(1)}) custom-call(bf16[1024,1024]{1,0:T(8,128)(2,1)S(1)} %copy-done, bf16[4,1024,256]{2,1,0:T(8,128)(2,1)S(1)} %filters.1.refs_3_.refs_1_, bf16[4,64,256]{2,1,0:T(8,128)(2,1)S(1)} %get-tuple-element.38.refs_2_, ...), custom_call_target="tpu_custom_call" | custom-call | flops 1 | bytes 1 | tf_op jit(solution)/shard_map/columns/pallas_call | solution.py:343
  24.0 0.4 collective-permute-start.15
  24.4 0.0 collective-permute-done.4.refs_1_.refs_2_
  24.4 0.1 far.2
  24.4 2.7 %collective-permute-start.5 = (bf16[256,256]{1,0:T(8,128)(2,1)S(1)}, bf16[256,256]{1,0:T(8,128)(2,1)S(1)}, u32[]{:S(2)}, u32[]{:S(2)}) collective-permute-start(bf16[256,256]{1,0:T(8,128)(2,1)S(1)} %far.2), channel_id=1, source_target_pairs={{0,8},{1,9},{2,10},{3,11},{4,12},{5,13},{6,14},{7,15},{8,0},{9,1},... | collective-permute-start | bytes 393224 | tf_op jit(solution)/shard_map/ppermute | solution.py:296
  27.1 0.0 collective-permute-start.18
  27.1 0.0 collective-permute-done.7.refs_4_.refs_1_
  27.1 1.5 %collective-permute-start.17 = (bf16[256,256]{1,0:T(8,128)(2,1)S(1)}, bf16[256,256]{1,0:T(8,128)(2,1)S(1)}, u32[]{:S(2)}, u32[]{:S(2)}) collective-permute-start(bf16[256,256]{1,0:T(8,128)(2,1)S(1)} %get-tuple-element.45), channel_id=1, source_target_pairs={{0,4},{1,5},{2,6},{3,7},{4,0},{5,1},{6,2},{7,3},{8,12},{9,13},{10,... | collective-permute-start | bytes 393224 | tf_op jit(solution)/shard_map/ppermute | solution.py:296
  28.6 0.0 collective-permute-done.6.refs_3_.refs_0_
  28.6 1.9 %collective-permute-done.15.refs_3_.refs_2_ = bf16[256,256]{1,0:T(8,128)(2,1)S(1)} collective-permute-done((bf16[256,256]{1,0:T(8,128)(2,1)S(1)}, bf16[256,256]{1,0:T(8,128)(2,1)S(1)}, u32[]{:S(2)}, u32[]{:S(2)}) %collective-permute-start.15) | collective-permute-done | bytes 131104 | tf_op jit(solution)/shard_map/ppermute | solution.py:296
  30.5 0.1 far.3
  30.5 2.4 %collective-permute-start.16 = (bf16[256,256]{1,0:T(8,128)(2,1)S(1)}, bf16[256,256]{1,0:T(8,128)(2,1)S(1)}, u32[]{:S(2)}, u32[]{:S(2)}) collective-permute-start(bf16[256,256]{1,0:T(8,128)(2,1)S(1)} %far.3), channel_id=1, source_target_pairs={{0,8},{1,9},{2,10},{3,11},{4,12},{5,13},{6,14},{7,15},{8,0},{9,1},... | collective-permute-start | bytes 393224 | tf_op jit(solution)/shard_map/ppermute | solution.py:296
  32.9 1.8 %collective-permute-done.5.refs_1_ = bf16[256,256]{1,0:T(8,128)(2,1)S(1)} collective-permute-done((bf16[256,256]{1,0:T(8,128)(2,1)S(1)}, bf16[256,256]{1,0:T(8,128)(2,1)S(1)}, u32[]{:S(2)}, u32[]{:S(2)}) %collective-permute-start.5) | collective-permute-done | bytes 131104 | tf_op jit(solution)/shard_map/ppermute | solution.py:296
  34.7 0.1 half.2
  34.8 1.5 %collective-permute-start.10 = (bf16[128,256]{1,0:T(8,128)(2,1)S(1)}, bf16[128,256]{1,0:T(8,128)(2,1)S(1)}, u32[]{:S(2)}, u32[]{:S(2)}) collective-permute-start(bf16[128,256]{1,0:T(8,128)(2,1)S(1)} %get-tuple-element.36.refs_1_), channel_id=1, source_target_pairs={{0,1},{1,0},{2,3},{3,2},{4,5},{5,4},{6,7},{7,6},{8,9},{9,8},{10,11... | collective-permute-start | bytes 196616 | tf_op jit(solution)/shard_map/ppermute | solution.py:296
  36.3 1.5 %collective-permute-start.9 = (bf16[128,256]{1,0:T(8,128)(2,1)S(1)}, bf16[128,256]{1,0:T(8,128)(2,1)S(1)}, u32[]{:S(2)}, u32[]{:S(2)}) collective-permute-start(bf16[128,256]{1,0:T(8,128)(2,1)S(1)} %get-tuple-element.37), channel_id=1, source_target_pairs={{0,3},{1,2},{2,1},{3,0},{4,7},{5,6},{6,5},{7,4},{8,11},{9,10},{10,... | collective-permute-start | bytes 196616 | tf_op jit(solution)/shard_map/ppermute | solution.py:296
  37.8 0.0 collective-permute-done.18.refs_4_
  37.8 0.5 %collective-permute-start.8 = (bf16[128,256]{1,0:T(8,128)(2,1)S(1)}, bf16[128,256]{1,0:T(8,128)(2,1)S(1)}, u32[]{:S(2)}, u32[]{:S(2)}) collective-permute-start(bf16[128,256]{1,0:T(8,128)(2,1)S(1)} %get-tuple-element.37), channel_id=1, source_target_pairs={{0,2},{1,3},{2,0},{3,1},{4,6},{5,7},{6,4},{7,5},{8,10},{9,11},{10,... | collective-permute-start | bytes 196616 | tf_op jit(solution)/shard_map/ppermute | solution.py:296
  38.3 0.0 collective-permute-done.17.refs_3_
  38.3 2.8 %collective-permute-done.16.refs_1_ = bf16[256,256]{1,0:T(8,128)(2,1)S(1)} collective-permute-done((bf16[256,256]{1,0:T(8,128)(2,1)S(1)}, bf16[256,256]{1,0:T(8,128)(2,1)S(1)}, u32[]{:S(2)}, u32[]{:S(2)}) %collective-permute-start.16) | collective-permute-done | bytes 131104 | tf_op jit(solution)/shard_map/ppermute | solution.py:296
  41.1 0.1 half.3
  41.2 1.3 %collective-permute-start.21 = (bf16[128,256]{1,0:T(8,128)(2,1)S(1)}, bf16[128,256]{1,0:T(8,128)(2,1)S(1)}, u32[]{:S(2)}, u32[]{:S(2)}) collective-permute-start(bf16[128,256]{1,0:T(8,128)(2,1)S(1)} %get-tuple-element.46.refs_1_), channel_id=1, source_target_pairs={{0,1},{1,0},{2,3},{3,2},{4,5},{5,4},{6,7},{7,6},{8,9},{9,8},{10,11... | collective-permute-start | bytes 196616 | tf_op jit(solution)/shard_map/ppermute | solution.py:296
  42.5 0.0 copy-start.1
  42.5 1.5 %collective-permute-start.20 = (bf16[128,256]{1,0:T(8,128)(2,1)S(1)}, bf16[128,256]{1,0:T(8,128)(2,1)S(1)}, u32[]{:S(2)}, u32[]{:S(2)}) collective-permute-start(bf16[128,256]{1,0:T(8,128)(2,1)S(1)} %get-tuple-element.47), channel_id=1, source_target_pairs={{0,3},{1,2},{2,1},{3,0},{4,7},{5,6},{6,5},{7,4},{8,11},{9,10},{10,... | collective-permute-start | bytes 196616 | tf_op jit(solution)/shard_map/ppermute | solution.py:296
  44.0 0.0 collective-permute-done.10.refs_4_
  44.0 0.8 %collective-permute-start.19 = (bf16[128,256]{1,0:T(8,128)(2,1)S(1)}, bf16[128,256]{1,0:T(8,128)(2,1)S(1)}, u32[]{:S(2)}, u32[]{:S(2)}) collective-permute-start(bf16[128,256]{1,0:T(8,128)(2,1)S(1)} %get-tuple-element.47), channel_id=1, source_target_pairs={{0,2},{1,3},{2,0},{3,1},{4,6},{5,7},{6,4},{7,5},{8,10},{9,11},{10,... | collective-permute-start | bytes 196616 | tf_op jit(solution)/shard_map/ppermute | solution.py:296
  44.8 0.0 collective-permute-done.9.refs_3_
  44.8 0.0 collective-permute-done.8.refs_2_
  44.8 0.5 phase.2.refs_3_
  45.2 0.1 collective-permute-start.11
  45.3 0.2 collective-permute-done.21.refs_4_
  45.5 2.2 %collective-permute-done.20.refs_3_ = bf16[128,256]{1,0:T(8,128)(2,1)S(1)} collective-permute-done((bf16[128,256]{1,0:T(8,128)(2,1)S(1)}, bf16[128,256]{1,0:T(8,128)(2,1)S(1)}, u32[]{:S(2)}, u32[]{:S(2)}) %collective-permute-start.20) | collective-permute-done | bytes 65568 | tf_op jit(solution)/shard_map/ppermute | solution.py:296
  47.7 0.7 %collective-permute-done.19.refs_2_ = bf16[128,256]{1,0:T(8,128)(2,1)S(1)} collective-permute-done((bf16[128,256]{1,0:T(8,128)(2,1)S(1)}, bf16[128,256]{1,0:T(8,128)(2,1)S(1)}, u32[]{:S(2)}, u32[]{:S(2)}) %collective-permute-start.19) | collective-permute-done | bytes 65568 | tf_op jit(solution)/shard_map/ppermute | solution.py:296
  48.4 0.5 phase.3.refs_5_
  48.9 0.1 collective-permute-start.22
  48.9 0.0 collective-permute-done.11.refs_4_
  48.9 0.0 copy-done.1
  49.0 0.0 copy-done.2
  49.0 0.0 copy-done.3
  49.0 1.2 %recon.2 = (f32[128,512]{1,0:T(8,128)S(1)}, bf16[1024,512]{1,0:T(8,128)(2,1)S(1)}, bf16[128,128]{1,0:T(8,128)(2,1)S(1)}) custom-call(s32[1,4]{1,0:T(1,128)S(1)} %copy-done.2, s32[16]{0:T(128)S(1)} %copy-done.3, bf16[4,1024,512]{2,1,0:T(8,128)(2,1)S(1)} %copy-done.1, bf16[128,1024]{1,0:T(8,128)(2,1)S(1)} %phase.2.refs_3_, ...), custom_call_target="tpu_custom_call" | custom-call | flops 1 | bytes 1 | tf_op jit(solution)/shard_map/recon/pallas_call | solution.py:396
  50.2 0.3 collective-permute-done.22.phase
  50.5 1.1 %recon.3 = bf16[128,512]{1,0:T(8,128)(2,1)} custom-call(bf16[1024,512]{1,0:T(8,128)(2,1)S(1)} %get-tuple-element.48.weights, bf16[128,1024]{1,0:T(8,128)(2,1)S(1)} %collective-permute-done.22.phase, f32[128,512]{1,0:T(8,128)S(1)} %get-tuple-element.49.before, bf16[128,128]{1,0:T(8,128)(2,1)S(1)} %get-tuple-element.50.select), custom_call_target="tpu_custom_call" | custom-call | flops 1 | bytes 1 | tf_op jit(solution)/shard_map/recon/pallas_call | solution.py:409
  (2 shorter events, 0.0 us)
Async XLA Ops:
  0.0 3.1 %copy-start = (bf16[1024,1024]{1,0:T(8,128)(2,1)S(1)}, bf16[1024,1024]{1,0:T(8,128)(2,1)}, u32[]{:S(2)}) copy-start(bf16[1024,1024]{1,0:T(8,128)(2,1)} %constant.2.clone.refs_2_.refs_0_) | copy-start | bytes 6291460
  0.0 3.1 %collective-permute-start = (bf16[4,2,64,1024]{3,2,1,0:T(8,128)(2,1)}, bf16[4,2,64,1024]{3,2,1,0:T(8,128)(2,1)S(1)}, u32[]{:S(2)}, u32[]{:S(2)}) collective-permute-start(bf16[4,2,64,1024]{3,2,1,0:T(8,128)(2,1)} %bitcast.1), channel_id=1, source_target_pairs={{0,16},{1,17},{2,18},{3,19},{4,20},{5,21},{6,22},{7,23},{8,24},{9,... | collective-permute-start | bytes 3145736 | tf_op jit(solution)/shard_map/ppermute | solution.py:296
  4.9 7.8 %collective-permute-start.1 = (bf16[4,64,256]{2,1,0:T(8,128)(2,1)S(1)}, bf16[4,64,256]{2,1,0:T(8,128)(2,1)S(1)}, u32[]{:S(2)}, u32[]{:S(2)}) collective-permute-start(bf16[4,64,256]{2,1,0:T(8,128)(2,1)S(1)} %get-tuple-element.29), channel_id=1, source_target_pairs={{0,2},{1,3},{2,0},{3,1},{4,6},{5,7},{6,4},{7,5},{8,10},{9,11},{10,... | collective-permute-start | bytes 393224 | tf_op jit(solution)/shard_map/ppermute | solution.py:296
  7.7 6.6 %collective-permute-start.2 = (bf16[4,64,256]{2,1,0:T(8,128)(2,1)S(1)}, bf16[4,64,256]{2,1,0:T(8,128)(2,1)S(1)}, u32[]{:S(2)}, u32[]{:S(2)}) collective-permute-start(bf16[4,64,256]{2,1,0:T(8,128)(2,1)S(1)} %get-tuple-element.30), channel_id=1, source_target_pairs={{0,1},{1,0},{2,3},{3,2},{4,5},{5,4},{6,7},{7,6},{8,9},{9,8},{10,11... | collective-permute-start | bytes 393224 | tf_op jit(solution)/shard_map/ppermute | solution.py:296
  9.2 7.4 %collective-permute-start.3 = (bf16[4,64,256]{2,1,0:T(8,128)(2,1)S(1)}, bf16[4,64,256]{2,1,0:T(8,128)(2,1)S(1)}, u32[]{:S(2)}, u32[]{:S(2)}) collective-permute-start(bf16[4,64,256]{2,1,0:T(8,128)(2,1)S(1)} %get-tuple-element.31), channel_id=1, source_target_pairs={{0,3},{1,2},{2,1},{3,0},{4,7},{5,6},{6,5},{7,4},{8,11},{9,10},{10,... | collective-permute-start | bytes 393224 | tf_op jit(solution)/shard_map/ppermute | solution.py:296
  9.3 10.3 %collective-permute-start.12 = (bf16[4,64,256]{2,1,0:T(8,128)(2,1)S(1)}, bf16[4,64,256]{2,1,0:T(8,128)(2,1)S(1)}, u32[]{:S(2)}, u32[]{:S(2)}) collective-permute-start(bf16[4,64,256]{2,1,0:T(8,128)(2,1)S(1)} %get-tuple-element.39), channel_id=1, source_target_pairs={{0,2},{1,3},{2,0},{3,1},{4,6},{5,7},{6,4},{7,5},{8,10},{9,11},{10,... | collective-permute-start | bytes 393224 | tf_op jit(solution)/shard_map/ppermute | solution.py:296
  11.2 11.5 %collective-permute-start.13 = (bf16[4,64,256]{2,1,0:T(8,128)(2,1)S(1)}, bf16[4,64,256]{2,1,0:T(8,128)(2,1)S(1)}, u32[]{:S(2)}, u32[]{:S(2)}) collective-permute-start(bf16[4,64,256]{2,1,0:T(8,128)(2,1)S(1)} %get-tuple-element.40), channel_id=1, source_target_pairs={{0,1},{1,0},{2,3},{3,2},{4,5},{5,4},{6,7},{7,6},{8,9},{9,8},{10,11... | collective-permute-start | bytes 393224 | tf_op jit(solution)/shard_map/ppermute | solution.py:296
  12.7 10.0 %collective-permute-start.14 = (bf16[4,64,256]{2,1,0:T(8,128)(2,1)S(1)}, bf16[4,64,256]{2,1,0:T(8,128)(2,1)S(1)}, u32[]{:S(2)}, u32[]{:S(2)}) collective-permute-start(bf16[4,64,256]{2,1,0:T(8,128)(2,1)S(1)} %get-tuple-element.41), channel_id=1, source_target_pairs={{0,3},{1,2},{2,1},{3,0},{4,7},{5,6},{6,5},{7,4},{8,11},{9,10},{10,... | collective-permute-start | bytes 393224 | tf_op jit(solution)/shard_map/ppermute | solution.py:296
  17.9 6.5 %collective-permute-start.4 = (bf16[256,256]{1,0:T(8,128)(2,1)S(1)}, bf16[256,256]{1,0:T(8,128)(2,1)S(1)}, u32[]{:S(2)}, u32[]{:S(2)}) collective-permute-start(bf16[256,256]{1,0:T(8,128)(2,1)S(1)} %get-tuple-element.34), channel_id=1, source_target_pairs={{0,4},{1,5},{2,6},{3,7},{4,0},{5,1},{6,2},{7,3},{8,12},{9,13},{10,... | collective-permute-start | bytes 393224 | tf_op jit(solution)/shard_map/ppermute | solution.py:296
  19.5 7.6 %collective-permute-start.7 = (bf16[256,256]{1,0:T(8,128)(2,1)S(1)}, bf16[256,256]{1,0:T(8,128)(2,1)S(1)}, u32[]{:S(2)}, u32[]{:S(2)}) collective-permute-start(bf16[256,256]{1,0:T(8,128)(2,1)S(1)} %get-tuple-element.35), channel_id=1, source_target_pairs={{0,16},{1,17},{2,18},{3,19},{4,8},{5,9},{6,10},{7,11},{8,4},{9,5},... | collective-permute-start | bytes 393224 | tf_op jit(solution)/shard_map/ppermute | solution.py:296
  19.5 9.1 %collective-permute-start.6 = (bf16[256,256]{1,0:T(8,128)(2,1)S(1)}, bf16[256,256]{1,0:T(8,128)(2,1)S(1)}, u32[]{:S(2)}, u32[]{:S(2)}) collective-permute-start(bf16[256,256]{1,0:T(8,128)(2,1)S(1)} %get-tuple-element.35), channel_id=1, source_target_pairs={{0,4},{1,5},{2,6},{3,7},{4,0},{5,1},{6,2},{7,3},{8,12},{9,13},{10,... | collective-permute-start | bytes 393224 | tf_op jit(solution)/shard_map/ppermute | solution.py:296
  24.0 6.5 %collective-permute-start.15 = (bf16[256,256]{1,0:T(8,128)(2,1)S(1)}, bf16[256,256]{1,0:T(8,128)(2,1)S(1)}, u32[]{:S(2)}, u32[]{:S(2)}) collective-permute-start(bf16[256,256]{1,0:T(8,128)(2,1)S(1)} %get-tuple-element.44), channel_id=1, source_target_pairs={{0,4},{1,5},{2,6},{3,7},{4,0},{5,1},{6,2},{7,3},{8,12},{9,13},{10,... | collective-permute-start | bytes 393224 | tf_op jit(solution)/shard_map/ppermute | solution.py:296
  24.4 10.3 %collective-permute-start.5 = (bf16[256,256]{1,0:T(8,128)(2,1)S(1)}, bf16[256,256]{1,0:T(8,128)(2,1)S(1)}, u32[]{:S(2)}, u32[]{:S(2)}) collective-permute-start(bf16[256,256]{1,0:T(8,128)(2,1)S(1)} %far.2), channel_id=1, source_target_pairs={{0,8},{1,9},{2,10},{3,11},{4,12},{5,13},{6,14},{7,15},{8,0},{9,1},... | collective-permute-start | bytes 393224 | tf_op jit(solution)/shard_map/ppermute | solution.py:296
  27.1 10.7 %collective-permute-start.18 = (bf16[256,256]{1,0:T(8,128)(2,1)S(1)}, bf16[256,256]{1,0:T(8,128)(2,1)S(1)}, u32[]{:S(2)}, u32[]{:S(2)}) collective-permute-start(bf16[256,256]{1,0:T(8,128)(2,1)S(1)} %get-tuple-element.45), channel_id=1, source_target_pairs={{0,16},{1,17},{2,18},{3,19},{4,8},{5,9},{6,10},{7,11},{8,4},{9,5},... | collective-permute-start | bytes 393224 | tf_op jit(solution)/shard_map/ppermute | solution.py:296
  27.1 11.2 %collective-permute-start.17 = (bf16[256,256]{1,0:T(8,128)(2,1)S(1)}, bf16[256,256]{1,0:T(8,128)(2,1)S(1)}, u32[]{:S(2)}, u32[]{:S(2)}) collective-permute-start(bf16[256,256]{1,0:T(8,128)(2,1)S(1)} %get-tuple-element.45), channel_id=1, source_target_pairs={{0,4},{1,5},{2,6},{3,7},{4,0},{5,1},{6,2},{7,3},{8,12},{9,13},{10,... | collective-permute-start | bytes 393224 | tf_op jit(solution)/shard_map/ppermute | solution.py:296
  30.5 10.6 %collective-permute-start.16 = (bf16[256,256]{1,0:T(8,128)(2,1)S(1)}, bf16[256,256]{1,0:T(8,128)(2,1)S(1)}, u32[]{:S(2)}, u32[]{:S(2)}) collective-permute-start(bf16[256,256]{1,0:T(8,128)(2,1)S(1)} %far.3), channel_id=1, source_target_pairs={{0,8},{1,9},{2,10},{3,11},{4,12},{5,13},{6,14},{7,15},{8,0},{9,1},... | collective-permute-start | bytes 393224 | tf_op jit(solution)/shard_map/ppermute | solution.py:296
  34.8 9.2 %collective-permute-start.10 = (bf16[128,256]{1,0:T(8,128)(2,1)S(1)}, bf16[128,256]{1,0:T(8,128)(2,1)S(1)}, u32[]{:S(2)}, u32[]{:S(2)}) collective-permute-start(bf16[128,256]{1,0:T(8,128)(2,1)S(1)} %get-tuple-element.36.refs_1_), channel_id=1, source_target_pairs={{0,1},{1,0},{2,3},{3,2},{4,5},{5,4},{6,7},{7,6},{8,9},{9,8},{10,11... | collective-permute-start | bytes 196616 | tf_op jit(solution)/shard_map/ppermute | solution.py:296
  36.3 8.4 %collective-permute-start.9 = (bf16[128,256]{1,0:T(8,128)(2,1)S(1)}, bf16[128,256]{1,0:T(8,128)(2,1)S(1)}, u32[]{:S(2)}, u32[]{:S(2)}) collective-permute-start(bf16[128,256]{1,0:T(8,128)(2,1)S(1)} %get-tuple-element.37), channel_id=1, source_target_pairs={{0,3},{1,2},{2,1},{3,0},{4,7},{5,6},{6,5},{7,4},{8,11},{9,10},{10,... | collective-permute-start | bytes 196616 | tf_op jit(solution)/shard_map/ppermute | solution.py:296
  37.8 7.0 %collective-permute-start.8 = (bf16[128,256]{1,0:T(8,128)(2,1)S(1)}, bf16[128,256]{1,0:T(8,128)(2,1)S(1)}, u32[]{:S(2)}, u32[]{:S(2)}) collective-permute-start(bf16[128,256]{1,0:T(8,128)(2,1)S(1)} %get-tuple-element.37), channel_id=1, source_target_pairs={{0,2},{1,3},{2,0},{3,1},{4,6},{5,7},{6,4},{7,5},{8,10},{9,11},{10,... | collective-permute-start | bytes 196616 | tf_op jit(solution)/shard_map/ppermute | solution.py:296
  41.2 4.3 %collective-permute-start.21 = (bf16[128,256]{1,0:T(8,128)(2,1)S(1)}, bf16[128,256]{1,0:T(8,128)(2,1)S(1)}, u32[]{:S(2)}, u32[]{:S(2)}) collective-permute-start(bf16[128,256]{1,0:T(8,128)(2,1)S(1)} %get-tuple-element.46.refs_1_), channel_id=1, source_target_pairs={{0,1},{1,0},{2,3},{3,2},{4,5},{5,4},{6,7},{7,6},{8,9},{9,8},{10,11... | collective-permute-start | bytes 196616 | tf_op jit(solution)/shard_map/ppermute | solution.py:296
  42.5 6.4 %copy-start.1 = (bf16[4,1024,512]{2,1,0:T(8,128)(2,1)S(1)}, bf16[4,1024,512]{2,1,0:T(8,128)(2,1)}, u32[]{:S(2)}) copy-start(bf16[4,1024,512]{2,1,0:T(8,128)(2,1)} %refs_2_.2) | copy-start | bytes 12582916
  42.5 6.4 %copy-start.2 = (s32[1,4]{1,0:T(1,128)S(1)}, s32[1,4]{1,0:T(1,128)}, u32[]{:S(2)}) copy-start(s32[1,4]{1,0:T(1,128)} %refs_0_.7) | copy-start | bytes 52
  42.5 6.4 %copy-start.3 = (s32[16]{0:T(128)S(1)}, s32[16]{0:T(128)}, u32[]{:S(2)}) copy-start(s32[16]{0:T(128)} %refs_1_.1) | copy-start | bytes 196
  42.5 5.2 %collective-permute-start.20 = (bf16[128,256]{1,0:T(8,128)(2,1)S(1)}, bf16[128,256]{1,0:T(8,128)(2,1)S(1)}, u32[]{:S(2)}, u32[]{:S(2)}) collective-permute-start(bf16[128,256]{1,0:T(8,128)(2,1)S(1)} %get-tuple-element.47), channel_id=1, source_target_pairs={{0,3},{1,2},{2,1},{3,0},{4,7},{5,6},{6,5},{7,4},{8,11},{9,10},{10,... | collective-permute-start | bytes 196616 | tf_op jit(solution)/shard_map/ppermute | solution.py:296
  44.0 4.4 %collective-permute-start.19 = (bf16[128,256]{1,0:T(8,128)(2,1)S(1)}, bf16[128,256]{1,0:T(8,128)(2,1)S(1)}, u32[]{:S(2)}, u32[]{:S(2)}) collective-permute-start(bf16[128,256]{1,0:T(8,128)(2,1)S(1)} %get-tuple-element.47), channel_id=1, source_target_pairs={{0,2},{1,3},{2,0},{3,1},{4,6},{5,7},{6,4},{7,5},{8,10},{9,11},{10,... | collective-permute-start | bytes 196616 | tf_op jit(solution)/shard_map/ppermute | solution.py:296
  45.2 3.7 %collective-permute-start.11 = (bf16[128,1024]{1,0:T(8,128)(2,1)S(1)}, bf16[128,1024]{1,0:T(8,128)(2,1)S(1)}, u32[]{:S(2)}, u32[]{:S(2)}) collective-permute-start(bf16[128,1024]{1,0:T(8,128)(2,1)S(1)} %phase.2.refs_3_), channel_id=1, source_target_pairs={{0,16},{1,17},{2,18},{3,19},{4,20},{5,21},{6,22},{7,23},{8,24},{9,... | collective-permute-start | bytes 786440 | tf_op jit(solution)/shard_map/ppermute | solution.py:296
  48.9 1.6 %collective-permute-start.22 = (bf16[128,1024]{1,0:T(8,128)(2,1)S(1)}, bf16[128,1024]{1,0:T(8,128)(2,1)S(1)}, u32[]{:S(2)}, u32[]{:S(2)}) collective-permute-start(bf16[128,1024]{1,0:T(8,128)(2,1)S(1)} %phase.3.refs_5_), channel_id=1, source_target_pairs={{0,16},{1,17},{2,18},{3,19},{4,20},{5,21},{6,22},{7,23},{8,24},{9,... | collective-permute-start | bytes 786440 | tf_op jit(solution)/shard_map/ppermute | solution.py:296

commit v19 on v18

--- a/solution.py
+++ b/solution.py
@@ -197,7 +197,7 @@
     out[...] = (ours[...].astype(f32) + more).astype(bf16)
 
 
-def half_kernel(inner, ours, far, near, next_near, across, other, mine):
+def half_kernel(inner, ours, far, near, next_near, across, other, mine, again):
     _, plane, spot = position(inner)
     middle = (plane == 1) | (plane == 2)
     capacity = mine.shape[0]
@@ -207,6 +207,7 @@
         more = jnp.where(middle, inside, near[rows, :].astype(f32))
         got = ours[rows, :].astype(f32) + far[rows, :].astype(f32) + more
         out[...] = got.astype(bf16)
+    again[...] = other[...]
 
 
 def phase_kernel(inner, table, *refs):
@@ -371,16 +372,16 @@
 
     phases = []
     for chunk in range(own):
-        second, first = pl.pallas_call(
+        second, first, again = pl.pallas_call(
             lambda *refs: half_kernel(inner, *refs),
-            out_shape=[shaped(capacity, block)] * 2,
+            out_shape=[shaped(capacity, block)] * 3,
             in_specs=vmem(5),
-            out_specs=vmem(2),
+            out_specs=vmem(3),
             compiler_params=params,
             cost_estimate=cheap,
             name="half",
         )(*sums[chunk])
-        pieces = spread([first, first, second, second], tail_order)
+        pieces = spread([first, first, second, again], tail_order)
         phase = pl.pallas_call(
             lambda *refs: phase_kernel(inner, *refs),
             out_shape=shaped(capacity, width),

time: 51.8 us -> 51.7 us (level)
  no operation moved by 1% of the time
where the time goes in v19:
time: 51.7 us; the launch traced here: 51.5 us
  starting transfers between devices  28.9 us (56%)
  waiting for transfers between devices  11.9 us (23%)
  Pallas kernels  10.6 us (21%)
    ppermute x23, starting transfers between devices, sent(): return lax.ppermute(value, ('dist', 'rows'), pairs)  28.9 us
    ppermute x23, waiting for transfers between devices, sent(): return lax.ppermute(value, ('dist', 'rows'), pairs)  11.9 us
    pallas_call x1, Pallas kernels, plane_plan(): pl.pallas_call(lambda *refs: filter_kernel(inner, dist_dev, *refs), out_s...  2.62 us
    pallas_call x2, Pallas kernels, plane_plan(): pl.pallas_call(lambda *refs: column_kernel(inner, outer, *refs), out_shap...  2.59 us
    pallas_call x1, Pallas kernels, plane_plan(): pl.pallas_call(lambda *refs: row_kernel(inner, *refs), out_shape=[shaped(...  1.83 us
    pallas_call x1, Pallas kernels, plane_plan(): pl.pallas_call(lambda *refs: recon_kernel(own, *refs), out_shape=[jax.Sha...  1.2 us
    pallas_call x1, Pallas kernels, plane_plan(): pl.pallas_call(recon_last_kernel, out_shape=shaped(capacity, pixels), in_...  1.12 us
  transfers between devices with their start and end apart: 23, of which 8 were waited for; matrix products, arithmetic and copies ran while one was open for 0% of the time, Pallas kernels for 15%

profile of v19, /device:TPU:0, one launch (start us, length us, event | category | flops | bytes accessed | tf_op | source)
XLA Modules:
  0.0 51.5 jit_solution(7694040261560327914)
XLA Ops:
  0.0 0.0 copy-start
  0.0 0.5 collective-permute-start
  0.5 2.6 %filters.1.refs_3_.refs_1_ = bf16[4,1024,256]{2,1,0:T(8,128)(2,1)S(1)} custom-call(f32[4]{0:T(128)} %refs_0_.6), custom_call_target="tpu_custom_call" | custom-call | flops 1 | bytes 1 | tf_op jit(solution)/shard_map/filters/pallas_call | solution.py:316
  3.1 0.0 collective-permute-done.refs_1_
  3.1 0.0 copy-done
  3.1 1.8 %row_spectra.1 = (bf16[4,64,256]{2,1,0:T(8,128)(2,1)S(1)}, bf16[4,64,256]{2,1,0:T(8,128)(2,1)S(1)}, bf16[4,64,256]{2,1,0:T(8,128)(2,1)S(1)}, bf16[4,64,256]{2,1,...) custom-call(bf16[4,2,64,1024]{3,2,1,0:T(8,128)(2,1)} %bitcast.2, ...), custom_call_target="tpu_custom_call" | custom-call | flops 1 | bytes 1 | tf_op jit(solution)/shard_map/row_spectra/pallas_call | solution.py:325
  4.9 2.8 %collective-permute-start.1 = (bf16[4,64,256]{2,1,0:T(8,128)(2,1)S(1)}, bf16[4,64,256]{2,1,0:T(8,128)(2,1)S(1)}, u32[]{:S(2)}, u32[]{:S(2)}) collective-permute-start(bf16[4,64,256]{2,1,0:T(8,128)(2,1)S(1)} %get-tuple-element.31), channel_id=1, source_target_pairs={{0,2},{1,3},{2,0},{3,1},{4,6},{5,7},{6,4},{7,5},{8,10},{9,11},{10,... | collective-permute-start | bytes 393224 | tf_op jit(solution)/shard_map/ppermute | solution.py:297
  7.7 1.5 %collective-permute-start.2 = (bf16[4,64,256]{2,1,0:T(8,128)(2,1)S(1)}, bf16[4,64,256]{2,1,0:T(8,128)(2,1)S(1)}, u32[]{:S(2)}, u32[]{:S(2)}) collective-permute-start(bf16[4,64,256]{2,1,0:T(8,128)(2,1)S(1)} %get-tuple-element.32), channel_id=1, source_target_pairs={{0,1},{1,0},{2,3},{3,2},{4,5},{5,4},{6,7},{7,6},{8,9},{9,8},{10,11... | collective-permute-start | bytes 393224 | tf_op jit(solution)/shard_map/ppermute | solution.py:297
  9.2 0.0 collective-permute-start.3
  9.3 1.9 %collective-permute-start.12 = (bf16[4,64,256]{2,1,0:T(8,128)(2,1)S(1)}, bf16[4,64,256]{2,1,0:T(8,128)(2,1)S(1)}, u32[]{:S(2)}, u32[]{:S(2)}) collective-permute-start(bf16[4,64,256]{2,1,0:T(8,128)(2,1)S(1)} %get-tuple-element.42), channel_id=1, source_target_pairs={{0,2},{1,3},{2,0},{3,1},{4,6},{5,7},{6,4},{7,5},{8,10},{9,11},{10,... | collective-permute-start | bytes 393224 | tf_op jit(solution)/shard_map/ppermute | solution.py:297
  11.2 1.5 %collective-permute-start.13 = (bf16[4,64,256]{2,1,0:T(8,128)(2,1)S(1)}, bf16[4,64,256]{2,1,0:T(8,128)(2,1)S(1)}, u32[]{:S(2)}, u32[]{:S(2)}) collective-permute-start(bf16[4,64,256]{2,1,0:T(8,128)(2,1)S(1)} %get-tuple-element.43), channel_id=1, source_target_pairs={{0,1},{1,0},{2,3},{3,2},{4,5},{5,4},{6,7},{7,6},{8,9},{9,8},{10,11... | collective-permute-start | bytes 393224 | tf_op jit(solution)/shard_map/ppermute | solution.py:297
  12.7 0.0 collective-permute-done.1.refs_3_
  12.7 1.6 %collective-permute-start.14 = (bf16[4,64,256]{2,1,0:T(8,128)(2,1)S(1)}, bf16[4,64,256]{2,1,0:T(8,128)(2,1)S(1)}, u32[]{:S(2)}, u32[]{:S(2)}) collective-permute-start(bf16[4,64,256]{2,1,0:T(8,128)(2,1)S(1)} %get-tuple-element.44), channel_id=1, source_target_pairs={{0,3},{1,2},{2,1},{3,0},{4,7},{5,6},{6,5},{7,4},{8,11},{9,10},{10,... | collective-permute-start | bytes 393224 | tf_op jit(solution)/shard_map/ppermute | solution.py:297
  14.3 0.0 collective-permute-done.2.refs_4_
  14.3 2.3 %collective-permute-done.3.refs_5_ = bf16[4,64,256]{2,1,0:T(8,128)(2,1)S(1)} collective-permute-done((bf16[4,64,256]{2,1,0:T(8,128)(2,1)S(1)}, bf16[4,64,256]{2,1,0:T(8,128)(2,1)S(1)}, u32[]{:S(2)}, u32[]{:S(2)}) %collective-permute-start.3) | collective-permute-done | bytes 131104 | tf_op jit(solution)/shard_map/ppermute | solution.py:297
  16.6 1.3 %columns.2 = (bf16[256,256]{1,0:T(8,128)(2,1)S(1)}, bf16[256,256]{1,0:T(8,128)(2,1)S(1)}, bf16[256,256]{1,0:T(8,128)(2,1)S(1)}, bf16[256,256]{1,0:T(8,128)(2,1)S(1)}) custom-call(bf16[1024,1024]{1,0:T(8,128)(2,1)S(1)} %copy-done, bf16[4,1024,256]{2,1,0:T(8,128)(2,1)S(1)} %filters.1.refs_3_.refs_1_, bf16[4,64,256]{2,1,0:T(8,128)(2,1)S(1)} %get-tuple-element.30.refs_2_, ...), custom_call_target="tpu_custom_call" | custom-call | flops 1 | bytes 1 | tf_op jit(solution)/shard_map/columns/pallas_call | solution.py:344
  17.9 1.6 %collective-permute-start.4 = (bf16[256,256]{1,0:T(8,128)(2,1)S(1)}, bf16[256,256]{1,0:T(8,128)(2,1)S(1)}, u32[]{:S(2)}, u32[]{:S(2)}) collective-permute-start(bf16[256,256]{1,0:T(8,128)(2,1)S(1)} %get-tuple-element.36), channel_id=1, source_target_pairs={{0,4},{1,5},{2,6},{3,7},{4,0},{5,1},{6,2},{7,3},{8,12},{9,13},{10,... | collective-permute-start | bytes 393224 | tf_op jit(solution)/shard_map/ppermute | solution.py:297
  19.5 0.0 collective-permute-start.7
  19.5 0.0 collective-permute-done.12.refs_3_
  19.5 3.2 %collective-permute-start.6 = (bf16[256,256]{1,0:T(8,128)(2,1)S(1)}, bf16[256,256]{1,0:T(8,128)(2,1)S(1)}, u32[]{:S(2)}, u32[]{:S(2)}) collective-permute-start(bf16[256,256]{1,0:T(8,128)(2,1)S(1)} %get-tuple-element.37), channel_id=1, source_target_pairs={{0,4},{1,5},{2,6},{3,7},{4,0},{5,1},{6,2},{7,3},{8,12},{9,13},{10,... | collective-permute-start | bytes 393224 | tf_op jit(solution)/shard_map/ppermute | solution.py:297
  22.7 0.0 collective-permute-done.13.refs_4_
  22.7 0.0 collective-permute-done.14.refs_5_
  22.7 1.3 %columns.3 = (bf16[256,256]{1,0:T(8,128)(2,1)S(1)}, bf16[256,256]{1,0:T(8,128)(2,1)S(1)}, bf16[256,256]{1,0:T(8,128)(2,1)S(1)}, bf16[256,256]{1,0:T(8,128)(2,1)S(1)}) custom-call(bf16[1024,1024]{1,0:T(8,128)(2,1)S(1)} %copy-done, bf16[4,1024,256]{2,1,0:T(8,128)(2,1)S(1)} %filters.1.refs_3_.refs_1_, bf16[4,64,256]{2,1,0:T(8,128)(2,1)S(1)} %get-tuple-element.41.refs_2_, ...), custom_call_target="tpu_custom_call" | custom-call | flops 1 | bytes 1 | tf_op jit(solution)/shard_map/columns/pallas_call | solution.py:344
  24.0 0.4 collective-permute-start.15
  24.4 0.0 collective-permute-done.4.refs_1_.refs_2_
  24.4 0.1 far.2
  24.4 2.7 %collective-permute-start.5 = (bf16[256,256]{1,0:T(8,128)(2,1)S(1)}, bf16[256,256]{1,0:T(8,128)(2,1)S(1)}, u32[]{:S(2)}, u32[]{:S(2)}) collective-permute-start(bf16[256,256]{1,0:T(8,128)(2,1)S(1)} %far.2), channel_id=1, source_target_pairs={{0,8},{1,9},{2,10},{3,11},{4,12},{5,13},{6,14},{7,15},{8,0},{9,1},... | collective-permute-start | bytes 393224 | tf_op jit(solution)/shard_map/ppermute | solution.py:297
  27.1 0.0 collective-permute-start.18
  27.1 0.0 collective-permute-done.7.refs_4_.refs_1_
  27.1 1.5 %collective-permute-start.17 = (bf16[256,256]{1,0:T(8,128)(2,1)S(1)}, bf16[256,256]{1,0:T(8,128)(2,1)S(1)}, u32[]{:S(2)}, u32[]{:S(2)}) collective-permute-start(bf16[256,256]{1,0:T(8,128)(2,1)S(1)} %get-tuple-element.48), channel_id=1, source_target_pairs={{0,4},{1,5},{2,6},{3,7},{4,0},{5,1},{6,2},{7,3},{8,12},{9,13},{10,... | collective-permute-start | bytes 393224 | tf_op jit(solution)/shard_map/ppermute | solution.py:297
  28.6 0.0 collective-permute-done.6.refs_3_.refs_0_
  28.6 1.9 %collective-permute-done.15.refs_3_.refs_2_ = bf16[256,256]{1,0:T(8,128)(2,1)S(1)} collective-permute-done((bf16[256,256]{1,0:T(8,128)(2,1)S(1)}, bf16[256,256]{1,0:T(8,128)(2,1)S(1)}, u32[]{:S(2)}, u32[]{:S(2)}) %collective-permute-start.15) | collective-permute-done | bytes 131104 | tf_op jit(solution)/shard_map/ppermute | solution.py:297
  30.5 0.1 far.3
  30.5 2.4 %collective-permute-start.16 = (bf16[256,256]{1,0:T(8,128)(2,1)S(1)}, bf16[256,256]{1,0:T(8,128)(2,1)S(1)}, u32[]{:S(2)}, u32[]{:S(2)}) collective-permute-start(bf16[256,256]{1,0:T(8,128)(2,1)S(1)} %far.3), channel_id=1, source_target_pairs={{0,8},{1,9},{2,10},{3,11},{4,12},{5,13},{6,14},{7,15},{8,0},{9,1},... | collective-permute-start | bytes 393224 | tf_op jit(solution)/shard_map/ppermute | solution.py:297
  32.9 1.8 %collective-permute-done.5.refs_1_ = bf16[256,256]{1,0:T(8,128)(2,1)S(1)} collective-permute-done((bf16[256,256]{1,0:T(8,128)(2,1)S(1)}, bf16[256,256]{1,0:T(8,128)(2,1)S(1)}, u32[]{:S(2)}, u32[]{:S(2)}) %collective-permute-start.5) | collective-permute-done | bytes 131104 | tf_op jit(solution)/shard_map/ppermute | solution.py:297
  34.7 0.1 half.2
  34.8 1.6 %collective-permute-start.8 = (bf16[128,256]{1,0:T(8,128)(2,1)S(1)}, bf16[128,256]{1,0:T(8,128)(2,1)S(1)}, u32[]{:S(2)}, u32[]{:S(2)}) collective-permute-start(bf16[128,256]{1,0:T(8,128)(2,1)S(1)} %get-tuple-element.39), channel_id=1, source_target_pairs={{0,2},{1,3},{2,0},{3,1},{4,6},{5,7},{6,4},{7,5},{8,10},{9,11},{10,... | collective-permute-start | bytes 196616 | tf_op jit(solution)/shard_map/ppermute | solution.py:297
  36.4 1.4 %collective-permute-start.9 = (bf16[128,256]{1,0:T(8,128)(2,1)S(1)}, bf16[128,256]{1,0:T(8,128)(2,1)S(1)}, u32[]{:S(2)}, u32[]{:S(2)}) collective-permute-start(bf16[128,256]{1,0:T(8,128)(2,1)S(1)} %get-tuple-element.40), channel_id=1, source_target_pairs={{0,3},{1,2},{2,1},{3,0},{4,7},{5,6},{6,5},{7,4},{8,11},{9,10},{10,... | collective-permute-start | bytes 196616 | tf_op jit(solution)/shard_map/ppermute | solution.py:297
  37.8 0.0 collective-permute-done.18.refs_4_
  37.8 0.5 %collective-permute-start.10 = (bf16[128,256]{1,0:T(8,128)(2,1)S(1)}, bf16[128,256]{1,0:T(8,128)(2,1)S(1)}, u32[]{:S(2)}, u32[]{:S(2)}) collective-permute-start(bf16[128,256]{1,0:T(8,128)(2,1)S(1)} %get-tuple-element.38.refs_1_), channel_id=1, source_target_pairs={{0,1},{1,0},{2,3},{3,2},{4,5},{5,4},{6,7},{7,6},{8,9},{9,8},{10,11... | collective-permute-start | bytes 196616 | tf_op jit(solution)/shard_map/ppermute | solution.py:297
  38.4 0.0 collective-permute-done.17.refs_3_
  38.4 2.8 %collective-permute-done.16.refs_1_ = bf16[256,256]{1,0:T(8,128)(2,1)S(1)} collective-permute-done((bf16[256,256]{1,0:T(8,128)(2,1)S(1)}, bf16[256,256]{1,0:T(8,128)(2,1)S(1)}, u32[]{:S(2)}, u32[]{:S(2)}) %collective-permute-start.16) | collective-permute-done | bytes 131104 | tf_op jit(solution)/shard_map/ppermute | solution.py:297
  41.1 0.1 half.3
  41.2 1.3 %collective-permute-start.19 = (bf16[128,256]{1,0:T(8,128)(2,1)S(1)}, bf16[128,256]{1,0:T(8,128)(2,1)S(1)}, u32[]{:S(2)}, u32[]{:S(2)}) collective-permute-start(bf16[128,256]{1,0:T(8,128)(2,1)S(1)} %get-tuple-element.50), channel_id=1, source_target_pairs={{0,2},{1,3},{2,0},{3,1},{4,6},{5,7},{6,4},{7,5},{8,10},{9,11},{10,... | collective-permute-start | bytes 196616 | tf_op jit(solution)/shard_map/ppermute | solution.py:297
  42.6 1.4 %collective-permute-start.20 = (bf16[128,256]{1,0:T(8,128)(2,1)S(1)}, bf16[128,256]{1,0:T(8,128)(2,1)S(1)}, u32[]{:S(2)}, u32[]{:S(2)}) collective-permute-start(bf16[128,256]{1,0:T(8,128)(2,1)S(1)} %get-tuple-element.51), channel_id=1, source_target_pairs={{0,3},{1,2},{2,1},{3,0},{4,7},{5,6},{6,5},{7,4},{8,11},{9,10},{10,... | collective-permute-start | bytes 196616 | tf_op jit(solution)/shard_map/ppermute | solution.py:297
  44.0 0.0 collective-permute-done.8.refs_2_
  44.0 0.0 copy-start.1
  44.0 0.8 %collective-permute-start.21 = (bf16[128,256]{1,0:T(8,128)(2,1)S(1)}, bf16[128,256]{1,0:T(8,128)(2,1)S(1)}, u32[]{:S(2)}, u32[]{:S(2)}) collective-permute-start(bf16[128,256]{1,0:T(8,128)(2,1)S(1)} %get-tuple-element.49.refs_1_), channel_id=1, source_target_pairs={{0,1},{1,0},{2,3},{3,2},{4,5},{5,4},{6,7},{7,6},{8,9},{9,8},{10,11... | collective-permute-start | bytes 196616 | tf_op jit(solution)/shard_map/ppermute | solution.py:297
  44.9 0.0 collective-permute-done.9.refs_3_
  44.9 0.0 collective-permute-done.10.refs_4_
  44.9 0.5 phase.2.refs_3_
  45.3 0.1 collective-permute-start.11
  45.4 0.1 collective-permute-done.19.refs_2_
  45.5 2.2 %collective-permute-done.20.refs_3_ = bf16[128,256]{1,0:T(8,128)(2,1)S(1)} collective-permute-done((bf16[128,256]{1,0:T(8,128)(2,1)S(1)}, bf16[128,256]{1,0:T(8,128)(2,1)S(1)}, u32[]{:S(2)}, u32[]{:S(2)}) %collective-permute-start.20) | collective-permute-done | bytes 65568 | tf_op jit(solution)/shard_map/ppermute | solution.py:297
  47.7 0.6 %collective-permute-done.21.refs_4_ = bf16[128,256]{1,0:T(8,128)(2,1)S(1)} collective-permute-done((bf16[128,256]{1,0:T(8,128)(2,1)S(1)}, bf16[128,256]{1,0:T(8,128)(2,1)S(1)}, u32[]{:S(2)}, u32[]{:S(2)}) %collective-permute-start.21) | collective-permute-done | bytes 65568 | tf_op jit(solution)/shard_map/ppermute | solution.py:297
  48.3 0.5 phase.3.refs_5_
  48.8 0.1 collective-permute-start.22
  48.9 0.0 collective-permute-done.11.refs_4_
  48.9 0.0 copy-done.1
  48.9 0.0 copy-done.2
  48.9 0.0 copy-done.3
  48.9 1.2 %recon.2 = (f32[128,512]{1,0:T(8,128)S(1)}, bf16[1024,512]{1,0:T(8,128)(2,1)S(1)}, bf16[128,128]{1,0:T(8,128)(2,1)S(1)}) custom-call(s32[1,4]{1,0:T(1,128)S(1)} %copy-done.2, s32[16]{0:T(128)S(1)} %copy-done.3, bf16[4,1024,512]{2,1,0:T(8,128)(2,1)S(1)} %copy-done.1, bf16[128,1024]{1,0:T(8,128)(2,1)S(1)} %phase.2.refs_3_, ...), custom_call_target="tpu_custom_call" | custom-call | flops 1 | bytes 1 | tf_op jit(solution)/shard_map/recon/pallas_call | solution.py:397
  50.1 0.3 collective-permute-done.22.phase
  50.4 1.1 %recon.3 = bf16[128,512]{1,0:T(8,128)(2,1)} custom-call(bf16[1024,512]{1,0:T(8,128)(2,1)S(1)} %get-tuple-element.52.weights, bf16[128,1024]{1,0:T(8,128)(2,1)S(1)} %collective-permute-done.22.phase, f32[128,512]{1,0:T(8,128)S(1)} %get-tuple-element.53.before, bf16[128,128]{1,0:T(8,128)(2,1)S(1)} %get-tuple-element.54.select), custom_call_target="tpu_custom_call" | custom-call | flops 1 | bytes 1 | tf_op jit(solution)/shard_map/recon/pallas_call | solution.py:410
  (2 shorter events, 0.0 us)
Async XLA Ops:
  0.0 3.1 %copy-start = (bf16[1024,1024]{1,0:T(8,128)(2,1)S(1)}, bf16[1024,1024]{1,0:T(8,128)(2,1)}, u32[]{:S(2)}) copy-start(bf16[1024,1024]{1,0:T(8,128)(2,1)} %constant.2.clone.refs_2_.refs_0_) | copy-start | bytes 6291460
  0.0 3.1 %collective-permute-start = (bf16[4,2,64,1024]{3,2,1,0:T(8,128)(2,1)}, bf16[4,2,64,1024]{3,2,1,0:T(8,128)(2,1)S(1)}, u32[]{:S(2)}, u32[]{:S(2)}) collective-permute-start(bf16[4,2,64,1024]{3,2,1,0:T(8,128)(2,1)} %bitcast.1), channel_id=1, source_target_pairs={{0,16},{1,17},{2,18},{3,19},{4,20},{5,21},{6,22},{7,23},{8,24},{9,... | collective-permute-start | bytes 3145736 | tf_op jit(solution)/shard_map/ppermute | solution.py:297
  4.9 7.8 %collective-permute-start.1 = (bf16[4,64,256]{2,1,0:T(8,128)(2,1)S(1)}, bf16[4,64,256]{2,1,0:T(8,128)(2,1)S(1)}, u32[]{:S(2)}, u32[]{:S(2)}) collective-permute-start(bf16[4,64,256]{2,1,0:T(8,128)(2,1)S(1)} %get-tuple-element.31), channel_id=1, source_target_pairs={{0,2},{1,3},{2,0},{3,1},{4,6},{5,7},{6,4},{7,5},{8,10},{9,11},{10,... | collective-permute-start | bytes 393224 | tf_op jit(solution)/shard_map/ppermute | solution.py:297
  7.7 6.6 %collective-permute-start.2 = (bf16[4,64,256]{2,1,0:T(8,128)(2,1)S(1)}, bf16[4,64,256]{2,1,0:T(8,128)(2,1)S(1)}, u32[]{:S(2)}, u32[]{:S(2)}) collective-permute-start(bf16[4,64,256]{2,1,0:T(8,128)(2,1)S(1)} %get-tuple-element.32), channel_id=1, source_target_pairs={{0,1},{1,0},{2,3},{3,2},{4,5},{5,4},{6,7},{7,6},{8,9},{9,8},{10,11... | collective-permute-start | bytes 393224 | tf_op jit(solution)/shard_map/ppermute | solution.py:297
  9.2 7.4 %collective-permute-start.3 = (bf16[4,64,256]{2,1,0:T(8,128)(2,1)S(1)}, bf16[4,64,256]{2,1,0:T(8,128)(2,1)S(1)}, u32[]{:S(2)}, u32[]{:S(2)}) collective-permute-start(bf16[4,64,256]{2,1,0:T(8,128)(2,1)S(1)} %get-tuple-element.33), channel_id=1, source_target_pairs={{0,3},{1,2},{2,1},{3,0},{4,7},{5,6},{6,5},{7,4},{8,11},{9,10},{10,... | collective-permute-start | bytes 393224 | tf_op jit(solution)/shard_map/ppermute | solution.py:297
  9.3 10.3 %collective-permute-start.12 = (bf16[4,64,256]{2,1,0:T(8,128)(2,1)S(1)}, bf16[4,64,256]{2,1,0:T(8,128)(2,1)S(1)}, u32[]{:S(2)}, u32[]{:S(2)}) collective-permute-start(bf16[4,64,256]{2,1,0:T(8,128)(2,1)S(1)} %get-tuple-element.42), channel_id=1, source_target_pairs={{0,2},{1,3},{2,0},{3,1},{4,6},{5,7},{6,4},{7,5},{8,10},{9,11},{10,... | collective-permute-start | bytes 393224 | tf_op jit(solution)/shard_map/ppermute | solution.py:297
  11.2 11.5 %collective-permute-start.13 = (bf16[4,64,256]{2,1,0:T(8,128)(2,1)S(1)}, bf16[4,64,256]{2,1,0:T(8,128)(2,1)S(1)}, u32[]{:S(2)}, u32[]{:S(2)}) collective-permute-start(bf16[4,64,256]{2,1,0:T(8,128)(2,1)S(1)} %get-tuple-element.43), channel_id=1, source_target_pairs={{0,1},{1,0},{2,3},{3,2},{4,5},{5,4},{6,7},{7,6},{8,9},{9,8},{10,11... | collective-permute-start | bytes 393224 | tf_op jit(solution)/shard_map/ppermute | solution.py:297
  12.7 10.0 %collective-permute-start.14 = (bf16[4,64,256]{2,1,0:T(8,128)(2,1)S(1)}, bf16[4,64,256]{2,1,0:T(8,128)(2,1)S(1)}, u32[]{:S(2)}, u32[]{:S(2)}) collective-permute-start(bf16[4,64,256]{2,1,0:T(8,128)(2,1)S(1)} %get-tuple-element.44), channel_id=1, source_target_pairs={{0,3},{1,2},{2,1},{3,0},{4,7},{5,6},{6,5},{7,4},{8,11},{9,10},{10,... | collective-permute-start | bytes 393224 | tf_op jit(solution)/shard_map/ppermute | solution.py:297
  17.9 6.5 %collective-permute-start.4 = (bf16[256,256]{1,0:T(8,128)(2,1)S(1)}, bf16[256,256]{1,0:T(8,128)(2,1)S(1)}, u32[]{:S(2)}, u32[]{:S(2)}) collective-permute-start(bf16[256,256]{1,0:T(8,128)(2,1)S(1)} %get-tuple-element.36), channel_id=1, source_target_pairs={{0,4},{1,5},{2,6},{3,7},{4,0},{5,1},{6,2},{7,3},{8,12},{9,13},{10,... | collective-permute-start | bytes 393224 | tf_op jit(solution)/shard_map/ppermute | solution.py:297
  19.5 7.6 %collective-permute-start.7 = (bf16[256,256]{1,0:T(8,128)(2,1)S(1)}, bf16[256,256]{1,0:T(8,128)(2,1)S(1)}, u32[]{:S(2)}, u32[]{:S(2)}) collective-permute-start(bf16[256,256]{1,0:T(8,128)(2,1)S(1)} %get-tuple-element.37), channel_id=1, source_target_pairs={{0,16},{1,17},{2,18},{3,19},{4,8},{5,9},{6,10},{7,11},{8,4},{9,5},... | collective-permute-start | bytes 393224 | tf_op jit(solution)/shard_map/ppermute | solution.py:297
  19.5 9.1 %collective-permute-start.6 = (bf16[256,256]{1,0:T(8,128)(2,1)S(1)}, bf16[256,256]{1,0:T(8,128)(2,1)S(1)}, u32[]{:S(2)}, u32[]{:S(2)}) collective-permute-start(bf16[256,256]{1,0:T(8,128)(2,1)S(1)} %get-tuple-element.37), channel_id=1, source_target_pairs={{0,4},{1,5},{2,6},{3,7},{4,0},{5,1},{6,2},{7,3},{8,12},{9,13},{10,... | collective-permute-start | bytes 393224 | tf_op jit(solution)/shard_map/ppermute | solution.py:297
  24.0 6.5 %collective-permute-start.15 = (bf16[256,256]{1,0:T(8,128)(2,1)S(1)}, bf16[256,256]{1,0:T(8,128)(2,1)S(1)}, u32[]{:S(2)}, u32[]{:S(2)}) collective-permute-start(bf16[256,256]{1,0:T(8,128)(2,1)S(1)} %get-tuple-element.47), channel_id=1, source_target_pairs={{0,4},{1,5},{2,6},{3,7},{4,0},{5,1},{6,2},{7,3},{8,12},{9,13},{10,... | collective-permute-start | bytes 393224 | tf_op jit(solution)/shard_map/ppermute | solution.py:297
  24.4 10.3 %collective-permute-start.5 = (bf16[256,256]{1,0:T(8,128)(2,1)S(1)}, bf16[256,256]{1,0:T(8,128)(2,1)S(1)}, u32[]{:S(2)}, u32[]{:S(2)}) collective-permute-start(bf16[256,256]{1,0:T(8,128)(2,1)S(1)} %far.2), channel_id=1, source_target_pairs={{0,8},{1,9},{2,10},{3,11},{4,12},{5,13},{6,14},{7,15},{8,0},{9,1},... | collective-permute-start | bytes 393224 | tf_op jit(solution)/shard_map/ppermute | solution.py:297
  27.1 10.7 %collective-permute-start.18 = (bf16[256,256]{1,0:T(8,128)(2,1)S(1)}, bf16[256,256]{1,0:T(8,128)(2,1)S(1)}, u32[]{:S(2)}, u32[]{:S(2)}) collective-permute-start(bf16[256,256]{1,0:T(8,128)(2,1)S(1)} %get-tuple-element.48), channel_id=1, source_target_pairs={{0,16},{1,17},{2,18},{3,19},{4,8},{5,9},{6,10},{7,11},{8,4},{9,5},... | collective-permute-start | bytes 393224 | tf_op jit(solution)/shard_map/ppermute | solution.py:297
  27.1 11.3 %collective-permute-start.17 = (bf16[256,256]{1,0:T(8,128)(2,1)S(1)}, bf16[256,256]{1,0:T(8,128)(2,1)S(1)}, u32[]{:S(2)}, u32[]{:S(2)}) collective-permute-start(bf16[256,256]{1,0:T(8,128)(2,1)S(1)} %get-tuple-element.48), channel_id=1, source_target_pairs={{0,4},{1,5},{2,6},{3,7},{4,0},{5,1},{6,2},{7,3},{8,12},{9,13},{10,... | collective-permute-start | bytes 393224 | tf_op jit(solution)/shard_map/ppermute | solution.py:297
  30.5 10.6 %collective-permute-start.16 = (bf16[256,256]{1,0:T(8,128)(2,1)S(1)}, bf16[256,256]{1,0:T(8,128)(2,1)S(1)}, u32[]{:S(2)}, u32[]{:S(2)}) collective-permute-start(bf16[256,256]{1,0:T(8,128)(2,1)S(1)} %far.3), channel_id=1, source_target_pairs={{0,8},{1,9},{2,10},{3,11},{4,12},{5,13},{6,14},{7,15},{8,0},{9,1},... | collective-permute-start | bytes 393224 | tf_op jit(solution)/shard_map/ppermute | solution.py:297
  34.8 9.2 %collective-permute-start.8 = (bf16[128,256]{1,0:T(8,128)(2,1)S(1)}, bf16[128,256]{1,0:T(8,128)(2,1)S(1)}, u32[]{:S(2)}, u32[]{:S(2)}) collective-permute-start(bf16[128,256]{1,0:T(8,128)(2,1)S(1)} %get-tuple-element.39), channel_id=1, source_target_pairs={{0,2},{1,3},{2,0},{3,1},{4,6},{5,7},{6,4},{7,5},{8,10},{9,11},{10,... | collective-permute-start | bytes 196616 | tf_op jit(solution)/shard_map/ppermute | solution.py:297
  36.4 8.5 %collective-permute-start.9 = (bf16[128,256]{1,0:T(8,128)(2,1)S(1)}, bf16[128,256]{1,0:T(8,128)(2,1)S(1)}, u32[]{:S(2)}, u32[]{:S(2)}) collective-permute-start(bf16[128,256]{1,0:T(8,128)(2,1)S(1)} %get-tuple-element.40), channel_id=1, source_target_pairs={{0,3},{1,2},{2,1},{3,0},{4,7},{5,6},{6,5},{7,4},{8,11},{9,10},{10,... | collective-permute-start | bytes 196616 | tf_op jit(solution)/shard_map/ppermute | solution.py:297
  37.8 7.0 %collective-permute-start.10 = (bf16[128,256]{1,0:T(8,128)(2,1)S(1)}, bf16[128,256]{1,0:T(8,128)(2,1)S(1)}, u32[]{:S(2)}, u32[]{:S(2)}) collective-permute-start(bf16[128,256]{1,0:T(8,128)(2,1)S(1)} %get-tuple-element.38.refs_1_), channel_id=1, source_target_pairs={{0,1},{1,0},{2,3},{3,2},{4,5},{5,4},{6,7},{7,6},{8,9},{9,8},{10,11... | collective-permute-start | bytes 196616 | tf_op jit(solution)/shard_map/ppermute | solution.py:297
  41.2 4.3 %collective-permute-start.19 = (bf16[128,256]{1,0:T(8,128)(2,1)S(1)}, bf16[128,256]{1,0:T(8,128)(2,1)S(1)}, u32[]{:S(2)}, u32[]{:S(2)}) collective-permute-start(bf16[128,256]{1,0:T(8,128)(2,1)S(1)} %get-tuple-element.50), channel_id=1, source_target_pairs={{0,2},{1,3},{2,0},{3,1},{4,6},{5,7},{6,4},{7,5},{8,10},{9,11},{10,... | collective-permute-start | bytes 196616 | tf_op jit(solution)/shard_map/ppermute | solution.py:297
  42.6 5.2 %collective-permute-start.20 = (bf16[128,256]{1,0:T(8,128)(2,1)S(1)}, bf16[128,256]{1,0:T(8,128)(2,1)S(1)}, u32[]{:S(2)}, u32[]{:S(2)}) collective-permute-start(bf16[128,256]{1,0:T(8,128)(2,1)S(1)} %get-tuple-element.51), channel_id=1, source_target_pairs={{0,3},{1,2},{2,1},{3,0},{4,7},{5,6},{6,5},{7,4},{8,11},{9,10},{10,... | collective-permute-start | bytes 196616 | tf_op jit(solution)/shard_map/ppermute | solution.py:297
  44.0 4.9 %copy-start.1 = (bf16[4,1024,512]{2,1,0:T(8,128)(2,1)S(1)}, bf16[4,1024,512]{2,1,0:T(8,128)(2,1)}, u32[]{:S(2)}) copy-start(bf16[4,1024,512]{2,1,0:T(8,128)(2,1)} %refs_2_.2) | copy-start | bytes 12582916
  44.0 4.9 %copy-start.2 = (s32[1,4]{1,0:T(1,128)S(1)}, s32[1,4]{1,0:T(1,128)}, u32[]{:S(2)}) copy-start(s32[1,4]{1,0:T(1,128)} %refs_0_.7) | copy-start | bytes 52
  44.0 4.9 %copy-start.3 = (s32[16]{0:T(128)S(1)}, s32[16]{0:T(128)}, u32[]{:S(2)}) copy-start(s32[16]{0:T(128)} %refs_1_.1) | copy-start | bytes 196
  44.0 4.3 %collective-permute-start.21 = (bf16[128,256]{1,0:T(8,128)(2,1)S(1)}, bf16[128,256]{1,0:T(8,128)(2,1)S(1)}, u32[]{:S(2)}, u32[]{:S(2)}) collective-permute-start(bf16[128,256]{1,0:T(8,128)(2,1)S(1)} %get-tuple-element.49.refs_1_), channel_id=1, source_target_pairs={{0,1},{1,0},{2,3},{3,2},{4,5},{5,4},{6,7},{7,6},{8,9},{9,8},{10,11... | collective-permute-start | bytes 196616 | tf_op jit(solution)/shard_map/ppermute | solution.py:297
  45.3 3.6 %collective-permute-start.11 = (bf16[128,1024]{1,0:T(8,128)(2,1)S(1)}, bf16[128,1024]{1,0:T(8,128)(2,1)S(1)}, u32[]{:S(2)}, u32[]{:S(2)}) collective-permute-start(bf16[128,1024]{1,0:T(8,128)(2,1)S(1)} %phase.2.refs_3_), channel_id=1, source_target_pairs={{0,16},{1,17},{2,18},{3,19},{4,20},{5,21},{6,22},{7,23},{8,24},{9,... | collective-permute-start | bytes 786440 | tf_op jit(solution)/shard_map/ppermute | solution.py:297
  48.8 1.6 %collective-permute-start.22 = (bf16[128,1024]{1,0:T(8,128)(2,1)S(1)}, bf16[128,1024]{1,0:T(8,128)(2,1)S(1)}, u32[]{:S(2)}, u32[]{:S(2)}) collective-permute-start(bf16[128,1024]{1,0:T(8,128)(2,1)S(1)} %phase.3.refs_5_), channel_id=1, source_target_pairs={{0,16},{1,17},{2,18},{3,19},{4,20},{5,21},{6,22},{7,23},{8,24},{9,... | collective-permute-start | bytes 786440 | tf_op jit(solution)/shard_map/ppermute | solution.py:297

commit v20 on v19

--- a/solution.py
+++ b/solution.py
@@ -189,6 +189,10 @@
         out[...] = value.astype(bf16)
 
 
+def hold_kernel(value, after, out):
+    out[...] = value[...]
+
+
 def far_kernel(inner, *refs):
     ours, got, out = refs[-3:]
     _, plane, _ = position(inner)
@@ -368,7 +372,18 @@
             name="far",
         )(*earlier, third, near)
         far = sent(message, to_plane(2))
-        sums.append([ours, far, near, sent(second, to_plane(1)), sent(second, to_middle)])
+        late = second
+        if sums:
+            late = pl.pallas_call(
+                hold_kernel,
+                out_shape=shaped(depth, block),
+                in_specs=vmem(1) + unread(1),
+                out_specs=one_out,
+                compiler_params=params,
+                cost_estimate=cheap,
+                name="hold",
+            )(second, sums[0][1])
+        sums.append([ours, far, near, sent(late, to_plane(1)), sent(second, to_middle)])
 
     phases = []
     for chunk in range(own):

time: 51.7 us -> 52.9 us (1.023)
  waiting for transfers between devices: 11.9 us -> 14.4 us
  starting transfers between devices: 28.9 us -> 27.5 us
    ppermute x23, waiting for transfers between devices: 11.9 us -> 14.4 us  [sent(): return lax.ppermute(value, ('dist', 'rows'), pairs)]
    ppermute x23, starting transfers between devices: 28.9 us -> 27.5 us  [sent(): return lax.ppermute(value, ('dist', 'rows'), pairs)]
  transfers between devices with their start and end apart: 23 -> 23, of which waited for: 8 -> 9; matrix products, arithmetic and copies ran while one was open for 0% -> 0% of each run, Pallas kernels for 15% -> 14%
where the time goes in v20:
time: 52.9 us; the launch traced here: 52.7 us
  starting transfers between devices  27.5 us (52%)
  waiting for transfers between devices  14.4 us (27%)
  Pallas kernels  10.6 us (20%)
    ppermute x23, starting transfers between devices, sent(): return lax.ppermute(value, ('dist', 'rows'), pairs)  27.5 us
    ppermute x23, waiting for transfers between devices, sent(): return lax.ppermute(value, ('dist', 'rows'), pairs)  14.4 us
    pallas_call x1, Pallas kernels, plane_plan(): pl.pallas_call(lambda *refs: filter_kernel(inner, dist_dev, *refs), out_s...  2.62 us
    pallas_call x2, Pallas kernels, plane_plan(): pl.pallas_call(lambda *refs: column_kernel(inner, outer, *refs), out_shap...  2.59 us
    pallas_call x1, Pallas kernels, plane_plan(): pl.pallas_call(lambda *refs: row_kernel(inner, *refs), out_shape=[shaped(...  1.83 us
    pallas_call x1, Pallas kernels, plane_plan(): pl.pallas_call(lambda *refs: recon_kernel(own, *refs), out_shape=[jax.Sha...  1.2 us
    pallas_call x1, Pallas kernels, plane_plan(): pl.pallas_call(recon_last_kernel, out_shape=shaped(capacity, pixels), in_...  1.13 us
  transfers between devices with their start and end apart: 23, of which 9 were waited for; matrix products, arithmetic and copies ran while one was open for 0% of the time, Pallas kernels for 14%

profile of v20, /device:TPU:0, one launch (start us, length us, event | category | flops | bytes accessed | tf_op | source)
XLA Modules:
  0.0 52.7 jit_solution(10333339476317047147)
XLA Ops:
  0.0 0.0 copy-start
  0.0 0.5 collective-permute-start
  0.5 2.6 %filters.1.refs_3_.refs_1_ = bf16[4,1024,256]{2,1,0:T(8,128)(2,1)S(1)} custom-call(f32[4]{0:T(128)} %refs_0_.6), custom_call_target="tpu_custom_call" | custom-call | flops 1 | bytes 1 | tf_op jit(solution)/shard_map/filters/pallas_call | solution.py:320
  3.1 0.0 collective-permute-done.refs_1_
  3.1 0.0 copy-done
  3.1 1.8 %row_spectra.1 = (bf16[4,64,256]{2,1,0:T(8,128)(2,1)S(1)}, bf16[4,64,256]{2,1,0:T(8,128)(2,1)S(1)}, bf16[4,64,256]{2,1,0:T(8,128)(2,1)S(1)}, bf16[4,64,256]{2,1,...) custom-call(bf16[4,2,64,1024]{3,2,1,0:T(8,128)(2,1)} %bitcast.2, ...), custom_call_target="tpu_custom_call" | custom-call | flops 1 | bytes 1 | tf_op jit(solution)/shard_map/row_spectra/pallas_call | solution.py:329
  4.9 2.8 %collective-permute-start.1 = (bf16[4,64,256]{2,1,0:T(8,128)(2,1)S(1)}, bf16[4,64,256]{2,1,0:T(8,128)(2,1)S(1)}, u32[]{:S(2)}, u32[]{:S(2)}) collective-permute-start(bf16[4,64,256]{2,1,0:T(8,128)(2,1)S(1)} %get-tuple-element.31), channel_id=1, source_target_pairs={{0,2},{1,3},{2,0},{3,1},{4,6},{5,7},{6,4},{7,5},{8,10},{9,11},{10,... | collective-permute-start | bytes 393224 | tf_op jit(solution)/shard_map/ppermute | solution.py:301
  7.7 1.5 %collective-permute-start.2 = (bf16[4,64,256]{2,1,0:T(8,128)(2,1)S(1)}, bf16[4,64,256]{2,1,0:T(8,128)(2,1)S(1)}, u32[]{:S(2)}, u32[]{:S(2)}) collective-permute-start(bf16[4,64,256]{2,1,0:T(8,128)(2,1)S(1)} %get-tuple-element.32), channel_id=1, source_target_pairs={{0,1},{1,0},{2,3},{3,2},{4,5},{5,4},{6,7},{7,6},{8,9},{9,8},{10,11... | collective-permute-start | bytes 393224 | tf_op jit(solution)/shard_map/ppermute | solution.py:301
  9.2 0.0 collective-permute-start.3
  9.3 1.9 %collective-permute-start.12 = (bf16[4,64,256]{2,1,0:T(8,128)(2,1)S(1)}, bf16[4,64,256]{2,1,0:T(8,128)(2,1)S(1)}, u32[]{:S(2)}, u32[]{:S(2)}) collective-permute-start(bf16[4,64,256]{2,1,0:T(8,128)(2,1)S(1)} %get-tuple-element.42), channel_id=1, source_target_pairs={{0,2},{1,3},{2,0},{3,1},{4,6},{5,7},{6,4},{7,5},{8,10},{9,11},{10,... | collective-permute-start | bytes 393224 | tf_op jit(solution)/shard_map/ppermute | solution.py:301
  11.2 1.5 %collective-permute-start.13 = (bf16[4,64,256]{2,1,0:T(8,128)(2,1)S(1)}, bf16[4,64,256]{2,1,0:T(8,128)(2,1)S(1)}, u32[]{:S(2)}, u32[]{:S(2)}) collective-permute-start(bf16[4,64,256]{2,1,0:T(8,128)(2,1)S(1)} %get-tuple-element.43), channel_id=1, source_target_pairs={{0,1},{1,0},{2,3},{3,2},{4,5},{5,4},{6,7},{7,6},{8,9},{9,8},{10,11... | collective-permute-start | bytes 393224 | tf_op jit(solution)/shard_map/ppermute | solution.py:301
  12.7 0.0 collective-permute-done.1.refs_3_
  12.7 1.6 %collective-permute-start.14 = (bf16[4,64,256]{2,1,0:T(8,128)(2,1)S(1)}, bf16[4,64,256]{2,1,0:T(8,128)(2,1)S(1)}, u32[]{:S(2)}, u32[]{:S(2)}) collective-permute-start(bf16[4,64,256]{2,1,0:T(8,128)(2,1)S(1)} %get-tuple-element.44), channel_id=1, source_target_pairs={{0,3},{1,2},{2,1},{3,0},{4,7},{5,6},{6,5},{7,4},{8,11},{9,10},{10,... | collective-permute-start | bytes 393224 | tf_op jit(solution)/shard_map/ppermute | solution.py:301
  14.3 0.0 collective-permute-done.2.refs_4_
  14.3 2.3 %collective-permute-done.3.refs_5_ = bf16[4,64,256]{2,1,0:T(8,128)(2,1)S(1)} collective-permute-done((bf16[4,64,256]{2,1,0:T(8,128)(2,1)S(1)}, bf16[4,64,256]{2,1,0:T(8,128)(2,1)S(1)}, u32[]{:S(2)}, u32[]{:S(2)}) %collective-permute-start.3) | collective-permute-done | bytes 131104 | tf_op jit(solution)/shard_map/ppermute | solution.py:301
  16.6 1.3 %columns.2 = (bf16[256,256]{1,0:T(8,128)(2,1)S(1)}, bf16[256,256]{1,0:T(8,128)(2,1)S(1)}, bf16[256,256]{1,0:T(8,128)(2,1)S(1)}, bf16[256,256]{1,0:T(8,128)(2,1)S(1)}) custom-call(bf16[1024,1024]{1,0:T(8,128)(2,1)S(1)} %copy-done, bf16[4,1024,256]{2,1,0:T(8,128)(2,1)S(1)} %filters.1.refs_3_.refs_1_, bf16[4,64,256]{2,1,0:T(8,128)(2,1)S(1)} %get-tuple-element.30.refs_2_, ...), custom_call_target="tpu_custom_call" | custom-call | flops 1 | bytes 1 | tf_op jit(solution)/shard_map/columns/pallas_call | solution.py:348
  17.9 1.6 %collective-permute-start.4 = (bf16[256,256]{1,0:T(8,128)(2,1)S(1)}, bf16[256,256]{1,0:T(8,128)(2,1)S(1)}, u32[]{:S(2)}, u32[]{:S(2)}) collective-permute-start(bf16[256,256]{1,0:T(8,128)(2,1)S(1)} %get-tuple-element.36), channel_id=1, source_target_pairs={{0,4},{1,5},{2,6},{3,7},{4,0},{5,1},{6,2},{7,3},{8,12},{9,13},{10,... | collective-permute-start | bytes 393224 | tf_op jit(solution)/shard_map/ppermute | solution.py:301
  19.5 0.0 collective-permute-start.7
  19.5 0.0 collective-permute-done.12.refs_3_
  19.5 3.2 %collective-permute-start.6 = (bf16[256,256]{1,0:T(8,128)(2,1)S(1)}, bf16[256,256]{1,0:T(8,128)(2,1)S(1)}, u32[]{:S(2)}, u32[]{:S(2)}) collective-permute-start(bf16[256,256]{1,0:T(8,128)(2,1)S(1)} %get-tuple-element.37), channel_id=1, source_target_pairs={{0,4},{1,5},{2,6},{3,7},{4,0},{5,1},{6,2},{7,3},{8,12},{9,13},{10,... | collective-permute-start | bytes 393224 | tf_op jit(solution)/shard_map/ppermute | solution.py:301
  22.7 0.0 collective-permute-done.13.refs_4_
  22.7 0.0 collective-permute-done.14.refs_5_
  22.7 1.3 %columns.3 = (bf16[256,256]{1,0:T(8,128)(2,1)S(1)}, bf16[256,256]{1,0:T(8,128)(2,1)S(1)}, bf16[256,256]{1,0:T(8,128)(2,1)S(1)}, bf16[256,256]{1,0:T(8,128)(2,1)S(1)}) custom-call(bf16[1024,1024]{1,0:T(8,128)(2,1)S(1)} %copy-done, bf16[4,1024,256]{2,1,0:T(8,128)(2,1)S(1)} %filters.1.refs_3_.refs_1_, bf16[4,64,256]{2,1,0:T(8,128)(2,1)S(1)} %get-tuple-element.41.refs_2_, ...), custom_call_target="tpu_custom_call" | custom-call | flops 1 | bytes 1 | tf_op jit(solution)/shard_map/columns/pallas_call | solution.py:348
  24.0 0.4 collective-permute-start.15
  24.4 0.0 collective-permute-done.4.refs_1_.refs_2_
  24.4 0.1 far.2
  24.4 2.7 %collective-permute-start.5 = (bf16[256,256]{1,0:T(8,128)(2,1)S(1)}, bf16[256,256]{1,0:T(8,128)(2,1)S(1)}, u32[]{:S(2)}, u32[]{:S(2)}) collective-permute-start(bf16[256,256]{1,0:T(8,128)(2,1)S(1)} %far.2), channel_id=1, source_target_pairs={{0,8},{1,9},{2,10},{3,11},{4,12},{5,13},{6,14},{7,15},{8,0},{9,1},... | collective-permute-start | bytes 393224 | tf_op jit(solution)/shard_map/ppermute | solution.py:301
  27.1 0.0 collective-permute-start.18
  27.1 0.0 collective-permute-done.7.refs_4_.refs_1_
  27.1 0.0 collective-permute-done.6.refs_3_.refs_0_
  27.1 3.3 %collective-permute-done.15.refs_3_.refs_2_ = bf16[256,256]{1,0:T(8,128)(2,1)S(1)} collective-permute-done((bf16[256,256]{1,0:T(8,128)(2,1)S(1)}, bf16[256,256]{1,0:T(8,128)(2,1)S(1)}, u32[]{:S(2)}, u32[]{:S(2)}) %collective-permute-start.15) | collective-permute-done | bytes 131104 | tf_op jit(solution)/shard_map/ppermute | solution.py:301
  30.4 0.1 far.3
  30.4 1.6 %collective-permute-start.16 = (bf16[256,256]{1,0:T(8,128)(2,1)S(1)}, bf16[256,256]{1,0:T(8,128)(2,1)S(1)}, u32[]{:S(2)}, u32[]{:S(2)}) collective-permute-start(bf16[256,256]{1,0:T(8,128)(2,1)S(1)} %far.3), channel_id=1, source_target_pairs={{0,8},{1,9},{2,10},{3,11},{4,12},{5,13},{6,14},{7,15},{8,0},{9,1},... | collective-permute-start | bytes 393224 | tf_op jit(solution)/shard_map/ppermute | solution.py:301
  32.0 4.2 %collective-permute-done.5.refs_1_.after = bf16[256,256]{1,0:T(8,128)(2,1)S(1)} collective-permute-done((bf16[256,256]{1,0:T(8,128)(2,1)S(1)}, bf16[256,256]{1,0:T(8,128)(2,1)S(1)}, u32[]{:S(2)}, u32[]{:S(2)}) %collective-permute-start.5) | collective-permute-done | bytes 131104 | tf_op jit(solution)/shard_map/ppermute | solution.py:301
  36.2 1.0 %collective-permute-start.17 = (bf16[256,256]{1,0:T(8,128)(2,1)S(1)}, bf16[256,256]{1,0:T(8,128)(2,1)S(1)}, u32[]{:S(2)}, u32[]{:S(2)}) collective-permute-start(bf16[256,256]{1,0:T(8,128)(2,1)S(1)} %hold.1), channel_id=1, source_target_pairs={{0,4},{1,5},{2,6},{3,7},{4,0},{5,1},{6,2},{7,3},{8,12},{9,13},{10,... | collective-permute-start | bytes 393224 | tf_op jit(solution)/shard_map/ppermute | solution.py:301
  37.2 0.1 half.2
  37.3 0.3 collective-permute-start.8
  37.7 1.5 %collective-permute-start.9 = (bf16[128,256]{1,0:T(8,128)(2,1)S(1)}, bf16[128,256]{1,0:T(8,128)(2,1)S(1)}, u32[]{:S(2)}, u32[]{:S(2)}) collective-permute-start(bf16[128,256]{1,0:T(8,128)(2,1)S(1)} %get-tuple-element.40), channel_id=1, source_target_pairs={{0,3},{1,2},{2,1},{3,0},{4,7},{5,6},{6,5},{7,4},{8,11},{9,10},{10,... | collective-permute-start | bytes 196616 | tf_op jit(solution)/shard_map/ppermute | solution.py:301
  39.1 0.0 collective-permute-done.18.refs_4_
  39.1 1.8 %collective-permute-start.10 = (bf16[128,256]{1,0:T(8,128)(2,1)S(1)}, bf16[128,256]{1,0:T(8,128)(2,1)S(1)}, u32[]{:S(2)}, u32[]{:S(2)}) collective-permute-start(bf16[128,256]{1,0:T(8,128)(2,1)S(1)} %get-tuple-element.38.refs_1_), channel_id=1, source_target_pairs={{0,1},{1,0},{2,3},{3,2},{4,5},{5,4},{6,7},{7,6},{8,9},{9,8},{10,11... | collective-permute-start | bytes 196616 | tf_op jit(solution)/shard_map/ppermute | solution.py:301
  40.9 0.3 collective-permute-done.16.refs_1_
  41.2 1.3 %collective-permute-done.17.refs_3_ = bf16[256,256]{1,0:T(8,128)(2,1)S(1)} collective-permute-done((bf16[256,256]{1,0:T(8,128)(2,1)S(1)}, bf16[256,256]{1,0:T(8,128)(2,1)S(1)}, u32[]{:S(2)}, u32[]{:S(2)}) %collective-permute-start.17) | collective-permute-done | bytes 131104 | tf_op jit(solution)/shard_map/ppermute | solution.py:301
  42.5 0.1 half.3
  42.6 1.1 %collective-permute-start.19 = (bf16[128,256]{1,0:T(8,128)(2,1)S(1)}, bf16[128,256]{1,0:T(8,128)(2,1)S(1)}, u32[]{:S(2)}, u32[]{:S(2)}) collective-permute-start(bf16[128,256]{1,0:T(8,128)(2,1)S(1)} %get-tuple-element.50), channel_id=1, source_target_pairs={{0,2},{1,3},{2,0},{3,1},{4,6},{5,7},{6,4},{7,5},{8,10},{9,11},{10,... | collective-permute-start | bytes 196616 | tf_op jit(solution)/shard_map/ppermute | solution.py:301
  43.7 1.4 %collective-permute-start.20 = (bf16[128,256]{1,0:T(8,128)(2,1)S(1)}, bf16[128,256]{1,0:T(8,128)(2,1)S(1)}, u32[]{:S(2)}, u32[]{:S(2)}) collective-permute-start(bf16[128,256]{1,0:T(8,128)(2,1)S(1)} %get-tuple-element.51), channel_id=1, source_target_pairs={{0,3},{1,2},{2,1},{3,0},{4,7},{5,6},{6,5},{7,4},{8,11},{9,10},{10,... | collective-permute-start | bytes 196616 | tf_op jit(solution)/shard_map/ppermute | solution.py:301
  45.2 0.0 collective-permute-done.8.refs_2_
  45.2 0.0 copy-start.1
  45.2 1.1 %collective-permute-start.21 = (bf16[128,256]{1,0:T(8,128)(2,1)S(1)}, bf16[128,256]{1,0:T(8,128)(2,1)S(1)}, u32[]{:S(2)}, u32[]{:S(2)}) collective-permute-start(bf16[128,256]{1,0:T(8,128)(2,1)S(1)} %get-tuple-element.49.refs_1_), channel_id=1, source_target_pairs={{0,1},{1,0},{2,3},{3,2},{4,5},{5,4},{6,7},{7,6},{8,9},{9,8},{10,11... | collective-permute-start | bytes 196616 | tf_op jit(solution)/shard_map/ppermute | solution.py:301
  46.3 0.0 collective-permute-done.9.refs_3_
  46.3 0.0 collective-permute-done.10.refs_4_
  46.3 0.5 phase.2.refs_3_
  46.7 0.1 collective-permute-start.11
  46.8 0.1 collective-permute-done.19.refs_2_
  47.0 1.9 %collective-permute-done.20.refs_3_ = bf16[128,256]{1,0:T(8,128)(2,1)S(1)} collective-permute-done((bf16[128,256]{1,0:T(8,128)(2,1)S(1)}, bf16[128,256]{1,0:T(8,128)(2,1)S(1)}, u32[]{:S(2)}, u32[]{:S(2)}) %collective-permute-start.20) | collective-permute-done | bytes 65568 | tf_op jit(solution)/shard_map/ppermute | solution.py:301
  48.9 0.6 %collective-permute-done.21.refs_4_ = bf16[128,256]{1,0:T(8,128)(2,1)S(1)} collective-permute-done((bf16[128,256]{1,0:T(8,128)(2,1)S(1)}, bf16[128,256]{1,0:T(8,128)(2,1)S(1)}, u32[]{:S(2)}, u32[]{:S(2)}) %collective-permute-start.21) | collective-permute-done | bytes 65568 | tf_op jit(solution)/shard_map/ppermute | solution.py:301
  49.5 0.5 phase.3.refs_5_
  50.0 0.1 collective-permute-start.22
  50.0 0.0 collective-permute-done.11.refs_4_
  50.1 0.0 copy-done.1
  50.1 0.0 copy-done.2
  50.1 0.0 copy-done.3
  50.1 1.2 %recon.2 = (f32[128,512]{1,0:T(8,128)S(1)}, bf16[1024,512]{1,0:T(8,128)(2,1)S(1)}, bf16[128,128]{1,0:T(8,128)(2,1)S(1)}) custom-call(s32[1,4]{1,0:T(1,128)S(1)} %copy-done.2, s32[16]{0:T(128)S(1)} %copy-done.3, bf16[4,1024,512]{2,1,0:T(8,128)(2,1)S(1)} %copy-done.1, bf16[128,1024]{1,0:T(8,128)(2,1)S(1)} %phase.2.refs_3_, ...), custom_call_target="tpu_custom_call" | custom-call | flops 1 | bytes 1 | tf_op jit(solution)/shard_map/recon/pallas_call | solution.py:412
  51.3 0.3 collective-permute-done.22.phase
  51.6 1.1 %recon.3 = bf16[128,512]{1,0:T(8,128)(2,1)} custom-call(bf16[1024,512]{1,0:T(8,128)(2,1)S(1)} %get-tuple-element.52.weights, bf16[128,1024]{1,0:T(8,128)(2,1)S(1)} %collective-permute-done.22.phase, f32[128,512]{1,0:T(8,128)S(1)} %get-tuple-element.53.before, bf16[128,128]{1,0:T(8,128)(2,1)S(1)} %get-tuple-element.54.select), custom_call_target="tpu_custom_call" | custom-call | flops 1 | bytes 1 | tf_op jit(solution)/shard_map/recon/pallas_call | solution.py:425
  (3 shorter events, 0.0 us)
Async XLA Ops:
  0.0 3.1 %copy-start = (bf16[1024,1024]{1,0:T(8,128)(2,1)S(1)}, bf16[1024,1024]{1,0:T(8,128)(2,1)}, u32[]{:S(2)}) copy-start(bf16[1024,1024]{1,0:T(8,128)(2,1)} %constant.2.clone.refs_2_.refs_0_) | copy-start | bytes 6291460
  0.0 3.1 %collective-permute-start = (bf16[4,2,64,1024]{3,2,1,0:T(8,128)(2,1)}, bf16[4,2,64,1024]{3,2,1,0:T(8,128)(2,1)S(1)}, u32[]{:S(2)}, u32[]{:S(2)}) collective-permute-start(bf16[4,2,64,1024]{3,2,1,0:T(8,128)(2,1)} %bitcast.1), channel_id=1, source_target_pairs={{0,16},{1,17},{2,18},{3,19},{4,20},{5,21},{6,22},{7,23},{8,24},{9,... | collective-permute-start | bytes 3145736 | tf_op jit(solution)/shard_map/ppermute | solution.py:301
  4.9 7.8 %collective-permute-start.1 = (bf16[4,64,256]{2,1,0:T(8,128)(2,1)S(1)}, bf16[4,64,256]{2,1,0:T(8,128)(2,1)S(1)}, u32[]{:S(2)}, u32[]{:S(2)}) collective-permute-start(bf16[4,64,256]{2,1,0:T(8,128)(2,1)S(1)} %get-tuple-element.31), channel_id=1, source_target_pairs={{0,2},{1,3},{2,0},{3,1},{4,6},{5,7},{6,4},{7,5},{8,10},{9,11},{10,... | collective-permute-start | bytes 393224 | tf_op jit(solution)/shard_map/ppermute | solution.py:301
  7.7 6.6 %collective-permute-start.2 = (bf16[4,64,256]{2,1,0:T(8,128)(2,1)S(1)}, bf16[4,64,256]{2,1,0:T(8,128)(2,1)S(1)}, u32[]{:S(2)}, u32[]{:S(2)}) collective-permute-start(bf16[4,64,256]{2,1,0:T(8,128)(2,1)S(1)} %get-tuple-element.32), channel_id=1, source_target_pairs={{0,1},{1,0},{2,3},{3,2},{4,5},{5,4},{6,7},{7,6},{8,9},{9,8},{10,11... | collective-permute-start | bytes 393224 | tf_op jit(solution)/shard_map/ppermute | solution.py:301
  9.2 7.4 %collective-permute-start.3 = (bf16[4,64,256]{2,1,0:T(8,128)(2,1)S(1)}, bf16[4,64,256]{2,1,0:T(8,128)(2,1)S(1)}, u32[]{:S(2)}, u32[]{:S(2)}) collective-permute-start(bf16[4,64,256]{2,1,0:T(8,128)(2,1)S(1)} %get-tuple-element.33), channel_id=1, source_target_pairs={{0,3},{1,2},{2,1},{3,0},{4,7},{5,6},{6,5},{7,4},{8,11},{9,10},{10,... | collective-permute-start | bytes 393224 | tf_op jit(solution)/shard_map/ppermute | solution.py:301
  9.3 10.3 %collective-permute-start.12 = (bf16[4,64,256]{2,1,0:T(8,128)(2,1)S(1)}, bf16[4,64,256]{2,1,0:T(8,128)(2,1)S(1)}, u32[]{:S(2)}, u32[]{:S(2)}) collective-permute-start(bf16[4,64,256]{2,1,0:T(8,128)(2,1)S(1)} %get-tuple-element.42), channel_id=1, source_target_pairs={{0,2},{1,3},{2,0},{3,1},{4,6},{5,7},{6,4},{7,5},{8,10},{9,11},{10,... | collective-permute-start | bytes 393224 | tf_op jit(solution)/shard_map/ppermute | solution.py:301
  11.2 11.5 %collective-permute-start.13 = (bf16[4,64,256]{2,1,0:T(8,128)(2,1)S(1)}, bf16[4,64,256]{2,1,0:T(8,128)(2,1)S(1)}, u32[]{:S(2)}, u32[]{:S(2)}) collective-permute-start(bf16[4,64,256]{2,1,0:T(8,128)(2,1)S(1)} %get-tuple-element.43), channel_id=1, source_target_pairs={{0,1},{1,0},{2,3},{3,2},{4,5},{5,4},{6,7},{7,6},{8,9},{9,8},{10,11... | collective-permute-start | bytes 393224 | tf_op jit(solution)/shard_map/ppermute | solution.py:301
  12.7 10.0 %collective-permute-start.14 = (bf16[4,64,256]{2,1,0:T(8,128)(2,1)S(1)}, bf16[4,64,256]{2,1,0:T(8,128)(2,1)S(1)}, u32[]{:S(2)}, u32[]{:S(2)}) collective-permute-start(bf16[4,64,256]{2,1,0:T(8,128)(2,1)S(1)} %get-tuple-element.44), channel_id=1, source_target_pairs={{0,3},{1,2},{2,1},{3,0},{4,7},{5,6},{6,5},{7,4},{8,11},{9,10},{10,... | collective-permute-start | bytes 393224 | tf_op jit(solution)/shard_map/ppermute | solution.py:301
  17.9 6.5 %collective-permute-start.4 = (bf16[256,256]{1,0:T(8,128)(2,1)S(1)}, bf16[256,256]{1,0:T(8,128)(2,1)S(1)}, u32[]{:S(2)}, u32[]{:S(2)}) collective-permute-start(bf16[256,256]{1,0:T(8,128)(2,1)S(1)} %get-tuple-element.36), channel_id=1, source_target_pairs={{0,4},{1,5},{2,6},{3,7},{4,0},{5,1},{6,2},{7,3},{8,12},{9,13},{10,... | collective-permute-start | bytes 393224 | tf_op jit(solution)/shard_map/ppermute | solution.py:301
  19.5 7.6 %collective-permute-start.7 = (bf16[256,256]{1,0:T(8,128)(2,1)S(1)}, bf16[256,256]{1,0:T(8,128)(2,1)S(1)}, u32[]{:S(2)}, u32[]{:S(2)}) collective-permute-start(bf16[256,256]{1,0:T(8,128)(2,1)S(1)} %get-tuple-element.37), channel_id=1, source_target_pairs={{0,16},{1,17},{2,18},{3,19},{4,8},{5,9},{6,10},{7,11},{8,4},{9,5},... | collective-permute-start | bytes 393224 | tf_op jit(solution)/shard_map/ppermute | solution.py:301
  19.5 7.6 %collective-permute-start.6 = (bf16[256,256]{1,0:T(8,128)(2,1)S(1)}, bf16[256,256]{1,0:T(8,128)(2,1)S(1)}, u32[]{:S(2)}, u32[]{:S(2)}) collective-permute-start(bf16[256,256]{1,0:T(8,128)(2,1)S(1)} %get-tuple-element.37), channel_id=1, source_target_pairs={{0,4},{1,5},{2,6},{3,7},{4,0},{5,1},{6,2},{7,3},{8,12},{9,13},{10,... | collective-permute-start | bytes 393224 | tf_op jit(solution)/shard_map/ppermute | solution.py:301
  24.0 6.4 %collective-permute-start.15 = (bf16[256,256]{1,0:T(8,128)(2,1)S(1)}, bf16[256,256]{1,0:T(8,128)(2,1)S(1)}, u32[]{:S(2)}, u32[]{:S(2)}) collective-permute-start(bf16[256,256]{1,0:T(8,128)(2,1)S(1)} %get-tuple-element.47), channel_id=1, source_target_pairs={{0,4},{1,5},{2,6},{3,7},{4,0},{5,1},{6,2},{7,3},{8,12},{9,13},{10,... | collective-permute-start | bytes 393224 | tf_op jit(solution)/shard_map/ppermute | solution.py:301
  24.4 11.8 %collective-permute-start.5 = (bf16[256,256]{1,0:T(8,128)(2,1)S(1)}, bf16[256,256]{1,0:T(8,128)(2,1)S(1)}, u32[]{:S(2)}, u32[]{:S(2)}) collective-permute-start(bf16[256,256]{1,0:T(8,128)(2,1)S(1)} %far.2), channel_id=1, source_target_pairs={{0,8},{1,9},{2,10},{3,11},{4,12},{5,13},{6,14},{7,15},{8,0},{9,1},... | collective-permute-start | bytes 393224 | tf_op jit(solution)/shard_map/ppermute | solution.py:301
  27.1 12.0 %collective-permute-start.18 = (bf16[256,256]{1,0:T(8,128)(2,1)S(1)}, bf16[256,256]{1,0:T(8,128)(2,1)S(1)}, u32[]{:S(2)}, u32[]{:S(2)}) collective-permute-start(bf16[256,256]{1,0:T(8,128)(2,1)S(1)} %get-tuple-element.48.value), channel_id=1, source_target_pairs={{0,16},{1,17},{2,18},{3,19},{4,8},{5,9},{6,10},{7,11},{8,4},{9,5},... | collective-permute-start | bytes 393224 | tf_op jit(solution)/shard_map/ppermute | solution.py:301
  30.4 10.8 %collective-permute-start.16 = (bf16[256,256]{1,0:T(8,128)(2,1)S(1)}, bf16[256,256]{1,0:T(8,128)(2,1)S(1)}, u32[]{:S(2)}, u32[]{:S(2)}) collective-permute-start(bf16[256,256]{1,0:T(8,128)(2,1)S(1)} %far.3), channel_id=1, source_target_pairs={{0,8},{1,9},{2,10},{3,11},{4,12},{5,13},{6,14},{7,15},{8,0},{9,1},... | collective-permute-start | bytes 393224 | tf_op jit(solution)/shard_map/ppermute | solution.py:301
  36.2 6.3 %collective-permute-start.17 = (bf16[256,256]{1,0:T(8,128)(2,1)S(1)}, bf16[256,256]{1,0:T(8,128)(2,1)S(1)}, u32[]{:S(2)}, u32[]{:S(2)}) collective-permute-start(bf16[256,256]{1,0:T(8,128)(2,1)S(1)} %hold.1), channel_id=1, source_target_pairs={{0,4},{1,5},{2,6},{3,7},{4,0},{5,1},{6,2},{7,3},{8,12},{9,13},{10,... | collective-permute-start | bytes 393224 | tf_op jit(solution)/shard_map/ppermute | solution.py:301
  37.3 7.8 %collective-permute-start.8 = (bf16[128,256]{1,0:T(8,128)(2,1)S(1)}, bf16[128,256]{1,0:T(8,128)(2,1)S(1)}, u32[]{:S(2)}, u32[]{:S(2)}) collective-permute-start(bf16[128,256]{1,0:T(8,128)(2,1)S(1)} %get-tuple-element.39), channel_id=1, source_target_pairs={{0,2},{1,3},{2,0},{3,1},{4,6},{5,7},{6,4},{7,5},{8,10},{9,11},{10,... | collective-permute-start | bytes 196616 | tf_op jit(solution)/shard_map/ppermute | solution.py:301
  37.7 8.6 %collective-permute-start.9 = (bf16[128,256]{1,0:T(8,128)(2,1)S(1)}, bf16[128,256]{1,0:T(8,128)(2,1)S(1)}, u32[]{:S(2)}, u32[]{:S(2)}) collective-permute-start(bf16[128,256]{1,0:T(8,128)(2,1)S(1)} %get-tuple-element.40), channel_id=1, source_target_pairs={{0,3},{1,2},{2,1},{3,0},{4,7},{5,6},{6,5},{7,4},{8,11},{9,10},{10,... | collective-permute-start | bytes 196616 | tf_op jit(solution)/shard_map/ppermute | solution.py:301
  39.1 7.1 %collective-permute-start.10 = (bf16[128,256]{1,0:T(8,128)(2,1)S(1)}, bf16[128,256]{1,0:T(8,128)(2,1)S(1)}, u32[]{:S(2)}, u32[]{:S(2)}) collective-permute-start(bf16[128,256]{1,0:T(8,128)(2,1)S(1)} %get-tuple-element.38.refs_1_), channel_id=1, source_target_pairs={{0,1},{1,0},{2,3},{3,2},{4,5},{5,4},{6,7},{7,6},{8,9},{9,8},{10,11... | collective-permute-start | bytes 196616 | tf_op jit(solution)/shard_map/ppermute | solution.py:301
  42.6 4.3 %collective-permute-start.19 = (bf16[128,256]{1,0:T(8,128)(2,1)S(1)}, bf16[128,256]{1,0:T(8,128)(2,1)S(1)}, u32[]{:S(2)}, u32[]{:S(2)}) collective-permute-start(bf16[128,256]{1,0:T(8,128)(2,1)S(1)} %get-tuple-element.50), channel_id=1, source_target_pairs={{0,2},{1,3},{2,0},{3,1},{4,6},{5,7},{6,4},{7,5},{8,10},{9,11},{10,... | collective-permute-start | bytes 196616 | tf_op jit(solution)/shard_map/ppermute | solution.py:301
  43.7 5.2 %collective-permute-start.20 = (bf16[128,256]{1,0:T(8,128)(2,1)S(1)}, bf16[128,256]{1,0:T(8,128)(2,1)S(1)}, u32[]{:S(2)}, u32[]{:S(2)}) collective-permute-start(bf16[128,256]{1,0:T(8,128)(2,1)S(1)} %get-tuple-element.51), channel_id=1, source_target_pairs={{0,3},{1,2},{2,1},{3,0},{4,7},{5,6},{6,5},{7,4},{8,11},{9,10},{10,... | collective-permute-start | bytes 196616 | tf_op jit(solution)/shard_map/ppermute | solution.py:301
  45.2 4.9 %copy-start.1 = (bf16[4,1024,512]{2,1,0:T(8,128)(2,1)S(1)}, bf16[4,1024,512]{2,1,0:T(8,128)(2,1)}, u32[]{:S(2)}) copy-start(bf16[4,1024,512]{2,1,0:T(8,128)(2,1)} %refs_2_.2) | copy-start | bytes 12582916
  45.2 4.9 %copy-start.2 = (s32[1,4]{1,0:T(1,128)S(1)}, s32[1,4]{1,0:T(1,128)}, u32[]{:S(2)}) copy-start(s32[1,4]{1,0:T(1,128)} %refs_0_.7) | copy-start | bytes 52
  45.2 4.9 %copy-start.3 = (s32[16]{0:T(128)S(1)}, s32[16]{0:T(128)}, u32[]{:S(2)}) copy-start(s32[16]{0:T(128)} %refs_1_.1) | copy-start | bytes 196
  45.2 4.3 %collective-permute-start.21 = (bf16[128,256]{1,0:T(8,128)(2,1)S(1)}, bf16[128,256]{1,0:T(8,128)(2,1)S(1)}, u32[]{:S(2)}, u32[]{:S(2)}) collective-permute-start(bf16[128,256]{1,0:T(8,128)(2,1)S(1)} %get-tuple-element.49.refs_1_), channel_id=1, source_target_pairs={{0,1},{1,0},{2,3},{3,2},{4,5},{5,4},{6,7},{7,6},{8,9},{9,8},{10,11... | collective-permute-start | bytes 196616 | tf_op jit(solution)/shard_map/ppermute | solution.py:301
  46.7 3.3 %collective-permute-start.11 = (bf16[128,1024]{1,0:T(8,128)(2,1)S(1)}, bf16[128,1024]{1,0:T(8,128)(2,1)S(1)}, u32[]{:S(2)}, u32[]{:S(2)}) collective-permute-start(bf16[128,1024]{1,0:T(8,128)(2,1)S(1)} %phase.2.refs_3_), channel_id=1, source_target_pairs={{0,16},{1,17},{2,18},{3,19},{4,20},{5,21},{6,22},{7,23},{8,24},{9,... | collective-permute-start | bytes 786440 | tf_op jit(solution)/shard_map/ppermute | solution.py:301
  50.0 1.6 %collective-permute-start.22 = (bf16[128,1024]{1,0:T(8,128)(2,1)S(1)}, bf16[128,1024]{1,0:T(8,128)(2,1)S(1)}, u32[]{:S(2)}, u32[]{:S(2)}) collective-permute-start(bf16[128,1024]{1,0:T(8,128)(2,1)S(1)} %phase.3.refs_5_), channel_id=1, source_target_pairs={{0,16},{1,17},{2,18},{3,19},{4,20},{5,21},{6,22},{7,23},{8,24},{9,... | collective-permute-start | bytes 786440 | tf_op jit(solution)/shard_map/ppermute | solution.py:301

commit v21 on v19

--- a/solution.py
+++ b/solution.py
@@ -293,7 +293,8 @@
         for c in range(cores):
             for r in range(groups):
                 to_core, to_row = target(c, r)
-                pairs.append((c * groups + r, to_core * groups + to_row))
+                if to_row is not None:
+                    pairs.append((c * groups + r, to_core * groups + to_row))
         return lax.ppermute(value, ("dist", "rows"), pairs)
 
     def to_other_core(c, r):
@@ -307,6 +308,10 @@
 
     def to_plane(rel):
         return lambda c, r: (c, (r // inner ^ rel) * inner + r % inner)
+
+    def from_ends(c, r):
+        z = r // inner
+        return c, None if z in (1, 2) else (z ^ 1) * inner + r % inner
 
     def to_middle(c, r):
         z = r // inner
@@ -368,7 +373,7 @@
             name="far",
         )(*earlier, third, near)
         far = sent(message, to_plane(2))
-        sums.append([ours, far, near, sent(second, to_plane(1)), sent(second, to_middle)])
+        sums.append([ours, far, near, sent(second, from_ends), sent(second, to_middle)])
 
     phases = []
     for chunk in range(own):

time: 51.7 us -> 52 us (level)
  starting transfers between devices: 28.9 us -> 30.8 us
  waiting for transfers between devices: 11.9 us -> 10.1 us
    ppermute x23, starting transfers between devices: 28.9 us -> 30.8 us  [sent(): return lax.ppermute(value, ('dist', 'rows'), pairs)]
    ppermute x23, waiting for transfers between devices: 11.9 us -> 10.1 us  [sent(): return lax.ppermute(value, ('dist', 'rows'), pairs)]
  transfers between devices with their start and end apart: 23 -> 23, of which waited for: 8 -> 7; matrix products, arithmetic and copies ran while one was open for 0% -> 0% of each run, Pallas kernels for 15% -> 15%
where the time goes in v21:
time: 52 us; the launch traced here: 51.7 us
  starting transfers between devices  30.8 us (59%)
  Pallas kernels  10.6 us (20%)
  waiting for transfers between devices  10.1 us (19%)
    ppermute x23, starting transfers between devices, sent(): return lax.ppermute(value, ('dist', 'rows'), pairs)  30.8 us
    ppermute x23, waiting for transfers between devices, sent(): return lax.ppermute(value, ('dist', 'rows'), pairs)  10.1 us
    pallas_call x1, Pallas kernels, plane_plan(): pl.pallas_call(lambda *refs: filter_kernel(inner, dist_dev, *refs), out_s...  2.62 us
    pallas_call x2, Pallas kernels, plane_plan(): pl.pallas_call(lambda *refs: column_kernel(inner, outer, *refs), out_shap...  2.59 us
    pallas_call x1, Pallas kernels, plane_plan(): pl.pallas_call(lambda *refs: row_kernel(inner, *refs), out_shape=[shaped(...  1.83 us
    pallas_call x1, Pallas kernels, plane_plan(): pl.pallas_call(lambda *refs: recon_kernel(own, *refs), out_shape=[jax.Sha...  1.2 us
    pallas_call x1, Pallas kernels, plane_plan(): pl.pallas_call(recon_last_kernel, out_shape=shaped(capacity, pixels), in_...  1.12 us
  transfers between devices with their start and end apart: 23, of which 7 were waited for; matrix products, arithmetic and copies ran while one was open for 0% of the time, Pallas kernels for 15%

profile of v21, /device:TPU:0, one launch (start us, length us, event | category | flops | bytes accessed | tf_op | source)
XLA Modules:
  0.0 51.7 jit_solution(13778159547401885730)
XLA Ops:
  0.0 0.0 copy-start
  0.0 0.5 collective-permute-start
  0.5 2.6 %filters.1.refs_3_.refs_1_ = bf16[4,1024,256]{2,1,0:T(8,128)(2,1)S(1)} custom-call(f32[4]{0:T(128)} %refs_0_.6), custom_call_target="tpu_custom_call" | custom-call | flops 1 | bytes 1 | tf_op jit(solution)/shard_map/filters/pallas_call | solution.py:321
  3.1 0.0 collective-permute-done.refs_1_
  3.1 0.0 copy-done
  3.1 1.8 %row_spectra.1 = (bf16[4,64,256]{2,1,0:T(8,128)(2,1)S(1)}, bf16[4,64,256]{2,1,0:T(8,128)(2,1)S(1)}, bf16[4,64,256]{2,1,0:T(8,128)(2,1)S(1)}, bf16[4,64,256]{2,1,...) custom-call(bf16[4,2,64,1024]{3,2,1,0:T(8,128)(2,1)} %bitcast.2, ...), custom_call_target="tpu_custom_call" | custom-call | flops 1 | bytes 1 | tf_op jit(solution)/shard_map/row_spectra/pallas_call | solution.py:330
  4.9 2.8 %collective-permute-start.1 = (bf16[4,64,256]{2,1,0:T(8,128)(2,1)S(1)}, bf16[4,64,256]{2,1,0:T(8,128)(2,1)S(1)}, u32[]{:S(2)}, u32[]{:S(2)}) collective-permute-start(bf16[4,64,256]{2,1,0:T(8,128)(2,1)S(1)} %get-tuple-element.31), channel_id=1, source_target_pairs={{0,2},{1,3},{2,0},{3,1},{4,6},{5,7},{6,4},{7,5},{8,10},{9,11},{10,... | collective-permute-start | bytes 393224 | tf_op jit(solution)/shard_map/ppermute | solution.py:298
  7.7 1.5 %collective-permute-start.2 = (bf16[4,64,256]{2,1,0:T(8,128)(2,1)S(1)}, bf16[4,64,256]{2,1,0:T(8,128)(2,1)S(1)}, u32[]{:S(2)}, u32[]{:S(2)}) collective-permute-start(bf16[4,64,256]{2,1,0:T(8,128)(2,1)S(1)} %get-tuple-element.32), channel_id=1, source_target_pairs={{0,1},{1,0},{2,3},{3,2},{4,5},{5,4},{6,7},{7,6},{8,9},{9,8},{10,11... | collective-permute-start | bytes 393224 | tf_op jit(solution)/shard_map/ppermute | solution.py:298
  9.2 0.0 collective-permute-start.3
  9.3 1.9 %collective-permute-start.12 = (bf16[4,64,256]{2,1,0:T(8,128)(2,1)S(1)}, bf16[4,64,256]{2,1,0:T(8,128)(2,1)S(1)}, u32[]{:S(2)}, u32[]{:S(2)}) collective-permute-start(bf16[4,64,256]{2,1,0:T(8,128)(2,1)S(1)} %get-tuple-element.42), channel_id=1, source_target_pairs={{0,2},{1,3},{2,0},{3,1},{4,6},{5,7},{6,4},{7,5},{8,10},{9,11},{10,... | collective-permute-start | bytes 393224 | tf_op jit(solution)/shard_map/ppermute | solution.py:298
  11.2 1.5 %collective-permute-start.13 = (bf16[4,64,256]{2,1,0:T(8,128)(2,1)S(1)}, bf16[4,64,256]{2,1,0:T(8,128)(2,1)S(1)}, u32[]{:S(2)}, u32[]{:S(2)}) collective-permute-start(bf16[4,64,256]{2,1,0:T(8,128)(2,1)S(1)} %get-tuple-element.43), channel_id=1, source_target_pairs={{0,1},{1,0},{2,3},{3,2},{4,5},{5,4},{6,7},{7,6},{8,9},{9,8},{10,11... | collective-permute-start | bytes 393224 | tf_op jit(solution)/shard_map/ppermute | solution.py:298
  12.7 0.0 collective-permute-done.1.refs_3_
  12.7 1.6 %collective-permute-start.14 = (bf16[4,64,256]{2,1,0:T(8,128)(2,1)S(1)}, bf16[4,64,256]{2,1,0:T(8,128)(2,1)S(1)}, u32[]{:S(2)}, u32[]{:S(2)}) collective-permute-start(bf16[4,64,256]{2,1,0:T(8,128)(2,1)S(1)} %get-tuple-element.44), channel_id=1, source_target_pairs={{0,3},{1,2},{2,1},{3,0},{4,7},{5,6},{6,5},{7,4},{8,11},{9,10},{10,... | collective-permute-start | bytes 393224 | tf_op jit(solution)/shard_map/ppermute | solution.py:298
  14.3 0.0 collective-permute-done.2.refs_4_
  14.3 2.3 %collective-permute-done.3.refs_5_ = bf16[4,64,256]{2,1,0:T(8,128)(2,1)S(1)} collective-permute-done((bf16[4,64,256]{2,1,0:T(8,128)(2,1)S(1)}, bf16[4,64,256]{2,1,0:T(8,128)(2,1)S(1)}, u32[]{:S(2)}, u32[]{:S(2)}) %collective-permute-start.3) | collective-permute-done | bytes 131104 | tf_op jit(solution)/shard_map/ppermute | solution.py:298
  16.6 1.3 %columns.2 = (bf16[256,256]{1,0:T(8,128)(2,1)S(1)}, bf16[256,256]{1,0:T(8,128)(2,1)S(1)}, bf16[256,256]{1,0:T(8,128)(2,1)S(1)}, bf16[256,256]{1,0:T(8,128)(2,1)S(1)}) custom-call(bf16[1024,1024]{1,0:T(8,128)(2,1)S(1)} %copy-done, bf16[4,1024,256]{2,1,0:T(8,128)(2,1)S(1)} %filters.1.refs_3_.refs_1_, bf16[4,64,256]{2,1,0:T(8,128)(2,1)S(1)} %get-tuple-element.30.refs_2_, ...), custom_call_target="tpu_custom_call" | custom-call | flops 1 | bytes 1 | tf_op jit(solution)/shard_map/columns/pallas_call | solution.py:349
  17.9 1.6 %collective-permute-start.4 = (bf16[256,256]{1,0:T(8,128)(2,1)S(1)}, bf16[256,256]{1,0:T(8,128)(2,1)S(1)}, u32[]{:S(2)}, u32[]{:S(2)}) collective-permute-start(bf16[256,256]{1,0:T(8,128)(2,1)S(1)} %get-tuple-element.36), channel_id=1, source_target_pairs={{0,4},{1,5},{2,6},{3,7},{4,0},{5,1},{6,2},{7,3},{8,12},{9,13},{10,... | collective-permute-start | bytes 393224 | tf_op jit(solution)/shard_map/ppermute | solution.py:298
  19.5 0.0 collective-permute-start.7
  19.5 0.0 collective-permute-done.12.refs_3_
  19.5 5.1 %collective-permute-start.6 = (bf16[256,256]{1,0:T(8,128)(2,1)S(1)}, bf16[256,256]{1,0:T(8,128)(2,1)S(1)}, u32[]{:S(2)}, u32[]{:S(2)}) collective-permute-start(bf16[256,256]{1,0:T(8,128)(2,1)S(1)} %get-tuple-element.37), channel_id=1, source_target_pairs={{0,4},{1,5},{2,6},{3,7},{12,8},{13,9},{14,10},{15,11},{16,20},{17,... | collective-permute-start | bytes 393224 | tf_op jit(solution)/shard_map/ppermute | solution.py:298
  24.6 0.0 collective-permute-done.13.refs_4_
  24.6 0.0 collective-permute-done.14.refs_5_
  24.6 1.3 %columns.3 = (bf16[256,256]{1,0:T(8,128)(2,1)S(1)}, bf16[256,256]{1,0:T(8,128)(2,1)S(1)}, bf16[256,256]{1,0:T(8,128)(2,1)S(1)}, bf16[256,256]{1,0:T(8,128)(2,1)S(1)}) custom-call(bf16[1024,1024]{1,0:T(8,128)(2,1)S(1)} %copy-done, bf16[4,1024,256]{2,1,0:T(8,128)(2,1)S(1)} %filters.1.refs_3_.refs_1_, bf16[4,64,256]{2,1,0:T(8,128)(2,1)S(1)} %get-tuple-element.41.refs_2_, ...), custom_call_target="tpu_custom_call" | custom-call | flops 1 | bytes 1 | tf_op jit(solution)/shard_map/columns/pallas_call | solution.py:349
  25.9 0.1 collective-permute-start.15
  26.0 0.0 collective-permute-done.4.refs_1_.refs_2_
  26.0 0.1 far.2
  26.1 1.5 %collective-permute-start.5 = (bf16[256,256]{1,0:T(8,128)(2,1)S(1)}, bf16[256,256]{1,0:T(8,128)(2,1)S(1)}, u32[]{:S(2)}, u32[]{:S(2)}) collective-permute-start(bf16[256,256]{1,0:T(8,128)(2,1)S(1)} %far.2), channel_id=1, source_target_pairs={{0,8},{1,9},{2,10},{3,11},{4,12},{5,13},{6,14},{7,15},{8,0},{9,1},... | collective-permute-start | bytes 393224 | tf_op jit(solution)/shard_map/ppermute | solution.py:298
  27.6 0.0 collective-permute-start.18
  27.6 0.0 collective-permute-done.7.refs_4_.refs_1_
  27.6 3.9 %collective-permute-start.17 = (bf16[256,256]{1,0:T(8,128)(2,1)S(1)}, bf16[256,256]{1,0:T(8,128)(2,1)S(1)}, u32[]{:S(2)}, u32[]{:S(2)}) collective-permute-start(bf16[256,256]{1,0:T(8,128)(2,1)S(1)} %get-tuple-element.48), channel_id=1, source_target_pairs={{0,4},{1,5},{2,6},{3,7},{12,8},{13,9},{14,10},{15,11},{16,20},{17,... | collective-permute-start | bytes 393224 | tf_op jit(solution)/shard_map/ppermute | solution.py:298
  31.5 0.0 collective-permute-done.6.refs_3_.refs_0_
  31.5 0.0 collective-permute-done.15.refs_3_.refs_2_
  31.6 0.1 far.3
  31.6 1.5 %collective-permute-start.16 = (bf16[256,256]{1,0:T(8,128)(2,1)S(1)}, bf16[256,256]{1,0:T(8,128)(2,1)S(1)}, u32[]{:S(2)}, u32[]{:S(2)}) collective-permute-start(bf16[256,256]{1,0:T(8,128)(2,1)S(1)} %far.3), channel_id=1, source_target_pairs={{0,8},{1,9},{2,10},{3,11},{4,12},{5,13},{6,14},{7,15},{8,0},{9,1},... | collective-permute-start | bytes 393224 | tf_op jit(solution)/shard_map/ppermute | solution.py:298
  33.1 1.8 %collective-permute-done.5.refs_1_ = bf16[256,256]{1,0:T(8,128)(2,1)S(1)} collective-permute-done((bf16[256,256]{1,0:T(8,128)(2,1)S(1)}, bf16[256,256]{1,0:T(8,128)(2,1)S(1)}, u32[]{:S(2)}, u32[]{:S(2)}) %collective-permute-start.5) | collective-permute-done | bytes 131104 | tf_op jit(solution)/shard_map/ppermute | solution.py:298
  34.9 0.1 half.2
  35.0 0.9 %collective-permute-start.8 = (bf16[128,256]{1,0:T(8,128)(2,1)S(1)}, bf16[128,256]{1,0:T(8,128)(2,1)S(1)}, u32[]{:S(2)}, u32[]{:S(2)}) collective-permute-start(bf16[128,256]{1,0:T(8,128)(2,1)S(1)} %get-tuple-element.39), channel_id=1, source_target_pairs={{0,2},{1,3},{2,0},{3,1},{4,6},{5,7},{6,4},{7,5},{8,10},{9,11},{10,... | collective-permute-start | bytes 196616 | tf_op jit(solution)/shard_map/ppermute | solution.py:298
  36.0 1.4 %collective-permute-start.9 = (bf16[128,256]{1,0:T(8,128)(2,1)S(1)}, bf16[128,256]{1,0:T(8,128)(2,1)S(1)}, u32[]{:S(2)}, u32[]{:S(2)}) collective-permute-start(bf16[128,256]{1,0:T(8,128)(2,1)S(1)} %get-tuple-element.40), channel_id=1, source_target_pairs={{0,3},{1,2},{2,1},{3,0},{4,7},{5,6},{6,5},{7,4},{8,11},{9,10},{10,... | collective-permute-start | bytes 196616 | tf_op jit(solution)/shard_map/ppermute | solution.py:298
  37.4 0.0 collective-permute-done.18.refs_4_
  37.4 1.2 %collective-permute-start.10 = (bf16[128,256]{1,0:T(8,128)(2,1)S(1)}, bf16[128,256]{1,0:T(8,128)(2,1)S(1)}, u32[]{:S(2)}, u32[]{:S(2)}) collective-permute-start(bf16[128,256]{1,0:T(8,128)(2,1)S(1)} %get-tuple-element.38.refs_1_), channel_id=1, source_target_pairs={{0,1},{1,0},{2,3},{3,2},{4,5},{5,4},{6,7},{7,6},{8,9},{9,8},{10,11... | collective-permute-start | bytes 196616 | tf_op jit(solution)/shard_map/ppermute | solution.py:298
  38.6 0.0 collective-permute-done.17.refs_3_
  38.6 2.9 %collective-permute-done.16.refs_1_ = bf16[256,256]{1,0:T(8,128)(2,1)S(1)} collective-permute-done((bf16[256,256]{1,0:T(8,128)(2,1)S(1)}, bf16[256,256]{1,0:T(8,128)(2,1)S(1)}, u32[]{:S(2)}, u32[]{:S(2)}) %collective-permute-start.16) | collective-permute-done | bytes 131104 | tf_op jit(solution)/shard_map/ppermute | solution.py:298
  41.5 0.1 half.3
  41.6 1.2 %collective-permute-start.19 = (bf16[128,256]{1,0:T(8,128)(2,1)S(1)}, bf16[128,256]{1,0:T(8,128)(2,1)S(1)}, u32[]{:S(2)}, u32[]{:S(2)}) collective-permute-start(bf16[128,256]{1,0:T(8,128)(2,1)S(1)} %get-tuple-element.50), channel_id=1, source_target_pairs={{0,2},{1,3},{2,0},{3,1},{4,6},{5,7},{6,4},{7,5},{8,10},{9,11},{10,... | collective-permute-start | bytes 196616 | tf_op jit(solution)/shard_map/ppermute | solution.py:298
  42.8 1.4 %collective-permute-start.20 = (bf16[128,256]{1,0:T(8,128)(2,1)S(1)}, bf16[128,256]{1,0:T(8,128)(2,1)S(1)}, u32[]{:S(2)}, u32[]{:S(2)}) collective-permute-start(bf16[128,256]{1,0:T(8,128)(2,1)S(1)} %get-tuple-element.51), channel_id=1, source_target_pairs={{0,3},{1,2},{2,1},{3,0},{4,7},{5,6},{6,5},{7,4},{8,11},{9,10},{10,... | collective-permute-start | bytes 196616 | tf_op jit(solution)/shard_map/ppermute | solution.py:298
  44.2 0.0 collective-permute-done.8.refs_2_
  44.2 0.0 copy-start.1
  44.2 1.0 %collective-permute-start.21 = (bf16[128,256]{1,0:T(8,128)(2,1)S(1)}, bf16[128,256]{1,0:T(8,128)(2,1)S(1)}, u32[]{:S(2)}, u32[]{:S(2)}) collective-permute-start(bf16[128,256]{1,0:T(8,128)(2,1)S(1)} %get-tuple-element.49.refs_1_), channel_id=1, source_target_pairs={{0,1},{1,0},{2,3},{3,2},{4,5},{5,4},{6,7},{7,6},{8,9},{9,8},{10,11... | collective-permute-start | bytes 196616 | tf_op jit(solution)/shard_map/ppermute | solution.py:298
  45.2 0.0 collective-permute-done.9.refs_3_
  45.2 0.0 collective-permute-done.10.refs_4_
  45.2 0.5 phase.2.refs_3_
  45.7 0.1 collective-permute-start.11
  45.8 0.1 collective-permute-done.19.refs_2_
  45.9 2.0 %collective-permute-done.20.refs_3_ = bf16[128,256]{1,0:T(8,128)(2,1)S(1)} collective-permute-done((bf16[128,256]{1,0:T(8,128)(2,1)S(1)}, bf16[128,256]{1,0:T(8,128)(2,1)S(1)}, u32[]{:S(2)}, u32[]{:S(2)}) %collective-permute-start.20) | collective-permute-done | bytes 65568 | tf_op jit(solution)/shard_map/ppermute | solution.py:298
  47.9 0.6 %collective-permute-done.21.refs_4_ = bf16[128,256]{1,0:T(8,128)(2,1)S(1)} collective-permute-done((bf16[128,256]{1,0:T(8,128)(2,1)S(1)}, bf16[128,256]{1,0:T(8,128)(2,1)S(1)}, u32[]{:S(2)}, u32[]{:S(2)}) %collective-permute-start.21) | collective-permute-done | bytes 65568 | tf_op jit(solution)/shard_map/ppermute | solution.py:298
  48.6 0.5 phase.3.refs_5_
  49.0 0.1 collective-permute-start.22
  49.1 0.0 collective-permute-done.11.refs_4_
  49.1 0.0 copy-done.1
  49.1 0.0 copy-done.2
  49.1 0.0 copy-done.3
  49.1 1.2 %recon.2 = (f32[128,512]{1,0:T(8,128)S(1)}, bf16[1024,512]{1,0:T(8,128)(2,1)S(1)}, bf16[128,128]{1,0:T(8,128)(2,1)S(1)}) custom-call(s32[1,4]{1,0:T(1,128)S(1)} %copy-done.2, s32[16]{0:T(128)S(1)} %copy-done.3, bf16[4,1024,512]{2,1,0:T(8,128)(2,1)S(1)} %copy-done.1, bf16[128,1024]{1,0:T(8,128)(2,1)S(1)} %phase.2.refs_3_, ...), custom_call_target="tpu_custom_call" | custom-call | flops 1 | bytes 1 | tf_op jit(solution)/shard_map/recon/pallas_call | solution.py:402
  50.3 0.3 collective-permute-done.22.phase
  50.6 1.1 %recon.3 = bf16[128,512]{1,0:T(8,128)(2,1)} custom-call(bf16[1024,512]{1,0:T(8,128)(2,1)S(1)} %get-tuple-element.52.weights, bf16[128,1024]{1,0:T(8,128)(2,1)S(1)} %collective-permute-done.22.phase, f32[128,512]{1,0:T(8,128)S(1)} %get-tuple-element.53.before, bf16[128,128]{1,0:T(8,128)(2,1)S(1)} %get-tuple-element.54.select), custom_call_target="tpu_custom_call" | custom-call | flops 1 | bytes 1 | tf_op jit(solution)/shard_map/recon/pallas_call | solution.py:415
  (2 shorter events, 0.0 us)
Async XLA Ops:
  0.0 3.1 %copy-start = (bf16[1024,1024]{1,0:T(8,128)(2,1)S(1)}, bf16[1024,1024]{1,0:T(8,128)(2,1)}, u32[]{:S(2)}) copy-start(bf16[1024,1024]{1,0:T(8,128)(2,1)} %constant.2.clone.refs_2_.refs_0_) | copy-start | bytes 6291460
  0.0 3.1 %collective-permute-start = (bf16[4,2,64,1024]{3,2,1,0:T(8,128)(2,1)}, bf16[4,2,64,1024]{3,2,1,0:T(8,128)(2,1)S(1)}, u32[]{:S(2)}, u32[]{:S(2)}) collective-permute-start(bf16[4,2,64,1024]{3,2,1,0:T(8,128)(2,1)} %bitcast.1), channel_id=1, source_target_pairs={{0,16},{1,17},{2,18},{3,19},{4,20},{5,21},{6,22},{7,23},{8,24},{9,... | collective-permute-start | bytes 3145736 | tf_op jit(solution)/shard_map/ppermute | solution.py:298
  4.9 7.8 %collective-permute-start.1 = (bf16[4,64,256]{2,1,0:T(8,128)(2,1)S(1)}, bf16[4,64,256]{2,1,0:T(8,128)(2,1)S(1)}, u32[]{:S(2)}, u32[]{:S(2)}) collective-permute-start(bf16[4,64,256]{2,1,0:T(8,128)(2,1)S(1)} %get-tuple-element.31), channel_id=1, source_target_pairs={{0,2},{1,3},{2,0},{3,1},{4,6},{5,7},{6,4},{7,5},{8,10},{9,11},{10,... | collective-permute-start | bytes 393224 | tf_op jit(solution)/shard_map/ppermute | solution.py:298
  7.7 6.6 %collective-permute-start.2 = (bf16[4,64,256]{2,1,0:T(8,128)(2,1)S(1)}, bf16[4,64,256]{2,1,0:T(8,128)(2,1)S(1)}, u32[]{:S(2)}, u32[]{:S(2)}) collective-permute-start(bf16[4,64,256]{2,1,0:T(8,128)(2,1)S(1)} %get-tuple-element.32), channel_id=1, source_target_pairs={{0,1},{1,0},{2,3},{3,2},{4,5},{5,4},{6,7},{7,6},{8,9},{9,8},{10,11... | collective-permute-start | bytes 393224 | tf_op jit(solution)/shard_map/ppermute | solution.py:298
  9.2 7.4 %collective-permute-start.3 = (bf16[4,64,256]{2,1,0:T(8,128)(2,1)S(1)}, bf16[4,64,256]{2,1,0:T(8,128)(2,1)S(1)}, u32[]{:S(2)}, u32[]{:S(2)}) collective-permute-start(bf16[4,64,256]{2,1,0:T(8,128)(2,1)S(1)} %get-tuple-element.33), channel_id=1, source_target_pairs={{0,3},{1,2},{2,1},{3,0},{4,7},{5,6},{6,5},{7,4},{8,11},{9,10},{10,... | collective-permute-start | bytes 393224 | tf_op jit(solution)/shard_map/ppermute | solution.py:298
  9.3 10.3 %collective-permute-start.12 = (bf16[4,64,256]{2,1,0:T(8,128)(2,1)S(1)}, bf16[4,64,256]{2,1,0:T(8,128)(2,1)S(1)}, u32[]{:S(2)}, u32[]{:S(2)}) collective-permute-start(bf16[4,64,256]{2,1,0:T(8,128)(2,1)S(1)} %get-tuple-element.42), channel_id=1, source_target_pairs={{0,2},{1,3},{2,0},{3,1},{4,6},{5,7},{6,4},{7,5},{8,10},{9,11},{10,... | collective-permute-start | bytes 393224 | tf_op jit(solution)/shard_map/ppermute | solution.py:298
  11.2 13.4 %collective-permute-start.13 = (bf16[4,64,256]{2,1,0:T(8,128)(2,1)S(1)}, bf16[4,64,256]{2,1,0:T(8,128)(2,1)S(1)}, u32[]{:S(2)}, u32[]{:S(2)}) collective-permute-start(bf16[4,64,256]{2,1,0:T(8,128)(2,1)S(1)} %get-tuple-element.43), channel_id=1, source_target_pairs={{0,1},{1,0},{2,3},{3,2},{4,5},{5,4},{6,7},{7,6},{8,9},{9,8},{10,11... | collective-permute-start | bytes 393224 | tf_op jit(solution)/shard_map/ppermute | solution.py:298
  12.7 11.9 %collective-permute-start.14 = (bf16[4,64,256]{2,1,0:T(8,128)(2,1)S(1)}, bf16[4,64,256]{2,1,0:T(8,128)(2,1)S(1)}, u32[]{:S(2)}, u32[]{:S(2)}) collective-permute-start(bf16[4,64,256]{2,1,0:T(8,128)(2,1)S(1)} %get-tuple-element.44), channel_id=1, source_target_pairs={{0,3},{1,2},{2,1},{3,0},{4,7},{5,6},{6,5},{7,4},{8,11},{9,10},{10,... | collective-permute-start | bytes 393224 | tf_op jit(solution)/shard_map/ppermute | solution.py:298
  17.9 8.1 %collective-permute-start.4 = (bf16[256,256]{1,0:T(8,128)(2,1)S(1)}, bf16[256,256]{1,0:T(8,128)(2,1)S(1)}, u32[]{:S(2)}, u32[]{:S(2)}) collective-permute-start(bf16[256,256]{1,0:T(8,128)(2,1)S(1)} %get-tuple-element.36), channel_id=1, source_target_pairs={{0,4},{1,5},{2,6},{3,7},{4,0},{5,1},{6,2},{7,3},{8,12},{9,13},{10,... | collective-permute-start | bytes 393224 | tf_op jit(solution)/shard_map/ppermute | solution.py:298
  19.5 8.1 %collective-permute-start.7 = (bf16[256,256]{1,0:T(8,128)(2,1)S(1)}, bf16[256,256]{1,0:T(8,128)(2,1)S(1)}, u32[]{:S(2)}, u32[]{:S(2)}) collective-permute-start(bf16[256,256]{1,0:T(8,128)(2,1)S(1)} %get-tuple-element.37), channel_id=1, source_target_pairs={{0,16},{1,17},{2,18},{3,19},{4,8},{5,9},{6,10},{7,11},{8,4},{9,5},... | collective-permute-start | bytes 393224 | tf_op jit(solution)/shard_map/ppermute | solution.py:298
  19.5 12.0 %collective-permute-start.6 = (bf16[256,256]{1,0:T(8,128)(2,1)S(1)}, bf16[256,256]{1,0:T(8,128)(2,1)S(1)}, u32[]{:S(2)}, u32[]{:S(2)}) collective-permute-start(bf16[256,256]{1,0:T(8,128)(2,1)S(1)} %get-tuple-element.37), channel_id=1, source_target_pairs={{0,4},{1,5},{2,6},{3,7},{12,8},{13,9},{14,10},{15,11},{16,20},{17,... | collective-permute-start | bytes 393224 | tf_op jit(solution)/shard_map/ppermute | solution.py:298
  25.9 5.6 %collective-permute-start.15 = (bf16[256,256]{1,0:T(8,128)(2,1)S(1)}, bf16[256,256]{1,0:T(8,128)(2,1)S(1)}, u32[]{:S(2)}, u32[]{:S(2)}) collective-permute-start(bf16[256,256]{1,0:T(8,128)(2,1)S(1)} %get-tuple-element.47), channel_id=1, source_target_pairs={{0,4},{1,5},{2,6},{3,7},{4,0},{5,1},{6,2},{7,3},{8,12},{9,13},{10,... | collective-permute-start | bytes 393224 | tf_op jit(solution)/shard_map/ppermute | solution.py:298
  26.1 8.9 %collective-permute-start.5 = (bf16[256,256]{1,0:T(8,128)(2,1)S(1)}, bf16[256,256]{1,0:T(8,128)(2,1)S(1)}, u32[]{:S(2)}, u32[]{:S(2)}) collective-permute-start(bf16[256,256]{1,0:T(8,128)(2,1)S(1)} %far.2), channel_id=1, source_target_pairs={{0,8},{1,9},{2,10},{3,11},{4,12},{5,13},{6,14},{7,15},{8,0},{9,1},... | collective-permute-start | bytes 393224 | tf_op jit(solution)/shard_map/ppermute | solution.py:298
  27.6 9.8 %collective-permute-start.18 = (bf16[256,256]{1,0:T(8,128)(2,1)S(1)}, bf16[256,256]{1,0:T(8,128)(2,1)S(1)}, u32[]{:S(2)}, u32[]{:S(2)}) collective-permute-start(bf16[256,256]{1,0:T(8,128)(2,1)S(1)} %get-tuple-element.48), channel_id=1, source_target_pairs={{0,16},{1,17},{2,18},{3,19},{4,8},{5,9},{6,10},{7,11},{8,4},{9,5},... | collective-permute-start | bytes 393224 | tf_op jit(solution)/shard_map/ppermute | solution.py:298
  27.6 11.0 %collective-permute-start.17 = (bf16[256,256]{1,0:T(8,128)(2,1)S(1)}, bf16[256,256]{1,0:T(8,128)(2,1)S(1)}, u32[]{:S(2)}, u32[]{:S(2)}) collective-permute-start(bf16[256,256]{1,0:T(8,128)(2,1)S(1)} %get-tuple-element.48), channel_id=1, source_target_pairs={{0,4},{1,5},{2,6},{3,7},{12,8},{13,9},{14,10},{15,11},{16,20},{17,... | collective-permute-start | bytes 393224 | tf_op jit(solution)/shard_map/ppermute | solution.py:298
  31.6 9.8 %collective-permute-start.16 = (bf16[256,256]{1,0:T(8,128)(2,1)S(1)}, bf16[256,256]{1,0:T(8,128)(2,1)S(1)}, u32[]{:S(2)}, u32[]{:S(2)}) collective-permute-start(bf16[256,256]{1,0:T(8,128)(2,1)S(1)} %far.3), channel_id=1, source_target_pairs={{0,8},{1,9},{2,10},{3,11},{4,12},{5,13},{6,14},{7,15},{8,0},{9,1},... | collective-permute-start | bytes 393224 | tf_op jit(solution)/shard_map/ppermute | solution.py:298
  35.0 9.2 %collective-permute-start.8 = (bf16[128,256]{1,0:T(8,128)(2,1)S(1)}, bf16[128,256]{1,0:T(8,128)(2,1)S(1)}, u32[]{:S(2)}, u32[]{:S(2)}) collective-permute-start(bf16[128,256]{1,0:T(8,128)(2,1)S(1)} %get-tuple-element.39), channel_id=1, source_target_pairs={{0,2},{1,3},{2,0},{3,1},{4,6},{5,7},{6,4},{7,5},{8,10},{9,11},{10,... | collective-permute-start | bytes 196616 | tf_op jit(solution)/shard_map/ppermute | solution.py:298
  36.0 9.2 %collective-permute-start.9 = (bf16[128,256]{1,0:T(8,128)(2,1)S(1)}, bf16[128,256]{1,0:T(8,128)(2,1)S(1)}, u32[]{:S(2)}, u32[]{:S(2)}) collective-permute-start(bf16[128,256]{1,0:T(8,128)(2,1)S(1)} %get-tuple-element.40), channel_id=1, source_target_pairs={{0,3},{1,2},{2,1},{3,0},{4,7},{5,6},{6,5},{7,4},{8,11},{9,10},{10,... | collective-permute-start | bytes 196616 | tf_op jit(solution)/shard_map/ppermute | solution.py:298
  37.4 7.8 %collective-permute-start.10 = (bf16[128,256]{1,0:T(8,128)(2,1)S(1)}, bf16[128,256]{1,0:T(8,128)(2,1)S(1)}, u32[]{:S(2)}, u32[]{:S(2)}) collective-permute-start(bf16[128,256]{1,0:T(8,128)(2,1)S(1)} %get-tuple-element.38.refs_1_), channel_id=1, source_target_pairs={{0,1},{1,0},{2,3},{3,2},{4,5},{5,4},{6,7},{7,6},{8,9},{9,8},{10,11... | collective-permute-start | bytes 196616 | tf_op jit(solution)/shard_map/ppermute | solution.py:298
  41.6 4.3 %collective-permute-start.19 = (bf16[128,256]{1,0:T(8,128)(2,1)S(1)}, bf16[128,256]{1,0:T(8,128)(2,1)S(1)}, u32[]{:S(2)}, u32[]{:S(2)}) collective-permute-start(bf16[128,256]{1,0:T(8,128)(2,1)S(1)} %get-tuple-element.50), channel_id=1, source_target_pairs={{0,2},{1,3},{2,0},{3,1},{4,6},{5,7},{6,4},{7,5},{8,10},{9,11},{10,... | collective-permute-start | bytes 196616 | tf_op jit(solution)/shard_map/ppermute | solution.py:298
  42.8 5.2 %collective-permute-start.20 = (bf16[128,256]{1,0:T(8,128)(2,1)S(1)}, bf16[128,256]{1,0:T(8,128)(2,1)S(1)}, u32[]{:S(2)}, u32[]{:S(2)}) collective-permute-start(bf16[128,256]{1,0:T(8,128)(2,1)S(1)} %get-tuple-element.51), channel_id=1, source_target_pairs={{0,3},{1,2},{2,1},{3,0},{4,7},{5,6},{6,5},{7,4},{8,11},{9,10},{10,... | collective-permute-start | bytes 196616 | tf_op jit(solution)/shard_map/ppermute | solution.py:298
  44.2 4.9 %copy-start.1 = (bf16[4,1024,512]{2,1,0:T(8,128)(2,1)S(1)}, bf16[4,1024,512]{2,1,0:T(8,128)(2,1)}, u32[]{:S(2)}) copy-start(bf16[4,1024,512]{2,1,0:T(8,128)(2,1)} %refs_2_.2) | copy-start | bytes 12582916
  44.2 4.9 %copy-start.2 = (s32[1,4]{1,0:T(1,128)S(1)}, s32[1,4]{1,0:T(1,128)}, u32[]{:S(2)}) copy-start(s32[1,4]{1,0:T(1,128)} %refs_0_.7) | copy-start | bytes 52
  44.2 4.9 %copy-start.3 = (s32[16]{0:T(128)S(1)}, s32[16]{0:T(128)}, u32[]{:S(2)}) copy-start(s32[16]{0:T(128)} %refs_1_.1) | copy-start | bytes 196
  44.2 4.3 %collective-permute-start.21 = (bf16[128,256]{1,0:T(8,128)(2,1)S(1)}, bf16[128,256]{1,0:T(8,128)(2,1)S(1)}, u32[]{:S(2)}, u32[]{:S(2)}) collective-permute-start(bf16[128,256]{1,0:T(8,128)(2,1)S(1)} %get-tuple-element.49.refs_1_), channel_id=1, source_target_pairs={{0,1},{1,0},{2,3},{3,2},{4,5},{5,4},{6,7},{7,6},{8,9},{9,8},{10,11... | collective-permute-start | bytes 196616 | tf_op jit(solution)/shard_map/ppermute | solution.py:298
  45.7 3.4 %collective-permute-start.11 = (bf16[128,1024]{1,0:T(8,128)(2,1)S(1)}, bf16[128,1024]{1,0:T(8,128)(2,1)S(1)}, u32[]{:S(2)}, u32[]{:S(2)}) collective-permute-start(bf16[128,1024]{1,0:T(8,128)(2,1)S(1)} %phase.2.refs_3_), channel_id=1, source_target_pairs={{0,16},{1,17},{2,18},{3,19},{4,20},{5,21},{6,22},{7,23},{8,24},{9,... | collective-permute-start | bytes 786440 | tf_op jit(solution)/shard_map/ppermute | solution.py:298
  49.0 1.6 %collective-permute-start.22 = (bf16[128,1024]{1,0:T(8,128)(2,1)S(1)}, bf16[128,1024]{1,0:T(8,128)(2,1)S(1)}, u32[]{:S(2)}, u32[]{:S(2)}) collective-permute-start(bf16[128,1024]{1,0:T(8,128)(2,1)S(1)} %phase.3.refs_5_), channel_id=1, source_target_pairs={{0,16},{1,17},{2,18},{3,19},{4,20},{5,21},{6,22},{7,23},{8,24},{9,... | collective-permute-start | bytes 786440 | tf_op jit(solution)/shard_map/ppermute | solution.py:298

commit v22 on v19

--- a/solution.py
+++ b/solution.py
@@ -182,29 +182,35 @@
             total[...] += got
     spectrum[...] = total[...].astype(bf16)
     middle = (plane == 1) | (plane == 2)
-    first = jnp.where(middle, 1, 3)
-    for rel, out in zip((0, first, 4 - first, 2), outs):
+
+    def rows_of(rel):
         rows = pl.ds(pl.multiple_of((plane ^ rel) * depth, depth), depth)
-        value = jnp.dot(table[rows, :], spectrum[...], preferred_element_type=f32)
-        out[...] = value.astype(bf16)
-
-
-def far_kernel(inner, *refs):
-    ours, got, out = refs[-3:]
+        return jnp.dot(table[rows, :], spectrum[...], preferred_element_type=f32)
+
+    ours, lead, third, fourth = outs
+    two, one, three = rows_of(2), rows_of(1), rows_of(3)
+    lead[0] = jnp.where(middle, one, three).astype(bf16)
+    lead[1] = two.astype(bf16)
+    third[...] = jnp.where(middle, two, one).astype(bf16)
+    fourth[...] = three.astype(bf16)
+    ours[...] = rows_of(0).astype(bf16)
+
+
+def far_kernel(inner, third, fourth, got, out_third, out_fourth):
     _, plane, _ = position(inner)
     middle = (plane == 1) | (plane == 2)
-    more = jnp.where(middle, got[...].astype(f32), 0.0)
-    out[...] = (ours[...].astype(f32) + more).astype(bf16)
-
-
-def half_kernel(inner, ours, far, near, next_near, across, other, mine, again):
+    for slot, ours, out in ((0, third, out_third), (1, fourth, out_fourth)):
+        more = jnp.where(middle, got[slot].astype(f32), 0.0)
+        out[...] = (ours[...].astype(f32) + more).astype(bf16)
+
+
+def half_kernel(inner, ours, far, near, across, other, mine, again):
     _, plane, spot = position(inner)
     middle = (plane == 1) | (plane == 2)
     capacity = mine.shape[0]
     for out, pair in ((mine, spot // 2), (other, 1 - spot // 2)):
         rows = pl.ds(pl.multiple_of(pair * capacity, capacity), capacity)
-        inside = next_near[rows, :].astype(f32) + across[rows, :].astype(f32)
-        more = jnp.where(middle, inside, near[rows, :].astype(f32))
+        more = jnp.where(middle, across[rows, :].astype(f32), near[0, rows, :].astype(f32))
         got = ours[rows, :].astype(f32) + far[rows, :].astype(f32) + more
         out[...] = got.astype(bf16)
     again[...] = other[...]
@@ -307,6 +313,9 @@
 
     def to_plane(rel):
         return lambda c, r: (c, (r // inner ^ rel) * inner + r % inner)
+
+    def around(c, r):
+        return c, (1, 3, 0, 2)[r // inner] * inner + r % inner
 
     def to_middle(c, r):
         z = r // inner
@@ -343,7 +352,7 @@
     for chunk in range(own):
         blocks = pl.pallas_call(
             lambda *refs: column_kernel(inner, outer, *refs),
-            out_shape=[shaped(depth, block)] * outer,
+            out_shape=[shaped(depth, block), shaped(2, depth, block)] + [shaped(depth, block)] * 2,
             in_specs=vmem(2 + inner),
             out_specs=vmem(outer),
             scratch_shapes=[
@@ -355,27 +364,25 @@
             cost_estimate=cheap,
             name="columns",
         )(table, gain, *arrived[chunk])
-        ours, first, second, third = blocks
-        near = sent(first, to_plane(1))
-        earlier = sums[-1][3:] if sums else []
-        message = pl.pallas_call(
+        ours, lead, third, fourth = blocks
+        near = sent(lead, to_plane(1))
+        third, fourth = pl.pallas_call(
             lambda *refs: far_kernel(inner, *refs),
-            out_shape=shaped(depth, block),
-            in_specs=unread(len(earlier)) + vmem(2),
-            out_specs=one_out,
+            out_shape=[shaped(depth, block)] * 2,
+            in_specs=vmem(3),
+            out_specs=vmem(2),
             compiler_params=params,
             cost_estimate=cheap,
             name="far",
-        )(*earlier, third, near)
-        far = sent(message, to_plane(2))
-        sums.append([ours, far, near, sent(second, to_plane(1)), sent(second, to_middle)])
+        )(third, fourth, near)
+        sums.append([ours, sent(third, around), near, sent(fourth, to_middle)])
 
     phases = []
     for chunk in range(own):
         second, first, again = pl.pallas_call(
             lambda *refs: half_kernel(inner, *refs),
             out_shape=[shaped(capacity, block)] * 3,
-            in_specs=vmem(5),
+            in_specs=vmem(4),
             out_specs=vmem(3),
             compiler_params=params,
             cost_estimate=cheap,

time: 51.7 us -> 54.1 us (1.046)
  waiting for transfers between devices: 11.9 us -> 19.3 us
  starting transfers between devices: 28.9 us -> 23.6 us
    ppermute x23 -> x21, waiting for transfers between devices: 11.9 us -> 19.3 us  [sent(): return lax.ppermute(value, ('dist', 'rows'), pairs)]
    ppermute x23 -> x21, starting transfers between devices: 28.9 us -> 23.6 us  [sent(): return lax.ppermute(value, ('dist', 'rows'), pairs)]
  transfers between devices with their start and end apart: 23 -> 21, of which waited for: 8 -> 11; matrix products, arithmetic and copies ran while one was open for 0% -> 0% of each run, Pallas kernels for 15% -> 14%
where the time goes in v22:
time: 54.1 us; the launch traced here: 53.7 us
  starting transfers between devices  23.6 us (44%)
  waiting for transfers between devices  19.3 us (36%)
  Pallas kernels  10.6 us (20%)
    ppermute x21, starting transfers between devices, sent(): return lax.ppermute(value, ('dist', 'rows'), pairs)  23.6 us
    ppermute x21, waiting for transfers between devices, sent(): return lax.ppermute(value, ('dist', 'rows'), pairs)  19.3 us
    pallas_call x1, Pallas kernels, plane_plan(): pl.pallas_call(lambda *refs: filter_kernel(inner, dist_dev, *refs), out_s...  2.62 us
    pallas_call x2, Pallas kernels, plane_plan(): pl.pallas_call(lambda *refs: column_kernel(inner, outer, *refs), out_shap...  2.6 us
    pallas_call x1, Pallas kernels, plane_plan(): pl.pallas_call(lambda *refs: row_kernel(inner, *refs), out_shape=[shaped(...  1.83 us
    pallas_call x1, Pallas kernels, plane_plan(): pl.pallas_call(lambda *refs: recon_kernel(own, *refs), out_shape=[jax.Sha...  1.2 us
    pallas_call x1, Pallas kernels, plane_plan(): pl.pallas_call(recon_last_kernel, out_shape=shaped(capacity, pixels), in_...  1.12 us
  transfers between devices with their start and end apart: 21, of which 11 were waited for; matrix products, arithmetic and copies ran while one was open for 0% of the time, Pallas kernels for 14%

profile of v22, /device:TPU:0, one launch (start us, length us, event | category | flops | bytes accessed | tf_op | source)
XLA Modules:
  0.0 53.7 jit_solution(8839744181155005928)
XLA Ops:
  0.0 0.0 copy-start
  0.0 0.5 collective-permute-start
  0.5 2.6 %filters.1.refs_3_.refs_1_ = bf16[4,1024,256]{2,1,0:T(8,128)(2,1)S(1)} custom-call(f32[4]{0:T(128)} %refs_0_.6), custom_call_target="tpu_custom_call" | custom-call | flops 1 | bytes 1 | tf_op jit(solution)/shard_map/filters/pallas_call | solution.py:325
  3.1 0.0 collective-permute-done.refs_1_
  3.1 0.0 copy-done
  3.1 1.8 %row_spectra.1 = (bf16[4,64,256]{2,1,0:T(8,128)(2,1)S(1)}, bf16[4,64,256]{2,1,0:T(8,128)(2,1)S(1)}, bf16[4,64,256]{2,1,0:T(8,128)(2,1)S(1)}, bf16[4,64,256]{2,1,...) custom-call(bf16[4,2,64,1024]{3,2,1,0:T(8,128)(2,1)} %bitcast.2, ...), custom_call_target="tpu_custom_call" | custom-call | flops 1 | bytes 1 | tf_op jit(solution)/shard_map/row_spectra/pallas_call | solution.py:334
  4.9 2.8 %collective-permute-start.1 = (bf16[4,64,256]{2,1,0:T(8,128)(2,1)S(1)}, bf16[4,64,256]{2,1,0:T(8,128)(2,1)S(1)}, u32[]{:S(2)}, u32[]{:S(2)}) collective-permute-start(bf16[4,64,256]{2,1,0:T(8,128)(2,1)S(1)} %get-tuple-element.35), channel_id=1, source_target_pairs={{0,2},{1,3},{2,0},{3,1},{4,6},{5,7},{6,4},{7,5},{8,10},{9,11},{10,... | collective-permute-start | bytes 393224 | tf_op jit(solution)/shard_map/ppermute | solution.py:303
  7.7 1.5 %collective-permute-start.2 = (bf16[4,64,256]{2,1,0:T(8,128)(2,1)S(1)}, bf16[4,64,256]{2,1,0:T(8,128)(2,1)S(1)}, u32[]{:S(2)}, u32[]{:S(2)}) collective-permute-start(bf16[4,64,256]{2,1,0:T(8,128)(2,1)S(1)} %get-tuple-element.36), channel_id=1, source_target_pairs={{0,1},{1,0},{2,3},{3,2},{4,5},{5,4},{6,7},{7,6},{8,9},{9,8},{10,11... | collective-permute-start | bytes 393224 | tf_op jit(solution)/shard_map/ppermute | solution.py:303
  9.2 0.0 collective-permute-start.3
  9.3 1.9 %collective-permute-start.11 = (bf16[4,64,256]{2,1,0:T(8,128)(2,1)S(1)}, bf16[4,64,256]{2,1,0:T(8,128)(2,1)S(1)}, u32[]{:S(2)}, u32[]{:S(2)}) collective-permute-start(bf16[4,64,256]{2,1,0:T(8,128)(2,1)S(1)} %get-tuple-element.48), channel_id=1, source_target_pairs={{0,2},{1,3},{2,0},{3,1},{4,6},{5,7},{6,4},{7,5},{8,10},{9,11},{10,... | collective-permute-start | bytes 393224 | tf_op jit(solution)/shard_map/ppermute | solution.py:303
  11.2 1.5 %collective-permute-start.12 = (bf16[4,64,256]{2,1,0:T(8,128)(2,1)S(1)}, bf16[4,64,256]{2,1,0:T(8,128)(2,1)S(1)}, u32[]{:S(2)}, u32[]{:S(2)}) collective-permute-start(bf16[4,64,256]{2,1,0:T(8,128)(2,1)S(1)} %get-tuple-element.49), channel_id=1, source_target_pairs={{0,1},{1,0},{2,3},{3,2},{4,5},{5,4},{6,7},{7,6},{8,9},{9,8},{10,11... | collective-permute-start | bytes 393224 | tf_op jit(solution)/shard_map/ppermute | solution.py:303
  12.7 0.0 collective-permute-done.1.refs_3_
  12.7 1.6 %collective-permute-start.13 = (bf16[4,64,256]{2,1,0:T(8,128)(2,1)S(1)}, bf16[4,64,256]{2,1,0:T(8,128)(2,1)S(1)}, u32[]{:S(2)}, u32[]{:S(2)}) collective-permute-start(bf16[4,64,256]{2,1,0:T(8,128)(2,1)S(1)} %get-tuple-element.50), channel_id=1, source_target_pairs={{0,3},{1,2},{2,1},{3,0},{4,7},{5,6},{6,5},{7,4},{8,11},{9,10},{10,... | collective-permute-start | bytes 393224 | tf_op jit(solution)/shard_map/ppermute | solution.py:303
  14.3 0.0 collective-permute-done.2.refs_4_
  14.3 2.3 %collective-permute-done.3.refs_5_ = bf16[4,64,256]{2,1,0:T(8,128)(2,1)S(1)} collective-permute-done((bf16[4,64,256]{2,1,0:T(8,128)(2,1)S(1)}, bf16[4,64,256]{2,1,0:T(8,128)(2,1)S(1)}, u32[]{:S(2)}, u32[]{:S(2)}) %collective-permute-start.3) | collective-permute-done | bytes 131104 | tf_op jit(solution)/shard_map/ppermute | solution.py:303
  16.6 1.3 %columns.2 = (bf16[256,256]{1,0:T(8,128)(2,1)S(1)}, bf16[2,256,256]{2,1,0:T(8,128)(2,1)S(1)}, bf16[256,256]{1,0:T(8,128)(2,1)S(1)}, bf16[256,256]{1,0:T(8,128)(2,1)S(1)}) custom-call(bf16[1024,1024]{1,0:T(8,128)(2,1)S(1)} %copy-done, bf16[4,1024,256]{2,1,0:T(8,128)(2,1)S(1)} %filters.1.refs_3_.refs_1_, bf16[4,64,256]{2,1,0:T(8,128)(2,1)S(1)} %get-tuple-element.34.refs_2_, ...), custom_call_target="tpu_custom_call" | custom-call | flops 1 | bytes 1 | tf_op jit(solution)/shard_map/columns/pallas_call | solution.py:353
  17.9 1.6 %collective-permute-start.4 = (bf16[2,256,256]{2,1,0:T(8,128)(2,1)S(1)}, bf16[2,256,256]{2,1,0:T(8,128)(2,1)S(1)}, u32[]{:S(2)}, u32[]{:S(2)}) collective-permute-start(bf16[2,256,256]{2,1,0:T(8,128)(2,1)S(1)} %get-tuple-element.41), channel_id=1, source_target_pairs={{0,4},{1,5},{2,6},{3,7},{4,0},{5,1},{6,2},{7,3},{8,12},{9,13},{10,... | collective-permute-start | bytes 786440 | tf_op jit(solution)/shard_map/ppermute | solution.py:303
  19.5 0.0 collective-permute-done.11.refs_3_
  19.5 0.2 collective-permute-done.12.refs_4_
  19.7 1.6 %collective-permute-done.13.refs_5_ = bf16[4,64,256]{2,1,0:T(8,128)(2,1)S(1)} collective-permute-done((bf16[4,64,256]{2,1,0:T(8,128)(2,1)S(1)}, bf16[4,64,256]{2,1,0:T(8,128)(2,1)S(1)}, u32[]{:S(2)}, u32[]{:S(2)}) %collective-permute-start.13) | collective-permute-done | bytes 131104 | tf_op jit(solution)/shard_map/ppermute | solution.py:303
  21.3 1.3 %columns.3 = (bf16[256,256]{1,0:T(8,128)(2,1)S(1)}, bf16[2,256,256]{2,1,0:T(8,128)(2,1)S(1)}, bf16[256,256]{1,0:T(8,128)(2,1)S(1)}, bf16[256,256]{1,0:T(8,128)(2,1)S(1)}) custom-call(bf16[1024,1024]{1,0:T(8,128)(2,1)S(1)} %copy-done, bf16[4,1024,256]{2,1,0:T(8,128)(2,1)S(1)} %filters.1.refs_3_.refs_1_, bf16[4,64,256]{2,1,0:T(8,128)(2,1)S(1)} %get-tuple-element.47.refs_2_, ...), custom_call_target="tpu_custom_call" | custom-call | flops 1 | bytes 1 | tf_op jit(solution)/shard_map/columns/pallas_call | solution.py:353
  22.6 1.8 %collective-permute-start.14 = (bf16[2,256,256]{2,1,0:T(8,128)(2,1)S(1)}, bf16[2,256,256]{2,1,0:T(8,128)(2,1)S(1)}, u32[]{:S(2)}, u32[]{:S(2)}) collective-permute-start(bf16[2,256,256]{2,1,0:T(8,128)(2,1)S(1)} %get-tuple-element.54), channel_id=1, source_target_pairs={{0,4},{1,5},{2,6},{3,7},{4,0},{5,1},{6,2},{7,3},{8,12},{9,13},{10,... | collective-permute-start | bytes 786440 | tf_op jit(solution)/shard_map/ppermute | solution.py:303
  24.4 0.2 collective-permute-done.4.refs_2_
  24.6 0.1 far.2
  24.7 1.8 %collective-permute-start.5 = (bf16[256,256]{1,0:T(8,128)(2,1)S(1)}, bf16[256,256]{1,0:T(8,128)(2,1)S(1)}, u32[]{:S(2)}, u32[]{:S(2)}) collective-permute-start(bf16[256,256]{1,0:T(8,128)(2,1)S(1)} %get-tuple-element.42), channel_id=1, source_target_pairs={{0,4},{1,5},{2,6},{3,7},{4,12},{5,13},{6,14},{7,15},{8,0},{9,1},{1... | collective-permute-start | bytes 393224 | tf_op jit(solution)/shard_map/ppermute | solution.py:303
  26.5 0.0 collective-permute-start.6
  26.5 6.5 %collective-permute-done.14.refs_2_ = bf16[2,256,256]{2,1,0:T(8,128)(2,1)S(1)} collective-permute-done((bf16[2,256,256]{2,1,0:T(8,128)(2,1)S(1)}, bf16[2,256,256]{2,1,0:T(8,128)(2,1)S(1)}, u32[]{:S(2)}, u32[]{:S(2)}) %collective-permute-start.14) | collective-permute-done | bytes 262176 | tf_op jit(solution)/shard_map/ppermute | solution.py:303
  33.0 0.1 far.3
  33.1 0.4 collective-permute-start.15
  33.5 0.0 collective-permute-start.16
  33.5 0.0 collective-permute-done.5.refs_1_
  33.5 0.0 collective-permute-done.6.refs_3_
  33.5 0.1 half.2
  33.6 1.4 %collective-permute-start.7 = (bf16[128,256]{1,0:T(8,128)(2,1)S(1)}, bf16[128,256]{1,0:T(8,128)(2,1)S(1)}, u32[]{:S(2)}, u32[]{:S(2)}) collective-permute-start(bf16[128,256]{1,0:T(8,128)(2,1)S(1)} %get-tuple-element.45), channel_id=1, source_target_pairs={{0,2},{1,3},{2,0},{3,1},{4,6},{5,7},{6,4},{7,5},{8,10},{9,11},{10,... | collective-permute-start | bytes 196616 | tf_op jit(solution)/shard_map/ppermute | solution.py:303
  35.0 5.1 %collective-permute-done.15.refs_1_ = bf16[256,256]{1,0:T(8,128)(2,1)S(1)} collective-permute-done((bf16[256,256]{1,0:T(8,128)(2,1)S(1)}, bf16[256,256]{1,0:T(8,128)(2,1)S(1)}, u32[]{:S(2)}, u32[]{:S(2)}) %collective-permute-start.15) | collective-permute-done | bytes 131104 | tf_op jit(solution)/shard_map/ppermute | solution.py:303
  40.2 0.0 collective-permute-done.16.refs_3_
  40.2 0.1 half.3
  40.2 1.6 %collective-permute-start.17 = (bf16[128,256]{1,0:T(8,128)(2,1)S(1)}, bf16[128,256]{1,0:T(8,128)(2,1)S(1)}, u32[]{:S(2)}, u32[]{:S(2)}) collective-permute-start(bf16[128,256]{1,0:T(8,128)(2,1)S(1)} %get-tuple-element.58), channel_id=1, source_target_pairs={{0,2},{1,3},{2,0},{3,1},{4,6},{5,7},{6,4},{7,5},{8,10},{9,11},{10,... | collective-permute-start | bytes 196616 | tf_op jit(solution)/shard_map/ppermute | solution.py:303
  41.8 1.4 %collective-permute-start.8 = (bf16[128,256]{1,0:T(8,128)(2,1)S(1)}, bf16[128,256]{1,0:T(8,128)(2,1)S(1)}, u32[]{:S(2)}, u32[]{:S(2)}) collective-permute-start(bf16[128,256]{1,0:T(8,128)(2,1)S(1)} %get-tuple-element.46), channel_id=1, source_target_pairs={{0,3},{1,2},{2,1},{3,0},{4,7},{5,6},{6,5},{7,4},{8,11},{9,10},{10,... | collective-permute-start | bytes 196616 | tf_op jit(solution)/shard_map/ppermute | solution.py:303
  43.2 0.6 %collective-permute-start.9 = (bf16[128,256]{1,0:T(8,128)(2,1)S(1)}, bf16[128,256]{1,0:T(8,128)(2,1)S(1)}, u32[]{:S(2)}, u32[]{:S(2)}) collective-permute-start(bf16[128,256]{1,0:T(8,128)(2,1)S(1)} %get-tuple-element.44.refs_1_), channel_id=1, source_target_pairs={{0,1},{1,0},{2,3},{3,2},{4,5},{5,4},{6,7},{7,6},{8,9},{9,8},{10,11... | collective-permute-start | bytes 196616 | tf_op jit(solution)/shard_map/ppermute | solution.py:303
  43.8 2.4 %collective-permute-start.18 = (bf16[128,256]{1,0:T(8,128)(2,1)S(1)}, bf16[128,256]{1,0:T(8,128)(2,1)S(1)}, u32[]{:S(2)}, u32[]{:S(2)}) collective-permute-start(bf16[128,256]{1,0:T(8,128)(2,1)S(1)} %get-tuple-element.59), channel_id=1, source_target_pairs={{0,3},{1,2},{2,1},{3,0},{4,7},{5,6},{6,5},{7,4},{8,11},{9,10},{10,... | collective-permute-start | bytes 196616 | tf_op jit(solution)/shard_map/ppermute | solution.py:303
  46.2 0.0 collective-permute-done.7.refs_2_
  46.2 0.0 copy-start.1
  46.2 0.0 copy-start.2
  46.2 0.0 copy-start.3
  46.2 0.6 %collective-permute-start.19 = (bf16[128,256]{1,0:T(8,128)(2,1)S(1)}, bf16[128,256]{1,0:T(8,128)(2,1)S(1)}, u32[]{:S(2)}, u32[]{:S(2)}) collective-permute-start(bf16[128,256]{1,0:T(8,128)(2,1)S(1)} %get-tuple-element.57.refs_1_), channel_id=1, source_target_pairs={{0,1},{1,0},{2,3},{3,2},{4,5},{5,4},{6,7},{7,6},{8,9},{9,8},{10,11... | collective-permute-start | bytes 196616 | tf_op jit(solution)/shard_map/ppermute | solution.py:303
  46.8 0.1 collective-permute-done.8.refs_3_
  47.0 0.5 collective-permute-done.9.refs_4_
  47.5 0.5 phase.2.refs_3_
  48.0 0.1 collective-permute-start.10
  48.0 0.0 collective-permute-done.17.refs_2_
  48.1 1.1 %collective-permute-done.18.refs_3_ = bf16[128,256]{1,0:T(8,128)(2,1)S(1)} collective-permute-done((bf16[128,256]{1,0:T(8,128)(2,1)S(1)}, bf16[128,256]{1,0:T(8,128)(2,1)S(1)}, u32[]{:S(2)}, u32[]{:S(2)}) %collective-permute-start.18) | collective-permute-done | bytes 65568 | tf_op jit(solution)/shard_map/ppermute | solution.py:303
  49.1 1.4 %collective-permute-done.19.refs_4_ = bf16[128,256]{1,0:T(8,128)(2,1)S(1)} collective-permute-done((bf16[128,256]{1,0:T(8,128)(2,1)S(1)}, bf16[128,256]{1,0:T(8,128)(2,1)S(1)}, u32[]{:S(2)}, u32[]{:S(2)}) %collective-permute-start.19) | collective-permute-done | bytes 65568 | tf_op jit(solution)/shard_map/ppermute | solution.py:303
  50.5 0.5 phase.3.refs_5_
  51.0 0.1 collective-permute-start.20
  51.1 0.0 collective-permute-done.10.refs_4_
  51.1 0.0 copy-done.1
  51.1 0.0 copy-done.2
  51.1 0.0 copy-done.3
  51.1 1.2 %recon.2 = (f32[128,512]{1,0:T(8,128)S(1)}, bf16[1024,512]{1,0:T(8,128)(2,1)S(1)}, bf16[128,128]{1,0:T(8,128)(2,1)S(1)}) custom-call(s32[1,4]{1,0:T(1,128)S(1)} %copy-done.2, s32[16]{0:T(128)S(1)} %copy-done.3, bf16[4,1024,512]{2,1,0:T(8,128)(2,1)S(1)} %copy-done.1, bf16[128,1024]{1,0:T(8,128)(2,1)S(1)} %phase.2.refs_3_, ...), custom_call_target="tpu_custom_call" | custom-call | flops 1 | bytes 1 | tf_op jit(solution)/shard_map/recon/pallas_call | solution.py:404
  52.3 0.3 collective-permute-done.20.phase
  52.6 1.1 %recon.3 = bf16[128,512]{1,0:T(8,128)(2,1)} custom-call(bf16[1024,512]{1,0:T(8,128)(2,1)S(1)} %get-tuple-element.60.weights, bf16[128,1024]{1,0:T(8,128)(2,1)S(1)} %collective-permute-done.20.phase, f32[128,512]{1,0:T(8,128)S(1)} %get-tuple-element.61.before, bf16[128,128]{1,0:T(8,128)(2,1)S(1)} %get-tuple-element.62.select), custom_call_target="tpu_custom_call" | custom-call | flops 1 | bytes 1 | tf_op jit(solution)/shard_map/recon/pallas_call | solution.py:417
Async XLA Ops:
  0.0 3.1 %copy-start = (bf16[1024,1024]{1,0:T(8,128)(2,1)S(1)}, bf16[1024,1024]{1,0:T(8,128)(2,1)}, u32[]{:S(2)}) copy-start(bf16[1024,1024]{1,0:T(8,128)(2,1)} %constant.2.clone.refs_2_.refs_0_) | copy-start | bytes 6291460
  0.0 3.1 %collective-permute-start = (bf16[4,2,64,1024]{3,2,1,0:T(8,128)(2,1)}, bf16[4,2,64,1024]{3,2,1,0:T(8,128)(2,1)S(1)}, u32[]{:S(2)}, u32[]{:S(2)}) collective-permute-start(bf16[4,2,64,1024]{3,2,1,0:T(8,128)(2,1)} %bitcast.1), channel_id=1, source_target_pairs={{0,16},{1,17},{2,18},{3,19},{4,20},{5,21},{6,22},{7,23},{8,24},{9,... | collective-permute-start | bytes 3145736 | tf_op jit(solution)/shard_map/ppermute | solution.py:303
  4.9 7.8 %collective-permute-start.1 = (bf16[4,64,256]{2,1,0:T(8,128)(2,1)S(1)}, bf16[4,64,256]{2,1,0:T(8,128)(2,1)S(1)}, u32[]{:S(2)}, u32[]{:S(2)}) collective-permute-start(bf16[4,64,256]{2,1,0:T(8,128)(2,1)S(1)} %get-tuple-element.35), channel_id=1, source_target_pairs={{0,2},{1,3},{2,0},{3,1},{4,6},{5,7},{6,4},{7,5},{8,10},{9,11},{10,... | collective-permute-start | bytes 393224 | tf_op jit(solution)/shard_map/ppermute | solution.py:303
  7.7 6.6 %collective-permute-start.2 = (bf16[4,64,256]{2,1,0:T(8,128)(2,1)S(1)}, bf16[4,64,256]{2,1,0:T(8,128)(2,1)S(1)}, u32[]{:S(2)}, u32[]{:S(2)}) collective-permute-start(bf16[4,64,256]{2,1,0:T(8,128)(2,1)S(1)} %get-tuple-element.36), channel_id=1, source_target_pairs={{0,1},{1,0},{2,3},{3,2},{4,5},{5,4},{6,7},{7,6},{8,9},{9,8},{10,11... | collective-permute-start | bytes 393224 | tf_op jit(solution)/shard_map/ppermute | solution.py:303
  9.2 7.4 %collective-permute-start.3 = (bf16[4,64,256]{2,1,0:T(8,128)(2,1)S(1)}, bf16[4,64,256]{2,1,0:T(8,128)(2,1)S(1)}, u32[]{:S(2)}, u32[]{:S(2)}) collective-permute-start(bf16[4,64,256]{2,1,0:T(8,128)(2,1)S(1)} %get-tuple-element.37), channel_id=1, source_target_pairs={{0,3},{1,2},{2,1},{3,0},{4,7},{5,6},{6,5},{7,4},{8,11},{9,10},{10,... | collective-permute-start | bytes 393224 | tf_op jit(solution)/shard_map/ppermute | solution.py:303
  9.3 10.3 %collective-permute-start.11 = (bf16[4,64,256]{2,1,0:T(8,128)(2,1)S(1)}, bf16[4,64,256]{2,1,0:T(8,128)(2,1)S(1)}, u32[]{:S(2)}, u32[]{:S(2)}) collective-permute-start(bf16[4,64,256]{2,1,0:T(8,128)(2,1)S(1)} %get-tuple-element.48), channel_id=1, source_target_pairs={{0,2},{1,3},{2,0},{3,1},{4,6},{5,7},{6,4},{7,5},{8,10},{9,11},{10,... | collective-permute-start | bytes 393224 | tf_op jit(solution)/shard_map/ppermute | solution.py:303
  11.2 8.5 %collective-permute-start.12 = (bf16[4,64,256]{2,1,0:T(8,128)(2,1)S(1)}, bf16[4,64,256]{2,1,0:T(8,128)(2,1)S(1)}, u32[]{:S(2)}, u32[]{:S(2)}) collective-permute-start(bf16[4,64,256]{2,1,0:T(8,128)(2,1)S(1)} %get-tuple-element.49), channel_id=1, source_target_pairs={{0,1},{1,0},{2,3},{3,2},{4,5},{5,4},{6,7},{7,6},{8,9},{9,8},{10,11... | collective-permute-start | bytes 393224 | tf_op jit(solution)/shard_map/ppermute | solution.py:303
  12.7 8.6 %collective-permute-start.13 = (bf16[4,64,256]{2,1,0:T(8,128)(2,1)S(1)}, bf16[4,64,256]{2,1,0:T(8,128)(2,1)S(1)}, u32[]{:S(2)}, u32[]{:S(2)}) collective-permute-start(bf16[4,64,256]{2,1,0:T(8,128)(2,1)S(1)} %get-tuple-element.50), channel_id=1, source_target_pairs={{0,3},{1,2},{2,1},{3,0},{4,7},{5,6},{6,5},{7,4},{8,11},{9,10},{10,... | collective-permute-start | bytes 393224 | tf_op jit(solution)/shard_map/ppermute | solution.py:303
  17.9 6.7 %collective-permute-start.4 = (bf16[2,256,256]{2,1,0:T(8,128)(2,1)S(1)}, bf16[2,256,256]{2,1,0:T(8,128)(2,1)S(1)}, u32[]{:S(2)}, u32[]{:S(2)}) collective-permute-start(bf16[2,256,256]{2,1,0:T(8,128)(2,1)S(1)} %get-tuple-element.41), channel_id=1, source_target_pairs={{0,4},{1,5},{2,6},{3,7},{4,0},{5,1},{6,2},{7,3},{8,12},{9,13},{10,... | collective-permute-start | bytes 786440 | tf_op jit(solution)/shard_map/ppermute | solution.py:303
  22.6 10.4 %collective-permute-start.14 = (bf16[2,256,256]{2,1,0:T(8,128)(2,1)S(1)}, bf16[2,256,256]{2,1,0:T(8,128)(2,1)S(1)}, u32[]{:S(2)}, u32[]{:S(2)}) collective-permute-start(bf16[2,256,256]{2,1,0:T(8,128)(2,1)S(1)} %get-tuple-element.54), channel_id=1, source_target_pairs={{0,4},{1,5},{2,6},{3,7},{4,0},{5,1},{6,2},{7,3},{8,12},{9,13},{10,... | collective-permute-start | bytes 786440 | tf_op jit(solution)/shard_map/ppermute | solution.py:303
  24.7 8.8 %collective-permute-start.5 = (bf16[256,256]{1,0:T(8,128)(2,1)S(1)}, bf16[256,256]{1,0:T(8,128)(2,1)S(1)}, u32[]{:S(2)}, u32[]{:S(2)}) collective-permute-start(bf16[256,256]{1,0:T(8,128)(2,1)S(1)} %get-tuple-element.42), channel_id=1, source_target_pairs={{0,4},{1,5},{2,6},{3,7},{4,12},{5,13},{6,14},{7,15},{8,0},{9,1},{1... | collective-permute-start | bytes 393224 | tf_op jit(solution)/shard_map/ppermute | solution.py:303
  26.5 7.0 %collective-permute-start.6 = (bf16[256,256]{1,0:T(8,128)(2,1)S(1)}, bf16[256,256]{1,0:T(8,128)(2,1)S(1)}, u32[]{:S(2)}, u32[]{:S(2)}) collective-permute-start(bf16[256,256]{1,0:T(8,128)(2,1)S(1)} %get-tuple-element.43), channel_id=1, source_target_pairs={{0,16},{1,17},{2,18},{3,19},{4,8},{5,9},{6,10},{7,11},{8,4},{9,5},... | collective-permute-start | bytes 393224 | tf_op jit(solution)/shard_map/ppermute | solution.py:303
  33.1 7.1 %collective-permute-start.15 = (bf16[256,256]{1,0:T(8,128)(2,1)S(1)}, bf16[256,256]{1,0:T(8,128)(2,1)S(1)}, u32[]{:S(2)}, u32[]{:S(2)}) collective-permute-start(bf16[256,256]{1,0:T(8,128)(2,1)S(1)} %get-tuple-element.55), channel_id=1, source_target_pairs={{0,4},{1,5},{2,6},{3,7},{4,12},{5,13},{6,14},{7,15},{8,0},{9,1},{1... | collective-permute-start | bytes 393224 | tf_op jit(solution)/shard_map/ppermute | solution.py:303
  33.5 6.7 %collective-permute-start.16 = (bf16[256,256]{1,0:T(8,128)(2,1)S(1)}, bf16[256,256]{1,0:T(8,128)(2,1)S(1)}, u32[]{:S(2)}, u32[]{:S(2)}) collective-permute-start(bf16[256,256]{1,0:T(8,128)(2,1)S(1)} %get-tuple-element.56), channel_id=1, source_target_pairs={{0,16},{1,17},{2,18},{3,19},{4,8},{5,9},{6,10},{7,11},{8,4},{9,5},... | collective-permute-start | bytes 393224 | tf_op jit(solution)/shard_map/ppermute | solution.py:303
  33.6 12.6 %collective-permute-start.7 = (bf16[128,256]{1,0:T(8,128)(2,1)S(1)}, bf16[128,256]{1,0:T(8,128)(2,1)S(1)}, u32[]{:S(2)}, u32[]{:S(2)}) collective-permute-start(bf16[128,256]{1,0:T(8,128)(2,1)S(1)} %get-tuple-element.45), channel_id=1, source_target_pairs={{0,2},{1,3},{2,0},{3,1},{4,6},{5,7},{6,4},{7,5},{8,10},{9,11},{10,... | collective-permute-start | bytes 196616 | tf_op jit(solution)/shard_map/ppermute | solution.py:303
  40.2 7.8 %collective-permute-start.17 = (bf16[128,256]{1,0:T(8,128)(2,1)S(1)}, bf16[128,256]{1,0:T(8,128)(2,1)S(1)}, u32[]{:S(2)}, u32[]{:S(2)}) collective-permute-start(bf16[128,256]{1,0:T(8,128)(2,1)S(1)} %get-tuple-element.58), channel_id=1, source_target_pairs={{0,2},{1,3},{2,0},{3,1},{4,6},{5,7},{6,4},{7,5},{8,10},{9,11},{10,... | collective-permute-start | bytes 196616 | tf_op jit(solution)/shard_map/ppermute | solution.py:303
  41.8 5.2 %collective-permute-start.8 = (bf16[128,256]{1,0:T(8,128)(2,1)S(1)}, bf16[128,256]{1,0:T(8,128)(2,1)S(1)}, u32[]{:S(2)}, u32[]{:S(2)}) collective-permute-start(bf16[128,256]{1,0:T(8,128)(2,1)S(1)} %get-tuple-element.46), channel_id=1, source_target_pairs={{0,3},{1,2},{2,1},{3,0},{4,7},{5,6},{6,5},{7,4},{8,11},{9,10},{10,... | collective-permute-start | bytes 196616 | tf_op jit(solution)/shard_map/ppermute | solution.py:303
  43.2 4.3 %collective-permute-start.9 = (bf16[128,256]{1,0:T(8,128)(2,1)S(1)}, bf16[128,256]{1,0:T(8,128)(2,1)S(1)}, u32[]{:S(2)}, u32[]{:S(2)}) collective-permute-start(bf16[128,256]{1,0:T(8,128)(2,1)S(1)} %get-tuple-element.44.refs_1_), channel_id=1, source_target_pairs={{0,1},{1,0},{2,3},{3,2},{4,5},{5,4},{6,7},{7,6},{8,9},{9,8},{10,11... | collective-permute-start | bytes 196616 | tf_op jit(solution)/shard_map/ppermute | solution.py:303
  43.8 5.3 %collective-permute-start.18 = (bf16[128,256]{1,0:T(8,128)(2,1)S(1)}, bf16[128,256]{1,0:T(8,128)(2,1)S(1)}, u32[]{:S(2)}, u32[]{:S(2)}) collective-permute-start(bf16[128,256]{1,0:T(8,128)(2,1)S(1)} %get-tuple-element.59), channel_id=1, source_target_pairs={{0,3},{1,2},{2,1},{3,0},{4,7},{5,6},{6,5},{7,4},{8,11},{9,10},{10,... | collective-permute-start | bytes 196616 | tf_op jit(solution)/shard_map/ppermute | solution.py:303
  46.2 4.9 %copy-start.1 = (bf16[4,1024,512]{2,1,0:T(8,128)(2,1)S(1)}, bf16[4,1024,512]{2,1,0:T(8,128)(2,1)}, u32[]{:S(2)}) copy-start(bf16[4,1024,512]{2,1,0:T(8,128)(2,1)} %refs_2_.2) | copy-start | bytes 12582916
  46.2 4.9 %copy-start.2 = (s32[1,4]{1,0:T(1,128)S(1)}, s32[1,4]{1,0:T(1,128)}, u32[]{:S(2)}) copy-start(s32[1,4]{1,0:T(1,128)} %refs_0_.7) | copy-start | bytes 52
  46.2 4.9 %copy-start.3 = (s32[16]{0:T(128)S(1)}, s32[16]{0:T(128)}, u32[]{:S(2)}) copy-start(s32[16]{0:T(128)} %refs_1_.1) | copy-start | bytes 196
  46.2 4.3 %collective-permute-start.19 = (bf16[128,256]{1,0:T(8,128)(2,1)S(1)}, bf16[128,256]{1,0:T(8,128)(2,1)S(1)}, u32[]{:S(2)}, u32[]{:S(2)}) collective-permute-start(bf16[128,256]{1,0:T(8,128)(2,1)S(1)} %get-tuple-element.57.refs_1_), channel_id=1, source_target_pairs={{0,1},{1,0},{2,3},{3,2},{4,5},{5,4},{6,7},{7,6},{8,9},{9,8},{10,11... | collective-permute-start | bytes 196616 | tf_op jit(solution)/shard_map/ppermute | solution.py:303
  48.0 3.1 %collective-permute-start.10 = (bf16[128,1024]{1,0:T(8,128)(2,1)S(1)}, bf16[128,1024]{1,0:T(8,128)(2,1)S(1)}, u32[]{:S(2)}, u32[]{:S(2)}) collective-permute-start(bf16[128,1024]{1,0:T(8,128)(2,1)S(1)} %phase.2.refs_3_), channel_id=1, source_target_pairs={{0,16},{1,17},{2,18},{3,19},{4,20},{5,21},{6,22},{7,23},{8,24},{9,... | collective-permute-start | bytes 786440 | tf_op jit(solution)/shard_map/ppermute | solution.py:303
  51.0 1.6 %collective-permute-start.20 = (bf16[128,1024]{1,0:T(8,128)(2,1)S(1)}, bf16[128,1024]{1,0:T(8,128)(2,1)S(1)}, u32[]{:S(2)}, u32[]{:S(2)}) collective-permute-start(bf16[128,1024]{1,0:T(8,128)(2,1)S(1)} %phase.3.refs_5_), channel_id=1, source_target_pairs={{0,16},{1,17},{2,18},{3,19},{4,20},{5,21},{6,22},{7,23},{8,24},{9,... | collective-permute-start | bytes 786440 | tf_op jit(solution)/shard_map/ppermute | solution.py:303

commit v23 on v19

--- a/solution.py
+++ b/solution.py
@@ -12,8 +12,8 @@
 regularizer = 0.05
 bf16 = jnp.bfloat16
 f32 = jnp.float32
-send_order = (0, 2, 1, 3)
-tail_order = (0, 2, 3, 1)
+send_order = (0, 3, 2, 1)
+tail_order = (0, 3, 2, 1)
 
 
 def hartley(length):

time: 51.7 us -> 52.3 us (1.012)
  waiting for transfers between devices: 11.9 us -> 13 us
  starting transfers between devices: 28.9 us -> 28.3 us
    ppermute x23, waiting for transfers between devices: 11.9 us -> 13 us  [sent(): return lax.ppermute(value, ('dist', 'rows'), pairs)]
    ppermute x23, starting transfers between devices: 28.9 us -> 28.3 us  [sent(): return lax.ppermute(value, ('dist', 'rows'), pairs)]
where the time goes in v23:
time: 52.3 us; the launch traced here: 52.1 us
  starting transfers between devices  28.3 us (54%)
  waiting for transfers between devices  13 us (25%)
  Pallas kernels  10.6 us (20%)
    ppermute x23, starting transfers between devices, sent(): return lax.ppermute(value, ('dist', 'rows'), pairs)  28.3 us
    ppermute x23, waiting for transfers between devices, sent(): return lax.ppermute(value, ('dist', 'rows'), pairs)  13 us
    pallas_call x1, Pallas kernels, plane_plan(): pl.pallas_call(lambda *refs: filter_kernel(inner, dist_dev, *refs), out_s...  2.62 us
    pallas_call x2, Pallas kernels, plane_plan(): pl.pallas_call(lambda *refs: column_kernel(inner, outer, *refs), out_shap...  2.6 us
    pallas_call x1, Pallas kernels, plane_plan(): pl.pallas_call(lambda *refs: row_kernel(inner, *refs), out_shape=[shaped(...  1.83 us
    pallas_call x1, Pallas kernels, plane_plan(): pl.pallas_call(lambda *refs: recon_kernel(own, *refs), out_shape=[jax.Sha...  1.2 us
    pallas_call x1, Pallas kernels, plane_plan(): pl.pallas_call(recon_last_kernel, out_shape=shaped(capacity, pixels), in_...  1.12 us
  transfers between devices with their start and end apart: 23, of which 8 were waited for; matrix products, arithmetic and copies ran while one was open for 0% of the time, Pallas kernels for 15%

profile of v23, /device:TPU:0, one launch (start us, length us, event | category | flops | bytes accessed | tf_op | source)
XLA Modules:
  0.0 52.1 jit_solution(11419515616053727243)
XLA Ops:
  0.0 0.0 copy-start
  0.0 0.5 collective-permute-start
  0.5 2.6 %filters.1.refs_3_.refs_1_ = bf16[4,1024,256]{2,1,0:T(8,128)(2,1)S(1)} custom-call(f32[4]{0:T(128)} %refs_0_.6), custom_call_target="tpu_custom_call" | custom-call | flops 1 | bytes 1 | tf_op jit(solution)/shard_map/filters/pallas_call | solution.py:316
  3.1 0.0 collective-permute-done.refs_1_
  3.1 0.0 copy-done
  3.1 1.8 %row_spectra.1 = (bf16[4,64,256]{2,1,0:T(8,128)(2,1)S(1)}, bf16[4,64,256]{2,1,0:T(8,128)(2,1)S(1)}, bf16[4,64,256]{2,1,0:T(8,128)(2,1)S(1)}, bf16[4,64,256]{2,1,...) custom-call(bf16[4,2,64,1024]{3,2,1,0:T(8,128)(2,1)} %bitcast.2, ...), custom_call_target="tpu_custom_call" | custom-call | flops 1 | bytes 1 | tf_op jit(solution)/shard_map/row_spectra/pallas_call | solution.py:325
  4.9 3.7 %collective-permute-start.1 = (bf16[4,64,256]{2,1,0:T(8,128)(2,1)S(1)}, bf16[4,64,256]{2,1,0:T(8,128)(2,1)S(1)}, u32[]{:S(2)}, u32[]{:S(2)}) collective-permute-start(bf16[4,64,256]{2,1,0:T(8,128)(2,1)S(1)} %get-tuple-element.31), channel_id=1, source_target_pairs={{0,3},{1,2},{2,1},{3,0},{4,7},{5,6},{6,5},{7,4},{8,11},{9,10},{10,... | collective-permute-start | bytes 393224 | tf_op jit(solution)/shard_map/ppermute | solution.py:297
  8.6 0.5 collective-permute-start.2
  9.2 0.1 collective-permute-start.3
  9.3 2.8 %collective-permute-start.12 = (bf16[4,64,256]{2,1,0:T(8,128)(2,1)S(1)}, bf16[4,64,256]{2,1,0:T(8,128)(2,1)S(1)}, u32[]{:S(2)}, u32[]{:S(2)}) collective-permute-start(bf16[4,64,256]{2,1,0:T(8,128)(2,1)S(1)} %get-tuple-element.42), channel_id=1, source_target_pairs={{0,3},{1,2},{2,1},{3,0},{4,7},{5,6},{6,5},{7,4},{8,11},{9,10},{10,... | collective-permute-start | bytes 393224 | tf_op jit(solution)/shard_map/ppermute | solution.py:297
  12.1 0.5 collective-permute-start.13
  12.6 0.0 collective-permute-done.1.refs_3_
  12.6 2.3 %collective-permute-start.14 = (bf16[4,64,256]{2,1,0:T(8,128)(2,1)S(1)}, bf16[4,64,256]{2,1,0:T(8,128)(2,1)S(1)}, u32[]{:S(2)}, u32[]{:S(2)}) collective-permute-start(bf16[4,64,256]{2,1,0:T(8,128)(2,1)S(1)} %get-tuple-element.44), channel_id=1, source_target_pairs={{0,1},{1,0},{2,3},{3,2},{4,5},{5,4},{6,7},{7,6},{8,9},{9,8},{10,11... | collective-permute-start | bytes 393224 | tf_op jit(solution)/shard_map/ppermute | solution.py:297
  15.0 1.7 %collective-permute-done.2.refs_4_ = bf16[4,64,256]{2,1,0:T(8,128)(2,1)S(1)} collective-permute-done((bf16[4,64,256]{2,1,0:T(8,128)(2,1)S(1)}, bf16[4,64,256]{2,1,0:T(8,128)(2,1)S(1)}, u32[]{:S(2)}, u32[]{:S(2)}) %collective-permute-start.2) | collective-permute-done | bytes 131104 | tf_op jit(solution)/shard_map/ppermute | solution.py:297
  16.6 0.0 collective-permute-done.3.refs_5_
  16.6 1.3 %columns.2 = (bf16[256,256]{1,0:T(8,128)(2,1)S(1)}, bf16[256,256]{1,0:T(8,128)(2,1)S(1)}, bf16[256,256]{1,0:T(8,128)(2,1)S(1)}, bf16[256,256]{1,0:T(8,128)(2,1)S(1)}) custom-call(bf16[1024,1024]{1,0:T(8,128)(2,1)S(1)} %copy-done, bf16[4,1024,256]{2,1,0:T(8,128)(2,1)S(1)} %filters.1.refs_3_.refs_1_, bf16[4,64,256]{2,1,0:T(8,128)(2,1)S(1)} %get-tuple-element.30.refs_2_, ...), custom_call_target="tpu_custom_call" | custom-call | flops 1 | bytes 1 | tf_op jit(solution)/shard_map/columns/pallas_call | solution.py:344
  17.9 1.6 %collective-permute-start.4 = (bf16[256,256]{1,0:T(8,128)(2,1)S(1)}, bf16[256,256]{1,0:T(8,128)(2,1)S(1)}, u32[]{:S(2)}, u32[]{:S(2)}) collective-permute-start(bf16[256,256]{1,0:T(8,128)(2,1)S(1)} %get-tuple-element.36), channel_id=1, source_target_pairs={{0,4},{1,5},{2,6},{3,7},{4,0},{5,1},{6,2},{7,3},{8,12},{9,13},{10,... | collective-permute-start | bytes 393224 | tf_op jit(solution)/shard_map/ppermute | solution.py:297
  19.6 0.0 collective-permute-start.7
  19.6 0.0 collective-permute-done.12.refs_3_
  19.6 3.2 %collective-permute-start.6 = (bf16[256,256]{1,0:T(8,128)(2,1)S(1)}, bf16[256,256]{1,0:T(8,128)(2,1)S(1)}, u32[]{:S(2)}, u32[]{:S(2)}) collective-permute-start(bf16[256,256]{1,0:T(8,128)(2,1)S(1)} %get-tuple-element.37), channel_id=1, source_target_pairs={{0,4},{1,5},{2,6},{3,7},{4,0},{5,1},{6,2},{7,3},{8,12},{9,13},{10,... | collective-permute-start | bytes 393224 | tf_op jit(solution)/shard_map/ppermute | solution.py:297
  22.7 0.0 collective-permute-done.13.refs_4_
  22.7 0.0 collective-permute-done.14.refs_5_
  22.7 1.3 %columns.3 = (bf16[256,256]{1,0:T(8,128)(2,1)S(1)}, bf16[256,256]{1,0:T(8,128)(2,1)S(1)}, bf16[256,256]{1,0:T(8,128)(2,1)S(1)}, bf16[256,256]{1,0:T(8,128)(2,1)S(1)}) custom-call(bf16[1024,1024]{1,0:T(8,128)(2,1)S(1)} %copy-done, bf16[4,1024,256]{2,1,0:T(8,128)(2,1)S(1)} %filters.1.refs_3_.refs_1_, bf16[4,64,256]{2,1,0:T(8,128)(2,1)S(1)} %get-tuple-element.41.refs_2_, ...), custom_call_target="tpu_custom_call" | custom-call | flops 1 | bytes 1 | tf_op jit(solution)/shard_map/columns/pallas_call | solution.py:344
  24.1 0.1 collective-permute-start.15
  24.2 0.0 collective-permute-done.4.refs_1_.refs_2_
  24.2 0.1 far.2
  24.2 2.9 %collective-permute-start.5 = (bf16[256,256]{1,0:T(8,128)(2,1)S(1)}, bf16[256,256]{1,0:T(8,128)(2,1)S(1)}, u32[]{:S(2)}, u32[]{:S(2)}) collective-permute-start(bf16[256,256]{1,0:T(8,128)(2,1)S(1)} %far.2), channel_id=1, source_target_pairs={{0,8},{1,9},{2,10},{3,11},{4,12},{5,13},{6,14},{7,15},{8,0},{9,1},... | collective-permute-start | bytes 393224 | tf_op jit(solution)/shard_map/ppermute | solution.py:297
  27.1 0.0 collective-permute-start.18
  27.1 0.0 collective-permute-done.7.refs_4_.refs_1_
  27.1 1.6 %collective-permute-start.17 = (bf16[256,256]{1,0:T(8,128)(2,1)S(1)}, bf16[256,256]{1,0:T(8,128)(2,1)S(1)}, u32[]{:S(2)}, u32[]{:S(2)}) collective-permute-start(bf16[256,256]{1,0:T(8,128)(2,1)S(1)} %get-tuple-element.48), channel_id=1, source_target_pairs={{0,4},{1,5},{2,6},{3,7},{4,0},{5,1},{6,2},{7,3},{8,12},{9,13},{10,... | collective-permute-start | bytes 393224 | tf_op jit(solution)/shard_map/ppermute | solution.py:297
  28.7 0.0 collective-permute-done.6.refs_3_.refs_0_
  28.7 3.2 %collective-permute-done.15.refs_3_.refs_2_ = bf16[256,256]{1,0:T(8,128)(2,1)S(1)} collective-permute-done((bf16[256,256]{1,0:T(8,128)(2,1)S(1)}, bf16[256,256]{1,0:T(8,128)(2,1)S(1)}, u32[]{:S(2)}, u32[]{:S(2)}) %collective-permute-start.15) | collective-permute-done | bytes 131104 | tf_op jit(solution)/shard_map/ppermute | solution.py:297
  31.9 0.1 far.3
  32.0 1.2 %collective-permute-start.16 = (bf16[256,256]{1,0:T(8,128)(2,1)S(1)}, bf16[256,256]{1,0:T(8,128)(2,1)S(1)}, u32[]{:S(2)}, u32[]{:S(2)}) collective-permute-start(bf16[256,256]{1,0:T(8,128)(2,1)S(1)} %far.3), channel_id=1, source_target_pairs={{0,8},{1,9},{2,10},{3,11},{4,12},{5,13},{6,14},{7,15},{8,0},{9,1},... | collective-permute-start | bytes 393224 | tf_op jit(solution)/shard_map/ppermute | solution.py:297
  33.1 1.1 %collective-permute-done.5.refs_1_ = bf16[256,256]{1,0:T(8,128)(2,1)S(1)} collective-permute-done((bf16[256,256]{1,0:T(8,128)(2,1)S(1)}, bf16[256,256]{1,0:T(8,128)(2,1)S(1)}, u32[]{:S(2)}, u32[]{:S(2)}) %collective-permute-start.5) | collective-permute-done | bytes 131104 | tf_op jit(solution)/shard_map/ppermute | solution.py:297
  34.3 0.1 half.2
  34.4 2.5 %collective-permute-start.8 = (bf16[128,256]{1,0:T(8,128)(2,1)S(1)}, bf16[128,256]{1,0:T(8,128)(2,1)S(1)}, u32[]{:S(2)}, u32[]{:S(2)}) collective-permute-start(bf16[128,256]{1,0:T(8,128)(2,1)S(1)} %get-tuple-element.39), channel_id=1, source_target_pairs={{0,3},{1,2},{2,1},{3,0},{4,7},{5,6},{6,5},{7,4},{8,11},{9,10},{10,... | collective-permute-start | bytes 196616 | tf_op jit(solution)/shard_map/ppermute | solution.py:297
  36.8 0.7 %collective-permute-start.9 = (bf16[128,256]{1,0:T(8,128)(2,1)S(1)}, bf16[128,256]{1,0:T(8,128)(2,1)S(1)}, u32[]{:S(2)}, u32[]{:S(2)}) collective-permute-start(bf16[128,256]{1,0:T(8,128)(2,1)S(1)} %get-tuple-element.40), channel_id=1, source_target_pairs={{0,2},{1,3},{2,0},{3,1},{4,6},{5,7},{6,4},{7,5},{8,10},{9,11},{10,... | collective-permute-start | bytes 196616 | tf_op jit(solution)/shard_map/ppermute | solution.py:297
  37.6 0.0 collective-permute-done.18.refs_4_
  37.6 0.4 collective-permute-start.10
  37.9 0.0 collective-permute-done.17.refs_3_
  37.9 3.5 %collective-permute-done.16.refs_1_ = bf16[256,256]{1,0:T(8,128)(2,1)S(1)} collective-permute-done((bf16[256,256]{1,0:T(8,128)(2,1)S(1)}, bf16[256,256]{1,0:T(8,128)(2,1)S(1)}, u32[]{:S(2)}, u32[]{:S(2)}) %collective-permute-start.16) | collective-permute-done | bytes 131104 | tf_op jit(solution)/shard_map/ppermute | solution.py:297
  41.4 0.1 half.3
  41.5 1.4 %collective-permute-start.19 = (bf16[128,256]{1,0:T(8,128)(2,1)S(1)}, bf16[128,256]{1,0:T(8,128)(2,1)S(1)}, u32[]{:S(2)}, u32[]{:S(2)}) collective-permute-start(bf16[128,256]{1,0:T(8,128)(2,1)S(1)} %get-tuple-element.50), channel_id=1, source_target_pairs={{0,3},{1,2},{2,1},{3,0},{4,7},{5,6},{6,5},{7,4},{8,11},{9,10},{10,... | collective-permute-start | bytes 196616 | tf_op jit(solution)/shard_map/ppermute | solution.py:297
  43.0 1.6 %collective-permute-start.20 = (bf16[128,256]{1,0:T(8,128)(2,1)S(1)}, bf16[128,256]{1,0:T(8,128)(2,1)S(1)}, u32[]{:S(2)}, u32[]{:S(2)}) collective-permute-start(bf16[128,256]{1,0:T(8,128)(2,1)S(1)} %get-tuple-element.51), channel_id=1, source_target_pairs={{0,2},{1,3},{2,0},{3,1},{4,6},{5,7},{6,4},{7,5},{8,10},{9,11},{10,... | collective-permute-start | bytes 196616 | tf_op jit(solution)/shard_map/ppermute | solution.py:297
  44.6 0.0 collective-permute-done.8.refs_2_
  44.6 0.0 copy-start.1
  44.6 0.6 %collective-permute-start.21 = (bf16[128,256]{1,0:T(8,128)(2,1)S(1)}, bf16[128,256]{1,0:T(8,128)(2,1)S(1)}, u32[]{:S(2)}, u32[]{:S(2)}) collective-permute-start(bf16[128,256]{1,0:T(8,128)(2,1)S(1)} %get-tuple-element.49.refs_1_), channel_id=1, source_target_pairs={{0,1},{1,0},{2,3},{3,2},{4,5},{5,4},{6,7},{7,6},{8,9},{9,8},{10,11... | collective-permute-start | bytes 196616 | tf_op jit(solution)/shard_map/ppermute | solution.py:297
  45.2 0.0 collective-permute-done.9.refs_3_
  45.2 0.0 collective-permute-done.10.refs_4_
  45.2 0.5 phase.2.refs_3_
  45.7 0.1 collective-permute-start.11
  45.7 1.1 %collective-permute-done.19.refs_2_ = bf16[128,256]{1,0:T(8,128)(2,1)S(1)} collective-permute-done((bf16[128,256]{1,0:T(8,128)(2,1)S(1)}, bf16[128,256]{1,0:T(8,128)(2,1)S(1)}, u32[]{:S(2)}, u32[]{:S(2)}) %collective-permute-start.19) | collective-permute-done | bytes 65568 | tf_op jit(solution)/shard_map/ppermute | solution.py:297
  46.8 0.7 %collective-permute-done.20.refs_3_ = bf16[128,256]{1,0:T(8,128)(2,1)S(1)} collective-permute-done((bf16[128,256]{1,0:T(8,128)(2,1)S(1)}, bf16[128,256]{1,0:T(8,128)(2,1)S(1)}, u32[]{:S(2)}, u32[]{:S(2)}) %collective-permute-start.20) | collective-permute-done | bytes 65568 | tf_op jit(solution)/shard_map/ppermute | solution.py:297
  47.5 1.4 %collective-permute-done.21.refs_4_ = bf16[128,256]{1,0:T(8,128)(2,1)S(1)} collective-permute-done((bf16[128,256]{1,0:T(8,128)(2,1)S(1)}, bf16[128,256]{1,0:T(8,128)(2,1)S(1)}, u32[]{:S(2)}, u32[]{:S(2)}) %collective-permute-start.21) | collective-permute-done | bytes 65568 | tf_op jit(solution)/shard_map/ppermute | solution.py:297
  48.9 0.5 phase.3.refs_5_
  49.4 0.1 collective-permute-start.22
  49.5 0.0 collective-permute-done.11.refs_4_
  49.5 0.0 copy-done.1
  49.5 0.0 copy-done.2
  49.5 0.0 copy-done.3
  49.5 1.2 %recon.2 = (f32[128,512]{1,0:T(8,128)S(1)}, bf16[1024,512]{1,0:T(8,128)(2,1)S(1)}, bf16[128,128]{1,0:T(8,128)(2,1)S(1)}) custom-call(s32[1,4]{1,0:T(1,128)S(1)} %copy-done.2, s32[16]{0:T(128)S(1)} %copy-done.3, bf16[4,1024,512]{2,1,0:T(8,128)(2,1)S(1)} %copy-done.1, bf16[128,1024]{1,0:T(8,128)(2,1)S(1)} %phase.2.refs_3_, ...), custom_call_target="tpu_custom_call" | custom-call | flops 1 | bytes 1 | tf_op jit(solution)/shard_map/recon/pallas_call | solution.py:397
  50.7 0.3 collective-permute-done.22.phase
  51.0 1.1 %recon.3 = bf16[128,512]{1,0:T(8,128)(2,1)} custom-call(bf16[1024,512]{1,0:T(8,128)(2,1)S(1)} %get-tuple-element.52.weights, bf16[128,1024]{1,0:T(8,128)(2,1)S(1)} %collective-permute-done.22.phase, f32[128,512]{1,0:T(8,128)S(1)} %get-tuple-element.53.before, bf16[128,128]{1,0:T(8,128)(2,1)S(1)} %get-tuple-element.54.select), custom_call_target="tpu_custom_call" | custom-call | flops 1 | bytes 1 | tf_op jit(solution)/shard_map/recon/pallas_call | solution.py:410
  (2 shorter events, 0.0 us)
Async XLA Ops:
  0.0 3.1 %copy-start = (bf16[1024,1024]{1,0:T(8,128)(2,1)S(1)}, bf16[1024,1024]{1,0:T(8,128)(2,1)}, u32[]{:S(2)}) copy-start(bf16[1024,1024]{1,0:T(8,128)(2,1)} %constant.2.clone.refs_2_.refs_0_) | copy-start | bytes 6291460
  0.0 3.1 %collective-permute-start = (bf16[4,2,64,1024]{3,2,1,0:T(8,128)(2,1)}, bf16[4,2,64,1024]{3,2,1,0:T(8,128)(2,1)S(1)}, u32[]{:S(2)}, u32[]{:S(2)}) collective-permute-start(bf16[4,2,64,1024]{3,2,1,0:T(8,128)(2,1)} %bitcast.1), channel_id=1, source_target_pairs={{0,16},{1,17},{2,18},{3,19},{4,20},{5,21},{6,22},{7,23},{8,24},{9,... | collective-permute-start | bytes 3145736 | tf_op jit(solution)/shard_map/ppermute | solution.py:297
  4.9 7.7 %collective-permute-start.1 = (bf16[4,64,256]{2,1,0:T(8,128)(2,1)S(1)}, bf16[4,64,256]{2,1,0:T(8,128)(2,1)S(1)}, u32[]{:S(2)}, u32[]{:S(2)}) collective-permute-start(bf16[4,64,256]{2,1,0:T(8,128)(2,1)S(1)} %get-tuple-element.31), channel_id=1, source_target_pairs={{0,3},{1,2},{2,1},{3,0},{4,7},{5,6},{6,5},{7,4},{8,11},{9,10},{10,... | collective-permute-start | bytes 393224 | tf_op jit(solution)/shard_map/ppermute | solution.py:297
  8.6 8.0 %collective-permute-start.2 = (bf16[4,64,256]{2,1,0:T(8,128)(2,1)S(1)}, bf16[4,64,256]{2,1,0:T(8,128)(2,1)S(1)}, u32[]{:S(2)}, u32[]{:S(2)}) collective-permute-start(bf16[4,64,256]{2,1,0:T(8,128)(2,1)S(1)} %get-tuple-element.32), channel_id=1, source_target_pairs={{0,2},{1,3},{2,0},{3,1},{4,6},{5,7},{6,4},{7,5},{8,10},{9,11},{10,... | collective-permute-start | bytes 393224 | tf_op jit(solution)/shard_map/ppermute | solution.py:297
  9.2 7.5 %collective-permute-start.3 = (bf16[4,64,256]{2,1,0:T(8,128)(2,1)S(1)}, bf16[4,64,256]{2,1,0:T(8,128)(2,1)S(1)}, u32[]{:S(2)}, u32[]{:S(2)}) collective-permute-start(bf16[4,64,256]{2,1,0:T(8,128)(2,1)S(1)} %get-tuple-element.33), channel_id=1, source_target_pairs={{0,1},{1,0},{2,3},{3,2},{4,5},{5,4},{6,7},{7,6},{8,9},{9,8},{10,11... | collective-permute-start | bytes 393224 | tf_op jit(solution)/shard_map/ppermute | solution.py:297
  9.3 10.3 %collective-permute-start.12 = (bf16[4,64,256]{2,1,0:T(8,128)(2,1)S(1)}, bf16[4,64,256]{2,1,0:T(8,128)(2,1)S(1)}, u32[]{:S(2)}, u32[]{:S(2)}) collective-permute-start(bf16[4,64,256]{2,1,0:T(8,128)(2,1)S(1)} %get-tuple-element.42), channel_id=1, source_target_pairs={{0,3},{1,2},{2,1},{3,0},{4,7},{5,6},{6,5},{7,4},{8,11},{9,10},{10,... | collective-permute-start | bytes 393224 | tf_op jit(solution)/shard_map/ppermute | solution.py:297
  12.1 10.6 %collective-permute-start.13 = (bf16[4,64,256]{2,1,0:T(8,128)(2,1)S(1)}, bf16[4,64,256]{2,1,0:T(8,128)(2,1)S(1)}, u32[]{:S(2)}, u32[]{:S(2)}) collective-permute-start(bf16[4,64,256]{2,1,0:T(8,128)(2,1)S(1)} %get-tuple-element.43), channel_id=1, source_target_pairs={{0,2},{1,3},{2,0},{3,1},{4,6},{5,7},{6,4},{7,5},{8,10},{9,11},{10,... | collective-permute-start | bytes 393224 | tf_op jit(solution)/shard_map/ppermute | solution.py:297
  12.6 10.1 %collective-permute-start.14 = (bf16[4,64,256]{2,1,0:T(8,128)(2,1)S(1)}, bf16[4,64,256]{2,1,0:T(8,128)(2,1)S(1)}, u32[]{:S(2)}, u32[]{:S(2)}) collective-permute-start(bf16[4,64,256]{2,1,0:T(8,128)(2,1)S(1)} %get-tuple-element.44), channel_id=1, source_target_pairs={{0,1},{1,0},{2,3},{3,2},{4,5},{5,4},{6,7},{7,6},{8,9},{9,8},{10,11... | collective-permute-start | bytes 393224 | tf_op jit(solution)/shard_map/ppermute | solution.py:297
  17.9 6.2 %collective-permute-start.4 = (bf16[256,256]{1,0:T(8,128)(2,1)S(1)}, bf16[256,256]{1,0:T(8,128)(2,1)S(1)}, u32[]{:S(2)}, u32[]{:S(2)}) collective-permute-start(bf16[256,256]{1,0:T(8,128)(2,1)S(1)} %get-tuple-element.36), channel_id=1, source_target_pairs={{0,4},{1,5},{2,6},{3,7},{4,0},{5,1},{6,2},{7,3},{8,12},{9,13},{10,... | collective-permute-start | bytes 393224 | tf_op jit(solution)/shard_map/ppermute | solution.py:297
  19.6 7.5 %collective-permute-start.7 = (bf16[256,256]{1,0:T(8,128)(2,1)S(1)}, bf16[256,256]{1,0:T(8,128)(2,1)S(1)}, u32[]{:S(2)}, u32[]{:S(2)}) collective-permute-start(bf16[256,256]{1,0:T(8,128)(2,1)S(1)} %get-tuple-element.37), channel_id=1, source_target_pairs={{0,16},{1,17},{2,18},{3,19},{4,8},{5,9},{6,10},{7,11},{8,4},{9,5},... | collective-permute-start | bytes 393224 | tf_op jit(solution)/shard_map/ppermute | solution.py:297
  19.6 9.1 %collective-permute-start.6 = (bf16[256,256]{1,0:T(8,128)(2,1)S(1)}, bf16[256,256]{1,0:T(8,128)(2,1)S(1)}, u32[]{:S(2)}, u32[]{:S(2)}) collective-permute-start(bf16[256,256]{1,0:T(8,128)(2,1)S(1)} %get-tuple-element.37), channel_id=1, source_target_pairs={{0,4},{1,5},{2,6},{3,7},{4,0},{5,1},{6,2},{7,3},{8,12},{9,13},{10,... | collective-permute-start | bytes 393224 | tf_op jit(solution)/shard_map/ppermute | solution.py:297
  24.1 7.9 %collective-permute-start.15 = (bf16[256,256]{1,0:T(8,128)(2,1)S(1)}, bf16[256,256]{1,0:T(8,128)(2,1)S(1)}, u32[]{:S(2)}, u32[]{:S(2)}) collective-permute-start(bf16[256,256]{1,0:T(8,128)(2,1)S(1)} %get-tuple-element.47), channel_id=1, source_target_pairs={{0,4},{1,5},{2,6},{3,7},{4,0},{5,1},{6,2},{7,3},{8,12},{9,13},{10,... | collective-permute-start | bytes 393224 | tf_op jit(solution)/shard_map/ppermute | solution.py:297
  24.2 10.0 %collective-permute-start.5 = (bf16[256,256]{1,0:T(8,128)(2,1)S(1)}, bf16[256,256]{1,0:T(8,128)(2,1)S(1)}, u32[]{:S(2)}, u32[]{:S(2)}) collective-permute-start(bf16[256,256]{1,0:T(8,128)(2,1)S(1)} %far.2), channel_id=1, source_target_pairs={{0,8},{1,9},{2,10},{3,11},{4,12},{5,13},{6,14},{7,15},{8,0},{9,1},... | collective-permute-start | bytes 393224 | tf_op jit(solution)/shard_map/ppermute | solution.py:297
  27.1 10.5 %collective-permute-start.18 = (bf16[256,256]{1,0:T(8,128)(2,1)S(1)}, bf16[256,256]{1,0:T(8,128)(2,1)S(1)}, u32[]{:S(2)}, u32[]{:S(2)}) collective-permute-start(bf16[256,256]{1,0:T(8,128)(2,1)S(1)} %get-tuple-element.48), channel_id=1, source_target_pairs={{0,16},{1,17},{2,18},{3,19},{4,8},{5,9},{6,10},{7,11},{8,4},{9,5},... | collective-permute-start | bytes 393224 | tf_op jit(solution)/shard_map/ppermute | solution.py:297
  27.1 10.8 %collective-permute-start.17 = (bf16[256,256]{1,0:T(8,128)(2,1)S(1)}, bf16[256,256]{1,0:T(8,128)(2,1)S(1)}, u32[]{:S(2)}, u32[]{:S(2)}) collective-permute-start(bf16[256,256]{1,0:T(8,128)(2,1)S(1)} %get-tuple-element.48), channel_id=1, source_target_pairs={{0,4},{1,5},{2,6},{3,7},{4,0},{5,1},{6,2},{7,3},{8,12},{9,13},{10,... | collective-permute-start | bytes 393224 | tf_op jit(solution)/shard_map/ppermute | solution.py:297
  32.0 9.5 %collective-permute-start.16 = (bf16[256,256]{1,0:T(8,128)(2,1)S(1)}, bf16[256,256]{1,0:T(8,128)(2,1)S(1)}, u32[]{:S(2)}, u32[]{:S(2)}) collective-permute-start(bf16[256,256]{1,0:T(8,128)(2,1)S(1)} %far.3), channel_id=1, source_target_pairs={{0,8},{1,9},{2,10},{3,11},{4,12},{5,13},{6,14},{7,15},{8,0},{9,1},... | collective-permute-start | bytes 393224 | tf_op jit(solution)/shard_map/ppermute | solution.py:297
  34.4 10.2 %collective-permute-start.8 = (bf16[128,256]{1,0:T(8,128)(2,1)S(1)}, bf16[128,256]{1,0:T(8,128)(2,1)S(1)}, u32[]{:S(2)}, u32[]{:S(2)}) collective-permute-start(bf16[128,256]{1,0:T(8,128)(2,1)S(1)} %get-tuple-element.39), channel_id=1, source_target_pairs={{0,3},{1,2},{2,1},{3,0},{4,7},{5,6},{6,5},{7,4},{8,11},{9,10},{10,... | collective-permute-start | bytes 196616 | tf_op jit(solution)/shard_map/ppermute | solution.py:297
  36.8 8.4 %collective-permute-start.9 = (bf16[128,256]{1,0:T(8,128)(2,1)S(1)}, bf16[128,256]{1,0:T(8,128)(2,1)S(1)}, u32[]{:S(2)}, u32[]{:S(2)}) collective-permute-start(bf16[128,256]{1,0:T(8,128)(2,1)S(1)} %get-tuple-element.40), channel_id=1, source_target_pairs={{0,2},{1,3},{2,0},{3,1},{4,6},{5,7},{6,4},{7,5},{8,10},{9,11},{10,... | collective-permute-start | bytes 196616 | tf_op jit(solution)/shard_map/ppermute | solution.py:297
  37.6 7.6 %collective-permute-start.10 = (bf16[128,256]{1,0:T(8,128)(2,1)S(1)}, bf16[128,256]{1,0:T(8,128)(2,1)S(1)}, u32[]{:S(2)}, u32[]{:S(2)}) collective-permute-start(bf16[128,256]{1,0:T(8,128)(2,1)S(1)} %get-tuple-element.38.refs_1_), channel_id=1, source_target_pairs={{0,1},{1,0},{2,3},{3,2},{4,5},{5,4},{6,7},{7,6},{8,9},{9,8},{10,11... | collective-permute-start | bytes 196616 | tf_op jit(solution)/shard_map/ppermute | solution.py:297
  41.5 5.3 %collective-permute-start.19 = (bf16[128,256]{1,0:T(8,128)(2,1)S(1)}, bf16[128,256]{1,0:T(8,128)(2,1)S(1)}, u32[]{:S(2)}, u32[]{:S(2)}) collective-permute-start(bf16[128,256]{1,0:T(8,128)(2,1)S(1)} %get-tuple-element.50), channel_id=1, source_target_pairs={{0,3},{1,2},{2,1},{3,0},{4,7},{5,6},{6,5},{7,4},{8,11},{9,10},{10,... | collective-permute-start | bytes 196616 | tf_op jit(solution)/shard_map/ppermute | solution.py:297
  43.0 4.5 %collective-permute-start.20 = (bf16[128,256]{1,0:T(8,128)(2,1)S(1)}, bf16[128,256]{1,0:T(8,128)(2,1)S(1)}, u32[]{:S(2)}, u32[]{:S(2)}) collective-permute-start(bf16[128,256]{1,0:T(8,128)(2,1)S(1)} %get-tuple-element.51), channel_id=1, source_target_pairs={{0,2},{1,3},{2,0},{3,1},{4,6},{5,7},{6,4},{7,5},{8,10},{9,11},{10,... | collective-permute-start | bytes 196616 | tf_op jit(solution)/shard_map/ppermute | solution.py:297
  44.6 4.9 %copy-start.1 = (bf16[4,1024,512]{2,1,0:T(8,128)(2,1)S(1)}, bf16[4,1024,512]{2,1,0:T(8,128)(2,1)}, u32[]{:S(2)}) copy-start(bf16[4,1024,512]{2,1,0:T(8,128)(2,1)} %refs_2_.2) | copy-start | bytes 12582916
  44.6 4.9 %copy-start.2 = (s32[1,4]{1,0:T(1,128)S(1)}, s32[1,4]{1,0:T(1,128)}, u32[]{:S(2)}) copy-start(s32[1,4]{1,0:T(1,128)} %refs_0_.7) | copy-start | bytes 52
  44.6 4.9 %copy-start.3 = (s32[16]{0:T(128)S(1)}, s32[16]{0:T(128)}, u32[]{:S(2)}) copy-start(s32[16]{0:T(128)} %refs_1_.1) | copy-start | bytes 196
  44.6 4.3 %collective-permute-start.21 = (bf16[128,256]{1,0:T(8,128)(2,1)S(1)}, bf16[128,256]{1,0:T(8,128)(2,1)S(1)}, u32[]{:S(2)}, u32[]{:S(2)}) collective-permute-start(bf16[128,256]{1,0:T(8,128)(2,1)S(1)} %get-tuple-element.49.refs_1_), channel_id=1, source_target_pairs={{0,1},{1,0},{2,3},{3,2},{4,5},{5,4},{6,7},{7,6},{8,9},{9,8},{10,11... | collective-permute-start | bytes 196616 | tf_op jit(solution)/shard_map/ppermute | solution.py:297
  45.7 3.8 %collective-permute-start.11 = (bf16[128,1024]{1,0:T(8,128)(2,1)S(1)}, bf16[128,1024]{1,0:T(8,128)(2,1)S(1)}, u32[]{:S(2)}, u32[]{:S(2)}) collective-permute-start(bf16[128,1024]{1,0:T(8,128)(2,1)S(1)} %phase.2.refs_3_), channel_id=1, source_target_pairs={{0,16},{1,17},{2,18},{3,19},{4,20},{5,21},{6,22},{7,23},{8,24},{9,... | collective-permute-start | bytes 786440 | tf_op jit(solution)/shard_map/ppermute | solution.py:297
  49.4 1.6 %collective-permute-start.22 = (bf16[128,1024]{1,0:T(8,128)(2,1)S(1)}, bf16[128,1024]{1,0:T(8,128)(2,1)S(1)}, u32[]{:S(2)}, u32[]{:S(2)}) collective-permute-start(bf16[128,1024]{1,0:T(8,128)(2,1)S(1)} %phase.3.refs_5_), channel_id=1, source_target_pairs={{0,16},{1,17},{2,18},{3,19},{4,20},{5,21},{6,22},{7,23},{8,24},{9,... | collective-permute-start | bytes 786440 | tf_op jit(solution)/shard_map/ppermute | solution.py:297

commit v24 on v19

--- a/solution.py
+++ b/solution.py
@@ -98,24 +98,34 @@
     return lax.axis_index("dist"), device // inner, device % inner
 
 
-def row_kernel(inner, holo, there, table, after, *refs):
-    outs, mine, loaded = refs[:-2], refs[-2], refs[-1]
+def take_kernel(holo, after, out, arrived):
+    own = out.shape[0]
+    core = lax.axis_index("dist")
+    copy = pltpu.make_async_copy(holo.at[pl.ds(core * own, own)], out, arrived)
+    copy.start()
+    copy.wait()
+
+
+def row_kernel(inner, mine, there, table, *outs):
     own = len(outs) // inner
     core, _, spot = position(inner)
     _, dist_dev, rows_dev, width = there.shape
     block = width // inner
-    copy = pltpu.make_async_copy(holo.at[pl.ds(core * own, own)], mine, loaded)
-    copy.start()
-    for first, source in ((dist_dev, there.at[pl.ds(core * own, own)]), (0, mine)):
-        if first == 0:
-            copy.wait()
-        rows = source[...].reshape(own * dist_dev * rows_dev, width)
-        for rel in range(inner):
-            part = table[:, pl.ds(pl.multiple_of((spot ^ rel) * block, block), block)]
-            got = jnp.dot(rows, part, preferred_element_type=f32).astype(bf16)
-            got = got.reshape(own, dist_dev, rows_dev, block)
-            for chunk in range(own):
-                outs[chunk * inner + rel][first : first + dist_dev] = got[chunk]
+    rows = jnp.concatenate(
+        [
+            source.reshape(own * dist_dev * rows_dev, width)
+            for source in (mine[...], there[pl.ds(core * own, own)])
+        ],
+        axis=0,
+    )
+    for rel in range(inner):
+        part = table[:, pl.ds(pl.multiple_of((spot ^ rel) * block, block), block)]
+        got = jnp.dot(rows, part, preferred_element_type=f32).astype(bf16)
+        got = got.reshape(2, own, dist_dev, rows_dev, block)
+        for chunk in range(own):
+            out = outs[chunk * inner + rel]
+            out[0:dist_dev] = got[0, chunk]
+            out[dist_dev:] = got[1, chunk]
 
 
 def whole_turns(scale, square):
@@ -123,8 +133,9 @@
     return (turns - jnp.round(turns)) * (2.0 * math.pi)
 
 
-def filter_kernel(inner, dist_dev, turns, out):
-    dists, width, block = out.shape
+def filter_kernel(inner, dist_dev, turns, after, out):
+    dists, height, block = out.shape
+    width = height
     core, _, spot = position(inner)
 
     def square(first, length):
@@ -141,14 +152,14 @@
             rows.append(whole_turns(scale, values))
         return jnp.concatenate(rows, axis=0)
 
-    along = phases(0, width)
+    along = phases(0, height)
     across = phases(spot * block, block)
     sin_b, cos_b = jnp.sin(across), jnp.cos(across)
     with_sin = 2.0 * (cos_b - absorb_ratio * sin_b)
     with_cos = 2.0 * (sin_b + absorb_ratio * cos_b)
     turned = jnp.concatenate([jnp.sin(along), jnp.cos(along)], axis=0).T
     step = 128
-    for at in range(0, width, step):
+    for at in range(0, height, step):
         rows = turned[at : at + step]
         transfer = [
             rows[:, d : d + 1] * with_sin[d : d + 1, :]
@@ -166,7 +177,7 @@
 def column_kernel(inner, outer, table, gain, *refs):
     pieces = dict(zip(send_order, refs[:inner]))
     *outs, stack, total, spectrum = refs[inner:]
-    _, plane, spot = position(inner)
+    core, plane, spot = position(inner)
     dists, rows_dev, block = pieces[0].shape
     depth = inner * rows_dev
     for rel in range(inner):
@@ -175,11 +186,11 @@
             stack[d, pl.ds(start, rows_dev), :] = pieces[rel][d]
     part = table[:, pl.ds(pl.multiple_of(plane * depth, depth), depth)]
     for d in range(dists):
-        got = jnp.dot(part, stack[d], preferred_element_type=f32) * gain[d].astype(f32)
+        value = jnp.dot(part, stack[d], preferred_element_type=f32) * gain[d].astype(f32)
         if d == 0:
-            total[...] = got
+            total[...] = value
         else:
-            total[...] += got
+            total[...] += value
     spectrum[...] = total[...].astype(bf16)
     middle = (plane == 1) | (plane == 2)
     first = jnp.where(middle, 1, 3)
@@ -313,31 +324,38 @@
         return (c, (3 - z) * inner + r % inner) if z in (1, 2) else (c ^ 1, r)
 
     partner = sent(holograms[0], to_other_core)
+    mine = pl.pallas_call(
+        take_kernel,
+        out_shape=shaped(own, dist_dev, rows_dev, width),
+        in_specs=in_hbm(1) + vmem(1),
+        out_specs=one_out,
+        scratch_shapes=[pltpu.SemaphoreType.DMA],
+        compiler_params=params,
+        cost_estimate=cheap,
+        name="take",
+    )(from_hbm(holograms[0]), table)
+    pieces = pl.pallas_call(
+        lambda *refs: row_kernel(inner, *refs),
+        out_shape=[shaped(dists, rows_dev, block)] * (own * inner),
+        in_specs=vmem(3),
+        out_specs=vmem(own * inner),
+        compiler_params=params,
+        cost_estimate=cheap,
+        name="row_spectra",
+    )(mine, partner, table)
+    arrived = [
+        spread(pieces[chunk * inner : (chunk + 1) * inner], send_order) for chunk in range(own)
+    ]
+
     gain = pl.pallas_call(
         lambda *refs: filter_kernel(inner, dist_dev, *refs),
         out_shape=shaped(dists, width, block),
-        in_specs=smem(1),
+        in_specs=smem(1) + unread(1),
         out_specs=one_out,
         compiler_params=params,
         cost_estimate=cheap,
         name="filters",
-    )(from_hbm(propagation))
-    pieces = pl.pallas_call(
-        lambda *refs: row_kernel(inner, *refs),
-        out_shape=[shaped(dists, rows_dev, block)] * (own * inner),
-        in_specs=in_hbm(1) + vmem(2) + unread(1),
-        out_specs=vmem(own * inner),
-        scratch_shapes=[
-            pltpu.VMEM((own, dist_dev, rows_dev, width), bf16),
-            pltpu.SemaphoreType.DMA,
-        ],
-        compiler_params=params,
-        cost_estimate=cheap,
-        name="row_spectra",
-    )(from_hbm(holograms[0]), partner, table, gain)
-    arrived = [
-        spread(pieces[chunk * inner : (chunk + 1) * inner], send_order) for chunk in range(own)
-    ]
+    )(from_hbm(propagation), pieces[0])
 
     sums = []
     for chunk in range(own):
@@ -357,7 +375,8 @@
         )(table, gain, *arrived[chunk])
         ours, first, second, third = blocks
         near = sent(first, to_plane(1))
-        earlier = sums[-1][3:] if sums else []
+        others = [sent(second, to_plane(1)), sent(second, to_middle)]
+        earlier = sums[-1][3:] if sums else others
         message = pl.pallas_call(
             lambda *refs: far_kernel(inner, *refs),
             out_shape=shaped(depth, block),
@@ -368,7 +387,7 @@
             name="far",
         )(*earlier, third, near)
         far = sent(message, to_plane(2))
-        sums.append([ours, far, near, sent(second, to_plane(1)), sent(second, to_middle)])
+        sums.append([ours, far, near, *others])
 
     phases = []
     for chunk in range(own):

time: 51.7 us -> 53.2 us (1.029)
  local copies, waits for them, and re-layouts: 0.01 us -> 1.61 us
  starting transfers between devices: 28.9 us -> 28.2 us
    unnamed x8 -> x10, local copies, waits for them, and re-layouts: 0.01 us -> 1.61 us
    pallas_call x0 -> x1, Pallas kernels: none -> 1.05 us  [plane_plan(): pl.pallas_call(take_kernel, out_shape=shaped(own, dist_dev, rows_dev, wid...]
    ppermute x23, starting transfers between devices: 28.9 us -> 28.2 us  [sent(): return lax.ppermute(value, ('dist', 'rows'), pairs)]
    pallas_call x1, Pallas kernels: 1.83 us -> 1.28 us  [plane_plan(): pl.pallas_call(lambda *refs: row_kernel(inner, *refs), out_shape=[shaped(...]
  transfers between devices with their start and end apart: 23 -> 23, of which waited for: 8 -> 7; matrix products, arithmetic and copies ran while one was open for 0% -> 0% of each run, Pallas kernels for 15% -> 16%
where the time goes in v24:
time: 53.2 us; the launch traced here: 53 us
  starting transfers between devices  28.2 us (53%)
  waiting for transfers between devices  12 us (23%)
  Pallas kernels  11 us (21%)
  local copies, waits for them, and re-layouts  1.61 us (3%)
    ppermute x23, starting transfers between devices, sent(): return lax.ppermute(value, ('dist', 'rows'), pairs)  28.2 us
    ppermute x23, waiting for transfers between devices, sent(): return lax.ppermute(value, ('dist', 'rows'), pairs)  12 us
    pallas_call x2, Pallas kernels, plane_plan(): pl.pallas_call(lambda *refs: column_kernel(inner, outer, *refs), out_shap...  2.59 us
    pallas_call x1, Pallas kernels, plane_plan(): pl.pallas_call(lambda *refs: filter_kernel(inner, dist_dev, *refs), out_s...  2.49 us
    unnamed x10, local copies, waits for them, and re-layouts  1.61 us
    pallas_call x1, Pallas kernels, plane_plan(): pl.pallas_call(lambda *refs: row_kernel(inner, *refs), out_shape=[shaped(...  1.28 us
    pallas_call x1, Pallas kernels, plane_plan(): pl.pallas_call(lambda *refs: recon_kernel(own, *refs), out_shape=[jax.Sha...  1.2 us
    pallas_call x1, Pallas kernels, plane_plan(): pl.pallas_call(recon_last_kernel, out_shape=shaped(capacity, pixels), in_...  1.12 us
  transfers between devices with their start and end apart: 23, of which 7 were waited for; matrix products, arithmetic and copies ran while one was open for 0% of the time, Pallas kernels for 16%

profile of v24, /device:TPU:0, one launch (start us, length us, event | category | flops | bytes accessed | tf_op | source)
XLA Modules:
  0.0 53.0 jit_solution(1021648855237147058)
XLA Ops:
  0.0 0.5 collective-permute-start
  0.5 1.6 %copy-done = bf16[1024,1024]{1,0:T(8,128)(2,1)S(1)} copy-done((bf16[1024,1024]{1,0:T(8,128)(2,1)S(1)}, bf16[1024,1024]{1,0:T(8,128)(2,1)}, u32[]{:S(2)}) %copy-start) | copy-done | bytes 2097176
  2.0 1.0 %take.1.refs_0_ = bf16[2,2,64,1024]{3,2,1,0:T(8,128)(2,1)S(1)} custom-call(bf16[4,2,64,1024]{3,2,1,0:T(8,128)(2,1)} %bitcast.2, bf16[1024,1024]{1,0:T(8,128)(2,1)S(1)} %copy-done), custom_call_target="tpu_custom_call" | custom-call | flops 1 | bytes 1 | tf_op jit(solution)/shard_map/take/pallas_call | solution.py:327
  3.1 0.0 copy-start.1
  3.1 0.0 collective-permute-done.refs_1_
  3.1 1.3 %row_spectra.1 = (bf16[4,64,256]{2,1,0:T(8,128)(2,1)S(1)}, bf16[4,64,256]{2,1,0:T(8,128)(2,1)S(1)}, bf16[4,64,256]{2,1,0:T(8,128)(2,1)S(1)}, bf16[4,64,256]{2,1,...) custom-call(bf16[2,2,64,1024]{3,2,1,0:T(8,128)(2,1)S(1)} %take.1.ref, ...), custom_call_target="tpu_custom_call" | custom-call | flops 1 | bytes 1 | tf_op jit(solution)/shard_map/row_spectra/pallas_call | solution.py:337
  4.4 2.8 %collective-permute-start.1 = (bf16[4,64,256]{2,1,0:T(8,128)(2,1)S(1)}, bf16[4,64,256]{2,1,0:T(8,128)(2,1)S(1)}, u32[]{:S(2)}, u32[]{:S(2)}) collective-permute-start(bf16[4,64,256]{2,1,0:T(8,128)(2,1)S(1)} %get-tuple-element.31), channel_id=1, source_target_pairs={{0,2},{1,3},{2,0},{3,1},{4,6},{5,7},{6,4},{7,5},{8,10},{9,11},{10,... | collective-permute-start | bytes 393224 | tf_op jit(solution)/shard_map/ppermute | solution.py:308
  7.2 1.5 %collective-permute-start.2 = (bf16[4,64,256]{2,1,0:T(8,128)(2,1)S(1)}, bf16[4,64,256]{2,1,0:T(8,128)(2,1)S(1)}, u32[]{:S(2)}, u32[]{:S(2)}) collective-permute-start(bf16[4,64,256]{2,1,0:T(8,128)(2,1)S(1)} %get-tuple-element.32), channel_id=1, source_target_pairs={{0,1},{1,0},{2,3},{3,2},{4,5},{5,4},{6,7},{7,6},{8,9},{9,8},{10,11... | collective-permute-start | bytes 393224 | tf_op jit(solution)/shard_map/ppermute | solution.py:308
  8.7 0.0 collective-permute-start.3
  8.7 1.9 %collective-permute-start.12 = (bf16[4,64,256]{2,1,0:T(8,128)(2,1)S(1)}, bf16[4,64,256]{2,1,0:T(8,128)(2,1)S(1)}, u32[]{:S(2)}, u32[]{:S(2)}) collective-permute-start(bf16[4,64,256]{2,1,0:T(8,128)(2,1)S(1)} %get-tuple-element.42), channel_id=1, source_target_pairs={{0,2},{1,3},{2,0},{3,1},{4,6},{5,7},{6,4},{7,5},{8,10},{9,11},{10,... | collective-permute-start | bytes 393224 | tf_op jit(solution)/shard_map/ppermute | solution.py:308
  10.7 1.5 %collective-permute-start.13 = (bf16[4,64,256]{2,1,0:T(8,128)(2,1)S(1)}, bf16[4,64,256]{2,1,0:T(8,128)(2,1)S(1)}, u32[]{:S(2)}, u32[]{:S(2)}) collective-permute-start(bf16[4,64,256]{2,1,0:T(8,128)(2,1)S(1)} %get-tuple-element.43), channel_id=1, source_target_pairs={{0,1},{1,0},{2,3},{3,2},{4,5},{5,4},{6,7},{7,6},{8,9},{9,8},{10,11... | collective-permute-start | bytes 393224 | tf_op jit(solution)/shard_map/ppermute | solution.py:308
  12.2 0.0 collective-permute-done.1.refs_3_
  12.2 1.8 %collective-permute-start.14 = (bf16[4,64,256]{2,1,0:T(8,128)(2,1)S(1)}, bf16[4,64,256]{2,1,0:T(8,128)(2,1)S(1)}, u32[]{:S(2)}, u32[]{:S(2)}) collective-permute-start(bf16[4,64,256]{2,1,0:T(8,128)(2,1)S(1)} %get-tuple-element.44), channel_id=1, source_target_pairs={{0,3},{1,2},{2,1},{3,0},{4,7},{5,6},{6,5},{7,4},{8,11},{9,10},{10,... | collective-permute-start | bytes 393224 | tf_op jit(solution)/shard_map/ppermute | solution.py:308
  13.9 2.5 %filters.1.refs_1_ = bf16[4,1024,256]{2,1,0:T(8,128)(2,1)S(1)} custom-call(f32[4]{0:T(128)} %refs_0_.6, bf16[4,64,256]{2,1,0:T(8,128)(2,1)S(1)} %get-tuple-element.30.refs_1_.refs_2_), custom_call_target="tpu_custom_call" | custom-call | flops 1 | bytes 1 | tf_op jit(solution)/shard_map/filters/pallas_call | solution.py:350
  16.4 0.0 collective-permute-done.2.refs_4_
  16.4 0.0 collective-permute-done.3.refs_5_
  16.4 0.0 copy-done.1
  16.4 1.3 %columns.2 = (bf16[256,256]{1,0:T(8,128)(2,1)S(1)}, bf16[256,256]{1,0:T(8,128)(2,1)S(1)}, bf16[256,256]{1,0:T(8,128)(2,1)S(1)}, bf16[256,256]{1,0:T(8,128)(2,1)S(1)}) custom-call(bf16[1024,1024]{1,0:T(8,128)(2,1)S(1)} %copy-done.1, bf16[4,1024,256]{2,1,0:T(8,128)(2,1)S(1)} %filters.1.refs_1_, bf16[4,64,256]{2,1,0:T(8,128)(2,1)S(1)} %get-tuple-element.30.refs_1_.refs_2_, ...), custom_call_target="tpu_custom_call" | custom-call | flops 1 | bytes 1 | tf_op jit(solution)/shard_map/columns/pallas_call | solution.py:362
  17.8 1.6 %collective-permute-start.6 = (bf16[256,256]{1,0:T(8,128)(2,1)S(1)}, bf16[256,256]{1,0:T(8,128)(2,1)S(1)}, u32[]{:S(2)}, u32[]{:S(2)}) collective-permute-start(bf16[256,256]{1,0:T(8,128)(2,1)S(1)} %get-tuple-element.37), channel_id=1, source_target_pairs={{0,4},{1,5},{2,6},{3,7},{4,0},{5,1},{6,2},{7,3},{8,12},{9,13},{10,... | collective-permute-start | bytes 393224 | tf_op jit(solution)/shard_map/ppermute | solution.py:308
  19.4 0.0 collective-permute-start.5
  19.4 0.0 collective-permute-done.12.refs_3_
  19.4 3.2 %collective-permute-start.4 = (bf16[256,256]{1,0:T(8,128)(2,1)S(1)}, bf16[256,256]{1,0:T(8,128)(2,1)S(1)}, u32[]{:S(2)}, u32[]{:S(2)}) collective-permute-start(bf16[256,256]{1,0:T(8,128)(2,1)S(1)} %get-tuple-element.35), channel_id=1, source_target_pairs={{0,4},{1,5},{2,6},{3,7},{4,0},{5,1},{6,2},{7,3},{8,12},{9,13},{10,... | collective-permute-start | bytes 393224 | tf_op jit(solution)/shard_map/ppermute | solution.py:308
  22.6 0.0 collective-permute-done.13.refs_4_
  22.6 0.0 collective-permute-done.14.refs_5_
  22.6 1.3 %columns.3 = (bf16[256,256]{1,0:T(8,128)(2,1)S(1)}, bf16[256,256]{1,0:T(8,128)(2,1)S(1)}, bf16[256,256]{1,0:T(8,128)(2,1)S(1)}, bf16[256,256]{1,0:T(8,128)(2,1)S(1)}) custom-call(bf16[1024,1024]{1,0:T(8,128)(2,1)S(1)} %copy-done.1, bf16[4,1024,256]{2,1,0:T(8,128)(2,1)S(1)} %filters.1.refs_1_, bf16[4,64,256]{2,1,0:T(8,128)(2,1)S(1)} %get-tuple-element.41.refs_2_, ...), custom_call_target="tpu_custom_call" | custom-call | flops 1 | bytes 1 | tf_op jit(solution)/shard_map/columns/pallas_call | solution.py:362
  23.9 0.1 collective-permute-start.15
  24.0 0.0 collective-permute-done.6.refs_3_.refs_2_
  24.0 0.0 collective-permute-done.5.refs_1_.refs_4_
  24.0 2.4 %collective-permute-done.4.refs_0_.refs_3_ = bf16[256,256]{1,0:T(8,128)(2,1)S(1)} collective-permute-done((bf16[256,256]{1,0:T(8,128)(2,1)S(1)}, bf16[256,256]{1,0:T(8,128)(2,1)S(1)}, u32[]{:S(2)}, u32[]{:S(2)}) %collective-permute-start.4) | collective-permute-done | bytes 131104 | tf_op jit(solution)/shard_map/ppermute | solution.py:308
  26.4 0.1 far.2
  26.5 2.5 %collective-permute-start.7 = (bf16[256,256]{1,0:T(8,128)(2,1)S(1)}, bf16[256,256]{1,0:T(8,128)(2,1)S(1)}, u32[]{:S(2)}, u32[]{:S(2)}) collective-permute-start(bf16[256,256]{1,0:T(8,128)(2,1)S(1)} %far.2), channel_id=1, source_target_pairs={{0,8},{1,9},{2,10},{3,11},{4,12},{5,13},{6,14},{7,15},{8,0},{9,1},... | collective-permute-start | bytes 393224 | tf_op jit(solution)/shard_map/ppermute | solution.py:308
  29.0 0.0 collective-permute-start.18
  29.0 1.9 %collective-permute-start.17 = (bf16[256,256]{1,0:T(8,128)(2,1)S(1)}, bf16[256,256]{1,0:T(8,128)(2,1)S(1)}, u32[]{:S(2)}, u32[]{:S(2)}) collective-permute-start(bf16[256,256]{1,0:T(8,128)(2,1)S(1)} %get-tuple-element.48), channel_id=1, source_target_pairs={{0,4},{1,5},{2,6},{3,7},{4,0},{5,1},{6,2},{7,3},{8,12},{9,13},{10,... | collective-permute-start | bytes 393224 | tf_op jit(solution)/shard_map/ppermute | solution.py:308
  30.9 0.0 collective-permute-done.15.refs_3_.refs_2_
  30.9 0.1 far.3
  31.0 1.5 %collective-permute-start.16 = (bf16[256,256]{1,0:T(8,128)(2,1)S(1)}, bf16[256,256]{1,0:T(8,128)(2,1)S(1)}, u32[]{:S(2)}, u32[]{:S(2)}) collective-permute-start(bf16[256,256]{1,0:T(8,128)(2,1)S(1)} %far.3), channel_id=1, source_target_pairs={{0,8},{1,9},{2,10},{3,11},{4,12},{5,13},{6,14},{7,15},{8,0},{9,1},... | collective-permute-start | bytes 393224 | tf_op jit(solution)/shard_map/ppermute | solution.py:308
  32.5 3.8 %collective-permute-done.7.refs_1_ = bf16[256,256]{1,0:T(8,128)(2,1)S(1)} collective-permute-done((bf16[256,256]{1,0:T(8,128)(2,1)S(1)}, bf16[256,256]{1,0:T(8,128)(2,1)S(1)}, u32[]{:S(2)}, u32[]{:S(2)}) %collective-permute-start.7) | collective-permute-done | bytes 131104 | tf_op jit(solution)/shard_map/ppermute | solution.py:308
  36.3 0.1 half.2
  36.4 2.1 %collective-permute-start.8 = (bf16[128,256]{1,0:T(8,128)(2,1)S(1)}, bf16[128,256]{1,0:T(8,128)(2,1)S(1)}, u32[]{:S(2)}, u32[]{:S(2)}) collective-permute-start(bf16[128,256]{1,0:T(8,128)(2,1)S(1)} %get-tuple-element.39), channel_id=1, source_target_pairs={{0,2},{1,3},{2,0},{3,1},{4,6},{5,7},{6,4},{7,5},{8,10},{9,11},{10,... | collective-permute-start | bytes 196616 | tf_op jit(solution)/shard_map/ppermute | solution.py:308
  38.5 1.4 %collective-permute-start.9 = (bf16[128,256]{1,0:T(8,128)(2,1)S(1)}, bf16[128,256]{1,0:T(8,128)(2,1)S(1)}, u32[]{:S(2)}, u32[]{:S(2)}) collective-permute-start(bf16[128,256]{1,0:T(8,128)(2,1)S(1)} %get-tuple-element.40), channel_id=1, source_target_pairs={{0,3},{1,2},{2,1},{3,0},{4,7},{5,6},{6,5},{7,4},{8,11},{9,10},{10,... | collective-permute-start | bytes 196616 | tf_op jit(solution)/shard_map/ppermute | solution.py:308
  39.9 0.0 collective-permute-done.18.refs_4_
  39.9 0.1 collective-permute-start.10
  40.0 0.0 collective-permute-done.17.refs_3_
  40.0 2.5 %collective-permute-done.16.refs_1_ = bf16[256,256]{1,0:T(8,128)(2,1)S(1)} collective-permute-done((bf16[256,256]{1,0:T(8,128)(2,1)S(1)}, bf16[256,256]{1,0:T(8,128)(2,1)S(1)}, u32[]{:S(2)}, u32[]{:S(2)}) %collective-permute-start.16) | collective-permute-done | bytes 131104 | tf_op jit(solution)/shard_map/ppermute | solution.py:308
  42.5 0.1 half.3
  42.6 1.4 %collective-permute-start.19 = (bf16[128,256]{1,0:T(8,128)(2,1)S(1)}, bf16[128,256]{1,0:T(8,128)(2,1)S(1)}, u32[]{:S(2)}, u32[]{:S(2)}) collective-permute-start(bf16[128,256]{1,0:T(8,128)(2,1)S(1)} %get-tuple-element.50), channel_id=1, source_target_pairs={{0,2},{1,3},{2,0},{3,1},{4,6},{5,7},{6,4},{7,5},{8,10},{9,11},{10,... | collective-permute-start | bytes 196616 | tf_op jit(solution)/shard_map/ppermute | solution.py:308
  44.0 1.4 %collective-permute-start.20 = (bf16[128,256]{1,0:T(8,128)(2,1)S(1)}, bf16[128,256]{1,0:T(8,128)(2,1)S(1)}, u32[]{:S(2)}, u32[]{:S(2)}) collective-permute-start(bf16[128,256]{1,0:T(8,128)(2,1)S(1)} %get-tuple-element.51), channel_id=1, source_target_pairs={{0,3},{1,2},{2,1},{3,0},{4,7},{5,6},{6,5},{7,4},{8,11},{9,10},{10,... | collective-permute-start | bytes 196616 | tf_op jit(solution)/shard_map/ppermute | solution.py:308
  45.4 0.0 collective-permute-done.8.refs_2_
  45.4 0.8 %collective-permute-start.21 = (bf16[128,256]{1,0:T(8,128)(2,1)S(1)}, bf16[128,256]{1,0:T(8,128)(2,1)S(1)}, u32[]{:S(2)}, u32[]{:S(2)}) collective-permute-start(bf16[128,256]{1,0:T(8,128)(2,1)S(1)} %get-tuple-element.49.refs_1_), channel_id=1, source_target_pairs={{0,1},{1,0},{2,3},{3,2},{4,5},{5,4},{6,7},{7,6},{8,9},{9,8},{10,11... | collective-permute-start | bytes 196616 | tf_op jit(solution)/shard_map/ppermute | solution.py:308
  46.2 0.0 collective-permute-done.9.refs_3_
  46.3 0.0 collective-permute-done.10.refs_4_
  46.3 0.5 phase.2.refs_3_
  46.7 0.1 collective-permute-start.11
  46.8 0.1 collective-permute-done.19.refs_2_
  46.9 2.2 %collective-permute-done.20.refs_3_ = bf16[128,256]{1,0:T(8,128)(2,1)S(1)} collective-permute-done((bf16[128,256]{1,0:T(8,128)(2,1)S(1)}, bf16[128,256]{1,0:T(8,128)(2,1)S(1)}, u32[]{:S(2)}, u32[]{:S(2)}) %collective-permute-start.20) | collective-permute-done | bytes 65568 | tf_op jit(solution)/shard_map/ppermute | solution.py:308
  49.2 0.6 %collective-permute-done.21.refs_4_ = bf16[128,256]{1,0:T(8,128)(2,1)S(1)} collective-permute-done((bf16[128,256]{1,0:T(8,128)(2,1)S(1)}, bf16[128,256]{1,0:T(8,128)(2,1)S(1)}, u32[]{:S(2)}, u32[]{:S(2)}) %collective-permute-start.21) | collective-permute-done | bytes 65568 | tf_op jit(solution)/shard_map/ppermute | solution.py:308
  49.8 0.5 phase.3.refs_5_
  50.2 0.1 collective-permute-start.22
  50.3 0.0 collective-permute-done.11.refs_4_
  50.3 0.0 copy-done.2
  50.3 0.0 copy-done.3
  50.4 1.2 %recon.2 = (f32[128,512]{1,0:T(8,128)S(1)}, bf16[1024,512]{1,0:T(8,128)(2,1)S(1)}, bf16[128,128]{1,0:T(8,128)(2,1)S(1)}) custom-call(s32[1,4]{1,0:T(1,128)S(1)} %copy-done.3, s32[16]{0:T(128)S(1)} %copy-done.4, bf16[4,1024,512]{2,1,0:T(8,128)(2,1)S(1)} %copy-done.2, bf16[128,1024]{1,0:T(8,128)(2,1)S(1)} %phase.2.refs_3_, ...), custom_call_target="tpu_custom_call" | custom-call | flops 1 | bytes 1 | tf_op jit(solution)/shard_map/recon/pallas_call | solution.py:416
  51.6 0.3 collective-permute-done.22.phase
  51.8 1.1 %recon.3 = bf16[128,512]{1,0:T(8,128)(2,1)} custom-call(bf16[1024,512]{1,0:T(8,128)(2,1)S(1)} %get-tuple-element.52.weights, bf16[128,1024]{1,0:T(8,128)(2,1)S(1)} %collective-permute-done.22.phase, f32[128,512]{1,0:T(8,128)S(1)} %get-tuple-element.53.before, bf16[128,128]{1,0:T(8,128)(2,1)S(1)} %get-tuple-element.54.select), custom_call_target="tpu_custom_call" | custom-call | flops 1 | bytes 1 | tf_op jit(solution)/shard_map/recon/pallas_call | solution.py:429
  (5 shorter events, 0.0 us)
Async XLA Ops:
  0.0 3.1 %collective-permute-start = (bf16[4,2,64,1024]{3,2,1,0:T(8,128)(2,1)}, bf16[4,2,64,1024]{3,2,1,0:T(8,128)(2,1)S(1)}, u32[]{:S(2)}, u32[]{:S(2)}) collective-permute-start(bf16[4,2,64,1024]{3,2,1,0:T(8,128)(2,1)} %bitcast.1), channel_id=1, source_target_pairs={{0,16},{1,17},{2,18},{3,19},{4,20},{5,21},{6,22},{7,23},{8,24},{9,... | collective-permute-start | bytes 3145736 | tf_op jit(solution)/shard_map/ppermute | solution.py:308
  0.5 1.6 %copy-start = (bf16[1024,1024]{1,0:T(8,128)(2,1)S(1)}, bf16[1024,1024]{1,0:T(8,128)(2,1)}, u32[]{:S(2)}) copy-start(bf16[1024,1024]{1,0:T(8,128)(2,1)} %constant.2.clone.after.refs_2_.refs_0_) | copy-start | bytes 6291460
  3.1 13.3 %copy-start.1 = (bf16[1024,1024]{1,0:T(8,128)(2,1)S(1)}, bf16[1024,1024]{1,0:T(8,128)(2,1)}, u32[]{:S(2)}) copy-start(bf16[1024,1024]{1,0:T(8,128)(2,1)} %constant.2.clone.after.refs_2_.refs_0_) | copy-start | bytes 6291460
  4.4 7.7 %collective-permute-start.1 = (bf16[4,64,256]{2,1,0:T(8,128)(2,1)S(1)}, bf16[4,64,256]{2,1,0:T(8,128)(2,1)S(1)}, u32[]{:S(2)}, u32[]{:S(2)}) collective-permute-start(bf16[4,64,256]{2,1,0:T(8,128)(2,1)S(1)} %get-tuple-element.31), channel_id=1, source_target_pairs={{0,2},{1,3},{2,0},{3,1},{4,6},{5,7},{6,4},{7,5},{8,10},{9,11},{10,... | collective-permute-start | bytes 393224 | tf_op jit(solution)/shard_map/ppermute | solution.py:308
  7.2 9.2 %collective-permute-start.2 = (bf16[4,64,256]{2,1,0:T(8,128)(2,1)S(1)}, bf16[4,64,256]{2,1,0:T(8,128)(2,1)S(1)}, u32[]{:S(2)}, u32[]{:S(2)}) collective-permute-start(bf16[4,64,256]{2,1,0:T(8,128)(2,1)S(1)} %get-tuple-element.32), channel_id=1, source_target_pairs={{0,1},{1,0},{2,3},{3,2},{4,5},{5,4},{6,7},{7,6},{8,9},{9,8},{10,11... | collective-permute-start | bytes 393224 | tf_op jit(solution)/shard_map/ppermute | solution.py:308
  8.7 7.8 %collective-permute-start.3 = (bf16[4,64,256]{2,1,0:T(8,128)(2,1)S(1)}, bf16[4,64,256]{2,1,0:T(8,128)(2,1)S(1)}, u32[]{:S(2)}, u32[]{:S(2)}) collective-permute-start(bf16[4,64,256]{2,1,0:T(8,128)(2,1)S(1)} %get-tuple-element.33), channel_id=1, source_target_pairs={{0,3},{1,2},{2,1},{3,0},{4,7},{5,6},{6,5},{7,4},{8,11},{9,10},{10,... | collective-permute-start | bytes 393224 | tf_op jit(solution)/shard_map/ppermute | solution.py:308
  8.7 10.7 %collective-permute-start.12 = (bf16[4,64,256]{2,1,0:T(8,128)(2,1)S(1)}, bf16[4,64,256]{2,1,0:T(8,128)(2,1)S(1)}, u32[]{:S(2)}, u32[]{:S(2)}) collective-permute-start(bf16[4,64,256]{2,1,0:T(8,128)(2,1)S(1)} %get-tuple-element.42), channel_id=1, source_target_pairs={{0,2},{1,3},{2,0},{3,1},{4,6},{5,7},{6,4},{7,5},{8,10},{9,11},{10,... | collective-permute-start | bytes 393224 | tf_op jit(solution)/shard_map/ppermute | solution.py:308
  10.7 11.9 %collective-permute-start.13 = (bf16[4,64,256]{2,1,0:T(8,128)(2,1)S(1)}, bf16[4,64,256]{2,1,0:T(8,128)(2,1)S(1)}, u32[]{:S(2)}, u32[]{:S(2)}) collective-permute-start(bf16[4,64,256]{2,1,0:T(8,128)(2,1)S(1)} %get-tuple-element.43), channel_id=1, source_target_pairs={{0,1},{1,0},{2,3},{3,2},{4,5},{5,4},{6,7},{7,6},{8,9},{9,8},{10,11... | collective-permute-start | bytes 393224 | tf_op jit(solution)/shard_map/ppermute | solution.py:308
  12.2 10.4 %collective-permute-start.14 = (bf16[4,64,256]{2,1,0:T(8,128)(2,1)S(1)}, bf16[4,64,256]{2,1,0:T(8,128)(2,1)S(1)}, u32[]{:S(2)}, u32[]{:S(2)}) collective-permute-start(bf16[4,64,256]{2,1,0:T(8,128)(2,1)S(1)} %get-tuple-element.44), channel_id=1, source_target_pairs={{0,3},{1,2},{2,1},{3,0},{4,7},{5,6},{6,5},{7,4},{8,11},{9,10},{10,... | collective-permute-start | bytes 393224 | tf_op jit(solution)/shard_map/ppermute | solution.py:308
  17.8 6.2 %collective-permute-start.6 = (bf16[256,256]{1,0:T(8,128)(2,1)S(1)}, bf16[256,256]{1,0:T(8,128)(2,1)S(1)}, u32[]{:S(2)}, u32[]{:S(2)}) collective-permute-start(bf16[256,256]{1,0:T(8,128)(2,1)S(1)} %get-tuple-element.37), channel_id=1, source_target_pairs={{0,4},{1,5},{2,6},{3,7},{4,0},{5,1},{6,2},{7,3},{8,12},{9,13},{10,... | collective-permute-start | bytes 393224 | tf_op jit(solution)/shard_map/ppermute | solution.py:308
  19.4 4.6 %collective-permute-start.5 = (bf16[256,256]{1,0:T(8,128)(2,1)S(1)}, bf16[256,256]{1,0:T(8,128)(2,1)S(1)}, u32[]{:S(2)}, u32[]{:S(2)}) collective-permute-start(bf16[256,256]{1,0:T(8,128)(2,1)S(1)} %get-tuple-element.35), channel_id=1, source_target_pairs={{0,16},{1,17},{2,18},{3,19},{4,8},{5,9},{6,10},{7,11},{8,4},{9,5},... | collective-permute-start | bytes 393224 | tf_op jit(solution)/shard_map/ppermute | solution.py:308
  19.4 7.0 %collective-permute-start.4 = (bf16[256,256]{1,0:T(8,128)(2,1)S(1)}, bf16[256,256]{1,0:T(8,128)(2,1)S(1)}, u32[]{:S(2)}, u32[]{:S(2)}) collective-permute-start(bf16[256,256]{1,0:T(8,128)(2,1)S(1)} %get-tuple-element.35), channel_id=1, source_target_pairs={{0,4},{1,5},{2,6},{3,7},{4,0},{5,1},{6,2},{7,3},{8,12},{9,13},{10,... | collective-permute-start | bytes 393224 | tf_op jit(solution)/shard_map/ppermute | solution.py:308
  23.9 7.0 %collective-permute-start.15 = (bf16[256,256]{1,0:T(8,128)(2,1)S(1)}, bf16[256,256]{1,0:T(8,128)(2,1)S(1)}, u32[]{:S(2)}, u32[]{:S(2)}) collective-permute-start(bf16[256,256]{1,0:T(8,128)(2,1)S(1)} %get-tuple-element.47), channel_id=1, source_target_pairs={{0,4},{1,5},{2,6},{3,7},{4,0},{5,1},{6,2},{7,3},{8,12},{9,13},{10,... | collective-permute-start | bytes 393224 | tf_op jit(solution)/shard_map/ppermute | solution.py:308
  26.5 9.8 %collective-permute-start.7 = (bf16[256,256]{1,0:T(8,128)(2,1)S(1)}, bf16[256,256]{1,0:T(8,128)(2,1)S(1)}, u32[]{:S(2)}, u32[]{:S(2)}) collective-permute-start(bf16[256,256]{1,0:T(8,128)(2,1)S(1)} %far.2), channel_id=1, source_target_pairs={{0,8},{1,9},{2,10},{3,11},{4,12},{5,13},{6,14},{7,15},{8,0},{9,1},... | collective-permute-start | bytes 393224 | tf_op jit(solution)/shard_map/ppermute | solution.py:308
  29.0 10.9 %collective-permute-start.18 = (bf16[256,256]{1,0:T(8,128)(2,1)S(1)}, bf16[256,256]{1,0:T(8,128)(2,1)S(1)}, u32[]{:S(2)}, u32[]{:S(2)}) collective-permute-start(bf16[256,256]{1,0:T(8,128)(2,1)S(1)} %get-tuple-element.48), channel_id=1, source_target_pairs={{0,16},{1,17},{2,18},{3,19},{4,8},{5,9},{6,10},{7,11},{8,4},{9,5},... | collective-permute-start | bytes 393224 | tf_op jit(solution)/shard_map/ppermute | solution.py:308
  29.0 11.0 %collective-permute-start.17 = (bf16[256,256]{1,0:T(8,128)(2,1)S(1)}, bf16[256,256]{1,0:T(8,128)(2,1)S(1)}, u32[]{:S(2)}, u32[]{:S(2)}) collective-permute-start(bf16[256,256]{1,0:T(8,128)(2,1)S(1)} %get-tuple-element.48), channel_id=1, source_target_pairs={{0,4},{1,5},{2,6},{3,7},{4,0},{5,1},{6,2},{7,3},{8,12},{9,13},{10,... | collective-permute-start | bytes 393224 | tf_op jit(solution)/shard_map/ppermute | solution.py:308
  31.0 11.5 %collective-permute-start.16 = (bf16[256,256]{1,0:T(8,128)(2,1)S(1)}, bf16[256,256]{1,0:T(8,128)(2,1)S(1)}, u32[]{:S(2)}, u32[]{:S(2)}) collective-permute-start(bf16[256,256]{1,0:T(8,128)(2,1)S(1)} %far.3), channel_id=1, source_target_pairs={{0,8},{1,9},{2,10},{3,11},{4,12},{5,13},{6,14},{7,15},{8,0},{9,1},... | collective-permute-start | bytes 393224 | tf_op jit(solution)/shard_map/ppermute | solution.py:308
  36.4 9.1 %collective-permute-start.8 = (bf16[128,256]{1,0:T(8,128)(2,1)S(1)}, bf16[128,256]{1,0:T(8,128)(2,1)S(1)}, u32[]{:S(2)}, u32[]{:S(2)}) collective-permute-start(bf16[128,256]{1,0:T(8,128)(2,1)S(1)} %get-tuple-element.39), channel_id=1, source_target_pairs={{0,2},{1,3},{2,0},{3,1},{4,6},{5,7},{6,4},{7,5},{8,10},{9,11},{10,... | collective-permute-start | bytes 196616 | tf_op jit(solution)/shard_map/ppermute | solution.py:308
  38.5 7.8 %collective-permute-start.9 = (bf16[128,256]{1,0:T(8,128)(2,1)S(1)}, bf16[128,256]{1,0:T(8,128)(2,1)S(1)}, u32[]{:S(2)}, u32[]{:S(2)}) collective-permute-start(bf16[128,256]{1,0:T(8,128)(2,1)S(1)} %get-tuple-element.40), channel_id=1, source_target_pairs={{0,3},{1,2},{2,1},{3,0},{4,7},{5,6},{6,5},{7,4},{8,11},{9,10},{10,... | collective-permute-start | bytes 196616 | tf_op jit(solution)/shard_map/ppermute | solution.py:308
  39.9 6.4 %collective-permute-start.10 = (bf16[128,256]{1,0:T(8,128)(2,1)S(1)}, bf16[128,256]{1,0:T(8,128)(2,1)S(1)}, u32[]{:S(2)}, u32[]{:S(2)}) collective-permute-start(bf16[128,256]{1,0:T(8,128)(2,1)S(1)} %get-tuple-element.38.refs_1_), channel_id=1, source_target_pairs={{0,1},{1,0},{2,3},{3,2},{4,5},{5,4},{6,7},{7,6},{8,9},{9,8},{10,11... | collective-permute-start | bytes 196616 | tf_op jit(solution)/shard_map/ppermute | solution.py:308
  42.6 4.3 %collective-permute-start.19 = (bf16[128,256]{1,0:T(8,128)(2,1)S(1)}, bf16[128,256]{1,0:T(8,128)(2,1)S(1)}, u32[]{:S(2)}, u32[]{:S(2)}) collective-permute-start(bf16[128,256]{1,0:T(8,128)(2,1)S(1)} %get-tuple-element.50), channel_id=1, source_target_pairs={{0,2},{1,3},{2,0},{3,1},{4,6},{5,7},{6,4},{7,5},{8,10},{9,11},{10,... | collective-permute-start | bytes 196616 | tf_op jit(solution)/shard_map/ppermute | solution.py:308
  44.0 5.2 %collective-permute-start.20 = (bf16[128,256]{1,0:T(8,128)(2,1)S(1)}, bf16[128,256]{1,0:T(8,128)(2,1)S(1)}, u32[]{:S(2)}, u32[]{:S(2)}) collective-permute-start(bf16[128,256]{1,0:T(8,128)(2,1)S(1)} %get-tuple-element.51), channel_id=1, source_target_pairs={{0,3},{1,2},{2,1},{3,0},{4,7},{5,6},{6,5},{7,4},{8,11},{9,10},{10,... | collective-permute-start | bytes 196616 | tf_op jit(solution)/shard_map/ppermute | solution.py:308
  45.4 4.9 %copy-start.2 = (bf16[4,1024,512]{2,1,0:T(8,128)(2,1)S(1)}, bf16[4,1024,512]{2,1,0:T(8,128)(2,1)}, u32[]{:S(2)}) copy-start(bf16[4,1024,512]{2,1,0:T(8,128)(2,1)} %refs_2_.2) | copy-start | bytes 12582916
  45.4 4.9 %copy-start.3 = (s32[1,4]{1,0:T(1,128)S(1)}, s32[1,4]{1,0:T(1,128)}, u32[]{:S(2)}) copy-start(s32[1,4]{1,0:T(1,128)} %refs_0_.7) | copy-start | bytes 52
  45.4 4.9 %copy-start.4 = (s32[16]{0:T(128)S(1)}, s32[16]{0:T(128)}, u32[]{:S(2)}) copy-start(s32[16]{0:T(128)} %refs_1_.1) | copy-start | bytes 196
  45.4 4.3 %collective-permute-start.21 = (bf16[128,256]{1,0:T(8,128)(2,1)S(1)}, bf16[128,256]{1,0:T(8,128)(2,1)S(1)}, u32[]{:S(2)}, u32[]{:S(2)}) collective-permute-start(bf16[128,256]{1,0:T(8,128)(2,1)S(1)} %get-tuple-element.49.refs_1_), channel_id=1, source_target_pairs={{0,1},{1,0},{2,3},{3,2},{4,5},{5,4},{6,7},{7,6},{8,9},{9,8},{10,11... | collective-permute-start | bytes 196616 | tf_op jit(solution)/shard_map/ppermute | solution.py:308
  46.7 3.6 %collective-permute-start.11 = (bf16[128,1024]{1,0:T(8,128)(2,1)S(1)}, bf16[128,1024]{1,0:T(8,128)(2,1)S(1)}, u32[]{:S(2)}, u32[]{:S(2)}) collective-permute-start(bf16[128,1024]{1,0:T(8,128)(2,1)S(1)} %phase.2.refs_3_), channel_id=1, source_target_pairs={{0,16},{1,17},{2,18},{3,19},{4,20},{5,21},{6,22},{7,23},{8,24},{9,... | collective-permute-start | bytes 786440 | tf_op jit(solution)/shard_map/ppermute | solution.py:308
  50.2 1.6 %collective-permute-start.22 = (bf16[128,1024]{1,0:T(8,128)(2,1)S(1)}, bf16[128,1024]{1,0:T(8,128)(2,1)S(1)}, u32[]{:S(2)}, u32[]{:S(2)}) collective-permute-start(bf16[128,1024]{1,0:T(8,128)(2,1)S(1)} %phase.3.refs_5_), channel_id=1, source_target_pairs={{0,16},{1,17},{2,18},{3,19},{4,20},{5,21},{6,22},{7,23},{8,24},{9,... | collective-permute-start | bytes 786440 | tf_op jit(solution)/shard_map/ppermute | solution.py:308

commit v25 on v19

--- a/solution.py
+++ b/solution.py
@@ -104,11 +104,19 @@
     core, _, spot = position(inner)
     _, dist_dev, rows_dev, width = there.shape
     block = width // inner
-    copy = pltpu.make_async_copy(holo.at[pl.ds(core * own, own)], mine, loaded)
-    copy.start()
+    copies = [
+        pltpu.make_async_copy(
+            holo.at[core * own + chunk, d], mine.at[chunk, d], loaded.at[chunk * dist_dev + d]
+        )
+        for chunk in range(own)
+        for d in range(dist_dev)
+    ]
+    for copy in copies:
+        copy.start()
     for first, source in ((dist_dev, there.at[pl.ds(core * own, own)]), (0, mine)):
         if first == 0:
-            copy.wait()
+            for copy in copies:
+                copy.wait()
         rows = source[...].reshape(own * dist_dev * rows_dev, width)
         for rel in range(inner):
             part = table[:, pl.ds(pl.multiple_of((spot ^ rel) * block, block), block)]
@@ -118,12 +126,18 @@
                 outs[chunk * inner + rel][first : first + dist_dev] = got[chunk]
 
 
-def whole_turns(scale, square):
-    turns = scale * square * (0.5 / math.pi)
-    return (turns - jnp.round(turns)) * (2.0 * math.pi)
-
-
-def filter_kernel(inner, dist_dev, turns, out):
+def sine_of_turns(turns):
+    turns = turns - jnp.round(turns)
+    folded = jnp.where(jnp.abs(turns) > 0.25, jnp.where(turns > 0, 0.5, -0.5) - turns, turns)
+    angle = folded * (2.0 * math.pi)
+    square = angle * angle
+    series = jnp.full_like(angle, 1.0 / math.factorial(13))
+    for order in range(11, 0, -2):
+        series = series * -square + 1.0 / math.factorial(order)
+    return angle * series
+
+
+def filter_kernel(inner, dist_dev, propagation, out):
     dists, width, block = out.shape
     core, _, spot = position(inner)
 
@@ -137,16 +151,17 @@
         rows = []
         for d in range(dists):
             other = d // dist_dev
-            scale = turns[(core ^ other) * dist_dev + d % dist_dev]
-            rows.append(whole_turns(scale, values))
-        return jnp.concatenate(rows, axis=0)
+            scale = propagation[(core ^ other) * dist_dev + d % dist_dev]
+            rows.append(scale * values * (0.5 / math.pi))
+        turns = jnp.concatenate(rows, axis=0)
+        return sine_of_turns(jnp.concatenate([turns, turns + 0.25], axis=0))
 
     along = phases(0, width)
     across = phases(spot * block, block)
-    sin_b, cos_b = jnp.sin(across), jnp.cos(across)
+    sin_b, cos_b = across[:dists], across[dists:]
     with_sin = 2.0 * (cos_b - absorb_ratio * sin_b)
     with_cos = 2.0 * (sin_b + absorb_ratio * cos_b)
-    turned = jnp.concatenate([jnp.sin(along), jnp.cos(along)], axis=0).T
+    turned = along.T
     step = 128
     for at in range(0, width, step):
         rows = turned[at : at + step]
@@ -329,7 +344,7 @@
         out_specs=vmem(own * inner),
         scratch_shapes=[
             pltpu.VMEM((own, dist_dev, rows_dev, width), bf16),
-            pltpu.SemaphoreType.DMA,
+            pltpu.SemaphoreType.DMA((own * dist_dev,)),
         ],
         compiler_params=params,
         cost_estimate=cheap,

time: 51.7 us -> 51.8 us (level)
  no operation moved by 1% of the time
where the time goes in v25:
time: 51.8 us; the launch traced here: 51.6 us
  starting transfers between devices  28.9 us (56%)
  waiting for transfers between devices  11.9 us (23%)
  Pallas kernels  10.6 us (20%)
    ppermute x23, starting transfers between devices, sent(): return lax.ppermute(value, ('dist', 'rows'), pairs)  28.9 us
    ppermute x23, waiting for transfers between devices, sent(): return lax.ppermute(value, ('dist', 'rows'), pairs)  11.9 us
    pallas_call x2, Pallas kernels, plane_plan(): pl.pallas_call(lambda *refs: column_kernel(inner, outer, *refs), out_shap...  2.6 us
    pallas_call x1, Pallas kernels, plane_plan(): pl.pallas_call(lambda *refs: filter_kernel(inner, dist_dev, *refs), out_s...  2.59 us
    pallas_call x1, Pallas kernels, plane_plan(): pl.pallas_call(lambda *refs: row_kernel(inner, *refs), out_shape=[shaped(...  1.9 us
    pallas_call x1, Pallas kernels, plane_plan(): pl.pallas_call(lambda *refs: recon_kernel(own, *refs), out_shape=[jax.Sha...  1.2 us
    pallas_call x1, Pallas kernels, plane_plan(): pl.pallas_call(recon_last_kernel, out_shape=shaped(capacity, pixels), in_...  1.12 us
  transfers between devices with their start and end apart: 23, of which 8 were waited for; matrix products, arithmetic and copies ran while one was open for 0% of the time, Pallas kernels for 15%

profile of v25, /device:TPU:0, one launch (start us, length us, event | category | flops | bytes accessed | tf_op | source)
XLA Modules:
  0.0 51.6 jit_solution(2844072823060753780)
XLA Ops:
  0.0 0.0 copy-start
  0.0 0.5 collective-permute-start
  0.5 2.6 %filters.1.refs_3_.refs_1_ = bf16[4,1024,256]{2,1,0:T(8,128)(2,1)S(1)} custom-call(f32[4]{0:T(128)} %refs_0_.6), custom_call_target="tpu_custom_call" | custom-call | flops 1 | bytes 1 | tf_op jit(solution)/shard_map/filters/pallas_call | solution.py:331
  3.1 0.0 collective-permute-done.refs_1_
  3.1 0.0 copy-done
  3.1 1.9 %row_spectra.1 = (bf16[4,64,256]{2,1,0:T(8,128)(2,1)S(1)}, bf16[4,64,256]{2,1,0:T(8,128)(2,1)S(1)}, bf16[4,64,256]{2,1,0:T(8,128)(2,1)S(1)}, bf16[4,64,256]{2,1,...) custom-call(bf16[4,2,64,1024]{3,2,1,0:T(8,128)(2,1)} %bitcast.2, ...), custom_call_target="tpu_custom_call" | custom-call | flops 1 | bytes 1 | tf_op jit(solution)/shard_map/row_spectra/pallas_call | solution.py:340
  5.0 2.8 %collective-permute-start.1 = (bf16[4,64,256]{2,1,0:T(8,128)(2,1)S(1)}, bf16[4,64,256]{2,1,0:T(8,128)(2,1)S(1)}, u32[]{:S(2)}, u32[]{:S(2)}) collective-permute-start(bf16[4,64,256]{2,1,0:T(8,128)(2,1)S(1)} %get-tuple-element.31), channel_id=1, source_target_pairs={{0,2},{1,3},{2,0},{3,1},{4,6},{5,7},{6,4},{7,5},{8,10},{9,11},{10,... | collective-permute-start | bytes 393224 | tf_op jit(solution)/shard_map/ppermute | solution.py:312
  7.8 1.5 %collective-permute-start.2 = (bf16[4,64,256]{2,1,0:T(8,128)(2,1)S(1)}, bf16[4,64,256]{2,1,0:T(8,128)(2,1)S(1)}, u32[]{:S(2)}, u32[]{:S(2)}) collective-permute-start(bf16[4,64,256]{2,1,0:T(8,128)(2,1)S(1)} %get-tuple-element.32), channel_id=1, source_target_pairs={{0,1},{1,0},{2,3},{3,2},{4,5},{5,4},{6,7},{7,6},{8,9},{9,8},{10,11... | collective-permute-start | bytes 393224 | tf_op jit(solution)/shard_map/ppermute | solution.py:312
  9.3 0.1 collective-permute-start.3
  9.3 1.9 %collective-permute-start.12 = (bf16[4,64,256]{2,1,0:T(8,128)(2,1)S(1)}, bf16[4,64,256]{2,1,0:T(8,128)(2,1)S(1)}, u32[]{:S(2)}, u32[]{:S(2)}) collective-permute-start(bf16[4,64,256]{2,1,0:T(8,128)(2,1)S(1)} %get-tuple-element.42), channel_id=1, source_target_pairs={{0,2},{1,3},{2,0},{3,1},{4,6},{5,7},{6,4},{7,5},{8,10},{9,11},{10,... | collective-permute-start | bytes 393224 | tf_op jit(solution)/shard_map/ppermute | solution.py:312
  11.3 1.5 %collective-permute-start.13 = (bf16[4,64,256]{2,1,0:T(8,128)(2,1)S(1)}, bf16[4,64,256]{2,1,0:T(8,128)(2,1)S(1)}, u32[]{:S(2)}, u32[]{:S(2)}) collective-permute-start(bf16[4,64,256]{2,1,0:T(8,128)(2,1)S(1)} %get-tuple-element.43), channel_id=1, source_target_pairs={{0,1},{1,0},{2,3},{3,2},{4,5},{5,4},{6,7},{7,6},{8,9},{9,8},{10,11... | collective-permute-start | bytes 393224 | tf_op jit(solution)/shard_map/ppermute | solution.py:312
  12.8 0.0 collective-permute-done.1.refs_3_
  12.8 1.6 %collective-permute-start.14 = (bf16[4,64,256]{2,1,0:T(8,128)(2,1)S(1)}, bf16[4,64,256]{2,1,0:T(8,128)(2,1)S(1)}, u32[]{:S(2)}, u32[]{:S(2)}) collective-permute-start(bf16[4,64,256]{2,1,0:T(8,128)(2,1)S(1)} %get-tuple-element.44), channel_id=1, source_target_pairs={{0,3},{1,2},{2,1},{3,0},{4,7},{5,6},{6,5},{7,4},{8,11},{9,10},{10,... | collective-permute-start | bytes 393224 | tf_op jit(solution)/shard_map/ppermute | solution.py:312
  14.4 0.0 collective-permute-done.2.refs_4_
  14.4 2.3 %collective-permute-done.3.refs_5_ = bf16[4,64,256]{2,1,0:T(8,128)(2,1)S(1)} collective-permute-done((bf16[4,64,256]{2,1,0:T(8,128)(2,1)S(1)}, bf16[4,64,256]{2,1,0:T(8,128)(2,1)S(1)}, u32[]{:S(2)}, u32[]{:S(2)}) %collective-permute-start.3) | collective-permute-done | bytes 131104 | tf_op jit(solution)/shard_map/ppermute | solution.py:312
  16.7 1.3 %columns.2 = (bf16[256,256]{1,0:T(8,128)(2,1)S(1)}, bf16[256,256]{1,0:T(8,128)(2,1)S(1)}, bf16[256,256]{1,0:T(8,128)(2,1)S(1)}, bf16[256,256]{1,0:T(8,128)(2,1)S(1)}) custom-call(bf16[1024,1024]{1,0:T(8,128)(2,1)S(1)} %copy-done, bf16[4,1024,256]{2,1,0:T(8,128)(2,1)S(1)} %filters.1.refs_3_.refs_1_, bf16[4,64,256]{2,1,0:T(8,128)(2,1)S(1)} %get-tuple-element.30.refs_2_, ...), custom_call_target="tpu_custom_call" | custom-call | flops 1 | bytes 1 | tf_op jit(solution)/shard_map/columns/pallas_call | solution.py:359
  18.0 1.6 %collective-permute-start.4 = (bf16[256,256]{1,0:T(8,128)(2,1)S(1)}, bf16[256,256]{1,0:T(8,128)(2,1)S(1)}, u32[]{:S(2)}, u32[]{:S(2)}) collective-permute-start(bf16[256,256]{1,0:T(8,128)(2,1)S(1)} %get-tuple-element.36), channel_id=1, source_target_pairs={{0,4},{1,5},{2,6},{3,7},{4,0},{5,1},{6,2},{7,3},{8,12},{9,13},{10,... | collective-permute-start | bytes 393224 | tf_op jit(solution)/shard_map/ppermute | solution.py:312
  19.6 0.0 collective-permute-start.7
  19.6 0.0 collective-permute-done.12.refs_3_
  19.6 3.1 %collective-permute-start.6 = (bf16[256,256]{1,0:T(8,128)(2,1)S(1)}, bf16[256,256]{1,0:T(8,128)(2,1)S(1)}, u32[]{:S(2)}, u32[]{:S(2)}) collective-permute-start(bf16[256,256]{1,0:T(8,128)(2,1)S(1)} %get-tuple-element.37), channel_id=1, source_target_pairs={{0,4},{1,5},{2,6},{3,7},{4,0},{5,1},{6,2},{7,3},{8,12},{9,13},{10,... | collective-permute-start | bytes 393224 | tf_op jit(solution)/shard_map/ppermute | solution.py:312
  22.8 0.0 collective-permute-done.13.refs_4_
  22.8 0.0 collective-permute-done.14.refs_5_
  22.8 1.3 %columns.3 = (bf16[256,256]{1,0:T(8,128)(2,1)S(1)}, bf16[256,256]{1,0:T(8,128)(2,1)S(1)}, bf16[256,256]{1,0:T(8,128)(2,1)S(1)}, bf16[256,256]{1,0:T(8,128)(2,1)S(1)}) custom-call(bf16[1024,1024]{1,0:T(8,128)(2,1)S(1)} %copy-done, bf16[4,1024,256]{2,1,0:T(8,128)(2,1)S(1)} %filters.1.refs_3_.refs_1_, bf16[4,64,256]{2,1,0:T(8,128)(2,1)S(1)} %get-tuple-element.41.refs_2_, ...), custom_call_target="tpu_custom_call" | custom-call | flops 1 | bytes 1 | tf_op jit(solution)/shard_map/columns/pallas_call | solution.py:359
  24.1 0.4 collective-permute-start.15
  24.4 0.0 collective-permute-done.4.refs_1_.refs_2_
  24.4 0.1 far.2
  24.5 2.7 %collective-permute-start.5 = (bf16[256,256]{1,0:T(8,128)(2,1)S(1)}, bf16[256,256]{1,0:T(8,128)(2,1)S(1)}, u32[]{:S(2)}, u32[]{:S(2)}) collective-permute-start(bf16[256,256]{1,0:T(8,128)(2,1)S(1)} %far.2), channel_id=1, source_target_pairs={{0,8},{1,9},{2,10},{3,11},{4,12},{5,13},{6,14},{7,15},{8,0},{9,1},... | collective-permute-start | bytes 393224 | tf_op jit(solution)/shard_map/ppermute | solution.py:312
  27.2 0.0 collective-permute-start.18
  27.2 0.0 collective-permute-done.7.refs_4_.refs_1_
  27.2 1.5 %collective-permute-start.17 = (bf16[256,256]{1,0:T(8,128)(2,1)S(1)}, bf16[256,256]{1,0:T(8,128)(2,1)S(1)}, u32[]{:S(2)}, u32[]{:S(2)}) collective-permute-start(bf16[256,256]{1,0:T(8,128)(2,1)S(1)} %get-tuple-element.48), channel_id=1, source_target_pairs={{0,4},{1,5},{2,6},{3,7},{4,0},{5,1},{6,2},{7,3},{8,12},{9,13},{10,... | collective-permute-start | bytes 393224 | tf_op jit(solution)/shard_map/ppermute | solution.py:312
  28.7 0.0 collective-permute-done.6.refs_3_.refs_0_
  28.7 1.9 %collective-permute-done.15.refs_3_.refs_2_ = bf16[256,256]{1,0:T(8,128)(2,1)S(1)} collective-permute-done((bf16[256,256]{1,0:T(8,128)(2,1)S(1)}, bf16[256,256]{1,0:T(8,128)(2,1)S(1)}, u32[]{:S(2)}, u32[]{:S(2)}) %collective-permute-start.15) | collective-permute-done | bytes 131104 | tf_op jit(solution)/shard_map/ppermute | solution.py:312
  30.6 0.1 far.3
  30.7 2.4 %collective-permute-start.16 = (bf16[256,256]{1,0:T(8,128)(2,1)S(1)}, bf16[256,256]{1,0:T(8,128)(2,1)S(1)}, u32[]{:S(2)}, u32[]{:S(2)}) collective-permute-start(bf16[256,256]{1,0:T(8,128)(2,1)S(1)} %far.3), channel_id=1, source_target_pairs={{0,8},{1,9},{2,10},{3,11},{4,12},{5,13},{6,14},{7,15},{8,0},{9,1},... | collective-permute-start | bytes 393224 | tf_op jit(solution)/shard_map/ppermute | solution.py:312
  33.1 1.7 %collective-permute-done.5.refs_1_ = bf16[256,256]{1,0:T(8,128)(2,1)S(1)} collective-permute-done((bf16[256,256]{1,0:T(8,128)(2,1)S(1)}, bf16[256,256]{1,0:T(8,128)(2,1)S(1)}, u32[]{:S(2)}, u32[]{:S(2)}) %collective-permute-start.5) | collective-permute-done | bytes 131104 | tf_op jit(solution)/shard_map/ppermute | solution.py:312
  34.8 0.1 half.2
  34.9 1.6 %collective-permute-start.8 = (bf16[128,256]{1,0:T(8,128)(2,1)S(1)}, bf16[128,256]{1,0:T(8,128)(2,1)S(1)}, u32[]{:S(2)}, u32[]{:S(2)}) collective-permute-start(bf16[128,256]{1,0:T(8,128)(2,1)S(1)} %get-tuple-element.39), channel_id=1, source_target_pairs={{0,2},{1,3},{2,0},{3,1},{4,6},{5,7},{6,4},{7,5},{8,10},{9,11},{10,... | collective-permute-start | bytes 196616 | tf_op jit(solution)/shard_map/ppermute | solution.py:312
  36.4 1.4 %collective-permute-start.9 = (bf16[128,256]{1,0:T(8,128)(2,1)S(1)}, bf16[128,256]{1,0:T(8,128)(2,1)S(1)}, u32[]{:S(2)}, u32[]{:S(2)}) collective-permute-start(bf16[128,256]{1,0:T(8,128)(2,1)S(1)} %get-tuple-element.40), channel_id=1, source_target_pairs={{0,3},{1,2},{2,1},{3,0},{4,7},{5,6},{6,5},{7,4},{8,11},{9,10},{10,... | collective-permute-start | bytes 196616 | tf_op jit(solution)/shard_map/ppermute | solution.py:312
  37.9 0.0 collective-permute-done.18.refs_4_
  37.9 0.5 %collective-permute-start.10 = (bf16[128,256]{1,0:T(8,128)(2,1)S(1)}, bf16[128,256]{1,0:T(8,128)(2,1)S(1)}, u32[]{:S(2)}, u32[]{:S(2)}) collective-permute-start(bf16[128,256]{1,0:T(8,128)(2,1)S(1)} %get-tuple-element.38.refs_1_), channel_id=1, source_target_pairs={{0,1},{1,0},{2,3},{3,2},{4,5},{5,4},{6,7},{7,6},{8,9},{9,8},{10,11... | collective-permute-start | bytes 196616 | tf_op jit(solution)/shard_map/ppermute | solution.py:312
  38.4 0.0 collective-permute-done.17.refs_3_
  38.4 2.7 %collective-permute-done.16.refs_1_ = bf16[256,256]{1,0:T(8,128)(2,1)S(1)} collective-permute-done((bf16[256,256]{1,0:T(8,128)(2,1)S(1)}, bf16[256,256]{1,0:T(8,128)(2,1)S(1)}, u32[]{:S(2)}, u32[]{:S(2)}) %collective-permute-start.16) | collective-permute-done | bytes 131104 | tf_op jit(solution)/shard_map/ppermute | solution.py:312
  41.2 0.1 half.3
  41.3 1.4 %collective-permute-start.19 = (bf16[128,256]{1,0:T(8,128)(2,1)S(1)}, bf16[128,256]{1,0:T(8,128)(2,1)S(1)}, u32[]{:S(2)}, u32[]{:S(2)}) collective-permute-start(bf16[128,256]{1,0:T(8,128)(2,1)S(1)} %get-tuple-element.50), channel_id=1, source_target_pairs={{0,2},{1,3},{2,0},{3,1},{4,6},{5,7},{6,4},{7,5},{8,10},{9,11},{10,... | collective-permute-start | bytes 196616 | tf_op jit(solution)/shard_map/ppermute | solution.py:312
  42.6 1.4 %collective-permute-start.20 = (bf16[128,256]{1,0:T(8,128)(2,1)S(1)}, bf16[128,256]{1,0:T(8,128)(2,1)S(1)}, u32[]{:S(2)}, u32[]{:S(2)}) collective-permute-start(bf16[128,256]{1,0:T(8,128)(2,1)S(1)} %get-tuple-element.51), channel_id=1, source_target_pairs={{0,3},{1,2},{2,1},{3,0},{4,7},{5,6},{6,5},{7,4},{8,11},{9,10},{10,... | collective-permute-start | bytes 196616 | tf_op jit(solution)/shard_map/ppermute | solution.py:312
  44.1 0.0 collective-permute-done.8.refs_2_
  44.1 0.0 copy-start.1
  44.1 0.8 %collective-permute-start.21 = (bf16[128,256]{1,0:T(8,128)(2,1)S(1)}, bf16[128,256]{1,0:T(8,128)(2,1)S(1)}, u32[]{:S(2)}, u32[]{:S(2)}) collective-permute-start(bf16[128,256]{1,0:T(8,128)(2,1)S(1)} %get-tuple-element.49.refs_1_), channel_id=1, source_target_pairs={{0,1},{1,0},{2,3},{3,2},{4,5},{5,4},{6,7},{7,6},{8,9},{9,8},{10,11... | collective-permute-start | bytes 196616 | tf_op jit(solution)/shard_map/ppermute | solution.py:312
  44.9 0.0 collective-permute-done.9.refs_3_
  44.9 0.0 collective-permute-done.10.refs_4_
  44.9 0.5 phase.2.refs_3_
  45.4 0.1 collective-permute-start.11
  45.5 0.1 collective-permute-done.19.refs_2_
  45.6 2.2 %collective-permute-done.20.refs_3_ = bf16[128,256]{1,0:T(8,128)(2,1)S(1)} collective-permute-done((bf16[128,256]{1,0:T(8,128)(2,1)S(1)}, bf16[128,256]{1,0:T(8,128)(2,1)S(1)}, u32[]{:S(2)}, u32[]{:S(2)}) %collective-permute-start.20) | collective-permute-done | bytes 65568 | tf_op jit(solution)/shard_map/ppermute | solution.py:312
  47.8 0.6 %collective-permute-done.21.refs_4_ = bf16[128,256]{1,0:T(8,128)(2,1)S(1)} collective-permute-done((bf16[128,256]{1,0:T(8,128)(2,1)S(1)}, bf16[128,256]{1,0:T(8,128)(2,1)S(1)}, u32[]{:S(2)}, u32[]{:S(2)}) %collective-permute-start.21) | collective-permute-done | bytes 65568 | tf_op jit(solution)/shard_map/ppermute | solution.py:312
  48.4 0.5 phase.3.refs_5_
  48.9 0.1 collective-permute-start.22
  49.0 0.0 collective-permute-done.11.refs_4_
  49.0 0.0 copy-done.1
  49.0 0.0 copy-done.2
  49.0 0.0 copy-done.3
  49.0 1.2 %recon.2 = (f32[128,512]{1,0:T(8,128)S(1)}, bf16[1024,512]{1,0:T(8,128)(2,1)S(1)}, bf16[128,128]{1,0:T(8,128)(2,1)S(1)}) custom-call(s32[1,4]{1,0:T(1,128)S(1)} %copy-done.2, s32[16]{0:T(128)S(1)} %copy-done.3, bf16[4,1024,512]{2,1,0:T(8,128)(2,1)S(1)} %copy-done.1, bf16[128,1024]{1,0:T(8,128)(2,1)S(1)} %phase.2.refs_3_, ...), custom_call_target="tpu_custom_call" | custom-call | flops 1 | bytes 1 | tf_op jit(solution)/shard_map/recon/pallas_call | solution.py:412
  50.2 0.3 collective-permute-done.22.phase
  50.5 1.1 %recon.3 = bf16[128,512]{1,0:T(8,128)(2,1)} custom-call(bf16[1024,512]{1,0:T(8,128)(2,1)S(1)} %get-tuple-element.52.weights, bf16[128,1024]{1,0:T(8,128)(2,1)S(1)} %collective-permute-done.22.phase, f32[128,512]{1,0:T(8,128)S(1)} %get-tuple-element.53.before, bf16[128,128]{1,0:T(8,128)(2,1)S(1)} %get-tuple-element.54.select), custom_call_target="tpu_custom_call" | custom-call | flops 1 | bytes 1 | tf_op jit(solution)/shard_map/recon/pallas_call | solution.py:425
  (2 shorter events, 0.0 us)
Async XLA Ops:
  0.0 3.1 %copy-start = (bf16[1024,1024]{1,0:T(8,128)(2,1)S(1)}, bf16[1024,1024]{1,0:T(8,128)(2,1)}, u32[]{:S(2)}) copy-start(bf16[1024,1024]{1,0:T(8,128)(2,1)} %constant.2.clone.refs_2_.refs_0_) | copy-start | bytes 6291460
  0.0 3.1 %collective-permute-start = (bf16[4,2,64,1024]{3,2,1,0:T(8,128)(2,1)}, bf16[4,2,64,1024]{3,2,1,0:T(8,128)(2,1)S(1)}, u32[]{:S(2)}, u32[]{:S(2)}) collective-permute-start(bf16[4,2,64,1024]{3,2,1,0:T(8,128)(2,1)} %bitcast.1), channel_id=1, source_target_pairs={{0,16},{1,17},{2,18},{3,19},{4,20},{5,21},{6,22},{7,23},{8,24},{9,... | collective-permute-start | bytes 3145736 | tf_op jit(solution)/shard_map/ppermute | solution.py:312
  5.0 7.8 %collective-permute-start.1 = (bf16[4,64,256]{2,1,0:T(8,128)(2,1)S(1)}, bf16[4,64,256]{2,1,0:T(8,128)(2,1)S(1)}, u32[]{:S(2)}, u32[]{:S(2)}) collective-permute-start(bf16[4,64,256]{2,1,0:T(8,128)(2,1)S(1)} %get-tuple-element.31), channel_id=1, source_target_pairs={{0,2},{1,3},{2,0},{3,1},{4,6},{5,7},{6,4},{7,5},{8,10},{9,11},{10,... | collective-permute-start | bytes 393224 | tf_op jit(solution)/shard_map/ppermute | solution.py:312
  7.8 6.6 %collective-permute-start.2 = (bf16[4,64,256]{2,1,0:T(8,128)(2,1)S(1)}, bf16[4,64,256]{2,1,0:T(8,128)(2,1)S(1)}, u32[]{:S(2)}, u32[]{:S(2)}) collective-permute-start(bf16[4,64,256]{2,1,0:T(8,128)(2,1)S(1)} %get-tuple-element.32), channel_id=1, source_target_pairs={{0,1},{1,0},{2,3},{3,2},{4,5},{5,4},{6,7},{7,6},{8,9},{9,8},{10,11... | collective-permute-start | bytes 393224 | tf_op jit(solution)/shard_map/ppermute | solution.py:312
  9.3 7.4 %collective-permute-start.3 = (bf16[4,64,256]{2,1,0:T(8,128)(2,1)S(1)}, bf16[4,64,256]{2,1,0:T(8,128)(2,1)S(1)}, u32[]{:S(2)}, u32[]{:S(2)}) collective-permute-start(bf16[4,64,256]{2,1,0:T(8,128)(2,1)S(1)} %get-tuple-element.33), channel_id=1, source_target_pairs={{0,3},{1,2},{2,1},{3,0},{4,7},{5,6},{6,5},{7,4},{8,11},{9,10},{10,... | collective-permute-start | bytes 393224 | tf_op jit(solution)/shard_map/ppermute | solution.py:312
  9.3 10.3 %collective-permute-start.12 = (bf16[4,64,256]{2,1,0:T(8,128)(2,1)S(1)}, bf16[4,64,256]{2,1,0:T(8,128)(2,1)S(1)}, u32[]{:S(2)}, u32[]{:S(2)}) collective-permute-start(bf16[4,64,256]{2,1,0:T(8,128)(2,1)S(1)} %get-tuple-element.42), channel_id=1, source_target_pairs={{0,2},{1,3},{2,0},{3,1},{4,6},{5,7},{6,4},{7,5},{8,10},{9,11},{10,... | collective-permute-start | bytes 393224 | tf_op jit(solution)/shard_map/ppermute | solution.py:312
  11.3 11.5 %collective-permute-start.13 = (bf16[4,64,256]{2,1,0:T(8,128)(2,1)S(1)}, bf16[4,64,256]{2,1,0:T(8,128)(2,1)S(1)}, u32[]{:S(2)}, u32[]{:S(2)}) collective-permute-start(bf16[4,64,256]{2,1,0:T(8,128)(2,1)S(1)} %get-tuple-element.43), channel_id=1, source_target_pairs={{0,1},{1,0},{2,3},{3,2},{4,5},{5,4},{6,7},{7,6},{8,9},{9,8},{10,11... | collective-permute-start | bytes 393224 | tf_op jit(solution)/shard_map/ppermute | solution.py:312
  12.8 10.0 %collective-permute-start.14 = (bf16[4,64,256]{2,1,0:T(8,128)(2,1)S(1)}, bf16[4,64,256]{2,1,0:T(8,128)(2,1)S(1)}, u32[]{:S(2)}, u32[]{:S(2)}) collective-permute-start(bf16[4,64,256]{2,1,0:T(8,128)(2,1)S(1)} %get-tuple-element.44), channel_id=1, source_target_pairs={{0,3},{1,2},{2,1},{3,0},{4,7},{5,6},{6,5},{7,4},{8,11},{9,10},{10,... | collective-permute-start | bytes 393224 | tf_op jit(solution)/shard_map/ppermute | solution.py:312
  18.0 6.5 %collective-permute-start.4 = (bf16[256,256]{1,0:T(8,128)(2,1)S(1)}, bf16[256,256]{1,0:T(8,128)(2,1)S(1)}, u32[]{:S(2)}, u32[]{:S(2)}) collective-permute-start(bf16[256,256]{1,0:T(8,128)(2,1)S(1)} %get-tuple-element.36), channel_id=1, source_target_pairs={{0,4},{1,5},{2,6},{3,7},{4,0},{5,1},{6,2},{7,3},{8,12},{9,13},{10,... | collective-permute-start | bytes 393224 | tf_op jit(solution)/shard_map/ppermute | solution.py:312
  19.6 7.6 %collective-permute-start.7 = (bf16[256,256]{1,0:T(8,128)(2,1)S(1)}, bf16[256,256]{1,0:T(8,128)(2,1)S(1)}, u32[]{:S(2)}, u32[]{:S(2)}) collective-permute-start(bf16[256,256]{1,0:T(8,128)(2,1)S(1)} %get-tuple-element.37), channel_id=1, source_target_pairs={{0,16},{1,17},{2,18},{3,19},{4,8},{5,9},{6,10},{7,11},{8,4},{9,5},... | collective-permute-start | bytes 393224 | tf_op jit(solution)/shard_map/ppermute | solution.py:312
  19.6 9.1 %collective-permute-start.6 = (bf16[256,256]{1,0:T(8,128)(2,1)S(1)}, bf16[256,256]{1,0:T(8,128)(2,1)S(1)}, u32[]{:S(2)}, u32[]{:S(2)}) collective-permute-start(bf16[256,256]{1,0:T(8,128)(2,1)S(1)} %get-tuple-element.37), channel_id=1, source_target_pairs={{0,4},{1,5},{2,6},{3,7},{4,0},{5,1},{6,2},{7,3},{8,12},{9,13},{10,... | collective-permute-start | bytes 393224 | tf_op jit(solution)/shard_map/ppermute | solution.py:312
  24.1 6.6 %collective-permute-start.15 = (bf16[256,256]{1,0:T(8,128)(2,1)S(1)}, bf16[256,256]{1,0:T(8,128)(2,1)S(1)}, u32[]{:S(2)}, u32[]{:S(2)}) collective-permute-start(bf16[256,256]{1,0:T(8,128)(2,1)S(1)} %get-tuple-element.47), channel_id=1, source_target_pairs={{0,4},{1,5},{2,6},{3,7},{4,0},{5,1},{6,2},{7,3},{8,12},{9,13},{10,... | collective-permute-start | bytes 393224 | tf_op jit(solution)/shard_map/ppermute | solution.py:312
  24.5 10.3 %collective-permute-start.5 = (bf16[256,256]{1,0:T(8,128)(2,1)S(1)}, bf16[256,256]{1,0:T(8,128)(2,1)S(1)}, u32[]{:S(2)}, u32[]{:S(2)}) collective-permute-start(bf16[256,256]{1,0:T(8,128)(2,1)S(1)} %far.2), channel_id=1, source_target_pairs={{0,8},{1,9},{2,10},{3,11},{4,12},{5,13},{6,14},{7,15},{8,0},{9,1},... | collective-permute-start | bytes 393224 | tf_op jit(solution)/shard_map/ppermute | solution.py:312
  27.2 10.7 %collective-permute-start.18 = (bf16[256,256]{1,0:T(8,128)(2,1)S(1)}, bf16[256,256]{1,0:T(8,128)(2,1)S(1)}, u32[]{:S(2)}, u32[]{:S(2)}) collective-permute-start(bf16[256,256]{1,0:T(8,128)(2,1)S(1)} %get-tuple-element.48), channel_id=1, source_target_pairs={{0,16},{1,17},{2,18},{3,19},{4,8},{5,9},{6,10},{7,11},{8,4},{9,5},... | collective-permute-start | bytes 393224 | tf_op jit(solution)/shard_map/ppermute | solution.py:312
  27.2 11.3 %collective-permute-start.17 = (bf16[256,256]{1,0:T(8,128)(2,1)S(1)}, bf16[256,256]{1,0:T(8,128)(2,1)S(1)}, u32[]{:S(2)}, u32[]{:S(2)}) collective-permute-start(bf16[256,256]{1,0:T(8,128)(2,1)S(1)} %get-tuple-element.48), channel_id=1, source_target_pairs={{0,4},{1,5},{2,6},{3,7},{4,0},{5,1},{6,2},{7,3},{8,12},{9,13},{10,... | collective-permute-start | bytes 393224 | tf_op jit(solution)/shard_map/ppermute | solution.py:312
  30.7 10.5 %collective-permute-start.16 = (bf16[256,256]{1,0:T(8,128)(2,1)S(1)}, bf16[256,256]{1,0:T(8,128)(2,1)S(1)}, u32[]{:S(2)}, u32[]{:S(2)}) collective-permute-start(bf16[256,256]{1,0:T(8,128)(2,1)S(1)} %far.3), channel_id=1, source_target_pairs={{0,8},{1,9},{2,10},{3,11},{4,12},{5,13},{6,14},{7,15},{8,0},{9,1},... | collective-permute-start | bytes 393224 | tf_op jit(solution)/shard_map/ppermute | solution.py:312
  34.9 9.2 %collective-permute-start.8 = (bf16[128,256]{1,0:T(8,128)(2,1)S(1)}, bf16[128,256]{1,0:T(8,128)(2,1)S(1)}, u32[]{:S(2)}, u32[]{:S(2)}) collective-permute-start(bf16[128,256]{1,0:T(8,128)(2,1)S(1)} %get-tuple-element.39), channel_id=1, source_target_pairs={{0,2},{1,3},{2,0},{3,1},{4,6},{5,7},{6,4},{7,5},{8,10},{9,11},{10,... | collective-permute-start | bytes 196616 | tf_op jit(solution)/shard_map/ppermute | solution.py:312
  36.4 8.5 %collective-permute-start.9 = (bf16[128,256]{1,0:T(8,128)(2,1)S(1)}, bf16[128,256]{1,0:T(8,128)(2,1)S(1)}, u32[]{:S(2)}, u32[]{:S(2)}) collective-permute-start(bf16[128,256]{1,0:T(8,128)(2,1)S(1)} %get-tuple-element.40), channel_id=1, source_target_pairs={{0,3},{1,2},{2,1},{3,0},{4,7},{5,6},{6,5},{7,4},{8,11},{9,10},{10,... | collective-permute-start | bytes 196616 | tf_op jit(solution)/shard_map/ppermute | solution.py:312
  37.9 7.0 %collective-permute-start.10 = (bf16[128,256]{1,0:T(8,128)(2,1)S(1)}, bf16[128,256]{1,0:T(8,128)(2,1)S(1)}, u32[]{:S(2)}, u32[]{:S(2)}) collective-permute-start(bf16[128,256]{1,0:T(8,128)(2,1)S(1)} %get-tuple-element.38.refs_1_), channel_id=1, source_target_pairs={{0,1},{1,0},{2,3},{3,2},{4,5},{5,4},{6,7},{7,6},{8,9},{9,8},{10,11... | collective-permute-start | bytes 196616 | tf_op jit(solution)/shard_map/ppermute | solution.py:312
  41.3 4.3 %collective-permute-start.19 = (bf16[128,256]{1,0:T(8,128)(2,1)S(1)}, bf16[128,256]{1,0:T(8,128)(2,1)S(1)}, u32[]{:S(2)}, u32[]{:S(2)}) collective-permute-start(bf16[128,256]{1,0:T(8,128)(2,1)S(1)} %get-tuple-element.50), channel_id=1, source_target_pairs={{0,2},{1,3},{2,0},{3,1},{4,6},{5,7},{6,4},{7,5},{8,10},{9,11},{10,... | collective-permute-start | bytes 196616 | tf_op jit(solution)/shard_map/ppermute | solution.py:312
  42.6 5.2 %collective-permute-start.20 = (bf16[128,256]{1,0:T(8,128)(2,1)S(1)}, bf16[128,256]{1,0:T(8,128)(2,1)S(1)}, u32[]{:S(2)}, u32[]{:S(2)}) collective-permute-start(bf16[128,256]{1,0:T(8,128)(2,1)S(1)} %get-tuple-element.51), channel_id=1, source_target_pairs={{0,3},{1,2},{2,1},{3,0},{4,7},{5,6},{6,5},{7,4},{8,11},{9,10},{10,... | collective-permute-start | bytes 196616 | tf_op jit(solution)/shard_map/ppermute | solution.py:312
  44.1 4.9 %copy-start.1 = (bf16[4,1024,512]{2,1,0:T(8,128)(2,1)S(1)}, bf16[4,1024,512]{2,1,0:T(8,128)(2,1)}, u32[]{:S(2)}) copy-start(bf16[4,1024,512]{2,1,0:T(8,128)(2,1)} %refs_2_.2) | copy-start | bytes 12582916
  44.1 4.9 %copy-start.2 = (s32[1,4]{1,0:T(1,128)S(1)}, s32[1,4]{1,0:T(1,128)}, u32[]{:S(2)}) copy-start(s32[1,4]{1,0:T(1,128)} %refs_0_.7) | copy-start | bytes 52
  44.1 4.9 %copy-start.3 = (s32[16]{0:T(128)S(1)}, s32[16]{0:T(128)}, u32[]{:S(2)}) copy-start(s32[16]{0:T(128)} %refs_1_.1) | copy-start | bytes 196
  44.1 4.3 %collective-permute-start.21 = (bf16[128,256]{1,0:T(8,128)(2,1)S(1)}, bf16[128,256]{1,0:T(8,128)(2,1)S(1)}, u32[]{:S(2)}, u32[]{:S(2)}) collective-permute-start(bf16[128,256]{1,0:T(8,128)(2,1)S(1)} %get-tuple-element.49.refs_1_), channel_id=1, source_target_pairs={{0,1},{1,0},{2,3},{3,2},{4,5},{5,4},{6,7},{7,6},{8,9},{9,8},{10,11... | collective-permute-start | bytes 196616 | tf_op jit(solution)/shard_map/ppermute | solution.py:312
  45.4 3.6 %collective-permute-start.11 = (bf16[128,1024]{1,0:T(8,128)(2,1)S(1)}, bf16[128,1024]{1,0:T(8,128)(2,1)S(1)}, u32[]{:S(2)}, u32[]{:S(2)}) collective-permute-start(bf16[128,1024]{1,0:T(8,128)(2,1)S(1)} %phase.2.refs_3_), channel_id=1, source_target_pairs={{0,16},{1,17},{2,18},{3,19},{4,20},{5,21},{6,22},{7,23},{8,24},{9,... | collective-permute-start | bytes 786440 | tf_op jit(solution)/shard_map/ppermute | solution.py:312
  48.9 1.6 %collective-permute-start.22 = (bf16[128,1024]{1,0:T(8,128)(2,1)S(1)}, bf16[128,1024]{1,0:T(8,128)(2,1)S(1)}, u32[]{:S(2)}, u32[]{:S(2)}) collective-permute-start(bf16[128,1024]{1,0:T(8,128)(2,1)S(1)} %phase.3.refs_5_), channel_id=1, source_target_pairs={{0,16},{1,17},{2,18},{3,19},{4,20},{5,21},{6,22},{7,23},{8,24},{9,... | collective-permute-start | bytes 786440 | tf_op jit(solution)/shard_map/ppermute | solution.py:312

commit v26 on v19

--- a/solution.py
+++ b/solution.py
@@ -165,7 +165,7 @@
 
 def column_kernel(inner, outer, table, gain, *refs):
     pieces = dict(zip(send_order, refs[:inner]))
-    *outs, stack, total, spectrum = refs[inner:]
+    ours, second, *halves, stack, total, spectrum = refs[inner:]
     _, plane, spot = position(inner)
     dists, rows_dev, block = pieces[0].shape
     depth = inner * rows_dev
@@ -183,10 +183,19 @@
     spectrum[...] = total[...].astype(bf16)
     middle = (plane == 1) | (plane == 2)
     first = jnp.where(middle, 1, 3)
-    for rel, out in zip((0, first, 4 - first, 2), outs):
+    splits = len(halves) // 2
+    wide = block // splits
+    for rel, targets in (
+        (first, halves[:splits]),
+        (4 - first, [second]),
+        (2, halves[splits:]),
+        (0, [ours]),
+    ):
         rows = pl.ds(pl.multiple_of((plane ^ rel) * depth, depth), depth)
-        value = jnp.dot(table[rows, :], spectrum[...], preferred_element_type=f32)
-        out[...] = value.astype(bf16)
+        value = jnp.dot(table[rows, :], spectrum[...], preferred_element_type=f32).astype(bf16)
+        for split, out in enumerate(targets):
+            width_here = out.shape[1]
+            out[...] = value[:, split * wide : split * wide + width_here]
 
 
 def far_kernel(inner, *refs):
@@ -197,16 +206,21 @@
     out[...] = (ours[...].astype(f32) + more).astype(bf16)
 
 
-def half_kernel(inner, ours, far, near, next_near, across, other, mine, again):
+def half_kernel(inner, splits, ours, next_near, across, *refs):
+    fars, nears = refs[:splits], refs[splits : 2 * splits]
+    other, mine, again = refs[-3:]
     _, plane, spot = position(inner)
     middle = (plane == 1) | (plane == 2)
-    capacity = mine.shape[0]
+    capacity, block = mine.shape
+    wide = block // splits
     for out, pair in ((mine, spot // 2), (other, 1 - spot // 2)):
         rows = pl.ds(pl.multiple_of(pair * capacity, capacity), capacity)
-        inside = next_near[rows, :].astype(f32) + across[rows, :].astype(f32)
-        more = jnp.where(middle, inside, near[rows, :].astype(f32))
-        got = ours[rows, :].astype(f32) + far[rows, :].astype(f32) + more
-        out[...] = got.astype(bf16)
+        for split in range(splits):
+            lanes = slice(split * wide, (split + 1) * wide)
+            inside = next_near[rows, lanes].astype(f32) + across[rows, lanes].astype(f32)
+            more = jnp.where(middle, inside, nears[split][rows, :].astype(f32))
+            got = ours[rows, lanes].astype(f32) + fars[split][rows, :].astype(f32) + more
+            out[:, lanes] = got.astype(bf16)
     again[...] = other[...]
 
 
@@ -339,13 +353,18 @@
         spread(pieces[chunk * inner : (chunk + 1) * inner], send_order) for chunk in range(own)
     ]
 
+    def parts_of(chunk):
+        return 2 if chunk == own - 1 and block % 256 == 0 else 1
+
     sums = []
     for chunk in range(own):
+        splits = parts_of(chunk)
         blocks = pl.pallas_call(
             lambda *refs: column_kernel(inner, outer, *refs),
-            out_shape=[shaped(depth, block)] * outer,
+            out_shape=[shaped(depth, block)] * 2
+            + [shaped(depth, block // splits)] * (2 * splits),
             in_specs=vmem(2 + inner),
-            out_specs=vmem(outer),
+            out_specs=vmem(2 + 2 * splits),
             scratch_shapes=[
                 pltpu.VMEM((dists, depth, block), bf16),
                 pltpu.VMEM((width, block), f32),
@@ -355,32 +374,37 @@
             cost_estimate=cheap,
             name="columns",
         )(table, gain, *arrived[chunk])
-        ours, first, second, third = blocks
-        near = sent(first, to_plane(1))
-        earlier = sums[-1][3:] if sums else []
-        message = pl.pallas_call(
-            lambda *refs: far_kernel(inner, *refs),
-            out_shape=shaped(depth, block),
-            in_specs=unread(len(earlier)) + vmem(2),
-            out_specs=one_out,
-            compiler_params=params,
-            cost_estimate=cheap,
-            name="far",
-        )(*earlier, third, near)
-        far = sent(message, to_plane(2))
-        sums.append([ours, far, near, sent(second, to_plane(1)), sent(second, to_middle)])
+        ours, second, *halves = blocks
+        earlier = sums[-1][1:3] if sums else []
+        nears = [sent(half, to_plane(1)) for half in halves[:splits]]
+        fars = []
+        for split in range(splits):
+            message = pl.pallas_call(
+                lambda *refs: far_kernel(inner, *refs),
+                out_shape=shaped(depth, block // splits),
+                in_specs=unread(len(earlier)) + vmem(2),
+                out_specs=one_out,
+                compiler_params=params,
+                cost_estimate=cheap,
+                name="far",
+            )(*earlier, halves[splits + split], nears[split])
+            fars.append(sent(message, to_plane(2)))
+        sums.append(
+            [ours, sent(second, to_plane(1)), sent(second, to_middle), *fars, *nears]
+        )
 
     phases = []
     for chunk in range(own):
+        sent_before = pieces[2:3] if chunk else []
         second, first, again = pl.pallas_call(
-            lambda *refs: half_kernel(inner, *refs),
+            lambda *refs, chunk=chunk: half_kernel(inner, parts_of(chunk), *refs),
             out_shape=[shaped(capacity, block)] * 3,
-            in_specs=vmem(5),
+            in_specs=vmem(len(sums[chunk])) + unread(len(sent_before)),
             out_specs=vmem(3),
             compiler_params=params,
             cost_estimate=cheap,
             name="half",
-        )(*sums[chunk])
+        )(*sums[chunk], *sent_before)
         pieces = spread([first, first, second, again], tail_order)
         phase = pl.pallas_call(
             lambda *refs: phase_kernel(inner, *refs),

time: 51.7 us -> 52.4 us (1.014)
  starting transfers between devices: 28.9 us -> 31.7 us
  waiting for transfers between devices: 11.9 us -> 9.72 us
    ppermute x23 -> x25, starting transfers between devices: 28.9 us -> 31.7 us  [sent(): return lax.ppermute(value, ('dist', 'rows'), pairs)]
    ppermute x23 -> x25, waiting for transfers between devices: 11.9 us -> 9.72 us  [sent(): return lax.ppermute(value, ('dist', 'rows'), pairs)]
  transfers between devices with their start and end apart: 23 -> 25, of which waited for: 8 -> 6; matrix products, arithmetic and copies ran while one was open for 0% -> 0% of each run, Pallas kernels for 15% -> 15%
where the time goes in v26:
time: 52.4 us; the launch traced here: 52.2 us
  starting transfers between devices  31.7 us (60%)
  Pallas kernels  10.6 us (20%)
  waiting for transfers between devices  9.72 us (19%)
    ppermute x25, starting transfers between devices, sent(): return lax.ppermute(value, ('dist', 'rows'), pairs)  31.7 us
    ppermute x25, waiting for transfers between devices, sent(): return lax.ppermute(value, ('dist', 'rows'), pairs)  9.72 us
    pallas_call x1, Pallas kernels, plane_plan(): pl.pallas_call(lambda *refs: filter_kernel(inner, dist_dev, *refs), out_s...  2.62 us
    pallas_call x2, Pallas kernels, plane_plan(): pl.pallas_call(lambda *refs: column_kernel(inner, outer, *refs), out_shap...  2.59 us
    pallas_call x1, Pallas kernels, plane_plan(): pl.pallas_call(lambda *refs: row_kernel(inner, *refs), out_shape=[shaped(...  1.83 us
    pallas_call x1, Pallas kernels, plane_plan(): pl.pallas_call(lambda *refs: recon_kernel(own, *refs), out_shape=[jax.Sha...  1.2 us
    pallas_call x1, Pallas kernels, plane_plan(): pl.pallas_call(recon_last_kernel, out_shape=shaped(capacity, pixels), in_...  1.12 us
  transfers between devices with their start and end apart: 25, of which 6 were waited for; matrix products, arithmetic and copies ran while one was open for 0% of the time, Pallas kernels for 15%

profile of v26, /device:TPU:0, one launch (start us, length us, event | category | flops | bytes accessed | tf_op | source)
XLA Modules:
  0.0 52.2 jit_solution(14185716054321468307)
XLA Ops:
  0.0 0.5 collective-permute-start
  0.5 2.6 %filters.1.refs_3_.refs_1_ = bf16[4,1024,256]{2,1,0:T(8,128)(2,1)S(1)} custom-call(f32[4]{0:T(128)} %refs_0_.6), custom_call_target="tpu_custom_call" | custom-call | flops 1 | bytes 1 | tf_op jit(solution)/shard_map/filters/pallas_call | solution.py:330
  3.1 0.0 collective-permute-done.refs_1_
  3.1 1.8 %row_spectra.1 = (bf16[4,64,256]{2,1,0:T(8,128)(2,1)S(1)}, bf16[4,64,256]{2,1,0:T(8,128)(2,1)S(1)}, bf16[4,64,256]{2,1,0:T(8,128)(2,1)S(1)}, bf16[4,64,256]{2,1,...) custom-call(bf16[4,2,64,1024]{3,2,1,0:T(8,128)(2,1)} %bitcast.2, ...), custom_call_target="tpu_custom_call" | custom-call | flops 1 | bytes 1 | tf_op jit(solution)/shard_map/row_spectra/pallas_call | solution.py:339
  4.9 2.8 %collective-permute-start.1 = (bf16[4,64,256]{2,1,0:T(8,128)(2,1)S(1)}, bf16[4,64,256]{2,1,0:T(8,128)(2,1)S(1)}, u32[]{:S(2)}, u32[]{:S(2)}) collective-permute-start(bf16[4,64,256]{2,1,0:T(8,128)(2,1)S(1)} %get-tuple-element.33), channel_id=1, source_target_pairs={{0,2},{1,3},{2,0},{3,1},{4,6},{5,7},{6,4},{7,5},{8,10},{9,11},{10,... | collective-permute-start | bytes 393224 | tf_op jit(solution)/shard_map/ppermute | solution.py:311
  7.7 1.5 %collective-permute-start.2 = (bf16[4,64,256]{2,1,0:T(8,128)(2,1)S(1)}, bf16[4,64,256]{2,1,0:T(8,128)(2,1)S(1)}, u32[]{:S(2)}, u32[]{:S(2)}) collective-permute-start(bf16[4,64,256]{2,1,0:T(8,128)(2,1)S(1)} %get-tuple-element.34), channel_id=1, source_target_pairs={{0,1},{1,0},{2,3},{3,2},{4,5},{5,4},{6,7},{7,6},{8,9},{9,8},{10,11... | collective-permute-start | bytes 393224 | tf_op jit(solution)/shard_map/ppermute | solution.py:311
  9.2 0.0 collective-permute-start.3
  9.3 1.9 %collective-permute-start.12 = (bf16[4,64,256]{2,1,0:T(8,128)(2,1)S(1)}, bf16[4,64,256]{2,1,0:T(8,128)(2,1)S(1)}, u32[]{:S(2)}, u32[]{:S(2)}) collective-permute-start(bf16[4,64,256]{2,1,0:T(8,128)(2,1)S(1)} %get-tuple-element.44), channel_id=1, source_target_pairs={{0,2},{1,3},{2,0},{3,1},{4,6},{5,7},{6,4},{7,5},{8,10},{9,11},{10,... | collective-permute-start | bytes 393224 | tf_op jit(solution)/shard_map/ppermute | solution.py:311
  11.2 1.5 %collective-permute-start.13 = (bf16[4,64,256]{2,1,0:T(8,128)(2,1)S(1)}, bf16[4,64,256]{2,1,0:T(8,128)(2,1)S(1)}, u32[]{:S(2)}, u32[]{:S(2)}) collective-permute-start(bf16[4,64,256]{2,1,0:T(8,128)(2,1)S(1)} %get-tuple-element.45), channel_id=1, source_target_pairs={{0,1},{1,0},{2,3},{3,2},{4,5},{5,4},{6,7},{7,6},{8,9},{9,8},{10,11... | collective-permute-start | bytes 393224 | tf_op jit(solution)/shard_map/ppermute | solution.py:311
  12.7 0.0 collective-permute-done.1.refs_3_
  12.7 1.6 %collective-permute-start.14 = (bf16[4,64,256]{2,1,0:T(8,128)(2,1)S(1)}, bf16[4,64,256]{2,1,0:T(8,128)(2,1)S(1)}, u32[]{:S(2)}, u32[]{:S(2)}) collective-permute-start(bf16[4,64,256]{2,1,0:T(8,128)(2,1)S(1)} %get-tuple-element.46), channel_id=1, source_target_pairs={{0,3},{1,2},{2,1},{3,0},{4,7},{5,6},{6,5},{7,4},{8,11},{9,10},{10,... | collective-permute-start | bytes 393224 | tf_op jit(solution)/shard_map/ppermute | solution.py:311
  14.3 0.0 collective-permute-done.2.refs_4_
  14.3 2.3 %collective-permute-done.3.refs_5_ = bf16[4,64,256]{2,1,0:T(8,128)(2,1)S(1)} collective-permute-done((bf16[4,64,256]{2,1,0:T(8,128)(2,1)S(1)}, bf16[4,64,256]{2,1,0:T(8,128)(2,1)S(1)}, u32[]{:S(2)}, u32[]{:S(2)}) %collective-permute-start.3) | collective-permute-done | bytes 131104 | tf_op jit(solution)/shard_map/ppermute | solution.py:311
  16.6 1.3 %columns.2 = (bf16[256,256]{1,0:T(8,128)(2,1)S(1)}, bf16[256,256]{1,0:T(8,128)(2,1)S(1)}, bf16[256,256]{1,0:T(8,128)(2,1)S(1)}, bf16[256,256]{1,0:T(8,128)(2,1)S(1)}) custom-call(bf16[1024,1024]{1,0:T(8,128)(2,1)S(1)} %copy-done, bf16[4,1024,256]{2,1,0:T(8,128)(2,1)S(1)} %filters.1.refs_3_.refs_1_, bf16[4,64,256]{2,1,0:T(8,128)(2,1)S(1)} %get-tuple-element.32.refs_2_, ...), custom_call_target="tpu_custom_call" | custom-call | flops 1 | bytes 1 | tf_op jit(solution)/shard_map/columns/pallas_call | solution.py:362
  17.9 1.6 %collective-permute-start.6 = (bf16[256,256]{1,0:T(8,128)(2,1)S(1)}, bf16[256,256]{1,0:T(8,128)(2,1)S(1)}, u32[]{:S(2)}, u32[]{:S(2)}) collective-permute-start(bf16[256,256]{1,0:T(8,128)(2,1)S(1)} %get-tuple-element.39), channel_id=1, source_target_pairs={{0,4},{1,5},{2,6},{3,7},{4,0},{5,1},{6,2},{7,3},{8,12},{9,13},{10,... | collective-permute-start | bytes 393224 | tf_op jit(solution)/shard_map/ppermute | solution.py:311
  19.5 0.0 collective-permute-start.5
  19.5 0.0 collective-permute-done.12.refs_3_
  19.5 3.2 %collective-permute-start.4 = (bf16[256,256]{1,0:T(8,128)(2,1)S(1)}, bf16[256,256]{1,0:T(8,128)(2,1)S(1)}, u32[]{:S(2)}, u32[]{:S(2)}) collective-permute-start(bf16[256,256]{1,0:T(8,128)(2,1)S(1)} %get-tuple-element.37), channel_id=1, source_target_pairs={{0,4},{1,5},{2,6},{3,7},{4,0},{5,1},{6,2},{7,3},{8,12},{9,13},{10,... | collective-permute-start | bytes 393224 | tf_op jit(solution)/shard_map/ppermute | solution.py:311
  22.7 0.0 collective-permute-done.13.refs_4_
  22.7 0.0 collective-permute-done.14.refs_5_
  22.7 1.3 %columns.3 = (bf16[256,256]{1,0:T(8,128)(2,1)S(1)}, bf16[256,256]{1,0:T(8,128)(2,1)S(1)}, bf16[256,128]{1,0:T(8,128)(2,1)S(1)}, bf16[256,128]{1,0:T(8,128)(2,1)S...) custom-call(bf16[1024,1024]{1,0:T(8,128)(2,1)S(1)} %copy-done, ...), custom_call_target="tpu_custom_call" | custom-call | flops 1 | bytes 1 | tf_op jit(solution)/shard_map/columns/pallas_call | solution.py:362
  24.0 0.4 collective-permute-start.17
  24.4 0.0 collective-permute-done.6.refs_1_.refs_4_
  24.4 0.1 far.3
  24.4 2.7 %collective-permute-start.7 = (bf16[256,256]{1,0:T(8,128)(2,1)S(1)}, bf16[256,256]{1,0:T(8,128)(2,1)S(1)}, u32[]{:S(2)}, u32[]{:S(2)}) collective-permute-start(bf16[256,256]{1,0:T(8,128)(2,1)S(1)} %far.3), channel_id=1, source_target_pairs={{0,8},{1,9},{2,10},{3,11},{4,12},{5,13},{6,14},{7,15},{8,0},{9,1},... | collective-permute-start | bytes 393224 | tf_op jit(solution)/shard_map/ppermute | solution.py:311
  27.1 1.5 %collective-permute-start.19 = (bf16[256,128]{1,0:T(8,128)(2,1)S(1)}, bf16[256,128]{1,0:T(8,128)(2,1)S(1)}, u32[]{:S(2)}, u32[]{:S(2)}) collective-permute-start(bf16[256,128]{1,0:T(8,128)(2,1)S(1)} %get-tuple-element.52), channel_id=1, source_target_pairs={{0,4},{1,5},{2,6},{3,7},{4,0},{5,1},{6,2},{7,3},{8,12},{9,13},{10,... | collective-permute-start | bytes 196616 | tf_op jit(solution)/shard_map/ppermute | solution.py:311
  28.6 1.6 %collective-permute-done.17.refs_3_.refs_5_ = bf16[256,128]{1,0:T(8,128)(2,1)S(1)} collective-permute-done((bf16[256,128]{1,0:T(8,128)(2,1)S(1)}, bf16[256,128]{1,0:T(8,128)(2,1)S(1)}, u32[]{:S(2)}, u32[]{:S(2)}) %collective-permute-start.17) | collective-permute-done | bytes 65568 | tf_op jit(solution)/shard_map/ppermute | solution.py:311
  30.2 0.0 collective-permute-start.16
  30.2 0.0 collective-permute-done.5.refs_2_.refs_1_
  30.2 1.3 %collective-permute-start.15 = (bf16[256,256]{1,0:T(8,128)(2,1)S(1)}, bf16[256,256]{1,0:T(8,128)(2,1)S(1)}, u32[]{:S(2)}, u32[]{:S(2)}) collective-permute-start(bf16[256,256]{1,0:T(8,128)(2,1)S(1)} %get-tuple-element.48), channel_id=1, source_target_pairs={{0,4},{1,5},{2,6},{3,7},{4,0},{5,1},{6,2},{7,3},{8,12},{9,13},{10,... | collective-permute-start | bytes 393224 | tf_op jit(solution)/shard_map/ppermute | solution.py:311
  31.6 0.0 collective-permute-done.4.refs_1_.refs_0_
  31.6 2.0 %collective-permute-start.18 = (bf16[256,128]{1,0:T(8,128)(2,1)S(1)}, bf16[256,128]{1,0:T(8,128)(2,1)S(1)}, u32[]{:S(2)}, u32[]{:S(2)}) collective-permute-start(bf16[256,128]{1,0:T(8,128)(2,1)S(1)} %far.4), channel_id=1, source_target_pairs={{0,8},{1,9},{2,10},{3,11},{4,12},{5,13},{6,14},{7,15},{8,0},{9,1},... | collective-permute-start | bytes 196616 | tf_op jit(solution)/shard_map/ppermute | solution.py:311
  33.6 0.0 collective-permute-done.19.refs_3_.refs_6_
  33.7 1.0 %collective-permute-start.20 = (bf16[256,128]{1,0:T(8,128)(2,1)S(1)}, bf16[256,128]{1,0:T(8,128)(2,1)S(1)}, u32[]{:S(2)}, u32[]{:S(2)}) collective-permute-start(bf16[256,128]{1,0:T(8,128)(2,1)S(1)} %far.5), channel_id=1, source_target_pairs={{0,8},{1,9},{2,10},{3,11},{4,12},{5,13},{6,14},{7,15},{8,0},{9,1},... | collective-permute-start | bytes 196616 | tf_op jit(solution)/shard_map/ppermute | solution.py:311
  34.7 0.0 collective-permute-done.7.refs_3_
  34.7 0.1 half.2
  34.8 2.8 %collective-permute-start.9 = (bf16[128,256]{1,0:T(8,128)(2,1)S(1)}, bf16[128,256]{1,0:T(8,128)(2,1)S(1)}, u32[]{:S(2)}, u32[]{:S(2)}) collective-permute-start(bf16[128,256]{1,0:T(8,128)(2,1)S(1)} %get-tuple-element.42), channel_id=1, source_target_pairs={{0,3},{1,2},{2,1},{3,0},{4,7},{5,6},{6,5},{7,4},{8,11},{9,10},{10,... | collective-permute-start | bytes 196616 | tf_op jit(solution)/shard_map/ppermute | solution.py:311
  37.7 0.0 collective-permute-done.16.refs_2_
  37.7 0.5 collective-permute-start.8
  38.2 0.0 collective-permute-done.15.refs_1_
  38.2 1.1 %collective-permute-start.10 = (bf16[128,256]{1,0:T(8,128)(2,1)S(1)}, bf16[128,256]{1,0:T(8,128)(2,1)S(1)}, u32[]{:S(2)}, u32[]{:S(2)}) collective-permute-start(bf16[128,256]{1,0:T(8,128)(2,1)S(1)} %get-tuple-element.40.refs_1_), channel_id=1, source_target_pairs={{0,1},{1,0},{2,3},{3,2},{4,5},{5,4},{6,7},{7,6},{8,9},{9,8},{10,11... | collective-permute-start | bytes 196616 | tf_op jit(solution)/shard_map/ppermute | solution.py:311
  39.3 0.0 collective-permute-done.18.refs_3_
  39.3 2.0 %collective-permute-done.20.refs_4_ = bf16[256,128]{1,0:T(8,128)(2,1)S(1)} collective-permute-done((bf16[256,128]{1,0:T(8,128)(2,1)S(1)}, bf16[256,128]{1,0:T(8,128)(2,1)S(1)}, u32[]{:S(2)}, u32[]{:S(2)}) %collective-permute-start.20) | collective-permute-done | bytes 65568 | tf_op jit(solution)/shard_map/ppermute | solution.py:311
  41.3 0.0 collective-permute-done.9.refs_3_.refs_7_
  41.3 0.1 half.3
  41.4 1.9 %collective-permute-start.21 = (bf16[128,256]{1,0:T(8,128)(2,1)S(1)}, bf16[128,256]{1,0:T(8,128)(2,1)S(1)}, u32[]{:S(2)}, u32[]{:S(2)}) collective-permute-start(bf16[128,256]{1,0:T(8,128)(2,1)S(1)} %get-tuple-element.54), channel_id=1, source_target_pairs={{0,2},{1,3},{2,0},{3,1},{4,6},{5,7},{6,4},{7,5},{8,10},{9,11},{10,... | collective-permute-start | bytes 196616 | tf_op jit(solution)/shard_map/ppermute | solution.py:311
  43.2 1.4 %collective-permute-start.22 = (bf16[128,256]{1,0:T(8,128)(2,1)S(1)}, bf16[128,256]{1,0:T(8,128)(2,1)S(1)}, u32[]{:S(2)}, u32[]{:S(2)}) collective-permute-start(bf16[128,256]{1,0:T(8,128)(2,1)S(1)} %get-tuple-element.55), channel_id=1, source_target_pairs={{0,3},{1,2},{2,1},{3,0},{4,7},{5,6},{6,5},{7,4},{8,11},{9,10},{10,... | collective-permute-start | bytes 196616 | tf_op jit(solution)/shard_map/ppermute | solution.py:311
  44.7 0.3 collective-permute-start.23
  44.9 0.0 collective-permute-done.8.refs_2_
  44.9 0.0 collective-permute-done.10.refs_4_
  44.9 0.5 phase.2.refs_3_
  45.4 0.1 collective-permute-start.11
  45.5 0.5 collective-permute-done.21.refs_2_
  45.9 3.1 %collective-permute-done.22.refs_3_ = bf16[128,256]{1,0:T(8,128)(2,1)S(1)} collective-permute-done((bf16[128,256]{1,0:T(8,128)(2,1)S(1)}, bf16[128,256]{1,0:T(8,128)(2,1)S(1)}, u32[]{:S(2)}, u32[]{:S(2)}) %collective-permute-start.22) | collective-permute-done | bytes 65568 | tf_op jit(solution)/shard_map/ppermute | solution.py:311
  49.0 0.0 collective-permute-done.23.refs_4_
  49.0 0.5 phase.3.refs_5_
  49.5 0.1 collective-permute-start.24
  49.6 0.0 collective-permute-done.11.refs_4_
  49.6 0.0 copy-done.1
  49.6 0.0 copy-done.2
  49.6 0.0 copy-done.3
  49.6 1.2 %recon.2 = (f32[128,512]{1,0:T(8,128)S(1)}, bf16[1024,512]{1,0:T(8,128)(2,1)S(1)}, bf16[128,128]{1,0:T(8,128)(2,1)S(1)}) custom-call(s32[1,4]{1,0:T(1,128)S(1)} %copy-done.2, s32[16]{0:T(128)S(1)} %copy-done.3, bf16[4,1024,512]{2,1,0:T(8,128)(2,1)S(1)} %copy-done.1, bf16[128,1024]{1,0:T(8,128)(2,1)S(1)} %phase.2.refs_3_, ...), custom_call_target="tpu_custom_call" | custom-call | flops 1 | bytes 1 | tf_op jit(solution)/shard_map/recon/pallas_call | solution.py:421
  50.8 0.3 collective-permute-done.24.phase
  51.1 1.1 %recon.3 = bf16[128,512]{1,0:T(8,128)(2,1)} custom-call(bf16[1024,512]{1,0:T(8,128)(2,1)S(1)} %get-tuple-element.56.weights, bf16[128,1024]{1,0:T(8,128)(2,1)S(1)} %collective-permute-done.24.phase, f32[128,512]{1,0:T(8,128)S(1)} %get-tuple-element.57.before, bf16[128,128]{1,0:T(8,128)(2,1)S(1)} %get-tuple-element.58.select), custom_call_target="tpu_custom_call" | custom-call | flops 1 | bytes 1 | tf_op jit(solution)/shard_map/recon/pallas_call | solution.py:434
  (7 shorter events, 0.1 us)
Async XLA Ops:
  0.0 3.1 %copy-start = (bf16[1024,1024]{1,0:T(8,128)(2,1)S(1)}, bf16[1024,1024]{1,0:T(8,128)(2,1)}, u32[]{:S(2)}) copy-start(bf16[1024,1024]{1,0:T(8,128)(2,1)} %constant.2.clone.refs_2_.refs_0_) | copy-start | bytes 6291460
  0.0 3.1 %collective-permute-start = (bf16[4,2,64,1024]{3,2,1,0:T(8,128)(2,1)}, bf16[4,2,64,1024]{3,2,1,0:T(8,128)(2,1)S(1)}, u32[]{:S(2)}, u32[]{:S(2)}) collective-permute-start(bf16[4,2,64,1024]{3,2,1,0:T(8,128)(2,1)} %bitcast.1), channel_id=1, source_target_pairs={{0,16},{1,17},{2,18},{3,19},{4,20},{5,21},{6,22},{7,23},{8,24},{9,... | collective-permute-start | bytes 3145736 | tf_op jit(solution)/shard_map/ppermute | solution.py:311
  4.9 7.8 %collective-permute-start.1 = (bf16[4,64,256]{2,1,0:T(8,128)(2,1)S(1)}, bf16[4,64,256]{2,1,0:T(8,128)(2,1)S(1)}, u32[]{:S(2)}, u32[]{:S(2)}) collective-permute-start(bf16[4,64,256]{2,1,0:T(8,128)(2,1)S(1)} %get-tuple-element.33), channel_id=1, source_target_pairs={{0,2},{1,3},{2,0},{3,1},{4,6},{5,7},{6,4},{7,5},{8,10},{9,11},{10,... | collective-permute-start | bytes 393224 | tf_op jit(solution)/shard_map/ppermute | solution.py:311
  7.7 6.6 %collective-permute-start.2 = (bf16[4,64,256]{2,1,0:T(8,128)(2,1)S(1)}, bf16[4,64,256]{2,1,0:T(8,128)(2,1)S(1)}, u32[]{:S(2)}, u32[]{:S(2)}) collective-permute-start(bf16[4,64,256]{2,1,0:T(8,128)(2,1)S(1)} %get-tuple-element.34), channel_id=1, source_target_pairs={{0,1},{1,0},{2,3},{3,2},{4,5},{5,4},{6,7},{7,6},{8,9},{9,8},{10,11... | collective-permute-start | bytes 393224 | tf_op jit(solution)/shard_map/ppermute | solution.py:311
  9.2 7.4 %collective-permute-start.3 = (bf16[4,64,256]{2,1,0:T(8,128)(2,1)S(1)}, bf16[4,64,256]{2,1,0:T(8,128)(2,1)S(1)}, u32[]{:S(2)}, u32[]{:S(2)}) collective-permute-start(bf16[4,64,256]{2,1,0:T(8,128)(2,1)S(1)} %get-tuple-element.35), channel_id=1, source_target_pairs={{0,3},{1,2},{2,1},{3,0},{4,7},{5,6},{6,5},{7,4},{8,11},{9,10},{10,... | collective-permute-start | bytes 393224 | tf_op jit(solution)/shard_map/ppermute | solution.py:311
  9.3 10.3 %collective-permute-start.12 = (bf16[4,64,256]{2,1,0:T(8,128)(2,1)S(1)}, bf16[4,64,256]{2,1,0:T(8,128)(2,1)S(1)}, u32[]{:S(2)}, u32[]{:S(2)}) collective-permute-start(bf16[4,64,256]{2,1,0:T(8,128)(2,1)S(1)} %get-tuple-element.44), channel_id=1, source_target_pairs={{0,2},{1,3},{2,0},{3,1},{4,6},{5,7},{6,4},{7,5},{8,10},{9,11},{10,... | collective-permute-start | bytes 393224 | tf_op jit(solution)/shard_map/ppermute | solution.py:311
  11.2 11.5 %collective-permute-start.13 = (bf16[4,64,256]{2,1,0:T(8,128)(2,1)S(1)}, bf16[4,64,256]{2,1,0:T(8,128)(2,1)S(1)}, u32[]{:S(2)}, u32[]{:S(2)}) collective-permute-start(bf16[4,64,256]{2,1,0:T(8,128)(2,1)S(1)} %get-tuple-element.45), channel_id=1, source_target_pairs={{0,1},{1,0},{2,3},{3,2},{4,5},{5,4},{6,7},{7,6},{8,9},{9,8},{10,11... | collective-permute-start | bytes 393224 | tf_op jit(solution)/shard_map/ppermute | solution.py:311
  12.7 10.0 %collective-permute-start.14 = (bf16[4,64,256]{2,1,0:T(8,128)(2,1)S(1)}, bf16[4,64,256]{2,1,0:T(8,128)(2,1)S(1)}, u32[]{:S(2)}, u32[]{:S(2)}) collective-permute-start(bf16[4,64,256]{2,1,0:T(8,128)(2,1)S(1)} %get-tuple-element.46), channel_id=1, source_target_pairs={{0,3},{1,2},{2,1},{3,0},{4,7},{5,6},{6,5},{7,4},{8,11},{9,10},{10,... | collective-permute-start | bytes 393224 | tf_op jit(solution)/shard_map/ppermute | solution.py:311
  17.9 6.5 %collective-permute-start.6 = (bf16[256,256]{1,0:T(8,128)(2,1)S(1)}, bf16[256,256]{1,0:T(8,128)(2,1)S(1)}, u32[]{:S(2)}, u32[]{:S(2)}) collective-permute-start(bf16[256,256]{1,0:T(8,128)(2,1)S(1)} %get-tuple-element.39), channel_id=1, source_target_pairs={{0,4},{1,5},{2,6},{3,7},{4,0},{5,1},{6,2},{7,3},{8,12},{9,13},{10,... | collective-permute-start | bytes 393224 | tf_op jit(solution)/shard_map/ppermute | solution.py:311
  19.5 10.7 %collective-permute-start.5 = (bf16[256,256]{1,0:T(8,128)(2,1)S(1)}, bf16[256,256]{1,0:T(8,128)(2,1)S(1)}, u32[]{:S(2)}, u32[]{:S(2)}) collective-permute-start(bf16[256,256]{1,0:T(8,128)(2,1)S(1)} %get-tuple-element.37), channel_id=1, source_target_pairs={{0,16},{1,17},{2,18},{3,19},{4,8},{5,9},{6,10},{7,11},{8,4},{9,5},... | collective-permute-start | bytes 393224 | tf_op jit(solution)/shard_map/ppermute | solution.py:311
  19.5 12.1 %collective-permute-start.4 = (bf16[256,256]{1,0:T(8,128)(2,1)S(1)}, bf16[256,256]{1,0:T(8,128)(2,1)S(1)}, u32[]{:S(2)}, u32[]{:S(2)}) collective-permute-start(bf16[256,256]{1,0:T(8,128)(2,1)S(1)} %get-tuple-element.37), channel_id=1, source_target_pairs={{0,4},{1,5},{2,6},{3,7},{4,0},{5,1},{6,2},{7,3},{8,12},{9,13},{10,... | collective-permute-start | bytes 393224 | tf_op jit(solution)/shard_map/ppermute | solution.py:311
  24.0 6.2 %collective-permute-start.17 = (bf16[256,128]{1,0:T(8,128)(2,1)S(1)}, bf16[256,128]{1,0:T(8,128)(2,1)S(1)}, u32[]{:S(2)}, u32[]{:S(2)}) collective-permute-start(bf16[256,128]{1,0:T(8,128)(2,1)S(1)} %get-tuple-element.50), channel_id=1, source_target_pairs={{0,4},{1,5},{2,6},{3,7},{4,0},{5,1},{6,2},{7,3},{8,12},{9,13},{10,... | collective-permute-start | bytes 196616 | tf_op jit(solution)/shard_map/ppermute | solution.py:311
  24.4 10.3 %collective-permute-start.7 = (bf16[256,256]{1,0:T(8,128)(2,1)S(1)}, bf16[256,256]{1,0:T(8,128)(2,1)S(1)}, u32[]{:S(2)}, u32[]{:S(2)}) collective-permute-start(bf16[256,256]{1,0:T(8,128)(2,1)S(1)} %far.3), channel_id=1, source_target_pairs={{0,8},{1,9},{2,10},{3,11},{4,12},{5,13},{6,14},{7,15},{8,0},{9,1},... | collective-permute-start | bytes 393224 | tf_op jit(solution)/shard_map/ppermute | solution.py:311
  27.1 6.5 %collective-permute-start.19 = (bf16[256,128]{1,0:T(8,128)(2,1)S(1)}, bf16[256,128]{1,0:T(8,128)(2,1)S(1)}, u32[]{:S(2)}, u32[]{:S(2)}) collective-permute-start(bf16[256,128]{1,0:T(8,128)(2,1)S(1)} %get-tuple-element.52), channel_id=1, source_target_pairs={{0,4},{1,5},{2,6},{3,7},{4,0},{5,1},{6,2},{7,3},{8,12},{9,13},{10,... | collective-permute-start | bytes 196616 | tf_op jit(solution)/shard_map/ppermute | solution.py:311
  30.2 7.4 %collective-permute-start.16 = (bf16[256,256]{1,0:T(8,128)(2,1)S(1)}, bf16[256,256]{1,0:T(8,128)(2,1)S(1)}, u32[]{:S(2)}, u32[]{:S(2)}) collective-permute-start(bf16[256,256]{1,0:T(8,128)(2,1)S(1)} %get-tuple-element.48), channel_id=1, source_target_pairs={{0,16},{1,17},{2,18},{3,19},{4,8},{5,9},{6,10},{7,11},{8,4},{9,5},... | collective-permute-start | bytes 393224 | tf_op jit(solution)/shard_map/ppermute | solution.py:311
  30.2 7.9 %collective-permute-start.15 = (bf16[256,256]{1,0:T(8,128)(2,1)S(1)}, bf16[256,256]{1,0:T(8,128)(2,1)S(1)}, u32[]{:S(2)}, u32[]{:S(2)}) collective-permute-start(bf16[256,256]{1,0:T(8,128)(2,1)S(1)} %get-tuple-element.48), channel_id=1, source_target_pairs={{0,4},{1,5},{2,6},{3,7},{4,0},{5,1},{6,2},{7,3},{8,12},{9,13},{10,... | collective-permute-start | bytes 393224 | tf_op jit(solution)/shard_map/ppermute | solution.py:311
  31.6 7.7 %collective-permute-start.18 = (bf16[256,128]{1,0:T(8,128)(2,1)S(1)}, bf16[256,128]{1,0:T(8,128)(2,1)S(1)}, u32[]{:S(2)}, u32[]{:S(2)}) collective-permute-start(bf16[256,128]{1,0:T(8,128)(2,1)S(1)} %far.4), channel_id=1, source_target_pairs={{0,8},{1,9},{2,10},{3,11},{4,12},{5,13},{6,14},{7,15},{8,0},{9,1},... | collective-permute-start | bytes 196616 | tf_op jit(solution)/shard_map/ppermute | solution.py:311
  33.7 7.6 %collective-permute-start.20 = (bf16[256,128]{1,0:T(8,128)(2,1)S(1)}, bf16[256,128]{1,0:T(8,128)(2,1)S(1)}, u32[]{:S(2)}, u32[]{:S(2)}) collective-permute-start(bf16[256,128]{1,0:T(8,128)(2,1)S(1)} %far.5), channel_id=1, source_target_pairs={{0,8},{1,9},{2,10},{3,11},{4,12},{5,13},{6,14},{7,15},{8,0},{9,1},... | collective-permute-start | bytes 196616 | tf_op jit(solution)/shard_map/ppermute | solution.py:311
  34.8 6.5 %collective-permute-start.9 = (bf16[128,256]{1,0:T(8,128)(2,1)S(1)}, bf16[128,256]{1,0:T(8,128)(2,1)S(1)}, u32[]{:S(2)}, u32[]{:S(2)}) collective-permute-start(bf16[128,256]{1,0:T(8,128)(2,1)S(1)} %get-tuple-element.42), channel_id=1, source_target_pairs={{0,3},{1,2},{2,1},{3,0},{4,7},{5,6},{6,5},{7,4},{8,11},{9,10},{10,... | collective-permute-start | bytes 196616 | tf_op jit(solution)/shard_map/ppermute | solution.py:311
  37.7 7.3 %collective-permute-start.8 = (bf16[128,256]{1,0:T(8,128)(2,1)S(1)}, bf16[128,256]{1,0:T(8,128)(2,1)S(1)}, u32[]{:S(2)}, u32[]{:S(2)}) collective-permute-start(bf16[128,256]{1,0:T(8,128)(2,1)S(1)} %get-tuple-element.41), channel_id=1, source_target_pairs={{0,2},{1,3},{2,0},{3,1},{4,6},{5,7},{6,4},{7,5},{8,10},{9,11},{10,... | collective-permute-start | bytes 196616 | tf_op jit(solution)/shard_map/ppermute | solution.py:311
  38.2 6.8 %collective-permute-start.10 = (bf16[128,256]{1,0:T(8,128)(2,1)S(1)}, bf16[128,256]{1,0:T(8,128)(2,1)S(1)}, u32[]{:S(2)}, u32[]{:S(2)}) collective-permute-start(bf16[128,256]{1,0:T(8,128)(2,1)S(1)} %get-tuple-element.40.refs_1_), channel_id=1, source_target_pairs={{0,1},{1,0},{2,3},{3,2},{4,5},{5,4},{6,7},{7,6},{8,9},{9,8},{10,11... | collective-permute-start | bytes 196616 | tf_op jit(solution)/shard_map/ppermute | solution.py:311
  41.4 4.6 %collective-permute-start.21 = (bf16[128,256]{1,0:T(8,128)(2,1)S(1)}, bf16[128,256]{1,0:T(8,128)(2,1)S(1)}, u32[]{:S(2)}, u32[]{:S(2)}) collective-permute-start(bf16[128,256]{1,0:T(8,128)(2,1)S(1)} %get-tuple-element.54), channel_id=1, source_target_pairs={{0,2},{1,3},{2,0},{3,1},{4,6},{5,7},{6,4},{7,5},{8,10},{9,11},{10,... | collective-permute-start | bytes 196616 | tf_op jit(solution)/shard_map/ppermute | solution.py:311
  43.2 5.8 %collective-permute-start.22 = (bf16[128,256]{1,0:T(8,128)(2,1)S(1)}, bf16[128,256]{1,0:T(8,128)(2,1)S(1)}, u32[]{:S(2)}, u32[]{:S(2)}) collective-permute-start(bf16[128,256]{1,0:T(8,128)(2,1)S(1)} %get-tuple-element.55), channel_id=1, source_target_pairs={{0,3},{1,2},{2,1},{3,0},{4,7},{5,6},{6,5},{7,4},{8,11},{9,10},{10,... | collective-permute-start | bytes 196616 | tf_op jit(solution)/shard_map/ppermute | solution.py:311
  44.7 4.9 %copy-start.1 = (bf16[4,1024,512]{2,1,0:T(8,128)(2,1)S(1)}, bf16[4,1024,512]{2,1,0:T(8,128)(2,1)}, u32[]{:S(2)}) copy-start(bf16[4,1024,512]{2,1,0:T(8,128)(2,1)} %refs_2_.2) | copy-start | bytes 12582916
  44.7 4.9 %copy-start.2 = (s32[1,4]{1,0:T(1,128)S(1)}, s32[1,4]{1,0:T(1,128)}, u32[]{:S(2)}) copy-start(s32[1,4]{1,0:T(1,128)} %refs_0_.7) | copy-start | bytes 52
  44.7 4.9 %copy-start.3 = (s32[16]{0:T(128)S(1)}, s32[16]{0:T(128)}, u32[]{:S(2)}) copy-start(s32[16]{0:T(128)} %refs_1_.1) | copy-start | bytes 196
  44.7 4.3 %collective-permute-start.23 = (bf16[128,256]{1,0:T(8,128)(2,1)S(1)}, bf16[128,256]{1,0:T(8,128)(2,1)S(1)}, u32[]{:S(2)}, u32[]{:S(2)}) collective-permute-start(bf16[128,256]{1,0:T(8,128)(2,1)S(1)} %get-tuple-element.53.refs_1_), channel_id=1, source_target_pairs={{0,1},{1,0},{2,3},{3,2},{4,5},{5,4},{6,7},{7,6},{8,9},{9,8},{10,11... | collective-permute-start | bytes 196616 | tf_op jit(solution)/shard_map/ppermute | solution.py:311
  45.4 4.2 %collective-permute-start.11 = (bf16[128,1024]{1,0:T(8,128)(2,1)S(1)}, bf16[128,1024]{1,0:T(8,128)(2,1)S(1)}, u32[]{:S(2)}, u32[]{:S(2)}) collective-permute-start(bf16[128,1024]{1,0:T(8,128)(2,1)S(1)} %phase.2.refs_3_), channel_id=1, source_target_pairs={{0,16},{1,17},{2,18},{3,19},{4,20},{5,21},{6,22},{7,23},{8,24},{9,... | collective-permute-start | bytes 786440 | tf_op jit(solution)/shard_map/ppermute | solution.py:311
  49.5 1.6 %collective-permute-start.24 = (bf16[128,1024]{1,0:T(8,128)(2,1)S(1)}, bf16[128,1024]{1,0:T(8,128)(2,1)S(1)}, u32[]{:S(2)}, u32[]{:S(2)}) collective-permute-start(bf16[128,1024]{1,0:T(8,128)(2,1)S(1)} %phase.3.refs_5_), channel_id=1, source_target_pairs={{0,16},{1,17},{2,18},{3,19},{4,20},{5,21},{6,22},{7,23},{8,24},{9,... | collective-permute-start | bytes 786440 | tf_op jit(solution)/shard_map/ppermute | solution.py:311

commit v27 on v21

--- a/solution.py
+++ b/solution.py
@@ -373,7 +373,8 @@
             name="far",
         )(*earlier, third, near)
         far = sent(message, to_plane(2))
-        sums.append([ours, far, near, sent(second, from_ends), sent(second, to_middle)])
+        to_next = from_ends if sums else to_plane(1)
+        sums.append([ours, far, near, sent(second, to_next), sent(second, to_middle)])
 
     phases = []
     for chunk in range(own):

time: 52 us -> 51.7 us (level)
  starting transfers between devices: 30.8 us -> 29.8 us
  waiting for transfers between devices: 10.1 us -> 10.9 us
    ppermute x23, starting transfers between devices: 30.8 us -> 29.8 us  [sent(): return lax.ppermute(value, ('dist', 'rows'), pairs)]
    ppermute x23, waiting for transfers between devices: 10.1 us -> 10.9 us  [sent(): return lax.ppermute(value, ('dist', 'rows'), pairs)]
where the time goes in v27:
time: 51.7 us; the launch traced here: 51.5 us
  starting transfers between devices  29.8 us (58%)
  waiting for transfers between devices  10.9 us (21%)
  Pallas kernels  10.6 us (21%)
    ppermute x23, starting transfers between devices, sent(): return lax.ppermute(value, ('dist', 'rows'), pairs)  29.8 us
    ppermute x23, waiting for transfers between devices, sent(): return lax.ppermute(value, ('dist', 'rows'), pairs)  10.9 us
    pallas_call x1, Pallas kernels, plane_plan(): pl.pallas_call(lambda *refs: filter_kernel(inner, dist_dev, *refs), out_s...  2.62 us
    pallas_call x2, Pallas kernels, plane_plan(): pl.pallas_call(lambda *refs: column_kernel(inner, outer, *refs), out_shap...  2.59 us
    pallas_call x1, Pallas kernels, plane_plan(): pl.pallas_call(lambda *refs: row_kernel(inner, *refs), out_shape=[shaped(...  1.83 us
    pallas_call x1, Pallas kernels, plane_plan(): pl.pallas_call(lambda *refs: recon_kernel(own, *refs), out_shape=[jax.Sha...  1.2 us
    pallas_call x1, Pallas kernels, plane_plan(): pl.pallas_call(recon_last_kernel, out_shape=shaped(capacity, pixels), in_...  1.12 us
  transfers between devices with their start and end apart: 23, of which 7 were waited for; matrix products, arithmetic and copies ran while one was open for 0% of the time, Pallas kernels for 15%

profile of v27, /device:TPU:0, one launch (start us, length us, event | category | flops | bytes accessed | tf_op | source)
XLA Modules:
  0.0 51.5 jit_solution(18224347893388984163)
XLA Ops:
  0.0 0.0 copy-start
  0.0 0.5 collective-permute-start
  0.5 2.6 %filters.1.refs_3_.refs_1_ = bf16[4,1024,256]{2,1,0:T(8,128)(2,1)S(1)} custom-call(f32[4]{0:T(128)} %refs_0_.6), custom_call_target="tpu_custom_call" | custom-call | flops 1 | bytes 1 | tf_op jit(solution)/shard_map/filters/pallas_call | solution.py:321
  3.1 0.0 collective-permute-done.refs_1_
  3.1 0.0 copy-done
  3.1 1.8 %row_spectra.1 = (bf16[4,64,256]{2,1,0:T(8,128)(2,1)S(1)}, bf16[4,64,256]{2,1,0:T(8,128)(2,1)S(1)}, bf16[4,64,256]{2,1,0:T(8,128)(2,1)S(1)}, bf16[4,64,256]{2,1,...) custom-call(bf16[4,2,64,1024]{3,2,1,0:T(8,128)(2,1)} %bitcast.2, ...), custom_call_target="tpu_custom_call" | custom-call | flops 1 | bytes 1 | tf_op jit(solution)/shard_map/row_spectra/pallas_call | solution.py:330
  4.9 2.8 %collective-permute-start.1 = (bf16[4,64,256]{2,1,0:T(8,128)(2,1)S(1)}, bf16[4,64,256]{2,1,0:T(8,128)(2,1)S(1)}, u32[]{:S(2)}, u32[]{:S(2)}) collective-permute-start(bf16[4,64,256]{2,1,0:T(8,128)(2,1)S(1)} %get-tuple-element.31), channel_id=1, source_target_pairs={{0,2},{1,3},{2,0},{3,1},{4,6},{5,7},{6,4},{7,5},{8,10},{9,11},{10,... | collective-permute-start | bytes 393224 | tf_op jit(solution)/shard_map/ppermute | solution.py:298
  7.7 1.5 %collective-permute-start.2 = (bf16[4,64,256]{2,1,0:T(8,128)(2,1)S(1)}, bf16[4,64,256]{2,1,0:T(8,128)(2,1)S(1)}, u32[]{:S(2)}, u32[]{:S(2)}) collective-permute-start(bf16[4,64,256]{2,1,0:T(8,128)(2,1)S(1)} %get-tuple-element.32), channel_id=1, source_target_pairs={{0,1},{1,0},{2,3},{3,2},{4,5},{5,4},{6,7},{7,6},{8,9},{9,8},{10,11... | collective-permute-start | bytes 393224 | tf_op jit(solution)/shard_map/ppermute | solution.py:298
  9.2 0.0 collective-permute-start.3
  9.3 1.9 %collective-permute-start.12 = (bf16[4,64,256]{2,1,0:T(8,128)(2,1)S(1)}, bf16[4,64,256]{2,1,0:T(8,128)(2,1)S(1)}, u32[]{:S(2)}, u32[]{:S(2)}) collective-permute-start(bf16[4,64,256]{2,1,0:T(8,128)(2,1)S(1)} %get-tuple-element.42), channel_id=1, source_target_pairs={{0,2},{1,3},{2,0},{3,1},{4,6},{5,7},{6,4},{7,5},{8,10},{9,11},{10,... | collective-permute-start | bytes 393224 | tf_op jit(solution)/shard_map/ppermute | solution.py:298
  11.2 1.5 %collective-permute-start.13 = (bf16[4,64,256]{2,1,0:T(8,128)(2,1)S(1)}, bf16[4,64,256]{2,1,0:T(8,128)(2,1)S(1)}, u32[]{:S(2)}, u32[]{:S(2)}) collective-permute-start(bf16[4,64,256]{2,1,0:T(8,128)(2,1)S(1)} %get-tuple-element.43), channel_id=1, source_target_pairs={{0,1},{1,0},{2,3},{3,2},{4,5},{5,4},{6,7},{7,6},{8,9},{9,8},{10,11... | collective-permute-start | bytes 393224 | tf_op jit(solution)/shard_map/ppermute | solution.py:298
  12.7 0.0 collective-permute-done.1.refs_3_
  12.7 1.6 %collective-permute-start.14 = (bf16[4,64,256]{2,1,0:T(8,128)(2,1)S(1)}, bf16[4,64,256]{2,1,0:T(8,128)(2,1)S(1)}, u32[]{:S(2)}, u32[]{:S(2)}) collective-permute-start(bf16[4,64,256]{2,1,0:T(8,128)(2,1)S(1)} %get-tuple-element.44), channel_id=1, source_target_pairs={{0,3},{1,2},{2,1},{3,0},{4,7},{5,6},{6,5},{7,4},{8,11},{9,10},{10,... | collective-permute-start | bytes 393224 | tf_op jit(solution)/shard_map/ppermute | solution.py:298
  14.3 0.0 collective-permute-done.2.refs_4_
  14.3 2.3 %collective-permute-done.3.refs_5_ = bf16[4,64,256]{2,1,0:T(8,128)(2,1)S(1)} collective-permute-done((bf16[4,64,256]{2,1,0:T(8,128)(2,1)S(1)}, bf16[4,64,256]{2,1,0:T(8,128)(2,1)S(1)}, u32[]{:S(2)}, u32[]{:S(2)}) %collective-permute-start.3) | collective-permute-done | bytes 131104 | tf_op jit(solution)/shard_map/ppermute | solution.py:298
  16.6 1.3 %columns.2 = (bf16[256,256]{1,0:T(8,128)(2,1)S(1)}, bf16[256,256]{1,0:T(8,128)(2,1)S(1)}, bf16[256,256]{1,0:T(8,128)(2,1)S(1)}, bf16[256,256]{1,0:T(8,128)(2,1)S(1)}) custom-call(bf16[1024,1024]{1,0:T(8,128)(2,1)S(1)} %copy-done, bf16[4,1024,256]{2,1,0:T(8,128)(2,1)S(1)} %filters.1.refs_3_.refs_1_, bf16[4,64,256]{2,1,0:T(8,128)(2,1)S(1)} %get-tuple-element.30.refs_2_, ...), custom_call_target="tpu_custom_call" | custom-call | flops 1 | bytes 1 | tf_op jit(solution)/shard_map/columns/pallas_call | solution.py:349
  17.9 1.6 %collective-permute-start.4 = (bf16[256,256]{1,0:T(8,128)(2,1)S(1)}, bf16[256,256]{1,0:T(8,128)(2,1)S(1)}, u32[]{:S(2)}, u32[]{:S(2)}) collective-permute-start(bf16[256,256]{1,0:T(8,128)(2,1)S(1)} %get-tuple-element.36), channel_id=1, source_target_pairs={{0,4},{1,5},{2,6},{3,7},{4,0},{5,1},{6,2},{7,3},{8,12},{9,13},{10,... | collective-permute-start | bytes 393224 | tf_op jit(solution)/shard_map/ppermute | solution.py:298
  19.5 0.0 collective-permute-start.7
  19.5 0.0 collective-permute-done.12.refs_3_
  19.5 3.2 %collective-permute-start.6 = (bf16[256,256]{1,0:T(8,128)(2,1)S(1)}, bf16[256,256]{1,0:T(8,128)(2,1)S(1)}, u32[]{:S(2)}, u32[]{:S(2)}) collective-permute-start(bf16[256,256]{1,0:T(8,128)(2,1)S(1)} %get-tuple-element.37), channel_id=1, source_target_pairs={{0,4},{1,5},{2,6},{3,7},{4,0},{5,1},{6,2},{7,3},{8,12},{9,13},{10,... | collective-permute-start | bytes 393224 | tf_op jit(solution)/shard_map/ppermute | solution.py:298
  22.7 0.0 collective-permute-done.13.refs_4_
  22.7 0.0 collective-permute-done.14.refs_5_
  22.7 1.3 %columns.3 = (bf16[256,256]{1,0:T(8,128)(2,1)S(1)}, bf16[256,256]{1,0:T(8,128)(2,1)S(1)}, bf16[256,256]{1,0:T(8,128)(2,1)S(1)}, bf16[256,256]{1,0:T(8,128)(2,1)S(1)}) custom-call(bf16[1024,1024]{1,0:T(8,128)(2,1)S(1)} %copy-done, bf16[4,1024,256]{2,1,0:T(8,128)(2,1)S(1)} %filters.1.refs_3_.refs_1_, bf16[4,64,256]{2,1,0:T(8,128)(2,1)S(1)} %get-tuple-element.41.refs_2_, ...), custom_call_target="tpu_custom_call" | custom-call | flops 1 | bytes 1 | tf_op jit(solution)/shard_map/columns/pallas_call | solution.py:349
  24.0 0.4 collective-permute-start.15
  24.4 0.0 collective-permute-done.4.refs_1_.refs_2_
  24.4 0.1 far.2
  24.4 2.7 %collective-permute-start.5 = (bf16[256,256]{1,0:T(8,128)(2,1)S(1)}, bf16[256,256]{1,0:T(8,128)(2,1)S(1)}, u32[]{:S(2)}, u32[]{:S(2)}) collective-permute-start(bf16[256,256]{1,0:T(8,128)(2,1)S(1)} %far.2), channel_id=1, source_target_pairs={{0,8},{1,9},{2,10},{3,11},{4,12},{5,13},{6,14},{7,15},{8,0},{9,1},... | collective-permute-start | bytes 393224 | tf_op jit(solution)/shard_map/ppermute | solution.py:298
  27.1 0.0 collective-permute-start.18
  27.1 0.0 collective-permute-done.7.refs_4_.refs_1_
  27.1 3.4 %collective-permute-start.17 = (bf16[256,256]{1,0:T(8,128)(2,1)S(1)}, bf16[256,256]{1,0:T(8,128)(2,1)S(1)}, u32[]{:S(2)}, u32[]{:S(2)}) collective-permute-start(bf16[256,256]{1,0:T(8,128)(2,1)S(1)} %get-tuple-element.48), channel_id=1, source_target_pairs={{0,4},{1,5},{2,6},{3,7},{12,8},{13,9},{14,10},{15,11},{16,20},{17,... | collective-permute-start | bytes 393224 | tf_op jit(solution)/shard_map/ppermute | solution.py:298
  30.5 0.0 collective-permute-done.6.refs_3_.refs_0_
  30.5 0.0 collective-permute-done.15.refs_3_.refs_2_
  30.5 0.1 far.3
  30.6 1.4 %collective-permute-start.16 = (bf16[256,256]{1,0:T(8,128)(2,1)S(1)}, bf16[256,256]{1,0:T(8,128)(2,1)S(1)}, u32[]{:S(2)}, u32[]{:S(2)}) collective-permute-start(bf16[256,256]{1,0:T(8,128)(2,1)S(1)} %far.3), channel_id=1, source_target_pairs={{0,8},{1,9},{2,10},{3,11},{4,12},{5,13},{6,14},{7,15},{8,0},{9,1},... | collective-permute-start | bytes 393224 | tf_op jit(solution)/shard_map/ppermute | solution.py:298
  32.0 2.6 %collective-permute-done.5.refs_1_ = bf16[256,256]{1,0:T(8,128)(2,1)S(1)} collective-permute-done((bf16[256,256]{1,0:T(8,128)(2,1)S(1)}, bf16[256,256]{1,0:T(8,128)(2,1)S(1)}, u32[]{:S(2)}, u32[]{:S(2)}) %collective-permute-start.5) | collective-permute-done | bytes 131104 | tf_op jit(solution)/shard_map/ppermute | solution.py:298
  34.6 0.1 half.2
  34.7 0.1 collective-permute-start.8
  34.8 1.4 %collective-permute-start.9 = (bf16[128,256]{1,0:T(8,128)(2,1)S(1)}, bf16[128,256]{1,0:T(8,128)(2,1)S(1)}, u32[]{:S(2)}, u32[]{:S(2)}) collective-permute-start(bf16[128,256]{1,0:T(8,128)(2,1)S(1)} %get-tuple-element.40), channel_id=1, source_target_pairs={{0,3},{1,2},{2,1},{3,0},{4,7},{5,6},{6,5},{7,4},{8,11},{9,10},{10,... | collective-permute-start | bytes 196616 | tf_op jit(solution)/shard_map/ppermute | solution.py:298
  36.2 0.0 collective-permute-done.18.refs_4_
  36.2 2.1 %collective-permute-start.10 = (bf16[128,256]{1,0:T(8,128)(2,1)S(1)}, bf16[128,256]{1,0:T(8,128)(2,1)S(1)}, u32[]{:S(2)}, u32[]{:S(2)}) collective-permute-start(bf16[128,256]{1,0:T(8,128)(2,1)S(1)} %get-tuple-element.38.refs_1_), channel_id=1, source_target_pairs={{0,1},{1,0},{2,3},{3,2},{4,5},{5,4},{6,7},{7,6},{8,9},{9,8},{10,11... | collective-permute-start | bytes 196616 | tf_op jit(solution)/shard_map/ppermute | solution.py:298
  38.3 0.0 collective-permute-done.17.refs_3_
  38.3 2.8 %collective-permute-done.16.refs_1_ = bf16[256,256]{1,0:T(8,128)(2,1)S(1)} collective-permute-done((bf16[256,256]{1,0:T(8,128)(2,1)S(1)}, bf16[256,256]{1,0:T(8,128)(2,1)S(1)}, u32[]{:S(2)}, u32[]{:S(2)}) %collective-permute-start.16) | collective-permute-done | bytes 131104 | tf_op jit(solution)/shard_map/ppermute | solution.py:298
  41.1 0.1 half.3
  41.2 1.3 %collective-permute-start.19 = (bf16[128,256]{1,0:T(8,128)(2,1)S(1)}, bf16[128,256]{1,0:T(8,128)(2,1)S(1)}, u32[]{:S(2)}, u32[]{:S(2)}) collective-permute-start(bf16[128,256]{1,0:T(8,128)(2,1)S(1)} %get-tuple-element.50), channel_id=1, source_target_pairs={{0,2},{1,3},{2,0},{3,1},{4,6},{5,7},{6,4},{7,5},{8,10},{9,11},{10,... | collective-permute-start | bytes 196616 | tf_op jit(solution)/shard_map/ppermute | solution.py:298
  42.6 1.4 %collective-permute-start.20 = (bf16[128,256]{1,0:T(8,128)(2,1)S(1)}, bf16[128,256]{1,0:T(8,128)(2,1)S(1)}, u32[]{:S(2)}, u32[]{:S(2)}) collective-permute-start(bf16[128,256]{1,0:T(8,128)(2,1)S(1)} %get-tuple-element.51), channel_id=1, source_target_pairs={{0,3},{1,2},{2,1},{3,0},{4,7},{5,6},{6,5},{7,4},{8,11},{9,10},{10,... | collective-permute-start | bytes 196616 | tf_op jit(solution)/shard_map/ppermute | solution.py:298
  44.0 0.0 collective-permute-done.8.refs_2_
  44.0 0.0 copy-start.1
  44.0 0.8 %collective-permute-start.21 = (bf16[128,256]{1,0:T(8,128)(2,1)S(1)}, bf16[128,256]{1,0:T(8,128)(2,1)S(1)}, u32[]{:S(2)}, u32[]{:S(2)}) collective-permute-start(bf16[128,256]{1,0:T(8,128)(2,1)S(1)} %get-tuple-element.49.refs_1_), channel_id=1, source_target_pairs={{0,1},{1,0},{2,3},{3,2},{4,5},{5,4},{6,7},{7,6},{8,9},{9,8},{10,11... | collective-permute-start | bytes 196616 | tf_op jit(solution)/shard_map/ppermute | solution.py:298
  44.9 0.0 collective-permute-done.9.refs_3_
  44.9 0.0 collective-permute-done.10.refs_4_
  44.9 0.5 phase.2.refs_3_
  45.3 0.1 collective-permute-start.11
  45.4 0.1 collective-permute-done.19.refs_2_
  45.5 2.2 %collective-permute-done.20.refs_3_ = bf16[128,256]{1,0:T(8,128)(2,1)S(1)} collective-permute-done((bf16[128,256]{1,0:T(8,128)(2,1)S(1)}, bf16[128,256]{1,0:T(8,128)(2,1)S(1)}, u32[]{:S(2)}, u32[]{:S(2)}) %collective-permute-start.20) | collective-permute-done | bytes 65568 | tf_op jit(solution)/shard_map/ppermute | solution.py:298
  47.7 0.6 %collective-permute-done.21.refs_4_ = bf16[128,256]{1,0:T(8,128)(2,1)S(1)} collective-permute-done((bf16[128,256]{1,0:T(8,128)(2,1)S(1)}, bf16[128,256]{1,0:T(8,128)(2,1)S(1)}, u32[]{:S(2)}, u32[]{:S(2)}) %collective-permute-start.21) | collective-permute-done | bytes 65568 | tf_op jit(solution)/shard_map/ppermute | solution.py:298
  48.3 0.5 phase.3.refs_5_
  48.8 0.1 collective-permute-start.22
  48.9 0.0 collective-permute-done.11.refs_4_
  48.9 0.0 copy-done.1
  48.9 0.0 copy-done.2
  48.9 0.0 copy-done.3
  48.9 1.2 %recon.2 = (f32[128,512]{1,0:T(8,128)S(1)}, bf16[1024,512]{1,0:T(8,128)(2,1)S(1)}, bf16[128,128]{1,0:T(8,128)(2,1)S(1)}) custom-call(s32[1,4]{1,0:T(1,128)S(1)} %copy-done.2, s32[16]{0:T(128)S(1)} %copy-done.3, bf16[4,1024,512]{2,1,0:T(8,128)(2,1)S(1)} %copy-done.1, bf16[128,1024]{1,0:T(8,128)(2,1)S(1)} %phase.2.refs_3_, ...), custom_call_target="tpu_custom_call" | custom-call | flops 1 | bytes 1 | tf_op jit(solution)/shard_map/recon/pallas_call | solution.py:403
  50.1 0.3 collective-permute-done.22.phase
  50.4 1.1 %recon.3 = bf16[128,512]{1,0:T(8,128)(2,1)} custom-call(bf16[1024,512]{1,0:T(8,128)(2,1)S(1)} %get-tuple-element.52.weights, bf16[128,1024]{1,0:T(8,128)(2,1)S(1)} %collective-permute-done.22.phase, f32[128,512]{1,0:T(8,128)S(1)} %get-tuple-element.53.before, bf16[128,128]{1,0:T(8,128)(2,1)S(1)} %get-tuple-element.54.select), custom_call_target="tpu_custom_call" | custom-call | flops 1 | bytes 1 | tf_op jit(solution)/shard_map/recon/pallas_call | solution.py:416
  (2 shorter events, 0.0 us)
Async XLA Ops:
  0.0 3.1 %copy-start = (bf16[1024,1024]{1,0:T(8,128)(2,1)S(1)}, bf16[1024,1024]{1,0:T(8,128)(2,1)}, u32[]{:S(2)}) copy-start(bf16[1024,1024]{1,0:T(8,128)(2,1)} %constant.2.clone.refs_2_.refs_0_) | copy-start | bytes 6291460
  0.0 3.1 %collective-permute-start = (bf16[4,2,64,1024]{3,2,1,0:T(8,128)(2,1)}, bf16[4,2,64,1024]{3,2,1,0:T(8,128)(2,1)S(1)}, u32[]{:S(2)}, u32[]{:S(2)}) collective-permute-start(bf16[4,2,64,1024]{3,2,1,0:T(8,128)(2,1)} %bitcast.1), channel_id=1, source_target_pairs={{0,16},{1,17},{2,18},{3,19},{4,20},{5,21},{6,22},{7,23},{8,24},{9,... | collective-permute-start | bytes 3145736 | tf_op jit(solution)/shard_map/ppermute | solution.py:298
  4.9 7.8 %collective-permute-start.1 = (bf16[4,64,256]{2,1,0:T(8,128)(2,1)S(1)}, bf16[4,64,256]{2,1,0:T(8,128)(2,1)S(1)}, u32[]{:S(2)}, u32[]{:S(2)}) collective-permute-start(bf16[4,64,256]{2,1,0:T(8,128)(2,1)S(1)} %get-tuple-element.31), channel_id=1, source_target_pairs={{0,2},{1,3},{2,0},{3,1},{4,6},{5,7},{6,4},{7,5},{8,10},{9,11},{10,... | collective-permute-start | bytes 393224 | tf_op jit(solution)/shard_map/ppermute | solution.py:298
  7.7 6.6 %collective-permute-start.2 = (bf16[4,64,256]{2,1,0:T(8,128)(2,1)S(1)}, bf16[4,64,256]{2,1,0:T(8,128)(2,1)S(1)}, u32[]{:S(2)}, u32[]{:S(2)}) collective-permute-start(bf16[4,64,256]{2,1,0:T(8,128)(2,1)S(1)} %get-tuple-element.32), channel_id=1, source_target_pairs={{0,1},{1,0},{2,3},{3,2},{4,5},{5,4},{6,7},{7,6},{8,9},{9,8},{10,11... | collective-permute-start | bytes 393224 | tf_op jit(solution)/shard_map/ppermute | solution.py:298
  9.2 7.4 %collective-permute-start.3 = (bf16[4,64,256]{2,1,0:T(8,128)(2,1)S(1)}, bf16[4,64,256]{2,1,0:T(8,128)(2,1)S(1)}, u32[]{:S(2)}, u32[]{:S(2)}) collective-permute-start(bf16[4,64,256]{2,1,0:T(8,128)(2,1)S(1)} %get-tuple-element.33), channel_id=1, source_target_pairs={{0,3},{1,2},{2,1},{3,0},{4,7},{5,6},{6,5},{7,4},{8,11},{9,10},{10,... | collective-permute-start | bytes 393224 | tf_op jit(solution)/shard_map/ppermute | solution.py:298
  9.3 10.3 %collective-permute-start.12 = (bf16[4,64,256]{2,1,0:T(8,128)(2,1)S(1)}, bf16[4,64,256]{2,1,0:T(8,128)(2,1)S(1)}, u32[]{:S(2)}, u32[]{:S(2)}) collective-permute-start(bf16[4,64,256]{2,1,0:T(8,128)(2,1)S(1)} %get-tuple-element.42), channel_id=1, source_target_pairs={{0,2},{1,3},{2,0},{3,1},{4,6},{5,7},{6,4},{7,5},{8,10},{9,11},{10,... | collective-permute-start | bytes 393224 | tf_op jit(solution)/shard_map/ppermute | solution.py:298
  11.2 11.5 %collective-permute-start.13 = (bf16[4,64,256]{2,1,0:T(8,128)(2,1)S(1)}, bf16[4,64,256]{2,1,0:T(8,128)(2,1)S(1)}, u32[]{:S(2)}, u32[]{:S(2)}) collective-permute-start(bf16[4,64,256]{2,1,0:T(8,128)(2,1)S(1)} %get-tuple-element.43), channel_id=1, source_target_pairs={{0,1},{1,0},{2,3},{3,2},{4,5},{5,4},{6,7},{7,6},{8,9},{9,8},{10,11... | collective-permute-start | bytes 393224 | tf_op jit(solution)/shard_map/ppermute | solution.py:298
  12.7 10.0 %collective-permute-start.14 = (bf16[4,64,256]{2,1,0:T(8,128)(2,1)S(1)}, bf16[4,64,256]{2,1,0:T(8,128)(2,1)S(1)}, u32[]{:S(2)}, u32[]{:S(2)}) collective-permute-start(bf16[4,64,256]{2,1,0:T(8,128)(2,1)S(1)} %get-tuple-element.44), channel_id=1, source_target_pairs={{0,3},{1,2},{2,1},{3,0},{4,7},{5,6},{6,5},{7,4},{8,11},{9,10},{10,... | collective-permute-start | bytes 393224 | tf_op jit(solution)/shard_map/ppermute | solution.py:298
  17.9 6.5 %collective-permute-start.4 = (bf16[256,256]{1,0:T(8,128)(2,1)S(1)}, bf16[256,256]{1,0:T(8,128)(2,1)S(1)}, u32[]{:S(2)}, u32[]{:S(2)}) collective-permute-start(bf16[256,256]{1,0:T(8,128)(2,1)S(1)} %get-tuple-element.36), channel_id=1, source_target_pairs={{0,4},{1,5},{2,6},{3,7},{4,0},{5,1},{6,2},{7,3},{8,12},{9,13},{10,... | collective-permute-start | bytes 393224 | tf_op jit(solution)/shard_map/ppermute | solution.py:298
  19.5 7.6 %collective-permute-start.7 = (bf16[256,256]{1,0:T(8,128)(2,1)S(1)}, bf16[256,256]{1,0:T(8,128)(2,1)S(1)}, u32[]{:S(2)}, u32[]{:S(2)}) collective-permute-start(bf16[256,256]{1,0:T(8,128)(2,1)S(1)} %get-tuple-element.37), channel_id=1, source_target_pairs={{0,16},{1,17},{2,18},{3,19},{4,8},{5,9},{6,10},{7,11},{8,4},{9,5},... | collective-permute-start | bytes 393224 | tf_op jit(solution)/shard_map/ppermute | solution.py:298
  19.5 11.0 %collective-permute-start.6 = (bf16[256,256]{1,0:T(8,128)(2,1)S(1)}, bf16[256,256]{1,0:T(8,128)(2,1)S(1)}, u32[]{:S(2)}, u32[]{:S(2)}) collective-permute-start(bf16[256,256]{1,0:T(8,128)(2,1)S(1)} %get-tuple-element.37), channel_id=1, source_target_pairs={{0,4},{1,5},{2,6},{3,7},{4,0},{5,1},{6,2},{7,3},{8,12},{9,13},{10,... | collective-permute-start | bytes 393224 | tf_op jit(solution)/shard_map/ppermute | solution.py:298
  24.0 6.5 %collective-permute-start.15 = (bf16[256,256]{1,0:T(8,128)(2,1)S(1)}, bf16[256,256]{1,0:T(8,128)(2,1)S(1)}, u32[]{:S(2)}, u32[]{:S(2)}) collective-permute-start(bf16[256,256]{1,0:T(8,128)(2,1)S(1)} %get-tuple-element.47), channel_id=1, source_target_pairs={{0,4},{1,5},{2,6},{3,7},{4,0},{5,1},{6,2},{7,3},{8,12},{9,13},{10,... | collective-permute-start | bytes 393224 | tf_op jit(solution)/shard_map/ppermute | solution.py:298
  24.4 10.2 %collective-permute-start.5 = (bf16[256,256]{1,0:T(8,128)(2,1)S(1)}, bf16[256,256]{1,0:T(8,128)(2,1)S(1)}, u32[]{:S(2)}, u32[]{:S(2)}) collective-permute-start(bf16[256,256]{1,0:T(8,128)(2,1)S(1)} %far.2), channel_id=1, source_target_pairs={{0,8},{1,9},{2,10},{3,11},{4,12},{5,13},{6,14},{7,15},{8,0},{9,1},... | collective-permute-start | bytes 393224 | tf_op jit(solution)/shard_map/ppermute | solution.py:298
  27.1 9.1 %collective-permute-start.18 = (bf16[256,256]{1,0:T(8,128)(2,1)S(1)}, bf16[256,256]{1,0:T(8,128)(2,1)S(1)}, u32[]{:S(2)}, u32[]{:S(2)}) collective-permute-start(bf16[256,256]{1,0:T(8,128)(2,1)S(1)} %get-tuple-element.48), channel_id=1, source_target_pairs={{0,16},{1,17},{2,18},{3,19},{4,8},{5,9},{6,10},{7,11},{8,4},{9,5},... | collective-permute-start | bytes 393224 | tf_op jit(solution)/shard_map/ppermute | solution.py:298
  27.1 11.2 %collective-permute-start.17 = (bf16[256,256]{1,0:T(8,128)(2,1)S(1)}, bf16[256,256]{1,0:T(8,128)(2,1)S(1)}, u32[]{:S(2)}, u32[]{:S(2)}) collective-permute-start(bf16[256,256]{1,0:T(8,128)(2,1)S(1)} %get-tuple-element.48), channel_id=1, source_target_pairs={{0,4},{1,5},{2,6},{3,7},{12,8},{13,9},{14,10},{15,11},{16,20},{17,... | collective-permute-start | bytes 393224 | tf_op jit(solution)/shard_map/ppermute | solution.py:298
  30.6 10.5 %collective-permute-start.16 = (bf16[256,256]{1,0:T(8,128)(2,1)S(1)}, bf16[256,256]{1,0:T(8,128)(2,1)S(1)}, u32[]{:S(2)}, u32[]{:S(2)}) collective-permute-start(bf16[256,256]{1,0:T(8,128)(2,1)S(1)} %far.3), channel_id=1, source_target_pairs={{0,8},{1,9},{2,10},{3,11},{4,12},{5,13},{6,14},{7,15},{8,0},{9,1},... | collective-permute-start | bytes 393224 | tf_op jit(solution)/shard_map/ppermute | solution.py:298
  34.7 9.2 %collective-permute-start.8 = (bf16[128,256]{1,0:T(8,128)(2,1)S(1)}, bf16[128,256]{1,0:T(8,128)(2,1)S(1)}, u32[]{:S(2)}, u32[]{:S(2)}) collective-permute-start(bf16[128,256]{1,0:T(8,128)(2,1)S(1)} %get-tuple-element.39), channel_id=1, source_target_pairs={{0,2},{1,3},{2,0},{3,1},{4,6},{5,7},{6,4},{7,5},{8,10},{9,11},{10,... | collective-permute-start | bytes 196616 | tf_op jit(solution)/shard_map/ppermute | solution.py:298
  34.8 10.0 %collective-permute-start.9 = (bf16[128,256]{1,0:T(8,128)(2,1)S(1)}, bf16[128,256]{1,0:T(8,128)(2,1)S(1)}, u32[]{:S(2)}, u32[]{:S(2)}) collective-permute-start(bf16[128,256]{1,0:T(8,128)(2,1)S(1)} %get-tuple-element.40), channel_id=1, source_target_pairs={{0,3},{1,2},{2,1},{3,0},{4,7},{5,6},{6,5},{7,4},{8,11},{9,10},{10,... | collective-permute-start | bytes 196616 | tf_op jit(solution)/shard_map/ppermute | solution.py:298
  36.2 8.6 %collective-permute-start.10 = (bf16[128,256]{1,0:T(8,128)(2,1)S(1)}, bf16[128,256]{1,0:T(8,128)(2,1)S(1)}, u32[]{:S(2)}, u32[]{:S(2)}) collective-permute-start(bf16[128,256]{1,0:T(8,128)(2,1)S(1)} %get-tuple-element.38.refs_1_), channel_id=1, source_target_pairs={{0,1},{1,0},{2,3},{3,2},{4,5},{5,4},{6,7},{7,6},{8,9},{9,8},{10,11... | collective-permute-start | bytes 196616 | tf_op jit(solution)/shard_map/ppermute | solution.py:298
  41.2 4.3 %collective-permute-start.19 = (bf16[128,256]{1,0:T(8,128)(2,1)S(1)}, bf16[128,256]{1,0:T(8,128)(2,1)S(1)}, u32[]{:S(2)}, u32[]{:S(2)}) collective-permute-start(bf16[128,256]{1,0:T(8,128)(2,1)S(1)} %get-tuple-element.50), channel_id=1, source_target_pairs={{0,2},{1,3},{2,0},{3,1},{4,6},{5,7},{6,4},{7,5},{8,10},{9,11},{10,... | collective-permute-start | bytes 196616 | tf_op jit(solution)/shard_map/ppermute | solution.py:298
  42.6 5.2 %collective-permute-start.20 = (bf16[128,256]{1,0:T(8,128)(2,1)S(1)}, bf16[128,256]{1,0:T(8,128)(2,1)S(1)}, u32[]{:S(2)}, u32[]{:S(2)}) collective-permute-start(bf16[128,256]{1,0:T(8,128)(2,1)S(1)} %get-tuple-element.51), channel_id=1, source_target_pairs={{0,3},{1,2},{2,1},{3,0},{4,7},{5,6},{6,5},{7,4},{8,11},{9,10},{10,... | collective-permute-start | bytes 196616 | tf_op jit(solution)/shard_map/ppermute | solution.py:298
  44.0 4.9 %copy-start.1 = (bf16[4,1024,512]{2,1,0:T(8,128)(2,1)S(1)}, bf16[4,1024,512]{2,1,0:T(8,128)(2,1)}, u32[]{:S(2)}) copy-start(bf16[4,1024,512]{2,1,0:T(8,128)(2,1)} %refs_2_.2) | copy-start | bytes 12582916
  44.0 4.9 %copy-start.2 = (s32[1,4]{1,0:T(1,128)S(1)}, s32[1,4]{1,0:T(1,128)}, u32[]{:S(2)}) copy-start(s32[1,4]{1,0:T(1,128)} %refs_0_.7) | copy-start | bytes 52
  44.0 4.9 %copy-start.3 = (s32[16]{0:T(128)S(1)}, s32[16]{0:T(128)}, u32[]{:S(2)}) copy-start(s32[16]{0:T(128)} %refs_1_.1) | copy-start | bytes 196
  44.0 4.3 %collective-permute-start.21 = (bf16[128,256]{1,0:T(8,128)(2,1)S(1)}, bf16[128,256]{1,0:T(8,128)(2,1)S(1)}, u32[]{:S(2)}, u32[]{:S(2)}) collective-permute-start(bf16[128,256]{1,0:T(8,128)(2,1)S(1)} %get-tuple-element.49.refs_1_), channel_id=1, source_target_pairs={{0,1},{1,0},{2,3},{3,2},{4,5},{5,4},{6,7},{7,6},{8,9},{9,8},{10,11... | collective-permute-start | bytes 196616 | tf_op jit(solution)/shard_map/ppermute | solution.py:298
  45.3 3.6 %collective-permute-start.11 = (bf16[128,1024]{1,0:T(8,128)(2,1)S(1)}, bf16[128,1024]{1,0:T(8,128)(2,1)S(1)}, u32[]{:S(2)}, u32[]{:S(2)}) collective-permute-start(bf16[128,1024]{1,0:T(8,128)(2,1)S(1)} %phase.2.refs_3_), channel_id=1, source_target_pairs={{0,16},{1,17},{2,18},{3,19},{4,20},{5,21},{6,22},{7,23},{8,24},{9,... | collective-permute-start | bytes 786440 | tf_op jit(solution)/shard_map/ppermute | solution.py:298
  48.8 1.6 %collective-permute-start.22 = (bf16[128,1024]{1,0:T(8,128)(2,1)S(1)}, bf16[128,1024]{1,0:T(8,128)(2,1)S(1)}, u32[]{:S(2)}, u32[]{:S(2)}) collective-permute-start(bf16[128,1024]{1,0:T(8,128)(2,1)S(1)} %phase.3.refs_5_), channel_id=1, source_target_pairs={{0,16},{1,17},{2,18},{3,19},{4,20},{5,21},{6,22},{7,23},{8,24},{9,... | collective-permute-start | bytes 786440 | tf_op jit(solution)/shard_map/ppermute | solution.py:298

commit v28 on v27

--- a/solution.py
+++ b/solution.py
@@ -165,7 +165,7 @@
 
 def column_kernel(inner, outer, table, gain, *refs):
     pieces = dict(zip(send_order, refs[:inner]))
-    *outs, stack, total, spectrum = refs[inner:]
+    spectrum, stack, total = refs[inner:]
     _, plane, spot = position(inner)
     dists, rows_dev, block = pieces[0].shape
     depth = inner * rows_dev
@@ -181,6 +181,12 @@
         else:
             total[...] += got
     spectrum[...] = total[...].astype(bf16)
+
+
+def block_kernel(inner, table, spectrum, *refs):
+    outs = refs[-4:]
+    _, plane, _ = position(inner)
+    depth = outs[0].shape[0]
     middle = (plane == 1) | (plane == 2)
     first = jnp.where(middle, 1, 3)
     for rel, out in zip((0, first, 4 - first, 2), outs):
@@ -346,23 +352,32 @@
 
     sums = []
     for chunk in range(own):
-        blocks = pl.pallas_call(
+        spectrum = pl.pallas_call(
             lambda *refs: column_kernel(inner, outer, *refs),
-            out_shape=[shaped(depth, block)] * outer,
+            out_shape=shaped(width, block),
             in_specs=vmem(2 + inner),
-            out_specs=vmem(outer),
+            out_specs=one_out,
             scratch_shapes=[
                 pltpu.VMEM((dists, depth, block), bf16),
                 pltpu.VMEM((width, block), f32),
-                pltpu.VMEM((width, block), bf16),
             ],
             compiler_params=params,
             cost_estimate=cheap,
             name="columns",
         )(table, gain, *arrived[chunk])
+        before = [message] if sums else []
+        blocks = pl.pallas_call(
+            lambda *refs: block_kernel(inner, *refs),
+            out_shape=[shaped(depth, block)] * outer,
+            in_specs=vmem(2) + unread(len(before)),
+            out_specs=vmem(outer),
+            compiler_params=params,
+            cost_estimate=cheap,
+            name="blocks",
+        )(table, spectrum, *before)
         ours, first, second, third = blocks
         near = sent(first, to_plane(1))
-        earlier = sums[-1][3:] if sums else []
+        earlier = sums[-1][1:2] + sums[-1][3:] if sums else []
         message = pl.pallas_call(
             lambda *refs: far_kernel(inner, *refs),
             out_shape=shaped(depth, block),

time: 51.7 us -> 52 us (level)
  starting transfers between devices: 29.8 us -> 31.6 us
  waiting for transfers between devices: 10.9 us -> 9.1 us
    ppermute x23, waiting for transfers between devices: 10.9 us -> 9.1 us  [sent(): return lax.ppermute(value, ('dist', 'rows'), pairs)]
    ppermute x23, starting transfers between devices: 29.8 us -> 31.6 us  [sent(): return lax.ppermute(value, ('dist', 'rows'), pairs)]
    pallas_call x0 -> x2, Pallas kernels: none -> 1.41 us  [plane_plan(): pl.pallas_call(lambda *refs: block_kernel(inner, *refs), out_shape=[shape...]
    pallas_call x2, Pallas kernels: 2.59 us -> 1.52 us  [plane_plan(): pl.pallas_call(lambda *refs: column_kernel(inner, outer, *refs), out_shap...]
  transfers between devices with their start and end apart: 23 -> 23, of which waited for: 7 -> 8; matrix products, arithmetic and copies ran while one was open for 0% -> 0% of each run, Pallas kernels for 15% -> 15%
where the time goes in v28:
time: 52 us; the launch traced here: 51.8 us
  starting transfers between devices  31.6 us (61%)
  Pallas kernels  10.9 us (21%)
  waiting for transfers between devices  9.1 us (18%)
    ppermute x23, starting transfers between devices, sent(): return lax.ppermute(value, ('dist', 'rows'), pairs)  31.6 us
    ppermute x23, waiting for transfers between devices, sent(): return lax.ppermute(value, ('dist', 'rows'), pairs)  9.1 us
    pallas_call x1, Pallas kernels, plane_plan(): pl.pallas_call(lambda *refs: filter_kernel(inner, dist_dev, *refs), out_s...  2.62 us
    pallas_call x1, Pallas kernels, plane_plan(): pl.pallas_call(lambda *refs: row_kernel(inner, *refs), out_shape=[shaped(...  1.83 us
    pallas_call x2, Pallas kernels, plane_plan(): pl.pallas_call(lambda *refs: column_kernel(inner, outer, *refs), out_shap...  1.52 us
    pallas_call x2, Pallas kernels, plane_plan(): pl.pallas_call(lambda *refs: block_kernel(inner, *refs), out_shape=[shape...  1.41 us
    pallas_call x1, Pallas kernels, plane_plan(): pl.pallas_call(lambda *refs: recon_kernel(own, *refs), out_shape=[jax.Sha...  1.2 us
    pallas_call x1, Pallas kernels, plane_plan(): pl.pallas_call(recon_last_kernel, out_shape=shaped(capacity, pixels), in_...  1.12 us
  transfers between devices with their start and end apart: 23, of which 8 were waited for; matrix products, arithmetic and copies ran while one was open for 0% of the time, Pallas kernels for 15%

profile of v28, /device:TPU:0, one launch (start us, length us, event | category | flops | bytes accessed | tf_op | source)
XLA Modules:
  0.0 51.8 jit_solution(8967363228292372196)
XLA Ops:
  0.0 0.5 collective-permute-start
  0.5 2.6 %filters.1.refs_3_.refs_1_ = bf16[4,1024,256]{2,1,0:T(8,128)(2,1)S(1)} custom-call(f32[4]{0:T(128)} %refs_0_.8), custom_call_target="tpu_custom_call" | custom-call | flops 1 | bytes 1 | tf_op jit(solution)/shard_map/filters/pallas_call | solution.py:327
  3.1 0.0 collective-permute-done.refs_1_
  3.1 0.0 copy-done
  3.1 1.8 %row_spectra.1 = (bf16[4,64,256]{2,1,0:T(8,128)(2,1)S(1)}, bf16[4,64,256]{2,1,0:T(8,128)(2,1)S(1)}, bf16[4,64,256]{2,1,0:T(8,128)(2,1)S(1)}, bf16[4,64,256]{2,1,...) custom-call(bf16[4,2,64,1024]{3,2,1,0:T(8,128)(2,1)} %bitcast.2, ...), custom_call_target="tpu_custom_call" | custom-call | flops 1 | bytes 1 | tf_op jit(solution)/shard_map/row_spectra/pallas_call | solution.py:336
  4.9 2.8 %collective-permute-start.1 = (bf16[4,64,256]{2,1,0:T(8,128)(2,1)S(1)}, bf16[4,64,256]{2,1,0:T(8,128)(2,1)S(1)}, u32[]{:S(2)}, u32[]{:S(2)}) collective-permute-start(bf16[4,64,256]{2,1,0:T(8,128)(2,1)S(1)} %get-tuple-element.31), channel_id=1, source_target_pairs={{0,2},{1,3},{2,0},{3,1},{4,6},{5,7},{6,4},{7,5},{8,10},{9,11},{10,... | collective-permute-start | bytes 393224 | tf_op jit(solution)/shard_map/ppermute | solution.py:304
  7.7 1.5 %collective-permute-start.2 = (bf16[4,64,256]{2,1,0:T(8,128)(2,1)S(1)}, bf16[4,64,256]{2,1,0:T(8,128)(2,1)S(1)}, u32[]{:S(2)}, u32[]{:S(2)}) collective-permute-start(bf16[4,64,256]{2,1,0:T(8,128)(2,1)S(1)} %get-tuple-element.32), channel_id=1, source_target_pairs={{0,1},{1,0},{2,3},{3,2},{4,5},{5,4},{6,7},{7,6},{8,9},{9,8},{10,11... | collective-permute-start | bytes 393224 | tf_op jit(solution)/shard_map/ppermute | solution.py:304
  9.2 0.0 collective-permute-start.3
  9.3 1.9 %collective-permute-start.12 = (bf16[4,64,256]{2,1,0:T(8,128)(2,1)S(1)}, bf16[4,64,256]{2,1,0:T(8,128)(2,1)S(1)}, u32[]{:S(2)}, u32[]{:S(2)}) collective-permute-start(bf16[4,64,256]{2,1,0:T(8,128)(2,1)S(1)} %get-tuple-element.42), channel_id=1, source_target_pairs={{0,2},{1,3},{2,0},{3,1},{4,6},{5,7},{6,4},{7,5},{8,10},{9,11},{10,... | collective-permute-start | bytes 393224 | tf_op jit(solution)/shard_map/ppermute | solution.py:304
  11.2 1.5 %collective-permute-start.13 = (bf16[4,64,256]{2,1,0:T(8,128)(2,1)S(1)}, bf16[4,64,256]{2,1,0:T(8,128)(2,1)S(1)}, u32[]{:S(2)}, u32[]{:S(2)}) collective-permute-start(bf16[4,64,256]{2,1,0:T(8,128)(2,1)S(1)} %get-tuple-element.43), channel_id=1, source_target_pairs={{0,1},{1,0},{2,3},{3,2},{4,5},{5,4},{6,7},{7,6},{8,9},{9,8},{10,11... | collective-permute-start | bytes 393224 | tf_op jit(solution)/shard_map/ppermute | solution.py:304
  12.7 0.0 collective-permute-done.1.refs_3_
  12.7 1.6 %collective-permute-start.14 = (bf16[4,64,256]{2,1,0:T(8,128)(2,1)S(1)}, bf16[4,64,256]{2,1,0:T(8,128)(2,1)S(1)}, u32[]{:S(2)}, u32[]{:S(2)}) collective-permute-start(bf16[4,64,256]{2,1,0:T(8,128)(2,1)S(1)} %get-tuple-element.44), channel_id=1, source_target_pairs={{0,3},{1,2},{2,1},{3,0},{4,7},{5,6},{6,5},{7,4},{8,11},{9,10},{10,... | collective-permute-start | bytes 393224 | tf_op jit(solution)/shard_map/ppermute | solution.py:304
  14.3 0.0 collective-permute-done.2.refs_4_
  14.3 2.3 %collective-permute-done.3.refs_5_ = bf16[4,64,256]{2,1,0:T(8,128)(2,1)S(1)} collective-permute-done((bf16[4,64,256]{2,1,0:T(8,128)(2,1)S(1)}, bf16[4,64,256]{2,1,0:T(8,128)(2,1)S(1)}, u32[]{:S(2)}, u32[]{:S(2)}) %collective-permute-start.3) | collective-permute-done | bytes 131104 | tf_op jit(solution)/shard_map/ppermute | solution.py:304
  16.6 0.8 %columns.2.refs_1_ = bf16[1024,256]{1,0:T(8,128)(2,1)S(1)} custom-call(bf16[1024,1024]{1,0:T(8,128)(2,1)S(1)} %copy-done, bf16[4,1024,256]{2,1,0:T(8,128)(2,1)S(1)} %filters.1.refs_3_.refs_1_, bf16[4,64,256]{2,1,0:T(8,128)(2,1)S(1)} %get-tuple-element.30.refs_2_, bf16[4,64,256]{2,1,0:T(8,128)(2,1)S(1)} %collective-permute-done.1.refs_3_, ...), custom_call_target="tpu_custom_call" | custom-call | flops 1 | bytes 1 | tf_op jit(solution)/shard_map/columns/pallas_call | solution.py:355
  17.3 0.7 %blocks.2 = (bf16[256,256]{1,0:T(8,128)(2,1)S(1)}, bf16[256,256]{1,0:T(8,128)(2,1)S(1)}, bf16[256,256]{1,0:T(8,128)(2,1)S(1)}, bf16[256,256]{1,0:T(8,128)(2,1)S(1)}) custom-call(bf16[1024,1024]{1,0:T(8,128)(2,1)S(1)} %copy-done, bf16[1024,256]{1,0:T(8,128)(2,1)S(1)} %columns.2.refs_1_), custom_call_target="tpu_custom_call" | custom-call | flops 1 | bytes 1 | tf_op jit(solution)/shard_map/blocks/pallas_call | solution.py:369
  18.1 1.6 %collective-permute-start.4 = (bf16[256,256]{1,0:T(8,128)(2,1)S(1)}, bf16[256,256]{1,0:T(8,128)(2,1)S(1)}, u32[]{:S(2)}, u32[]{:S(2)}) collective-permute-start(bf16[256,256]{1,0:T(8,128)(2,1)S(1)} %get-tuple-element.36), channel_id=1, source_target_pairs={{0,4},{1,5},{2,6},{3,7},{4,0},{5,1},{6,2},{7,3},{8,12},{9,13},{10,... | collective-permute-start | bytes 393224 | tf_op jit(solution)/shard_map/ppermute | solution.py:304
  19.7 0.0 collective-permute-start.7
  19.7 0.0 collective-permute-done.12.refs_3_
  19.7 3.2 %collective-permute-start.6 = (bf16[256,256]{1,0:T(8,128)(2,1)S(1)}, bf16[256,256]{1,0:T(8,128)(2,1)S(1)}, u32[]{:S(2)}, u32[]{:S(2)}) collective-permute-start(bf16[256,256]{1,0:T(8,128)(2,1)S(1)} %get-tuple-element.37), channel_id=1, source_target_pairs={{0,4},{1,5},{2,6},{3,7},{4,0},{5,1},{6,2},{7,3},{8,12},{9,13},{10,... | collective-permute-start | bytes 393224 | tf_op jit(solution)/shard_map/ppermute | solution.py:304
  22.9 0.0 collective-permute-done.13.refs_4_
  22.9 0.0 collective-permute-done.14.refs_5_
  22.9 0.8 %columns.3.refs_1_ = bf16[1024,256]{1,0:T(8,128)(2,1)S(1)} custom-call(bf16[1024,1024]{1,0:T(8,128)(2,1)S(1)} %copy-done, bf16[4,1024,256]{2,1,0:T(8,128)(2,1)S(1)} %filters.1.refs_3_.refs_1_, bf16[4,64,256]{2,1,0:T(8,128)(2,1)S(1)} %get-tuple-element.41.refs_2_, bf16[4,64,256]{2,1,0:T(8,128)(2,1)S(1)} %collective-permute-done.12.refs_3_, ...), custom_call_target="tpu_custom_call" | custom-call | flops 1 | bytes 1 | tf_op jit(solution)/shard_map/columns/pallas_call | solution.py:355
  23.6 0.0 collective-permute-done.4.refs_1_.refs_2_
  23.7 0.1 far.2.refs_2_
  23.7 3.4 %collective-permute-start.5 = (bf16[256,256]{1,0:T(8,128)(2,1)S(1)}, bf16[256,256]{1,0:T(8,128)(2,1)S(1)}, u32[]{:S(2)}, u32[]{:S(2)}) collective-permute-start(bf16[256,256]{1,0:T(8,128)(2,1)S(1)} %far.2.refs_2_), channel_id=1, source_target_pairs={{0,8},{1,9},{2,10},{3,11},{4,12},{5,13},{6,14},{7,15},{8,0},{9,1},... | collective-permute-start | bytes 393224 | tf_op jit(solution)/shard_map/ppermute | solution.py:304
  27.1 0.7 %blocks.3 = (bf16[256,256]{1,0:T(8,128)(2,1)S(1)}, bf16[256,256]{1,0:T(8,128)(2,1)S(1)}, bf16[256,256]{1,0:T(8,128)(2,1)S(1)}, bf16[256,256]{1,0:T(8,128)(2,1)S(1)}) custom-call(bf16[1024,1024]{1,0:T(8,128)(2,1)S(1)} %copy-done, bf16[1024,256]{1,0:T(8,128)(2,1)S(1)} %columns.3.refs_1_, bf16[256,256]{1,0:T(8,128)(2,1)S(1)} %far.2.refs_2_), custom_call_target="tpu_custom_call" | custom-call | flops 1 | bytes 1 | tf_op jit(solution)/shard_map/blocks/pallas_call | solution.py:369
  27.8 1.7 %collective-permute-start.15 = (bf16[256,256]{1,0:T(8,128)(2,1)S(1)}, bf16[256,256]{1,0:T(8,128)(2,1)S(1)}, u32[]{:S(2)}, u32[]{:S(2)}) collective-permute-start(bf16[256,256]{1,0:T(8,128)(2,1)S(1)} %get-tuple-element.47), channel_id=1, source_target_pairs={{0,4},{1,5},{2,6},{3,7},{4,0},{5,1},{6,2},{7,3},{8,12},{9,13},{10,... | collective-permute-start | bytes 393224 | tf_op jit(solution)/shard_map/ppermute | solution.py:304
  29.6 0.0 collective-permute-start.18
  29.6 0.0 collective-permute-done.7.refs_4_.refs_2_
  29.6 2.6 %collective-permute-start.17 = (bf16[256,256]{1,0:T(8,128)(2,1)S(1)}, bf16[256,256]{1,0:T(8,128)(2,1)S(1)}, u32[]{:S(2)}, u32[]{:S(2)}) collective-permute-start(bf16[256,256]{1,0:T(8,128)(2,1)S(1)} %get-tuple-element.48), channel_id=1, source_target_pairs={{0,4},{1,5},{2,6},{3,7},{12,8},{13,9},{14,10},{15,11},{16,20},{17,... | collective-permute-start | bytes 393224 | tf_op jit(solution)/shard_map/ppermute | solution.py:304
  32.1 0.0 collective-permute-done.6.refs_3_.refs_1_
  32.1 1.0 %collective-permute-done.5.refs_1_.refs_0_ = bf16[256,256]{1,0:T(8,128)(2,1)S(1)} collective-permute-done((bf16[256,256]{1,0:T(8,128)(2,1)S(1)}, bf16[256,256]{1,0:T(8,128)(2,1)S(1)}, u32[]{:S(2)}, u32[]{:S(2)}) %collective-permute-start.5) | collective-permute-done | bytes 131104 | tf_op jit(solution)/shard_map/ppermute | solution.py:304
  33.1 0.2 collective-permute-done.15.refs_4_.refs_2_
  33.4 0.1 far.3
  33.4 1.9 %collective-permute-start.16 = (bf16[256,256]{1,0:T(8,128)(2,1)S(1)}, bf16[256,256]{1,0:T(8,128)(2,1)S(1)}, u32[]{:S(2)}, u32[]{:S(2)}) collective-permute-start(bf16[256,256]{1,0:T(8,128)(2,1)S(1)} %far.3), channel_id=1, source_target_pairs={{0,8},{1,9},{2,10},{3,11},{4,12},{5,13},{6,14},{7,15},{8,0},{9,1},... | collective-permute-start | bytes 393224 | tf_op jit(solution)/shard_map/ppermute | solution.py:304
  35.4 0.1 half.2
  35.5 1.8 %collective-permute-start.8 = (bf16[128,256]{1,0:T(8,128)(2,1)S(1)}, bf16[128,256]{1,0:T(8,128)(2,1)S(1)}, u32[]{:S(2)}, u32[]{:S(2)}) collective-permute-start(bf16[128,256]{1,0:T(8,128)(2,1)S(1)} %get-tuple-element.39), channel_id=1, source_target_pairs={{0,2},{1,3},{2,0},{3,1},{4,6},{5,7},{6,4},{7,5},{8,10},{9,11},{10,... | collective-permute-start | bytes 196616 | tf_op jit(solution)/shard_map/ppermute | solution.py:304
  37.2 1.4 %collective-permute-start.9 = (bf16[128,256]{1,0:T(8,128)(2,1)S(1)}, bf16[128,256]{1,0:T(8,128)(2,1)S(1)}, u32[]{:S(2)}, u32[]{:S(2)}) collective-permute-start(bf16[128,256]{1,0:T(8,128)(2,1)S(1)} %get-tuple-element.40), channel_id=1, source_target_pairs={{0,3},{1,2},{2,1},{3,0},{4,7},{5,6},{6,5},{7,4},{8,11},{9,10},{10,... | collective-permute-start | bytes 196616 | tf_op jit(solution)/shard_map/ppermute | solution.py:304
  38.7 0.0 collective-permute-done.18.refs_4_
  38.7 0.3 collective-permute-start.10
  39.0 0.0 collective-permute-done.17.refs_3_
  39.0 1.7 %collective-permute-done.16.refs_1_ = bf16[256,256]{1,0:T(8,128)(2,1)S(1)} collective-permute-done((bf16[256,256]{1,0:T(8,128)(2,1)S(1)}, bf16[256,256]{1,0:T(8,128)(2,1)S(1)}, u32[]{:S(2)}, u32[]{:S(2)}) %collective-permute-start.16) | collective-permute-done | bytes 131104 | tf_op jit(solution)/shard_map/ppermute | solution.py:304
  40.8 0.1 half.3
  40.9 1.9 %collective-permute-start.19 = (bf16[128,256]{1,0:T(8,128)(2,1)S(1)}, bf16[128,256]{1,0:T(8,128)(2,1)S(1)}, u32[]{:S(2)}, u32[]{:S(2)}) collective-permute-start(bf16[128,256]{1,0:T(8,128)(2,1)S(1)} %get-tuple-element.50), channel_id=1, source_target_pairs={{0,2},{1,3},{2,0},{3,1},{4,6},{5,7},{6,4},{7,5},{8,10},{9,11},{10,... | collective-permute-start | bytes 196616 | tf_op jit(solution)/shard_map/ppermute | solution.py:304
  42.8 1.4 %collective-permute-start.20 = (bf16[128,256]{1,0:T(8,128)(2,1)S(1)}, bf16[128,256]{1,0:T(8,128)(2,1)S(1)}, u32[]{:S(2)}, u32[]{:S(2)}) collective-permute-start(bf16[128,256]{1,0:T(8,128)(2,1)S(1)} %get-tuple-element.51), channel_id=1, source_target_pairs={{0,3},{1,2},{2,1},{3,0},{4,7},{5,6},{6,5},{7,4},{8,11},{9,10},{10,... | collective-permute-start | bytes 196616 | tf_op jit(solution)/shard_map/ppermute | solution.py:304
  44.3 0.0 collective-permute-done.8.refs_2_
  44.3 0.2 collective-permute-start.21
  44.5 0.0 collective-permute-done.9.refs_3_
  44.5 0.0 collective-permute-done.10.refs_4_
  44.5 0.5 phase.2.refs_3_
  45.0 0.1 collective-permute-start.11
  45.1 0.1 collective-permute-done.19.refs_2_
  45.2 2.8 %collective-permute-done.20.refs_3_ = bf16[128,256]{1,0:T(8,128)(2,1)S(1)} collective-permute-done((bf16[128,256]{1,0:T(8,128)(2,1)S(1)}, bf16[128,256]{1,0:T(8,128)(2,1)S(1)}, u32[]{:S(2)}, u32[]{:S(2)}) %collective-permute-start.20) | collective-permute-done | bytes 65568 | tf_op jit(solution)/shard_map/ppermute | solution.py:304
  48.0 0.6 %collective-permute-done.21.refs_4_ = bf16[128,256]{1,0:T(8,128)(2,1)S(1)} collective-permute-done((bf16[128,256]{1,0:T(8,128)(2,1)S(1)}, bf16[128,256]{1,0:T(8,128)(2,1)S(1)}, u32[]{:S(2)}, u32[]{:S(2)}) %collective-permute-start.21) | collective-permute-done | bytes 65568 | tf_op jit(solution)/shard_map/ppermute | solution.py:304
  48.6 0.5 phase.3.refs_5_
  49.1 0.1 collective-permute-start.22
  49.1 0.0 collective-permute-done.11.refs_4_
  49.2 0.0 copy-done.1
  49.2 0.0 copy-done.2
  49.2 0.0 copy-done.3
  49.2 1.2 %recon.2 = (f32[128,512]{1,0:T(8,128)S(1)}, bf16[1024,512]{1,0:T(8,128)(2,1)S(1)}, bf16[128,128]{1,0:T(8,128)(2,1)S(1)}) custom-call(s32[1,4]{1,0:T(1,128)S(1)} %copy-done.2, s32[16]{0:T(128)S(1)} %copy-done.3, bf16[4,1024,512]{2,1,0:T(8,128)(2,1)S(1)} %copy-done.1, bf16[128,1024]{1,0:T(8,128)(2,1)S(1)} %phase.2.refs_3_, ...), custom_call_target="tpu_custom_call" | custom-call | flops 1 | bytes 1 | tf_op jit(solution)/shard_map/recon/pallas_call | solution.py:418
  50.4 0.3 collective-permute-done.22.phase
  50.7 1.1 %recon.3 = bf16[128,512]{1,0:T(8,128)(2,1)} custom-call(bf16[1024,512]{1,0:T(8,128)(2,1)S(1)} %get-tuple-element.52.weights, bf16[128,1024]{1,0:T(8,128)(2,1)S(1)} %collective-permute-done.22.phase, f32[128,512]{1,0:T(8,128)S(1)} %get-tuple-element.53.before, bf16[128,128]{1,0:T(8,128)(2,1)S(1)} %get-tuple-element.54.select), custom_call_target="tpu_custom_call" | custom-call | flops 1 | bytes 1 | tf_op jit(solution)/shard_map/recon/pallas_call | solution.py:431
  (4 shorter events, 0.0 us)
Async XLA Ops:
  0.0 3.1 %copy-start = (bf16[1024,1024]{1,0:T(8,128)(2,1)S(1)}, bf16[1024,1024]{1,0:T(8,128)(2,1)}, u32[]{:S(2)}) copy-start(bf16[1024,1024]{1,0:T(8,128)(2,1)} %constant.2.clone.refs_2_.refs_0_) | copy-start | bytes 6291460
  0.0 3.1 %collective-permute-start = (bf16[4,2,64,1024]{3,2,1,0:T(8,128)(2,1)}, bf16[4,2,64,1024]{3,2,1,0:T(8,128)(2,1)S(1)}, u32[]{:S(2)}, u32[]{:S(2)}) collective-permute-start(bf16[4,2,64,1024]{3,2,1,0:T(8,128)(2,1)} %bitcast.1), channel_id=1, source_target_pairs={{0,16},{1,17},{2,18},{3,19},{4,20},{5,21},{6,22},{7,23},{8,24},{9,... | collective-permute-start | bytes 3145736 | tf_op jit(solution)/shard_map/ppermute | solution.py:304
  4.9 7.8 %collective-permute-start.1 = (bf16[4,64,256]{2,1,0:T(8,128)(2,1)S(1)}, bf16[4,64,256]{2,1,0:T(8,128)(2,1)S(1)}, u32[]{:S(2)}, u32[]{:S(2)}) collective-permute-start(bf16[4,64,256]{2,1,0:T(8,128)(2,1)S(1)} %get-tuple-element.31), channel_id=1, source_target_pairs={{0,2},{1,3},{2,0},{3,1},{4,6},{5,7},{6,4},{7,5},{8,10},{9,11},{10,... | collective-permute-start | bytes 393224 | tf_op jit(solution)/shard_map/ppermute | solution.py:304
  7.7 6.6 %collective-permute-start.2 = (bf16[4,64,256]{2,1,0:T(8,128)(2,1)S(1)}, bf16[4,64,256]{2,1,0:T(8,128)(2,1)S(1)}, u32[]{:S(2)}, u32[]{:S(2)}) collective-permute-start(bf16[4,64,256]{2,1,0:T(8,128)(2,1)S(1)} %get-tuple-element.32), channel_id=1, source_target_pairs={{0,1},{1,0},{2,3},{3,2},{4,5},{5,4},{6,7},{7,6},{8,9},{9,8},{10,11... | collective-permute-start | bytes 393224 | tf_op jit(solution)/shard_map/ppermute | solution.py:304
  9.2 7.4 %collective-permute-start.3 = (bf16[4,64,256]{2,1,0:T(8,128)(2,1)S(1)}, bf16[4,64,256]{2,1,0:T(8,128)(2,1)S(1)}, u32[]{:S(2)}, u32[]{:S(2)}) collective-permute-start(bf16[4,64,256]{2,1,0:T(8,128)(2,1)S(1)} %get-tuple-element.33), channel_id=1, source_target_pairs={{0,3},{1,2},{2,1},{3,0},{4,7},{5,6},{6,5},{7,4},{8,11},{9,10},{10,... | collective-permute-start | bytes 393224 | tf_op jit(solution)/shard_map/ppermute | solution.py:304
  9.3 10.4 %collective-permute-start.12 = (bf16[4,64,256]{2,1,0:T(8,128)(2,1)S(1)}, bf16[4,64,256]{2,1,0:T(8,128)(2,1)S(1)}, u32[]{:S(2)}, u32[]{:S(2)}) collective-permute-start(bf16[4,64,256]{2,1,0:T(8,128)(2,1)S(1)} %get-tuple-element.42), channel_id=1, source_target_pairs={{0,2},{1,3},{2,0},{3,1},{4,6},{5,7},{6,4},{7,5},{8,10},{9,11},{10,... | collective-permute-start | bytes 393224 | tf_op jit(solution)/shard_map/ppermute | solution.py:304
  11.2 11.7 %collective-permute-start.13 = (bf16[4,64,256]{2,1,0:T(8,128)(2,1)S(1)}, bf16[4,64,256]{2,1,0:T(8,128)(2,1)S(1)}, u32[]{:S(2)}, u32[]{:S(2)}) collective-permute-start(bf16[4,64,256]{2,1,0:T(8,128)(2,1)S(1)} %get-tuple-element.43), channel_id=1, source_target_pairs={{0,1},{1,0},{2,3},{3,2},{4,5},{5,4},{6,7},{7,6},{8,9},{9,8},{10,11... | collective-permute-start | bytes 393224 | tf_op jit(solution)/shard_map/ppermute | solution.py:304
  12.7 10.2 %collective-permute-start.14 = (bf16[4,64,256]{2,1,0:T(8,128)(2,1)S(1)}, bf16[4,64,256]{2,1,0:T(8,128)(2,1)S(1)}, u32[]{:S(2)}, u32[]{:S(2)}) collective-permute-start(bf16[4,64,256]{2,1,0:T(8,128)(2,1)S(1)} %get-tuple-element.44), channel_id=1, source_target_pairs={{0,3},{1,2},{2,1},{3,0},{4,7},{5,6},{6,5},{7,4},{8,11},{9,10},{10,... | collective-permute-start | bytes 393224 | tf_op jit(solution)/shard_map/ppermute | solution.py:304
  18.1 5.6 %collective-permute-start.4 = (bf16[256,256]{1,0:T(8,128)(2,1)S(1)}, bf16[256,256]{1,0:T(8,128)(2,1)S(1)}, u32[]{:S(2)}, u32[]{:S(2)}) collective-permute-start(bf16[256,256]{1,0:T(8,128)(2,1)S(1)} %get-tuple-element.36), channel_id=1, source_target_pairs={{0,4},{1,5},{2,6},{3,7},{4,0},{5,1},{6,2},{7,3},{8,12},{9,13},{10,... | collective-permute-start | bytes 393224 | tf_op jit(solution)/shard_map/ppermute | solution.py:304
  19.7 9.9 %collective-permute-start.7 = (bf16[256,256]{1,0:T(8,128)(2,1)S(1)}, bf16[256,256]{1,0:T(8,128)(2,1)S(1)}, u32[]{:S(2)}, u32[]{:S(2)}) collective-permute-start(bf16[256,256]{1,0:T(8,128)(2,1)S(1)} %get-tuple-element.37), channel_id=1, source_target_pairs={{0,16},{1,17},{2,18},{3,19},{4,8},{5,9},{6,10},{7,11},{8,4},{9,5},... | collective-permute-start | bytes 393224 | tf_op jit(solution)/shard_map/ppermute | solution.py:304
  19.7 12.4 %collective-permute-start.6 = (bf16[256,256]{1,0:T(8,128)(2,1)S(1)}, bf16[256,256]{1,0:T(8,128)(2,1)S(1)}, u32[]{:S(2)}, u32[]{:S(2)}) collective-permute-start(bf16[256,256]{1,0:T(8,128)(2,1)S(1)} %get-tuple-element.37), channel_id=1, source_target_pairs={{0,4},{1,5},{2,6},{3,7},{4,0},{5,1},{6,2},{7,3},{8,12},{9,13},{10,... | collective-permute-start | bytes 393224 | tf_op jit(solution)/shard_map/ppermute | solution.py:304
  23.7 9.4 %collective-permute-start.5 = (bf16[256,256]{1,0:T(8,128)(2,1)S(1)}, bf16[256,256]{1,0:T(8,128)(2,1)S(1)}, u32[]{:S(2)}, u32[]{:S(2)}) collective-permute-start(bf16[256,256]{1,0:T(8,128)(2,1)S(1)} %far.2.refs_2_), channel_id=1, source_target_pairs={{0,8},{1,9},{2,10},{3,11},{4,12},{5,13},{6,14},{7,15},{8,0},{9,1},... | collective-permute-start | bytes 393224 | tf_op jit(solution)/shard_map/ppermute | solution.py:304
  27.8 5.5 %collective-permute-start.15 = (bf16[256,256]{1,0:T(8,128)(2,1)S(1)}, bf16[256,256]{1,0:T(8,128)(2,1)S(1)}, u32[]{:S(2)}, u32[]{:S(2)}) collective-permute-start(bf16[256,256]{1,0:T(8,128)(2,1)S(1)} %get-tuple-element.47), channel_id=1, source_target_pairs={{0,4},{1,5},{2,6},{3,7},{4,0},{5,1},{6,2},{7,3},{8,12},{9,13},{10,... | collective-permute-start | bytes 393224 | tf_op jit(solution)/shard_map/ppermute | solution.py:304
  29.6 9.1 %collective-permute-start.18 = (bf16[256,256]{1,0:T(8,128)(2,1)S(1)}, bf16[256,256]{1,0:T(8,128)(2,1)S(1)}, u32[]{:S(2)}, u32[]{:S(2)}) collective-permute-start(bf16[256,256]{1,0:T(8,128)(2,1)S(1)} %get-tuple-element.48), channel_id=1, source_target_pairs={{0,16},{1,17},{2,18},{3,19},{4,8},{5,9},{6,10},{7,11},{8,4},{9,5},... | collective-permute-start | bytes 393224 | tf_op jit(solution)/shard_map/ppermute | solution.py:304
  29.6 9.5 %collective-permute-start.17 = (bf16[256,256]{1,0:T(8,128)(2,1)S(1)}, bf16[256,256]{1,0:T(8,128)(2,1)S(1)}, u32[]{:S(2)}, u32[]{:S(2)}) collective-permute-start(bf16[256,256]{1,0:T(8,128)(2,1)S(1)} %get-tuple-element.48), channel_id=1, source_target_pairs={{0,4},{1,5},{2,6},{3,7},{12,8},{13,9},{14,10},{15,11},{16,20},{17,... | collective-permute-start | bytes 393224 | tf_op jit(solution)/shard_map/ppermute | solution.py:304
  33.4 7.3 %collective-permute-start.16 = (bf16[256,256]{1,0:T(8,128)(2,1)S(1)}, bf16[256,256]{1,0:T(8,128)(2,1)S(1)}, u32[]{:S(2)}, u32[]{:S(2)}) collective-permute-start(bf16[256,256]{1,0:T(8,128)(2,1)S(1)} %far.3), channel_id=1, source_target_pairs={{0,8},{1,9},{2,10},{3,11},{4,12},{5,13},{6,14},{7,15},{8,0},{9,1},... | collective-permute-start | bytes 393224 | tf_op jit(solution)/shard_map/ppermute | solution.py:304
  35.5 8.8 %collective-permute-start.8 = (bf16[128,256]{1,0:T(8,128)(2,1)S(1)}, bf16[128,256]{1,0:T(8,128)(2,1)S(1)}, u32[]{:S(2)}, u32[]{:S(2)}) collective-permute-start(bf16[128,256]{1,0:T(8,128)(2,1)S(1)} %get-tuple-element.39), channel_id=1, source_target_pairs={{0,2},{1,3},{2,0},{3,1},{4,6},{5,7},{6,4},{7,5},{8,10},{9,11},{10,... | collective-permute-start | bytes 196616 | tf_op jit(solution)/shard_map/ppermute | solution.py:304
  37.2 7.3 %collective-permute-start.9 = (bf16[128,256]{1,0:T(8,128)(2,1)S(1)}, bf16[128,256]{1,0:T(8,128)(2,1)S(1)}, u32[]{:S(2)}, u32[]{:S(2)}) collective-permute-start(bf16[128,256]{1,0:T(8,128)(2,1)S(1)} %get-tuple-element.40), channel_id=1, source_target_pairs={{0,3},{1,2},{2,1},{3,0},{4,7},{5,6},{6,5},{7,4},{8,11},{9,10},{10,... | collective-permute-start | bytes 196616 | tf_op jit(solution)/shard_map/ppermute | solution.py:304
  38.7 5.8 %collective-permute-start.10 = (bf16[128,256]{1,0:T(8,128)(2,1)S(1)}, bf16[128,256]{1,0:T(8,128)(2,1)S(1)}, u32[]{:S(2)}, u32[]{:S(2)}) collective-permute-start(bf16[128,256]{1,0:T(8,128)(2,1)S(1)} %get-tuple-element.38.refs_1_), channel_id=1, source_target_pairs={{0,1},{1,0},{2,3},{3,2},{4,5},{5,4},{6,7},{7,6},{8,9},{9,8},{10,11... | collective-permute-start | bytes 196616 | tf_op jit(solution)/shard_map/ppermute | solution.py:304
  40.9 4.3 %collective-permute-start.19 = (bf16[128,256]{1,0:T(8,128)(2,1)S(1)}, bf16[128,256]{1,0:T(8,128)(2,1)S(1)}, u32[]{:S(2)}, u32[]{:S(2)}) collective-permute-start(bf16[128,256]{1,0:T(8,128)(2,1)S(1)} %get-tuple-element.50), channel_id=1, source_target_pairs={{0,2},{1,3},{2,0},{3,1},{4,6},{5,7},{6,4},{7,5},{8,10},{9,11},{10,... | collective-permute-start | bytes 196616 | tf_op jit(solution)/shard_map/ppermute | solution.py:304
  42.8 5.2 %collective-permute-start.20 = (bf16[128,256]{1,0:T(8,128)(2,1)S(1)}, bf16[128,256]{1,0:T(8,128)(2,1)S(1)}, u32[]{:S(2)}, u32[]{:S(2)}) collective-permute-start(bf16[128,256]{1,0:T(8,128)(2,1)S(1)} %get-tuple-element.51), channel_id=1, source_target_pairs={{0,3},{1,2},{2,1},{3,0},{4,7},{5,6},{6,5},{7,4},{8,11},{9,10},{10,... | collective-permute-start | bytes 196616 | tf_op jit(solution)/shard_map/ppermute | solution.py:304
  44.3 4.9 %copy-start.1 = (bf16[4,1024,512]{2,1,0:T(8,128)(2,1)S(1)}, bf16[4,1024,512]{2,1,0:T(8,128)(2,1)}, u32[]{:S(2)}) copy-start(bf16[4,1024,512]{2,1,0:T(8,128)(2,1)} %refs_2_.2) | copy-start | bytes 12582916
  44.3 4.9 %copy-start.2 = (s32[1,4]{1,0:T(1,128)S(1)}, s32[1,4]{1,0:T(1,128)}, u32[]{:S(2)}) copy-start(s32[1,4]{1,0:T(1,128)} %refs_0_.9) | copy-start | bytes 52
  44.3 4.9 %copy-start.3 = (s32[16]{0:T(128)S(1)}, s32[16]{0:T(128)}, u32[]{:S(2)}) copy-start(s32[16]{0:T(128)} %refs_1_.1) | copy-start | bytes 196
  44.3 4.3 %collective-permute-start.21 = (bf16[128,256]{1,0:T(8,128)(2,1)S(1)}, bf16[128,256]{1,0:T(8,128)(2,1)S(1)}, u32[]{:S(2)}, u32[]{:S(2)}) collective-permute-start(bf16[128,256]{1,0:T(8,128)(2,1)S(1)} %get-tuple-element.49.refs_1_), channel_id=1, source_target_pairs={{0,1},{1,0},{2,3},{3,2},{4,5},{5,4},{6,7},{7,6},{8,9},{9,8},{10,11... | collective-permute-start | bytes 196616 | tf_op jit(solution)/shard_map/ppermute | solution.py:304
  45.0 4.2 %collective-permute-start.11 = (bf16[128,1024]{1,0:T(8,128)(2,1)S(1)}, bf16[128,1024]{1,0:T(8,128)(2,1)S(1)}, u32[]{:S(2)}, u32[]{:S(2)}) collective-permute-start(bf16[128,1024]{1,0:T(8,128)(2,1)S(1)} %phase.2.refs_3_), channel_id=1, source_target_pairs={{0,16},{1,17},{2,18},{3,19},{4,20},{5,21},{6,22},{7,23},{8,24},{9,... | collective-permute-start | bytes 786440 | tf_op jit(solution)/shard_map/ppermute | solution.py:304
  49.1 1.6 %collective-permute-start.22 = (bf16[128,1024]{1,0:T(8,128)(2,1)S(1)}, bf16[128,1024]{1,0:T(8,128)(2,1)S(1)}, u32[]{:S(2)}, u32[]{:S(2)}) collective-permute-start(bf16[128,1024]{1,0:T(8,128)(2,1)S(1)} %phase.3.refs_5_), channel_id=1, source_target_pairs={{0,16},{1,17},{2,18},{3,19},{4,20},{5,21},{6,22},{7,23},{8,24},{9,... | collective-permute-start | bytes 786440 | tf_op jit(solution)/shard_map/ppermute | solution.py:304

commit v29 on v27

--- a/solution.py
+++ b/solution.py
@@ -222,8 +222,8 @@
 
 
 def recon_kernel(own, order, slabs, weights, *refs):
-    phases = refs[: 2 * own - 1]
-    out, chosen, select = refs[2 * own - 1 :]
+    phases = refs[: 2 * own - 2]
+    out, chosen, select = refs[2 * own - 2 :]
     core = lax.axis_index("dist")
     device = lax.axis_index("rows")
     total = None
@@ -232,7 +232,8 @@
         got = jnp.dot(phase[...], here, preferred_element_type=f32)
         total = got if total is None else total + got
     out[...] = total
-    chosen[...] = weights[order[0, (core ^ 1) * own + own - 1]]
+    for other in range(2):
+        chosen[other] = weights[order[0, (core ^ other) * own + own - 1]]
     parity = device % 2
     offset = parity * slabs[device - parity]
     slot = lax.broadcasted_iota(jnp.int32, select.shape, 0)
@@ -241,8 +242,20 @@
     select[...] = jnp.where(picked, 1.0, 0.0).astype(bf16)
 
 
-def recon_last_kernel(weights, phase, before, select, out):
-    total = before[...] + jnp.dot(phase[...], weights[...], preferred_element_type=f32)
+def recon_last_kernel(inner, table, weights, before, select, *refs):
+    out, joined = refs[-2:]
+    _, _, spot = position(inner)
+    capacity, block = refs[0].shape
+    for other in range(2):
+        pieces = dict(zip(tail_order, refs[other * inner : (other + 1) * inner]))
+        for rel in range(inner):
+            columns = pl.ds(pl.multiple_of((spot ^ rel) * block, block), block)
+            joined[other * capacity : (other + 1) * capacity, columns] = pieces[rel][...]
+    phase = jnp.dot(joined[...], table[...], preferred_element_type=f32).astype(bf16)
+    total = before[...]
+    for other in range(2):
+        ours = phase[other * capacity : (other + 1) * capacity]
+        total = total + jnp.dot(ours, weights[other], preferred_element_type=f32)
     got = jnp.dot(select[...], total.astype(bf16), preferred_element_type=f32)
     out[...] = got.astype(bf16)
 
@@ -388,6 +401,8 @@
             name="half",
         )(*sums[chunk])
         pieces = spread([first, first, second, again], tail_order)
+        if chunk == own - 1:
+            break
         phase = pl.pallas_call(
             lambda *refs: phase_kernel(inner, *refs),
             out_shape=shaped(capacity, width),
@@ -404,24 +419,26 @@
         lambda *refs: recon_kernel(own, *refs),
         out_shape=[
             jax.ShapeDtypeStruct((capacity, pixels), f32),
-            shaped(width, pixels),
+            shaped(2, width, pixels),
             shaped(capacity, capacity),
         ],
-        in_specs=smem(2) + vmem(2 * own),
+        in_specs=smem(2) + vmem(1 + len(phases)),
         out_specs=vmem(3),
         compiler_params=params,
         cost_estimate=cheap,
         name="recon",
-    )(angle_order, slab_rows, weights, *phases[:-1])
+    )(angle_order, slab_rows, weights, *phases)
+    there = [sent(piece, to_other_core) for piece in pieces]
     return pl.pallas_call(
-        recon_last_kernel,
+        lambda *refs: recon_last_kernel(inner, *refs),
         out_shape=shaped(capacity, pixels),
-        in_specs=vmem(4),
+        in_specs=vmem(4 + 2 * inner),
         out_specs=one_out,
+        scratch_shapes=[pltpu.VMEM((2 * capacity, width), bf16)],
         compiler_params=params,
         cost_estimate=cheap,
         name="recon",
-    )(chosen, phases[-1], total, select)
+    )(table, chosen, total, select, *pieces, *there)
 
 
 def on_device(holograms, propagation, weights, angle_order, slab_rows):

time: 51.7 us -> 59.5 us (1.15)
  waiting for transfers between devices: 10.9 us -> 21.9 us
  starting transfers between devices: 29.8 us -> 26.3 us
    ppermute x23 -> x26, waiting for transfers between devices: 10.9 us -> 21.9 us  [sent(): return lax.ppermute(value, ('dist', 'rows'), pairs)]
    ppermute x23 -> x26, starting transfers between devices: 29.8 us -> 26.3 us  [sent(): return lax.ppermute(value, ('dist', 'rows'), pairs)]
    pallas_call x1, Pallas kernels: 1.12 us -> 1.85 us  [plane_plan(): pl.pallas_call(lambda *refs: recon_last_kernel(inner, *refs), out_shape=s...]
  transfers between devices with their start and end apart: 23 -> 26, of which waited for: 7 -> 11; matrix products, arithmetic and copies ran while one was open for 0% -> 0% of each run, Pallas kernels for 15% -> 10%
where the time goes in v29:
time: 59.5 us; the launch traced here: 59.3 us
  starting transfers between devices  26.3 us (44%)
  waiting for transfers between devices  21.9 us (37%)
  Pallas kernels  10.8 us (18%)
    ppermute x26, starting transfers between devices, sent(): return lax.ppermute(value, ('dist', 'rows'), pairs)  26.3 us
    ppermute x26, waiting for transfers between devices, sent(): return lax.ppermute(value, ('dist', 'rows'), pairs)  21.9 us
    pallas_call x2, Pallas kernels, plane_plan(): pl.pallas_call(lambda *refs: column_kernel(inner, outer, *refs), out_shap...  2.65 us
    pallas_call x1, Pallas kernels, plane_plan(): pl.pallas_call(lambda *refs: filter_kernel(inner, dist_dev, *refs), out_s...  2.62 us
    pallas_call x1, Pallas kernels, plane_plan(): pl.pallas_call(lambda *refs: recon_last_kernel(inner, *refs), out_shape=s...  1.85 us
    pallas_call x1, Pallas kernels, plane_plan(): pl.pallas_call(lambda *refs: row_kernel(inner, *refs), out_shape=[shaped(...  1.81 us
  transfers between devices with their start and end apart: 26, of which 11 were waited for; matrix products, arithmetic and copies ran while one was open for 0% of the time, Pallas kernels for 10%

profile of v29, /device:TPU:0, one launch (start us, length us, event | category | flops | bytes accessed | tf_op | source)
XLA Modules:
  0.0 59.3 jit_solution(2437342423950031425)
XLA Ops:
  0.0 0.5 collective-permute-start
  0.5 2.6 %filters.1.refs_3_.refs_1_ = bf16[4,1024,256]{2,1,0:T(8,128)(2,1)S(1)} custom-call(f32[4]{0:T(128)} %refs_0_.6), custom_call_target="tpu_custom_call" | custom-call | flops 1 | bytes 1 | tf_op jit(solution)/shard_map/filters/pallas_call | solution.py:334
  3.1 0.0 collective-permute-done.refs_1_
  3.1 1.8 %row_spectra.1 = (bf16[4,64,256]{2,1,0:T(8,128)(2,1)S(1)}, bf16[4,64,256]{2,1,0:T(8,128)(2,1)S(1)}, bf16[4,64,256]{2,1,0:T(8,128)(2,1)S(1)}, bf16[4,64,256]{2,1,...) custom-call(bf16[4,2,64,1024]{3,2,1,0:T(8,128)(2,1)} %bitcast.2, ...), custom_call_target="tpu_custom_call" | custom-call | flops 1 | bytes 1 | tf_op jit(solution)/shard_map/row_spectra/pallas_call | solution.py:343
  4.9 2.8 %collective-permute-start.1 = (bf16[4,64,256]{2,1,0:T(8,128)(2,1)S(1)}, bf16[4,64,256]{2,1,0:T(8,128)(2,1)S(1)}, u32[]{:S(2)}, u32[]{:S(2)}) collective-permute-start(bf16[4,64,256]{2,1,0:T(8,128)(2,1)S(1)} %get-tuple-element.31), channel_id=1, source_target_pairs={{0,2},{1,3},{2,0},{3,1},{4,6},{5,7},{6,4},{7,5},{8,10},{9,11},{10,... | collective-permute-start | bytes 393224 | tf_op jit(solution)/shard_map/ppermute | solution.py:311
  7.7 1.5 %collective-permute-start.2 = (bf16[4,64,256]{2,1,0:T(8,128)(2,1)S(1)}, bf16[4,64,256]{2,1,0:T(8,128)(2,1)S(1)}, u32[]{:S(2)}, u32[]{:S(2)}) collective-permute-start(bf16[4,64,256]{2,1,0:T(8,128)(2,1)S(1)} %get-tuple-element.32), channel_id=1, source_target_pairs={{0,1},{1,0},{2,3},{3,2},{4,5},{5,4},{6,7},{7,6},{8,9},{9,8},{10,11... | collective-permute-start | bytes 393224 | tf_op jit(solution)/shard_map/ppermute | solution.py:311
  9.2 0.1 collective-permute-start.3
  9.3 2.3 %collective-permute-done.1.refs_3_ = bf16[4,64,256]{2,1,0:T(8,128)(2,1)S(1)} collective-permute-done((bf16[4,64,256]{2,1,0:T(8,128)(2,1)S(1)}, bf16[4,64,256]{2,1,0:T(8,128)(2,1)S(1)}, u32[]{:S(2)}, u32[]{:S(2)}) %collective-permute-start.1) | collective-permute-done | bytes 131104 | tf_op jit(solution)/shard_map/ppermute | solution.py:311
  11.6 2.6 %collective-permute-done.2.refs_4_ = bf16[4,64,256]{2,1,0:T(8,128)(2,1)S(1)} collective-permute-done((bf16[4,64,256]{2,1,0:T(8,128)(2,1)S(1)}, bf16[4,64,256]{2,1,0:T(8,128)(2,1)S(1)}, u32[]{:S(2)}, u32[]{:S(2)}) %collective-permute-start.2) | collective-permute-done | bytes 131104 | tf_op jit(solution)/shard_map/ppermute | solution.py:311
  14.1 1.5 %collective-permute-done.3.refs_5_ = bf16[4,64,256]{2,1,0:T(8,128)(2,1)S(1)} collective-permute-done((bf16[4,64,256]{2,1,0:T(8,128)(2,1)S(1)}, bf16[4,64,256]{2,1,0:T(8,128)(2,1)S(1)}, u32[]{:S(2)}, u32[]{:S(2)}) %collective-permute-start.3) | collective-permute-done | bytes 131104 | tf_op jit(solution)/shard_map/ppermute | solution.py:311
  15.6 1.3 %columns.2 = (bf16[256,256]{1,0:T(8,128)(2,1)S(1)}, bf16[256,256]{1,0:T(8,128)(2,1)S(1)}, bf16[256,256]{1,0:T(8,128)(2,1)S(1)}, bf16[256,256]{1,0:T(8,128)(2,1)S(1)}) custom-call(bf16[1024,1024]{1,0:T(8,128)(2,1)S(1)} %copy-done, bf16[4,1024,256]{2,1,0:T(8,128)(2,1)S(1)} %filters.1.refs_3_.refs_1_, bf16[4,64,256]{2,1,0:T(8,128)(2,1)S(1)} %get-tuple-element.30.refs_2_, ...), custom_call_target="tpu_custom_call" | custom-call | flops 1 | bytes 1 | tf_op jit(solution)/shard_map/columns/pallas_call | solution.py:362
  17.0 1.8 %collective-permute-start.4 = (bf16[256,256]{1,0:T(8,128)(2,1)S(1)}, bf16[256,256]{1,0:T(8,128)(2,1)S(1)}, u32[]{:S(2)}, u32[]{:S(2)}) collective-permute-start(bf16[256,256]{1,0:T(8,128)(2,1)S(1)} %get-tuple-element.36), channel_id=1, source_target_pairs={{0,4},{1,5},{2,6},{3,7},{4,0},{5,1},{6,2},{7,3},{8,12},{9,13},{10,... | collective-permute-start | bytes 393224 | tf_op jit(solution)/shard_map/ppermute | solution.py:311
  18.7 1.5 %collective-permute-start.12 = (bf16[4,64,256]{2,1,0:T(8,128)(2,1)S(1)}, bf16[4,64,256]{2,1,0:T(8,128)(2,1)S(1)}, u32[]{:S(2)}, u32[]{:S(2)}) collective-permute-start(bf16[4,64,256]{2,1,0:T(8,128)(2,1)S(1)} %get-tuple-element.45), channel_id=1, source_target_pairs={{0,2},{1,3},{2,0},{3,1},{4,6},{5,7},{6,4},{7,5},{8,10},{9,11},{10,... | collective-permute-start | bytes 393224 | tf_op jit(solution)/shard_map/ppermute | solution.py:311
  20.3 1.5 %collective-permute-start.13 = (bf16[4,64,256]{2,1,0:T(8,128)(2,1)S(1)}, bf16[4,64,256]{2,1,0:T(8,128)(2,1)S(1)}, u32[]{:S(2)}, u32[]{:S(2)}) collective-permute-start(bf16[4,64,256]{2,1,0:T(8,128)(2,1)S(1)} %get-tuple-element.46), channel_id=1, source_target_pairs={{0,1},{1,0},{2,3},{3,2},{4,5},{5,4},{6,7},{7,6},{8,9},{9,8},{10,11... | collective-permute-start | bytes 393224 | tf_op jit(solution)/shard_map/ppermute | solution.py:311
  21.7 0.5 collective-permute-start.14
  22.2 0.0 collective-permute-start.7
  22.2 0.0 collective-permute-done.4.refs_1_.refs_2_
  22.2 3.2 %collective-permute-start.6 = (bf16[256,256]{1,0:T(8,128)(2,1)S(1)}, bf16[256,256]{1,0:T(8,128)(2,1)S(1)}, u32[]{:S(2)}, u32[]{:S(2)}) collective-permute-start(bf16[256,256]{1,0:T(8,128)(2,1)S(1)} %get-tuple-element.37), channel_id=1, source_target_pairs={{0,4},{1,5},{2,6},{3,7},{4,0},{5,1},{6,2},{7,3},{8,12},{9,13},{10,... | collective-permute-start | bytes 393224 | tf_op jit(solution)/shard_map/ppermute | solution.py:311
  25.4 0.1 far.2
  25.4 0.0 collective-permute-done.12.refs_3_
  25.5 1.5 %collective-permute-start.5 = (bf16[256,256]{1,0:T(8,128)(2,1)S(1)}, bf16[256,256]{1,0:T(8,128)(2,1)S(1)}, u32[]{:S(2)}, u32[]{:S(2)}) collective-permute-start(bf16[256,256]{1,0:T(8,128)(2,1)S(1)} %far.2), channel_id=1, source_target_pairs={{0,8},{1,9},{2,10},{3,11},{4,12},{5,13},{6,14},{7,15},{8,0},{9,1},... | collective-permute-start | bytes 393224 | tf_op jit(solution)/shard_map/ppermute | solution.py:311
  26.9 0.0 collective-permute-done.13.refs_4_
  26.9 0.7 %collective-permute-done.14.refs_5_ = bf16[4,64,256]{2,1,0:T(8,128)(2,1)S(1)} collective-permute-done((bf16[4,64,256]{2,1,0:T(8,128)(2,1)S(1)}, bf16[4,64,256]{2,1,0:T(8,128)(2,1)S(1)}, u32[]{:S(2)}, u32[]{:S(2)}) %collective-permute-start.14) | collective-permute-done | bytes 131104 | tf_op jit(solution)/shard_map/ppermute | solution.py:311
  27.6 1.3 %columns.3 = (bf16[256,256]{1,0:T(8,128)(2,1)S(1)}, bf16[256,256]{1,0:T(8,128)(2,1)S(1)}, bf16[256,256]{1,0:T(8,128)(2,1)S(1)}, bf16[256,256]{1,0:T(8,128)(2,1)S(1)}) custom-call(bf16[1024,1024]{1,0:T(8,128)(2,1)S(1)} %copy-done, bf16[4,1024,256]{2,1,0:T(8,128)(2,1)S(1)} %filters.1.refs_3_.refs_1_, bf16[4,64,256]{2,1,0:T(8,128)(2,1)S(1)} %get-tuple-element.44.refs_2_, ...), custom_call_target="tpu_custom_call" | custom-call | flops 1 | bytes 1 | tf_op jit(solution)/shard_map/columns/pallas_call | solution.py:362
  28.9 0.5 collective-permute-start.15
  29.5 0.0 collective-permute-done.7.refs_4_.refs_1_
  29.5 0.0 collective-permute-done.6.refs_3_.refs_0_
  29.5 4.0 %collective-permute-done.5.refs_1_ = bf16[256,256]{1,0:T(8,128)(2,1)S(1)} collective-permute-done((bf16[256,256]{1,0:T(8,128)(2,1)S(1)}, bf16[256,256]{1,0:T(8,128)(2,1)S(1)}, u32[]{:S(2)}, u32[]{:S(2)}) %collective-permute-start.5) | collective-permute-done | bytes 131104 | tf_op jit(solution)/shard_map/ppermute | solution.py:311
  33.5 0.1 half.2
  33.6 0.0 copy-start.2
  33.6 0.0 copy-start.3
  33.6 1.6 %collective-permute-start.8 = (bf16[128,256]{1,0:T(8,128)(2,1)S(1)}, bf16[128,256]{1,0:T(8,128)(2,1)S(1)}, u32[]{:S(2)}, u32[]{:S(2)}) collective-permute-start(bf16[128,256]{1,0:T(8,128)(2,1)S(1)} %get-tuple-element.39), channel_id=1, source_target_pairs={{0,2},{1,3},{2,0},{3,1},{4,6},{5,7},{6,4},{7,5},{8,10},{9,11},{10,... | collective-permute-start | bytes 196616 | tf_op jit(solution)/shard_map/ppermute | solution.py:311
  35.2 1.4 %collective-permute-start.9 = (bf16[128,256]{1,0:T(8,128)(2,1)S(1)}, bf16[128,256]{1,0:T(8,128)(2,1)S(1)}, u32[]{:S(2)}, u32[]{:S(2)}) collective-permute-start(bf16[128,256]{1,0:T(8,128)(2,1)S(1)} %get-tuple-element.40), channel_id=1, source_target_pairs={{0,3},{1,2},{2,1},{3,0},{4,7},{5,6},{6,5},{7,4},{8,11},{9,10},{10,... | collective-permute-start | bytes 196616 | tf_op jit(solution)/shard_map/ppermute | solution.py:311
  36.6 0.5 collective-permute-start.10
  37.2 0.0 collective-permute-start.18
  37.2 0.0 collective-permute-done.15.refs_3_.refs_2_
  37.2 3.8 %collective-permute-start.17 = (bf16[256,256]{1,0:T(8,128)(2,1)S(1)}, bf16[256,256]{1,0:T(8,128)(2,1)S(1)}, u32[]{:S(2)}, u32[]{:S(2)}) collective-permute-start(bf16[256,256]{1,0:T(8,128)(2,1)S(1)} %get-tuple-element.51), channel_id=1, source_target_pairs={{0,4},{1,5},{2,6},{3,7},{12,8},{13,9},{14,10},{15,11},{16,20},{17,... | collective-permute-start | bytes 393224 | tf_op jit(solution)/shard_map/ppermute | solution.py:311
  41.0 0.1 far.3
  41.1 0.0 collective-permute-done.8.refs_2_
  41.1 0.1 collective-permute-start.16
  41.2 0.0 collective-permute-done.9.refs_3_
  41.2 0.0 collective-permute-done.10.refs_4_
  41.2 0.5 phase.1.refs_3_
  41.7 0.1 collective-permute-start.11
  41.7 0.0 collective-permute-done.18.refs_4_
  41.7 1.8 %collective-permute-done.17.refs_3_ = bf16[256,256]{1,0:T(8,128)(2,1)S(1)} collective-permute-done((bf16[256,256]{1,0:T(8,128)(2,1)S(1)}, bf16[256,256]{1,0:T(8,128)(2,1)S(1)}, u32[]{:S(2)}, u32[]{:S(2)}) %collective-permute-start.17) | collective-permute-done | bytes 131104 | tf_op jit(solution)/shard_map/ppermute | solution.py:311
  43.5 5.5 %collective-permute-done.16.refs_1_ = bf16[256,256]{1,0:T(8,128)(2,1)S(1)} collective-permute-done((bf16[256,256]{1,0:T(8,128)(2,1)S(1)}, bf16[256,256]{1,0:T(8,128)(2,1)S(1)}, u32[]{:S(2)}, u32[]{:S(2)}) %collective-permute-start.16) | collective-permute-done | bytes 131104 | tf_op jit(solution)/shard_map/ppermute | solution.py:311
  49.0 0.1 half.3
  49.1 1.4 %collective-permute-start.19 = (bf16[128,256]{1,0:T(8,128)(2,1)S(1)}, bf16[128,256]{1,0:T(8,128)(2,1)S(1)}, u32[]{:S(2)}, u32[]{:S(2)}) collective-permute-start(bf16[128,256]{1,0:T(8,128)(2,1)S(1)} %get-tuple-element.53), channel_id=1, source_target_pairs={{0,2},{1,3},{2,0},{3,1},{4,6},{5,7},{6,4},{7,5},{8,10},{9,11},{10,... | collective-permute-start | bytes 196616 | tf_op jit(solution)/shard_map/ppermute | solution.py:311
  50.5 1.4 %collective-permute-start.20 = (bf16[128,256]{1,0:T(8,128)(2,1)S(1)}, bf16[128,256]{1,0:T(8,128)(2,1)S(1)}, u32[]{:S(2)}, u32[]{:S(2)}) collective-permute-start(bf16[128,256]{1,0:T(8,128)(2,1)S(1)} %get-tuple-element.54), channel_id=1, source_target_pairs={{0,3},{1,2},{2,1},{3,0},{4,7},{5,6},{6,5},{7,4},{8,11},{9,10},{10,... | collective-permute-start | bytes 196616 | tf_op jit(solution)/shard_map/ppermute | solution.py:311
  51.9 0.7 %collective-permute-start.21 = (bf16[128,256]{1,0:T(8,128)(2,1)S(1)}, bf16[128,256]{1,0:T(8,128)(2,1)S(1)}, u32[]{:S(2)}, u32[]{:S(2)}) collective-permute-start(bf16[128,256]{1,0:T(8,128)(2,1)S(1)} %get-tuple-element.52.refs_4_), channel_id=1, source_target_pairs={{0,1},{1,0},{2,3},{3,2},{4,5},{5,4},{6,7},{7,6},{8,9},{9,8},{10,11... | collective-permute-start | bytes 196616 | tf_op jit(solution)/shard_map/ppermute | solution.py:311
  52.6 0.0 collective-permute-start.22
  52.7 0.8 %collective-permute-done.19.refs_5_ = bf16[128,256]{1,0:T(8,128)(2,1)S(1)} collective-permute-done((bf16[128,256]{1,0:T(8,128)(2,1)S(1)}, bf16[128,256]{1,0:T(8,128)(2,1)S(1)}, u32[]{:S(2)}, u32[]{:S(2)}) %collective-permute-start.19) | collective-permute-done | bytes 65568 | tf_op jit(solution)/shard_map/ppermute | solution.py:311
  53.4 0.0 collective-permute-start.23
  53.4 2.2 %collective-permute-done.20.refs_6_ = bf16[128,256]{1,0:T(8,128)(2,1)S(1)} collective-permute-done((bf16[128,256]{1,0:T(8,128)(2,1)S(1)}, bf16[128,256]{1,0:T(8,128)(2,1)S(1)}, u32[]{:S(2)}, u32[]{:S(2)}) %collective-permute-start.20) | collective-permute-done | bytes 65568 | tf_op jit(solution)/shard_map/ppermute | solution.py:311
  55.7 0.0 collective-permute-start.24
  55.7 0.5 collective-permute-done.21.refs_7_
  56.2 0.0 collective-permute-start.25
  56.2 0.0 collective-permute-done.11.refs_4_
  56.2 1.1 %recon.2 = (f32[128,512]{1,0:T(8,128)S(1)}, bf16[2,1024,512]{2,1,0:T(8,128)(2,1)S(1)}, bf16[128,128]{1,0:T(8,128)(2,1)S(1)}) custom-call(s32[1,4]{1,0:T(1,128)S(1)} %copy-done.2, s32[16]{0:T(128)S(1)} %copy-done.3, bf16[4,1024,512]{2,1,0:T(8,128)(2,1)S(1)} %copy-done.1, bf16[128,1024]{1,0:T(8,128)(2,1)S(1)} %phase.1.refs_3_, ...), custom_call_target="tpu_custom_call" | custom-call | flops 1 | bytes 1 | tf_op jit(solution)/shard_map/recon/pallas_call | solution.py:418
  57.3 0.0 collective-permute-done.22.refs_8_
  57.4 0.0 collective-permute-done.24.refs_10_
  57.4 0.1 collective-permute-done.25.refs_11_
  57.4 1.9 %recon.3 = bf16[128,512]{1,0:T(8,128)(2,1)} custom-call(bf16[1024,1024]{1,0:T(8,128)(2,1)S(1)} %copy-done, bf16[2,1024,512]{2,1,0:T(8,128)(2,1)S(1)} %get-tuple-element.41.refs_1_, f32[128,512]{1,0:T(8,128)S(1)} %get-tuple-element.42.refs_2_, bf16[128,128]{1,0:T(8,128)(2,1)S(1)} %get-tuple-element.43.refs_3_, ...), custom_call_target="tpu_custom_call" | custom-call | flops 1 | bytes 1 | tf_op jit(solution)/shard_map/recon/pallas_call | solution.py:432
  (7 shorter events, 0.0 us)
Async XLA Ops:
  0.0 3.1 %copy-start = (bf16[1024,1024]{1,0:T(8,128)(2,1)S(1)}, bf16[1024,1024]{1,0:T(8,128)(2,1)}, u32[]{:S(2)}) copy-start(bf16[1024,1024]{1,0:T(8,128)(2,1)} %constant.2.clone.refs_2_.refs_0_) | copy-start | bytes 6291460
  0.0 3.1 %collective-permute-start = (bf16[4,2,64,1024]{3,2,1,0:T(8,128)(2,1)}, bf16[4,2,64,1024]{3,2,1,0:T(8,128)(2,1)S(1)}, u32[]{:S(2)}, u32[]{:S(2)}) collective-permute-start(bf16[4,2,64,1024]{3,2,1,0:T(8,128)(2,1)} %bitcast.1), channel_id=1, source_target_pairs={{0,16},{1,17},{2,18},{3,19},{4,20},{5,21},{6,22},{7,23},{8,24},{9,... | collective-permute-start | bytes 3145736 | tf_op jit(solution)/shard_map/ppermute | solution.py:311
  4.9 6.6 %collective-permute-start.1 = (bf16[4,64,256]{2,1,0:T(8,128)(2,1)S(1)}, bf16[4,64,256]{2,1,0:T(8,128)(2,1)S(1)}, u32[]{:S(2)}, u32[]{:S(2)}) collective-permute-start(bf16[4,64,256]{2,1,0:T(8,128)(2,1)S(1)} %get-tuple-element.31), channel_id=1, source_target_pairs={{0,2},{1,3},{2,0},{3,1},{4,6},{5,7},{6,4},{7,5},{8,10},{9,11},{10,... | collective-permute-start | bytes 393224 | tf_op jit(solution)/shard_map/ppermute | solution.py:311
  7.7 6.4 %collective-permute-start.2 = (bf16[4,64,256]{2,1,0:T(8,128)(2,1)S(1)}, bf16[4,64,256]{2,1,0:T(8,128)(2,1)S(1)}, u32[]{:S(2)}, u32[]{:S(2)}) collective-permute-start(bf16[4,64,256]{2,1,0:T(8,128)(2,1)S(1)} %get-tuple-element.32), channel_id=1, source_target_pairs={{0,1},{1,0},{2,3},{3,2},{4,5},{5,4},{6,7},{7,6},{8,9},{9,8},{10,11... | collective-permute-start | bytes 393224 | tf_op jit(solution)/shard_map/ppermute | solution.py:311
  9.2 6.4 %collective-permute-start.3 = (bf16[4,64,256]{2,1,0:T(8,128)(2,1)S(1)}, bf16[4,64,256]{2,1,0:T(8,128)(2,1)S(1)}, u32[]{:S(2)}, u32[]{:S(2)}) collective-permute-start(bf16[4,64,256]{2,1,0:T(8,128)(2,1)S(1)} %get-tuple-element.33), channel_id=1, source_target_pairs={{0,3},{1,2},{2,1},{3,0},{4,7},{5,6},{6,5},{7,4},{8,11},{9,10},{10,... | collective-permute-start | bytes 393224 | tf_op jit(solution)/shard_map/ppermute | solution.py:311
  17.0 5.3 %collective-permute-start.4 = (bf16[256,256]{1,0:T(8,128)(2,1)S(1)}, bf16[256,256]{1,0:T(8,128)(2,1)S(1)}, u32[]{:S(2)}, u32[]{:S(2)}) collective-permute-start(bf16[256,256]{1,0:T(8,128)(2,1)S(1)} %get-tuple-element.36), channel_id=1, source_target_pairs={{0,4},{1,5},{2,6},{3,7},{4,0},{5,1},{6,2},{7,3},{8,12},{9,13},{10,... | collective-permute-start | bytes 393224 | tf_op jit(solution)/shard_map/ppermute | solution.py:311
  18.7 6.7 %collective-permute-start.12 = (bf16[4,64,256]{2,1,0:T(8,128)(2,1)S(1)}, bf16[4,64,256]{2,1,0:T(8,128)(2,1)S(1)}, u32[]{:S(2)}, u32[]{:S(2)}) collective-permute-start(bf16[4,64,256]{2,1,0:T(8,128)(2,1)S(1)} %get-tuple-element.45), channel_id=1, source_target_pairs={{0,2},{1,3},{2,0},{3,1},{4,6},{5,7},{6,4},{7,5},{8,10},{9,11},{10,... | collective-permute-start | bytes 393224 | tf_op jit(solution)/shard_map/ppermute | solution.py:311
  20.3 6.7 %collective-permute-start.13 = (bf16[4,64,256]{2,1,0:T(8,128)(2,1)S(1)}, bf16[4,64,256]{2,1,0:T(8,128)(2,1)S(1)}, u32[]{:S(2)}, u32[]{:S(2)}) collective-permute-start(bf16[4,64,256]{2,1,0:T(8,128)(2,1)S(1)} %get-tuple-element.46), channel_id=1, source_target_pairs={{0,1},{1,0},{2,3},{3,2},{4,5},{5,4},{6,7},{7,6},{8,9},{9,8},{10,11... | collective-permute-start | bytes 393224 | tf_op jit(solution)/shard_map/ppermute | solution.py:311
  21.7 5.9 %collective-permute-start.14 = (bf16[4,64,256]{2,1,0:T(8,128)(2,1)S(1)}, bf16[4,64,256]{2,1,0:T(8,128)(2,1)S(1)}, u32[]{:S(2)}, u32[]{:S(2)}) collective-permute-start(bf16[4,64,256]{2,1,0:T(8,128)(2,1)S(1)} %get-tuple-element.47), channel_id=1, source_target_pairs={{0,3},{1,2},{2,1},{3,0},{4,7},{5,6},{6,5},{7,4},{8,11},{9,10},{10,... | collective-permute-start | bytes 393224 | tf_op jit(solution)/shard_map/ppermute | solution.py:311
  22.2 7.3 %collective-permute-start.7 = (bf16[256,256]{1,0:T(8,128)(2,1)S(1)}, bf16[256,256]{1,0:T(8,128)(2,1)S(1)}, u32[]{:S(2)}, u32[]{:S(2)}) collective-permute-start(bf16[256,256]{1,0:T(8,128)(2,1)S(1)} %get-tuple-element.37), channel_id=1, source_target_pairs={{0,16},{1,17},{2,18},{3,19},{4,8},{5,9},{6,10},{7,11},{8,4},{9,5},... | collective-permute-start | bytes 393224 | tf_op jit(solution)/shard_map/ppermute | solution.py:311
  22.2 7.3 %collective-permute-start.6 = (bf16[256,256]{1,0:T(8,128)(2,1)S(1)}, bf16[256,256]{1,0:T(8,128)(2,1)S(1)}, u32[]{:S(2)}, u32[]{:S(2)}) collective-permute-start(bf16[256,256]{1,0:T(8,128)(2,1)S(1)} %get-tuple-element.37), channel_id=1, source_target_pairs={{0,4},{1,5},{2,6},{3,7},{4,0},{5,1},{6,2},{7,3},{8,12},{9,13},{10,... | collective-permute-start | bytes 393224 | tf_op jit(solution)/shard_map/ppermute | solution.py:311
  25.5 8.0 %collective-permute-start.5 = (bf16[256,256]{1,0:T(8,128)(2,1)S(1)}, bf16[256,256]{1,0:T(8,128)(2,1)S(1)}, u32[]{:S(2)}, u32[]{:S(2)}) collective-permute-start(bf16[256,256]{1,0:T(8,128)(2,1)S(1)} %far.2), channel_id=1, source_target_pairs={{0,8},{1,9},{2,10},{3,11},{4,12},{5,13},{6,14},{7,15},{8,0},{9,1},... | collective-permute-start | bytes 393224 | tf_op jit(solution)/shard_map/ppermute | solution.py:311
  28.9 8.2 %collective-permute-start.15 = (bf16[256,256]{1,0:T(8,128)(2,1)S(1)}, bf16[256,256]{1,0:T(8,128)(2,1)S(1)}, u32[]{:S(2)}, u32[]{:S(2)}) collective-permute-start(bf16[256,256]{1,0:T(8,128)(2,1)S(1)} %get-tuple-element.50), channel_id=1, source_target_pairs={{0,4},{1,5},{2,6},{3,7},{4,0},{5,1},{6,2},{7,3},{8,12},{9,13},{10,... | collective-permute-start | bytes 393224 | tf_op jit(solution)/shard_map/ppermute | solution.py:311
  33.5 22.7 %copy-start.1 = (bf16[4,1024,512]{2,1,0:T(8,128)(2,1)S(1)}, bf16[4,1024,512]{2,1,0:T(8,128)(2,1)}, u32[]{:S(2)}) copy-start(bf16[4,1024,512]{2,1,0:T(8,128)(2,1)} %refs_2_.2) | copy-start | bytes 12582916
  33.6 22.6 %copy-start.2 = (s32[1,4]{1,0:T(1,128)S(1)}, s32[1,4]{1,0:T(1,128)}, u32[]{:S(2)}) copy-start(s32[1,4]{1,0:T(1,128)} %refs_0_.7) | copy-start | bytes 52
  33.6 22.6 %copy-start.3 = (s32[16]{0:T(128)S(1)}, s32[16]{0:T(128)}, u32[]{:S(2)}) copy-start(s32[16]{0:T(128)} %refs_1_.1) | copy-start | bytes 196
  33.6 7.5 %collective-permute-start.8 = (bf16[128,256]{1,0:T(8,128)(2,1)S(1)}, bf16[128,256]{1,0:T(8,128)(2,1)S(1)}, u32[]{:S(2)}, u32[]{:S(2)}) collective-permute-start(bf16[128,256]{1,0:T(8,128)(2,1)S(1)} %get-tuple-element.39), channel_id=1, source_target_pairs={{0,2},{1,3},{2,0},{3,1},{4,6},{5,7},{6,4},{7,5},{8,10},{9,11},{10,... | collective-permute-start | bytes 196616 | tf_op jit(solution)/shard_map/ppermute | solution.py:311
  35.2 6.0 %collective-permute-start.9 = (bf16[128,256]{1,0:T(8,128)(2,1)S(1)}, bf16[128,256]{1,0:T(8,128)(2,1)S(1)}, u32[]{:S(2)}, u32[]{:S(2)}) collective-permute-start(bf16[128,256]{1,0:T(8,128)(2,1)S(1)} %get-tuple-element.40), channel_id=1, source_target_pairs={{0,3},{1,2},{2,1},{3,0},{4,7},{5,6},{6,5},{7,4},{8,11},{9,10},{10,... | collective-permute-start | bytes 196616 | tf_op jit(solution)/shard_map/ppermute | solution.py:311
  36.6 4.5 %collective-permute-start.10 = (bf16[128,256]{1,0:T(8,128)(2,1)S(1)}, bf16[128,256]{1,0:T(8,128)(2,1)S(1)}, u32[]{:S(2)}, u32[]{:S(2)}) collective-permute-start(bf16[128,256]{1,0:T(8,128)(2,1)S(1)} %get-tuple-element.38.refs_1_), channel_id=1, source_target_pairs={{0,1},{1,0},{2,3},{3,2},{4,5},{5,4},{6,7},{7,6},{8,9},{9,8},{10,11... | collective-permute-start | bytes 196616 | tf_op jit(solution)/shard_map/ppermute | solution.py:311
  37.2 4.6 %collective-permute-start.18 = (bf16[256,256]{1,0:T(8,128)(2,1)S(1)}, bf16[256,256]{1,0:T(8,128)(2,1)S(1)}, u32[]{:S(2)}, u32[]{:S(2)}) collective-permute-start(bf16[256,256]{1,0:T(8,128)(2,1)S(1)} %get-tuple-element.51), channel_id=1, source_target_pairs={{0,16},{1,17},{2,18},{3,19},{4,8},{5,9},{6,10},{7,11},{8,4},{9,5},... | collective-permute-start | bytes 393224 | tf_op jit(solution)/shard_map/ppermute | solution.py:311
  37.2 6.4 %collective-permute-start.17 = (bf16[256,256]{1,0:T(8,128)(2,1)S(1)}, bf16[256,256]{1,0:T(8,128)(2,1)S(1)}, u32[]{:S(2)}, u32[]{:S(2)}) collective-permute-start(bf16[256,256]{1,0:T(8,128)(2,1)S(1)} %get-tuple-element.51), channel_id=1, source_target_pairs={{0,4},{1,5},{2,6},{3,7},{12,8},{13,9},{14,10},{15,11},{16,20},{17,... | collective-permute-start | bytes 393224 | tf_op jit(solution)/shard_map/ppermute | solution.py:311
  41.1 7.9 %collective-permute-start.16 = (bf16[256,256]{1,0:T(8,128)(2,1)S(1)}, bf16[256,256]{1,0:T(8,128)(2,1)S(1)}, u32[]{:S(2)}, u32[]{:S(2)}) collective-permute-start(bf16[256,256]{1,0:T(8,128)(2,1)S(1)} %far.3), channel_id=1, source_target_pairs={{0,8},{1,9},{2,10},{3,11},{4,12},{5,13},{6,14},{7,15},{8,0},{9,1},... | collective-permute-start | bytes 393224 | tf_op jit(solution)/shard_map/ppermute | solution.py:311
  41.7 14.5 %collective-permute-start.11 = (bf16[128,1024]{1,0:T(8,128)(2,1)S(1)}, bf16[128,1024]{1,0:T(8,128)(2,1)S(1)}, u32[]{:S(2)}, u32[]{:S(2)}) collective-permute-start(bf16[128,1024]{1,0:T(8,128)(2,1)S(1)} %phase.1.refs_3_), channel_id=1, source_target_pairs={{0,16},{1,17},{2,18},{3,19},{4,20},{5,21},{6,22},{7,23},{8,24},{9,... | collective-permute-start | bytes 786440 | tf_op jit(solution)/shard_map/ppermute | solution.py:311
  49.1 4.3 %collective-permute-start.19 = (bf16[128,256]{1,0:T(8,128)(2,1)S(1)}, bf16[128,256]{1,0:T(8,128)(2,1)S(1)}, u32[]{:S(2)}, u32[]{:S(2)}) collective-permute-start(bf16[128,256]{1,0:T(8,128)(2,1)S(1)} %get-tuple-element.53), channel_id=1, source_target_pairs={{0,2},{1,3},{2,0},{3,1},{4,6},{5,7},{6,4},{7,5},{8,10},{9,11},{10,... | collective-permute-start | bytes 196616 | tf_op jit(solution)/shard_map/ppermute | solution.py:311
  50.5 5.2 %collective-permute-start.20 = (bf16[128,256]{1,0:T(8,128)(2,1)S(1)}, bf16[128,256]{1,0:T(8,128)(2,1)S(1)}, u32[]{:S(2)}, u32[]{:S(2)}) collective-permute-start(bf16[128,256]{1,0:T(8,128)(2,1)S(1)} %get-tuple-element.54), channel_id=1, source_target_pairs={{0,3},{1,2},{2,1},{3,0},{4,7},{5,6},{6,5},{7,4},{8,11},{9,10},{10,... | collective-permute-start | bytes 196616 | tf_op jit(solution)/shard_map/ppermute | solution.py:311
  51.9 4.3 %collective-permute-start.21 = (bf16[128,256]{1,0:T(8,128)(2,1)S(1)}, bf16[128,256]{1,0:T(8,128)(2,1)S(1)}, u32[]{:S(2)}, u32[]{:S(2)}) collective-permute-start(bf16[128,256]{1,0:T(8,128)(2,1)S(1)} %get-tuple-element.52.refs_4_), channel_id=1, source_target_pairs={{0,1},{1,0},{2,3},{3,2},{4,5},{5,4},{6,7},{7,6},{8,9},{9,8},{10,11... | collective-permute-start | bytes 196616 | tf_op jit(solution)/shard_map/ppermute | solution.py:311
  52.6 4.7 %collective-permute-start.22 = (bf16[128,256]{1,0:T(8,128)(2,1)S(1)}, bf16[128,256]{1,0:T(8,128)(2,1)S(1)}, u32[]{:S(2)}, u32[]{:S(2)}) collective-permute-start(bf16[128,256]{1,0:T(8,128)(2,1)S(1)} %get-tuple-element.52.refs_4_), channel_id=1, source_target_pairs={{0,16},{1,17},{2,18},{3,19},{4,20},{5,21},{6,22},{7,23},{8,24},{9,... | collective-permute-start | bytes 196616 | tf_op jit(solution)/shard_map/ppermute | solution.py:311
  53.4 3.9 %collective-permute-start.23 = (bf16[128,256]{1,0:T(8,128)(2,1)S(1)}, bf16[128,256]{1,0:T(8,128)(2,1)S(1)}, u32[]{:S(2)}, u32[]{:S(2)}) collective-permute-start(bf16[128,256]{1,0:T(8,128)(2,1)S(1)} %collective-permute-done.19.refs_5_), channel_id=1, source_target_pairs={{0,16},{1,17},{2,18},{3,19},{4,20},{5,21},{6,22},{7,23},{8,24},{9,... | collective-permute-start | bytes 196616 | tf_op jit(solution)/shard_map/ppermute | solution.py:311
  55.7 1.7 %collective-permute-start.24 = (bf16[128,256]{1,0:T(8,128)(2,1)S(1)}, bf16[128,256]{1,0:T(8,128)(2,1)S(1)}, u32[]{:S(2)}, u32[]{:S(2)}) collective-permute-start(bf16[128,256]{1,0:T(8,128)(2,1)S(1)} %collective-permute-done.20.refs_6_), channel_id=1, source_target_pairs={{0,16},{1,17},{2,18},{3,19},{4,20},{5,21},{6,22},{7,23},{8,24},{9,... | collective-permute-start | bytes 196616 | tf_op jit(solution)/shard_map/ppermute | solution.py:311
  56.2 1.3 %collective-permute-start.25 = (bf16[128,256]{1,0:T(8,128)(2,1)S(1)}, bf16[128,256]{1,0:T(8,128)(2,1)S(1)}, u32[]{:S(2)}, u32[]{:S(2)}) collective-permute-start(bf16[128,256]{1,0:T(8,128)(2,1)S(1)} %collective-permute-done.21.refs_7_), channel_id=1, source_target_pairs={{0,16},{1,17},{2,18},{3,19},{4,20},{5,21},{6,22},{7,23},{8,24},{9,... | collective-permute-start | bytes 196616 | tf_op jit(solution)/shard_map/ppermute | solution.py:311

commit v30 on v27

--- a/solution.py
+++ b/solution.py
@@ -104,18 +104,28 @@
     core, _, spot = position(inner)
     _, dist_dev, rows_dev, width = there.shape
     block = width // inner
-    copy = pltpu.make_async_copy(holo.at[pl.ds(core * own, own)], mine, loaded)
-    copy.start()
-    for first, source in ((dist_dev, there.at[pl.ds(core * own, own)]), (0, mine)):
-        if first == 0:
-            copy.wait()
-        rows = source[...].reshape(own * dist_dev * rows_dev, width)
-        for rel in range(inner):
-            part = table[:, pl.ds(pl.multiple_of((spot ^ rel) * block, block), block)]
-            got = jnp.dot(rows, part, preferred_element_type=f32).astype(bf16)
-            got = got.reshape(own, dist_dev, rows_dev, block)
-            for chunk in range(own):
-                outs[chunk * inner + rel][first : first + dist_dev] = got[chunk]
+    copies = [
+        pltpu.make_async_copy(
+            holo.at[core * own + chunk, d], mine.at[chunk, d], loaded.at[chunk * dist_dev + d]
+        )
+        for chunk in range(own)
+        for d in range(dist_dev)
+    ]
+    for copy in copies:
+        copy.start()
+    partner = there[pl.ds(core * own, own)].reshape(own * dist_dev * rows_dev, width)
+    for copy in copies:
+        copy.wait()
+    ours = mine[...].reshape(own * dist_dev * rows_dev, width)
+    rows = jnp.concatenate([ours, partner], axis=0)
+    for rel in range(inner):
+        part = table[:, pl.ds(pl.multiple_of((spot ^ rel) * block, block), block)]
+        got = jnp.dot(rows, part, preferred_element_type=f32).astype(bf16)
+        got = got.reshape(2, own, dist_dev, rows_dev, block)
+        for chunk in range(own):
+            out = outs[chunk * inner + rel]
+            out[0:dist_dev] = got[0, chunk]
+            out[dist_dev:] = got[1, chunk]
 
 
 def whole_turns(scale, square):
@@ -334,7 +344,7 @@
         out_specs=vmem(own * inner),
         scratch_shapes=[
             pltpu.VMEM((own, dist_dev, rows_dev, width), bf16),
-            pltpu.SemaphoreType.DMA,
+            pltpu.SemaphoreType.DMA((own * dist_dev,)),
         ],
         compiler_params=params,
         cost_estimate=cheap,

time: 51.7 us -> 52.3 us (1.012)
  Pallas kernels: 10.6 us -> 11.2 us
    pallas_call x1, Pallas kernels: 1.83 us -> 2.42 us  [plane_plan(): pl.pallas_call(lambda *refs: row_kernel(inner, *refs), out_shape=[shaped(...]
where the time goes in v30:
time: 52.3 us; the launch traced here: 52.1 us
  starting transfers between devices  29.8 us (57%)
  Pallas kernels  11.2 us (21%)
  waiting for transfers between devices  10.9 us (21%)
    ppermute x23, starting transfers between devices, sent(): return lax.ppermute(value, ('dist', 'rows'), pairs)  29.8 us
    ppermute x23, waiting for transfers between devices, sent(): return lax.ppermute(value, ('dist', 'rows'), pairs)  10.9 us
    pallas_call x1, Pallas kernels, plane_plan(): pl.pallas_call(lambda *refs: filter_kernel(inner, dist_dev, *refs), out_s...  2.62 us
    pallas_call x2, Pallas kernels, plane_plan(): pl.pallas_call(lambda *refs: column_kernel(inner, outer, *refs), out_shap...  2.6 us
    pallas_call x1, Pallas kernels, plane_plan(): pl.pallas_call(lambda *refs: row_kernel(inner, *refs), out_shape=[shaped(...  2.42 us
    pallas_call x1, Pallas kernels, plane_plan(): pl.pallas_call(lambda *refs: recon_kernel(own, *refs), out_shape=[jax.Sha...  1.2 us
    pallas_call x1, Pallas kernels, plane_plan(): pl.pallas_call(recon_last_kernel, out_shape=shaped(capacity, pixels), in_...  1.12 us
  transfers between devices with their start and end apart: 23, of which 7 were waited for; matrix products, arithmetic and copies ran while one was open for 0% of the time, Pallas kernels for 15%

profile of v30, /device:TPU:0, one launch (start us, length us, event | category | flops | bytes accessed | tf_op | source)
XLA Modules:
  0.0 52.1 jit_solution(12388437595139291798)
XLA Ops:
  0.0 0.0 copy-start
  0.0 0.5 collective-permute-start
  0.5 2.6 %filters.1.refs_3_.refs_1_ = bf16[4,1024,256]{2,1,0:T(8,128)(2,1)S(1)} custom-call(f32[4]{0:T(128)} %refs_0_.6), custom_call_target="tpu_custom_call" | custom-call | flops 1 | bytes 1 | tf_op jit(solution)/shard_map/filters/pallas_call | solution.py:331
  3.1 0.0 collective-permute-done.refs_1_
  3.1 0.0 copy-done
  3.1 2.4 %row_spectra.1 = (bf16[4,64,256]{2,1,0:T(8,128)(2,1)S(1)}, bf16[4,64,256]{2,1,0:T(8,128)(2,1)S(1)}, bf16[4,64,256]{2,1,0:T(8,128)(2,1)S(1)}, bf16[4,64,256]{2,1,...) custom-call(bf16[4,2,64,1024]{3,2,1,0:T(8,128)(2,1)} %bitcast.2, ...), custom_call_target="tpu_custom_call" | custom-call | flops 1 | bytes 1 | tf_op jit(solution)/shard_map/row_spectra/pallas_call | solution.py:340
  5.5 2.8 %collective-permute-start.1 = (bf16[4,64,256]{2,1,0:T(8,128)(2,1)S(1)}, bf16[4,64,256]{2,1,0:T(8,128)(2,1)S(1)}, u32[]{:S(2)}, u32[]{:S(2)}) collective-permute-start(bf16[4,64,256]{2,1,0:T(8,128)(2,1)S(1)} %get-tuple-element.31), channel_id=1, source_target_pairs={{0,2},{1,3},{2,0},{3,1},{4,6},{5,7},{6,4},{7,5},{8,10},{9,11},{10,... | collective-permute-start | bytes 393224 | tf_op jit(solution)/shard_map/ppermute | solution.py:308
  8.3 1.5 %collective-permute-start.2 = (bf16[4,64,256]{2,1,0:T(8,128)(2,1)S(1)}, bf16[4,64,256]{2,1,0:T(8,128)(2,1)S(1)}, u32[]{:S(2)}, u32[]{:S(2)}) collective-permute-start(bf16[4,64,256]{2,1,0:T(8,128)(2,1)S(1)} %get-tuple-element.32), channel_id=1, source_target_pairs={{0,1},{1,0},{2,3},{3,2},{4,5},{5,4},{6,7},{7,6},{8,9},{9,8},{10,11... | collective-permute-start | bytes 393224 | tf_op jit(solution)/shard_map/ppermute | solution.py:308
  9.8 0.0 collective-permute-start.3
  9.9 1.9 %collective-permute-start.12 = (bf16[4,64,256]{2,1,0:T(8,128)(2,1)S(1)}, bf16[4,64,256]{2,1,0:T(8,128)(2,1)S(1)}, u32[]{:S(2)}, u32[]{:S(2)}) collective-permute-start(bf16[4,64,256]{2,1,0:T(8,128)(2,1)S(1)} %get-tuple-element.42), channel_id=1, source_target_pairs={{0,2},{1,3},{2,0},{3,1},{4,6},{5,7},{6,4},{7,5},{8,10},{9,11},{10,... | collective-permute-start | bytes 393224 | tf_op jit(solution)/shard_map/ppermute | solution.py:308
  11.8 1.5 %collective-permute-start.13 = (bf16[4,64,256]{2,1,0:T(8,128)(2,1)S(1)}, bf16[4,64,256]{2,1,0:T(8,128)(2,1)S(1)}, u32[]{:S(2)}, u32[]{:S(2)}) collective-permute-start(bf16[4,64,256]{2,1,0:T(8,128)(2,1)S(1)} %get-tuple-element.43), channel_id=1, source_target_pairs={{0,1},{1,0},{2,3},{3,2},{4,5},{5,4},{6,7},{7,6},{8,9},{9,8},{10,11... | collective-permute-start | bytes 393224 | tf_op jit(solution)/shard_map/ppermute | solution.py:308
  13.3 0.0 collective-permute-done.1.refs_3_
  13.3 1.6 %collective-permute-start.14 = (bf16[4,64,256]{2,1,0:T(8,128)(2,1)S(1)}, bf16[4,64,256]{2,1,0:T(8,128)(2,1)S(1)}, u32[]{:S(2)}, u32[]{:S(2)}) collective-permute-start(bf16[4,64,256]{2,1,0:T(8,128)(2,1)S(1)} %get-tuple-element.44), channel_id=1, source_target_pairs={{0,3},{1,2},{2,1},{3,0},{4,7},{5,6},{6,5},{7,4},{8,11},{9,10},{10,... | collective-permute-start | bytes 393224 | tf_op jit(solution)/shard_map/ppermute | solution.py:308
  14.9 0.0 collective-permute-done.2.refs_4_
  14.9 2.3 %collective-permute-done.3.refs_5_ = bf16[4,64,256]{2,1,0:T(8,128)(2,1)S(1)} collective-permute-done((bf16[4,64,256]{2,1,0:T(8,128)(2,1)S(1)}, bf16[4,64,256]{2,1,0:T(8,128)(2,1)S(1)}, u32[]{:S(2)}, u32[]{:S(2)}) %collective-permute-start.3) | collective-permute-done | bytes 131104 | tf_op jit(solution)/shard_map/ppermute | solution.py:308
  17.2 1.3 %columns.2 = (bf16[256,256]{1,0:T(8,128)(2,1)S(1)}, bf16[256,256]{1,0:T(8,128)(2,1)S(1)}, bf16[256,256]{1,0:T(8,128)(2,1)S(1)}, bf16[256,256]{1,0:T(8,128)(2,1)S(1)}) custom-call(bf16[1024,1024]{1,0:T(8,128)(2,1)S(1)} %copy-done, bf16[4,1024,256]{2,1,0:T(8,128)(2,1)S(1)} %filters.1.refs_3_.refs_1_, bf16[4,64,256]{2,1,0:T(8,128)(2,1)S(1)} %get-tuple-element.30.refs_2_, ...), custom_call_target="tpu_custom_call" | custom-call | flops 1 | bytes 1 | tf_op jit(solution)/shard_map/columns/pallas_call | solution.py:359
  18.5 1.6 %collective-permute-start.4 = (bf16[256,256]{1,0:T(8,128)(2,1)S(1)}, bf16[256,256]{1,0:T(8,128)(2,1)S(1)}, u32[]{:S(2)}, u32[]{:S(2)}) collective-permute-start(bf16[256,256]{1,0:T(8,128)(2,1)S(1)} %get-tuple-element.36), channel_id=1, source_target_pairs={{0,4},{1,5},{2,6},{3,7},{4,0},{5,1},{6,2},{7,3},{8,12},{9,13},{10,... | collective-permute-start | bytes 393224 | tf_op jit(solution)/shard_map/ppermute | solution.py:308
  20.1 0.0 collective-permute-start.7
  20.1 0.0 collective-permute-done.12.refs_3_
  20.1 3.2 %collective-permute-start.6 = (bf16[256,256]{1,0:T(8,128)(2,1)S(1)}, bf16[256,256]{1,0:T(8,128)(2,1)S(1)}, u32[]{:S(2)}, u32[]{:S(2)}) collective-permute-start(bf16[256,256]{1,0:T(8,128)(2,1)S(1)} %get-tuple-element.37), channel_id=1, source_target_pairs={{0,4},{1,5},{2,6},{3,7},{4,0},{5,1},{6,2},{7,3},{8,12},{9,13},{10,... | collective-permute-start | bytes 393224 | tf_op jit(solution)/shard_map/ppermute | solution.py:308
  23.3 0.0 collective-permute-done.13.refs_4_
  23.3 0.0 collective-permute-done.14.refs_5_
  23.3 1.3 %columns.3 = (bf16[256,256]{1,0:T(8,128)(2,1)S(1)}, bf16[256,256]{1,0:T(8,128)(2,1)S(1)}, bf16[256,256]{1,0:T(8,128)(2,1)S(1)}, bf16[256,256]{1,0:T(8,128)(2,1)S(1)}) custom-call(bf16[1024,1024]{1,0:T(8,128)(2,1)S(1)} %copy-done, bf16[4,1024,256]{2,1,0:T(8,128)(2,1)S(1)} %filters.1.refs_3_.refs_1_, bf16[4,64,256]{2,1,0:T(8,128)(2,1)S(1)} %get-tuple-element.41.refs_2_, ...), custom_call_target="tpu_custom_call" | custom-call | flops 1 | bytes 1 | tf_op jit(solution)/shard_map/columns/pallas_call | solution.py:359
  24.6 0.4 collective-permute-start.15
  25.0 0.0 collective-permute-done.4.refs_1_.refs_2_
  25.0 0.1 far.2
  25.0 2.7 %collective-permute-start.5 = (bf16[256,256]{1,0:T(8,128)(2,1)S(1)}, bf16[256,256]{1,0:T(8,128)(2,1)S(1)}, u32[]{:S(2)}, u32[]{:S(2)}) collective-permute-start(bf16[256,256]{1,0:T(8,128)(2,1)S(1)} %far.2), channel_id=1, source_target_pairs={{0,8},{1,9},{2,10},{3,11},{4,12},{5,13},{6,14},{7,15},{8,0},{9,1},... | collective-permute-start | bytes 393224 | tf_op jit(solution)/shard_map/ppermute | solution.py:308
  27.7 0.0 collective-permute-start.18
  27.7 0.0 collective-permute-done.7.refs_4_.refs_1_
  27.7 3.4 %collective-permute-start.17 = (bf16[256,256]{1,0:T(8,128)(2,1)S(1)}, bf16[256,256]{1,0:T(8,128)(2,1)S(1)}, u32[]{:S(2)}, u32[]{:S(2)}) collective-permute-start(bf16[256,256]{1,0:T(8,128)(2,1)S(1)} %get-tuple-element.48), channel_id=1, source_target_pairs={{0,4},{1,5},{2,6},{3,7},{12,8},{13,9},{14,10},{15,11},{16,20},{17,... | collective-permute-start | bytes 393224 | tf_op jit(solution)/shard_map/ppermute | solution.py:308
  31.1 0.0 collective-permute-done.6.refs_3_.refs_0_
  31.1 0.0 collective-permute-done.15.refs_3_.refs_2_
  31.1 0.1 far.3
  31.2 1.4 %collective-permute-start.16 = (bf16[256,256]{1,0:T(8,128)(2,1)S(1)}, bf16[256,256]{1,0:T(8,128)(2,1)S(1)}, u32[]{:S(2)}, u32[]{:S(2)}) collective-permute-start(bf16[256,256]{1,0:T(8,128)(2,1)S(1)} %far.3), channel_id=1, source_target_pairs={{0,8},{1,9},{2,10},{3,11},{4,12},{5,13},{6,14},{7,15},{8,0},{9,1},... | collective-permute-start | bytes 393224 | tf_op jit(solution)/shard_map/ppermute | solution.py:308
  32.6 2.6 %collective-permute-done.5.refs_1_ = bf16[256,256]{1,0:T(8,128)(2,1)S(1)} collective-permute-done((bf16[256,256]{1,0:T(8,128)(2,1)S(1)}, bf16[256,256]{1,0:T(8,128)(2,1)S(1)}, u32[]{:S(2)}, u32[]{:S(2)}) %collective-permute-start.5) | collective-permute-done | bytes 131104 | tf_op jit(solution)/shard_map/ppermute | solution.py:308
  35.3 0.1 half.2
  35.4 0.1 collective-permute-start.8
  35.4 1.3 %collective-permute-start.9 = (bf16[128,256]{1,0:T(8,128)(2,1)S(1)}, bf16[128,256]{1,0:T(8,128)(2,1)S(1)}, u32[]{:S(2)}, u32[]{:S(2)}) collective-permute-start(bf16[128,256]{1,0:T(8,128)(2,1)S(1)} %get-tuple-element.40), channel_id=1, source_target_pairs={{0,3},{1,2},{2,1},{3,0},{4,7},{5,6},{6,5},{7,4},{8,11},{9,10},{10,... | collective-permute-start | bytes 196616 | tf_op jit(solution)/shard_map/ppermute | solution.py:308
  36.8 0.0 collective-permute-done.18.refs_4_
  36.8 2.1 %collective-permute-start.10 = (bf16[128,256]{1,0:T(8,128)(2,1)S(1)}, bf16[128,256]{1,0:T(8,128)(2,1)S(1)}, u32[]{:S(2)}, u32[]{:S(2)}) collective-permute-start(bf16[128,256]{1,0:T(8,128)(2,1)S(1)} %get-tuple-element.38.refs_1_), channel_id=1, source_target_pairs={{0,1},{1,0},{2,3},{3,2},{4,5},{5,4},{6,7},{7,6},{8,9},{9,8},{10,11... | collective-permute-start | bytes 196616 | tf_op jit(solution)/shard_map/ppermute | solution.py:308
  38.9 0.0 collective-permute-done.17.refs_3_
  38.9 2.8 %collective-permute-done.16.refs_1_ = bf16[256,256]{1,0:T(8,128)(2,1)S(1)} collective-permute-done((bf16[256,256]{1,0:T(8,128)(2,1)S(1)}, bf16[256,256]{1,0:T(8,128)(2,1)S(1)}, u32[]{:S(2)}, u32[]{:S(2)}) %collective-permute-start.16) | collective-permute-done | bytes 131104 | tf_op jit(solution)/shard_map/ppermute | solution.py:308
  41.7 0.1 half.3
  41.8 1.3 %collective-permute-start.19 = (bf16[128,256]{1,0:T(8,128)(2,1)S(1)}, bf16[128,256]{1,0:T(8,128)(2,1)S(1)}, u32[]{:S(2)}, u32[]{:S(2)}) collective-permute-start(bf16[128,256]{1,0:T(8,128)(2,1)S(1)} %get-tuple-element.50), channel_id=1, source_target_pairs={{0,2},{1,3},{2,0},{3,1},{4,6},{5,7},{6,4},{7,5},{8,10},{9,11},{10,... | collective-permute-start | bytes 196616 | tf_op jit(solution)/shard_map/ppermute | solution.py:308
  43.1 1.4 %collective-permute-start.20 = (bf16[128,256]{1,0:T(8,128)(2,1)S(1)}, bf16[128,256]{1,0:T(8,128)(2,1)S(1)}, u32[]{:S(2)}, u32[]{:S(2)}) collective-permute-start(bf16[128,256]{1,0:T(8,128)(2,1)S(1)} %get-tuple-element.51), channel_id=1, source_target_pairs={{0,3},{1,2},{2,1},{3,0},{4,7},{5,6},{6,5},{7,4},{8,11},{9,10},{10,... | collective-permute-start | bytes 196616 | tf_op jit(solution)/shard_map/ppermute | solution.py:308
  44.6 0.0 collective-permute-done.8.refs_2_
  44.6 0.0 copy-start.1
  44.6 0.9 %collective-permute-start.21 = (bf16[128,256]{1,0:T(8,128)(2,1)S(1)}, bf16[128,256]{1,0:T(8,128)(2,1)S(1)}, u32[]{:S(2)}, u32[]{:S(2)}) collective-permute-start(bf16[128,256]{1,0:T(8,128)(2,1)S(1)} %get-tuple-element.49.refs_1_), channel_id=1, source_target_pairs={{0,1},{1,0},{2,3},{3,2},{4,5},{5,4},{6,7},{7,6},{8,9},{9,8},{10,11... | collective-permute-start | bytes 196616 | tf_op jit(solution)/shard_map/ppermute | solution.py:308
  45.4 0.0 collective-permute-done.9.refs_3_
  45.5 0.0 collective-permute-done.10.refs_4_
  45.5 0.5 phase.2.refs_3_
  45.9 0.1 collective-permute-start.11
  46.0 0.1 collective-permute-done.19.refs_2_
  46.1 2.2 %collective-permute-done.20.refs_3_ = bf16[128,256]{1,0:T(8,128)(2,1)S(1)} collective-permute-done((bf16[128,256]{1,0:T(8,128)(2,1)S(1)}, bf16[128,256]{1,0:T(8,128)(2,1)S(1)}, u32[]{:S(2)}, u32[]{:S(2)}) %collective-permute-start.20) | collective-permute-done | bytes 65568 | tf_op jit(solution)/shard_map/ppermute | solution.py:308
  48.3 0.6 %collective-permute-done.21.refs_4_ = bf16[128,256]{1,0:T(8,128)(2,1)S(1)} collective-permute-done((bf16[128,256]{1,0:T(8,128)(2,1)S(1)}, bf16[128,256]{1,0:T(8,128)(2,1)S(1)}, u32[]{:S(2)}, u32[]{:S(2)}) %collective-permute-start.21) | collective-permute-done | bytes 65568 | tf_op jit(solution)/shard_map/ppermute | solution.py:308
  48.9 0.5 phase.3.refs_5_
  49.4 0.1 collective-permute-start.22
  49.5 0.0 collective-permute-done.11.refs_4_
  49.5 0.0 copy-done.1
  49.5 0.0 copy-done.2
  49.5 0.0 copy-done.3
  49.5 1.2 %recon.2 = (f32[128,512]{1,0:T(8,128)S(1)}, bf16[1024,512]{1,0:T(8,128)(2,1)S(1)}, bf16[128,128]{1,0:T(8,128)(2,1)S(1)}) custom-call(s32[1,4]{1,0:T(1,128)S(1)} %copy-done.2, s32[16]{0:T(128)S(1)} %copy-done.3, bf16[4,1024,512]{2,1,0:T(8,128)(2,1)S(1)} %copy-done.1, bf16[128,1024]{1,0:T(8,128)(2,1)S(1)} %phase.2.refs_3_, ...), custom_call_target="tpu_custom_call" | custom-call | flops 1 | bytes 1 | tf_op jit(solution)/shard_map/recon/pallas_call | solution.py:413
  50.7 0.3 collective-permute-done.22.phase
  51.0 1.1 %recon.3 = bf16[128,512]{1,0:T(8,128)(2,1)} custom-call(bf16[1024,512]{1,0:T(8,128)(2,1)S(1)} %get-tuple-element.52.weights, bf16[128,1024]{1,0:T(8,128)(2,1)S(1)} %collective-permute-done.22.phase, f32[128,512]{1,0:T(8,128)S(1)} %get-tuple-element.53.before, bf16[128,128]{1,0:T(8,128)(2,1)S(1)} %get-tuple-element.54.select), custom_call_target="tpu_custom_call" | custom-call | flops 1 | bytes 1 | tf_op jit(solution)/shard_map/recon/pallas_call | solution.py:426
  (2 shorter events, 0.0 us)
Async XLA Ops:
  0.0 3.1 %copy-start = (bf16[1024,1024]{1,0:T(8,128)(2,1)S(1)}, bf16[1024,1024]{1,0:T(8,128)(2,1)}, u32[]{:S(2)}) copy-start(bf16[1024,1024]{1,0:T(8,128)(2,1)} %constant.2.clone.refs_2_.refs_0_) | copy-start | bytes 6291460
  0.0 3.1 %collective-permute-start = (bf16[4,2,64,1024]{3,2,1,0:T(8,128)(2,1)}, bf16[4,2,64,1024]{3,2,1,0:T(8,128)(2,1)S(1)}, u32[]{:S(2)}, u32[]{:S(2)}) collective-permute-start(bf16[4,2,64,1024]{3,2,1,0:T(8,128)(2,1)} %bitcast.1), channel_id=1, source_target_pairs={{0,16},{1,17},{2,18},{3,19},{4,20},{5,21},{6,22},{7,23},{8,24},{9,... | collective-permute-start | bytes 3145736 | tf_op jit(solution)/shard_map/ppermute | solution.py:308
  5.5 7.8 %collective-permute-start.1 = (bf16[4,64,256]{2,1,0:T(8,128)(2,1)S(1)}, bf16[4,64,256]{2,1,0:T(8,128)(2,1)S(1)}, u32[]{:S(2)}, u32[]{:S(2)}) collective-permute-start(bf16[4,64,256]{2,1,0:T(8,128)(2,1)S(1)} %get-tuple-element.31), channel_id=1, source_target_pairs={{0,2},{1,3},{2,0},{3,1},{4,6},{5,7},{6,4},{7,5},{8,10},{9,11},{10,... | collective-permute-start | bytes 393224 | tf_op jit(solution)/shard_map/ppermute | solution.py:308
  8.3 6.6 %collective-permute-start.2 = (bf16[4,64,256]{2,1,0:T(8,128)(2,1)S(1)}, bf16[4,64,256]{2,1,0:T(8,128)(2,1)S(1)}, u32[]{:S(2)}, u32[]{:S(2)}) collective-permute-start(bf16[4,64,256]{2,1,0:T(8,128)(2,1)S(1)} %get-tuple-element.32), channel_id=1, source_target_pairs={{0,1},{1,0},{2,3},{3,2},{4,5},{5,4},{6,7},{7,6},{8,9},{9,8},{10,11... | collective-permute-start | bytes 393224 | tf_op jit(solution)/shard_map/ppermute | solution.py:308
  9.8 7.4 %collective-permute-start.3 = (bf16[4,64,256]{2,1,0:T(8,128)(2,1)S(1)}, bf16[4,64,256]{2,1,0:T(8,128)(2,1)S(1)}, u32[]{:S(2)}, u32[]{:S(2)}) collective-permute-start(bf16[4,64,256]{2,1,0:T(8,128)(2,1)S(1)} %get-tuple-element.33), channel_id=1, source_target_pairs={{0,3},{1,2},{2,1},{3,0},{4,7},{5,6},{6,5},{7,4},{8,11},{9,10},{10,... | collective-permute-start | bytes 393224 | tf_op jit(solution)/shard_map/ppermute | solution.py:308
  9.9 10.3 %collective-permute-start.12 = (bf16[4,64,256]{2,1,0:T(8,128)(2,1)S(1)}, bf16[4,64,256]{2,1,0:T(8,128)(2,1)S(1)}, u32[]{:S(2)}, u32[]{:S(2)}) collective-permute-start(bf16[4,64,256]{2,1,0:T(8,128)(2,1)S(1)} %get-tuple-element.42), channel_id=1, source_target_pairs={{0,2},{1,3},{2,0},{3,1},{4,6},{5,7},{6,4},{7,5},{8,10},{9,11},{10,... | collective-permute-start | bytes 393224 | tf_op jit(solution)/shard_map/ppermute | solution.py:308
  11.8 11.5 %collective-permute-start.13 = (bf16[4,64,256]{2,1,0:T(8,128)(2,1)S(1)}, bf16[4,64,256]{2,1,0:T(8,128)(2,1)S(1)}, u32[]{:S(2)}, u32[]{:S(2)}) collective-permute-start(bf16[4,64,256]{2,1,0:T(8,128)(2,1)S(1)} %get-tuple-element.43), channel_id=1, source_target_pairs={{0,1},{1,0},{2,3},{3,2},{4,5},{5,4},{6,7},{7,6},{8,9},{9,8},{10,11... | collective-permute-start | bytes 393224 | tf_op jit(solution)/shard_map/ppermute | solution.py:308
  13.3 10.0 %collective-permute-start.14 = (bf16[4,64,256]{2,1,0:T(8,128)(2,1)S(1)}, bf16[4,64,256]{2,1,0:T(8,128)(2,1)S(1)}, u32[]{:S(2)}, u32[]{:S(2)}) collective-permute-start(bf16[4,64,256]{2,1,0:T(8,128)(2,1)S(1)} %get-tuple-element.44), channel_id=1, source_target_pairs={{0,3},{1,2},{2,1},{3,0},{4,7},{5,6},{6,5},{7,4},{8,11},{9,10},{10,... | collective-permute-start | bytes 393224 | tf_op jit(solution)/shard_map/ppermute | solution.py:308
  18.5 6.5 %collective-permute-start.4 = (bf16[256,256]{1,0:T(8,128)(2,1)S(1)}, bf16[256,256]{1,0:T(8,128)(2,1)S(1)}, u32[]{:S(2)}, u32[]{:S(2)}) collective-permute-start(bf16[256,256]{1,0:T(8,128)(2,1)S(1)} %get-tuple-element.36), channel_id=1, source_target_pairs={{0,4},{1,5},{2,6},{3,7},{4,0},{5,1},{6,2},{7,3},{8,12},{9,13},{10,... | collective-permute-start | bytes 393224 | tf_op jit(solution)/shard_map/ppermute | solution.py:308
  20.1 7.6 %collective-permute-start.7 = (bf16[256,256]{1,0:T(8,128)(2,1)S(1)}, bf16[256,256]{1,0:T(8,128)(2,1)S(1)}, u32[]{:S(2)}, u32[]{:S(2)}) collective-permute-start(bf16[256,256]{1,0:T(8,128)(2,1)S(1)} %get-tuple-element.37), channel_id=1, source_target_pairs={{0,16},{1,17},{2,18},{3,19},{4,8},{5,9},{6,10},{7,11},{8,4},{9,5},... | collective-permute-start | bytes 393224 | tf_op jit(solution)/shard_map/ppermute | solution.py:308
  20.1 11.0 %collective-permute-start.6 = (bf16[256,256]{1,0:T(8,128)(2,1)S(1)}, bf16[256,256]{1,0:T(8,128)(2,1)S(1)}, u32[]{:S(2)}, u32[]{:S(2)}) collective-permute-start(bf16[256,256]{1,0:T(8,128)(2,1)S(1)} %get-tuple-element.37), channel_id=1, source_target_pairs={{0,4},{1,5},{2,6},{3,7},{4,0},{5,1},{6,2},{7,3},{8,12},{9,13},{10,... | collective-permute-start | bytes 393224 | tf_op jit(solution)/shard_map/ppermute | solution.py:308
  24.6 6.5 %collective-permute-start.15 = (bf16[256,256]{1,0:T(8,128)(2,1)S(1)}, bf16[256,256]{1,0:T(8,128)(2,1)S(1)}, u32[]{:S(2)}, u32[]{:S(2)}) collective-permute-start(bf16[256,256]{1,0:T(8,128)(2,1)S(1)} %get-tuple-element.47), channel_id=1, source_target_pairs={{0,4},{1,5},{2,6},{3,7},{4,0},{5,1},{6,2},{7,3},{8,12},{9,13},{10,... | collective-permute-start | bytes 393224 | tf_op jit(solution)/shard_map/ppermute | solution.py:308
  25.0 10.2 %collective-permute-start.5 = (bf16[256,256]{1,0:T(8,128)(2,1)S(1)}, bf16[256,256]{1,0:T(8,128)(2,1)S(1)}, u32[]{:S(2)}, u32[]{:S(2)}) collective-permute-start(bf16[256,256]{1,0:T(8,128)(2,1)S(1)} %far.2), channel_id=1, source_target_pairs={{0,8},{1,9},{2,10},{3,11},{4,12},{5,13},{6,14},{7,15},{8,0},{9,1},... | collective-permute-start | bytes 393224 | tf_op jit(solution)/shard_map/ppermute | solution.py:308
  27.7 9.1 %collective-permute-start.18 = (bf16[256,256]{1,0:T(8,128)(2,1)S(1)}, bf16[256,256]{1,0:T(8,128)(2,1)S(1)}, u32[]{:S(2)}, u32[]{:S(2)}) collective-permute-start(bf16[256,256]{1,0:T(8,128)(2,1)S(1)} %get-tuple-element.48), channel_id=1, source_target_pairs={{0,16},{1,17},{2,18},{3,19},{4,8},{5,9},{6,10},{7,11},{8,4},{9,5},... | collective-permute-start | bytes 393224 | tf_op jit(solution)/shard_map/ppermute | solution.py:308
  27.7 11.2 %collective-permute-start.17 = (bf16[256,256]{1,0:T(8,128)(2,1)S(1)}, bf16[256,256]{1,0:T(8,128)(2,1)S(1)}, u32[]{:S(2)}, u32[]{:S(2)}) collective-permute-start(bf16[256,256]{1,0:T(8,128)(2,1)S(1)} %get-tuple-element.48), channel_id=1, source_target_pairs={{0,4},{1,5},{2,6},{3,7},{12,8},{13,9},{14,10},{15,11},{16,20},{17,... | collective-permute-start | bytes 393224 | tf_op jit(solution)/shard_map/ppermute | solution.py:308
  31.2 10.5 %collective-permute-start.16 = (bf16[256,256]{1,0:T(8,128)(2,1)S(1)}, bf16[256,256]{1,0:T(8,128)(2,1)S(1)}, u32[]{:S(2)}, u32[]{:S(2)}) collective-permute-start(bf16[256,256]{1,0:T(8,128)(2,1)S(1)} %far.3), channel_id=1, source_target_pairs={{0,8},{1,9},{2,10},{3,11},{4,12},{5,13},{6,14},{7,15},{8,0},{9,1},... | collective-permute-start | bytes 393224 | tf_op jit(solution)/shard_map/ppermute | solution.py:308
  35.4 9.2 %collective-permute-start.8 = (bf16[128,256]{1,0:T(8,128)(2,1)S(1)}, bf16[128,256]{1,0:T(8,128)(2,1)S(1)}, u32[]{:S(2)}, u32[]{:S(2)}) collective-permute-start(bf16[128,256]{1,0:T(8,128)(2,1)S(1)} %get-tuple-element.39), channel_id=1, source_target_pairs={{0,2},{1,3},{2,0},{3,1},{4,6},{5,7},{6,4},{7,5},{8,10},{9,11},{10,... | collective-permute-start | bytes 196616 | tf_op jit(solution)/shard_map/ppermute | solution.py:308
  35.4 10.0 %collective-permute-start.9 = (bf16[128,256]{1,0:T(8,128)(2,1)S(1)}, bf16[128,256]{1,0:T(8,128)(2,1)S(1)}, u32[]{:S(2)}, u32[]{:S(2)}) collective-permute-start(bf16[128,256]{1,0:T(8,128)(2,1)S(1)} %get-tuple-element.40), channel_id=1, source_target_pairs={{0,3},{1,2},{2,1},{3,0},{4,7},{5,6},{6,5},{7,4},{8,11},{9,10},{10,... | collective-permute-start | bytes 196616 | tf_op jit(solution)/shard_map/ppermute | solution.py:308
  36.8 8.7 %collective-permute-start.10 = (bf16[128,256]{1,0:T(8,128)(2,1)S(1)}, bf16[128,256]{1,0:T(8,128)(2,1)S(1)}, u32[]{:S(2)}, u32[]{:S(2)}) collective-permute-start(bf16[128,256]{1,0:T(8,128)(2,1)S(1)} %get-tuple-element.38.refs_1_), channel_id=1, source_target_pairs={{0,1},{1,0},{2,3},{3,2},{4,5},{5,4},{6,7},{7,6},{8,9},{9,8},{10,11... | collective-permute-start | bytes 196616 | tf_op jit(solution)/shard_map/ppermute | solution.py:308
  41.8 4.3 %collective-permute-start.19 = (bf16[128,256]{1,0:T(8,128)(2,1)S(1)}, bf16[128,256]{1,0:T(8,128)(2,1)S(1)}, u32[]{:S(2)}, u32[]{:S(2)}) collective-permute-start(bf16[128,256]{1,0:T(8,128)(2,1)S(1)} %get-tuple-element.50), channel_id=1, source_target_pairs={{0,2},{1,3},{2,0},{3,1},{4,6},{5,7},{6,4},{7,5},{8,10},{9,11},{10,... | collective-permute-start | bytes 196616 | tf_op jit(solution)/shard_map/ppermute | solution.py:308
  43.1 5.2 %collective-permute-start.20 = (bf16[128,256]{1,0:T(8,128)(2,1)S(1)}, bf16[128,256]{1,0:T(8,128)(2,1)S(1)}, u32[]{:S(2)}, u32[]{:S(2)}) collective-permute-start(bf16[128,256]{1,0:T(8,128)(2,1)S(1)} %get-tuple-element.51), channel_id=1, source_target_pairs={{0,3},{1,2},{2,1},{3,0},{4,7},{5,6},{6,5},{7,4},{8,11},{9,10},{10,... | collective-permute-start | bytes 196616 | tf_op jit(solution)/shard_map/ppermute | solution.py:308
  44.6 4.9 %copy-start.1 = (bf16[4,1024,512]{2,1,0:T(8,128)(2,1)S(1)}, bf16[4,1024,512]{2,1,0:T(8,128)(2,1)}, u32[]{:S(2)}) copy-start(bf16[4,1024,512]{2,1,0:T(8,128)(2,1)} %refs_2_.2) | copy-start | bytes 12582916
  44.6 4.9 %copy-start.2 = (s32[1,4]{1,0:T(1,128)S(1)}, s32[1,4]{1,0:T(1,128)}, u32[]{:S(2)}) copy-start(s32[1,4]{1,0:T(1,128)} %refs_0_.7) | copy-start | bytes 52
  44.6 4.9 %copy-start.3 = (s32[16]{0:T(128)S(1)}, s32[16]{0:T(128)}, u32[]{:S(2)}) copy-start(s32[16]{0:T(128)} %refs_1_.1) | copy-start | bytes 196
  44.6 4.3 %collective-permute-start.21 = (bf16[128,256]{1,0:T(8,128)(2,1)S(1)}, bf16[128,256]{1,0:T(8,128)(2,1)S(1)}, u32[]{:S(2)}, u32[]{:S(2)}) collective-permute-start(bf16[128,256]{1,0:T(8,128)(2,1)S(1)} %get-tuple-element.49.refs_1_), channel_id=1, source_target_pairs={{0,1},{1,0},{2,3},{3,2},{4,5},{5,4},{6,7},{7,6},{8,9},{9,8},{10,11... | collective-permute-start | bytes 196616 | tf_op jit(solution)/shard_map/ppermute | solution.py:308
  45.9 3.6 %collective-permute-start.11 = (bf16[128,1024]{1,0:T(8,128)(2,1)S(1)}, bf16[128,1024]{1,0:T(8,128)(2,1)S(1)}, u32[]{:S(2)}, u32[]{:S(2)}) collective-permute-start(bf16[128,1024]{1,0:T(8,128)(2,1)S(1)} %phase.2.refs_3_), channel_id=1, source_target_pairs={{0,16},{1,17},{2,18},{3,19},{4,20},{5,21},{6,22},{7,23},{8,24},{9,... | collective-permute-start | bytes 786440 | tf_op jit(solution)/shard_map/ppermute | solution.py:308
  49.4 1.6 %collective-permute-start.22 = (bf16[128,1024]{1,0:T(8,128)(2,1)S(1)}, bf16[128,1024]{1,0:T(8,128)(2,1)S(1)}, u32[]{:S(2)}, u32[]{:S(2)}) collective-permute-start(bf16[128,1024]{1,0:T(8,128)(2,1)S(1)} %phase.3.refs_5_), channel_id=1, source_target_pairs={{0,16},{1,17},{2,18},{3,19},{4,20},{5,21},{6,22},{7,23},{8,24},{9,... | collective-permute-start | bytes 786440 | tf_op jit(solution)/shard_map/ppermute | solution.py:308

commit v31 on v27

--- a/solution.py
+++ b/solution.py
@@ -13,7 +13,7 @@
 bf16 = jnp.bfloat16
 f32 = jnp.float32
 send_order = (0, 2, 1, 3)
-tail_order = (0, 2, 3, 1)
+tail_order = (0, 3, 2, 1)
 
 
 def hartley(length):

time: 51.7 us -> 51.7 us (level)
  no operation moved by 1% of the time
where the time goes in v31:
time: 51.7 us; the launch traced here: 51.5 us
  starting transfers between devices  29.8 us (58%)
  waiting for transfers between devices  10.9 us (21%)
  Pallas kernels  10.6 us (21%)
    ppermute x23, starting transfers between devices, sent(): return lax.ppermute(value, ('dist', 'rows'), pairs)  29.8 us
    ppermute x23, waiting for transfers between devices, sent(): return lax.ppermute(value, ('dist', 'rows'), pairs)  10.9 us
    pallas_call x1, Pallas kernels, plane_plan(): pl.pallas_call(lambda *refs: filter_kernel(inner, dist_dev, *refs), out_s...  2.62 us
    pallas_call x2, Pallas kernels, plane_plan(): pl.pallas_call(lambda *refs: column_kernel(inner, outer, *refs), out_shap...  2.59 us
    pallas_call x1, Pallas kernels, plane_plan(): pl.pallas_call(lambda *refs: row_kernel(inner, *refs), out_shape=[shaped(...  1.83 us
    pallas_call x1, Pallas kernels, plane_plan(): pl.pallas_call(lambda *refs: recon_kernel(own, *refs), out_shape=[jax.Sha...  1.2 us
    pallas_call x1, Pallas kernels, plane_plan(): pl.pallas_call(recon_last_kernel, out_shape=shaped(capacity, pixels), in_...  1.13 us
  transfers between devices with their start and end apart: 23, of which 7 were waited for; matrix products, arithmetic and copies ran while one was open for 0% of the time, Pallas kernels for 15%

profile of v31, /device:TPU:0, one launch (start us, length us, event | category | flops | bytes accessed | tf_op | source)
XLA Modules:
  0.0 51.5 jit_solution(17772055170633195198)
XLA Ops:
  0.0 0.5 collective-permute-start
  0.5 2.6 %filters.1.refs_3_.refs_1_ = bf16[4,1024,256]{2,1,0:T(8,128)(2,1)S(1)} custom-call(f32[4]{0:T(128)} %refs_0_.6), custom_call_target="tpu_custom_call" | custom-call | flops 1 | bytes 1 | tf_op jit(solution)/shard_map/filters/pallas_call | solution.py:321
  3.1 0.0 collective-permute-done.refs_1_
  3.1 0.0 copy-done
  3.1 1.8 %row_spectra.1 = (bf16[4,64,256]{2,1,0:T(8,128)(2,1)S(1)}, bf16[4,64,256]{2,1,0:T(8,128)(2,1)S(1)}, bf16[4,64,256]{2,1,0:T(8,128)(2,1)S(1)}, bf16[4,64,256]{2,1,...) custom-call(bf16[4,2,64,1024]{3,2,1,0:T(8,128)(2,1)} %bitcast.2, ...), custom_call_target="tpu_custom_call" | custom-call | flops 1 | bytes 1 | tf_op jit(solution)/shard_map/row_spectra/pallas_call | solution.py:330
  4.9 2.8 %collective-permute-start.1 = (bf16[4,64,256]{2,1,0:T(8,128)(2,1)S(1)}, bf16[4,64,256]{2,1,0:T(8,128)(2,1)S(1)}, u32[]{:S(2)}, u32[]{:S(2)}) collective-permute-start(bf16[4,64,256]{2,1,0:T(8,128)(2,1)S(1)} %get-tuple-element.31), channel_id=1, source_target_pairs={{0,2},{1,3},{2,0},{3,1},{4,6},{5,7},{6,4},{7,5},{8,10},{9,11},{10,... | collective-permute-start | bytes 393224 | tf_op jit(solution)/shard_map/ppermute | solution.py:298
  7.7 1.5 %collective-permute-start.2 = (bf16[4,64,256]{2,1,0:T(8,128)(2,1)S(1)}, bf16[4,64,256]{2,1,0:T(8,128)(2,1)S(1)}, u32[]{:S(2)}, u32[]{:S(2)}) collective-permute-start(bf16[4,64,256]{2,1,0:T(8,128)(2,1)S(1)} %get-tuple-element.32), channel_id=1, source_target_pairs={{0,1},{1,0},{2,3},{3,2},{4,5},{5,4},{6,7},{7,6},{8,9},{9,8},{10,11... | collective-permute-start | bytes 393224 | tf_op jit(solution)/shard_map/ppermute | solution.py:298
  9.2 0.0 collective-permute-start.3
  9.3 1.9 %collective-permute-start.12 = (bf16[4,64,256]{2,1,0:T(8,128)(2,1)S(1)}, bf16[4,64,256]{2,1,0:T(8,128)(2,1)S(1)}, u32[]{:S(2)}, u32[]{:S(2)}) collective-permute-start(bf16[4,64,256]{2,1,0:T(8,128)(2,1)S(1)} %get-tuple-element.42), channel_id=1, source_target_pairs={{0,2},{1,3},{2,0},{3,1},{4,6},{5,7},{6,4},{7,5},{8,10},{9,11},{10,... | collective-permute-start | bytes 393224 | tf_op jit(solution)/shard_map/ppermute | solution.py:298
  11.2 1.5 %collective-permute-start.13 = (bf16[4,64,256]{2,1,0:T(8,128)(2,1)S(1)}, bf16[4,64,256]{2,1,0:T(8,128)(2,1)S(1)}, u32[]{:S(2)}, u32[]{:S(2)}) collective-permute-start(bf16[4,64,256]{2,1,0:T(8,128)(2,1)S(1)} %get-tuple-element.43), channel_id=1, source_target_pairs={{0,1},{1,0},{2,3},{3,2},{4,5},{5,4},{6,7},{7,6},{8,9},{9,8},{10,11... | collective-permute-start | bytes 393224 | tf_op jit(solution)/shard_map/ppermute | solution.py:298
  12.7 0.0 collective-permute-done.1.refs_3_
  12.7 1.6 %collective-permute-start.14 = (bf16[4,64,256]{2,1,0:T(8,128)(2,1)S(1)}, bf16[4,64,256]{2,1,0:T(8,128)(2,1)S(1)}, u32[]{:S(2)}, u32[]{:S(2)}) collective-permute-start(bf16[4,64,256]{2,1,0:T(8,128)(2,1)S(1)} %get-tuple-element.44), channel_id=1, source_target_pairs={{0,3},{1,2},{2,1},{3,0},{4,7},{5,6},{6,5},{7,4},{8,11},{9,10},{10,... | collective-permute-start | bytes 393224 | tf_op jit(solution)/shard_map/ppermute | solution.py:298
  14.3 0.0 collective-permute-done.2.refs_4_
  14.3 2.3 %collective-permute-done.3.refs_5_ = bf16[4,64,256]{2,1,0:T(8,128)(2,1)S(1)} collective-permute-done((bf16[4,64,256]{2,1,0:T(8,128)(2,1)S(1)}, bf16[4,64,256]{2,1,0:T(8,128)(2,1)S(1)}, u32[]{:S(2)}, u32[]{:S(2)}) %collective-permute-start.3) | collective-permute-done | bytes 131104 | tf_op jit(solution)/shard_map/ppermute | solution.py:298
  16.6 1.3 %columns.2 = (bf16[256,256]{1,0:T(8,128)(2,1)S(1)}, bf16[256,256]{1,0:T(8,128)(2,1)S(1)}, bf16[256,256]{1,0:T(8,128)(2,1)S(1)}, bf16[256,256]{1,0:T(8,128)(2,1)S(1)}) custom-call(bf16[1024,1024]{1,0:T(8,128)(2,1)S(1)} %copy-done, bf16[4,1024,256]{2,1,0:T(8,128)(2,1)S(1)} %filters.1.refs_3_.refs_1_, bf16[4,64,256]{2,1,0:T(8,128)(2,1)S(1)} %get-tuple-element.30.refs_2_, ...), custom_call_target="tpu_custom_call" | custom-call | flops 1 | bytes 1 | tf_op jit(solution)/shard_map/columns/pallas_call | solution.py:349
  17.9 1.6 %collective-permute-start.4 = (bf16[256,256]{1,0:T(8,128)(2,1)S(1)}, bf16[256,256]{1,0:T(8,128)(2,1)S(1)}, u32[]{:S(2)}, u32[]{:S(2)}) collective-permute-start(bf16[256,256]{1,0:T(8,128)(2,1)S(1)} %get-tuple-element.36), channel_id=1, source_target_pairs={{0,4},{1,5},{2,6},{3,7},{4,0},{5,1},{6,2},{7,3},{8,12},{9,13},{10,... | collective-permute-start | bytes 393224 | tf_op jit(solution)/shard_map/ppermute | solution.py:298
  19.5 0.0 collective-permute-start.7
  19.5 0.0 collective-permute-done.12.refs_3_
  19.5 3.2 %collective-permute-start.6 = (bf16[256,256]{1,0:T(8,128)(2,1)S(1)}, bf16[256,256]{1,0:T(8,128)(2,1)S(1)}, u32[]{:S(2)}, u32[]{:S(2)}) collective-permute-start(bf16[256,256]{1,0:T(8,128)(2,1)S(1)} %get-tuple-element.37), channel_id=1, source_target_pairs={{0,4},{1,5},{2,6},{3,7},{4,0},{5,1},{6,2},{7,3},{8,12},{9,13},{10,... | collective-permute-start | bytes 393224 | tf_op jit(solution)/shard_map/ppermute | solution.py:298
  22.7 0.0 collective-permute-done.13.refs_4_
  22.7 0.0 collective-permute-done.14.refs_5_
  22.7 1.3 %columns.3 = (bf16[256,256]{1,0:T(8,128)(2,1)S(1)}, bf16[256,256]{1,0:T(8,128)(2,1)S(1)}, bf16[256,256]{1,0:T(8,128)(2,1)S(1)}, bf16[256,256]{1,0:T(8,128)(2,1)S(1)}) custom-call(bf16[1024,1024]{1,0:T(8,128)(2,1)S(1)} %copy-done, bf16[4,1024,256]{2,1,0:T(8,128)(2,1)S(1)} %filters.1.refs_3_.refs_1_, bf16[4,64,256]{2,1,0:T(8,128)(2,1)S(1)} %get-tuple-element.41.refs_2_, ...), custom_call_target="tpu_custom_call" | custom-call | flops 1 | bytes 1 | tf_op jit(solution)/shard_map/columns/pallas_call | solution.py:349
  24.0 0.4 collective-permute-start.15
  24.4 0.0 collective-permute-done.4.refs_1_.refs_2_
  24.4 0.1 far.2
  24.4 2.7 %collective-permute-start.5 = (bf16[256,256]{1,0:T(8,128)(2,1)S(1)}, bf16[256,256]{1,0:T(8,128)(2,1)S(1)}, u32[]{:S(2)}, u32[]{:S(2)}) collective-permute-start(bf16[256,256]{1,0:T(8,128)(2,1)S(1)} %far.2), channel_id=1, source_target_pairs={{0,8},{1,9},{2,10},{3,11},{4,12},{5,13},{6,14},{7,15},{8,0},{9,1},... | collective-permute-start | bytes 393224 | tf_op jit(solution)/shard_map/ppermute | solution.py:298
  27.1 0.0 collective-permute-start.18
  27.1 0.0 collective-permute-done.7.refs_4_.refs_1_
  27.1 3.4 %collective-permute-start.17 = (bf16[256,256]{1,0:T(8,128)(2,1)S(1)}, bf16[256,256]{1,0:T(8,128)(2,1)S(1)}, u32[]{:S(2)}, u32[]{:S(2)}) collective-permute-start(bf16[256,256]{1,0:T(8,128)(2,1)S(1)} %get-tuple-element.48), channel_id=1, source_target_pairs={{0,4},{1,5},{2,6},{3,7},{12,8},{13,9},{14,10},{15,11},{16,20},{17,... | collective-permute-start | bytes 393224 | tf_op jit(solution)/shard_map/ppermute | solution.py:298
  30.5 0.0 collective-permute-done.6.refs_3_.refs_0_
  30.5 0.0 collective-permute-done.15.refs_3_.refs_2_
  30.5 0.1 far.3
  30.6 1.4 %collective-permute-start.16 = (bf16[256,256]{1,0:T(8,128)(2,1)S(1)}, bf16[256,256]{1,0:T(8,128)(2,1)S(1)}, u32[]{:S(2)}, u32[]{:S(2)}) collective-permute-start(bf16[256,256]{1,0:T(8,128)(2,1)S(1)} %far.3), channel_id=1, source_target_pairs={{0,8},{1,9},{2,10},{3,11},{4,12},{5,13},{6,14},{7,15},{8,0},{9,1},... | collective-permute-start | bytes 393224 | tf_op jit(solution)/shard_map/ppermute | solution.py:298
  32.0 2.6 %collective-permute-done.5.refs_1_ = bf16[256,256]{1,0:T(8,128)(2,1)S(1)} collective-permute-done((bf16[256,256]{1,0:T(8,128)(2,1)S(1)}, bf16[256,256]{1,0:T(8,128)(2,1)S(1)}, u32[]{:S(2)}, u32[]{:S(2)}) %collective-permute-start.5) | collective-permute-done | bytes 131104 | tf_op jit(solution)/shard_map/ppermute | solution.py:298
  34.6 0.1 half.2
  34.7 0.9 %collective-permute-start.8 = (bf16[128,256]{1,0:T(8,128)(2,1)S(1)}, bf16[128,256]{1,0:T(8,128)(2,1)S(1)}, u32[]{:S(2)}, u32[]{:S(2)}) collective-permute-start(bf16[128,256]{1,0:T(8,128)(2,1)S(1)} %get-tuple-element.39), channel_id=1, source_target_pairs={{0,3},{1,2},{2,1},{3,0},{4,7},{5,6},{6,5},{7,4},{8,11},{9,10},{10,... | collective-permute-start | bytes 196616 | tf_op jit(solution)/shard_map/ppermute | solution.py:298
  35.7 0.6 %collective-permute-start.9 = (bf16[128,256]{1,0:T(8,128)(2,1)S(1)}, bf16[128,256]{1,0:T(8,128)(2,1)S(1)}, u32[]{:S(2)}, u32[]{:S(2)}) collective-permute-start(bf16[128,256]{1,0:T(8,128)(2,1)S(1)} %get-tuple-element.40), channel_id=1, source_target_pairs={{0,2},{1,3},{2,0},{3,1},{4,6},{5,7},{6,4},{7,5},{8,10},{9,11},{10,... | collective-permute-start | bytes 196616 | tf_op jit(solution)/shard_map/ppermute | solution.py:298
  36.2 0.0 collective-permute-done.18.refs_4_
  36.2 2.1 %collective-permute-start.10 = (bf16[128,256]{1,0:T(8,128)(2,1)S(1)}, bf16[128,256]{1,0:T(8,128)(2,1)S(1)}, u32[]{:S(2)}, u32[]{:S(2)}) collective-permute-start(bf16[128,256]{1,0:T(8,128)(2,1)S(1)} %get-tuple-element.38.refs_1_), channel_id=1, source_target_pairs={{0,1},{1,0},{2,3},{3,2},{4,5},{5,4},{6,7},{7,6},{8,9},{9,8},{10,11... | collective-permute-start | bytes 196616 | tf_op jit(solution)/shard_map/ppermute | solution.py:298
  38.3 0.0 collective-permute-done.17.refs_3_
  38.3 2.8 %collective-permute-done.16.refs_1_ = bf16[256,256]{1,0:T(8,128)(2,1)S(1)} collective-permute-done((bf16[256,256]{1,0:T(8,128)(2,1)S(1)}, bf16[256,256]{1,0:T(8,128)(2,1)S(1)}, u32[]{:S(2)}, u32[]{:S(2)}) %collective-permute-start.16) | collective-permute-done | bytes 131104 | tf_op jit(solution)/shard_map/ppermute | solution.py:298
  41.1 0.1 half.3
  41.2 2.3 %collective-permute-start.19 = (bf16[128,256]{1,0:T(8,128)(2,1)S(1)}, bf16[128,256]{1,0:T(8,128)(2,1)S(1)}, u32[]{:S(2)}, u32[]{:S(2)}) collective-permute-start(bf16[128,256]{1,0:T(8,128)(2,1)S(1)} %get-tuple-element.50), channel_id=1, source_target_pairs={{0,3},{1,2},{2,1},{3,0},{4,7},{5,6},{6,5},{7,4},{8,11},{9,10},{10,... | collective-permute-start | bytes 196616 | tf_op jit(solution)/shard_map/ppermute | solution.py:298
  43.5 0.5 %collective-permute-start.20 = (bf16[128,256]{1,0:T(8,128)(2,1)S(1)}, bf16[128,256]{1,0:T(8,128)(2,1)S(1)}, u32[]{:S(2)}, u32[]{:S(2)}) collective-permute-start(bf16[128,256]{1,0:T(8,128)(2,1)S(1)} %get-tuple-element.51), channel_id=1, source_target_pairs={{0,2},{1,3},{2,0},{3,1},{4,6},{5,7},{6,4},{7,5},{8,10},{9,11},{10,... | collective-permute-start | bytes 196616 | tf_op jit(solution)/shard_map/ppermute | solution.py:298
  44.0 0.0 collective-permute-done.8.refs_2_
  44.0 0.0 copy-start.1
  44.0 0.0 copy-start.2
  44.0 0.8 %collective-permute-start.21 = (bf16[128,256]{1,0:T(8,128)(2,1)S(1)}, bf16[128,256]{1,0:T(8,128)(2,1)S(1)}, u32[]{:S(2)}, u32[]{:S(2)}) collective-permute-start(bf16[128,256]{1,0:T(8,128)(2,1)S(1)} %get-tuple-element.49.refs_1_), channel_id=1, source_target_pairs={{0,1},{1,0},{2,3},{3,2},{4,5},{5,4},{6,7},{7,6},{8,9},{9,8},{10,11... | collective-permute-start | bytes 196616 | tf_op jit(solution)/shard_map/ppermute | solution.py:298
  44.9 0.0 collective-permute-done.9.refs_3_
  44.9 0.0 collective-permute-done.10.refs_4_
  44.9 0.5 phase.2.refs_3_
  45.3 0.1 collective-permute-start.11
  45.4 1.4 %collective-permute-done.19.refs_2_ = bf16[128,256]{1,0:T(8,128)(2,1)S(1)} collective-permute-done((bf16[128,256]{1,0:T(8,128)(2,1)S(1)}, bf16[128,256]{1,0:T(8,128)(2,1)S(1)}, u32[]{:S(2)}, u32[]{:S(2)}) %collective-permute-start.19) | collective-permute-done | bytes 65568 | tf_op jit(solution)/shard_map/ppermute | solution.py:298
  46.8 1.0 %collective-permute-done.20.refs_3_ = bf16[128,256]{1,0:T(8,128)(2,1)S(1)} collective-permute-done((bf16[128,256]{1,0:T(8,128)(2,1)S(1)}, bf16[128,256]{1,0:T(8,128)(2,1)S(1)}, u32[]{:S(2)}, u32[]{:S(2)}) %collective-permute-start.20) | collective-permute-done | bytes 65568 | tf_op jit(solution)/shard_map/ppermute | solution.py:298
  47.7 0.6 %collective-permute-done.21.refs_4_ = bf16[128,256]{1,0:T(8,128)(2,1)S(1)} collective-permute-done((bf16[128,256]{1,0:T(8,128)(2,1)S(1)}, bf16[128,256]{1,0:T(8,128)(2,1)S(1)}, u32[]{:S(2)}, u32[]{:S(2)}) %collective-permute-start.21) | collective-permute-done | bytes 65568 | tf_op jit(solution)/shard_map/ppermute | solution.py:298
  48.3 0.5 phase.3.refs_5_
  48.8 0.1 collective-permute-start.22
  48.9 0.0 collective-permute-done.11.refs_4_
  48.9 0.0 copy-done.1
  48.9 0.0 copy-done.2
  48.9 0.0 copy-done.3
  48.9 1.2 %recon.2 = (f32[128,512]{1,0:T(8,128)S(1)}, bf16[1024,512]{1,0:T(8,128)(2,1)S(1)}, bf16[128,128]{1,0:T(8,128)(2,1)S(1)}) custom-call(s32[1,4]{1,0:T(1,128)S(1)} %copy-done.2, s32[16]{0:T(128)S(1)} %copy-done.3, bf16[4,1024,512]{2,1,0:T(8,128)(2,1)S(1)} %copy-done.1, bf16[128,1024]{1,0:T(8,128)(2,1)S(1)} %phase.2.refs_3_, ...), custom_call_target="tpu_custom_call" | custom-call | flops 1 | bytes 1 | tf_op jit(solution)/shard_map/recon/pallas_call | solution.py:403
  50.1 0.3 collective-permute-done.22.phase
  50.4 1.1 %recon.3 = bf16[128,512]{1,0:T(8,128)(2,1)} custom-call(bf16[1024,512]{1,0:T(8,128)(2,1)S(1)} %get-tuple-element.52.weights, bf16[128,1024]{1,0:T(8,128)(2,1)S(1)} %collective-permute-done.22.phase, f32[128,512]{1,0:T(8,128)S(1)} %get-tuple-element.53.before, bf16[128,128]{1,0:T(8,128)(2,1)S(1)} %get-tuple-element.54.select), custom_call_target="tpu_custom_call" | custom-call | flops 1 | bytes 1 | tf_op jit(solution)/shard_map/recon/pallas_call | solution.py:416
  (2 shorter events, 0.0 us)
Async XLA Ops:
  0.0 3.1 %copy-start = (bf16[1024,1024]{1,0:T(8,128)(2,1)S(1)}, bf16[1024,1024]{1,0:T(8,128)(2,1)}, u32[]{:S(2)}) copy-start(bf16[1024,1024]{1,0:T(8,128)(2,1)} %constant.2.clone.refs_2_.refs_0_) | copy-start | bytes 6291460
  0.0 3.1 %collective-permute-start = (bf16[4,2,64,1024]{3,2,1,0:T(8,128)(2,1)}, bf16[4,2,64,1024]{3,2,1,0:T(8,128)(2,1)S(1)}, u32[]{:S(2)}, u32[]{:S(2)}) collective-permute-start(bf16[4,2,64,1024]{3,2,1,0:T(8,128)(2,1)} %bitcast.1), channel_id=1, source_target_pairs={{0,16},{1,17},{2,18},{3,19},{4,20},{5,21},{6,22},{7,23},{8,24},{9,... | collective-permute-start | bytes 3145736 | tf_op jit(solution)/shard_map/ppermute | solution.py:298
  4.9 7.8 %collective-permute-start.1 = (bf16[4,64,256]{2,1,0:T(8,128)(2,1)S(1)}, bf16[4,64,256]{2,1,0:T(8,128)(2,1)S(1)}, u32[]{:S(2)}, u32[]{:S(2)}) collective-permute-start(bf16[4,64,256]{2,1,0:T(8,128)(2,1)S(1)} %get-tuple-element.31), channel_id=1, source_target_pairs={{0,2},{1,3},{2,0},{3,1},{4,6},{5,7},{6,4},{7,5},{8,10},{9,11},{10,... | collective-permute-start | bytes 393224 | tf_op jit(solution)/shard_map/ppermute | solution.py:298
  7.7 6.6 %collective-permute-start.2 = (bf16[4,64,256]{2,1,0:T(8,128)(2,1)S(1)}, bf16[4,64,256]{2,1,0:T(8,128)(2,1)S(1)}, u32[]{:S(2)}, u32[]{:S(2)}) collective-permute-start(bf16[4,64,256]{2,1,0:T(8,128)(2,1)S(1)} %get-tuple-element.32), channel_id=1, source_target_pairs={{0,1},{1,0},{2,3},{3,2},{4,5},{5,4},{6,7},{7,6},{8,9},{9,8},{10,11... | collective-permute-start | bytes 393224 | tf_op jit(solution)/shard_map/ppermute | solution.py:298
  9.2 7.4 %collective-permute-start.3 = (bf16[4,64,256]{2,1,0:T(8,128)(2,1)S(1)}, bf16[4,64,256]{2,1,0:T(8,128)(2,1)S(1)}, u32[]{:S(2)}, u32[]{:S(2)}) collective-permute-start(bf16[4,64,256]{2,1,0:T(8,128)(2,1)S(1)} %get-tuple-element.33), channel_id=1, source_target_pairs={{0,3},{1,2},{2,1},{3,0},{4,7},{5,6},{6,5},{7,4},{8,11},{9,10},{10,... | collective-permute-start | bytes 393224 | tf_op jit(solution)/shard_map/ppermute | solution.py:298
  9.3 10.3 %collective-permute-start.12 = (bf16[4,64,256]{2,1,0:T(8,128)(2,1)S(1)}, bf16[4,64,256]{2,1,0:T(8,128)(2,1)S(1)}, u32[]{:S(2)}, u32[]{:S(2)}) collective-permute-start(bf16[4,64,256]{2,1,0:T(8,128)(2,1)S(1)} %get-tuple-element.42), channel_id=1, source_target_pairs={{0,2},{1,3},{2,0},{3,1},{4,6},{5,7},{6,4},{7,5},{8,10},{9,11},{10,... | collective-permute-start | bytes 393224 | tf_op jit(solution)/shard_map/ppermute | solution.py:298
  11.2 11.5 %collective-permute-start.13 = (bf16[4,64,256]{2,1,0:T(8,128)(2,1)S(1)}, bf16[4,64,256]{2,1,0:T(8,128)(2,1)S(1)}, u32[]{:S(2)}, u32[]{:S(2)}) collective-permute-start(bf16[4,64,256]{2,1,0:T(8,128)(2,1)S(1)} %get-tuple-element.43), channel_id=1, source_target_pairs={{0,1},{1,0},{2,3},{3,2},{4,5},{5,4},{6,7},{7,6},{8,9},{9,8},{10,11... | collective-permute-start | bytes 393224 | tf_op jit(solution)/shard_map/ppermute | solution.py:298
  12.7 10.0 %collective-permute-start.14 = (bf16[4,64,256]{2,1,0:T(8,128)(2,1)S(1)}, bf16[4,64,256]{2,1,0:T(8,128)(2,1)S(1)}, u32[]{:S(2)}, u32[]{:S(2)}) collective-permute-start(bf16[4,64,256]{2,1,0:T(8,128)(2,1)S(1)} %get-tuple-element.44), channel_id=1, source_target_pairs={{0,3},{1,2},{2,1},{3,0},{4,7},{5,6},{6,5},{7,4},{8,11},{9,10},{10,... | collective-permute-start | bytes 393224 | tf_op jit(solution)/shard_map/ppermute | solution.py:298
  17.9 6.5 %collective-permute-start.4 = (bf16[256,256]{1,0:T(8,128)(2,1)S(1)}, bf16[256,256]{1,0:T(8,128)(2,1)S(1)}, u32[]{:S(2)}, u32[]{:S(2)}) collective-permute-start(bf16[256,256]{1,0:T(8,128)(2,1)S(1)} %get-tuple-element.36), channel_id=1, source_target_pairs={{0,4},{1,5},{2,6},{3,7},{4,0},{5,1},{6,2},{7,3},{8,12},{9,13},{10,... | collective-permute-start | bytes 393224 | tf_op jit(solution)/shard_map/ppermute | solution.py:298
  19.5 7.6 %collective-permute-start.7 = (bf16[256,256]{1,0:T(8,128)(2,1)S(1)}, bf16[256,256]{1,0:T(8,128)(2,1)S(1)}, u32[]{:S(2)}, u32[]{:S(2)}) collective-permute-start(bf16[256,256]{1,0:T(8,128)(2,1)S(1)} %get-tuple-element.37), channel_id=1, source_target_pairs={{0,16},{1,17},{2,18},{3,19},{4,8},{5,9},{6,10},{7,11},{8,4},{9,5},... | collective-permute-start | bytes 393224 | tf_op jit(solution)/shard_map/ppermute | solution.py:298
  19.5 11.0 %collective-permute-start.6 = (bf16[256,256]{1,0:T(8,128)(2,1)S(1)}, bf16[256,256]{1,0:T(8,128)(2,1)S(1)}, u32[]{:S(2)}, u32[]{:S(2)}) collective-permute-start(bf16[256,256]{1,0:T(8,128)(2,1)S(1)} %get-tuple-element.37), channel_id=1, source_target_pairs={{0,4},{1,5},{2,6},{3,7},{4,0},{5,1},{6,2},{7,3},{8,12},{9,13},{10,... | collective-permute-start | bytes 393224 | tf_op jit(solution)/shard_map/ppermute | solution.py:298
  24.0 6.5 %collective-permute-start.15 = (bf16[256,256]{1,0:T(8,128)(2,1)S(1)}, bf16[256,256]{1,0:T(8,128)(2,1)S(1)}, u32[]{:S(2)}, u32[]{:S(2)}) collective-permute-start(bf16[256,256]{1,0:T(8,128)(2,1)S(1)} %get-tuple-element.47), channel_id=1, source_target_pairs={{0,4},{1,5},{2,6},{3,7},{4,0},{5,1},{6,2},{7,3},{8,12},{9,13},{10,... | collective-permute-start | bytes 393224 | tf_op jit(solution)/shard_map/ppermute | solution.py:298
  24.4 10.2 %collective-permute-start.5 = (bf16[256,256]{1,0:T(8,128)(2,1)S(1)}, bf16[256,256]{1,0:T(8,128)(2,1)S(1)}, u32[]{:S(2)}, u32[]{:S(2)}) collective-permute-start(bf16[256,256]{1,0:T(8,128)(2,1)S(1)} %far.2), channel_id=1, source_target_pairs={{0,8},{1,9},{2,10},{3,11},{4,12},{5,13},{6,14},{7,15},{8,0},{9,1},... | collective-permute-start | bytes 393224 | tf_op jit(solution)/shard_map/ppermute | solution.py:298
  27.1 9.1 %collective-permute-start.18 = (bf16[256,256]{1,0:T(8,128)(2,1)S(1)}, bf16[256,256]{1,0:T(8,128)(2,1)S(1)}, u32[]{:S(2)}, u32[]{:S(2)}) collective-permute-start(bf16[256,256]{1,0:T(8,128)(2,1)S(1)} %get-tuple-element.48), channel_id=1, source_target_pairs={{0,16},{1,17},{2,18},{3,19},{4,8},{5,9},{6,10},{7,11},{8,4},{9,5},... | collective-permute-start | bytes 393224 | tf_op jit(solution)/shard_map/ppermute | solution.py:298
  27.1 11.2 %collective-permute-start.17 = (bf16[256,256]{1,0:T(8,128)(2,1)S(1)}, bf16[256,256]{1,0:T(8,128)(2,1)S(1)}, u32[]{:S(2)}, u32[]{:S(2)}) collective-permute-start(bf16[256,256]{1,0:T(8,128)(2,1)S(1)} %get-tuple-element.48), channel_id=1, source_target_pairs={{0,4},{1,5},{2,6},{3,7},{12,8},{13,9},{14,10},{15,11},{16,20},{17,... | collective-permute-start | bytes 393224 | tf_op jit(solution)/shard_map/ppermute | solution.py:298
  30.6 10.5 %collective-permute-start.16 = (bf16[256,256]{1,0:T(8,128)(2,1)S(1)}, bf16[256,256]{1,0:T(8,128)(2,1)S(1)}, u32[]{:S(2)}, u32[]{:S(2)}) collective-permute-start(bf16[256,256]{1,0:T(8,128)(2,1)S(1)} %far.3), channel_id=1, source_target_pairs={{0,8},{1,9},{2,10},{3,11},{4,12},{5,13},{6,14},{7,15},{8,0},{9,1},... | collective-permute-start | bytes 393224 | tf_op jit(solution)/shard_map/ppermute | solution.py:298
  34.7 9.2 %collective-permute-start.8 = (bf16[128,256]{1,0:T(8,128)(2,1)S(1)}, bf16[128,256]{1,0:T(8,128)(2,1)S(1)}, u32[]{:S(2)}, u32[]{:S(2)}) collective-permute-start(bf16[128,256]{1,0:T(8,128)(2,1)S(1)} %get-tuple-element.39), channel_id=1, source_target_pairs={{0,3},{1,2},{2,1},{3,0},{4,7},{5,6},{6,5},{7,4},{8,11},{9,10},{10,... | collective-permute-start | bytes 196616 | tf_op jit(solution)/shard_map/ppermute | solution.py:298
  35.7 9.2 %collective-permute-start.9 = (bf16[128,256]{1,0:T(8,128)(2,1)S(1)}, bf16[128,256]{1,0:T(8,128)(2,1)S(1)}, u32[]{:S(2)}, u32[]{:S(2)}) collective-permute-start(bf16[128,256]{1,0:T(8,128)(2,1)S(1)} %get-tuple-element.40), channel_id=1, source_target_pairs={{0,2},{1,3},{2,0},{3,1},{4,6},{5,7},{6,4},{7,5},{8,10},{9,11},{10,... | collective-permute-start | bytes 196616 | tf_op jit(solution)/shard_map/ppermute | solution.py:298
  36.2 8.6 %collective-permute-start.10 = (bf16[128,256]{1,0:T(8,128)(2,1)S(1)}, bf16[128,256]{1,0:T(8,128)(2,1)S(1)}, u32[]{:S(2)}, u32[]{:S(2)}) collective-permute-start(bf16[128,256]{1,0:T(8,128)(2,1)S(1)} %get-tuple-element.38.refs_1_), channel_id=1, source_target_pairs={{0,1},{1,0},{2,3},{3,2},{4,5},{5,4},{6,7},{7,6},{8,9},{9,8},{10,11... | collective-permute-start | bytes 196616 | tf_op jit(solution)/shard_map/ppermute | solution.py:298
  41.2 5.6 %collective-permute-start.19 = (bf16[128,256]{1,0:T(8,128)(2,1)S(1)}, bf16[128,256]{1,0:T(8,128)(2,1)S(1)}, u32[]{:S(2)}, u32[]{:S(2)}) collective-permute-start(bf16[128,256]{1,0:T(8,128)(2,1)S(1)} %get-tuple-element.50), channel_id=1, source_target_pairs={{0,3},{1,2},{2,1},{3,0},{4,7},{5,6},{6,5},{7,4},{8,11},{9,10},{10,... | collective-permute-start | bytes 196616 | tf_op jit(solution)/shard_map/ppermute | solution.py:298
  43.5 4.3 %collective-permute-start.20 = (bf16[128,256]{1,0:T(8,128)(2,1)S(1)}, bf16[128,256]{1,0:T(8,128)(2,1)S(1)}, u32[]{:S(2)}, u32[]{:S(2)}) collective-permute-start(bf16[128,256]{1,0:T(8,128)(2,1)S(1)} %get-tuple-element.51), channel_id=1, source_target_pairs={{0,2},{1,3},{2,0},{3,1},{4,6},{5,7},{6,4},{7,5},{8,10},{9,11},{10,... | collective-permute-start | bytes 196616 | tf_op jit(solution)/shard_map/ppermute | solution.py:298
  44.0 4.9 %copy-start.1 = (bf16[4,1024,512]{2,1,0:T(8,128)(2,1)S(1)}, bf16[4,1024,512]{2,1,0:T(8,128)(2,1)}, u32[]{:S(2)}) copy-start(bf16[4,1024,512]{2,1,0:T(8,128)(2,1)} %refs_2_.2) | copy-start | bytes 12582916
  44.0 4.9 %copy-start.2 = (s32[1,4]{1,0:T(1,128)S(1)}, s32[1,4]{1,0:T(1,128)}, u32[]{:S(2)}) copy-start(s32[1,4]{1,0:T(1,128)} %refs_0_.7) | copy-start | bytes 52
  44.0 4.9 %copy-start.3 = (s32[16]{0:T(128)S(1)}, s32[16]{0:T(128)}, u32[]{:S(2)}) copy-start(s32[16]{0:T(128)} %refs_1_.1) | copy-start | bytes 196
  44.0 4.3 %collective-permute-start.21 = (bf16[128,256]{1,0:T(8,128)(2,1)S(1)}, bf16[128,256]{1,0:T(8,128)(2,1)S(1)}, u32[]{:S(2)}, u32[]{:S(2)}) collective-permute-start(bf16[128,256]{1,0:T(8,128)(2,1)S(1)} %get-tuple-element.49.refs_1_), channel_id=1, source_target_pairs={{0,1},{1,0},{2,3},{3,2},{4,5},{5,4},{6,7},{7,6},{8,9},{9,8},{10,11... | collective-permute-start | bytes 196616 | tf_op jit(solution)/shard_map/ppermute | solution.py:298
  45.3 3.6 %collective-permute-start.11 = (bf16[128,1024]{1,0:T(8,128)(2,1)S(1)}, bf16[128,1024]{1,0:T(8,128)(2,1)S(1)}, u32[]{:S(2)}, u32[]{:S(2)}) collective-permute-start(bf16[128,1024]{1,0:T(8,128)(2,1)S(1)} %phase.2.refs_3_), channel_id=1, source_target_pairs={{0,16},{1,17},{2,18},{3,19},{4,20},{5,21},{6,22},{7,23},{8,24},{9,... | collective-permute-start | bytes 786440 | tf_op jit(solution)/shard_map/ppermute | solution.py:298
  48.8 1.6 %collective-permute-start.22 = (bf16[128,1024]{1,0:T(8,128)(2,1)S(1)}, bf16[128,1024]{1,0:T(8,128)(2,1)S(1)}, u32[]{:S(2)}, u32[]{:S(2)}) collective-permute-start(bf16[128,1024]{1,0:T(8,128)(2,1)S(1)} %phase.3.refs_5_), channel_id=1, source_target_pairs={{0,16},{1,17},{2,18},{3,19},{4,20},{5,21},{6,22},{7,23},{8,24},{9,... | collective-permute-start | bytes 786440 | tf_op jit(solution)/shard_map/ppermute | solution.py:298
